TPU v7x, 32 devices: a whole 2x2x4 slice. The times are simulated.
32 devices in a mesh: patch: 16 (over z, y, x), head: 2 (over core).
Axes of the slice: x: 2, y: 2, z: 4, core: 2. Of those that a mesh axis runs over, the one named last changes fastest.
Arguments:
- inputs: bfloat16 [2, 512, 3072], P(None, 'patch', 'head'), may hold values from -111 to 111
- stale_kv: bfloat16 [2, 512, 512], P(None, 'patch', 'head'), may hold values from -16 to 16
- w_qkv: bfloat16 [3072, 3, 512], P(None, None, 'head'), may hold values from -4 to 4
- w_out: bfloat16 [512, 3072], P('head', 'patch'), may hold values from -0.375 to 0.375
- mod_table: float32 [4, 3, 3072], P(None, None, 'head'), may hold values from -2 to 2
- step_ids: int32 [2], replicated, may hold values from 0 to 3
- slab_order: int32 [16], P('patch'), may hold values from 0 to 15, each once
Outputs:
- branch: bfloat16 [2, 512, 3072], P(None, 'patch', 'head')
Inputs may be any that keep to these rules, and one draw needn't show every extreme that they name: `slab_order`: every slab number once.
All inputs are finite; a program needn't handle non-finite values.
Results may differ from a plain program's by a relative error of at most 0.02.
Values may be sent and summed in bfloat16 or wider, within the bound.
No kernel may reach another device: no remote copies, remote signals or barrier semaphores. Data moves between devices by JAX's collectives and lax.ppermute only.
A program may use at most 64 MiB of HBM per device.

v0:
```python
import math

import jax
import jax.numpy as jnp
from jax import lax
from jax.sharding import PartitionSpec as P

DH = 128
STEPS = 2


def angle_tables(positions, head_size):
    half_size = head_size // 2
    frequency = 10000.0 ** (-(2.0 * jnp.arange(half_size, dtype=jnp.float32)) / head_size)
    angle_grid = positions.astype(jnp.float32)[:, None] * frequency[None, :]
    return (jnp.cos(angle_grid)[:, None, :], jnp.sin(angle_grid)[:, None, :])


def rotate(values, cos_table, sin_table):
    half_size = values.shape[-1] // 2
    front_half = values[..., :half_size]
    back_half = values[..., half_size:]
    return jnp.concatenate(
        [
            front_half * cos_table - back_half * sin_table,
            front_half * sin_table + back_half * cos_table,
        ],
        axis=-1,
    )


def body(inputs, stale_kv, w_qkv, w_out, mod_table, step_ids, slab_order):
    tok_rows = inputs.shape[1]
    feat_cols = inputs.shape[2]
    model_width = w_qkv.shape[0]
    head_cols = w_qkv.shape[2]
    heads_dev = head_cols // DH
    table_rows = mod_table.shape[0]
    inv_root = 1.0 / math.sqrt(DH)
    own_start = lax.axis_index("patch") * tok_rows
    positions = slab_order[0] * tok_rows + jnp.arange(tok_rows, dtype=jnp.int32)
    cos_table, sin_table = angle_tables(positions, DH)
    w_flat = w_qkv.reshape(model_width, 3 * head_cols)
    w_full = lax.all_gather(w_out, "patch", axis=1, tiled=True)
    previous = stale_kv
    results = []
    for step in range(STEPS):
        chooser = jnp.arange(table_rows, dtype=jnp.int32) == step_ids[step]
        modulation = jnp.sum(jnp.where(chooser[:, None, None], mod_table, 0.0), axis=0)
        hidden = inputs[step].astype(jnp.float32)
        statistics = lax.psum((jnp.sum(hidden, axis=1), jnp.sum(hidden * hidden, axis=1)), "head")
        row_mean = statistics[0][:, None] / model_width
        row_square = statistics[1][:, None] / model_width
        inv_scale = lax.rsqrt(row_square - row_mean * row_mean + 1e-06)
        normed = ((hidden - row_mean) * inv_scale * (1.0 + modulation[1]) + modulation[0]).astype(
            jnp.bfloat16
        )
        projected = jnp.dot(
            lax.all_gather(normed, "head", axis=1, tiled=True),
            w_flat,
            preferred_element_type=jnp.float32,
        ).reshape(tok_rows, 3, heads_dev, DH)
        queries = rotate(projected[:, 0], cos_table, sin_table).astype(jnp.bfloat16)
        fresh_k = rotate(projected[:, 1], cos_table, sin_table).astype(jnp.bfloat16)
        fresh_v = projected[:, 2].astype(jnp.bfloat16)
        own_scores = (
            jnp.einsum("qhd,khd->hqk", queries, fresh_k, preferred_element_type=jnp.float32)
            * inv_root
        )
        own_max = jnp.max(own_scores, axis=2, keepdims=True)
        own_weights = jnp.exp(own_scores - own_max)
        own_totals = jnp.sum(own_weights, axis=2, keepdims=True)
        own_weighted = jnp.einsum(
            "hqk,khd->hqd",
            own_weights.astype(jnp.bfloat16),
            fresh_v,
            preferred_element_type=jnp.float32,
        )
        block_rows = lax.all_gather(previous, "patch", axis=1, tiled=True)
        totals = own_totals
        weighted = own_weighted
        piece_rows = block_rows.shape[1]
        key_rows = block_rows[0].reshape(piece_rows, heads_dev, DH)
        value_rows = block_rows[1].reshape(piece_rows, heads_dev, DH)
        scores = (
            jnp.einsum("qhd,khd->hqk", queries, key_rows, preferred_element_type=jnp.float32)
            * inv_root
        )
        row_ids = jnp.arange(piece_rows, dtype=jnp.int32)
        own_mask = (row_ids >= own_start) & (row_ids < own_start + tok_rows)
        scores = jnp.where(own_mask[None, None, :], -1e30, scores)
        new_max = jnp.maximum(own_max, jnp.max(scores, axis=2, keepdims=True))
        rescale = jnp.exp(own_max - new_max)
        weights = jnp.exp(scores - new_max)
        totals = totals * rescale + jnp.sum(weights, axis=2, keepdims=True)
        weighted = weighted * rescale + jnp.einsum(
            "hqk,khd->hqd",
            weights.astype(jnp.bfloat16),
            value_rows,
            preferred_element_type=jnp.float32,
        )
        attended = jnp.transpose((weighted / totals).astype(jnp.bfloat16), (1, 0, 2)).reshape(
            tok_rows, head_cols
        )
        partial_value = jnp.dot(attended, w_full, preferred_element_type=jnp.float32)
        summed = lax.psum(partial_value.astype(jnp.bfloat16), "head").astype(jnp.float32)
        own_cols = lax.dynamic_slice_in_dim(
            summed, lax.axis_index("head") * feat_cols, feat_cols, 1
        )
        results.append((modulation[2] * own_cols).astype(jnp.bfloat16))
        previous = jnp.stack(
            [fresh_k.reshape(tok_rows, head_cols), fresh_v.reshape(tok_rows, head_cols)]
        )
    return jnp.stack(results)


def solution(mesh):
    in_specs = (
        P(None, "patch", "head"),
        P(None, "patch", "head"),
        P(None, None, "head"),
        P("head", "patch"),
        P(None, None, "head"),
        P(),
        P("patch"),
    )
    out_specs = P(None, "patch", "head")
    return jax.shard_map(body, mesh=mesh, in_specs=in_specs, out_specs=out_specs, check_vma=False)
```

profile of v0, /device:TPU:0, one launch (start us, length us, event | category | flops | bytes accessed | tf_op | source)
XLA Modules:
  0.0 155.7 jit_solution(14300233938591025767)
XLA Ops:
  6.5 0.0 all-gather.2.cloned.1.call-start
  6.5 0.7 all-gather.2.cloned.1.call-update
  7.3 0.0 all-reduce.4.cloned.1.call-start
  7.3 1.1 convert_reduce_fusion.1
  8.4 1.1 fusion.20
  9.5 1.3 fusion.71
  10.8 0.6 iota_compare_fusion.2
  11.5 0.7 iota_compare_fusion.3
  12.2 1.1 select_reduce_fusion.1
  13.2 0.1 slice_reduce_fusion.1
  13.3 2.6 %all-reduce = (f32[32]{0:T(128)S(1)}, f32[32]{0:T(128)S(1)}, f32[32]{0:T(128)S(1)}, f32[32]{0:T(128)S(1)}) all-reduce(f32[32]{0:T(128)S(1)} %get-tuple-element.8, f32[32]{0:T(128)S(1)} %get-tuple-element.6, f32[32]{0:T(128)S(1)} %get-tuple-element.7, f32[32]{0:T(128)S(1)} %get-tuple-element.5), channel_id=1, replica_groups=mesh['patch'=16,'head'=2] {'head'}, use_global_device_ids=true, to_apply=%region_14.15 | all-reduce | flops 128 | bytes 1024 | tf_op jit(solution)/shard_map/psum | solution.py:51
  15.9 1.1 fusion.19
  17.0 1.9 %all_gather.15 = bf16[32,3072]{1,0:T(8,128)(2,1)S(1)} all-gather(bf16[32,1536]{1,0:T(8,128)(2,1)S(1)} %get-tuple-element.31), channel_id=1, replica_groups=mesh['patch'=16,'head'=2] {'head'}, dimensions={1}, use_global_device_ids=true | all-gather | bytes 294912 | tf_op jit(solution)/shard_map/all_gather | solution.py:59
  19.0 6.6 %copy.24 = bf16[3072,3,256]{0,2,1:T(8,128)(2,1)} copy(bf16[3072,3,256]{2,0,1:T(8,128)(2,1)} %param.9) | data formatting | bytes 9437184 | tf_op args[2]
  25.6 4.0 %fusion.28 = f32[32,3,2,128]{3,0,2,1:T(8,128)S(1)} fusion(bf16[3,2,128,3072]{3,2,1,0:T(8,128)(2,1)} %bitcast.145, bf16[32,3072]{1,0:T(8,128)(2,1)S(1)} %all_gather.15), kind=kOutput, calls=%fused_computation.43 | convolution fusion | flops 150994944 | bytes 5013504 | tf_op jit(solution)/shard_map/dot_general | solution.py:58
  30.3 1.9 %all_gather.18 = bf16[32,3072]{1,0:T(8,128)(2,1)S(1)} all-gather(bf16[32,1536]{1,0:T(8,128)(2,1)S(1)} %get-tuple-element.32), channel_id=1, replica_groups=mesh['patch'=16,'head'=2] {'head'}, dimensions={1}, use_global_device_ids=true | all-gather | bytes 294912 | tf_op jit(solution)/shard_map/all_gather | solution.py:59
  32.3 0.0 copy-done
  32.3 1.5 fusion.26
  33.7 0.1 copy.26
  33.8 46.8 %all_gather.16 = bf16[2,512,256]{2,0,1:T(2,128)(2,1)S(1)} all-gather(bf16[2,32,256]{2,0,1:T(2,128)(2,1)S(1)} %copy.26), channel_id=1, replica_groups=mesh['patch'=16,'head'=2] {'patch'}, dimensions={1}, use_global_device_ids=true | all-gather | bytes 557056 | tf_op jit(solution)/shard_map/all_gather | solution.py:79
  80.6 0.7 fusion.69
  81.4 0.1 multiply_cosine_fusion
  81.5 0.1 multiply_subtract_fusion
  81.6 0.1 maximum_convert_fusion
  81.8 38.5 %all_gather.19 = bf16[2,512,256]{2,1,0:T(8,128)(2,1)S(1)} all-gather(bf16[2,32,256]{2,1,0:T(8,128)(2,1)S(1)} %pad_maximum_fusion.1), channel_id=1, replica_groups=mesh['patch'=16,'head'=2] {'patch'}, dimensions={1}, use_global_device_ids=true | all-gather | bytes 557056 | tf_op jit(solution)/shard_map/all_gather | solution.py:79
  120.4 0.7 copy.48
  121.0 0.7 copy.49
  121.7 0.1 copy.35
  121.9 0.1 copy.37
  122.0 0.1 subtract_convert_fusion.2
  122.1 0.2 fusion.74
  122.4 0.3 fusion.75
  122.7 0.2 fusion.72
  122.9 0.3 fusion.73
  123.3 0.2 fusion.30
  123.5 0.2 fusion.32
  123.7 0.1 fusion.5
  123.8 0.3 fusion.10
  124.1 0.1 fusion.3
  124.3 0.3 fusion.11
  124.6 0.0 all-gather.2.cloned.1.call-done
  124.6 2.6 %convolution_convert_fusion.1 = bf16[32,3072]{1,0:T(8,128)(2,1)} fusion(bf16[256,3072]{0,1:T(8,128)(2,1)} %all-gather.2.cloned.1.call-done, bf16[2,4,8,128]{3,2,1,0:T(8,128)(2,1)S(1)} %fusion.10), kind=kOutput, calls=%fused_computation.1 | convolution fusion | flops 50429952 | bytes 1785856 | tf_op jit(solution)/shard_map/dot_general | solution.py:105
  127.3 2.7 %convolution_convert_fusion = bf16[32,3072]{1,0:T(8,128)(2,1)} fusion(bf16[256,3072]{0,1:T(8,128)(2,1)} %all-gather.2.cloned.1.call-done, bf16[2,4,8,128]{3,2,1,0:T(8,128)(2,1)S(1)} %fusion.11), kind=kOutput, calls=%fused_computation | convolution fusion | flops 50429952 | bytes 1785856 | tf_op jit(solution)/shard_map/dot_general | solution.py:105
  129.9 0.0 all-reduce.4.cloned.1.call-update
  129.9 16.4 %all-reduce.4.cloned.1.call-done = (bf16[32,3072]{1,0:T(8,128)(2,1)}, bf16[32,3072]{1,0:T(8,128)(2,1)}) async-done(((bf16[32,3072]{1,0:T(8,128)(2,1)}, bf16[32,3072]{1,0:T(8,128)(2,1)}), (bf16[32,3072]{1,0:T(8,128)(2,1)}, bf16[32,3072]{1,0:T(8,128)(2,1)})) %all-reduce.4.cloned.1.call-update) | async-done | bytes 393232 | tf_op jit(solution)/shard_map/psum | solution.py:106
  146.4 0.9 fusion.34
  147.3 0.9 fusion.35
  148.2 0.7 pad_maximum_fusion
  (22 shorter events, 0.3 us)
Async XLA Ops:
  6.5 118.1 %all-gather.2.cloned.1.call-start = ((), (), s32[]{:S(2)}) async-start(), calls=%async_computation | async-start | bytes 1671168 | tf_op jit(solution)/shard_map/all_gather | solution.py:44
  7.3 139.1 %all-reduce.4.cloned.1.call-start = ((), (), s32[]{:S(2)}) async-start(), calls=%async_computation.1 | async-start | bytes 786432 | tf_op jit(solution)/shard_map/psum | solution.py:106
  25.6 6.6 %copy-start = (bf16[3072,3,256]{0,2,1:T(8,128)(2,1)S(1)}, bf16[3072,3,256]{0,2,1:T(8,128)(2,1)}, u32[]{:S(2)}) copy-start(bf16[3072,3,256]{0,2,1:T(8,128)(2,1)} %copy.24) | copy-start | bytes 14155780
  25.6 8.1 %copy-start.1 = (bf16[2,32,256]{2,1,0:T(8,128)(2,1)S(1)}, bf16[2,32,256]{2,1,0:T(8,128)(2,1)}, u32[]{:S(2)}) copy-start(bf16[2,32,256]{2,1,0:T(8,128)(2,1)} %param.8) | copy-start | bytes 98308
Sparse Core Ops, SparseCore 0:
  10.1 63.2 all-gather.1
  130.1 16.2 all-reduce.3
where the time goes:
time: 156 us
  blocking collectives  91.8 us (59%)
  waiting for transfers between devices  17.2 us (11%)
  between operations  14.3 us (9%)
  matrix products  12.7 us (8%)
  local copies, waits for them, and re-layouts  10.5 us (7%)
  other arithmetic  9.18 us (6%)
    all_gather x2, blocking collectives, body(): block_rows = lax.all_gather(previous, 'patch', axis=1, tiled=True)  85.4 us
    psum x1, waiting for transfers between devices, body(): lax.psum(partial_value.astype(jnp.bfloat16), 'head').astype(jnp.float32)  16.4 us
    unnamed x8, local copies, waits for them, and re-layouts  8.04 us
    dot_general x2, matrix products, body(): jnp.dot(lax.all_gather(normed, 'head', axis=1, tiled=True), w_flat, prefe...  5.46 us
    dot_general x2, matrix products, body(): jnp.dot(attended, w_full, preferred_element_type=jnp.float32)  5.31 us
    all_gather x2, blocking collectives, body(): lax.all_gather(normed, 'head', axis=1, tiled=True)  3.89 us
  transfers between devices with their start and end apart: 2, of which 1 were waited for; matrix products, arithmetic and copies ran while one was open for 16% of the time, Pallas kernels for 0%

commit v1 on v0

v1 whole, which is shorter than its diff:
```python
import functools
import math

import jax
import jax.numpy as jnp
from jax import lax
from jax.experimental import pallas as pl
from jax.experimental.pallas import tpu as pltpu
from jax.sharding import PartitionSpec as P

DH = 128
STEPS = 2
PLANE = 4
VMEM_KERNEL = 16 * 1024 * 1024
VMEM = pl.BlockSpec(memory_space=pltpu.VMEM)
SMEM = pl.BlockSpec(memory_space=pltpu.SMEM)


def angle_tables(positions):
    half = DH // 2
    frequency = 10000.0 ** (-(2.0 * jnp.arange(half, dtype=jnp.float32)) / DH)
    grid = positions.astype(jnp.float32)[:, None] * frequency[None, :]
    cos, sin = jnp.cos(grid), jnp.sin(grid)
    return jnp.concatenate([cos, cos], axis=1), jnp.concatenate([-sin, sin], axis=1)


def swap(values, axis, count, bit):
    return lax.ppermute(values, axis, [(i, i ^ bit) for i in range(count)])


def qkv_kernel(n_head, ids, head, *refs):
    x_refs, mod_refs = refs[:n_head], refs[n_head : 2 * n_head]
    w_ref, cos_ref, sin_ref, q_ref, kv0_ref, kv1_ref, a_ref = refs[2 * n_head :]
    rows, feats = x_refs[0].shape[1:]
    width = n_head * feats
    cols = w_ref.shape[2]
    for step in range(STEPS):
        total, square = 0.0, 0.0
        for x_ref in x_refs:
            hidden = x_ref[step].astype(jnp.float32)
            total += jnp.sum(hidden, axis=1, keepdims=True)
            square += jnp.sum(hidden * hidden, axis=1, keepdims=True)
        mean = total / width
        inv = lax.rsqrt(square / width - mean * mean + 1e-06)
        for part in range(n_head):
            shift = mod_refs[part][0, pl.ds(ids[step], 1), :]
            scale = mod_refs[part][1, pl.ds(ids[step], 1), :]
            hidden = x_refs[part][step].astype(jnp.float32)
            a = (hidden - mean) * inv * (1.0 + scale) + shift
            a_ref[part, step * rows : (step + 1) * rows, :] = a.astype(jnp.bfloat16)
    cos, sin = cos_ref[...], sin_ref[...]
    for slot in range(3):
        total = jnp.zeros((STEPS * rows, cols), jnp.float32)
        for part in range(n_head):
            start = pl.multiple_of((head[0] ^ part) * feats, feats)
            total += jnp.dot(
                a_ref[part], w_ref[slot, pl.ds(start, feats), :], preferred_element_type=jnp.float32
            )
        for step in range(STEPS):
            for block in range(cols // DH):
                lanes = slice(block * DH, (block + 1) * DH)
                u = total[step * rows : (step + 1) * rows, lanes]
                if slot < 2:
                    u = u * cos + pltpu.roll(u, DH // 2, 1) * sin
                u = u.astype(jnp.bfloat16)
                if slot == 0:
                    q_ref[step, :, lanes] = u
                else:
                    (kv0_ref, kv1_ref)[step][slot - 1, :, lanes] = u


def attend_kernel(step, q_ref, own_ref, *refs):
    quad_refs, o_ref = refs[:-1], refs[-1]
    cols = q_ref.shape[2]
    for block in range(cols // DH):
        lanes = slice(block * DH, (block + 1) * DH)

        def rows_of(kind):
            pieces = [own_ref[kind, :, lanes]]
            for number, ref in enumerate(quad_refs):
                for place in range(1 if number == 0 else 0, ref.shape[0]):
                    pieces.append(ref[place, kind, :, lanes])
            return jnp.concatenate(pieces, axis=0)

        scores = lax.dot_general(
            q_ref[step, :, lanes],
            rows_of(0),
            (((1,), (1,)), ((), ())),
            preferred_element_type=jnp.float32,
        ) * (1.0 / math.sqrt(DH))
        weights = jnp.exp(scores - jnp.max(scores, axis=1, keepdims=True))
        totals = jnp.sum(weights, axis=1, keepdims=True)
        mixed = jnp.dot(
            weights.astype(jnp.bfloat16), rows_of(1), preferred_element_type=jnp.float32
        )
        o_ref[:, lanes] = (mixed / totals).astype(jnp.bfloat16)


def out_kernel(n_head, ids, patch, head, *refs):
    o_refs = refs[: STEPS * n_head]
    mod_ref = refs[STEPS * n_head]
    quad_refs = refs[STEPS * n_head + 1 : -3]
    out_ref, o_all, sums = refs[-3:]
    rows = o_refs[0].shape[0]
    high = quad_refs[0].shape[0]
    piece = quad_refs[0].shape[1]
    n_patch = high * len(quad_refs)
    blocks = n_patch // n_head
    for part in range(n_head):
        for step in range(STEPS):
            o_all[head[0] ^ part, step * rows : (step + 1) * rows, :] = o_refs[
                part * STEPS + step
            ][...]
    for low in range(blocks):
        total = 0.0
        for part in range(n_head):
            number = part * blocks + low
            source = patch[0] ^ number
            w = quad_refs[number % len(quad_refs)][number // len(quad_refs)]
            total += lax.dot_general(
                o_all[source // blocks], w, (((1,), (1,)), ((), ())), preferred_element_type=jnp.float32
            )
        sums[(patch[0] ^ low) % blocks] = total
    for step in range(STEPS):
        gate = mod_ref[2, pl.ds(ids[step], 1), :]
        out = jnp.concatenate(
            [sums[c, step * rows : (step + 1) * rows, :] for c in range(blocks)], axis=1
        )
        out_ref[step] = (gate * out).astype(jnp.bfloat16)


def call(kernel, shapes, n_smem, n_vmem, scratch=(), flops=0, size=0):
    return pl.pallas_call(
        kernel,
        out_shape=shapes,
        in_specs=[SMEM] * n_smem + [VMEM] * n_vmem,
        out_specs=jax.tree.map(lambda _: VMEM, shapes),
        scratch_shapes=scratch,
        compiler_params=pltpu.CompilerParams(vmem_limit_bytes=VMEM_KERNEL),
        cost_estimate=pl.CostEstimate(flops=flops, bytes_accessed=size, transcendentals=0),
    )


def body(n_patch, n_head, inputs, stale_kv, w_qkv, w_out, mod_table, step_ids, slab_order):
    rows, feats = inputs.shape[1:]
    cols = w_qkv.shape[2]
    patch = lax.axis_index("patch").astype(jnp.int32)[None]
    head = lax.axis_index("head").astype(jnp.int32)[None]
    bf16 = jnp.bfloat16

    def gather(own):
        quad = jnp.stack(
            [own] + [swap(own, "patch", n_patch, PLANE * k) for k in range(1, n_patch // PLANE)]
        )
        return [quad] + [swap(quad, "patch", n_patch, k) for k in range(1, PLANE)]

    x_parts = [inputs] + [swap(inputs, "head", n_head, k) for k in range(1, n_head)]
    mod_parts = [mod_table] + [swap(mod_table, "head", n_head, k) for k in range(1, n_head)]
    mod_parts = [jnp.transpose(part, (1, 0, 2)) for part in mod_parts]
    stale = gather(stale_kv)
    blocks = n_patch // n_head
    turned = lax.ppermute(
        w_out.T,
        ("patch", "head"),
        [
            ((hi * blocks + lo) * n_head + h, (h * blocks + lo) * n_head + hi)
            for hi in range(n_head)
            for lo in range(blocks)
            for h in range(n_head)
        ],
    )
    w_quads = gather(turned)

    positions = slab_order[0] * rows + jnp.arange(rows, dtype=jnp.int32)
    cos, sin = angle_tables(positions)
    kv_shape = jax.ShapeDtypeStruct((2, rows, cols), bf16)
    q, kv0, kv1 = call(
        functools.partial(qkv_kernel, n_head),
        (jax.ShapeDtypeStruct((STEPS, rows, cols), bf16), kv_shape, kv_shape),
        2,
        2 * n_head + 3,
        [pltpu.VMEM((n_head, STEPS * rows, feats), bf16)],
        2 * STEPS * rows * w_qkv.size,
        2 * w_qkv.size,
    )(step_ids, head, *x_parts, *mod_parts, jnp.transpose(w_qkv, (1, 0, 2)), cos, sin)
    o_shape = jax.ShapeDtypeStruct((rows, cols), bf16)

    def attend(step, own, quads):
        size = n_patch * rows * cols
        return call(
            functools.partial(attend_kernel, step), o_shape, 0, 2 + len(quads), (), 4 * rows * size, 4 * size
        )(q, own, *quads)

    fresh = gather(kv0)
    o0 = attend(0, kv0, stale)
    o1 = attend(1, kv1, fresh)
    o_parts = [o0, o1]
    for k in range(1, n_head):
        o_parts += [swap(o0, "head", n_head, k), swap(o1, "head", n_head, k)]
    piece = w_out.shape[1]
    return call(
        functools.partial(out_kernel, n_head),
        jax.ShapeDtypeStruct((STEPS, rows, feats), bf16),
        3,
        STEPS * n_head + 1 + PLANE,
        [
            pltpu.VMEM((n_head, STEPS * rows, cols), bf16),
            pltpu.VMEM((blocks, STEPS * rows, piece), jnp.float32),
        ],
        2 * STEPS * rows * n_patch * w_out.size,
        2 * n_patch * w_out.size,
    )(step_ids, patch, head, *o_parts, mod_parts[0], *w_quads)


def solution(mesh):
    in_specs = (
        P(None, "patch", "head"),
        P(None, "patch", "head"),
        P(None, None, "head"),
        P("head", "patch"),
        P(None, None, "head"),
        P(),
        P("patch"),
    )
    run = functools.partial(body, mesh.shape["patch"], mesh.shape["head"])
    return jax.shard_map(
        run, mesh=mesh, in_specs=in_specs, out_specs=P(None, "patch", "head"), check_vma=False
    )
```

time: 156 us -> 67.3 us (0.43)
  blocking collectives: 91.8 us -> 0 us
  starting transfers between devices: 0.04 us -> 30.5 us
  between operations: 14.3 us -> 0.79 us
  matrix products: 12.7 us -> 0 us
  other arithmetic: 9.18 us -> 1.08 us
  waiting for transfers between devices: 17.2 us -> 24.8 us
  local copies, waits for them, and re-layouts: 10.5 us -> 4.81 us
  Pallas kernels: 0 us -> 4.89 us
    all_gather x4 -> x0, blocking collectives: 89.3 us -> none  [the longest x2 85.4 us: body(): block_rows = lax.all_gather(previous, 'patch', axis=1, tiled=True)]
    ppermute x0 -> x23, starting transfers between devices: none -> 30.5 us  [the longest x22 29 us: swap(): return lax.ppermute(values, axis, [(i, i ^ bit) for i in range(count)])]
    ppermute x0 -> x23, waiting for transfers between devices: none -> 24.8 us  [the longest x22 24.8 us: swap(): return lax.ppermute(values, axis, [(i, i ^ bit) for i in range(count)])]
    psum x1 -> x0, waiting for transfers between devices: 16.4 us -> none  [body(): lax.psum(partial_value.astype(jnp.bfloat16), 'head').astype(jnp.float32)]
    dot_general x12 -> x0, matrix products: 12.7 us -> none  [the longest x2 5.46 us: body(): jnp.dot(lax.all_gather(normed, 'head', axis=1, tiled=True), w_flat, prefe...]
    pallas_call x0 -> x4, Pallas kernels: none -> 4.89 us  [the longest x1 1.98 us: body(): call(functools.partial(out_kernel, n_head), jax.ShapeDtypeStruct((STEPS,...]
    reduce_sum x7 -> x0, other arithmetic: 3.63 us -> none  [the longest x1 1.09 us: body(): jnp.sum(hidden * hidden, axis=1)]
    unnamed x8 -> x12, local copies, waits for them, and re-layouts: 8.04 us -> 4.81 us
  transfers between devices with their start and end apart: 2 -> 23, of which waited for: 1 -> 7; matrix products, arithmetic and copies ran while one was open for 16% -> 2% of each run, Pallas kernels for 0% -> 4%
where the time goes in v1:
time: 67.3 us; the launch traced here: 66.9 us
  starting transfers between devices  30.5 us (45%)
  waiting for transfers between devices  24.8 us (37%)
  Pallas kernels  4.89 us (7%)
  local copies, waits for them, and re-layouts  4.81 us (7%)
  other arithmetic  1.08 us (2%)
  between operations  0.79 us (1%)
    ppermute x22, starting transfers between devices, swap(): return lax.ppermute(values, axis, [(i, i ^ bit) for i in range(count)])  29 us
    ppermute x22, waiting for transfers between devices, swap(): return lax.ppermute(values, axis, [(i, i ^ bit) for i in range(count)])  24.8 us
    unnamed x12, local copies, waits for them, and re-layouts  4.81 us
    pallas_call x1, Pallas kernels, body(): call(functools.partial(out_kernel, n_head), jax.ShapeDtypeStruct((STEPS,...  1.98 us
    pallas_call x1, Pallas kernels, body(): call(functools.partial(qkv_kernel, n_head), (jax.ShapeDtypeStruct((STEPS,...  1.7 us
    ppermute x1, starting transfers between devices, body(): lax.ppermute(w_out.T, ('patch', 'head'), [((hi * blocks + lo) * n_head +...  1.54 us
  transfers between devices with their start and end apart: 23, of which 7 were waited for; matrix products, arithmetic and copies ran while one was open for 2% of the time, Pallas kernels for 4%

profile of v1, /device:TPU:0, one launch (start us, length us, event | category | flops | bytes accessed | tf_op | source)
XLA Modules:
  0.0 66.9 jit_solution(13769506801236845132)
XLA Ops:
  0.0 3.0 %collective-permute-start.2 = (bf16[2,32,256]{2,1,0:T(8,128)(2,1)}, bf16[2,32,256]{2,1,0:T(8,128)(2,1)S(1)}, u32[]{:S(2)}, u32[]{:S(2)}) collective-permute-start(bf16[2,32,256]{2,1,0:T(8,128)(2,1)} %param.8), channel_id=1, source_target_pairs={{0,8},{2,10},{4,12},{6,14},{8,0},{10,2},{12,4},{14,6},{16,24},{18,... | collective-permute-start | bytes 98312 | tf_op jit(solution)/shard_map/ppermute | solution.py:28
  3.0 2.5 %collective-permute-start.4 = (bf16[2,32,256]{2,1,0:T(8,128)(2,1)}, bf16[2,32,256]{2,1,0:T(8,128)(2,1)S(1)}, u32[]{:S(2)}, u32[]{:S(2)}) collective-permute-start(bf16[2,32,256]{2,1,0:T(8,128)(2,1)} %param.8), channel_id=1, source_target_pairs={{0,24},{2,26},{4,28},{6,30},{8,16},{10,18},{12,20},{14,22},{16,8},... | collective-permute-start | bytes 98312 | tf_op jit(solution)/shard_map/ppermute | solution.py:28
  5.5 0.1 collective-permute-start.3
  5.6 1.5 %collective-permute-start.16 = (bf16[192,256]{1,0:T(8,128)(2,1)}, bf16[192,256]{1,0:T(8,128)(2,1)S(1)}, u32[]{:S(2)}, u32[]{:S(2)}) collective-permute-start(bf16[192,256]{1,0:T(8,128)(2,1)} %bitcast.35), channel_id=1, source_target_pairs={{0,0},{1,16},{2,2},{3,18},{4,4},{5,20},{6,6},{7,22},{8,8},{9,24},{... | collective-permute-start | bytes 294920 | tf_op jit(solution)/shard_map/ppermute | solution.py:162
  7.2 3.4 %collective-permute-start = (bf16[2,32,1536]{2,1,0:T(8,128)(2,1)}, bf16[2,32,1536]{2,1,0:T(8,128)(2,1)S(1)}, u32[]{:S(2)}, u32[]{:S(2)}) collective-permute-start(bf16[2,32,1536]{2,1,0:T(8,128)(2,1)} %refs_0_.1), channel_id=1, source_target_pairs={{0,1},{1,0},{2,3},{3,2},{4,5},{5,4},{6,7},{7,6},{8,9},{9,8},{10,11... | collective-permute-start | bytes 589832 | tf_op jit(solution)/shard_map/ppermute | solution.py:28
  11.2 0.1 fusion
  11.3 0.1 pad_maximum_fusion.3
  11.4 0.0 collective-permute-done.2
  11.4 0.1 collective-permute-start.1
  11.5 0.0 collective-permute-done.16
  11.5 5.1 %collective-permute-start.19 = (bf16[192,256]{1,0:T(8,128)(2,1)S(1)}, bf16[192,256]{1,0:T(8,128)(2,1)S(1)}, u32[]{:S(2)}, u32[]{:S(2)}) collective-permute-start(bf16[192,256]{1,0:T(8,128)(2,1)S(1)} %collective-permute-done.16), channel_id=1, source_target_pairs={{0,24},{2,26},{4,28},{6,30},{8,16},{10,18},{12,20},{14,22},{16,8},... | collective-permute-start | bytes 294920 | tf_op jit(solution)/shard_map/ppermute | solution.py:28
  16.6 0.0 collective-permute-done.4
  16.6 0.0 collective-permute-start.18
  16.6 0.0 collective-permute-done.3
  16.6 0.6 collective-permute-start.17
  17.2 0.8 %pad_maximum_fusion.1.refs_0_ = bf16[4,2,32,256]{3,2,1,0:T(8,128)(2,1)S(1)} fusion(bf16[1,2,32,256]{3,2,1,0:T(8,128)(2,1)S(1)} %bitcast.30, bf16[1,2,32,256]{3,2,1,0:T(8,128)(2,1)S(1)} %bitcast.31, bf16[1,2,32,256]{3,2,1,0:T(8,128)(2,1)S(1)} %bitcast.29, bf16[1,2,32,256]{3,2,1,0:T(8,128)(2,1)} %bitcast.28), kind=kLoop, calls=%fused_computation.1 | loop fusion | flops 196608 | bytes 262144 | tf_op jit(solution)/shard_map/stack | solution.py:152
  18.0 2.5 %collective-permute-start.7 = (bf16[4,2,32,256]{3,2,1,0:T(8,128)(2,1)S(1)}, bf16[4,2,32,256]{3,2,1,0:T(8,128)(2,1)S(1)}, u32[]{:S(2)}, u32[]{:S(2)}) collective-permute-start(bf16[4,2,32,256]{3,2,1,0:T(8,128)(2,1)S(1)} %pad_maximum_fusion.1.refs_0_), channel_id=1, source_target_pairs={{0,6},{2,4},{4,2},{6,0},{8,14},{10,12},{12,10},{14,8},{16,22},{18,... | collective-permute-start | bytes 393224 | tf_op jit(solution)/shard_map/ppermute | solution.py:28
  20.5 0.5 collective-permute-start.6
  21.0 2.3 %copy-done = bf16[3072,3,256]{2,0,1:T(8,128)(2,1)S(1)} copy-done((bf16[3072,3,256]{2,0,1:T(8,128)(2,1)S(1)}, bf16[3072,3,256]{2,0,1:T(8,128)(2,1)}, u32[]{:S(2)}) %copy-start) | copy-done | bytes 4718616
  23.4 0.9 %copy-done.1 = f32[4,3,1536]{2,0,1:T(4,128)S(1)} copy-done((f32[4,3,1536]{2,0,1:T(4,128)S(1)}, f32[4,3,1536]{2,0,1:T(4,128)}, u32[]{:S(2)}) %copy-start.1) | copy-done | bytes 73752
  24.2 0.9 %copy-done.3 = bf16[2,32,1536]{2,1,0:T(8,128)(2,1)S(1)} copy-done((bf16[2,32,1536]{2,1,0:T(8,128)(2,1)S(1)}, bf16[2,32,1536]{2,1,0:T(8,128)(2,1)}, u32[]{:S(2)}) %copy-start.3) | copy-done | bytes 196632
  25.2 0.7 copy-done.4
  25.8 1.7 %shard_map.73 = (bf16[2,32,256]{2,1,0:T(8,128)(2,1)S(1)}, bf16[2,32,256]{2,1,0:T(8,128)(2,1)S(1)}, bf16[2,32,256]{2,1,0:T(8,128)(2,1)S(1)}) custom-call(s32[2]{0:T(128)S(1)} %copy-done.4, s32[1]{0:T(128)} %bitcast.1.head, bf16[2,32,1536]{2,1,0:T(8,128)(2,1)S(1)} %copy-done.3, bf16[2,32,1536]{2,1,0:T(8,128)(2,1)S(1)} %collective-permute-done.refs_1_, ...), custom_call_target="tpu_custom_call" | custom-call | flops 301989888 | bytes 4718592 | tf_op jit(solution)/shard_map/pallas_call | solution.py:177
  27.5 0.0 collective-permute-done.19
  27.5 3.9 %collective-permute-start.10 = (bf16[2,32,256]{2,1,0:T(8,128)(2,1)S(1)}, bf16[2,32,256]{2,1,0:T(8,128)(2,1)S(1)}, u32[]{:S(2)}, u32[]{:S(2)}) collective-permute-start(bf16[2,32,256]{2,1,0:T(8,128)(2,1)S(1)} %get-tuple-element.9.own_ref), channel_id=1, source_target_pairs={{0,24},{2,26},{4,28},{6,30},{8,16},{10,18},{12,20},{14,22},{16,8},... | collective-permute-start | bytes 98312 | tf_op jit(solution)/shard_map/ppermute | solution.py:28
  31.4 0.0 collective-permute-done.18
  31.4 0.6 collective-permute-start.8
  32.1 0.1 pad_maximum_fusion.refs_5_
  32.1 1.2 %collective-permute-done.10 = bf16[2,32,256]{2,1,0:T(8,128)(2,1)S(1)} collective-permute-done((bf16[2,32,256]{2,1,0:T(8,128)(2,1)S(1)}, bf16[2,32,256]{2,1,0:T(8,128)(2,1)S(1)}, u32[]{:S(2)}, u32[]{:S(2)}) %collective-permute-start.10) | collective-permute-done | bytes 32800 | tf_op jit(solution)/shard_map/ppermute | solution.py:28
  33.3 1.5 %collective-permute-start.22 = (bf16[4,192,256]{2,1,0:T(8,128)(2,1)S(1)}, bf16[4,192,256]{2,1,0:T(8,128)(2,1)S(1)}, u32[]{:S(2)}, u32[]{:S(2)}) collective-permute-start(bf16[4,192,256]{2,1,0:T(8,128)(2,1)S(1)} %pad_maximum_fusion.refs_5_), channel_id=1, source_target_pairs={{0,6},{2,4},{4,2},{6,0},{8,14},{10,12},{12,10},{14,8},{16,22},{18,... | collective-permute-start | bytes 1179656 | tf_op jit(solution)/shard_map/ppermute | solution.py:28
  34.8 1.4 %collective-permute-done.9 = bf16[2,32,256]{2,1,0:T(8,128)(2,1)S(1)} collective-permute-done((bf16[2,32,256]{2,1,0:T(8,128)(2,1)S(1)}, bf16[2,32,256]{2,1,0:T(8,128)(2,1)S(1)}, u32[]{:S(2)}, u32[]{:S(2)}) %collective-permute-start.9) | collective-permute-done | bytes 32800 | tf_op jit(solution)/shard_map/ppermute | solution.py:28
  36.2 1.5 %collective-permute-start.21 = (bf16[4,192,256]{2,1,0:T(8,128)(2,1)S(1)}, bf16[4,192,256]{2,1,0:T(8,128)(2,1)S(1)}, u32[]{:S(2)}, u32[]{:S(2)}) collective-permute-start(bf16[4,192,256]{2,1,0:T(8,128)(2,1)S(1)} %pad_maximum_fusion.refs_5_), channel_id=1, source_target_pairs={{0,4},{2,6},{4,0},{6,2},{8,12},{10,14},{12,8},{14,10},{16,20},{18,... | collective-permute-start | bytes 1179656 | tf_op jit(solution)/shard_map/ppermute | solution.py:28
  37.8 0.0 collective-permute-done.8
  37.8 0.5 collective-permute-start.20
  38.3 0.0 collective-permute-done.7.refs_3_
  38.3 1.6 %collective-permute-start.5 = (bf16[4,2,32,256]{3,2,1,0:T(8,128)(2,1)S(1)}, bf16[4,2,32,256]{3,2,1,0:T(8,128)(2,1)S(1)}, u32[]{:S(2)}, u32[]{:S(2)}) collective-permute-start(bf16[4,2,32,256]{3,2,1,0:T(8,128)(2,1)S(1)} %pad_maximum_fusion.1.refs_0_), channel_id=1, source_target_pairs={{0,2},{2,0},{4,6},{6,4},{8,10},{10,8},{12,14},{14,12},{16,18},{18,... | collective-permute-start | bytes 393224 | tf_op jit(solution)/shard_map/ppermute | solution.py:28
  39.9 0.5 collective-permute-start.13
  40.4 16.2 %collective-permute-done.5.refs_1_ = bf16[4,2,32,256]{3,2,1,0:T(8,128)(2,1)S(1)} collective-permute-done((bf16[4,2,32,256]{3,2,1,0:T(8,128)(2,1)S(1)}, bf16[4,2,32,256]{3,2,1,0:T(8,128)(2,1)S(1)}, u32[]{:S(2)}, u32[]{:S(2)}) %collective-permute-start.5) | collective-permute-done | bytes 131104 | tf_op jit(solution)/shard_map/ppermute | solution.py:28
  56.6 0.5 collective-permute-start.12
  57.1 0.9 %collective-permute-done.13.refs_3_ = bf16[4,2,32,256]{3,2,1,0:T(8,128)(2,1)S(1)} collective-permute-done((bf16[4,2,32,256]{3,2,1,0:T(8,128)(2,1)S(1)}, bf16[4,2,32,256]{3,2,1,0:T(8,128)(2,1)S(1)}, u32[]{:S(2)}, u32[]{:S(2)}) %collective-permute-start.13) | collective-permute-done | bytes 131104 | tf_op jit(solution)/shard_map/ppermute | solution.py:28
  58.1 0.5 collective-permute-start.11
  58.6 0.6 shard_map.74.refs_0_
  59.2 2.4 %collective-permute-done.12.refs_2_ = bf16[4,2,32,256]{3,2,1,0:T(8,128)(2,1)S(1)} collective-permute-done((bf16[4,2,32,256]{3,2,1,0:T(8,128)(2,1)S(1)}, bf16[4,2,32,256]{3,2,1,0:T(8,128)(2,1)S(1)}, u32[]{:S(2)}, u32[]{:S(2)}) %collective-permute-start.12) | collective-permute-done | bytes 131104 | tf_op jit(solution)/shard_map/ppermute | solution.py:28
  61.6 1.4 %collective-permute-done.11.refs_1_ = bf16[4,2,32,256]{3,2,1,0:T(8,128)(2,1)S(1)} collective-permute-done((bf16[4,2,32,256]{3,2,1,0:T(8,128)(2,1)S(1)}, bf16[4,2,32,256]{3,2,1,0:T(8,128)(2,1)S(1)}, u32[]{:S(2)}, u32[]{:S(2)}) %collective-permute-start.11) | collective-permute-done | bytes 131104 | tf_op jit(solution)/shard_map/ppermute | solution.py:28
  63.0 0.6 shard_map.75.refs_1_
  63.6 0.1 collective-permute-start.15
  63.7 1.2 %collective-permute-done.15.refs_3_ = bf16[32,256]{1,0:T(8,128)(2,1)S(1)} collective-permute-done((bf16[32,256]{1,0:T(8,128)(2,1)S(1)}, bf16[32,256]{1,0:T(8,128)(2,1)S(1)}, u32[]{:S(2)}, u32[]{:S(2)}) %collective-permute-start.15) | collective-permute-done | bytes 16416 | tf_op jit(solution)/shard_map/ppermute | solution.py:28
  64.9 2.0 %shard_map.76 = bf16[2,32,1536]{2,1,0:T(8,128)(2,1)} custom-call(s32[2]{0:T(128)S(1)} %copy-done.5, s32[1]{0:T(128)} %bitcast.patch, s32[1]{0:T(128)} %bitcast.1.head, bf16[32,256]{1,0:T(8,128)(2,1)S(1)} %shard_map.74.refs_0_, bf16[32,256]{1,0:T(8,128)(2,1)S(1)} %shard_map.75.refs_1_, bf16[32,256]{1,0:T(8,128)(2,1)S(1)} %collective-permute-done.14.refs_2_, ...), custom_call_target="tpu_custom_call" | custom-call | flops 100663296 | bytes 1572864 | tf_op jit(solution)/shard_map/pallas_call | solution.py:201
  (21 shorter events, 0.1 us)
Async XLA Ops:
  0.0 64.9 %copy-start.2 = (f32[4,3,1536]{2,0,1:T(4,128)S(1)}, f32[4,3,1536]{2,0,1:T(4,128)}, u32[]{:S(2)}) copy-start(f32[4,3,1536]{2,0,1:T(4,128)} %param.11) | copy-start | bytes 221188
  0.0 64.9 %copy-start.5 = (s32[2]{0:T(128)S(1)}, s32[2]{0:T(128)}, u32[]{:S(2)}) copy-start(s32[2]{0:T(128)} %ids.3) | copy-start | bytes 28
  0.0 11.4 %collective-permute-start.2 = (bf16[2,32,256]{2,1,0:T(8,128)(2,1)}, bf16[2,32,256]{2,1,0:T(8,128)(2,1)S(1)}, u32[]{:S(2)}, u32[]{:S(2)}) collective-permute-start(bf16[2,32,256]{2,1,0:T(8,128)(2,1)} %param.8), channel_id=1, source_target_pairs={{0,8},{2,10},{4,12},{6,14},{8,0},{10,2},{12,4},{14,6},{16,24},{18,... | collective-permute-start | bytes 98312 | tf_op jit(solution)/shard_map/ppermute | solution.py:28
  3.0 13.6 %collective-permute-start.4 = (bf16[2,32,256]{2,1,0:T(8,128)(2,1)}, bf16[2,32,256]{2,1,0:T(8,128)(2,1)S(1)}, u32[]{:S(2)}, u32[]{:S(2)}) collective-permute-start(bf16[2,32,256]{2,1,0:T(8,128)(2,1)} %param.8), channel_id=1, source_target_pairs={{0,24},{2,26},{4,28},{6,30},{8,16},{10,18},{12,20},{14,22},{16,8},... | collective-permute-start | bytes 98312 | tf_op jit(solution)/shard_map/ppermute | solution.py:28
  5.5 11.1 %collective-permute-start.3 = (bf16[2,32,256]{2,1,0:T(8,128)(2,1)}, bf16[2,32,256]{2,1,0:T(8,128)(2,1)S(1)}, u32[]{:S(2)}, u32[]{:S(2)}) collective-permute-start(bf16[2,32,256]{2,1,0:T(8,128)(2,1)} %param.8), channel_id=1, source_target_pairs={{0,16},{2,18},{4,20},{6,22},{8,24},{10,26},{12,28},{14,30},{16,0},... | collective-permute-start | bytes 98312 | tf_op jit(solution)/shard_map/ppermute | solution.py:28
  5.6 5.9 %collective-permute-start.16 = (bf16[192,256]{1,0:T(8,128)(2,1)}, bf16[192,256]{1,0:T(8,128)(2,1)S(1)}, u32[]{:S(2)}, u32[]{:S(2)}) collective-permute-start(bf16[192,256]{1,0:T(8,128)(2,1)} %bitcast.35), channel_id=1, source_target_pairs={{0,0},{1,16},{2,2},{3,18},{4,4},{5,20},{6,6},{7,22},{8,8},{9,24},{... | collective-permute-start | bytes 294920 | tf_op jit(solution)/shard_map/ppermute | solution.py:162
  7.2 13.3 %collective-permute-start = (bf16[2,32,1536]{2,1,0:T(8,128)(2,1)}, bf16[2,32,1536]{2,1,0:T(8,128)(2,1)S(1)}, u32[]{:S(2)}, u32[]{:S(2)}) collective-permute-start(bf16[2,32,1536]{2,1,0:T(8,128)(2,1)} %refs_0_.1), channel_id=1, source_target_pairs={{0,1},{1,0},{2,3},{3,2},{4,5},{5,4},{6,7},{7,6},{8,9},{9,8},{10,11... | collective-permute-start | bytes 589832 | tf_op jit(solution)/shard_map/ppermute | solution.py:28
  11.4 6.6 %collective-permute-start.1 = (f32[4,3,1536]{2,0,1:T(4,128)}, f32[4,3,1536]{2,0,1:T(4,128)S(1)}, u32[]{:S(2)}, u32[]{:S(2)}) collective-permute-start(f32[4,3,1536]{2,0,1:T(4,128)} %param.11), channel_id=1, source_target_pairs={{0,1},{1,0},{2,3},{3,2},{4,5},{5,4},{6,7},{7,6},{8,9},{9,8},{10,11... | collective-permute-start | bytes 221192 | tf_op jit(solution)/shard_map/ppermute | solution.py:28
  11.5 16.0 %collective-permute-start.19 = (bf16[192,256]{1,0:T(8,128)(2,1)S(1)}, bf16[192,256]{1,0:T(8,128)(2,1)S(1)}, u32[]{:S(2)}, u32[]{:S(2)}) collective-permute-start(bf16[192,256]{1,0:T(8,128)(2,1)S(1)} %collective-permute-done.16), channel_id=1, source_target_pairs={{0,24},{2,26},{4,28},{6,30},{8,16},{10,18},{12,20},{14,22},{16,8},... | collective-permute-start | bytes 294920 | tf_op jit(solution)/shard_map/ppermute | solution.py:28
  16.6 14.8 %collective-permute-start.18 = (bf16[192,256]{1,0:T(8,128)(2,1)S(1)}, bf16[192,256]{1,0:T(8,128)(2,1)S(1)}, u32[]{:S(2)}, u32[]{:S(2)}) collective-permute-start(bf16[192,256]{1,0:T(8,128)(2,1)S(1)} %collective-permute-done.16), channel_id=1, source_target_pairs={{0,16},{2,18},{4,20},{6,22},{8,24},{10,26},{12,28},{14,30},{16,0},... | collective-permute-start | bytes 294920 | tf_op jit(solution)/shard_map/ppermute | solution.py:28
  16.6 14.8 %collective-permute-start.17 = (bf16[192,256]{1,0:T(8,128)(2,1)S(1)}, bf16[192,256]{1,0:T(8,128)(2,1)S(1)}, u32[]{:S(2)}, u32[]{:S(2)}) collective-permute-start(bf16[192,256]{1,0:T(8,128)(2,1)S(1)} %collective-permute-done.16), channel_id=1, source_target_pairs={{0,8},{2,10},{4,12},{6,14},{8,0},{10,2},{12,4},{14,6},{16,24},{18,... | collective-permute-start | bytes 294920 | tf_op jit(solution)/shard_map/ppermute | solution.py:28
  18.0 20.3 %collective-permute-start.7 = (bf16[4,2,32,256]{3,2,1,0:T(8,128)(2,1)S(1)}, bf16[4,2,32,256]{3,2,1,0:T(8,128)(2,1)S(1)}, u32[]{:S(2)}, u32[]{:S(2)}) collective-permute-start(bf16[4,2,32,256]{3,2,1,0:T(8,128)(2,1)S(1)} %pad_maximum_fusion.1.refs_0_), channel_id=1, source_target_pairs={{0,6},{2,4},{4,2},{6,0},{8,14},{10,12},{12,10},{14,8},{16,22},{18,... | collective-permute-start | bytes 393224 | tf_op jit(solution)/shard_map/ppermute | solution.py:28
  20.5 19.4 %collective-permute-start.6 = (bf16[4,2,32,256]{3,2,1,0:T(8,128)(2,1)S(1)}, bf16[4,2,32,256]{3,2,1,0:T(8,128)(2,1)S(1)}, u32[]{:S(2)}, u32[]{:S(2)}) collective-permute-start(bf16[4,2,32,256]{3,2,1,0:T(8,128)(2,1)S(1)} %pad_maximum_fusion.1.refs_0_), channel_id=1, source_target_pairs={{0,4},{2,6},{4,0},{6,2},{8,12},{10,14},{12,8},{14,10},{16,20},{18,... | collective-permute-start | bytes 393224 | tf_op jit(solution)/shard_map/ppermute | solution.py:28
  21.0 2.3 %copy-start = (bf16[3072,3,256]{2,0,1:T(8,128)(2,1)S(1)}, bf16[3072,3,256]{2,0,1:T(8,128)(2,1)}, u32[]{:S(2)}) copy-start(bf16[3072,3,256]{2,0,1:T(8,128)(2,1)} %param.9) | copy-start | bytes 14155780
  23.4 0.9 %copy-start.1 = (f32[4,3,1536]{2,0,1:T(4,128)S(1)}, f32[4,3,1536]{2,0,1:T(4,128)}, u32[]{:S(2)}) copy-start(f32[4,3,1536]{2,0,1:T(4,128)} %param.11) | copy-start | bytes 221188
  24.2 0.9 %copy-start.3 = (bf16[2,32,1536]{2,1,0:T(8,128)(2,1)S(1)}, bf16[2,32,1536]{2,1,0:T(8,128)(2,1)}, u32[]{:S(2)}) copy-start(bf16[2,32,1536]{2,1,0:T(8,128)(2,1)} %refs_0_.1) | copy-start | bytes 589828
  25.2 0.7 copy-start.4
  27.5 5.8 %collective-permute-start.10 = (bf16[2,32,256]{2,1,0:T(8,128)(2,1)S(1)}, bf16[2,32,256]{2,1,0:T(8,128)(2,1)S(1)}, u32[]{:S(2)}, u32[]{:S(2)}) collective-permute-start(bf16[2,32,256]{2,1,0:T(8,128)(2,1)S(1)} %get-tuple-element.9.own_ref), channel_id=1, source_target_pairs={{0,24},{2,26},{4,28},{6,30},{8,16},{10,18},{12,20},{14,22},{16,8},... | collective-permute-start | bytes 98312 | tf_op jit(solution)/shard_map/ppermute | solution.py:28
  31.4 4.8 %collective-permute-start.9 = (bf16[2,32,256]{2,1,0:T(8,128)(2,1)S(1)}, bf16[2,32,256]{2,1,0:T(8,128)(2,1)S(1)}, u32[]{:S(2)}, u32[]{:S(2)}) collective-permute-start(bf16[2,32,256]{2,1,0:T(8,128)(2,1)S(1)} %get-tuple-element.9.own_ref), channel_id=1, source_target_pairs={{0,16},{2,18},{4,20},{6,22},{8,24},{10,26},{12,28},{14,30},{16,0},... | collective-permute-start | bytes 98312 | tf_op jit(solution)/shard_map/ppermute | solution.py:28
  31.4 6.3 %collective-permute-start.8 = (bf16[2,32,256]{2,1,0:T(8,128)(2,1)S(1)}, bf16[2,32,256]{2,1,0:T(8,128)(2,1)S(1)}, u32[]{:S(2)}, u32[]{:S(2)}) collective-permute-start(bf16[2,32,256]{2,1,0:T(8,128)(2,1)S(1)} %get-tuple-element.9.own_ref), channel_id=1, source_target_pairs={{0,8},{2,10},{4,12},{6,14},{8,0},{10,2},{12,4},{14,6},{16,24},{18,... | collective-permute-start | bytes 98312 | tf_op jit(solution)/shard_map/ppermute | solution.py:28
  33.3 31.6 %collective-permute-start.22 = (bf16[4,192,256]{2,1,0:T(8,128)(2,1)S(1)}, bf16[4,192,256]{2,1,0:T(8,128)(2,1)S(1)}, u32[]{:S(2)}, u32[]{:S(2)}) collective-permute-start(bf16[4,192,256]{2,1,0:T(8,128)(2,1)S(1)} %pad_maximum_fusion.refs_5_), channel_id=1, source_target_pairs={{0,6},{2,4},{4,2},{6,0},{8,14},{10,12},{12,10},{14,8},{16,22},{18,... | collective-permute-start | bytes 1179656 | tf_op jit(solution)/shard_map/ppermute | solution.py:28
  36.2 28.7 %collective-permute-start.21 = (bf16[4,192,256]{2,1,0:T(8,128)(2,1)S(1)}, bf16[4,192,256]{2,1,0:T(8,128)(2,1)S(1)}, u32[]{:S(2)}, u32[]{:S(2)}) collective-permute-start(bf16[4,192,256]{2,1,0:T(8,128)(2,1)S(1)} %pad_maximum_fusion.refs_5_), channel_id=1, source_target_pairs={{0,4},{2,6},{4,0},{6,2},{8,12},{10,14},{12,8},{14,10},{16,20},{18,... | collective-permute-start | bytes 1179656 | tf_op jit(solution)/shard_map/ppermute | solution.py:28
  37.8 27.1 %collective-permute-start.20 = (bf16[4,192,256]{2,1,0:T(8,128)(2,1)S(1)}, bf16[4,192,256]{2,1,0:T(8,128)(2,1)S(1)}, u32[]{:S(2)}, u32[]{:S(2)}) collective-permute-start(bf16[4,192,256]{2,1,0:T(8,128)(2,1)S(1)} %pad_maximum_fusion.refs_5_), channel_id=1, source_target_pairs={{0,2},{2,0},{4,6},{6,4},{8,10},{10,8},{12,14},{14,12},{16,18},{18,... | collective-permute-start | bytes 1179656 | tf_op jit(solution)/shard_map/ppermute | solution.py:28
  38.3 18.3 %collective-permute-start.5 = (bf16[4,2,32,256]{3,2,1,0:T(8,128)(2,1)S(1)}, bf16[4,2,32,256]{3,2,1,0:T(8,128)(2,1)S(1)}, u32[]{:S(2)}, u32[]{:S(2)}) collective-permute-start(bf16[4,2,32,256]{3,2,1,0:T(8,128)(2,1)S(1)} %pad_maximum_fusion.1.refs_0_), channel_id=1, source_target_pairs={{0,2},{2,0},{4,6},{6,4},{8,10},{10,8},{12,14},{14,12},{16,18},{18,... | collective-permute-start | bytes 393224 | tf_op jit(solution)/shard_map/ppermute | solution.py:28
  39.9 18.2 %collective-permute-start.13 = (bf16[4,2,32,256]{3,2,1,0:T(8,128)(2,1)S(1)}, bf16[4,2,32,256]{3,2,1,0:T(8,128)(2,1)S(1)}, u32[]{:S(2)}, u32[]{:S(2)}) collective-permute-start(bf16[4,2,32,256]{3,2,1,0:T(8,128)(2,1)S(1)} %pad_maximum_fusion.2.refs_0_), channel_id=1, source_target_pairs={{0,6},{2,4},{4,2},{6,0},{8,14},{10,12},{12,10},{14,8},{16,22},{18,... | collective-permute-start | bytes 393224 | tf_op jit(solution)/shard_map/ppermute | solution.py:28
  56.6 5.0 %collective-permute-start.12 = (bf16[4,2,32,256]{3,2,1,0:T(8,128)(2,1)S(1)}, bf16[4,2,32,256]{3,2,1,0:T(8,128)(2,1)S(1)}, u32[]{:S(2)}, u32[]{:S(2)}) collective-permute-start(bf16[4,2,32,256]{3,2,1,0:T(8,128)(2,1)S(1)} %pad_maximum_fusion.2.refs_0_), channel_id=1, source_target_pairs={{0,4},{2,6},{4,0},{6,2},{8,12},{10,14},{12,8},{14,10},{16,20},{18,... | collective-permute-start | bytes 393224 | tf_op jit(solution)/shard_map/ppermute | solution.py:28
  58.1 5.0 %collective-permute-start.11 = (bf16[4,2,32,256]{3,2,1,0:T(8,128)(2,1)S(1)}, bf16[4,2,32,256]{3,2,1,0:T(8,128)(2,1)S(1)}, u32[]{:S(2)}, u32[]{:S(2)}) collective-permute-start(bf16[4,2,32,256]{3,2,1,0:T(8,128)(2,1)S(1)} %pad_maximum_fusion.2.refs_0_), channel_id=1, source_target_pairs={{0,2},{2,0},{4,6},{6,4},{8,10},{10,8},{12,14},{14,12},{16,18},{18,... | collective-permute-start | bytes 393224 | tf_op jit(solution)/shard_map/ppermute | solution.py:28
  61.6 2.1 %collective-permute-start.14 = (bf16[32,256]{1,0:T(8,128)(2,1)S(1)}, bf16[32,256]{1,0:T(8,128)(2,1)S(1)}, u32[]{:S(2)}, u32[]{:S(2)}) collective-permute-start(bf16[32,256]{1,0:T(8,128)(2,1)S(1)} %shard_map.74.refs_0_), channel_id=1, source_target_pairs={{0,1},{1,0},{2,3},{3,2},{4,5},{5,4},{6,7},{7,6},{8,9},{9,8},{10,11... | collective-permute-start | bytes 49160 | tf_op jit(solution)/shard_map/ppermute | solution.py:28
  63.6 1.2 %collective-permute-start.15 = (bf16[32,256]{1,0:T(8,128)(2,1)S(1)}, bf16[32,256]{1,0:T(8,128)(2,1)S(1)}, u32[]{:S(2)}, u32[]{:S(2)}) collective-permute-start(bf16[32,256]{1,0:T(8,128)(2,1)S(1)} %shard_map.75.refs_1_), channel_id=1, source_target_pairs={{0,1},{1,0},{2,3},{3,2},{4,5},{5,4},{6,7},{7,6},{8,9},{9,8},{10,11... | collective-permute-start | bytes 49160 | tf_op jit(solution)/shard_map/ppermute | solution.py:28

commit v2 on v1

v2 whole, which is shorter than its diff:
```python
import functools
import math

import jax
import jax.numpy as jnp
from jax import lax
from jax.experimental import pallas as pl
from jax.experimental.pallas import tpu as pltpu
from jax.sharding import PartitionSpec as P

DH = 128
STEPS = 2
PLANE = 4
MIB = 1024 * 1024
VMEM = pl.BlockSpec(memory_space=pltpu.VMEM)
SMEM = pl.BlockSpec(memory_space=pltpu.SMEM)
ANY = pl.BlockSpec(memory_space=pl.ANY)
BF16, F32 = jnp.bfloat16, jnp.float32
NT = (((1,), (1,)), ((), ()))


def angle_tables(positions):
    half = DH // 2
    frequency = 10000.0 ** (-(2.0 * jnp.arange(half, dtype=F32)) / DH)
    grid = positions.astype(F32)[:, None] * frequency[None, :]
    cos, sin = jnp.cos(grid), jnp.sin(grid)
    return jnp.concatenate([cos, cos], axis=1), jnp.concatenate([-sin, sin], axis=1)


def swap(values, axis, count, bit):
    return lax.ppermute(values, axis, [(i, i ^ bit) for i in range(count)])


def load_kernel(*refs):
    count = len(refs) // 2
    sems = refs[-1]
    copies = [
        pltpu.make_async_copy(refs[i], refs[count + i], sems.at[i]) for i in range(count)
    ]
    for copy in copies:
        copy.start()
    for copy in copies:
        copy.wait()


def qkv_kernel(n_head, ids, head, *refs):
    x_refs, mod_refs = refs[:n_head], refs[n_head : 2 * n_head]
    w_ref, cos_ref, sin_ref, q_ref, kv0_ref, kv1_ref, a_ref = refs[2 * n_head :]
    rows, feats = x_refs[0].shape[1:]
    width = n_head * feats
    cols = w_ref.shape[2]
    for step in range(STEPS):
        total, square = 0.0, 0.0
        for x_ref in x_refs:
            hidden = x_ref[step].astype(F32)
            total += jnp.sum(hidden, axis=1, keepdims=True)
            square += jnp.sum(hidden * hidden, axis=1, keepdims=True)
        mean = total / width
        inv = lax.rsqrt(square / width - mean * mean + 1e-06)
        for part in range(n_head):
            shift = mod_refs[part][0, pl.ds(ids[step], 1), :]
            scale = mod_refs[part][1, pl.ds(ids[step], 1), :]
            hidden = x_refs[part][step].astype(F32)
            a = (hidden - mean) * inv * (1.0 + scale) + shift
            a_ref[part, step * rows : (step + 1) * rows, :] = a.astype(BF16)
    cos, sin = cos_ref[...], sin_ref[...]
    for slot in range(3):
        total = jnp.zeros((STEPS * rows, cols), F32)
        for part in range(n_head):
            start = pl.multiple_of((head[0] ^ part) * feats, feats)
            total += jnp.dot(
                a_ref[part], w_ref[slot, pl.ds(start, feats), :], preferred_element_type=F32
            )
        for step in range(STEPS):
            for block in range(cols // DH):
                lanes = slice(block * DH, (block + 1) * DH)
                u = total[step * rows : (step + 1) * rows, lanes]
                if slot < 2:
                    u = u * cos + pltpu.roll(u, DH // 2, 1) * sin
                u = u.astype(BF16)
                if slot == 0:
                    q_ref[step, :, lanes] = u
                else:
                    (kv0_ref, kv1_ref)[step][slot - 1, :, lanes] = u


def split3(values):
    high = values.astype(BF16).astype(F32)
    middle = (values - high).astype(BF16).astype(F32)
    return [high, middle, values - high - middle]


def attend_kernel(line, *refs):
    q_refs, refs = refs[:PLANE], refs[PLANE:]
    kv1_ref, kv0_refs, stale_refs = refs[0], refs[1 : 1 + line], refs[1 + line : 1 + 2 * line]
    own_out, peer_outs = refs[1 + 2 * line], refs[2 + 2 * line :]
    rows, cols = q_refs[0].shape[1:]
    heads = cols // DH
    for step in range(STEPS):
        before = (stale_refs, kv0_refs)[step]
        mine = (kv0_refs[0], kv1_ref)[step]
        for own in (True, False):
            queries = q_refs[:1] if own else q_refs[1:]
            keys = (mine if own else before[0], *before[1:])
            lane = lax.broadcasted_iota(jnp.int32, (rows * len(queries), DH), 1)
            stats = jnp.zeros((rows * len(queries), DH), F32)
            mixed = []
            for block in range(heads):
                lanes = slice(block * DH, (block + 1) * DH)
                scores = lax.dot_general(
                    jnp.concatenate([ref[step, :, lanes] for ref in queries], axis=0),
                    jnp.concatenate([ref[0, :, lanes] for ref in keys], axis=0),
                    NT,
                    preferred_element_type=F32,
                ) * (1.0 / math.sqrt(DH))
                top = jnp.max(scores, axis=1, keepdims=True)
                weights = jnp.exp(scores - top)
                totals = jnp.sum(weights, axis=1, keepdims=True)
                values = jnp.concatenate([ref[1, :, lanes] for ref in keys], axis=0)
                mixed.append(
                    jnp.dot(weights.astype(BF16), values, preferred_element_type=F32) / totals
                )
                for place, piece in enumerate(split3(top) + split3(totals)):
                    stats = jnp.where(lane == block * 8 + place, piece, stats)
            packed = jnp.concatenate([*mixed, stats], axis=1)
            spot = slice(step * rows, (step + 1) * rows)
            if own:
                own_out[spot, :] = packed
            else:
                for number, ref in enumerate(peer_outs):
                    ref[spot, :] = packed[number * rows : (number + 1) * rows].astype(BF16)


def merge_kernel(*refs):
    parts, o_ref = [ref[...].astype(F32) for ref in refs[:-1]], refs[-1]
    cols = o_ref.shape[1]
    for block in range(cols // DH):
        place = cols + block * 8
        tops = [jnp.sum(p[:, place : place + 3], axis=1, keepdims=True) for p in parts]
        sums = [jnp.sum(p[:, place + 3 : place + 6], axis=1, keepdims=True) for p in parts]
        best = functools.reduce(jnp.maximum, tops)
        scales = [s * jnp.exp(t - best) for s, t in zip(sums, tops)]
        lanes = slice(block * DH, (block + 1) * DH)
        mixed = sum(s * p[:, lanes] for s, p in zip(scales, parts))
        o_ref[:, lanes] = (mixed / sum(scales)).astype(BF16)


def out_kernel(n_head, n_patch, ids, patch, head, *refs):
    o_refs, refs = refs[: 2 * n_head], refs[2 * n_head :]
    mod_ref, w_refs = refs[0], refs[1 : 1 + PLANE]
    own_out, mate_out, o_all, sums = refs[1 + PLANE :]
    rows = o_refs[0].shape[0]
    piece = w_refs[0].shape[1]
    per_head = n_patch // n_head
    for part in range(n_head):
        for mate in range(2):
            spot = slice(mate * rows, (mate + 1) * rows)
            o_all[head[0] ^ part, spot, :] = o_refs[2 * part + mate][...]
    for near in range(PLANE):
        total = jnp.zeros((2 * rows, piece), F32)
        for part in range(n_head):
            o = o_all[(patch[0] // per_head) ^ part]
            total += lax.dot_general(o, w_refs[near][part], NT, preferred_element_type=F32)
        sums[(patch[0] % PLANE) ^ near] = total
    out = jnp.concatenate([sums[c] for c in range(PLANE)], axis=1)
    second = (patch[0] // PLANE) % 2 == 1
    for step in range(STEPS):
        gate = mod_ref[2, pl.ds(ids[step], 1), :]
        gate = jnp.where(second, gate[:, PLANE * piece :], gate[:, : PLANE * piece])
        each = rows // STEPS
        for mate, ref in enumerate((own_out, mate_out)):
            start = mate * rows + step * each
            ref[step] = (gate * out[start : start + each]).astype(BF16)


def call(kernel, shapes, ins, scratch=(), flops=0, size=0, limit=16):
    return pl.pallas_call(
        kernel,
        out_shape=shapes,
        in_specs=ins,
        out_specs=jax.tree.map(lambda _: VMEM, shapes),
        scratch_shapes=scratch,
        compiler_params=pltpu.CompilerParams(vmem_limit_bytes=limit * MIB),
        cost_estimate=pl.CostEstimate(flops=flops, bytes_accessed=size, transcendentals=0),
    )


def body(n_patch, n_head, inputs, stale_kv, w_qkv, w_out, mod_table, step_ids, slab_order):
    rows, feats = inputs.shape[1:]
    cols = w_qkv.shape[2]
    piece = w_out.shape[1]
    line = n_patch // PLANE
    per_head = n_patch // n_head
    patch = lax.axis_index("patch").astype(jnp.int32)
    head = lax.axis_index("head").astype(jnp.int32)
    shaped = jax.ShapeDtypeStruct

    x_parts = [swap(inputs, "head", n_head, k) for k in range(1, n_head)]
    mod_parts = [swap(mod_table, "head", n_head, k) for k in range(1, n_head)]
    first = (jnp.transpose(w_qkv, (1, 0, 2)), inputs, mod_table, stale_kv, w_out.T)
    w, x_own, mod_own, stale, w_mine = call(
        load_kernel,
        tuple(shaped(v.shape, v.dtype) for v in first),
        [ANY] * len(first),
        [pltpu.SemaphoreType.DMA((len(first),))],
        size=2 * w_qkv.size,
        limit=50,
    )(*first)
    x_parts = [x_own] + x_parts
    mod_parts = [jnp.transpose(part, (1, 0, 2)) for part in [mod_own] + mod_parts]

    stale_line = [stale] + [swap(stale, "patch", n_patch, PLANE * k) for k in range(1, line)]
    w_quad = jnp.stack(
        [
            lax.ppermute(
                w_mine,
                ("patch", "head"),
                [
                    ((hi * per_head + lo) * n_head + h, ((h ^ k) * per_head + lo) * n_head + hi)
                    for hi in range(n_head)
                    for lo in range(per_head)
                    for h in range(n_head)
                ],
            )
            for k in range(n_head)
        ]
    )
    w_quads = [w_quad] + [swap(w_quad, "patch", n_patch, k) for k in range(1, PLANE)]

    positions = slab_order[0] * rows + jnp.arange(rows, dtype=jnp.int32)
    cos, sin = angle_tables(positions)
    kv_shape = shaped((2, rows, cols), BF16)
    q, kv0, kv1 = call(
        functools.partial(qkv_kernel, n_head),
        (shaped((STEPS, rows, cols), BF16), kv_shape, kv_shape),
        [SMEM] * 2 + [VMEM] * (2 * n_head + 3),
        [pltpu.VMEM((n_head, STEPS * rows, feats), BF16)],
        2 * STEPS * rows * w_qkv.size,
        2 * w_qkv.size,
    )(step_ids, head[None], *x_parts, *mod_parts, w, cos, sin)

    kv0_line = [kv0] + [swap(kv0, "patch", n_patch, PLANE * k) for k in range(1, line)]
    q_plane = [q] + [swap(q, "patch", n_patch, k) for k in range(1, PLANE)]
    packed = (STEPS * rows, cols + DH)
    own, *peers = call(
        functools.partial(attend_kernel, line),
        (shaped(packed, F32),) + (shaped(packed, BF16),) * (PLANE - 1),
        [VMEM] * (PLANE + 1 + 2 * line),
        flops=8 * STEPS * rows * n_patch * rows * cols,
    )(*q_plane, kv1, *kv0_line, *stale_line)
    peers = [swap(peer, "patch", n_patch, k + 1) for k, peer in enumerate(peers)]
    o = call(merge_kernel, shaped((STEPS * rows, cols), BF16), [VMEM] * PLANE)(own, *peers)

    o_parts = []
    for k in range(n_head):
        for mate in range(2):
            pairs = [
                (p * n_head + h, (p ^ (PLANE * mate)) * n_head + (h ^ k))
                for p in range(n_patch)
                for h in range(n_head)
            ]
            o_parts.append(lax.ppermute(o, ("patch", "head"), pairs) if k or mate else o)
    half = shaped((STEPS, rows, PLANE * piece), BF16)
    out_own, out_mate = call(
        functools.partial(out_kernel, n_head, n_patch),
        (half, half),
        [SMEM] * 3 + [VMEM] * (2 * n_head + 1 + PLANE),
        [
            pltpu.VMEM((n_head, 2 * STEPS * rows, cols), BF16),
            pltpu.VMEM((PLANE, 2 * STEPS * rows, piece), F32),
        ],
        2 * STEPS * rows * n_patch * w_out.size,
        n_patch * w_out.size,
    )(step_ids, patch[None], head[None], *o_parts, mod_parts[0], *w_quads)
    out_back = swap(out_mate, "patch", n_patch, PLANE)
    second = (patch // PLANE) % 2 == 1
    return jnp.concatenate(
        [jnp.where(second, out_back, out_own), jnp.where(second, out_own, out_back)], axis=2
    )


def solution(mesh):
    in_specs = (
        P(None, "patch", "head"),
        P(None, "patch", "head"),
        P(None, None, "head"),
        P("head", "patch"),
        P(None, None, "head"),
        P(),
        P("patch"),
    )
    run = functools.partial(body, mesh.shape["patch"], mesh.shape["head"])
    return jax.shard_map(
        run, mesh=mesh, in_specs=in_specs, out_specs=P(None, "patch", "head"), check_vma=False
    )
```

time: 67.3 us -> 64.9 us (0.964)
  waiting for transfers between devices: 24.8 us -> 16.4 us
  Pallas kernels: 4.89 us -> 10.3 us
  local copies, waits for them, and re-layouts: 4.81 us -> 5.87 us
    ppermute x22 -> x18, waiting for transfers between devices: 24.8 us -> 14.4 us  [swap(): return lax.ppermute(values, axis, [(i, i ^ bit) for i in range(count)])]
    ppermute x22 -> x18, starting transfers between devices: 29 us -> 21.9 us  [swap(): return lax.ppermute(values, axis, [(i, i ^ bit) for i in range(count)])]
    ppermute x1 -> x5, starting transfers between devices: 1.54 us -> 8.2 us  [the longest x2 6.01 us: body(): lax.ppermute(w_mine, ('patch', 'head'), [((hi * per_head + lo) * n_head +...]
    pallas_call x4 -> x5, Pallas kernels: 4.89 us -> 10.3 us  [the longest x1 4.53 us: body(): call(load_kernel, tuple((shaped(v.shape, v.dtype) for v in first)), [ANY]...]
    ppermute x1 -> x5, waiting for transfers between devices: 0.01 us -> 1.95 us  [the longest x3 1.95 us: body(): lax.ppermute(o, ('patch', 'head'), pairs)]
    unnamed x12 -> x11, local copies, waits for them, and re-layouts: 4.81 us -> 5.84 us
    another operation x3 -> x1, other arithmetic: 0.85 us -> 0.02 us  [body(): jnp.stack([lax.ppermute(w_mine, ('patch', 'head'), [((hi * per_head + lo)...]
    concatenate x0 -> x1, other arithmetic: none -> 0.69 us  [body(): jnp.concatenate([jnp.where(second, out_back, out_own), jnp.where(second,...]
  transfers between devices with their start and end apart: 23 -> 23, of which waited for: 7 -> 7; matrix products, arithmetic and copies ran while one was open for 2% -> 2% of each run, Pallas kernels for 4% -> 14%
where the time goes in v2:
time: 64.9 us; the launch traced here: 64.5 us
  starting transfers between devices  30.1 us (46%)
  waiting for transfers between devices  16.4 us (25%)
  Pallas kernels  10.3 us (16%)
  local copies, waits for them, and re-layouts  5.87 us (9%)
  other arithmetic  0.96 us (1%)
  between operations  0.78 us (1%)
    ppermute x18, starting transfers between devices, swap(): return lax.ppermute(values, axis, [(i, i ^ bit) for i in range(count)])  21.9 us
    ppermute x18, waiting for transfers between devices, swap(): return lax.ppermute(values, axis, [(i, i ^ bit) for i in range(count)])  14.4 us
    ppermute x2, starting transfers between devices, body(): lax.ppermute(w_mine, ('patch', 'head'), [((hi * per_head + lo) * n_head +...  6.01 us
    unnamed x11, local copies, waits for them, and re-layouts  5.84 us
    pallas_call x1, Pallas kernels, body(): call(load_kernel, tuple((shaped(v.shape, v.dtype) for v in first)), [ANY]...  4.53 us
    ppermute x3, starting transfers between devices, body(): lax.ppermute(o, ('patch', 'head'), pairs)  2.19 us
    pallas_call x1, Pallas kernels, body(): call(functools.partial(attend_kernel, line), (shaped(packed, F32),) + (sh...  2.03 us
    ppermute x3, waiting for transfers between devices, body(): lax.ppermute(o, ('patch', 'head'), pairs)  1.95 us
  transfers between devices with their start and end apart: 23, of which 7 were waited for; matrix products, arithmetic and copies ran while one was open for 2% of the time, Pallas kernels for 14%

profile of v2, /device:TPU:0, one launch (start us, length us, event | category | flops | bytes accessed | tf_op | source)
XLA Modules:
  0.0 64.5 jit_solution(7420459755744551842)
XLA Ops:
  0.0 0.5 collective-permute-start
  0.5 0.1 collective-permute-start.1
  0.5 0.9 %copy.8.refs_2_ = f32[4,3,1536]{2,1,0:T(4,128)S(1)} copy(f32[4,3,1536]{2,0,1:T(4,128)} %param.11) | data formatting | bytes 147456 | tf_op args[4]
  1.4 0.0 copy-start.1
  1.5 0.9 %copy-done.1 = bf16[2,32,1536]{2,1,0:T(8,128)(2,1)S(1)} copy-done((bf16[2,32,1536]{2,1,0:T(8,128)(2,1)S(1)}, bf16[2,32,1536]{2,1,0:T(8,128)(2,1)}, u32[]{:S(2)}) %copy-start.1) | copy-done | bytes 196632
  2.4 0.9 %copy-done.2 = bf16[256,192]{0,1:T(8,128)(2,1)S(1)} copy-done((bf16[256,192]{0,1:T(8,128)(2,1)S(1)}, bf16[256,192]{0,1:T(8,128)(2,1)}, u32[]{:S(2)}) %copy-start.2) | copy-done | bytes 98328
  3.3 0.8 %copy-done.3 = bf16[2,32,256]{2,1,0:T(8,128)(2,1)S(1)} copy-done((bf16[2,32,256]{2,1,0:T(8,128)(2,1)S(1)}, bf16[2,32,256]{2,1,0:T(8,128)(2,1)}, u32[]{:S(2)}) %copy-start.3) | copy-done | bytes 32792
  4.0 4.5 %shard_map.73 = (bf16[3,3072,256]{2,1,0:T(8,128)(2,1)}, bf16[2,32,1536]{2,1,0:T(8,128)(2,1)S(1)}, f32[4,3,1536]{2,1,0:T(4,128)S(1)}, bf16[2,32,256]{2,1,0:T(8,128)(2,1)S(1)}, bf16[192,256]{1,0:T(8,128)(2,1)S(1)}) custom-call(bf16[3,3072,256]{2,1,0:T(8,128)(2,1)} %bitcast.15, bf16[2,32,1536]{2,1,0:T(8,128)(2,1)S(1)} %copy-done.1, ...), custom_call_target="tpu_custom_call" | custom-call | bytes 4718592 | tf_op jit(solution)/shard_map/pallas_call | solution.py:201
  8.6 0.7 %collective-permute-start.17 = (bf16[192,256]{1,0:T(8,128)(2,1)S(1)}, bf16[192,256]{1,0:T(8,128)(2,1)S(1)}, u32[]{:S(2)}, u32[]{:S(2)}) collective-permute-start(bf16[192,256]{1,0:T(8,128)(2,1)S(1)} %get-tuple-element.30), channel_id=1, source_target_pairs={{0,0},{1,16},{2,2},{3,18},{4,4},{5,20},{6,6},{7,22},{8,8},{9,24},{... | collective-permute-start | bytes 294920 | tf_op jit(solution)/shard_map/ppermute | solution.py:215
  9.2 5.3 %collective-permute-start.18 = (bf16[192,256]{1,0:T(8,128)(2,1)S(1)}, bf16[192,256]{1,0:T(8,128)(2,1)S(1)}, u32[]{:S(2)}, u32[]{:S(2)}) collective-permute-start(bf16[192,256]{1,0:T(8,128)(2,1)S(1)} %get-tuple-element.30), channel_id=1, source_target_pairs={{0,16},{1,0},{2,18},{3,2},{4,20},{5,4},{6,22},{7,6},{8,24},{9,8},{... | collective-permute-start | bytes 294920 | tf_op jit(solution)/shard_map/ppermute | solution.py:215
  14.6 1.1 %collective-permute-start.10 = (bf16[2,32,256]{2,1,0:T(8,128)(2,1)S(1)}, bf16[2,32,256]{2,1,0:T(8,128)(2,1)S(1)}, u32[]{:S(2)}, u32[]{:S(2)}) collective-permute-start(bf16[2,32,256]{2,1,0:T(8,128)(2,1)S(1)} %get-tuple-element.25.refs_9_), channel_id=1, source_target_pairs={{0,24},{2,26},{4,28},{6,30},{8,16},{10,18},{12,20},{14,22},{16,8},... | collective-permute-start | bytes 98312 | tf_op jit(solution)/shard_map/ppermute | solution.py:31
  16.4 0.1 fusion
  16.5 0.1 pad_maximum_fusion.2
  16.6 0.0 collective-permute-done.1
  16.6 0.6 collective-permute-start.8
  17.2 0.0 collective-permute-done.refs_1_
  17.2 2.8 %collective-permute-start.9 = (bf16[2,32,256]{2,1,0:T(8,128)(2,1)S(1)}, bf16[2,32,256]{2,1,0:T(8,128)(2,1)S(1)}, u32[]{:S(2)}, u32[]{:S(2)}) collective-permute-start(bf16[2,32,256]{2,1,0:T(8,128)(2,1)S(1)} %get-tuple-element.25.refs_9_), channel_id=1, source_target_pairs={{0,16},{2,18},{4,20},{6,22},{8,24},{10,26},{12,28},{14,30},{16,0},... | collective-permute-start | bytes 98312 | tf_op jit(solution)/shard_map/ppermute | solution.py:31
  20.0 2.3 %copy-done = bf16[3,3072,256]{2,1,0:T(8,128)(2,1)S(1)} copy-done((bf16[3,3072,256]{2,1,0:T(8,128)(2,1)S(1)}, bf16[3,3072,256]{2,1,0:T(8,128)(2,1)}, u32[]{:S(2)}) %copy-start) | copy-done | bytes 4718616
  22.3 1.7 %shard_map.74 = (bf16[2,32,256]{2,1,0:T(8,128)(2,1)S(1)}, bf16[2,32,256]{2,1,0:T(8,128)(2,1)S(1)}, bf16[2,32,256]{2,1,0:T(8,128)(2,1)S(1)}) custom-call(s32[2]{0:T(128)S(1)} %copy-done.4, s32[1]{0:T(128)} %bitcast.1.head, bf16[2,32,1536]{2,1,0:T(8,128)(2,1)S(1)} %get-tuple-element.19.refs_0_, bf16[2,32,1536]{2,1,0:T(8,128)(2,1)S(1)} %collective-permute-done.refs_1_, ...), custom_call_target="tpu_custom_call" | custom-call | flops 301989888 | bytes 4718592 | tf_op jit(solution)/shard_map/pallas_call | solution.py:233
  24.0 0.0 collective-permute-done.17
  24.0 1.6 %collective-permute-start.2 = (bf16[2,32,256]{2,1,0:T(8,128)(2,1)S(1)}, bf16[2,32,256]{2,1,0:T(8,128)(2,1)S(1)}, u32[]{:S(2)}, u32[]{:S(2)}) collective-permute-start(bf16[2,32,256]{2,1,0:T(8,128)(2,1)S(1)} %get-tuple-element.22.refs_0_), channel_id=1, source_target_pairs={{0,2},{2,0},{4,6},{6,4},{8,10},{10,8},{12,14},{14,12},{16,18},{18,... | collective-permute-start | bytes 98312 | tf_op jit(solution)/shard_map/ppermute | solution.py:31
  25.6 1.5 %collective-permute-start.3 = (bf16[2,32,256]{2,1,0:T(8,128)(2,1)S(1)}, bf16[2,32,256]{2,1,0:T(8,128)(2,1)S(1)}, u32[]{:S(2)}, u32[]{:S(2)}) collective-permute-start(bf16[2,32,256]{2,1,0:T(8,128)(2,1)S(1)} %get-tuple-element.22.refs_0_), channel_id=1, source_target_pairs={{0,4},{2,6},{4,0},{6,2},{8,12},{10,14},{12,8},{14,10},{16,20},{18,... | collective-permute-start | bytes 98312 | tf_op jit(solution)/shard_map/ppermute | solution.py:31
  27.1 0.0 collective-permute-done.10.refs_12_
  27.1 0.6 collective-permute-start.19
  27.7 1.4 %collective-permute-start.4 = (bf16[2,32,256]{2,1,0:T(8,128)(2,1)S(1)}, bf16[2,32,256]{2,1,0:T(8,128)(2,1)S(1)}, u32[]{:S(2)}, u32[]{:S(2)}) collective-permute-start(bf16[2,32,256]{2,1,0:T(8,128)(2,1)S(1)} %get-tuple-element.22.refs_0_), channel_id=1, source_target_pairs={{0,6},{2,4},{4,2},{6,0},{8,14},{10,12},{12,10},{14,8},{16,22},{18,... | collective-permute-start | bytes 98312 | tf_op jit(solution)/shard_map/ppermute | solution.py:31
  29.2 0.7 %collective-permute-start.5 = (bf16[2,32,256]{2,1,0:T(8,128)(2,1)S(1)}, bf16[2,32,256]{2,1,0:T(8,128)(2,1)S(1)}, u32[]{:S(2)}, u32[]{:S(2)}) collective-permute-start(bf16[2,32,256]{2,1,0:T(8,128)(2,1)S(1)} %get-tuple-element.24.refs_5_), channel_id=1, source_target_pairs={{0,8},{2,10},{4,12},{6,14},{8,0},{10,2},{12,4},{14,6},{16,24},{18,... | collective-permute-start | bytes 98312 | tf_op jit(solution)/shard_map/ppermute | solution.py:31
  29.9 1.5 %collective-permute-start.20 = (bf16[2,192,256]{2,1,0:T(8,128)(2,1)S(1)}, bf16[2,192,256]{2,1,0:T(8,128)(2,1)S(1)}, u32[]{:S(2)}, u32[]{:S(2)}) collective-permute-start(bf16[2,192,256]{2,1,0:T(8,128)(2,1)S(1)} %pad_maximum_fusion.refs_5_), channel_id=1, source_target_pairs={{0,4},{2,6},{4,0},{6,2},{8,12},{10,14},{12,8},{14,10},{16,20},{18,... | collective-permute-start | bytes 589832 | tf_op jit(solution)/shard_map/ppermute | solution.py:31
  31.4 0.5 collective-permute-start.21
  31.9 2.5 %collective-permute-done.4.refs_3_ = bf16[2,32,256]{2,1,0:T(8,128)(2,1)S(1)} collective-permute-done((bf16[2,32,256]{2,1,0:T(8,128)(2,1)S(1)}, bf16[2,32,256]{2,1,0:T(8,128)(2,1)S(1)}, u32[]{:S(2)}, u32[]{:S(2)}) %collective-permute-start.4) | collective-permute-done | bytes 32800 | tf_op jit(solution)/shard_map/ppermute | solution.py:31
  34.3 1.3 %collective-permute-start.6 = (bf16[2,32,256]{2,1,0:T(8,128)(2,1)S(1)}, bf16[2,32,256]{2,1,0:T(8,128)(2,1)S(1)}, u32[]{:S(2)}, u32[]{:S(2)}) collective-permute-start(bf16[2,32,256]{2,1,0:T(8,128)(2,1)S(1)} %get-tuple-element.24.refs_5_), channel_id=1, source_target_pairs={{0,16},{2,18},{4,20},{6,22},{8,24},{10,26},{12,28},{14,30},{16,0},... | collective-permute-start | bytes 98312 | tf_op jit(solution)/shard_map/ppermute | solution.py:31
  35.7 2.7 %collective-permute-start.7 = (bf16[2,32,256]{2,1,0:T(8,128)(2,1)S(1)}, bf16[2,32,256]{2,1,0:T(8,128)(2,1)S(1)}, u32[]{:S(2)}, u32[]{:S(2)}) collective-permute-start(bf16[2,32,256]{2,1,0:T(8,128)(2,1)S(1)} %get-tuple-element.24.refs_5_), channel_id=1, source_target_pairs={{0,24},{2,26},{4,28},{6,30},{8,16},{10,18},{12,20},{14,22},{16,8},... | collective-permute-start | bytes 98312 | tf_op jit(solution)/shard_map/ppermute | solution.py:31
  38.4 0.9 %collective-permute-done.6.refs_7_ = bf16[2,32,256]{2,1,0:T(8,128)(2,1)S(1)} collective-permute-done((bf16[2,32,256]{2,1,0:T(8,128)(2,1)S(1)}, bf16[2,32,256]{2,1,0:T(8,128)(2,1)S(1)}, u32[]{:S(2)}, u32[]{:S(2)}) %collective-permute-start.6) | collective-permute-done | bytes 32800 | tf_op jit(solution)/shard_map/ppermute | solution.py:31
  39.3 2.1 %collective-permute-done.7.refs_8_ = bf16[2,32,256]{2,1,0:T(8,128)(2,1)S(1)} collective-permute-done((bf16[2,32,256]{2,1,0:T(8,128)(2,1)S(1)}, bf16[2,32,256]{2,1,0:T(8,128)(2,1)S(1)}, u32[]{:S(2)}, u32[]{:S(2)}) %collective-permute-start.7) | collective-permute-done | bytes 32800 | tf_op jit(solution)/shard_map/ppermute | solution.py:31
  41.4 2.0 %shard_map.75 = (f32[64,384]{1,0:T(8,128)S(1)}, bf16[64,384]{1,0:T(8,128)(2,1)S(1)}, bf16[64,384]{1,0:T(8,128)(2,1)S(1)}, bf16[64,384]{1,0:T(8,128)(2,1)S(1)}) custom-call(bf16[2,32,256]{2,1,0:T(8,128)(2,1)S(1)} %get-tuple-element.22.refs_0_, bf16[2,32,256]{2,1,0:T(8,128)(2,1)S(1)} %collective-permute-done.2.refs_1_, ...), custom_call_target="tpu_custom_call" | custom-call | flops 67108864 | tf_op jit(solution)/shard_map/pallas_call | solution.py:245
  43.4 0.6 collective-permute-start.11
  44.0 1.6 %collective-permute-start.12 = (bf16[64,384]{1,0:T(8,128)(2,1)S(1)}, bf16[64,384]{1,0:T(8,128)(2,1)S(1)}, u32[]{:S(2)}, u32[]{:S(2)}) collective-permute-start(bf16[64,384]{1,0:T(8,128)(2,1)S(1)} %get-tuple-element.28), channel_id=1, source_target_pairs={{0,4},{2,6},{4,0},{6,2},{8,12},{10,14},{12,8},{14,10},{16,20},{18,... | collective-permute-start | bytes 147464 | tf_op jit(solution)/shard_map/ppermute | solution.py:31
  45.6 2.0 %collective-permute-done.11.refs_1_ = bf16[64,384]{1,0:T(8,128)(2,1)S(1)} collective-permute-done((bf16[64,384]{1,0:T(8,128)(2,1)S(1)}, bf16[64,384]{1,0:T(8,128)(2,1)S(1)}, u32[]{:S(2)}, u32[]{:S(2)}) %collective-permute-start.11) | collective-permute-done | bytes 49184 | tf_op jit(solution)/shard_map/ppermute | solution.py:31
  47.6 1.6 %collective-permute-start.13 = (bf16[64,384]{1,0:T(8,128)(2,1)S(1)}, bf16[64,384]{1,0:T(8,128)(2,1)S(1)}, u32[]{:S(2)}, u32[]{:S(2)}) collective-permute-start(bf16[64,384]{1,0:T(8,128)(2,1)S(1)} %get-tuple-element.29), channel_id=1, source_target_pairs={{0,6},{2,4},{4,2},{6,0},{8,14},{10,12},{12,10},{14,8},{16,22},{18,... | collective-permute-start | bytes 147464 | tf_op jit(solution)/shard_map/ppermute | solution.py:31
  49.2 3.3 %collective-permute-done.13.refs_3_ = bf16[64,384]{1,0:T(8,128)(2,1)S(1)} collective-permute-done((bf16[64,384]{1,0:T(8,128)(2,1)S(1)}, bf16[64,384]{1,0:T(8,128)(2,1)S(1)}, u32[]{:S(2)}, u32[]{:S(2)}) %collective-permute-start.13) | collective-permute-done | bytes 49184 | tf_op jit(solution)/shard_map/ppermute | solution.py:31
  52.6 1.0 %shard_map.76.refs_0_ = bf16[64,256]{1,0:T(8,128)(2,1)S(1)} custom-call(f32[64,384]{1,0:T(8,128)S(1)} %get-tuple-element.26.refs_0_, bf16[64,384]{1,0:T(8,128)(2,1)S(1)} %collective-permute-done.11.refs_1_, bf16[64,384]{1,0:T(8,128)(2,1)S(1)} %collective-permute-done.12.refs_2_, bf16[64,384]{1,0:T(8,128)(2,1)S(1)} %collective-permute-done.13.refs_3_), custom_call_target="tpu_custom_call" | custom-call | tf_op jit(solution)/shard_map/pallas_call | solution.py:252
  53.6 0.1 collective-permute-start.14
  53.7 0.1 collective-permute-start.15
  53.8 2.0 %collective-permute-start.16 = (bf16[64,256]{1,0:T(8,128)(2,1)S(1)}, bf16[64,256]{1,0:T(8,128)(2,1)S(1)}, u32[]{:S(2)}, u32[]{:S(2)}) collective-permute-start(bf16[64,256]{1,0:T(8,128)(2,1)S(1)} %shard_map.76.refs_0_), channel_id=1, source_target_pairs={{0,9},{1,8},{2,11},{3,10},{4,13},{5,12},{6,15},{7,14},{8,1},{9,0},... | collective-permute-start | bytes 98312 | tf_op jit(solution)/shard_map/ppermute | solution.py:262
  55.8 1.9 %collective-permute-done.14.refs_1_ = bf16[64,256]{1,0:T(8,128)(2,1)S(1)} collective-permute-done((bf16[64,256]{1,0:T(8,128)(2,1)S(1)}, bf16[64,256]{1,0:T(8,128)(2,1)S(1)}, u32[]{:S(2)}, u32[]{:S(2)}) %collective-permute-start.14) | collective-permute-done | bytes 32800 | tf_op jit(solution)/shard_map/ppermute | solution.py:262
  57.8 1.1 %shard_map.77 = (bf16[2,32,768]{2,1,0:T(8,128)(2,1)S(1)}, bf16[2,32,768]{2,1,0:T(8,128)(2,1)S(1)}) custom-call(s32[2]{0:T(128)S(1)} %copy-done.4, s32[1]{0:T(128)} %bitcast.patch, s32[1]{0:T(128)} %bitcast.1.head, bf16[64,256]{1,0:T(8,128)(2,1)S(1)} %shard_map.76.refs_0_, bf16[64,256]{1,0:T(8,128)(2,1)S(1)} %collective-permute-done.14.refs_1_, ...), custom_call_target="tpu_custom_call" | custom-call | flops 100663296 | bytes 786432 | tf_op jit(solution)/shard_map/pallas_call | solution.py:264
  58.8 1.3 %collective-permute-start.22 = (bf16[2,32,768]{2,1,0:T(8,128)(2,1)S(1)}, bf16[2,32,768]{2,1,0:T(8,128)(2,1)S(1)}, u32[]{:S(2)}, u32[]{:S(2)}) collective-permute-start(bf16[2,32,768]{2,1,0:T(8,128)(2,1)S(1)} %get-tuple-element.31), channel_id=1, source_target_pairs={{0,8},{2,10},{4,12},{6,14},{8,0},{10,2},{12,4},{14,6},{16,24},{18,... | collective-permute-start | bytes 294920 | tf_op jit(solution)/shard_map/ppermute | solution.py:31
  60.2 3.6 %collective-permute-done.22 = bf16[2,32,768]{2,1,0:T(8,128)(2,1)S(1)} collective-permute-done((bf16[2,32,768]{2,1,0:T(8,128)(2,1)S(1)}, bf16[2,32,768]{2,1,0:T(8,128)(2,1)S(1)}, u32[]{:S(2)}, u32[]{:S(2)}) %collective-permute-start.22) | collective-permute-done | bytes 98336 | tf_op jit(solution)/shard_map/ppermute | solution.py:31
  63.8 0.7 %pad_maximum_fusion.1 = bf16[2,32,1536]{2,1,0:T(8,128)(2,1)} fusion(bf16[2,32,768]{2,1,0:T(8,128)(2,1)S(1)} %get-tuple-element.34, bf16[2,32,768]{2,1,0:T(8,128)(2,1)S(1)} %get-tuple-element.33), kind=kLoop, calls=%fused_computation.1 | loop fusion | flops 393216 | bytes 393216 | tf_op jit(solution)/shard_map/concatenate | solution.py:277
  (22 shorter events, 0.1 us)
Async XLA Ops:
  0.0 20.0 %copy-start.4 = (s32[2]{0:T(128)S(1)}, s32[2]{0:T(128)}, u32[]{:S(2)}) copy-start(s32[2]{0:T(128)} %ids.3) | copy-start | bytes 28
  0.0 17.2 %collective-permute-start = (bf16[2,32,1536]{2,1,0:T(8,128)(2,1)}, bf16[2,32,1536]{2,1,0:T(8,128)(2,1)S(1)}, u32[]{:S(2)}, u32[]{:S(2)}) collective-permute-start(bf16[2,32,1536]{2,1,0:T(8,128)(2,1)} %refs_1_.1), channel_id=1, source_target_pairs={{0,1},{1,0},{2,3},{3,2},{4,5},{5,4},{6,7},{7,6},{8,9},{9,8},{10,11... | collective-permute-start | bytes 589832 | tf_op jit(solution)/shard_map/ppermute | solution.py:31
  0.5 16.2 %collective-permute-start.1 = (f32[4,3,1536]{2,0,1:T(4,128)}, f32[4,3,1536]{2,0,1:T(4,128)S(1)}, u32[]{:S(2)}, u32[]{:S(2)}) collective-permute-start(f32[4,3,1536]{2,0,1:T(4,128)} %param.11), channel_id=1, source_target_pairs={{0,1},{1,0},{2,3},{3,2},{4,5},{5,4},{6,7},{7,6},{8,9},{9,8},{10,11... | collective-permute-start | bytes 221192 | tf_op jit(solution)/shard_map/ppermute | solution.py:31
  1.4 0.9 %copy-start.1 = (bf16[2,32,1536]{2,1,0:T(8,128)(2,1)S(1)}, bf16[2,32,1536]{2,1,0:T(8,128)(2,1)}, u32[]{:S(2)}) copy-start(bf16[2,32,1536]{2,1,0:T(8,128)(2,1)} %refs_1_.1) | copy-start | bytes 589828
  2.4 0.9 %copy-start.2 = (bf16[256,192]{0,1:T(8,128)(2,1)S(1)}, bf16[256,192]{0,1:T(8,128)(2,1)}, u32[]{:S(2)}) copy-start(bf16[256,192]{0,1:T(8,128)(2,1)} %param.10) | copy-start | bytes 294916
  3.3 0.8 %copy-start.3 = (bf16[2,32,256]{2,1,0:T(8,128)(2,1)S(1)}, bf16[2,32,256]{2,1,0:T(8,128)(2,1)}, u32[]{:S(2)}) copy-start(bf16[2,32,256]{2,1,0:T(8,128)(2,1)} %refs_3_.1) | copy-start | bytes 98308
  8.6 15.5 %collective-permute-start.17 = (bf16[192,256]{1,0:T(8,128)(2,1)S(1)}, bf16[192,256]{1,0:T(8,128)(2,1)S(1)}, u32[]{:S(2)}, u32[]{:S(2)}) collective-permute-start(bf16[192,256]{1,0:T(8,128)(2,1)S(1)} %get-tuple-element.30), channel_id=1, source_target_pairs={{0,0},{1,16},{2,2},{3,18},{4,4},{5,20},{6,6},{7,22},{8,8},{9,24},{... | collective-permute-start | bytes 294920 | tf_op jit(solution)/shard_map/ppermute | solution.py:215
  9.2 16.4 %collective-permute-start.18 = (bf16[192,256]{1,0:T(8,128)(2,1)S(1)}, bf16[192,256]{1,0:T(8,128)(2,1)S(1)}, u32[]{:S(2)}, u32[]{:S(2)}) collective-permute-start(bf16[192,256]{1,0:T(8,128)(2,1)S(1)} %get-tuple-element.30), channel_id=1, source_target_pairs={{0,16},{1,0},{2,18},{3,2},{4,20},{5,4},{6,22},{7,6},{8,24},{9,8},{... | collective-permute-start | bytes 294920 | tf_op jit(solution)/shard_map/ppermute | solution.py:215
  14.6 12.6 %collective-permute-start.10 = (bf16[2,32,256]{2,1,0:T(8,128)(2,1)S(1)}, bf16[2,32,256]{2,1,0:T(8,128)(2,1)S(1)}, u32[]{:S(2)}, u32[]{:S(2)}) collective-permute-start(bf16[2,32,256]{2,1,0:T(8,128)(2,1)S(1)} %get-tuple-element.25.refs_9_), channel_id=1, source_target_pairs={{0,24},{2,26},{4,28},{6,30},{8,16},{10,18},{12,20},{14,22},{16,8},... | collective-permute-start | bytes 98312 | tf_op jit(solution)/shard_map/ppermute | solution.py:31
  16.6 11.1 %collective-permute-start.8 = (bf16[2,32,256]{2,1,0:T(8,128)(2,1)S(1)}, bf16[2,32,256]{2,1,0:T(8,128)(2,1)S(1)}, u32[]{:S(2)}, u32[]{:S(2)}) collective-permute-start(bf16[2,32,256]{2,1,0:T(8,128)(2,1)S(1)} %get-tuple-element.25.refs_9_), channel_id=1, source_target_pairs={{0,8},{2,10},{4,12},{6,14},{8,0},{10,2},{12,4},{14,6},{16,24},{18,... | collective-permute-start | bytes 98312 | tf_op jit(solution)/shard_map/ppermute | solution.py:31
  17.2 12.0 %collective-permute-start.9 = (bf16[2,32,256]{2,1,0:T(8,128)(2,1)S(1)}, bf16[2,32,256]{2,1,0:T(8,128)(2,1)S(1)}, u32[]{:S(2)}, u32[]{:S(2)}) collective-permute-start(bf16[2,32,256]{2,1,0:T(8,128)(2,1)S(1)} %get-tuple-element.25.refs_9_), channel_id=1, source_target_pairs={{0,16},{2,18},{4,20},{6,22},{8,24},{10,26},{12,28},{14,30},{16,0},... | collective-permute-start | bytes 98312 | tf_op jit(solution)/shard_map/ppermute | solution.py:31
  20.0 2.3 %copy-start = (bf16[3,3072,256]{2,1,0:T(8,128)(2,1)S(1)}, bf16[3,3072,256]{2,1,0:T(8,128)(2,1)}, u32[]{:S(2)}) copy-start(bf16[3,3072,256]{2,1,0:T(8,128)(2,1)} %get-tuple-element.21.refs_4_) | copy-start | bytes 14155780
  24.0 5.8 %collective-permute-start.2 = (bf16[2,32,256]{2,1,0:T(8,128)(2,1)S(1)}, bf16[2,32,256]{2,1,0:T(8,128)(2,1)S(1)}, u32[]{:S(2)}, u32[]{:S(2)}) collective-permute-start(bf16[2,32,256]{2,1,0:T(8,128)(2,1)S(1)} %get-tuple-element.22.refs_0_), channel_id=1, source_target_pairs={{0,2},{2,0},{4,6},{6,4},{8,10},{10,8},{12,14},{14,12},{16,18},{18,... | collective-permute-start | bytes 98312 | tf_op jit(solution)/shard_map/ppermute | solution.py:31
  25.6 5.8 %collective-permute-start.3 = (bf16[2,32,256]{2,1,0:T(8,128)(2,1)S(1)}, bf16[2,32,256]{2,1,0:T(8,128)(2,1)S(1)}, u32[]{:S(2)}, u32[]{:S(2)}) collective-permute-start(bf16[2,32,256]{2,1,0:T(8,128)(2,1)S(1)} %get-tuple-element.22.refs_0_), channel_id=1, source_target_pairs={{0,4},{2,6},{4,0},{6,2},{8,12},{10,14},{12,8},{14,10},{16,20},{18,... | collective-permute-start | bytes 98312 | tf_op jit(solution)/shard_map/ppermute | solution.py:31
  27.1 26.6 %collective-permute-start.19 = (bf16[2,192,256]{2,1,0:T(8,128)(2,1)S(1)}, bf16[2,192,256]{2,1,0:T(8,128)(2,1)S(1)}, u32[]{:S(2)}, u32[]{:S(2)}) collective-permute-start(bf16[2,192,256]{2,1,0:T(8,128)(2,1)S(1)} %pad_maximum_fusion.refs_5_), channel_id=1, source_target_pairs={{0,2},{2,0},{4,6},{6,4},{8,10},{10,8},{12,14},{14,12},{16,18},{18,... | collective-permute-start | bytes 589832 | tf_op jit(solution)/shard_map/ppermute | solution.py:31
  27.7 6.6 %collective-permute-start.4 = (bf16[2,32,256]{2,1,0:T(8,128)(2,1)S(1)}, bf16[2,32,256]{2,1,0:T(8,128)(2,1)S(1)}, u32[]{:S(2)}, u32[]{:S(2)}) collective-permute-start(bf16[2,32,256]{2,1,0:T(8,128)(2,1)S(1)} %get-tuple-element.22.refs_0_), channel_id=1, source_target_pairs={{0,6},{2,4},{4,2},{6,0},{8,14},{10,12},{12,10},{14,8},{16,22},{18,... | collective-permute-start | bytes 98312 | tf_op jit(solution)/shard_map/ppermute | solution.py:31
  29.2 6.5 %collective-permute-start.5 = (bf16[2,32,256]{2,1,0:T(8,128)(2,1)S(1)}, bf16[2,32,256]{2,1,0:T(8,128)(2,1)S(1)}, u32[]{:S(2)}, u32[]{:S(2)}) collective-permute-start(bf16[2,32,256]{2,1,0:T(8,128)(2,1)S(1)} %get-tuple-element.24.refs_5_), channel_id=1, source_target_pairs={{0,8},{2,10},{4,12},{6,14},{8,0},{10,2},{12,4},{14,6},{16,24},{18,... | collective-permute-start | bytes 98312 | tf_op jit(solution)/shard_map/ppermute | solution.py:31
  29.9 25.9 %collective-permute-start.20 = (bf16[2,192,256]{2,1,0:T(8,128)(2,1)S(1)}, bf16[2,192,256]{2,1,0:T(8,128)(2,1)S(1)}, u32[]{:S(2)}, u32[]{:S(2)}) collective-permute-start(bf16[2,192,256]{2,1,0:T(8,128)(2,1)S(1)} %pad_maximum_fusion.refs_5_), channel_id=1, source_target_pairs={{0,4},{2,6},{4,0},{6,2},{8,12},{10,14},{12,8},{14,10},{16,20},{18,... | collective-permute-start | bytes 589832 | tf_op jit(solution)/shard_map/ppermute | solution.py:31
  31.4 24.4 %collective-permute-start.21 = (bf16[2,192,256]{2,1,0:T(8,128)(2,1)S(1)}, bf16[2,192,256]{2,1,0:T(8,128)(2,1)S(1)}, u32[]{:S(2)}, u32[]{:S(2)}) collective-permute-start(bf16[2,192,256]{2,1,0:T(8,128)(2,1)S(1)} %pad_maximum_fusion.refs_5_), channel_id=1, source_target_pairs={{0,6},{2,4},{4,2},{6,0},{8,14},{10,12},{12,10},{14,8},{16,22},{18,... | collective-permute-start | bytes 589832 | tf_op jit(solution)/shard_map/ppermute | solution.py:31
  34.3 5.0 %collective-permute-start.6 = (bf16[2,32,256]{2,1,0:T(8,128)(2,1)S(1)}, bf16[2,32,256]{2,1,0:T(8,128)(2,1)S(1)}, u32[]{:S(2)}, u32[]{:S(2)}) collective-permute-start(bf16[2,32,256]{2,1,0:T(8,128)(2,1)S(1)} %get-tuple-element.24.refs_5_), channel_id=1, source_target_pairs={{0,16},{2,18},{4,20},{6,22},{8,24},{10,26},{12,28},{14,30},{16,0},... | collective-permute-start | bytes 98312 | tf_op jit(solution)/shard_map/ppermute | solution.py:31
  35.7 5.7 %collective-permute-start.7 = (bf16[2,32,256]{2,1,0:T(8,128)(2,1)S(1)}, bf16[2,32,256]{2,1,0:T(8,128)(2,1)S(1)}, u32[]{:S(2)}, u32[]{:S(2)}) collective-permute-start(bf16[2,32,256]{2,1,0:T(8,128)(2,1)S(1)} %get-tuple-element.24.refs_5_), channel_id=1, source_target_pairs={{0,24},{2,26},{4,28},{6,30},{8,16},{10,18},{12,20},{14,22},{16,8},... | collective-permute-start | bytes 98312 | tf_op jit(solution)/shard_map/ppermute | solution.py:31
  43.4 4.2 %collective-permute-start.11 = (bf16[64,384]{1,0:T(8,128)(2,1)S(1)}, bf16[64,384]{1,0:T(8,128)(2,1)S(1)}, u32[]{:S(2)}, u32[]{:S(2)}) collective-permute-start(bf16[64,384]{1,0:T(8,128)(2,1)S(1)} %get-tuple-element.27), channel_id=1, source_target_pairs={{0,2},{2,0},{4,6},{6,4},{8,10},{10,8},{12,14},{14,12},{16,18},{18,... | collective-permute-start | bytes 147464 | tf_op jit(solution)/shard_map/ppermute | solution.py:31
  44.0 5.2 %collective-permute-start.12 = (bf16[64,384]{1,0:T(8,128)(2,1)S(1)}, bf16[64,384]{1,0:T(8,128)(2,1)S(1)}, u32[]{:S(2)}, u32[]{:S(2)}) collective-permute-start(bf16[64,384]{1,0:T(8,128)(2,1)S(1)} %get-tuple-element.28), channel_id=1, source_target_pairs={{0,4},{2,6},{4,0},{6,2},{8,12},{10,14},{12,8},{14,10},{16,20},{18,... | collective-permute-start | bytes 147464 | tf_op jit(solution)/shard_map/ppermute | solution.py:31
  47.6 5.0 %collective-permute-start.13 = (bf16[64,384]{1,0:T(8,128)(2,1)S(1)}, bf16[64,384]{1,0:T(8,128)(2,1)S(1)}, u32[]{:S(2)}, u32[]{:S(2)}) collective-permute-start(bf16[64,384]{1,0:T(8,128)(2,1)S(1)} %get-tuple-element.29), channel_id=1, source_target_pairs={{0,6},{2,4},{4,2},{6,0},{8,14},{10,12},{12,10},{14,8},{16,22},{18,... | collective-permute-start | bytes 147464 | tf_op jit(solution)/shard_map/ppermute | solution.py:31
  53.6 4.2 %collective-permute-start.14 = (bf16[64,256]{1,0:T(8,128)(2,1)S(1)}, bf16[64,256]{1,0:T(8,128)(2,1)S(1)}, u32[]{:S(2)}, u32[]{:S(2)}) collective-permute-start(bf16[64,256]{1,0:T(8,128)(2,1)S(1)} %shard_map.76.refs_0_), channel_id=1, source_target_pairs={{0,8},{1,9},{2,10},{3,11},{4,12},{5,13},{6,14},{7,15},{8,0},{9,1},... | collective-permute-start | bytes 98312 | tf_op jit(solution)/shard_map/ppermute | solution.py:262
  53.7 4.1 %collective-permute-start.15 = (bf16[64,256]{1,0:T(8,128)(2,1)S(1)}, bf16[64,256]{1,0:T(8,128)(2,1)S(1)}, u32[]{:S(2)}, u32[]{:S(2)}) collective-permute-start(bf16[64,256]{1,0:T(8,128)(2,1)S(1)} %shard_map.76.refs_0_), channel_id=1, source_target_pairs={{0,1},{1,0},{2,3},{3,2},{4,5},{5,4},{6,7},{7,6},{8,9},{9,8},{10,11... | collective-permute-start | bytes 98312 | tf_op jit(solution)/shard_map/ppermute | solution.py:262
  53.8 4.0 %collective-permute-start.16 = (bf16[64,256]{1,0:T(8,128)(2,1)S(1)}, bf16[64,256]{1,0:T(8,128)(2,1)S(1)}, u32[]{:S(2)}, u32[]{:S(2)}) collective-permute-start(bf16[64,256]{1,0:T(8,128)(2,1)S(1)} %shard_map.76.refs_0_), channel_id=1, source_target_pairs={{0,9},{1,8},{2,11},{3,10},{4,13},{5,12},{6,15},{7,14},{8,1},{9,0},... | collective-permute-start | bytes 98312 | tf_op jit(solution)/shard_map/ppermute | solution.py:262
  58.8 4.9 %collective-permute-start.22 = (bf16[2,32,768]{2,1,0:T(8,128)(2,1)S(1)}, bf16[2,32,768]{2,1,0:T(8,128)(2,1)S(1)}, u32[]{:S(2)}, u32[]{:S(2)}) collective-permute-start(bf16[2,32,768]{2,1,0:T(8,128)(2,1)S(1)} %get-tuple-element.31), channel_id=1, source_target_pairs={{0,8},{2,10},{4,12},{6,14},{8,0},{10,2},{12,4},{14,6},{16,24},{18,... | collective-permute-start | bytes 294920 | tf_op jit(solution)/shard_map/ppermute | solution.py:31

commit v3 on v2

--- a/solution.py
+++ b/solution.py
@@ -43,12 +43,15 @@
         copy.wait()
 
 
-def qkv_kernel(n_head, ids, head, *refs):
+def qkv_kernel(n_head, head, ids_ref, *refs):
     x_refs, mod_refs = refs[:n_head], refs[n_head : 2 * n_head]
-    w_ref, cos_ref, sin_ref, q_ref, kv0_ref, kv1_ref, a_ref = refs[2 * n_head :]
+    w_ref, cos_ref, sin_ref, q_ref, kv0_ref, kv1_ref, a_ref, ids, sem = refs[2 * n_head :]
+    copy = pltpu.make_async_copy(ids_ref, ids, sem)
+    copy.start()
     rows, feats = x_refs[0].shape[1:]
     width = n_head * feats
     cols = w_ref.shape[2]
+    stats = []
     for step in range(STEPS):
         total, square = 0.0, 0.0
         for x_ref in x_refs:
@@ -56,7 +59,10 @@
             total += jnp.sum(hidden, axis=1, keepdims=True)
             square += jnp.sum(hidden * hidden, axis=1, keepdims=True)
         mean = total / width
-        inv = lax.rsqrt(square / width - mean * mean + 1e-06)
+        stats.append((mean, lax.rsqrt(square / width - mean * mean + 1e-06)))
+    copy.wait()
+    for step in range(STEPS):
+        mean, inv = stats[step]
         for part in range(n_head):
             shift = mod_refs[part][0, pl.ds(ids[step], 1), :]
             scale = mod_refs[part][1, pl.ds(ids[step], 1), :]
@@ -79,9 +85,13 @@
                     u = u * cos + pltpu.roll(u, DH // 2, 1) * sin
                 u = u.astype(BF16)
                 if slot == 0:
-                    q_ref[step, :, lanes] = u
+                    for place in range(q_ref.shape[0]):
+                        q_ref[place, step, :, lanes] = u
+                elif step == 0:
+                    for place in range(kv0_ref.shape[0]):
+                        kv0_ref[place, slot - 1, :, lanes] = u
                 else:
-                    (kv0_ref, kv1_ref)[step][slot - 1, :, lanes] = u
+                    kv1_ref[slot - 1, :, lanes] = u
 
 
 def split3(values):
@@ -90,49 +100,44 @@
     return [high, middle, values - high - middle]
 
 
-def attend_kernel(line, *refs):
-    q_refs, refs = refs[:PLANE], refs[PLANE:]
-    kv1_ref, kv0_refs, stale_refs = refs[0], refs[1 : 1 + line], refs[1 + line : 1 + 2 * line]
-    own_out, peer_outs = refs[1 + 2 * line], refs[2 + 2 * line :]
-    rows, cols = q_refs[0].shape[1:]
-    heads = cols // DH
+def attend_kernel(patch, q_ref, kv1_ref, kv0_sent, kv0_ref, stale_ref, out_ref):
+    line = kv0_ref.shape[0]
+    rows, cols = q_ref.shape[2:]
+    near, far = patch[0] % PLANE, patch[0] // PLANE
+    shape = (PLANE * rows, line * rows + rows)
+    mine = lax.broadcasted_iota(jnp.int32, shape, 0) // rows == near
+    spot = lax.broadcasted_iota(jnp.int32, shape, 1) // rows
+    drop = jnp.where(mine, spot, line - spot) == jnp.where(mine, far, 0)
+    lane = lax.broadcasted_iota(jnp.int32, (PLANE * rows, DH), 1)
     for step in range(STEPS):
-        before = (stale_refs, kv0_refs)[step]
-        mine = (kv0_refs[0], kv1_ref)[step]
-        for own in (True, False):
-            queries = q_refs[:1] if own else q_refs[1:]
-            keys = (mine if own else before[0], *before[1:])
-            lane = lax.broadcasted_iota(jnp.int32, (rows * len(queries), DH), 1)
-            stats = jnp.zeros((rows * len(queries), DH), F32)
-            mixed = []
-            for block in range(heads):
-                lanes = slice(block * DH, (block + 1) * DH)
-                scores = lax.dot_general(
-                    jnp.concatenate([ref[step, :, lanes] for ref in queries], axis=0),
-                    jnp.concatenate([ref[0, :, lanes] for ref in keys], axis=0),
-                    NT,
-                    preferred_element_type=F32,
-                ) * (1.0 / math.sqrt(DH))
-                top = jnp.max(scores, axis=1, keepdims=True)
-                weights = jnp.exp(scores - top)
-                totals = jnp.sum(weights, axis=1, keepdims=True)
-                values = jnp.concatenate([ref[1, :, lanes] for ref in keys], axis=0)
-                mixed.append(
-                    jnp.dot(weights.astype(BF16), values, preferred_element_type=F32) / totals
-                )
-                for place, piece in enumerate(split3(top) + split3(totals)):
-                    stats = jnp.where(lane == block * 8 + place, piece, stats)
-            packed = jnp.concatenate([*mixed, stats], axis=1)
-            spot = slice(step * rows, (step + 1) * rows)
-            if own:
-                own_out[spot, :] = packed
-            else:
-                for number, ref in enumerate(peer_outs):
-                    ref[spot, :] = packed[number * rows : (number + 1) * rows].astype(BF16)
-
-
-def merge_kernel(*refs):
-    parts, o_ref = [ref[...].astype(F32) for ref in refs[:-1]], refs[-1]
+        before = (stale_ref, kv0_ref)[step]
+        fresh = (kv0_sent.at[0], kv1_ref)[step]
+        stats = jnp.zeros((PLANE * rows, DH), F32)
+        mixed = []
+        for block in range(cols // DH):
+            lanes = slice(block * DH, (block + 1) * DH)
+
+            def rows_of(kind):
+                old = before[:, kind, :, lanes].reshape(line * rows, DH)
+                return jnp.concatenate([old, fresh[kind, :, lanes]], axis=0)
+
+            queries = q_ref[:, step, :, lanes].reshape(PLANE * rows, DH)
+            scores = lax.dot_general(queries, rows_of(0), NT, preferred_element_type=F32)
+            scores = jnp.where(drop, -1e30, scores * (1.0 / math.sqrt(DH)))
+            top = jnp.max(scores, axis=1, keepdims=True)
+            weights = jnp.exp(scores - top)
+            totals = jnp.sum(weights, axis=1, keepdims=True)
+            mixed.append(
+                jnp.dot(weights.astype(BF16), rows_of(1), preferred_element_type=F32) / totals
+            )
+            for place, piece in enumerate(split3(top) + split3(totals)):
+                stats = jnp.where(lane == block * 8 + place, piece, stats)
+        packed = jnp.concatenate([*mixed, stats], axis=1).astype(BF16)
+        out_ref[:, step * rows : (step + 1) * rows, :] = packed.reshape(PLANE, rows, cols + DH)
+
+
+def merge_kernel(parts_ref, o_ref):
+    parts = [parts_ref[k].astype(F32) for k in range(PLANE)]
     cols = o_ref.shape[1]
     for block in range(cols // DH):
         place = cols + block * 8
@@ -173,6 +178,10 @@
             ref[step] = (gate * out[start : start + each]).astype(BF16)
 
 
+def in_hbm(values):
+    return pltpu.with_memory_space_constraint(values, pltpu.HBM)
+
+
 def call(kernel, shapes, ins, scratch=(), flops=0, size=0, limit=16):
     return pl.pallas_call(
         kernel,
@@ -197,23 +206,28 @@
 
     x_parts = [swap(inputs, "head", n_head, k) for k in range(1, n_head)]
     mod_parts = [swap(mod_table, "head", n_head, k) for k in range(1, n_head)]
-    first = (jnp.transpose(w_qkv, (1, 0, 2)), inputs, mod_table, stale_kv, w_out.T)
-    w, x_own, mod_own, stale, w_mine = call(
+    first = (jnp.transpose(w_qkv, (1, 0, 2)), inputs, jnp.transpose(mod_table, (1, 0, 2)))
+    w, x_own, mod_own = call(
         load_kernel,
-        tuple(shaped(v.shape, v.dtype) for v in first),
+        tuple(pltpu.VMEM(v.shape, v.dtype) for v in first),
         [ANY] * len(first),
         [pltpu.SemaphoreType.DMA((len(first),))],
         size=2 * w_qkv.size,
-        limit=50,
-    )(*first)
+    )(*map(in_hbm, first))
     x_parts = [x_own] + x_parts
-    mod_parts = [jnp.transpose(part, (1, 0, 2)) for part in [mod_own] + mod_parts]
-
-    stale_line = [stale] + [swap(stale, "patch", n_patch, PLANE * k) for k in range(1, line)]
+    mod_parts = [mod_own] + [jnp.transpose(part, (1, 0, 2)) for part in mod_parts]
+
+    lines = [[PLANE * i + j for i in range(line)] for j in range(PLANE)]
+    planes = [[PLANE * i + j for j in range(PLANE)] for i in range(line)]
+
+    def exchange(values, groups):
+        return lax.all_to_all(values, "patch", 0, 0, axis_index_groups=groups)
+
+    stale = exchange(jnp.broadcast_to(stale_kv[None], (line, *stale_kv.shape)), lines)
     w_quad = jnp.stack(
         [
             lax.ppermute(
-                w_mine,
+                w_out.T,
                 ("patch", "head"),
                 [
                     ((hi * per_head + lo) * n_head + h, ((h ^ k) * per_head + lo) * n_head + hi)
@@ -229,27 +243,30 @@
 
     positions = slab_order[0] * rows + jnp.arange(rows, dtype=jnp.int32)
     cos, sin = angle_tables(positions)
-    kv_shape = shaped((2, rows, cols), BF16)
+    kv_shape = (2, rows, cols)
     q, kv0, kv1 = call(
         functools.partial(qkv_kernel, n_head),
-        (shaped((STEPS, rows, cols), BF16), kv_shape, kv_shape),
-        [SMEM] * 2 + [VMEM] * (2 * n_head + 3),
-        [pltpu.VMEM((n_head, STEPS * rows, feats), BF16)],
+        (shaped((PLANE, *kv_shape), BF16), shaped((line, *kv_shape), BF16), shaped(kv_shape, BF16)),
+        [SMEM, ANY] + [VMEM] * (2 * n_head + 3),
+        [
+            pltpu.VMEM((n_head, STEPS * rows, feats), BF16),
+            pltpu.SMEM(step_ids.shape, jnp.int32),
+            pltpu.SemaphoreType.DMA,
+        ],
         2 * STEPS * rows * w_qkv.size,
         2 * w_qkv.size,
-    )(step_ids, head[None], *x_parts, *mod_parts, w, cos, sin)
-
-    kv0_line = [kv0] + [swap(kv0, "patch", n_patch, PLANE * k) for k in range(1, line)]
-    q_plane = [q] + [swap(q, "patch", n_patch, k) for k in range(1, PLANE)]
-    packed = (STEPS * rows, cols + DH)
-    own, *peers = call(
-        functools.partial(attend_kernel, line),
-        (shaped(packed, F32),) + (shaped(packed, BF16),) * (PLANE - 1),
-        [VMEM] * (PLANE + 1 + 2 * line),
+    )(head[None], in_hbm(step_ids), *x_parts, *mod_parts, w, cos, sin)
+
+    kv0_line = exchange(kv0, lines)
+    q_plane = exchange(q, planes)
+    parts = call(
+        attend_kernel,
+        shaped((PLANE, STEPS * rows, cols + DH), BF16),
+        [SMEM] + [VMEM] * 5,
         flops=8 * STEPS * rows * n_patch * rows * cols,
-    )(*q_plane, kv1, *kv0_line, *stale_line)
-    peers = [swap(peer, "patch", n_patch, k + 1) for k, peer in enumerate(peers)]
-    o = call(merge_kernel, shaped((STEPS * rows, cols), BF16), [VMEM] * PLANE)(own, *peers)
+    )(patch[None], q_plane, kv1, kv0, kv0_line, stale)
+    parts = exchange(parts, planes)
+    o = call(merge_kernel, shaped((STEPS * rows, cols), BF16), [VMEM])(parts)
 
     o_parts = []
     for k in range(n_head):
@@ -271,7 +288,7 @@
         ],
         2 * STEPS * rows * n_patch * w_out.size,
         n_patch * w_out.size,
-    )(step_ids, patch[None], head[None], *o_parts, mod_parts[0], *w_quads)
+    )(step_ids, patch[None], head[None], *o_parts, mod_own, *w_quads)
     out_back = swap(out_mate, "patch", n_patch, PLANE)
     second = (patch // PLANE) % 2 == 1
     return jnp.concatenate(

time: 64.9 us -> 57.1 us (0.88)
  blocking collectives: 0 us -> 8.03 us
  waiting for transfers between devices: 16.4 us -> 10.2 us
  local copies, waits for them, and re-layouts: 5.87 us -> 1.42 us
  starting transfers between devices: 30.1 us -> 26.6 us
  Pallas kernels: 10.3 us -> 8.51 us
    ppermute x18 -> x6, starting transfers between devices: 21.9 us -> 5.08 us  [swap(): return lax.ppermute(values, axis, [(i, i ^ bit) for i in range(count)])]
    all_to_all x0 -> x3, starting transfers between devices: none -> 14.8 us  [exchange(): return lax.all_to_all(values, 'patch', 0, 0, axis_index_groups=groups)]
    ppermute x18 -> x6, waiting for transfers between devices: 14.4 us -> 4.29 us  [swap(): return lax.ppermute(values, axis, [(i, i ^ bit) for i in range(count)])]
    all_to_all x0 -> x1, blocking collectives: none -> 8.03 us  [exchange(): return lax.all_to_all(values, 'patch', 0, 0, axis_index_groups=groups)]
    unnamed x11 -> x4, local copies, waits for them, and re-layouts: 5.84 us -> 0.01 us
    all_to_all x0 -> x3, waiting for transfers between devices: none -> 3.27 us  [exchange(): return lax.all_to_all(values, 'patch', 0, 0, axis_index_groups=groups)]
    pallas_call x4, Pallas kernels: 9.27 us -> 7.43 us  [the longest x1 2.42 us: body(): call(load_kernel, tuple((pltpu.VMEM(v.shape, v.dtype) for v in first)), [...]
    ppermute x2, starting transfers between devices: 6.01 us -> 4.56 us  [body(): lax.ppermute(w_out.T, ('patch', 'head'), [((hi * per_head + lo) * n_head...]
  transfers between devices with their start and end apart: 23 -> 14, of which waited for: 7 -> 6; matrix products, arithmetic and copies ran while one was open for 2% -> 3% of each run, Pallas kernels for 14% -> 13%
where the time goes in v3:
time: 57.1 us; the launch traced here: 56.6 us
  starting transfers between devices  26.6 us (47%)
  waiting for transfers between devices  10.2 us (18%)
  Pallas kernels  8.51 us (15%)
  blocking collectives  8.03 us (14%)
  local copies, waits for them, and re-layouts  1.42 us (2%)
  other arithmetic  0.97 us (2%)
  between operations  0.77 us (1%)
    all_to_all x3, starting transfers between devices, exchange(): return lax.all_to_all(values, 'patch', 0, 0, axis_index_groups=groups)  14.8 us
    all_to_all x1, blocking collectives, exchange(): return lax.all_to_all(values, 'patch', 0, 0, axis_index_groups=groups)  8.03 us
    ppermute x6, starting transfers between devices, swap(): return lax.ppermute(values, axis, [(i, i ^ bit) for i in range(count)])  5.08 us
    ppermute x2, starting transfers between devices, body(): lax.ppermute(w_out.T, ('patch', 'head'), [((hi * per_head + lo) * n_head...  4.56 us
    ppermute x6, waiting for transfers between devices, swap(): return lax.ppermute(values, axis, [(i, i ^ bit) for i in range(count)])  4.29 us
    all_to_all x3, waiting for transfers between devices, exchange(): return lax.all_to_all(values, 'patch', 0, 0, axis_index_groups=groups)  3.27 us
    ppermute x3, waiting for transfers between devices, body(): lax.ppermute(o, ('patch', 'head'), pairs)  2.66 us
    pallas_call x1, Pallas kernels, body(): call(load_kernel, tuple((pltpu.VMEM(v.shape, v.dtype) for v in first)), [...  2.42 us
  transfers between devices with their start and end apart: 14, of which 6 were waited for; matrix products, arithmetic and copies ran while one was open for 3% of the time, Pallas kernels for 13%

profile of v3, /device:TPU:0, one launch (start us, length us, event | category | flops | bytes accessed | tf_op | source)
XLA Modules:
  0.0 56.6 jit_solution(7266398730738544927)
XLA Ops:
  0.0 0.5 collective-permute-start
  0.5 0.1 collective-permute-start.1
  0.5 1.4 %broadcast_in_dim.8 = bf16[4,2,32,256]{3,2,1,0:T(8,128)(2,1)} broadcast(bf16[2,32,256]{2,1,0:T(8,128)(2,1)} %param.8), dimensions={1,2,3} | broadcast | bytes 163840 | tf_op jit(solution)/shard_map/broadcast_in_dim | solution.py:226
  1.9 6.3 %all-to-all-start.2 = ((bf16[4,2,32,256]{3,2,1,0:T(8,128)(2,1)}), bf16[4,2,32,256]{3,2,1,0:T(8,128)(2,1)S(1)}, u32[]{:S(2)}, u32[]{:S(2)}) async-start(bf16[4,2,32,256]{3,2,1,0:T(8,128)(2,1)} %broadcast_in_dim.8), calls=%async_computation.2 | async-start | bytes 262144 | tf_op jit(solution)/shard_map/all_to_all | solution.py:224
  8.9 0.1 fusion
  9.1 0.0 copy-start.1
  9.1 2.4 %shard_map.73 = (bf16[3,3072,256]{2,1,0:T(8,128)(2,1)S(1)}, bf16[2,32,1536]{2,1,0:T(8,128)(2,1)S(1)}, f32[3,4,1536]{2,1,0:T(4,128)S(1)}) custom-call(bf16[3,3072,256]{2,1,0:T(8,128)(2,1)} %bitcast.10, bf16[2,32,1536]{2,1,0:T(8,128)(2,1)} %refs_1_.1, f32[3,4,1536]{2,1,0:T(4,128)} %bitcast.13), custom_call_target="tpu_custom_call" | custom-call | bytes 4718592 | tf_op jit(solution)/shard_map/pallas_call | solution.py:210
  11.5 0.0 copy-start
  11.5 0.1 pad_maximum_fusion.2
  11.6 0.0 collective-permute-done.1
  11.6 0.0 collective-permute-done.refs_1_
  11.6 2.3 %shard_map.74 = (bf16[4,2,32,256]{3,2,1,0:T(8,128)(2,1)}, bf16[4,2,32,256]{3,2,1,0:T(8,128)(2,1)}, bf16[2,32,256]{2,1,0:T(8,128)(2,1)S(1)}) custom-call(s32[1]{0:T(128)} %bitcast.1.head, s32[2]{0:T(128)} %ids.1, bf16[2,32,1536]{2,1,0:T(8,128)(2,1)S(1)} %get-tuple-element.13.refs_0_, bf16[2,32,1536]{2,1,0:T(8,128)(2,1)S(1)} %collective-permute-done.refs_1_, ...), custom_call_target="tpu_custom_call" | custom-call | flops 301989888 | bytes 4718592 | tf_op jit(solution)/shard_map/pallas_call | solution.py:247
  14.0 0.4 all-to-all-done.2.stale_ref
  14.3 3.7 %all-to-all-start = ((bf16[4,2,32,256]{3,2,1,0:T(8,128)(2,1)}), bf16[4,2,32,256]{3,2,1,0:T(8,128)(2,1)S(1)}, u32[]{:S(2)}, u32[]{:S(2)}) async-start(bf16[4,2,32,256]{3,2,1,0:T(8,128)(2,1)} %get-tuple-element.16), calls=%async_computation | async-start | bytes 262144 | tf_op jit(solution)/shard_map/all_to_all | solution.py:224
  18.0 0.0 copy-done.1
  18.0 0.7 %collective-permute-start.5 = (bf16[192,256]{1,0:T(8,128)(2,1)S(1)}, bf16[192,256]{1,0:T(8,128)(2,1)S(1)}, u32[]{:S(2)}, u32[]{:S(2)}) collective-permute-start(bf16[192,256]{1,0:T(8,128)(2,1)S(1)} %bitcast.14), channel_id=1, source_target_pairs={{0,0},{1,16},{2,2},{3,18},{4,4},{5,20},{6,6},{7,22},{8,8},{9,24},{... | collective-permute-start | bytes 294920 | tf_op jit(solution)/shard_map/ppermute | solution.py:229
  18.7 3.9 %collective-permute-start.6 = (bf16[192,256]{1,0:T(8,128)(2,1)S(1)}, bf16[192,256]{1,0:T(8,128)(2,1)S(1)}, u32[]{:S(2)}, u32[]{:S(2)}) collective-permute-start(bf16[192,256]{1,0:T(8,128)(2,1)S(1)} %bitcast.15), channel_id=1, source_target_pairs={{0,16},{1,0},{2,18},{3,2},{4,20},{5,4},{6,22},{7,6},{8,24},{9,8},{... | collective-permute-start | bytes 294920 | tf_op jit(solution)/shard_map/ppermute | solution.py:229
  22.6 0.4 all-to-all-done.q_ref
  23.1 4.8 %all-to-all-start.1 = ((bf16[4,2,32,256]{3,2,1,0:T(8,128)(2,1)}), bf16[4,2,32,256]{3,2,1,0:T(8,128)(2,1)S(1)}, u32[]{:S(2)}, u32[]{:S(2)}) async-start(bf16[4,2,32,256]{3,2,1,0:T(8,128)(2,1)} %get-tuple-element.18.kv0_sent), calls=%async_computation.1 | async-start | bytes 262144 | tf_op jit(solution)/shard_map/all_to_all | solution.py:224
  27.8 0.0 collective-permute-done.5
  27.8 0.0 collective-permute-done.6
  27.9 1.0 %collective-permute-start.7 = (bf16[2,192,256]{2,1,0:T(8,128)(2,1)S(1)}, bf16[2,192,256]{2,1,0:T(8,128)(2,1)S(1)}, u32[]{:S(2)}, u32[]{:S(2)}) collective-permute-start(bf16[2,192,256]{2,1,0:T(8,128)(2,1)S(1)} %pad_maximum_fusion.refs_5_), channel_id=1, source_target_pairs={{0,2},{2,0},{4,6},{6,4},{8,10},{10,8},{12,14},{14,12},{16,18},{18,... | collective-permute-start | bytes 589832 | tf_op jit(solution)/shard_map/ppermute | solution.py:31
  28.8 0.7 %collective-permute-start.8 = (bf16[2,192,256]{2,1,0:T(8,128)(2,1)S(1)}, bf16[2,192,256]{2,1,0:T(8,128)(2,1)S(1)}, u32[]{:S(2)}, u32[]{:S(2)}) collective-permute-start(bf16[2,192,256]{2,1,0:T(8,128)(2,1)S(1)} %pad_maximum_fusion.refs_5_), channel_id=1, source_target_pairs={{0,4},{2,6},{4,0},{6,2},{8,12},{10,14},{12,8},{14,10},{16,20},{18,... | collective-permute-start | bytes 589832 | tf_op jit(solution)/shard_map/ppermute | solution.py:31
  29.5 1.9 %collective-permute-start.9 = (bf16[2,192,256]{2,1,0:T(8,128)(2,1)S(1)}, bf16[2,192,256]{2,1,0:T(8,128)(2,1)S(1)}, u32[]{:S(2)}, u32[]{:S(2)}) collective-permute-start(bf16[2,192,256]{2,1,0:T(8,128)(2,1)S(1)} %pad_maximum_fusion.refs_5_), channel_id=1, source_target_pairs={{0,6},{2,4},{4,2},{6,0},{8,14},{10,12},{12,10},{14,8},{16,22},{18,... | collective-permute-start | bytes 589832 | tf_op jit(solution)/shard_map/ppermute | solution.py:31
  31.4 2.5 %all-to-all-done.1.kv0_ref = bf16[4,2,32,256]{3,2,1,0:T(8,128)(2,1)S(1)} async-done(((bf16[4,2,32,256]{3,2,1,0:T(8,128)(2,1)}), bf16[4,2,32,256]{3,2,1,0:T(8,128)(2,1)S(1)}, u32[]{:S(2)}, u32[]{:S(2)}) %all-to-all-start.1) | async-done | bytes 131104 | tf_op jit(solution)/shard_map/all_to_all | solution.py:224
  33.9 1.6 %shard_map.75 = bf16[4,64,384]{2,1,0:T(8,128)(2,1)S(1)} custom-call(s32[1]{0:T(128)} %bitcast.patch, bf16[4,2,32,256]{3,2,1,0:T(8,128)(2,1)S(1)} %all-to-all-done.q_ref, bf16[2,32,256]{2,1,0:T(8,128)(2,1)S(1)} %get-tuple-element.17.kv1_ref, bf16[4,2,32,256]{3,2,1,0:T(8,128)(2,1)} %get-tuple-element.18.kv0_sent, ...), custom_call_target="tpu_custom_call" | custom-call | flops 67108864 | tf_op jit(solution)/shard_map/pallas_call | solution.py:262
  35.5 8.0 %all_to_all.20.parts_ref = bf16[4,64,384]{2,1,0:T(8,128)(2,1)S(1)} all-to-all(bf16[4,64,384]{2,1,0:T(8,128)(2,1)S(1)} %shard_map.75), channel_id=1, replica_groups={{0,2,4,6},{8,10,12,14},{16,18,20,22},{24,26,28,30},{1,3,5,7},{9,11,13,1..., dimensions={0} | all-to-all | bytes 393216 | tf_op jit(solution)/shard_map/all_to_all | solution.py:224
  43.6 1.0 %shard_map.76.refs_0_ = bf16[64,256]{1,0:T(8,128)(2,1)S(1)} custom-call(bf16[4,64,384]{2,1,0:T(8,128)(2,1)S(1)} %all_to_all.20.parts_ref), custom_call_target="tpu_custom_call" | custom-call | tf_op jit(solution)/shard_map/pallas_call | solution.py:269
  44.6 1.5 %collective-permute-start.2 = (bf16[64,256]{1,0:T(8,128)(2,1)S(1)}, bf16[64,256]{1,0:T(8,128)(2,1)S(1)}, u32[]{:S(2)}, u32[]{:S(2)}) collective-permute-start(bf16[64,256]{1,0:T(8,128)(2,1)S(1)} %shard_map.76.refs_0_), channel_id=1, source_target_pairs={{0,8},{1,9},{2,10},{3,11},{4,12},{5,13},{6,14},{7,15},{8,0},{9,1},... | collective-permute-start | bytes 98312 | tf_op jit(solution)/shard_map/ppermute | solution.py:279
  46.1 0.0 collective-permute-start.3
  46.1 0.0 collective-permute-done.7.refs_6_
  46.1 0.7 %collective-permute-start.4 = (bf16[64,256]{1,0:T(8,128)(2,1)S(1)}, bf16[64,256]{1,0:T(8,128)(2,1)S(1)}, u32[]{:S(2)}, u32[]{:S(2)}) collective-permute-start(bf16[64,256]{1,0:T(8,128)(2,1)S(1)} %shard_map.76.refs_0_), channel_id=1, source_target_pairs={{0,9},{1,8},{2,11},{3,10},{4,13},{5,12},{6,15},{7,14},{8,1},{9,0},... | collective-permute-start | bytes 98312 | tf_op jit(solution)/shard_map/ppermute | solution.py:279
  46.8 0.0 collective-permute-done.8.refs_7_
  46.8 0.0 collective-permute-done.9.refs_8_
  46.8 1.8 %collective-permute-done.2.refs_1_ = bf16[64,256]{1,0:T(8,128)(2,1)S(1)} collective-permute-done((bf16[64,256]{1,0:T(8,128)(2,1)S(1)}, bf16[64,256]{1,0:T(8,128)(2,1)S(1)}, u32[]{:S(2)}, u32[]{:S(2)}) %collective-permute-start.2) | collective-permute-done | bytes 32800 | tf_op jit(solution)/shard_map/ppermute | solution.py:279
  48.6 0.0 collective-permute-done.3.refs_2_
  48.6 0.9 %collective-permute-done.4.refs_3_ = bf16[64,256]{1,0:T(8,128)(2,1)S(1)} collective-permute-done((bf16[64,256]{1,0:T(8,128)(2,1)S(1)}, bf16[64,256]{1,0:T(8,128)(2,1)S(1)}, u32[]{:S(2)}, u32[]{:S(2)}) %collective-permute-start.4) | collective-permute-done | bytes 32800 | tf_op jit(solution)/shard_map/ppermute | solution.py:279
  49.5 0.0 copy-done
  49.5 1.1 %shard_map.77 = (bf16[2,32,768]{2,1,0:T(8,128)(2,1)S(1)}, bf16[2,32,768]{2,1,0:T(8,128)(2,1)S(1)}) custom-call(s32[2]{0:T(128)S(1)} %copy-done, s32[1]{0:T(128)} %bitcast.patch, s32[1]{0:T(128)} %bitcast.1.head, bf16[64,256]{1,0:T(8,128)(2,1)S(1)} %shard_map.76.refs_0_, bf16[64,256]{1,0:T(8,128)(2,1)S(1)} %collective-permute-done.2.refs_1_, ...), custom_call_target="tpu_custom_call" | custom-call | flops 100663296 | bytes 786432 | tf_op jit(solution)/shard_map/pallas_call | solution.py:281
  50.6 1.0 %collective-permute-start.10 = (bf16[2,32,768]{2,1,0:T(8,128)(2,1)S(1)}, bf16[2,32,768]{2,1,0:T(8,128)(2,1)S(1)}, u32[]{:S(2)}, u32[]{:S(2)}) collective-permute-start(bf16[2,32,768]{2,1,0:T(8,128)(2,1)S(1)} %get-tuple-element.19), channel_id=1, source_target_pairs={{0,8},{2,10},{4,12},{6,14},{8,0},{10,2},{12,4},{14,6},{16,24},{18,... | collective-permute-start | bytes 294920 | tf_op jit(solution)/shard_map/ppermute | solution.py:31
  51.6 4.3 %collective-permute-done.10 = bf16[2,32,768]{2,1,0:T(8,128)(2,1)S(1)} collective-permute-done((bf16[2,32,768]{2,1,0:T(8,128)(2,1)S(1)}, bf16[2,32,768]{2,1,0:T(8,128)(2,1)S(1)}, u32[]{:S(2)}, u32[]{:S(2)}) %collective-permute-start.10) | collective-permute-done | bytes 98336 | tf_op jit(solution)/shard_map/ppermute | solution.py:31
  55.9 0.7 %pad_maximum_fusion.1 = bf16[2,32,1536]{2,1,0:T(8,128)(2,1)} fusion(bf16[2,32,768]{2,1,0:T(8,128)(2,1)S(1)} %get-tuple-element.22, bf16[2,32,768]{2,1,0:T(8,128)(2,1)S(1)} %get-tuple-element.21), kind=kLoop, calls=%fused_computation.1 | loop fusion | flops 393216 | bytes 393216 | tf_op jit(solution)/shard_map/concatenate | solution.py:294
  (4 shorter events, 0.1 us)
Async XLA Ops:
  0.0 11.6 %collective-permute-start = (bf16[2,32,1536]{2,1,0:T(8,128)(2,1)}, bf16[2,32,1536]{2,1,0:T(8,128)(2,1)S(1)}, u32[]{:S(2)}, u32[]{:S(2)}) collective-permute-start(bf16[2,32,1536]{2,1,0:T(8,128)(2,1)} %refs_1_.1), channel_id=1, source_target_pairs={{0,1},{1,0},{2,3},{3,2},{4,5},{5,4},{6,7},{7,6},{8,9},{9,8},{10,11... | collective-permute-start | bytes 589832 | tf_op jit(solution)/shard_map/ppermute | solution.py:31
  0.5 11.2 %collective-permute-start.1 = (f32[4,3,1536]{2,0,1:T(4,128)}, f32[4,3,1536]{2,0,1:T(4,128)S(1)}, u32[]{:S(2)}, u32[]{:S(2)}) collective-permute-start(f32[4,3,1536]{2,0,1:T(4,128)} %param.11), channel_id=1, source_target_pairs={{0,1},{1,0},{2,3},{3,2},{4,5},{5,4},{6,7},{7,6},{8,9},{9,8},{10,11... | collective-permute-start | bytes 221192 | tf_op jit(solution)/shard_map/ppermute | solution.py:31
  1.9 12.4 %all-to-all-start.2 = ((bf16[4,2,32,256]{3,2,1,0:T(8,128)(2,1)}), bf16[4,2,32,256]{3,2,1,0:T(8,128)(2,1)S(1)}, u32[]{:S(2)}, u32[]{:S(2)}) async-start(bf16[4,2,32,256]{3,2,1,0:T(8,128)(2,1)} %broadcast_in_dim.8), calls=%async_computation.2 | async-start | bytes 262144 | tf_op jit(solution)/shard_map/all_to_all | solution.py:224
  9.1 9.0 %copy-start.1 = (bf16[256,192]{0,1:T(8,128)(2,1)S(1)}, bf16[256,192]{0,1:T(8,128)(2,1)}, u32[]{:S(2)}) copy-start(bf16[256,192]{0,1:T(8,128)(2,1)} %param.10) | copy-start | bytes 294916
  11.5 38.0 %copy-start = (s32[2]{0:T(128)S(1)}, s32[2]{0:T(128)}, u32[]{:S(2)}) copy-start(s32[2]{0:T(128)} %ids.1) | copy-start | bytes 28
  14.3 8.7 %all-to-all-start = ((bf16[4,2,32,256]{3,2,1,0:T(8,128)(2,1)}), bf16[4,2,32,256]{3,2,1,0:T(8,128)(2,1)S(1)}, u32[]{:S(2)}, u32[]{:S(2)}) async-start(bf16[4,2,32,256]{3,2,1,0:T(8,128)(2,1)} %get-tuple-element.16), calls=%async_computation | async-start | bytes 262144 | tf_op jit(solution)/shard_map/all_to_all | solution.py:224
  18.0 9.8 %collective-permute-start.5 = (bf16[192,256]{1,0:T(8,128)(2,1)S(1)}, bf16[192,256]{1,0:T(8,128)(2,1)S(1)}, u32[]{:S(2)}, u32[]{:S(2)}) collective-permute-start(bf16[192,256]{1,0:T(8,128)(2,1)S(1)} %bitcast.14), channel_id=1, source_target_pairs={{0,0},{1,16},{2,2},{3,18},{4,4},{5,20},{6,6},{7,22},{8,8},{9,24},{... | collective-permute-start | bytes 294920 | tf_op jit(solution)/shard_map/ppermute | solution.py:229
  18.7 9.1 %collective-permute-start.6 = (bf16[192,256]{1,0:T(8,128)(2,1)S(1)}, bf16[192,256]{1,0:T(8,128)(2,1)S(1)}, u32[]{:S(2)}, u32[]{:S(2)}) collective-permute-start(bf16[192,256]{1,0:T(8,128)(2,1)S(1)} %bitcast.15), channel_id=1, source_target_pairs={{0,16},{1,0},{2,18},{3,2},{4,20},{5,4},{6,22},{7,6},{8,24},{9,8},{... | collective-permute-start | bytes 294920 | tf_op jit(solution)/shard_map/ppermute | solution.py:229
  23.1 10.8 %all-to-all-start.1 = ((bf16[4,2,32,256]{3,2,1,0:T(8,128)(2,1)}), bf16[4,2,32,256]{3,2,1,0:T(8,128)(2,1)S(1)}, u32[]{:S(2)}, u32[]{:S(2)}) async-start(bf16[4,2,32,256]{3,2,1,0:T(8,128)(2,1)} %get-tuple-element.18.kv0_sent), calls=%async_computation.1 | async-start | bytes 262144 | tf_op jit(solution)/shard_map/all_to_all | solution.py:224
  27.9 18.3 %collective-permute-start.7 = (bf16[2,192,256]{2,1,0:T(8,128)(2,1)S(1)}, bf16[2,192,256]{2,1,0:T(8,128)(2,1)S(1)}, u32[]{:S(2)}, u32[]{:S(2)}) collective-permute-start(bf16[2,192,256]{2,1,0:T(8,128)(2,1)S(1)} %pad_maximum_fusion.refs_5_), channel_id=1, source_target_pairs={{0,2},{2,0},{4,6},{6,4},{8,10},{10,8},{12,14},{14,12},{16,18},{18,... | collective-permute-start | bytes 589832 | tf_op jit(solution)/shard_map/ppermute | solution.py:31
  28.8 18.0 %collective-permute-start.8 = (bf16[2,192,256]{2,1,0:T(8,128)(2,1)S(1)}, bf16[2,192,256]{2,1,0:T(8,128)(2,1)S(1)}, u32[]{:S(2)}, u32[]{:S(2)}) collective-permute-start(bf16[2,192,256]{2,1,0:T(8,128)(2,1)S(1)} %pad_maximum_fusion.refs_5_), channel_id=1, source_target_pairs={{0,4},{2,6},{4,0},{6,2},{8,12},{10,14},{12,8},{14,10},{16,20},{18,... | collective-permute-start | bytes 589832 | tf_op jit(solution)/shard_map/ppermute | solution.py:31
  29.5 17.3 %collective-permute-start.9 = (bf16[2,192,256]{2,1,0:T(8,128)(2,1)S(1)}, bf16[2,192,256]{2,1,0:T(8,128)(2,1)S(1)}, u32[]{:S(2)}, u32[]{:S(2)}) collective-permute-start(bf16[2,192,256]{2,1,0:T(8,128)(2,1)S(1)} %pad_maximum_fusion.refs_5_), channel_id=1, source_target_pairs={{0,6},{2,4},{4,2},{6,0},{8,14},{10,12},{12,10},{14,8},{16,22},{18,... | collective-permute-start | bytes 589832 | tf_op jit(solution)/shard_map/ppermute | solution.py:31
  44.6 4.0 %collective-permute-start.2 = (bf16[64,256]{1,0:T(8,128)(2,1)S(1)}, bf16[64,256]{1,0:T(8,128)(2,1)S(1)}, u32[]{:S(2)}, u32[]{:S(2)}) collective-permute-start(bf16[64,256]{1,0:T(8,128)(2,1)S(1)} %shard_map.76.refs_0_), channel_id=1, source_target_pairs={{0,8},{1,9},{2,10},{3,11},{4,12},{5,13},{6,14},{7,15},{8,0},{9,1},... | collective-permute-start | bytes 98312 | tf_op jit(solution)/shard_map/ppermute | solution.py:279
  46.1 2.4 %collective-permute-start.3 = (bf16[64,256]{1,0:T(8,128)(2,1)S(1)}, bf16[64,256]{1,0:T(8,128)(2,1)S(1)}, u32[]{:S(2)}, u32[]{:S(2)}) collective-permute-start(bf16[64,256]{1,0:T(8,128)(2,1)S(1)} %shard_map.76.refs_0_), channel_id=1, source_target_pairs={{0,1},{1,0},{2,3},{3,2},{4,5},{5,4},{6,7},{7,6},{8,9},{9,8},{10,11... | collective-permute-start | bytes 98312 | tf_op jit(solution)/shard_map/ppermute | solution.py:279
  46.1 3.3 %collective-permute-start.4 = (bf16[64,256]{1,0:T(8,128)(2,1)S(1)}, bf16[64,256]{1,0:T(8,128)(2,1)S(1)}, u32[]{:S(2)}, u32[]{:S(2)}) collective-permute-start(bf16[64,256]{1,0:T(8,128)(2,1)S(1)} %shard_map.76.refs_0_), channel_id=1, source_target_pairs={{0,9},{1,8},{2,11},{3,10},{4,13},{5,12},{6,15},{7,14},{8,1},{9,0},... | collective-permute-start | bytes 98312 | tf_op jit(solution)/shard_map/ppermute | solution.py:279
  50.6 5.3 %collective-permute-start.10 = (bf16[2,32,768]{2,1,0:T(8,128)(2,1)S(1)}, bf16[2,32,768]{2,1,0:T(8,128)(2,1)S(1)}, u32[]{:S(2)}, u32[]{:S(2)}) collective-permute-start(bf16[2,32,768]{2,1,0:T(8,128)(2,1)S(1)} %get-tuple-element.19), channel_id=1, source_target_pairs={{0,8},{2,10},{4,12},{6,14},{8,0},{10,2},{12,4},{14,6},{16,24},{18,... | collective-permute-start | bytes 294920 | tf_op jit(solution)/shard_map/ppermute | solution.py:31

commit v4 on v3

v4 whole, which is shorter than its diff:
```python
import functools
import math

import jax
import jax.numpy as jnp
from jax import lax
from jax.experimental import pallas as pl
from jax.experimental.pallas import tpu as pltpu
from jax.sharding import PartitionSpec as P

DH = 128
STEPS = 2
PLANE = 4
MIB = 1024 * 1024
VMEM = pl.BlockSpec(memory_space=pltpu.VMEM)
SMEM = pl.BlockSpec(memory_space=pltpu.SMEM)
ANY = pl.BlockSpec(memory_space=pl.ANY)
BF16, F32 = jnp.bfloat16, jnp.float32
NT = (((1,), (1,)), ((), ()))


def angle_tables(positions):
    half = DH // 2
    frequency = 10000.0 ** (-(2.0 * jnp.arange(half, dtype=F32)) / DH)
    grid = positions.astype(F32)[:, None] * frequency[None, :]
    cos, sin = jnp.cos(grid), jnp.sin(grid)
    return jnp.concatenate([cos, cos], axis=1), jnp.concatenate([-sin, sin], axis=1)


def swap(values, axis, count, bit):
    return lax.ppermute(values, axis, [(i, i ^ bit) for i in range(count)])


def load_kernel(ids, *refs):
    count = len(refs) // 2 - 1
    ids_out, sems = refs[-2:]
    copies = [
        pltpu.make_async_copy(refs[i], refs[count + i], sems.at[i]) for i in range(count)
    ]
    for copy in copies:
        copy.start()
    row = lax.broadcasted_iota(jnp.int32, ids_out.shape, 0)
    tile = jnp.zeros(ids_out.shape, jnp.int32)
    for step in range(STEPS):
        tile = jnp.where(row == step, ids[step], tile)
    ids_out[...] = tile
    for copy in copies:
        copy.wait()


def table_row(mod_ref, kind, ids_ref, step):
    chosen = ids_ref[step : step + 1, :1]
    table = mod_ref[kind]
    return sum(
        jnp.where(chosen == r, table[r : r + 1], 0.0) for r in range(table.shape[0])
    )


def qkv_kernel(n_head, head, ids_ref, *refs):
    x_refs, mod_refs = refs[:n_head], refs[n_head : 2 * n_head]
    w_ref, cos_ref, sin_ref = refs[2 * n_head : 2 * n_head + 3]
    q_ref, kv0_ref, kv1_ref, a_ref = refs[-4:]
    rows, feats = x_refs[0].shape[1:]
    width = n_head * feats
    cols = w_ref.shape[2]
    for step in range(STEPS):
        total, square = 0.0, 0.0
        for x_ref in x_refs:
            hidden = x_ref[step].astype(F32)
            total += jnp.sum(hidden, axis=1, keepdims=True)
            square += jnp.sum(hidden * hidden, axis=1, keepdims=True)
        mean = total / width
        inv = lax.rsqrt(square / width - mean * mean + 1e-06)
        for part in range(n_head):
            shift = table_row(mod_refs[part], 0, ids_ref, step)
            scale = table_row(mod_refs[part], 1, ids_ref, step)
            hidden = x_refs[part][step].astype(F32)
            a = (hidden - mean) * inv * (1.0 + scale) + shift
            a_ref[part, step * rows : (step + 1) * rows, :] = a.astype(BF16)
    cos, sin = cos_ref[...], sin_ref[...]
    for slot in range(3):
        total = jnp.zeros((STEPS * rows, cols), F32)
        for part in range(n_head):
            start = pl.multiple_of((head[0] ^ part) * feats, feats)
            total += jnp.dot(
                a_ref[part], w_ref[slot, pl.ds(start, feats), :], preferred_element_type=F32
            )
        for step in range(STEPS):
            for block in range(cols // DH):
                lanes = slice(block * DH, (block + 1) * DH)
                u = total[step * rows : (step + 1) * rows, lanes]
                if slot < 2:
                    u = u * cos + pltpu.roll(u, DH // 2, 1) * sin
                u = u.astype(BF16)
                if slot == 0:
                    q_ref[step, :, lanes] = u
                else:
                    (kv0_ref, kv1_ref)[step][slot - 1, :, lanes] = u


def split3(values):
    high = values.astype(BF16).astype(F32)
    middle = (values - high).astype(BF16).astype(F32)
    return [high, middle, values - high - middle]


def attend_kernel(line, *refs):
    q_refs, refs = refs[:line], refs[line:]
    kv1_ref, kv0_refs, stale_refs = refs[0], refs[1 : 1 + PLANE], refs[1 + PLANE : 1 + 2 * PLANE]
    outs = refs[1 + 2 * PLANE :]
    rows, cols = q_refs[0].shape[1:]
    shape = (line * rows, PLANE * rows + rows)
    stray = jnp.where(lax.broadcasted_iota(jnp.int32, shape, 0) < rows, 0, PLANE)
    drop = lax.broadcasted_iota(jnp.int32, shape, 1) // rows == stray
    lane = lax.broadcasted_iota(jnp.int32, (line * rows, DH), 1)
    for step in range(STEPS):
        keys = ((*stale_refs, kv0_refs[0]), (*kv0_refs, kv1_ref))[step]
        stats = jnp.zeros((line * rows, DH), F32)
        mixed = []
        for block in range(cols // DH):
            lanes = slice(block * DH, (block + 1) * DH)
            scores = lax.dot_general(
                jnp.concatenate([ref[step, :, lanes] for ref in q_refs], axis=0),
                jnp.concatenate([ref[0, :, lanes] for ref in keys], axis=0),
                NT,
                preferred_element_type=F32,
            )
            scores = jnp.where(drop, -1e30, scores * (1.0 / math.sqrt(DH)))
            top = jnp.max(scores, axis=1, keepdims=True)
            weights = jnp.exp(scores - top)
            totals = jnp.sum(weights, axis=1, keepdims=True)
            values = jnp.concatenate([ref[1, :, lanes] for ref in keys], axis=0)
            mixed.append(
                jnp.dot(weights.astype(BF16), values, preferred_element_type=F32) / totals
            )
            for place, piece in enumerate(split3(top) + split3(totals)):
                stats = jnp.where(lane == block * 8 + place, piece, stats)
        packed = jnp.concatenate([*mixed, stats], axis=1).astype(BF16)
        for number, ref in enumerate(outs):
            ref[step * rows : (step + 1) * rows, :] = packed[number * rows : (number + 1) * rows]


def merge_kernel(*refs):
    part_refs, o_ref = refs[:-1], refs[-1]
    cols = o_ref.shape[1]
    source = lax.broadcasted_iota(jnp.int32, (DH, DH), 0)
    for block in range(cols // DH):
        lanes = slice(block * DH, (block + 1) * DH)

        def spread(ref, first):
            pick = (source >= block * 8 + first) & (source < block * 8 + first + 3)
            return jnp.dot(ref[:, cols:], pick.astype(F32).astype(BF16), preferred_element_type=F32)

        tops = [spread(ref, 0) for ref in part_refs]
        best = functools.reduce(jnp.maximum, tops)
        scales = [spread(ref, 3) * jnp.exp(t - best) for ref, t in zip(part_refs, tops)]
        mixed = sum(s * ref[:, lanes].astype(F32) for s, ref in zip(scales, part_refs))
        o_ref[:, lanes] = (mixed / sum(scales)).astype(BF16)


def out_kernel(n_head, n_patch, patch, head, ids_ref, *refs):
    o_refs, refs = refs[: 2 * n_head], refs[2 * n_head :]
    mod_ref, w_refs = refs[0], refs[1 : 1 + PLANE]
    own_out, mate_out, o_all, sums = refs[1 + PLANE :]
    rows = o_refs[0].shape[0]
    piece = w_refs[0].shape[1]
    per_head = n_patch // n_head
    for part in range(n_head):
        for mate in range(2):
            spot = slice(mate * rows, (mate + 1) * rows)
            o_all[head[0] ^ part, spot, :] = o_refs[2 * part + mate][...]
    for near in range(PLANE):
        total = jnp.zeros((2 * rows, piece), F32)
        for part in range(n_head):
            o = o_all[(patch[0] // per_head) ^ part]
            total += lax.dot_general(o, w_refs[near][part], NT, preferred_element_type=F32)
        sums[(patch[0] % PLANE) ^ near] = total
    out = jnp.concatenate([sums[c] for c in range(PLANE)], axis=1)
    second = (patch[0] // PLANE) % 2 == 1
    for step in range(STEPS):
        gate = table_row(mod_ref, 2, ids_ref, step)
        gate = jnp.where(second, gate[:, PLANE * piece :], gate[:, : PLANE * piece])
        each = rows // STEPS
        for mate, ref in enumerate((own_out, mate_out)):
            start = mate * rows + step * each
            ref[step] = (gate * out[start : start + each]).astype(BF16)


def in_hbm(values):
    return pltpu.with_memory_space_constraint(values, pltpu.HBM)


def call(kernel, shapes, ins, scratch=(), flops=0, size=0, limit=16):
    return pl.pallas_call(
        kernel,
        out_shape=shapes,
        in_specs=ins,
        out_specs=jax.tree.map(lambda _: VMEM, shapes),
        scratch_shapes=scratch,
        compiler_params=pltpu.CompilerParams(vmem_limit_bytes=limit * MIB),
        cost_estimate=pl.CostEstimate(flops=flops, bytes_accessed=size, transcendentals=0),
    )


def body(n_patch, n_head, inputs, stale_kv, w_qkv, w_out, mod_table, step_ids, slab_order):
    rows, feats = inputs.shape[1:]
    cols = w_qkv.shape[2]
    piece = w_out.shape[1]
    line = n_patch // PLANE
    per_head = n_patch // n_head
    patch = lax.axis_index("patch").astype(jnp.int32)
    head = lax.axis_index("head").astype(jnp.int32)
    shaped = jax.ShapeDtypeStruct

    x_parts = [swap(inputs, "head", n_head, k) for k in range(1, n_head)]
    mod_parts = [swap(mod_table, "head", n_head, k) for k in range(1, n_head)]
    first = (jnp.transpose(w_qkv, (1, 0, 2)), inputs, jnp.transpose(mod_table, (1, 0, 2)))
    w, x_own, mod_own, ids = call(
        load_kernel,
        tuple(pltpu.VMEM(v.shape, v.dtype) for v in first) + (shaped((8, DH), jnp.int32),),
        [SMEM] + [ANY] * len(first),
        [pltpu.SemaphoreType.DMA((len(first),))],
        size=2 * w_qkv.size,
    )(*map(in_hbm, (step_ids, *first)))
    x_parts = [x_own] + x_parts
    mod_parts = [mod_own] + [jnp.transpose(part, (1, 0, 2)) for part in mod_parts]

    def plane_of(values):
        return [values] + [swap(values, "patch", n_patch, k) for k in range(1, PLANE)]

    def line_of(values):
        return [values] + [swap(values, "patch", n_patch, PLANE * k) for k in range(1, line)]

    stale_plane = plane_of(stale_kv)
    w_quad = jnp.stack(
        [
            lax.ppermute(
                w_out.T,
                ("patch", "head"),
                [
                    ((hi * per_head + lo) * n_head + h, ((h ^ k) * per_head + lo) * n_head + hi)
                    for hi in range(n_head)
                    for lo in range(per_head)
                    for h in range(n_head)
                ],
            )
            for k in range(n_head)
        ]
    )
    w_quads = plane_of(w_quad)

    positions = slab_order[0] * rows + jnp.arange(rows, dtype=jnp.int32)
    cos, sin = angle_tables(positions)
    kv_shape = shaped((2, rows, cols), BF16)
    q, kv0, kv1 = call(
        functools.partial(qkv_kernel, n_head),
        (kv_shape,) * 3,
        [SMEM] + [VMEM] * (2 * n_head + 4) + [ANY] * PLANE,
        [pltpu.VMEM((n_head, STEPS * rows, feats), BF16)],
        2 * STEPS * rows * w_qkv.size,
        2 * w_qkv.size,
    )(head[None], ids, *x_parts, *mod_parts, w, cos, sin, w_quad, *stale_plane[1:])

    kv0_plane = plane_of(kv0)
    parts = call(
        functools.partial(attend_kernel, line),
        (shaped((STEPS * rows, cols + DH), BF16),) * line,
        [VMEM] * (line + 1 + 2 * PLANE),
        flops=8 * STEPS * rows * n_patch * rows * cols,
    )(*line_of(q), kv1, *kv0_plane, *stale_plane)
    parts = [
        swap(part, "patch", n_patch, PLANE * k) if k else part for k, part in enumerate(parts)
    ]
    o = call(merge_kernel, shaped((STEPS * rows, cols), BF16), [VMEM] * line)(*parts)

    o_parts = []
    for k in range(n_head):
        for mate in range(2):
            pairs = [
                (p * n_head + h, (p ^ (PLANE * mate)) * n_head + (h ^ k))
                for p in range(n_patch)
                for h in range(n_head)
            ]
            o_parts.append(lax.ppermute(o, ("patch", "head"), pairs) if k or mate else o)
    half = shaped((STEPS, rows, PLANE * piece), BF16)
    out_own, out_mate = call(
        functools.partial(out_kernel, n_head, n_patch),
        (half, half),
        [SMEM] * 2 + [VMEM] * (2 * n_head + 2 + PLANE),
        [
            pltpu.VMEM((n_head, 2 * STEPS * rows, cols), BF16),
            pltpu.VMEM((PLANE, 2 * STEPS * rows, piece), F32),
        ],
        2 * STEPS * rows * n_patch * w_out.size,
        n_patch * w_out.size,
    )(patch[None], head[None], ids, *o_parts, mod_own, *w_quads)
    out_back = swap(out_mate, "patch", n_patch, PLANE)
    second = (patch // PLANE) % 2 == 1
    return jnp.concatenate(
        [jnp.where(second, out_back, out_own), jnp.where(second, out_own, out_back)], axis=2
    )


def solution(mesh):
    in_specs = (
        P(None, "patch", "head"),
        P(None, "patch", "head"),
        P(None, None, "head"),
        P("head", "patch"),
        P(None, None, "head"),
        P(),
        P("patch"),
    )
    run = functools.partial(body, mesh.shape["patch"], mesh.shape["head"])
    return jax.shard_map(
        run, mesh=mesh, in_specs=in_specs, out_specs=P(None, "patch", "head"), check_vma=False
    )
```

time: 57.1 us -> 58.5 us (1.025)
  blocking collectives: 8.03 us -> 0 us
  waiting for transfers between devices: 10.2 us -> 17.9 us
  starting transfers between devices: 26.6 us -> 33 us
  Pallas kernels: 8.51 us -> 5.75 us
  local copies, waits for them, and re-layouts: 1.42 us -> 0.01 us
    ppermute x6 -> x18, starting transfers between devices: 5.08 us -> 24.6 us  [swap(): return lax.ppermute(values, axis, [(i, i ^ bit) for i in range(count)])]
    all_to_all x3 -> x0, starting transfers between devices: 14.8 us -> none  [exchange(): return lax.all_to_all(values, 'patch', 0, 0, axis_index_groups=groups)]
    ppermute x6 -> x18, waiting for transfers between devices: 4.29 us -> 15.7 us  [swap(): return lax.ppermute(values, axis, [(i, i ^ bit) for i in range(count)])]
    all_to_all x1 -> x0, blocking collectives: 8.03 us -> none  [exchange(): return lax.all_to_all(values, 'patch', 0, 0, axis_index_groups=groups)]
    all_to_all x3 -> x0, waiting for transfers between devices: 3.27 us -> none  [exchange(): return lax.all_to_all(values, 'patch', 0, 0, axis_index_groups=groups)]
    pallas_call x4, Pallas kernels: 7.43 us -> 5.21 us  [the longest x1 3.05 us: body(): call(load_kernel, tuple((pltpu.VMEM(v.shape, v.dtype) for v in first)) +...]
    ppermute x2, starting transfers between devices: 4.56 us -> 6.15 us  [body(): lax.ppermute(w_out.T, ('patch', 'head'), [((hi * per_head + lo) * n_head...]
    broadcast_in_dim x1 -> x0, local copies, waits for them, and re-layouts: 1.41 us -> none  [body(): jnp.broadcast_to(stale_kv[None], (line, *stale_kv.shape))]
  transfers between devices with their start and end apart: 14 -> 23, of which waited for: 6 -> 8; matrix products, arithmetic and copies ran while one was open for 3% -> 0% of each run, Pallas kernels for 13% -> 7%
where the time goes in v4:
time: 58.5 us; the launch traced here: 58.3 us
  starting transfers between devices  33 us (56%)
  waiting for transfers between devices  17.9 us (31%)
  Pallas kernels  5.75 us (10%)
  other arithmetic  0.97 us (2%)
  between operations  0.75 us (1%)
    ppermute x18, starting transfers between devices, swap(): return lax.ppermute(values, axis, [(i, i ^ bit) for i in range(count)])  24.6 us
    ppermute x18, waiting for transfers between devices, swap(): return lax.ppermute(values, axis, [(i, i ^ bit) for i in range(count)])  15.7 us
    ppermute x2, starting transfers between devices, body(): lax.ppermute(w_out.T, ('patch', 'head'), [((hi * per_head + lo) * n_head...  6.15 us
    pallas_call x1, Pallas kernels, body(): call(load_kernel, tuple((pltpu.VMEM(v.shape, v.dtype) for v in first)) +...  3.05 us
    ppermute x3, starting transfers between devices, body(): lax.ppermute(o, ('patch', 'head'), pairs)  2.21 us
    ppermute x3, waiting for transfers between devices, body(): lax.ppermute(o, ('patch', 'head'), pairs)  2.11 us
    pallas_call x1, Pallas kernels, body(): call(functools.partial(qkv_kernel, n_head), (kv_shape,) * 3, [SMEM] + [VM...  1.19 us
  transfers between devices with their start and end apart: 23, of which 8 were waited for; matrix products, arithmetic and copies ran while one was open for 0% of the time, Pallas kernels for 7%

profile of v4, /device:TPU:0, one launch (start us, length us, event | category | flops | bytes accessed | tf_op | source)
XLA Modules:
  0.0 58.3 jit_solution(325778904326510579)
XLA Ops:
  0.0 1.7 %collective-permute-start.2 = (bf16[192,256]{1,0:T(8,128)(2,1)}, bf16[192,256]{1,0:T(8,128)(2,1)S(1)}, u32[]{:S(2)}, u32[]{:S(2)}) collective-permute-start(bf16[192,256]{1,0:T(8,128)(2,1)} %bitcast.14), channel_id=1, source_target_pairs={{0,0},{1,16},{2,2},{3,18},{4,4},{5,20},{6,6},{7,22},{8,8},{9,24},{... | collective-permute-start | bytes 294920 | tf_op jit(solution)/shard_map/ppermute | solution.py:237
  1.7 4.5 %collective-permute-start.3 = (bf16[192,256]{1,0:T(8,128)(2,1)}, bf16[192,256]{1,0:T(8,128)(2,1)S(1)}, u32[]{:S(2)}, u32[]{:S(2)}) collective-permute-start(bf16[192,256]{1,0:T(8,128)(2,1)} %bitcast.15), channel_id=1, source_target_pairs={{0,16},{1,0},{2,18},{3,2},{4,20},{5,4},{6,22},{7,6},{8,24},{9,8},{... | collective-permute-start | bytes 294920 | tf_op jit(solution)/shard_map/ppermute | solution.py:237
  6.2 1.5 %collective-permute-start.4 = (bf16[2,32,256]{2,1,0:T(8,128)(2,1)}, bf16[2,32,256]{2,1,0:T(8,128)(2,1)S(1)}, u32[]{:S(2)}, u32[]{:S(2)}) collective-permute-start(bf16[2,32,256]{2,1,0:T(8,128)(2,1)} %refs_9_.1), channel_id=1, source_target_pairs={{0,2},{2,0},{4,6},{6,4},{8,10},{10,8},{12,14},{14,12},{16,18},{18,... | collective-permute-start | bytes 98312 | tf_op jit(solution)/shard_map/ppermute | solution.py:31
  7.6 1.5 %collective-permute-start.5 = (bf16[2,32,256]{2,1,0:T(8,128)(2,1)}, bf16[2,32,256]{2,1,0:T(8,128)(2,1)S(1)}, u32[]{:S(2)}, u32[]{:S(2)}) collective-permute-start(bf16[2,32,256]{2,1,0:T(8,128)(2,1)} %refs_9_.1), channel_id=1, source_target_pairs={{0,4},{2,6},{4,0},{6,2},{8,12},{10,14},{12,8},{14,10},{16,20},{18,... | collective-permute-start | bytes 98312 | tf_op jit(solution)/shard_map/ppermute | solution.py:31
  9.2 0.0 collective-permute-start
  9.8 0.1 fusion
  10.0 3.1 %shard_map.73 = (bf16[3,3072,256]{2,1,0:T(8,128)(2,1)S(1)}, bf16[2,32,1536]{2,1,0:T(8,128)(2,1)S(1)}, f32[3,4,1536]{2,1,0:T(4,128)S(1)}, s32[8,128]{1,0:T(8,128)S(1)}) custom-call(s32[2]{0:T(128)} %ids.1, bf16[3,3072,256]{2,1,0:T(8,128)(2,1)} %bitcast.10, bf16[2,32,1536]{2,1,0:T(8,128)(2,1)} %refs_1_.1, f32[3,4,1536]{2,1,0:T(4,128)} %bitcast.13), custom_call_target="tpu_custom_call" | custom-call | bytes 4718592 | tf_op jit(solution)/shard_map/pallas_call | solution.py:218
  13.1 0.1 pad_maximum_fusion.2
  13.1 0.0 collective-permute-done.2
  13.1 0.5 collective-permute-start.6
  13.7 0.2 collective-permute-start.1
  13.9 0.0 collective-permute-done.4.refs_8_.refs_10_
  14.0 4.1 %collective-permute-done.6.refs_10_.refs_12_ = bf16[2,32,256]{2,1,0:T(8,128)(2,1)S(1)} collective-permute-done((bf16[2,32,256]{2,1,0:T(8,128)(2,1)S(1)}, bf16[2,32,256]{2,1,0:T(8,128)(2,1)S(1)}, u32[]{:S(2)}, u32[]{:S(2)}) %collective-permute-start.6) | collective-permute-done | bytes 32800 | tf_op jit(solution)/shard_map/ppermute | solution.py:31
  18.0 0.0 collective-permute-done.refs_1_
  18.0 1.2 %shard_map.74 = (bf16[2,32,256]{2,1,0:T(8,128)(2,1)S(1)}, bf16[2,32,256]{2,1,0:T(8,128)(2,1)S(1)}, bf16[2,32,256]{2,1,0:T(8,128)(2,1)S(1)}) custom-call(s32[1]{0:T(128)} %bitcast.1.head, s32[8,128]{1,0:T(8,128)S(1)} %get-tuple-element.18.ids_ref, bf16[2,32,1536]{2,1,0:T(8,128)(2,1)S(1)} %get-tuple-element.19.refs_0_, ...), custom_call_target="tpu_custom_call" | custom-call | flops 301989888 | bytes 4718592 | tf_op jit(solution)/shard_map/pallas_call | solution.py:255
  19.2 0.6 %collective-permute-start.10 = (bf16[2,32,256]{2,1,0:T(8,128)(2,1)S(1)}, bf16[2,32,256]{2,1,0:T(8,128)(2,1)S(1)}, u32[]{:S(2)}, u32[]{:S(2)}) collective-permute-start(bf16[2,32,256]{2,1,0:T(8,128)(2,1)S(1)} %get-tuple-element.24.refs_5_), channel_id=1, source_target_pairs={{0,2},{2,0},{4,6},{6,4},{8,10},{10,8},{12,14},{14,12},{16,18},{18,... | collective-permute-start | bytes 98312 | tf_op jit(solution)/shard_map/ppermute | solution.py:31
  19.8 0.5 collective-permute-start.11
  20.3 1.5 %collective-permute-start.19 = (bf16[2,192,256]{2,1,0:T(8,128)(2,1)S(1)}, bf16[2,192,256]{2,1,0:T(8,128)(2,1)S(1)}, u32[]{:S(2)}, u32[]{:S(2)}) collective-permute-start(bf16[2,192,256]{2,1,0:T(8,128)(2,1)S(1)} %pad_maximum_fusion.refs_7_.refs_5_), channel_id=1, source_target_pairs={{0,2},{2,0},{4,6},{6,4},{8,10},{10,8},{12,14},{14,12},{16,18},{18,... | collective-permute-start | bytes 589832 | tf_op jit(solution)/shard_map/ppermute | solution.py:31
  21.8 1.5 %collective-permute-start.12 = (bf16[2,32,256]{2,1,0:T(8,128)(2,1)S(1)}, bf16[2,32,256]{2,1,0:T(8,128)(2,1)S(1)}, u32[]{:S(2)}, u32[]{:S(2)}) collective-permute-start(bf16[2,32,256]{2,1,0:T(8,128)(2,1)S(1)} %get-tuple-element.24.refs_5_), channel_id=1, source_target_pairs={{0,6},{2,4},{4,2},{6,0},{8,14},{10,12},{12,10},{14,8},{16,22},{18,... | collective-permute-start | bytes 98312 | tf_op jit(solution)/shard_map/ppermute | solution.py:31
  23.3 1.6 %collective-permute-start.7 = (bf16[2,32,256]{2,1,0:T(8,128)(2,1)S(1)}, bf16[2,32,256]{2,1,0:T(8,128)(2,1)S(1)}, u32[]{:S(2)}, u32[]{:S(2)}) collective-permute-start(bf16[2,32,256]{2,1,0:T(8,128)(2,1)S(1)} %get-tuple-element.22.refs_0_), channel_id=1, source_target_pairs={{0,8},{2,10},{4,12},{6,14},{8,0},{10,2},{12,4},{14,6},{16,24},{18,... | collective-permute-start | bytes 98312 | tf_op jit(solution)/shard_map/ppermute | solution.py:31
  24.9 0.0 collective-permute-done.10.refs_6_
  24.9 0.5 collective-permute-start.20
  25.4 0.0 collective-permute-done.11.refs_7_
  25.4 2.4 %collective-permute-start.21 = (bf16[2,192,256]{2,1,0:T(8,128)(2,1)S(1)}, bf16[2,192,256]{2,1,0:T(8,128)(2,1)S(1)}, u32[]{:S(2)}, u32[]{:S(2)}) collective-permute-start(bf16[2,192,256]{2,1,0:T(8,128)(2,1)S(1)} %pad_maximum_fusion.refs_7_.refs_5_), channel_id=1, source_target_pairs={{0,6},{2,4},{4,2},{6,0},{8,14},{10,12},{12,10},{14,8},{16,22},{18,... | collective-permute-start | bytes 589832 | tf_op jit(solution)/shard_map/ppermute | solution.py:31
  27.9 1.5 %collective-permute-done.12.refs_8_ = bf16[2,32,256]{2,1,0:T(8,128)(2,1)S(1)} collective-permute-done((bf16[2,32,256]{2,1,0:T(8,128)(2,1)S(1)}, bf16[2,32,256]{2,1,0:T(8,128)(2,1)S(1)}, u32[]{:S(2)}, u32[]{:S(2)}) %collective-permute-start.12) | collective-permute-done | bytes 32800 | tf_op jit(solution)/shard_map/ppermute | solution.py:31
  29.3 1.4 %collective-permute-start.8 = (bf16[2,32,256]{2,1,0:T(8,128)(2,1)S(1)}, bf16[2,32,256]{2,1,0:T(8,128)(2,1)S(1)}, u32[]{:S(2)}, u32[]{:S(2)}) collective-permute-start(bf16[2,32,256]{2,1,0:T(8,128)(2,1)S(1)} %get-tuple-element.22.refs_0_), channel_id=1, source_target_pairs={{0,16},{2,18},{4,20},{6,22},{8,24},{10,26},{12,28},{14,30},{16,0},... | collective-permute-start | bytes 98312 | tf_op jit(solution)/shard_map/ppermute | solution.py:31
  30.7 0.0 collective-permute-done.7.refs_1_
  30.7 3.1 %collective-permute-start.9 = (bf16[2,32,256]{2,1,0:T(8,128)(2,1)S(1)}, bf16[2,32,256]{2,1,0:T(8,128)(2,1)S(1)}, u32[]{:S(2)}, u32[]{:S(2)}) collective-permute-start(bf16[2,32,256]{2,1,0:T(8,128)(2,1)S(1)} %get-tuple-element.22.refs_0_), channel_id=1, source_target_pairs={{0,24},{2,26},{4,28},{6,30},{8,16},{10,18},{12,20},{14,22},{16,8},... | collective-permute-start | bytes 98312 | tf_op jit(solution)/shard_map/ppermute | solution.py:31
  33.9 0.3 collective-permute-done.8.refs_2_
  34.2 2.5 %collective-permute-done.9.refs_3_ = bf16[2,32,256]{2,1,0:T(8,128)(2,1)S(1)} collective-permute-done((bf16[2,32,256]{2,1,0:T(8,128)(2,1)S(1)}, bf16[2,32,256]{2,1,0:T(8,128)(2,1)S(1)}, u32[]{:S(2)}, u32[]{:S(2)}) %collective-permute-start.9) | collective-permute-done | bytes 32800 | tf_op jit(solution)/shard_map/ppermute | solution.py:31
  36.6 0.7 %shard_map.75 = (bf16[64,384]{1,0:T(8,128)(2,1)S(1)}, bf16[64,384]{1,0:T(8,128)(2,1)S(1)}, bf16[64,384]{1,0:T(8,128)(2,1)S(1)}, bf16[64,384]{1,0:T(8,128)(2,1)S(1)}) custom-call(bf16[2,32,256]{2,1,0:T(8,128)(2,1)S(1)} %get-tuple-element.22.refs_0_, bf16[2,32,256]{2,1,0:T(8,128)(2,1)S(1)} %collective-permute-done.7.refs_1_, ...), custom_call_target="tpu_custom_call" | custom-call | flops 67108864 | tf_op jit(solution)/shard_map/pallas_call | solution.py:265
  37.4 1.8 %collective-permute-start.13 = (bf16[64,384]{1,0:T(8,128)(2,1)S(1)}, bf16[64,384]{1,0:T(8,128)(2,1)S(1)}, u32[]{:S(2)}, u32[]{:S(2)}) collective-permute-start(bf16[64,384]{1,0:T(8,128)(2,1)S(1)} %get-tuple-element.26), channel_id=1, source_target_pairs={{0,8},{2,10},{4,12},{6,14},{8,0},{10,2},{12,4},{14,6},{16,24},{18,... | collective-permute-start | bytes 147464 | tf_op jit(solution)/shard_map/ppermute | solution.py:31
  39.2 1.8 %collective-permute-start.14 = (bf16[64,384]{1,0:T(8,128)(2,1)S(1)}, bf16[64,384]{1,0:T(8,128)(2,1)S(1)}, u32[]{:S(2)}, u32[]{:S(2)}) collective-permute-start(bf16[64,384]{1,0:T(8,128)(2,1)S(1)} %get-tuple-element.27), channel_id=1, source_target_pairs={{0,16},{2,18},{4,20},{6,22},{8,24},{10,26},{12,28},{14,30},{16,0},... | collective-permute-start | bytes 147464 | tf_op jit(solution)/shard_map/ppermute | solution.py:31
  41.0 0.6 collective-permute-done.13.refs_1_
  41.5 2.9 %collective-permute-start.15 = (bf16[64,384]{1,0:T(8,128)(2,1)S(1)}, bf16[64,384]{1,0:T(8,128)(2,1)S(1)}, u32[]{:S(2)}, u32[]{:S(2)}) collective-permute-start(bf16[64,384]{1,0:T(8,128)(2,1)S(1)} %get-tuple-element.28), channel_id=1, source_target_pairs={{0,24},{2,26},{4,28},{6,30},{8,16},{10,18},{12,20},{14,22},{16,8},... | collective-permute-start | bytes 147464 | tf_op jit(solution)/shard_map/ppermute | solution.py:31
  44.5 3.0 %collective-permute-done.15.refs_3_ = bf16[64,384]{1,0:T(8,128)(2,1)S(1)} collective-permute-done((bf16[64,384]{1,0:T(8,128)(2,1)S(1)}, bf16[64,384]{1,0:T(8,128)(2,1)S(1)}, u32[]{:S(2)}, u32[]{:S(2)}) %collective-permute-start.15) | collective-permute-done | bytes 49184 | tf_op jit(solution)/shard_map/ppermute | solution.py:31
  47.5 0.2 shard_map.76.refs_0_
  47.8 0.7 %collective-permute-start.16 = (bf16[64,256]{1,0:T(8,128)(2,1)S(1)}, bf16[64,256]{1,0:T(8,128)(2,1)S(1)}, u32[]{:S(2)}, u32[]{:S(2)}) collective-permute-start(bf16[64,256]{1,0:T(8,128)(2,1)S(1)} %shard_map.76.refs_0_), channel_id=1, source_target_pairs={{0,8},{1,9},{2,10},{3,11},{4,12},{5,13},{6,14},{7,15},{8,0},{9,1},... | collective-permute-start | bytes 98312 | tf_op jit(solution)/shard_map/ppermute | solution.py:284
  48.4 1.6 %collective-permute-start.18 = (bf16[64,256]{1,0:T(8,128)(2,1)S(1)}, bf16[64,256]{1,0:T(8,128)(2,1)S(1)}, u32[]{:S(2)}, u32[]{:S(2)}) collective-permute-start(bf16[64,256]{1,0:T(8,128)(2,1)S(1)} %shard_map.76.refs_0_), channel_id=1, source_target_pairs={{0,9},{1,8},{2,11},{3,10},{4,13},{5,12},{6,15},{7,14},{8,1},{9,0},... | collective-permute-start | bytes 98312 | tf_op jit(solution)/shard_map/ppermute | solution.py:284
  50.0 0.0 collective-permute-done.20.refs_7_
  50.0 0.0 collective-permute-done.21.refs_8_
  50.0 2.1 %collective-permute-done.16.refs_1_ = bf16[64,256]{1,0:T(8,128)(2,1)S(1)} collective-permute-done((bf16[64,256]{1,0:T(8,128)(2,1)S(1)}, bf16[64,256]{1,0:T(8,128)(2,1)S(1)}, u32[]{:S(2)}, u32[]{:S(2)}) %collective-permute-start.16) | collective-permute-done | bytes 32800 | tf_op jit(solution)/shard_map/ppermute | solution.py:284
  52.1 0.0 collective-permute-done.17.refs_2_
  52.1 0.0 collective-permute-done.18.refs_3_
  52.1 0.5 shard_map.77
  52.6 1.2 %collective-permute-start.22 = (bf16[2,32,768]{2,1,0:T(8,128)(2,1)S(1)}, bf16[2,32,768]{2,1,0:T(8,128)(2,1)S(1)}, u32[]{:S(2)}, u32[]{:S(2)}) collective-permute-start(bf16[2,32,768]{2,1,0:T(8,128)(2,1)S(1)} %get-tuple-element.29), channel_id=1, source_target_pairs={{0,8},{2,10},{4,12},{6,14},{8,0},{10,2},{12,4},{14,6},{16,24},{18,... | collective-permute-start | bytes 294920 | tf_op jit(solution)/shard_map/ppermute | solution.py:31
  53.8 3.8 %collective-permute-done.22 = bf16[2,32,768]{2,1,0:T(8,128)(2,1)S(1)} collective-permute-done((bf16[2,32,768]{2,1,0:T(8,128)(2,1)S(1)}, bf16[2,32,768]{2,1,0:T(8,128)(2,1)S(1)}, u32[]{:S(2)}, u32[]{:S(2)}) %collective-permute-start.22) | collective-permute-done | bytes 98336 | tf_op jit(solution)/shard_map/ppermute | solution.py:31
  57.6 0.7 %pad_maximum_fusion.1 = bf16[2,32,1536]{2,1,0:T(8,128)(2,1)} fusion(bf16[2,32,768]{2,1,0:T(8,128)(2,1)S(1)} %get-tuple-element.32, bf16[2,32,768]{2,1,0:T(8,128)(2,1)S(1)} %get-tuple-element.31), kind=kLoop, calls=%fused_computation.1 | loop fusion | flops 393216 | bytes 393216 | tf_op jit(solution)/shard_map/concatenate | solution.py:299
  (14 shorter events, 0.1 us)
Async XLA Ops:
  0.0 13.1 %copy-start = (bf16[2,32,256]{2,1,0:T(8,128)(2,1)S(1)}, bf16[2,32,256]{2,1,0:T(8,128)(2,1)}, u32[]{:S(2)}) copy-start(bf16[2,32,256]{2,1,0:T(8,128)(2,1)} %refs_9_.1) | copy-start | bytes 98308
  0.0 13.7 %copy-start.1 = (f32[4,3,1536]{2,0,1:T(4,128)S(1)}, f32[4,3,1536]{2,0,1:T(4,128)}, u32[]{:S(2)}) copy-start(f32[4,3,1536]{2,0,1:T(4,128)} %param.11) | copy-start | bytes 221188
  0.0 13.1 %collective-permute-start.2 = (bf16[192,256]{1,0:T(8,128)(2,1)}, bf16[192,256]{1,0:T(8,128)(2,1)S(1)}, u32[]{:S(2)}, u32[]{:S(2)}) collective-permute-start(bf16[192,256]{1,0:T(8,128)(2,1)} %bitcast.14), channel_id=1, source_target_pairs={{0,0},{1,16},{2,2},{3,18},{4,4},{5,20},{6,6},{7,22},{8,8},{9,24},{... | collective-permute-start | bytes 294920 | tf_op jit(solution)/shard_map/ppermute | solution.py:237
  1.7 12.0 %collective-permute-start.3 = (bf16[192,256]{1,0:T(8,128)(2,1)}, bf16[192,256]{1,0:T(8,128)(2,1)S(1)}, u32[]{:S(2)}, u32[]{:S(2)}) collective-permute-start(bf16[192,256]{1,0:T(8,128)(2,1)} %bitcast.15), channel_id=1, source_target_pairs={{0,16},{1,0},{2,18},{3,2},{4,20},{5,4},{6,22},{7,6},{8,24},{9,8},{... | collective-permute-start | bytes 294920 | tf_op jit(solution)/shard_map/ppermute | solution.py:237
  6.2 7.8 %collective-permute-start.4 = (bf16[2,32,256]{2,1,0:T(8,128)(2,1)}, bf16[2,32,256]{2,1,0:T(8,128)(2,1)S(1)}, u32[]{:S(2)}, u32[]{:S(2)}) collective-permute-start(bf16[2,32,256]{2,1,0:T(8,128)(2,1)} %refs_9_.1), channel_id=1, source_target_pairs={{0,2},{2,0},{4,6},{6,4},{8,10},{10,8},{12,14},{14,12},{16,18},{18,... | collective-permute-start | bytes 98312 | tf_op jit(solution)/shard_map/ppermute | solution.py:31
  7.6 6.3 %collective-permute-start.5 = (bf16[2,32,256]{2,1,0:T(8,128)(2,1)}, bf16[2,32,256]{2,1,0:T(8,128)(2,1)S(1)}, u32[]{:S(2)}, u32[]{:S(2)}) collective-permute-start(bf16[2,32,256]{2,1,0:T(8,128)(2,1)} %refs_9_.1), channel_id=1, source_target_pairs={{0,4},{2,6},{4,0},{6,2},{8,12},{10,14},{12,8},{14,10},{16,20},{18,... | collective-permute-start | bytes 98312 | tf_op jit(solution)/shard_map/ppermute | solution.py:31
  9.2 8.9 %collective-permute-start = (bf16[2,32,1536]{2,1,0:T(8,128)(2,1)}, bf16[2,32,1536]{2,1,0:T(8,128)(2,1)S(1)}, u32[]{:S(2)}, u32[]{:S(2)}) collective-permute-start(bf16[2,32,1536]{2,1,0:T(8,128)(2,1)} %refs_1_.1), channel_id=1, source_target_pairs={{0,1},{1,0},{2,3},{3,2},{4,5},{5,4},{6,7},{7,6},{8,9},{9,8},{10,11... | collective-permute-start | bytes 589832 | tf_op jit(solution)/shard_map/ppermute | solution.py:31
  13.1 4.9 %collective-permute-start.6 = (bf16[2,32,256]{2,1,0:T(8,128)(2,1)S(1)}, bf16[2,32,256]{2,1,0:T(8,128)(2,1)S(1)}, u32[]{:S(2)}, u32[]{:S(2)}) collective-permute-start(bf16[2,32,256]{2,1,0:T(8,128)(2,1)S(1)} %copy-done), channel_id=1, source_target_pairs={{0,6},{2,4},{4,2},{6,0},{8,14},{10,12},{12,10},{14,8},{16,22},{18,... | collective-permute-start | bytes 98312 | tf_op jit(solution)/shard_map/ppermute | solution.py:31
  13.7 4.3 %collective-permute-start.1 = (f32[4,3,1536]{2,0,1:T(4,128)S(1)}, f32[4,3,1536]{2,0,1:T(4,128)S(1)}, u32[]{:S(2)}, u32[]{:S(2)}) collective-permute-start(f32[4,3,1536]{2,0,1:T(4,128)S(1)} %copy-done.1), channel_id=1, source_target_pairs={{0,1},{1,0},{2,3},{3,2},{4,5},{5,4},{6,7},{7,6},{8,9},{9,8},{10,11... | collective-permute-start | bytes 221192 | tf_op jit(solution)/shard_map/ppermute | solution.py:31
  19.2 5.7 %collective-permute-start.10 = (bf16[2,32,256]{2,1,0:T(8,128)(2,1)S(1)}, bf16[2,32,256]{2,1,0:T(8,128)(2,1)S(1)}, u32[]{:S(2)}, u32[]{:S(2)}) collective-permute-start(bf16[2,32,256]{2,1,0:T(8,128)(2,1)S(1)} %get-tuple-element.24.refs_5_), channel_id=1, source_target_pairs={{0,2},{2,0},{4,6},{6,4},{8,10},{10,8},{12,14},{14,12},{16,18},{18,... | collective-permute-start | bytes 98312 | tf_op jit(solution)/shard_map/ppermute | solution.py:31
  19.8 5.6 %collective-permute-start.11 = (bf16[2,32,256]{2,1,0:T(8,128)(2,1)S(1)}, bf16[2,32,256]{2,1,0:T(8,128)(2,1)S(1)}, u32[]{:S(2)}, u32[]{:S(2)}) collective-permute-start(bf16[2,32,256]{2,1,0:T(8,128)(2,1)S(1)} %get-tuple-element.24.refs_5_), channel_id=1, source_target_pairs={{0,4},{2,6},{4,0},{6,2},{8,12},{10,14},{12,8},{14,10},{16,20},{18,... | collective-permute-start | bytes 98312 | tf_op jit(solution)/shard_map/ppermute | solution.py:31
  20.3 28.1 %collective-permute-start.19 = (bf16[2,192,256]{2,1,0:T(8,128)(2,1)S(1)}, bf16[2,192,256]{2,1,0:T(8,128)(2,1)S(1)}, u32[]{:S(2)}, u32[]{:S(2)}) collective-permute-start(bf16[2,192,256]{2,1,0:T(8,128)(2,1)S(1)} %pad_maximum_fusion.refs_7_.refs_5_), channel_id=1, source_target_pairs={{0,2},{2,0},{4,6},{6,4},{8,10},{10,8},{12,14},{14,12},{16,18},{18,... | collective-permute-start | bytes 589832 | tf_op jit(solution)/shard_map/ppermute | solution.py:31
  21.8 7.5 %collective-permute-start.12 = (bf16[2,32,256]{2,1,0:T(8,128)(2,1)S(1)}, bf16[2,32,256]{2,1,0:T(8,128)(2,1)S(1)}, u32[]{:S(2)}, u32[]{:S(2)}) collective-permute-start(bf16[2,32,256]{2,1,0:T(8,128)(2,1)S(1)} %get-tuple-element.24.refs_5_), channel_id=1, source_target_pairs={{0,6},{2,4},{4,2},{6,0},{8,14},{10,12},{12,10},{14,8},{16,22},{18,... | collective-permute-start | bytes 98312 | tf_op jit(solution)/shard_map/ppermute | solution.py:31
  23.3 7.4 %collective-permute-start.7 = (bf16[2,32,256]{2,1,0:T(8,128)(2,1)S(1)}, bf16[2,32,256]{2,1,0:T(8,128)(2,1)S(1)}, u32[]{:S(2)}, u32[]{:S(2)}) collective-permute-start(bf16[2,32,256]{2,1,0:T(8,128)(2,1)S(1)} %get-tuple-element.22.refs_0_), channel_id=1, source_target_pairs={{0,8},{2,10},{4,12},{6,14},{8,0},{10,2},{12,4},{14,6},{16,24},{18,... | collective-permute-start | bytes 98312 | tf_op jit(solution)/shard_map/ppermute | solution.py:31
  24.9 25.1 %collective-permute-start.20 = (bf16[2,192,256]{2,1,0:T(8,128)(2,1)S(1)}, bf16[2,192,256]{2,1,0:T(8,128)(2,1)S(1)}, u32[]{:S(2)}, u32[]{:S(2)}) collective-permute-start(bf16[2,192,256]{2,1,0:T(8,128)(2,1)S(1)} %pad_maximum_fusion.refs_7_.refs_5_), channel_id=1, source_target_pairs={{0,4},{2,6},{4,0},{6,2},{8,12},{10,14},{12,8},{14,10},{16,20},{18,... | collective-permute-start | bytes 589832 | tf_op jit(solution)/shard_map/ppermute | solution.py:31
  25.4 24.6 %collective-permute-start.21 = (bf16[2,192,256]{2,1,0:T(8,128)(2,1)S(1)}, bf16[2,192,256]{2,1,0:T(8,128)(2,1)S(1)}, u32[]{:S(2)}, u32[]{:S(2)}) collective-permute-start(bf16[2,192,256]{2,1,0:T(8,128)(2,1)S(1)} %pad_maximum_fusion.refs_7_.refs_5_), channel_id=1, source_target_pairs={{0,6},{2,4},{4,2},{6,0},{8,14},{10,12},{12,10},{14,8},{16,22},{18,... | collective-permute-start | bytes 589832 | tf_op jit(solution)/shard_map/ppermute | solution.py:31
  29.3 4.8 %collective-permute-start.8 = (bf16[2,32,256]{2,1,0:T(8,128)(2,1)S(1)}, bf16[2,32,256]{2,1,0:T(8,128)(2,1)S(1)}, u32[]{:S(2)}, u32[]{:S(2)}) collective-permute-start(bf16[2,32,256]{2,1,0:T(8,128)(2,1)S(1)} %get-tuple-element.22.refs_0_), channel_id=1, source_target_pairs={{0,16},{2,18},{4,20},{6,22},{8,24},{10,26},{12,28},{14,30},{16,0},... | collective-permute-start | bytes 98312 | tf_op jit(solution)/shard_map/ppermute | solution.py:31
  30.7 5.9 %collective-permute-start.9 = (bf16[2,32,256]{2,1,0:T(8,128)(2,1)S(1)}, bf16[2,32,256]{2,1,0:T(8,128)(2,1)S(1)}, u32[]{:S(2)}, u32[]{:S(2)}) collective-permute-start(bf16[2,32,256]{2,1,0:T(8,128)(2,1)S(1)} %get-tuple-element.22.refs_0_), channel_id=1, source_target_pairs={{0,24},{2,26},{4,28},{6,30},{8,16},{10,18},{12,20},{14,22},{16,8},... | collective-permute-start | bytes 98312 | tf_op jit(solution)/shard_map/ppermute | solution.py:31
  37.4 4.2 %collective-permute-start.13 = (bf16[64,384]{1,0:T(8,128)(2,1)S(1)}, bf16[64,384]{1,0:T(8,128)(2,1)S(1)}, u32[]{:S(2)}, u32[]{:S(2)}) collective-permute-start(bf16[64,384]{1,0:T(8,128)(2,1)S(1)} %get-tuple-element.26), channel_id=1, source_target_pairs={{0,8},{2,10},{4,12},{6,14},{8,0},{10,2},{12,4},{14,6},{16,24},{18,... | collective-permute-start | bytes 147464 | tf_op jit(solution)/shard_map/ppermute | solution.py:31
  39.2 5.3 %collective-permute-start.14 = (bf16[64,384]{1,0:T(8,128)(2,1)S(1)}, bf16[64,384]{1,0:T(8,128)(2,1)S(1)}, u32[]{:S(2)}, u32[]{:S(2)}) collective-permute-start(bf16[64,384]{1,0:T(8,128)(2,1)S(1)} %get-tuple-element.27), channel_id=1, source_target_pairs={{0,16},{2,18},{4,20},{6,22},{8,24},{10,26},{12,28},{14,30},{16,0},... | collective-permute-start | bytes 147464 | tf_op jit(solution)/shard_map/ppermute | solution.py:31
  41.5 6.0 %collective-permute-start.15 = (bf16[64,384]{1,0:T(8,128)(2,1)S(1)}, bf16[64,384]{1,0:T(8,128)(2,1)S(1)}, u32[]{:S(2)}, u32[]{:S(2)}) collective-permute-start(bf16[64,384]{1,0:T(8,128)(2,1)S(1)} %get-tuple-element.28), channel_id=1, source_target_pairs={{0,24},{2,26},{4,28},{6,30},{8,16},{10,18},{12,20},{14,22},{16,8},... | collective-permute-start | bytes 147464 | tf_op jit(solution)/shard_map/ppermute | solution.py:31
  47.8 4.3 %collective-permute-start.16 = (bf16[64,256]{1,0:T(8,128)(2,1)S(1)}, bf16[64,256]{1,0:T(8,128)(2,1)S(1)}, u32[]{:S(2)}, u32[]{:S(2)}) collective-permute-start(bf16[64,256]{1,0:T(8,128)(2,1)S(1)} %shard_map.76.refs_0_), channel_id=1, source_target_pairs={{0,8},{1,9},{2,10},{3,11},{4,12},{5,13},{6,14},{7,15},{8,0},{9,1},... | collective-permute-start | bytes 98312 | tf_op jit(solution)/shard_map/ppermute | solution.py:284
  48.4 3.7 %collective-permute-start.17 = (bf16[64,256]{1,0:T(8,128)(2,1)S(1)}, bf16[64,256]{1,0:T(8,128)(2,1)S(1)}, u32[]{:S(2)}, u32[]{:S(2)}) collective-permute-start(bf16[64,256]{1,0:T(8,128)(2,1)S(1)} %shard_map.76.refs_0_), channel_id=1, source_target_pairs={{0,1},{1,0},{2,3},{3,2},{4,5},{5,4},{6,7},{7,6},{8,9},{9,8},{10,11... | collective-permute-start | bytes 98312 | tf_op jit(solution)/shard_map/ppermute | solution.py:284
  48.4 3.7 %collective-permute-start.18 = (bf16[64,256]{1,0:T(8,128)(2,1)S(1)}, bf16[64,256]{1,0:T(8,128)(2,1)S(1)}, u32[]{:S(2)}, u32[]{:S(2)}) collective-permute-start(bf16[64,256]{1,0:T(8,128)(2,1)S(1)} %shard_map.76.refs_0_), channel_id=1, source_target_pairs={{0,9},{1,8},{2,11},{3,10},{4,13},{5,12},{6,15},{7,14},{8,1},{9,0},... | collective-permute-start | bytes 98312 | tf_op jit(solution)/shard_map/ppermute | solution.py:284
  52.6 5.0 %collective-permute-start.22 = (bf16[2,32,768]{2,1,0:T(8,128)(2,1)S(1)}, bf16[2,32,768]{2,1,0:T(8,128)(2,1)S(1)}, u32[]{:S(2)}, u32[]{:S(2)}) collective-permute-start(bf16[2,32,768]{2,1,0:T(8,128)(2,1)S(1)} %get-tuple-element.29), channel_id=1, source_target_pairs={{0,8},{2,10},{4,12},{6,14},{8,0},{10,2},{12,4},{14,6},{16,24},{18,... | collective-permute-start | bytes 294920 | tf_op jit(solution)/shard_map/ppermute | solution.py:31

commit v5 on v4

v5 whole, which is shorter than its diff:
```python
import functools
import math

import jax
import jax.numpy as jnp
from jax import lax
from jax.experimental import pallas as pl
from jax.experimental.pallas import tpu as pltpu
from jax.sharding import PartitionSpec as P

DH = 128
STEPS = 2
PLANE = 4
MIB = 1024 * 1024
VMEM = pl.BlockSpec(memory_space=pltpu.VMEM)
SMEM = pl.BlockSpec(memory_space=pltpu.SMEM)
ANY = pl.BlockSpec(memory_space=pl.ANY)
BF16, F32 = jnp.bfloat16, jnp.float32
NT = (((1,), (1,)), ((), ()))


def angle_tables(positions):
    half = DH // 2
    frequency = 10000.0 ** (-(2.0 * jnp.arange(half, dtype=F32)) / DH)
    grid = positions.astype(F32)[:, None] * frequency[None, :]
    cos, sin = jnp.cos(grid), jnp.sin(grid)
    return jnp.concatenate([cos, cos], axis=1), jnp.concatenate([-sin, sin], axis=1)


def swap(values, axis, count, bit):
    return lax.ppermute(values, axis, [(i, i ^ bit) for i in range(count)])


def load_kernel(ids, *refs):
    count = len(refs) // 2 - 1
    ids_out, sems = refs[-2:]
    copies = [
        pltpu.make_async_copy(refs[i], refs[count + i], sems.at[i]) for i in range(count)
    ]
    for copy in copies:
        copy.start()
    row = lax.broadcasted_iota(jnp.int32, ids_out.shape, 0)
    tile = jnp.zeros(ids_out.shape, jnp.int32)
    for step in range(STEPS):
        tile = jnp.where(row == step, ids[step], tile)
    ids_out[...] = tile
    for copy in copies:
        copy.wait()


def table_row(mod_ref, kind, ids_ref, step):
    chosen = ids_ref[step : step + 1, :1]
    table = mod_ref[kind]
    return sum(
        jnp.where(chosen == r, table[r : r + 1], 0.0) for r in range(table.shape[0])
    )


def qkv_kernel(n_head, head, ids_ref, *refs):
    x_refs, mod_refs = refs[:n_head], refs[n_head : 2 * n_head]
    w_ref, cos_ref, sin_ref, stale_ref = refs[2 * n_head : 2 * n_head + 4]
    q_ref, kv0_ref, kv1_ref, a_ref = refs[-4:]
    rows, feats = x_refs[0].shape[1:]
    width = n_head * feats
    cols = w_ref.shape[2]
    kv0_ref[:2] = stale_ref[...]
    for step in range(STEPS):
        total, square = 0.0, 0.0
        for x_ref in x_refs:
            hidden = x_ref[step].astype(F32)
            total += jnp.sum(hidden, axis=1, keepdims=True)
            square += jnp.sum(hidden * hidden, axis=1, keepdims=True)
        mean = total / width
        inv = lax.rsqrt(square / width - mean * mean + 1e-06)
        for part in range(n_head):
            shift = table_row(mod_refs[part], 0, ids_ref, step)
            scale = table_row(mod_refs[part], 1, ids_ref, step)
            hidden = x_refs[part][step].astype(F32)
            a = (hidden - mean) * inv * (1.0 + scale) + shift
            a_ref[part, step * rows : (step + 1) * rows, :] = a.astype(BF16)
    cos, sin = cos_ref[...], sin_ref[...]
    for slot in range(3):
        total = jnp.zeros((STEPS * rows, cols), F32)
        for part in range(n_head):
            start = pl.multiple_of((head[0] ^ part) * feats, feats)
            total += jnp.dot(
                a_ref[part], w_ref[slot, pl.ds(start, feats), :], preferred_element_type=F32
            )
        for step in range(STEPS):
            for block in range(cols // DH):
                lanes = slice(block * DH, (block + 1) * DH)
                u = total[step * rows : (step + 1) * rows, lanes]
                if slot < 2:
                    u = u * cos + pltpu.roll(u, DH // 2, 1) * sin
                u = u.astype(BF16)
                if slot == 0:
                    for place in range(q_ref.shape[0]):
                        q_ref[place, step, :, lanes] = u
                elif step == 0:
                    kv0_ref[slot + 1, :, lanes] = u
                else:
                    kv1_ref[slot - 1, :, lanes] = u


def split3(values):
    high = values.astype(BF16).astype(F32)
    middle = (values - high).astype(BF16).astype(F32)
    return [high, middle, values - high - middle]


def attend_kernel(patch, q_ref, kv1_ref, *refs):
    kv_refs, out_ref = refs[:PLANE], refs[PLANE]
    line, _, rows, cols = q_ref.shape
    shape = (line * rows, PLANE * rows + rows)
    mine = lax.broadcasted_iota(jnp.int32, shape, 0) // rows == patch[0] // PLANE
    drop = lax.broadcasted_iota(jnp.int32, shape, 1) // rows == jnp.where(mine, 0, PLANE)
    lane = lax.broadcasted_iota(jnp.int32, (line * rows, DH), 1)
    for step in range(STEPS):
        fresh = (kv_refs[0].at[2:], kv1_ref)[step]
        stats = jnp.zeros((line * rows, DH), F32)
        mixed = []
        for block in range(cols // DH):
            lanes = slice(block * DH, (block + 1) * DH)

            def rows_of(kind):
                old = [ref[2 * step + kind, :, lanes] for ref in kv_refs]
                return jnp.concatenate([*old, fresh[kind, :, lanes]], axis=0)

            queries = q_ref[:, step, :, lanes].reshape(line * rows, DH)
            scores = lax.dot_general(queries, rows_of(0), NT, preferred_element_type=F32)
            scores = jnp.where(drop, -1e30, scores * (1.0 / math.sqrt(DH)))
            top = jnp.max(scores, axis=1, keepdims=True)
            weights = jnp.exp(scores - top)
            totals = jnp.sum(weights, axis=1, keepdims=True)
            mixed.append(
                jnp.dot(weights.astype(BF16), rows_of(1), preferred_element_type=F32) / totals
            )
            for place, piece in enumerate(split3(top) + split3(totals)):
                stats = jnp.where(lane == block * 8 + place, piece, stats)
        packed = jnp.concatenate([*mixed, stats], axis=1).astype(BF16)
        out_ref[:, step * rows : (step + 1) * rows, :] = packed.reshape(line, rows, cols + DH)


def merge_kernel(*refs):
    parts_ref, o_ref = refs
    part_refs = [parts_ref.at[k] for k in range(parts_ref.shape[0])]
    cols = o_ref.shape[1]
    source = lax.broadcasted_iota(jnp.int32, (DH, DH), 0)
    for block in range(cols // DH):
        lanes = slice(block * DH, (block + 1) * DH)

        def spread(ref, first):
            pick = (source >= block * 8 + first) & (source < block * 8 + first + 3)
            return jnp.dot(ref[:, cols:], pick.astype(F32).astype(BF16), preferred_element_type=F32)

        tops = [spread(ref, 0) for ref in part_refs]
        best = functools.reduce(jnp.maximum, tops)
        scales = [spread(ref, 3) * jnp.exp(t - best) for ref, t in zip(part_refs, tops)]
        mixed = sum(s * ref[:, lanes].astype(F32) for s, ref in zip(scales, part_refs))
        o_ref[:, lanes] = (mixed / sum(scales)).astype(BF16)


def project_kernel(n_head, n_patch, bit, patch, head, *refs):
    o_refs, w_refs, (out_ref, sums) = refs[:2], refs[2 : 2 + PLANE], refs[2 + PLANE :]
    rows = o_refs[0].shape[0]
    slot = head[0] ^ bit ^ (patch[0] // (n_patch // n_head))
    o = jnp.concatenate([ref[...] for ref in o_refs], axis=0)
    for near in range(PLANE):
        sums[(patch[0] % PLANE) ^ near] = lax.dot_general(
            o, w_refs[near][slot], NT, preferred_element_type=F32
        )
    out = jnp.concatenate([sums[c] for c in range(PLANE)], axis=1)
    out_ref[...] = out.astype(out_ref.dtype)


def gate_kernel(n_patch, patch, ids_ref, mod_ref, *refs):
    sum_refs, (own_out, mate_out) = refs[:-2], refs[-2:]
    total = sum(ref[...].astype(F32) for ref in sum_refs)
    rows, width = total.shape
    each = rows // 2 // STEPS
    second = (patch[0] // PLANE) % 2 == 1
    for step in range(STEPS):
        gate = table_row(mod_ref, 2, ids_ref, step)
        gate = jnp.where(second, gate[:, width:], gate[:, :width])
        for mate, ref in enumerate((own_out, mate_out)):
            start = mate * (rows // 2) + step * each
            ref[step] = (gate * total[start : start + each]).astype(BF16)


def in_hbm(values):
    return pltpu.with_memory_space_constraint(values, pltpu.HBM)


def call(kernel, shapes, ins, scratch=(), flops=0, size=0, limit=16):
    return pl.pallas_call(
        kernel,
        out_shape=shapes,
        in_specs=ins,
        out_specs=jax.tree.map(lambda _: VMEM, shapes),
        scratch_shapes=scratch,
        compiler_params=pltpu.CompilerParams(vmem_limit_bytes=limit * MIB),
        cost_estimate=pl.CostEstimate(flops=flops, bytes_accessed=size, transcendentals=0),
    )


def body(n_patch, n_head, inputs, stale_kv, w_qkv, w_out, mod_table, step_ids, slab_order):
    rows, feats = inputs.shape[1:]
    cols = w_qkv.shape[2]
    piece = w_out.shape[1]
    line = n_patch // PLANE
    patch = lax.axis_index("patch").astype(jnp.int32)
    head = lax.axis_index("head").astype(jnp.int32)
    shaped = jax.ShapeDtypeStruct

    x_parts = [swap(inputs, "head", n_head, k) for k in range(1, n_head)]
    mod_parts = [swap(mod_table, "head", n_head, k) for k in range(1, n_head)]
    first = (jnp.transpose(w_qkv, (1, 0, 2)), inputs, jnp.transpose(mod_table, (1, 0, 2)), stale_kv)
    w, x_own, mod_own, stale, ids = call(
        load_kernel,
        tuple(pltpu.VMEM(v.shape, v.dtype) for v in first) + (shaped((8, DH), jnp.int32),),
        [SMEM] + [ANY] * len(first),
        [pltpu.SemaphoreType.DMA((len(first),))],
        size=2 * w_qkv.size,
    )(*map(in_hbm, (step_ids, *first)))
    x_parts = [x_own] + x_parts
    mod_parts = [mod_own] + [jnp.transpose(part, (1, 0, 2)) for part in mod_parts]

    def plane_of(values):
        return [values] + [swap(values, "patch", n_patch, k) for k in range(1, PLANE)]

    lines = [[PLANE * i + j for i in range(line)] for j in range(PLANE)]

    def trade(values):
        return lax.all_to_all(values, "patch", 0, 0, axis_index_groups=lines)

    rise = 2 * PLANE
    w_pair = jnp.stack(
        [w_out.T] + [swap(w_out.T, "patch", n_patch, rise * k) for k in range(1, n_head)]
    )

    positions = slab_order[0] * rows + jnp.arange(rows, dtype=jnp.int32)
    cos, sin = angle_tables(positions)
    q, kv0, kv1 = call(
        functools.partial(qkv_kernel, n_head),
        tuple(shaped((*n, rows, cols), BF16) for n in ((line, STEPS), (4,), (2,))),
        [SMEM] + [VMEM] * (2 * n_head + 5),
        [pltpu.VMEM((n_head, STEPS * rows, feats), BF16)],
        2 * STEPS * rows * w_qkv.size,
        2 * w_qkv.size,
    )(head[None], ids, *x_parts, *mod_parts, w, cos, sin, stale)

    kv_plane = plane_of(kv0)
    q_line = trade(q)
    w_pair, q_line = lax.optimization_barrier((w_pair, q_line))
    w_plane = plane_of(w_pair)
    parts = call(
        attend_kernel,
        shaped((line, STEPS * rows, cols + DH), BF16),
        [SMEM] + [VMEM] * (PLANE + 2),
        flops=8 * STEPS * rows * n_patch * rows * cols,
    )(patch[None], q_line, kv1, *kv_plane)
    o = call(merge_kernel, shaped((STEPS * rows, cols), BF16), [VMEM])(trade(parts))
    o_mate = swap(o, "patch", n_patch, PLANE)

    wide = (2 * STEPS * rows, PLANE * piece)

    def project(bit, dtype):
        return call(
            functools.partial(project_kernel, n_head, n_patch, bit),
            shaped(wide, dtype),
            [SMEM] * 2 + [VMEM] * (2 + PLANE),
            [pltpu.VMEM((PLANE, 2 * STEPS * rows, piece), F32)],
            2 * wide[0] * wide[1] * cols,
            2 * wide[1] * cols,
        )(patch[None], head[None], o, o_mate, *w_plane)

    sums = [swap(project(k, BF16), "head", n_head, k) for k in range(1, n_head)]
    sums = [project(0, F32)] + sums
    out_half = shaped((STEPS, rows, PLANE * piece), BF16)
    out_own, out_mate = call(
        functools.partial(gate_kernel, n_patch),
        (out_half, out_half),
        [SMEM] + [VMEM] * (2 + n_head),
    )(patch[None], ids, mod_own, *sums)
    out_back = swap(out_mate, "patch", n_patch, PLANE)
    second = (patch // PLANE) % 2 == 1
    return jnp.concatenate(
        [jnp.where(second, out_back, out_own), jnp.where(second, out_own, out_back)], axis=2
    )


def solution(mesh):
    in_specs = (
        P(None, "patch", "head"),
        P(None, "patch", "head"),
        P(None, None, "head"),
        P("head", "patch"),
        P(None, None, "head"),
        P(),
        P("patch"),
    )
    run = functools.partial(body, mesh.shape["patch"], mesh.shape["head"])
    return jax.shard_map(
        run, mesh=mesh, in_specs=in_specs, out_specs=P(None, "patch", "head"), check_vma=False
    )
```

time: 58.5 us -> 46.9 us (0.80)
  starting transfers between devices: 33 us -> 23.5 us
  waiting for transfers between devices: 17.9 us -> 13.9 us
  Pallas kernels: 5.75 us -> 7.39 us
    ppermute x18 -> x12, starting transfers between devices: 24.6 us -> 15.2 us  [swap(): return lax.ppermute(values, axis, [(i, i ^ bit) for i in range(count)])]
    ppermute x5 -> x0, starting transfers between devices: 8.35 us -> none  [the longest x2 6.15 us: body(): lax.ppermute(w_out.T, ('patch', 'head'), [((hi * per_head + lo) * n_head...]
    all_to_all x0 -> x2, starting transfers between devices: none -> 8.31 us  [trade(): return lax.all_to_all(values, 'patch', 0, 0, axis_index_groups=lines)]
    ppermute x18 -> x12, waiting for transfers between devices: 15.7 us -> 8.57 us  [swap(): return lax.ppermute(values, axis, [(i, i ^ bit) for i in range(count)])]
    all_to_all x0 -> x2, waiting for transfers between devices: none -> 5.33 us  [trade(): return lax.all_to_all(values, 'patch', 0, 0, axis_index_groups=lines)]
    ppermute x5 -> x0, waiting for transfers between devices: 2.12 us -> none  [the longest x3 2.11 us: body(): lax.ppermute(o, ('patch', 'head'), pairs)]
    pallas_call x4 -> x6, Pallas kernels: 2.7 us -> 4.2 us  [the longest x1 1.62 us: body(): call(functools.partial(qkv_kernel, n_head), tuple((shaped((*n, rows, cols...]
  transfers between devices with their start and end apart: 23 -> 14, of which waited for: 8 -> 7; matrix products, arithmetic and copies ran while one was open for 0% -> 1% of each run, Pallas kernels for 7% -> 12%
where the time goes in v5:
time: 46.9 us; the launch traced here: 46.5 us
  starting transfers between devices  23.5 us (50%)
  waiting for transfers between devices  13.9 us (30%)
  Pallas kernels  7.39 us (16%)
  other arithmetic  0.96 us (2%)
  between operations  0.77 us (2%)
    ppermute x12, starting transfers between devices, swap(): return lax.ppermute(values, axis, [(i, i ^ bit) for i in range(count)])  15.2 us
    ppermute x12, waiting for transfers between devices, swap(): return lax.ppermute(values, axis, [(i, i ^ bit) for i in range(count)])  8.57 us
    all_to_all x2, starting transfers between devices, trade(): return lax.all_to_all(values, 'patch', 0, 0, axis_index_groups=lines)  8.31 us
    all_to_all x2, waiting for transfers between devices, trade(): return lax.all_to_all(values, 'patch', 0, 0, axis_index_groups=lines)  5.33 us
    pallas_call x1, Pallas kernels, body(): call(load_kernel, tuple((pltpu.VMEM(v.shape, v.dtype) for v in first)) +...  3.2 us
    pallas_call x1, Pallas kernels, body(): call(functools.partial(qkv_kernel, n_head), tuple((shaped((*n, rows, cols...  1.62 us
    pallas_call x1, Pallas kernels, body(): call(attend_kernel, shaped((line, STEPS * rows, cols + DH), BF16), [SMEM]...  1.42 us
  transfers between devices with their start and end apart: 14, of which 7 were waited for; matrix products, arithmetic and copies ran while one was open for 1% of the time, Pallas kernels for 12%

profile of v5, /device:TPU:0, one launch (start us, length us, event | category | flops | bytes accessed | tf_op | source)
XLA Modules:
  0.0 46.5 jit_solution(9754395951032542435)
XLA Ops:
  0.0 0.5 collective-permute-start.1
  0.5 0.1 collective-permute-start.2
  0.5 4.0 %collective-permute-start = (bf16[192,256]{1,0:T(8,128)(2,1)}, bf16[192,256]{1,0:T(8,128)(2,1)S(1)}, u32[]{:S(2)}, u32[]{:S(2)}) collective-permute-start(bf16[192,256]{1,0:T(8,128)(2,1)} %bitcast.12), channel_id=1, source_target_pairs={{0,16},{2,18},{4,20},{6,22},{8,24},{10,26},{12,28},{14,30},{16,0},... | collective-permute-start | bytes 294920 | tf_op jit(solution)/shard_map/ppermute | solution.py:31
  5.2 0.1 fusion
  5.4 0.0 copy-start
  5.4 3.2 %shard_map.73 = (bf16[3,3072,256]{2,1,0:T(8,128)(2,1)S(1)}, bf16[2,32,1536]{2,1,0:T(8,128)(2,1)S(1)}, f32[3,4,1536]{2,1,0:T(4,128)S(1)}, bf16[2,32,256]{2,1,0:T(8,128)(2,1)S(1)}, s32[8,128]{1,0:T(8,128)S(1)}) custom-call(s32[2]{0:T(128)} %ids.1, bf16[3,3072,256]{2,1,0:T(8,128)(2,1)} %bitcast.11, bf16[2,32,1536]{2,1,0:T(8,128)(2,1)} %refs_1_.1, ...), custom_call_target="tpu_custom_call" | custom-call | bytes 4718592 | tf_op jit(solution)/shard_map/pallas_call | solution.py:218
  8.6 0.1 pad_maximum_fusion.2
  8.7 0.0 collective-permute-done.2
  8.7 0.0 collective-permute-done.1.refs_1_
  8.7 1.6 %shard_map.74 = (bf16[4,2,32,256]{3,2,1,0:T(8,128)(2,1)}, bf16[4,32,256]{2,1,0:T(8,128)(2,1)S(1)}, bf16[2,32,256]{2,1,0:T(8,128)(2,1)S(1)}) custom-call(s32[1]{0:T(128)} %bitcast.3.head, s32[8,128]{1,0:T(8,128)S(1)} %get-tuple-element.17.ids_ref, bf16[2,32,1536]{2,1,0:T(8,128)(2,1)S(1)} %get-tuple-element.19.refs_0_, ...), custom_call_target="tpu_custom_call" | custom-call | flops 301989888 | bytes 4718592 | tf_op jit(solution)/shard_map/pallas_call | solution.py:243
  10.3 3.3 %all-to-all-start = ((bf16[4,2,32,256]{3,2,1,0:T(8,128)(2,1)}), bf16[4,2,32,256]{3,2,1,0:T(8,128)(2,1)S(1)}, u32[]{:S(2)}, u32[]{:S(2)}) async-start(bf16[4,2,32,256]{3,2,1,0:T(8,128)(2,1)} %get-tuple-element.22), calls=%async_computation | async-start | bytes 262144 | tf_op jit(solution)/shard_map/all_to_all | solution.py:234
  13.6 1.6 %collective-permute-start.3 = (bf16[4,32,256]{2,1,0:T(8,128)(2,1)S(1)}, bf16[4,32,256]{2,1,0:T(8,128)(2,1)S(1)}, u32[]{:S(2)}, u32[]{:S(2)}) collective-permute-start(bf16[4,32,256]{2,1,0:T(8,128)(2,1)S(1)} %get-tuple-element.25.refs_0_), channel_id=1, source_target_pairs={{0,2},{2,0},{4,6},{6,4},{8,10},{10,8},{12,14},{14,12},{16,18},{18,... | collective-permute-start | bytes 196616 | tf_op jit(solution)/shard_map/ppermute | solution.py:31
  15.2 1.5 %collective-permute-start.4 = (bf16[4,32,256]{2,1,0:T(8,128)(2,1)S(1)}, bf16[4,32,256]{2,1,0:T(8,128)(2,1)S(1)}, u32[]{:S(2)}, u32[]{:S(2)}) collective-permute-start(bf16[4,32,256]{2,1,0:T(8,128)(2,1)S(1)} %get-tuple-element.25.refs_0_), channel_id=1, source_target_pairs={{0,4},{2,6},{4,0},{6,2},{8,12},{10,14},{12,8},{14,10},{16,20},{18,... | collective-permute-start | bytes 196616 | tf_op jit(solution)/shard_map/ppermute | solution.py:31
  16.7 0.5 %collective-permute-start.5 = (bf16[4,32,256]{2,1,0:T(8,128)(2,1)S(1)}, bf16[4,32,256]{2,1,0:T(8,128)(2,1)S(1)}, u32[]{:S(2)}, u32[]{:S(2)}) collective-permute-start(bf16[4,32,256]{2,1,0:T(8,128)(2,1)S(1)} %get-tuple-element.25.refs_0_), channel_id=1, source_target_pairs={{0,6},{2,4},{4,2},{6,0},{8,14},{10,12},{12,10},{14,8},{16,22},{18,... | collective-permute-start | bytes 196616 | tf_op jit(solution)/shard_map/ppermute | solution.py:31
  17.2 0.0 collective-permute-done
  17.2 0.0 copy-done
  17.2 2.5 %all-to-all-done.q_ref = bf16[4,2,32,256]{3,2,1,0:T(8,128)(2,1)S(1)} async-done(((bf16[4,2,32,256]{3,2,1,0:T(8,128)(2,1)}), bf16[4,2,32,256]{3,2,1,0:T(8,128)(2,1)S(1)}, u32[]{:S(2)}, u32[]{:S(2)}) %all-to-all-start) | async-done | bytes 131104 | tf_op jit(solution)/shard_map/all_to_all | solution.py:234
  19.7 0.0 collective-permute-done.3.refs_1_
  19.7 0.0 collective-permute-done.4.refs_2_
  19.7 2.2 %collective-permute-done.5.refs_3_ = bf16[4,32,256]{2,1,0:T(8,128)(2,1)S(1)} collective-permute-done((bf16[4,32,256]{2,1,0:T(8,128)(2,1)S(1)}, bf16[4,32,256]{2,1,0:T(8,128)(2,1)S(1)}, u32[]{:S(2)}, u32[]{:S(2)}) %collective-permute-start.5) | collective-permute-done | bytes 65568 | tf_op jit(solution)/shard_map/ppermute | solution.py:31
  21.9 1.4 %shard_map.75 = bf16[4,64,384]{2,1,0:T(8,128)(2,1)} custom-call(s32[1]{0:T(128)} %bitcast.patch, bf16[4,2,32,256]{3,2,1,0:T(8,128)(2,1)S(1)} %all-to-all-done.q_ref, bf16[2,32,256]{2,1,0:T(8,128)(2,1)S(1)} %get-tuple-element.24.kv1_ref, bf16[4,32,256]{2,1,0:T(8,128)(2,1)S(1)} %get-tuple-element.25.refs_0_, ...), custom_call_target="tpu_custom_call" | custom-call | flops 67108864 | tf_op jit(solution)/shard_map/pallas_call | solution.py:256
  23.3 5.0 %all-to-all-start.1 = ((bf16[4,64,384]{2,1,0:T(8,128)(2,1)}), bf16[4,64,384]{2,1,0:T(8,128)(2,1)S(1)}, u32[]{:S(2)}, u32[]{:S(2)}) async-start(bf16[4,64,384]{2,1,0:T(8,128)(2,1)} %shard_map.75), calls=%async_computation.1 | async-start | bytes 393216 | tf_op jit(solution)/shard_map/all_to_all | solution.py:234
  28.3 0.5 %collective-permute-start.7 = (bf16[2,192,256]{2,1,0:T(8,128)(2,1)S(1)}, bf16[2,192,256]{2,1,0:T(8,128)(2,1)S(1)}, u32[]{:S(2)}, u32[]{:S(2)}) collective-permute-start(bf16[2,192,256]{2,1,0:T(8,128)(2,1)S(1)} %pad_maximum_fusion.refs_2_), channel_id=1, source_target_pairs={{0,2},{2,0},{4,6},{6,4},{8,10},{10,8},{12,14},{14,12},{16,18},{18,... | collective-permute-start | bytes 589832 | tf_op jit(solution)/shard_map/ppermute | solution.py:31
  28.8 0.5 %collective-permute-start.8 = (bf16[2,192,256]{2,1,0:T(8,128)(2,1)S(1)}, bf16[2,192,256]{2,1,0:T(8,128)(2,1)S(1)}, u32[]{:S(2)}, u32[]{:S(2)}) collective-permute-start(bf16[2,192,256]{2,1,0:T(8,128)(2,1)S(1)} %pad_maximum_fusion.refs_2_), channel_id=1, source_target_pairs={{0,4},{2,6},{4,0},{6,2},{8,12},{10,14},{12,8},{14,10},{16,20},{18,... | collective-permute-start | bytes 589832 | tf_op jit(solution)/shard_map/ppermute | solution.py:31
  29.3 2.4 %collective-permute-start.9 = (bf16[2,192,256]{2,1,0:T(8,128)(2,1)S(1)}, bf16[2,192,256]{2,1,0:T(8,128)(2,1)S(1)}, u32[]{:S(2)}, u32[]{:S(2)}) collective-permute-start(bf16[2,192,256]{2,1,0:T(8,128)(2,1)S(1)} %pad_maximum_fusion.refs_2_), channel_id=1, source_target_pairs={{0,6},{2,4},{4,2},{6,0},{8,14},{10,12},{12,10},{14,8},{16,22},{18,... | collective-permute-start | bytes 589832 | tf_op jit(solution)/shard_map/ppermute | solution.py:31
  31.8 2.9 %all-to-all-done.1.refs_0_ = bf16[4,64,384]{2,1,0:T(8,128)(2,1)S(1)} async-done(((bf16[4,64,384]{2,1,0:T(8,128)(2,1)}), bf16[4,64,384]{2,1,0:T(8,128)(2,1)S(1)}, u32[]{:S(2)}, u32[]{:S(2)}) %all-to-all-start.1) | async-done | bytes 196640 | tf_op jit(solution)/shard_map/all_to_all | solution.py:234
  34.7 0.2 shard_map.76.refs_0_
  34.9 1.8 %collective-permute-start.6 = (bf16[64,256]{1,0:T(8,128)(2,1)S(1)}, bf16[64,256]{1,0:T(8,128)(2,1)S(1)}, u32[]{:S(2)}, u32[]{:S(2)}) collective-permute-start(bf16[64,256]{1,0:T(8,128)(2,1)S(1)} %shard_map.76.refs_0_), channel_id=1, source_target_pairs={{0,8},{2,10},{4,12},{6,14},{8,0},{10,2},{12,4},{14,6},{16,24},{18,... | collective-permute-start | bytes 98312 | tf_op jit(solution)/shard_map/ppermute | solution.py:31
  36.6 0.0 collective-permute-done.7.refs_3_
  36.7 1.0 %collective-permute-done.8.refs_4_ = bf16[2,192,256]{2,1,0:T(8,128)(2,1)S(1)} collective-permute-done((bf16[2,192,256]{2,1,0:T(8,128)(2,1)S(1)}, bf16[2,192,256]{2,1,0:T(8,128)(2,1)S(1)}, u32[]{:S(2)}, u32[]{:S(2)}) %collective-permute-start.8) | collective-permute-done | bytes 196640 | tf_op jit(solution)/shard_map/ppermute | solution.py:31
  37.6 0.0 collective-permute-done.9.refs_5_
  37.6 1.2 %collective-permute-done.6.refs_1_ = bf16[64,256]{1,0:T(8,128)(2,1)S(1)} collective-permute-done((bf16[64,256]{1,0:T(8,128)(2,1)S(1)}, bf16[64,256]{1,0:T(8,128)(2,1)S(1)}, u32[]{:S(2)}, u32[]{:S(2)}) %collective-permute-start.6) | collective-permute-done | bytes 32800 | tf_op jit(solution)/shard_map/ppermute | solution.py:31
  38.9 0.4 shard_map.78
  39.3 0.1 collective-permute-start.10
  39.3 0.4 shard_map.77.refs_0_
  39.8 1.0 %collective-permute-done.10.refs_1_ = bf16[128,768]{1,0:T(8,128)(2,1)S(1)} collective-permute-done((bf16[128,768]{1,0:T(8,128)(2,1)S(1)}, bf16[128,768]{1,0:T(8,128)(2,1)S(1)}, u32[]{:S(2)}, u32[]{:S(2)}) %collective-permute-start.10) | collective-permute-done | bytes 196640 | tf_op jit(solution)/shard_map/ppermute | solution.py:31
  40.8 0.1 shard_map.79
  40.9 1.8 %collective-permute-start.11 = (bf16[2,32,768]{2,1,0:T(8,128)(2,1)S(1)}, bf16[2,32,768]{2,1,0:T(8,128)(2,1)S(1)}, u32[]{:S(2)}, u32[]{:S(2)}) collective-permute-start(bf16[2,32,768]{2,1,0:T(8,128)(2,1)S(1)} %get-tuple-element.27), channel_id=1, source_target_pairs={{0,8},{2,10},{4,12},{6,14},{8,0},{10,2},{12,4},{14,6},{16,24},{18,... | collective-permute-start | bytes 294920 | tf_op jit(solution)/shard_map/ppermute | solution.py:31
  42.7 3.1 %collective-permute-done.11 = bf16[2,32,768]{2,1,0:T(8,128)(2,1)S(1)} collective-permute-done((bf16[2,32,768]{2,1,0:T(8,128)(2,1)S(1)}, bf16[2,32,768]{2,1,0:T(8,128)(2,1)S(1)}, u32[]{:S(2)}, u32[]{:S(2)}) %collective-permute-start.11) | collective-permute-done | bytes 98336 | tf_op jit(solution)/shard_map/ppermute | solution.py:31
  45.8 0.7 %pad_maximum_fusion.1 = bf16[2,32,1536]{2,1,0:T(8,128)(2,1)} fusion(bf16[2,32,768]{2,1,0:T(8,128)(2,1)S(1)} %get-tuple-element.30, bf16[2,32,768]{2,1,0:T(8,128)(2,1)S(1)} %get-tuple-element.29), kind=kLoop, calls=%fused_computation.1 | loop fusion | flops 393216 | bytes 393216 | tf_op jit(solution)/shard_map/concatenate | solution.py:287
  (4 shorter events, 0.1 us)
Async XLA Ops:
  0.0 8.7 %collective-permute-start.1 = (bf16[2,32,1536]{2,1,0:T(8,128)(2,1)}, bf16[2,32,1536]{2,1,0:T(8,128)(2,1)S(1)}, u32[]{:S(2)}, u32[]{:S(2)}) collective-permute-start(bf16[2,32,1536]{2,1,0:T(8,128)(2,1)} %refs_1_.1), channel_id=1, source_target_pairs={{0,1},{1,0},{2,3},{3,2},{4,5},{5,4},{6,7},{7,6},{8,9},{9,8},{10,11... | collective-permute-start | bytes 589832 | tf_op jit(solution)/shard_map/ppermute | solution.py:31
  0.5 8.2 %collective-permute-start.2 = (f32[4,3,1536]{2,0,1:T(4,128)}, f32[4,3,1536]{2,0,1:T(4,128)S(1)}, u32[]{:S(2)}, u32[]{:S(2)}) collective-permute-start(f32[4,3,1536]{2,0,1:T(4,128)} %param.11), channel_id=1, source_target_pairs={{0,1},{1,0},{2,3},{3,2},{4,5},{5,4},{6,7},{7,6},{8,9},{9,8},{10,11... | collective-permute-start | bytes 221192 | tf_op jit(solution)/shard_map/ppermute | solution.py:31
  0.5 16.7 %collective-permute-start = (bf16[192,256]{1,0:T(8,128)(2,1)}, bf16[192,256]{1,0:T(8,128)(2,1)S(1)}, u32[]{:S(2)}, u32[]{:S(2)}) collective-permute-start(bf16[192,256]{1,0:T(8,128)(2,1)} %bitcast.12), channel_id=1, source_target_pairs={{0,16},{2,18},{4,20},{6,22},{8,24},{10,26},{12,28},{14,30},{16,0},... | collective-permute-start | bytes 294920 | tf_op jit(solution)/shard_map/ppermute | solution.py:31
  5.4 11.8 %copy-start = (bf16[256,192]{0,1:T(8,128)(2,1)S(1)}, bf16[256,192]{0,1:T(8,128)(2,1)}, u32[]{:S(2)}) copy-start(bf16[256,192]{0,1:T(8,128)(2,1)} %param.10) | copy-start | bytes 294916
  10.3 9.4 %all-to-all-start = ((bf16[4,2,32,256]{3,2,1,0:T(8,128)(2,1)}), bf16[4,2,32,256]{3,2,1,0:T(8,128)(2,1)S(1)}, u32[]{:S(2)}, u32[]{:S(2)}) async-start(bf16[4,2,32,256]{3,2,1,0:T(8,128)(2,1)} %get-tuple-element.22), calls=%async_computation | async-start | bytes 262144 | tf_op jit(solution)/shard_map/all_to_all | solution.py:234
  13.6 6.0 %collective-permute-start.3 = (bf16[4,32,256]{2,1,0:T(8,128)(2,1)S(1)}, bf16[4,32,256]{2,1,0:T(8,128)(2,1)S(1)}, u32[]{:S(2)}, u32[]{:S(2)}) collective-permute-start(bf16[4,32,256]{2,1,0:T(8,128)(2,1)S(1)} %get-tuple-element.25.refs_0_), channel_id=1, source_target_pairs={{0,2},{2,0},{4,6},{6,4},{8,10},{10,8},{12,14},{14,12},{16,18},{18,... | collective-permute-start | bytes 196616 | tf_op jit(solution)/shard_map/ppermute | solution.py:31
  15.2 4.5 %collective-permute-start.4 = (bf16[4,32,256]{2,1,0:T(8,128)(2,1)S(1)}, bf16[4,32,256]{2,1,0:T(8,128)(2,1)S(1)}, u32[]{:S(2)}, u32[]{:S(2)}) collective-permute-start(bf16[4,32,256]{2,1,0:T(8,128)(2,1)S(1)} %get-tuple-element.25.refs_0_), channel_id=1, source_target_pairs={{0,4},{2,6},{4,0},{6,2},{8,12},{10,14},{12,8},{14,10},{16,20},{18,... | collective-permute-start | bytes 196616 | tf_op jit(solution)/shard_map/ppermute | solution.py:31
  16.7 5.2 %collective-permute-start.5 = (bf16[4,32,256]{2,1,0:T(8,128)(2,1)S(1)}, bf16[4,32,256]{2,1,0:T(8,128)(2,1)S(1)}, u32[]{:S(2)}, u32[]{:S(2)}) collective-permute-start(bf16[4,32,256]{2,1,0:T(8,128)(2,1)S(1)} %get-tuple-element.25.refs_0_), channel_id=1, source_target_pairs={{0,6},{2,4},{4,2},{6,0},{8,14},{10,12},{12,10},{14,8},{16,22},{18,... | collective-permute-start | bytes 196616 | tf_op jit(solution)/shard_map/ppermute | solution.py:31
  23.3 11.4 %all-to-all-start.1 = ((bf16[4,64,384]{2,1,0:T(8,128)(2,1)}), bf16[4,64,384]{2,1,0:T(8,128)(2,1)S(1)}, u32[]{:S(2)}, u32[]{:S(2)}) async-start(bf16[4,64,384]{2,1,0:T(8,128)(2,1)} %shard_map.75), calls=%async_computation.1 | async-start | bytes 393216 | tf_op jit(solution)/shard_map/all_to_all | solution.py:234
  28.3 8.4 %collective-permute-start.7 = (bf16[2,192,256]{2,1,0:T(8,128)(2,1)S(1)}, bf16[2,192,256]{2,1,0:T(8,128)(2,1)S(1)}, u32[]{:S(2)}, u32[]{:S(2)}) collective-permute-start(bf16[2,192,256]{2,1,0:T(8,128)(2,1)S(1)} %pad_maximum_fusion.refs_2_), channel_id=1, source_target_pairs={{0,2},{2,0},{4,6},{6,4},{8,10},{10,8},{12,14},{14,12},{16,18},{18,... | collective-permute-start | bytes 589832 | tf_op jit(solution)/shard_map/ppermute | solution.py:31
  28.8 8.8 %collective-permute-start.8 = (bf16[2,192,256]{2,1,0:T(8,128)(2,1)S(1)}, bf16[2,192,256]{2,1,0:T(8,128)(2,1)S(1)}, u32[]{:S(2)}, u32[]{:S(2)}) collective-permute-start(bf16[2,192,256]{2,1,0:T(8,128)(2,1)S(1)} %pad_maximum_fusion.refs_2_), channel_id=1, source_target_pairs={{0,4},{2,6},{4,0},{6,2},{8,12},{10,14},{12,8},{14,10},{16,20},{18,... | collective-permute-start | bytes 589832 | tf_op jit(solution)/shard_map/ppermute | solution.py:31
  29.3 8.3 %collective-permute-start.9 = (bf16[2,192,256]{2,1,0:T(8,128)(2,1)S(1)}, bf16[2,192,256]{2,1,0:T(8,128)(2,1)S(1)}, u32[]{:S(2)}, u32[]{:S(2)}) collective-permute-start(bf16[2,192,256]{2,1,0:T(8,128)(2,1)S(1)} %pad_maximum_fusion.refs_2_), channel_id=1, source_target_pairs={{0,6},{2,4},{4,2},{6,0},{8,14},{10,12},{12,10},{14,8},{16,22},{18,... | collective-permute-start | bytes 589832 | tf_op jit(solution)/shard_map/ppermute | solution.py:31
  34.9 4.0 %collective-permute-start.6 = (bf16[64,256]{1,0:T(8,128)(2,1)S(1)}, bf16[64,256]{1,0:T(8,128)(2,1)S(1)}, u32[]{:S(2)}, u32[]{:S(2)}) collective-permute-start(bf16[64,256]{1,0:T(8,128)(2,1)S(1)} %shard_map.76.refs_0_), channel_id=1, source_target_pairs={{0,8},{2,10},{4,12},{6,14},{8,0},{10,2},{12,4},{14,6},{16,24},{18,... | collective-permute-start | bytes 98312 | tf_op jit(solution)/shard_map/ppermute | solution.py:31
  39.3 1.5 %collective-permute-start.10 = (bf16[128,768]{1,0:T(8,128)(2,1)S(1)}, bf16[128,768]{1,0:T(8,128)(2,1)S(1)}, u32[]{:S(2)}, u32[]{:S(2)}) collective-permute-start(bf16[128,768]{1,0:T(8,128)(2,1)S(1)} %shard_map.78), channel_id=1, source_target_pairs={{0,1},{1,0},{2,3},{3,2},{4,5},{5,4},{6,7},{7,6},{8,9},{9,8},{10,11... | collective-permute-start | bytes 589832 | tf_op jit(solution)/shard_map/ppermute | solution.py:31
  40.9 4.9 %collective-permute-start.11 = (bf16[2,32,768]{2,1,0:T(8,128)(2,1)S(1)}, bf16[2,32,768]{2,1,0:T(8,128)(2,1)S(1)}, u32[]{:S(2)}, u32[]{:S(2)}) collective-permute-start(bf16[2,32,768]{2,1,0:T(8,128)(2,1)S(1)} %get-tuple-element.27), channel_id=1, source_target_pairs={{0,8},{2,10},{4,12},{6,14},{8,0},{10,2},{12,4},{14,6},{16,24},{18,... | collective-permute-start | bytes 294920 | tf_op jit(solution)/shard_map/ppermute | solution.py:31

commit v6 on v5

--- a/solution.py
+++ b/solution.py
@@ -58,12 +58,11 @@
 
 def qkv_kernel(n_head, head, ids_ref, *refs):
     x_refs, mod_refs = refs[:n_head], refs[n_head : 2 * n_head]
-    w_ref, cos_ref, sin_ref, stale_ref = refs[2 * n_head : 2 * n_head + 4]
+    w_ref, cos_ref, sin_ref = refs[2 * n_head : 2 * n_head + 3]
     q_ref, kv0_ref, kv1_ref, a_ref = refs[-4:]
     rows, feats = x_refs[0].shape[1:]
     width = n_head * feats
     cols = w_ref.shape[2]
-    kv0_ref[:2] = stale_ref[...]
     for step in range(STEPS):
         total, square = 0.0, 0.0
         for x_ref in x_refs:
@@ -94,12 +93,9 @@
                     u = u * cos + pltpu.roll(u, DH // 2, 1) * sin
                 u = u.astype(BF16)
                 if slot == 0:
-                    for place in range(q_ref.shape[0]):
-                        q_ref[place, step, :, lanes] = u
-                elif step == 0:
-                    kv0_ref[slot + 1, :, lanes] = u
+                    q_ref[step, :, lanes] = u
                 else:
-                    kv1_ref[slot - 1, :, lanes] = u
+                    (kv0_ref, kv1_ref)[step][slot - 1, :, lanes] = u
 
 
 def split3(values):
@@ -108,25 +104,28 @@
     return [high, middle, values - high - middle]
 
 
-def attend_kernel(patch, q_ref, kv1_ref, *refs):
+def attend_kernel(q_ref, mate_ref, kv1_ref, *refs):
     kv_refs, out_ref = refs[:PLANE], refs[PLANE]
-    line, _, rows, cols = q_ref.shape
-    shape = (line * rows, PLANE * rows + rows)
-    mine = lax.broadcasted_iota(jnp.int32, shape, 0) // rows == patch[0] // PLANE
-    drop = lax.broadcasted_iota(jnp.int32, shape, 1) // rows == jnp.where(mine, 0, PLANE)
-    lane = lax.broadcasted_iota(jnp.int32, (line * rows, DH), 1)
+    blocks, _, rows, cols = kv_refs[0].shape
+    blocks = blocks // STEPS
+    old_rows = PLANE * blocks * rows
+    shape = (2 * rows, old_rows + rows)
+    mine = lax.broadcasted_iota(jnp.int32, shape, 0) < rows
+    drop = lax.broadcasted_iota(jnp.int32, shape, 1) // rows == jnp.where(mine, 0, PLANE * blocks)
+    lane = lax.broadcasted_iota(jnp.int32, (2 * rows, DH), 1)
     for step in range(STEPS):
-        fresh = (kv_refs[0].at[2:], kv1_ref)[step]
-        stats = jnp.zeros((line * rows, DH), F32)
+        spot = slice(step * blocks, (step + 1) * blocks)
+        fresh = (kv_refs[0].at[blocks], kv1_ref)[step]
+        stats = jnp.zeros((2 * rows, DH), F32)
         mixed = []
-        for block in range(cols // DH):
-            lanes = slice(block * DH, (block + 1) * DH)
+        for head in range(cols // DH):
+            lanes = slice(head * DH, (head + 1) * DH)
 
             def rows_of(kind):
-                old = [ref[2 * step + kind, :, lanes] for ref in kv_refs]
+                old = [ref[spot, kind, :, lanes].reshape(blocks * rows, DH) for ref in kv_refs]
                 return jnp.concatenate([*old, fresh[kind, :, lanes]], axis=0)
 
-            queries = q_ref[:, step, :, lanes].reshape(line * rows, DH)
+            queries = jnp.concatenate([q_ref[step, :, lanes], mate_ref[step, :, lanes]], axis=0)
             scores = lax.dot_general(queries, rows_of(0), NT, preferred_element_type=F32)
             scores = jnp.where(drop, -1e30, scores * (1.0 / math.sqrt(DH)))
             top = jnp.max(scores, axis=1, keepdims=True)
@@ -136,38 +135,41 @@
                 jnp.dot(weights.astype(BF16), rows_of(1), preferred_element_type=F32) / totals
             )
             for place, piece in enumerate(split3(top) + split3(totals)):
-                stats = jnp.where(lane == block * 8 + place, piece, stats)
+                stats = jnp.where(lane == head * 8 + place, piece, stats)
         packed = jnp.concatenate([*mixed, stats], axis=1).astype(BF16)
-        out_ref[:, step * rows : (step + 1) * rows, :] = packed.reshape(line, rows, cols + DH)
-
-
-def merge_kernel(*refs):
-    parts_ref, o_ref = refs
-    part_refs = [parts_ref.at[k] for k in range(parts_ref.shape[0])]
+        for mate in range(2):
+            start = (mate * STEPS + step) * rows
+            out_ref[start : start + rows, :] = packed[mate * rows : (mate + 1) * rows]
+
+
+def merge_kernel(part_ref, other_ref, o_ref):
+    rows = part_ref.shape[0] // 2
     cols = o_ref.shape[1]
     source = lax.broadcasted_iota(jnp.int32, (DH, DH), 0)
-    for block in range(cols // DH):
-        lanes = slice(block * DH, (block + 1) * DH)
-
-        def spread(ref, first):
-            pick = (source >= block * 8 + first) & (source < block * 8 + first + 3)
-            return jnp.dot(ref[:, cols:], pick.astype(F32).astype(BF16), preferred_element_type=F32)
-
-        tops = [spread(ref, 0) for ref in part_refs]
+    parts = [
+        part_ref[...],
+        jnp.concatenate([other_ref[rows:], other_ref[:rows]], axis=0),
+    ]
+    for head in range(cols // DH):
+        lanes = slice(head * DH, (head + 1) * DH)
+
+        def spread(part, first):
+            pick = (source >= head * 8 + first) & (source < head * 8 + first + 3)
+            return jnp.dot(part[:, cols:], pick.astype(F32).astype(BF16), preferred_element_type=F32)
+
+        tops = [spread(part, 0) for part in parts]
         best = functools.reduce(jnp.maximum, tops)
-        scales = [spread(ref, 3) * jnp.exp(t - best) for ref, t in zip(part_refs, tops)]
-        mixed = sum(s * ref[:, lanes].astype(F32) for s, ref in zip(scales, part_refs))
+        scales = [spread(part, 3) * jnp.exp(t - best) for part, t in zip(parts, tops)]
+        mixed = sum(s * part[:, lanes].astype(F32) for s, part in zip(scales, parts))
         o_ref[:, lanes] = (mixed / sum(scales)).astype(BF16)
 
 
 def project_kernel(n_head, n_patch, bit, patch, head, *refs):
-    o_refs, w_refs, (out_ref, sums) = refs[:2], refs[2 : 2 + PLANE], refs[2 + PLANE :]
-    rows = o_refs[0].shape[0]
+    o_ref, w_refs, (out_ref, sums) = refs[0], refs[1 : 1 + PLANE], refs[1 + PLANE :]
     slot = head[0] ^ bit ^ (patch[0] // (n_patch // n_head))
-    o = jnp.concatenate([ref[...] for ref in o_refs], axis=0)
     for near in range(PLANE):
         sums[(patch[0] % PLANE) ^ near] = lax.dot_general(
-            o, w_refs[near][slot], NT, preferred_element_type=F32
+            o_ref[...], w_refs[near][slot], NT, preferred_element_type=F32
         )
     out = jnp.concatenate([sums[c] for c in range(PLANE)], axis=1)
     out_ref[...] = out.astype(out_ref.dtype)
@@ -207,15 +209,14 @@
     rows, feats = inputs.shape[1:]
     cols = w_qkv.shape[2]
     piece = w_out.shape[1]
-    line = n_patch // PLANE
     patch = lax.axis_index("patch").astype(jnp.int32)
     head = lax.axis_index("head").astype(jnp.int32)
     shaped = jax.ShapeDtypeStruct
 
     x_parts = [swap(inputs, "head", n_head, k) for k in range(1, n_head)]
     mod_parts = [swap(mod_table, "head", n_head, k) for k in range(1, n_head)]
-    first = (jnp.transpose(w_qkv, (1, 0, 2)), inputs, jnp.transpose(mod_table, (1, 0, 2)), stale_kv)
-    w, x_own, mod_own, stale, ids = call(
+    first = (jnp.transpose(w_qkv, (1, 0, 2)), inputs, jnp.transpose(mod_table, (1, 0, 2)))
+    w, x_own, mod_own, ids = call(
         load_kernel,
         tuple(pltpu.VMEM(v.shape, v.dtype) for v in first) + (shaped((8, DH), jnp.int32),),
         [SMEM] + [ANY] * len(first),
@@ -225,64 +226,64 @@
     x_parts = [x_own] + x_parts
     mod_parts = [mod_own] + [jnp.transpose(part, (1, 0, 2)) for part in mod_parts]
 
+    def across(values, k):
+        return swap(values, "patch", n_patch, k)
+
+    def line_of(values):
+        return [values] + [across(values, k) for k in range(2 * PLANE, n_patch, 2 * PLANE)]
+
     def plane_of(values):
-        return [values] + [swap(values, "patch", n_patch, k) for k in range(1, PLANE)]
-
-    lines = [[PLANE * i + j for i in range(line)] for j in range(PLANE)]
-
-    def trade(values):
-        return lax.all_to_all(values, "patch", 0, 0, axis_index_groups=lines)
-
-    rise = 2 * PLANE
-    w_pair = jnp.stack(
-        [w_out.T] + [swap(w_out.T, "patch", n_patch, rise * k) for k in range(1, n_head)]
-    )
+        return [values] + [across(values, k) for k in range(1, PLANE)]
+
+    stale_pair = line_of(stale_kv)
+    w_pair = line_of(w_out.T)
 
     positions = slab_order[0] * rows + jnp.arange(rows, dtype=jnp.int32)
     cos, sin = angle_tables(positions)
+    kv_shape = shaped((2, rows, cols), BF16)
     q, kv0, kv1 = call(
         functools.partial(qkv_kernel, n_head),
-        tuple(shaped((*n, rows, cols), BF16) for n in ((line, STEPS), (4,), (2,))),
-        [SMEM] + [VMEM] * (2 * n_head + 5),
+        (kv_shape,) * 3,
+        [SMEM] + [VMEM] * (2 * n_head + 4) + [ANY] * (n_head - 1),
         [pltpu.VMEM((n_head, STEPS * rows, feats), BF16)],
         2 * STEPS * rows * w_qkv.size,
         2 * w_qkv.size,
-    )(head[None], ids, *x_parts, *mod_parts, w, cos, sin, stale)
-
-    kv_plane = plane_of(kv0)
-    q_line = trade(q)
-    w_pair, q_line = lax.optimization_barrier((w_pair, q_line))
-    w_plane = plane_of(w_pair)
-    parts = call(
+    )(head[None], ids, *x_parts, *mod_parts, w, cos, sin, *stale_pair[1:])
+
+    kv_pair = line_of(kv0)
+    q_mate = across(q, PLANE)
+    w_pair, kv_pair = lax.optimization_barrier((w_pair, kv_pair))
+    kv_plane = plane_of(jnp.stack(stale_pair + kv_pair))
+    w_plane = plane_of(jnp.stack(w_pair))
+    tall = 2 * STEPS * rows
+    part = call(
         attend_kernel,
-        shaped((line, STEPS * rows, cols + DH), BF16),
-        [SMEM] + [VMEM] * (PLANE + 2),
-        flops=8 * STEPS * rows * n_patch * rows * cols,
-    )(patch[None], q_line, kv1, *kv_plane)
-    o = call(merge_kernel, shaped((STEPS * rows, cols), BF16), [VMEM])(trade(parts))
-    o_mate = swap(o, "patch", n_patch, PLANE)
-
-    wide = (2 * STEPS * rows, PLANE * piece)
+        shaped((tall, cols + DH), BF16),
+        [VMEM] * (3 + PLANE),
+        flops=4 * STEPS * rows * n_patch * rows * cols,
+    )(q, q_mate, kv1, *kv_plane)
+    o = call(merge_kernel, shaped((tall, cols), BF16), [VMEM] * 2)(part, across(part, PLANE))
+    wide = PLANE * piece
 
     def project(bit, dtype):
         return call(
             functools.partial(project_kernel, n_head, n_patch, bit),
-            shaped(wide, dtype),
-            [SMEM] * 2 + [VMEM] * (2 + PLANE),
-            [pltpu.VMEM((PLANE, 2 * STEPS * rows, piece), F32)],
-            2 * wide[0] * wide[1] * cols,
-            2 * wide[1] * cols,
-        )(patch[None], head[None], o, o_mate, *w_plane)
+            shaped((tall, wide), dtype),
+            [SMEM] * 2 + [VMEM] * (1 + PLANE),
+            [pltpu.VMEM((PLANE, tall, piece), F32)],
+            2 * tall * wide * cols,
+            2 * wide * cols,
+        )(patch[None], head[None], o, *w_plane)
 
     sums = [swap(project(k, BF16), "head", n_head, k) for k in range(1, n_head)]
     sums = [project(0, F32)] + sums
-    out_half = shaped((STEPS, rows, PLANE * piece), BF16)
+    out_half = shaped((STEPS, rows, wide), BF16)
     out_own, out_mate = call(
         functools.partial(gate_kernel, n_patch),
         (out_half, out_half),
         [SMEM] + [VMEM] * (2 + n_head),
     )(patch[None], ids, mod_own, *sums)
-    out_back = swap(out_mate, "patch", n_patch, PLANE)
+    out_back = across(out_mate, PLANE)
     second = (patch // PLANE) % 2 == 1
     return jnp.concatenate(
         [jnp.where(second, out_back, out_own), jnp.where(second, out_own, out_back)], axis=2

time: 46.9 us -> 42.3 us (0.902)
  starting transfers between devices: 23.5 us -> 16.5 us
  waiting for transfers between devices: 13.9 us -> 17.3 us
  Pallas kernels: 7.39 us -> 6.61 us
    ppermute x12 -> x15, waiting for transfers between devices: 8.57 us -> 17.3 us  [swap(): return lax.ppermute(values, axis, [(i, i ^ bit) for i in range(count)])]
    all_to_all x2 -> x0, starting transfers between devices: 8.31 us -> none  [trade(): return lax.all_to_all(values, 'patch', 0, 0, axis_index_groups=lines)]
    all_to_all x2 -> x0, waiting for transfers between devices: 5.33 us -> none  [trade(): return lax.all_to_all(values, 'patch', 0, 0, axis_index_groups=lines)]
    ppermute x12 -> x15, starting transfers between devices: 15.2 us -> 16.5 us  [swap(): return lax.ppermute(values, axis, [(i, i ^ bit) for i in range(count)])]
    pallas_call x5, Pallas kernels: 4.08 us -> 3.3 us  [the longest x1 1.17 us: body(): call(functools.partial(qkv_kernel, n_head), (kv_shape,) * 3, [SMEM] + [VM...]
  transfers between devices with their start and end apart: 14 -> 15, of which waited for: 7 -> 5; matrix products, arithmetic and copies ran while one was open for 1% -> 1% of each run, Pallas kernels for 12% -> 14%
where the time goes in v6:
time: 42.3 us; the launch traced here: 42.2 us
  waiting for transfers between devices  17.3 us (41%)
  starting transfers between devices  16.5 us (39%)
  Pallas kernels  6.61 us (16%)
  other arithmetic  0.98 us (2%)
  between operations  0.83 us (2%)
    ppermute x15, waiting for transfers between devices, swap(): return lax.ppermute(values, axis, [(i, i ^ bit) for i in range(count)])  17.3 us
    ppermute x15, starting transfers between devices, swap(): return lax.ppermute(values, axis, [(i, i ^ bit) for i in range(count)])  16.5 us
    pallas_call x1, Pallas kernels, body(): call(load_kernel, tuple((pltpu.VMEM(v.shape, v.dtype) for v in first)) +...  3.19 us
    pallas_call x1, Pallas kernels, body(): call(functools.partial(qkv_kernel, n_head), (kv_shape,) * 3, [SMEM] + [VM...  1.17 us
    pallas_call x1, Pallas kernels, body(): call(attend_kernel, shaped((tall, cols + DH), BF16), [VMEM] * (3 + PLANE)...  1.11 us
  transfers between devices with their start and end apart: 15, of which 5 were waited for; matrix products, arithmetic and copies ran while one was open for 1% of the time, Pallas kernels for 14%

profile of v6, /device:TPU:0, one launch (start us, length us, event | category | flops | bytes accessed | tf_op | source)
XLA Modules:
  0.0 42.2 jit_solution(14770374624339990386)
XLA Ops:
  0.0 4.0 %collective-permute-start.2 = (bf16[2,32,256]{2,1,0:T(8,128)(2,1)}, bf16[2,32,256]{2,1,0:T(8,128)(2,1)S(1)}, u32[]{:S(2)}, u32[]{:S(2)}) collective-permute-start(bf16[2,32,256]{2,1,0:T(8,128)(2,1)} %param.8), channel_id=1, source_target_pairs={{0,16},{2,18},{4,20},{6,22},{8,24},{10,26},{12,28},{14,30},{16,0},... | collective-permute-start | bytes 98312 | tf_op jit(solution)/shard_map/ppermute | solution.py:31
  4.0 0.0 collective-permute-start
  4.0 0.5 %collective-permute-start.1 = (f32[4,3,1536]{2,0,1:T(4,128)}, f32[4,3,1536]{2,0,1:T(4,128)S(1)}, u32[]{:S(2)}, u32[]{:S(2)}) collective-permute-start(f32[4,3,1536]{2,0,1:T(4,128)} %param.11), channel_id=1, source_target_pairs={{0,1},{1,0},{2,3},{3,2},{4,5},{5,4},{6,7},{7,6},{8,9},{9,8},{10,11... | collective-permute-start | bytes 221192 | tf_op jit(solution)/shard_map/ppermute | solution.py:31
  4.5 0.0 collective-permute-start.4
  5.2 0.1 fusion
  5.4 0.1 pad_maximum_fusion.3
  5.5 0.0 copy-start.1
  5.5 0.0 copy-start
  5.5 3.2 %shard_map.73 = (bf16[3,3072,256]{2,1,0:T(8,128)(2,1)S(1)}, bf16[2,32,1536]{2,1,0:T(8,128)(2,1)S(1)}, f32[3,4,1536]{2,1,0:T(4,128)S(1)}, s32[8,128]{1,0:T(8,128)S(1)}) custom-call(s32[2]{0:T(128)} %ids.1, bf16[3,3072,256]{2,1,0:T(8,128)(2,1)} %bitcast.16, bf16[2,32,1536]{2,1,0:T(8,128)(2,1)} %refs_1_.1, f32[3,4,1536]{2,1,0:T(4,128)} %bitcast.20), custom_call_target="tpu_custom_call" | custom-call | bytes 4718592 | tf_op jit(solution)/shard_map/pallas_call | solution.py:219
  8.7 0.0 collective-permute-done.2.refs_7_
  8.7 0.0 collective-permute-done.1
  8.7 0.0 collective-permute-done.refs_1_
  8.7 1.2 %shard_map.74 = (bf16[2,32,256]{2,1,0:T(8,128)(2,1)S(1)}, bf16[2,32,256]{2,1,0:T(8,128)(2,1)S(1)}, bf16[2,32,256]{2,1,0:T(8,128)(2,1)S(1)}) custom-call(s32[1]{0:T(128)} %bitcast.3.head, s32[8,128]{1,0:T(8,128)S(1)} %get-tuple-element.18.ids_ref, bf16[2,32,1536]{2,1,0:T(8,128)(2,1)S(1)} %get-tuple-element.20.refs_0_, ...), custom_call_target="tpu_custom_call" | custom-call | flops 301989888 | bytes 4718592 | tf_op jit(solution)/shard_map/pallas_call | solution.py:244
  9.9 3.0 %collective-permute-start.5 = (bf16[2,32,256]{2,1,0:T(8,128)(2,1)S(1)}, bf16[2,32,256]{2,1,0:T(8,128)(2,1)S(1)}, u32[]{:S(2)}, u32[]{:S(2)}) collective-permute-start(bf16[2,32,256]{2,1,0:T(8,128)(2,1)S(1)} %get-tuple-element.25), channel_id=1, source_target_pairs={{0,16},{2,18},{4,20},{6,22},{8,24},{10,26},{12,28},{14,30},{16,0},... | collective-permute-start | bytes 98312 | tf_op jit(solution)/shard_map/ppermute | solution.py:31
  12.8 0.0 collective-permute-done.4
  12.9 2.2 %collective-permute-done.5 = bf16[2,32,256]{2,1,0:T(8,128)(2,1)S(1)} collective-permute-done((bf16[2,32,256]{2,1,0:T(8,128)(2,1)S(1)}, bf16[2,32,256]{2,1,0:T(8,128)(2,1)S(1)}, u32[]{:S(2)}, u32[]{:S(2)}) %collective-permute-start.5) | collective-permute-done | bytes 32800 | tf_op jit(solution)/shard_map/ppermute | solution.py:31
  15.1 0.0 copy-done.1
  15.1 1.7 %collective-permute-start.6 = (bf16[4,2,32,256]{3,2,1,0:T(8,128)(2,1)S(1)}, bf16[4,2,32,256]{3,2,1,0:T(8,128)(2,1)S(1)}, u32[]{:S(2)}, u32[]{:S(2)}) collective-permute-start(bf16[4,2,32,256]{3,2,1,0:T(8,128)(2,1)S(1)} %pad_maximum_fusion.2.refs_0_), channel_id=1, source_target_pairs={{0,2},{2,0},{4,6},{6,4},{8,10},{10,8},{12,14},{14,12},{16,18},{18,... | collective-permute-start | bytes 393224 | tf_op jit(solution)/shard_map/ppermute | solution.py:31
  16.8 1.5 %collective-permute-start.3 = (bf16[2,32,256]{2,1,0:T(8,128)(2,1)S(1)}, bf16[2,32,256]{2,1,0:T(8,128)(2,1)S(1)}, u32[]{:S(2)}, u32[]{:S(2)}) collective-permute-start(bf16[2,32,256]{2,1,0:T(8,128)(2,1)S(1)} %get-tuple-element.22.q_ref), channel_id=1, source_target_pairs={{0,8},{2,10},{4,12},{6,14},{8,0},{10,2},{12,4},{14,6},{16,24},{18,... | collective-permute-start | bytes 98312 | tf_op jit(solution)/shard_map/ppermute | solution.py:31
  18.2 1.5 %collective-permute-start.7 = (bf16[4,2,32,256]{3,2,1,0:T(8,128)(2,1)S(1)}, bf16[4,2,32,256]{3,2,1,0:T(8,128)(2,1)S(1)}, u32[]{:S(2)}, u32[]{:S(2)}) collective-permute-start(bf16[4,2,32,256]{3,2,1,0:T(8,128)(2,1)S(1)} %pad_maximum_fusion.2.refs_0_), channel_id=1, source_target_pairs={{0,4},{2,6},{4,0},{6,2},{8,12},{10,14},{12,8},{14,10},{16,20},{18,... | collective-permute-start | bytes 393224 | tf_op jit(solution)/shard_map/ppermute | solution.py:31
  19.7 0.5 %collective-permute-start.8 = (bf16[4,2,32,256]{3,2,1,0:T(8,128)(2,1)S(1)}, bf16[4,2,32,256]{3,2,1,0:T(8,128)(2,1)S(1)}, u32[]{:S(2)}, u32[]{:S(2)}) collective-permute-start(bf16[4,2,32,256]{3,2,1,0:T(8,128)(2,1)S(1)} %pad_maximum_fusion.2.refs_0_), channel_id=1, source_target_pairs={{0,6},{2,4},{4,2},{6,0},{8,14},{10,12},{12,10},{14,8},{16,22},{18,... | collective-permute-start | bytes 393224 | tf_op jit(solution)/shard_map/ppermute | solution.py:31
  20.2 0.0 copy-done
  20.3 1.6 %collective-permute-start.10 = (bf16[2,192,256]{2,1,0:T(8,128)(2,1)S(1)}, bf16[2,192,256]{2,1,0:T(8,128)(2,1)S(1)}, u32[]{:S(2)}, u32[]{:S(2)}) collective-permute-start(bf16[2,192,256]{2,1,0:T(8,128)(2,1)S(1)} %pad_maximum_fusion.refs_1_), channel_id=1, source_target_pairs={{0,2},{2,0},{4,6},{6,4},{8,10},{10,8},{12,14},{14,12},{16,18},{18,... | collective-permute-start | bytes 589832 | tf_op jit(solution)/shard_map/ppermute | solution.py:31
  21.8 0.0 collective-permute-done.3.mate_ref
  21.8 1.5 %collective-permute-start.11 = (bf16[2,192,256]{2,1,0:T(8,128)(2,1)S(1)}, bf16[2,192,256]{2,1,0:T(8,128)(2,1)S(1)}, u32[]{:S(2)}, u32[]{:S(2)}) collective-permute-start(bf16[2,192,256]{2,1,0:T(8,128)(2,1)S(1)} %pad_maximum_fusion.refs_1_), channel_id=1, source_target_pairs={{0,4},{2,6},{4,0},{6,2},{8,12},{10,14},{12,8},{14,10},{16,20},{18,... | collective-permute-start | bytes 589832 | tf_op jit(solution)/shard_map/ppermute | solution.py:31
  23.3 0.0 collective-permute-done.6.refs_1_
  23.3 0.5 %collective-permute-start.12 = (bf16[2,192,256]{2,1,0:T(8,128)(2,1)S(1)}, bf16[2,192,256]{2,1,0:T(8,128)(2,1)S(1)}, u32[]{:S(2)}, u32[]{:S(2)}) collective-permute-start(bf16[2,192,256]{2,1,0:T(8,128)(2,1)S(1)} %pad_maximum_fusion.refs_1_), channel_id=1, source_target_pairs={{0,6},{2,4},{4,2},{6,0},{8,14},{10,12},{12,10},{14,8},{16,22},{18,... | collective-permute-start | bytes 589832 | tf_op jit(solution)/shard_map/ppermute | solution.py:31
  23.9 4.6 %collective-permute-done.7.refs_2_ = bf16[4,2,32,256]{3,2,1,0:T(8,128)(2,1)S(1)} collective-permute-done((bf16[4,2,32,256]{3,2,1,0:T(8,128)(2,1)S(1)}, bf16[4,2,32,256]{3,2,1,0:T(8,128)(2,1)S(1)}, u32[]{:S(2)}, u32[]{:S(2)}) %collective-permute-start.7) | collective-permute-done | bytes 131104 | tf_op jit(solution)/shard_map/ppermute | solution.py:31
  28.5 0.0 collective-permute-done.8.refs_3_
  28.5 1.1 %shard_map.75.part_ref = bf16[128,384]{1,0:T(8,128)(2,1)S(1)} custom-call(bf16[2,32,256]{2,1,0:T(8,128)(2,1)S(1)} %get-tuple-element.22.q_ref, bf16[2,32,256]{2,1,0:T(8,128)(2,1)S(1)} %collective-permute-done.3.mate_ref, bf16[2,32,256]{2,1,0:T(8,128)(2,1)S(1)} %get-tuple-element.23.kv1_ref, bf16[4,2,32,256]{3,2,1,0:T(8,128)(2,1)S(1)} %pad_maximum_fusion.2.refs_0_, ...), custom_call_target="tpu_custom_call" | custom-call | flops 33554432 | tf_op jit(solution)/shard_map/pallas_call | solution.py:259
  29.6 0.1 collective-permute-start.9
  29.7 4.6 %collective-permute-done.9.other_ref = bf16[128,384]{1,0:T(8,128)(2,1)S(1)} collective-permute-done((bf16[128,384]{1,0:T(8,128)(2,1)S(1)}, bf16[128,384]{1,0:T(8,128)(2,1)S(1)}, u32[]{:S(2)}, u32[]{:S(2)}) %collective-permute-start.9) | collective-permute-done | bytes 98336 | tf_op jit(solution)/shard_map/ppermute | solution.py:31
  34.3 0.2 shard_map.76.refs_0_
  34.5 0.0 collective-permute-done.10.refs_2_
  34.5 0.0 collective-permute-done.11.refs_3_
  34.5 0.0 collective-permute-done.12.refs_4_
  34.5 0.4 shard_map.78
  34.9 0.1 collective-permute-start.13
  35.0 0.4 shard_map.77.refs_0_
  35.4 1.0 %collective-permute-done.13.refs_1_ = bf16[128,768]{1,0:T(8,128)(2,1)S(1)} collective-permute-done((bf16[128,768]{1,0:T(8,128)(2,1)S(1)}, bf16[128,768]{1,0:T(8,128)(2,1)S(1)}, u32[]{:S(2)}, u32[]{:S(2)}) %collective-permute-start.13) | collective-permute-done | bytes 196640 | tf_op jit(solution)/shard_map/ppermute | solution.py:31
  36.4 0.1 shard_map.79
  36.5 0.1 collective-permute-start.14
  36.7 4.8 %collective-permute-done.14 = bf16[2,32,768]{2,1,0:T(8,128)(2,1)S(1)} collective-permute-done((bf16[2,32,768]{2,1,0:T(8,128)(2,1)S(1)}, bf16[2,32,768]{2,1,0:T(8,128)(2,1)S(1)}, u32[]{:S(2)}, u32[]{:S(2)}) %collective-permute-start.14) | collective-permute-done | bytes 98336 | tf_op jit(solution)/shard_map/ppermute | solution.py:31
  41.5 0.7 %pad_maximum_fusion.1 = bf16[2,32,1536]{2,1,0:T(8,128)(2,1)} fusion(bf16[2,32,768]{2,1,0:T(8,128)(2,1)S(1)} %get-tuple-element.32, bf16[2,32,768]{2,1,0:T(8,128)(2,1)S(1)} %get-tuple-element.31), kind=kLoop, calls=%fused_computation.1 | loop fusion | flops 393216 | bytes 393216 | tf_op jit(solution)/shard_map/concatenate | solution.py:288
  (5 shorter events, 0.1 us)
Async XLA Ops:
  0.0 8.7 %collective-permute-start.2 = (bf16[2,32,256]{2,1,0:T(8,128)(2,1)}, bf16[2,32,256]{2,1,0:T(8,128)(2,1)S(1)}, u32[]{:S(2)}, u32[]{:S(2)}) collective-permute-start(bf16[2,32,256]{2,1,0:T(8,128)(2,1)} %param.8), channel_id=1, source_target_pairs={{0,16},{2,18},{4,20},{6,22},{8,24},{10,26},{12,28},{14,30},{16,0},... | collective-permute-start | bytes 98312 | tf_op jit(solution)/shard_map/ppermute | solution.py:31
  4.0 4.6 %collective-permute-start = (bf16[2,32,1536]{2,1,0:T(8,128)(2,1)}, bf16[2,32,1536]{2,1,0:T(8,128)(2,1)S(1)}, u32[]{:S(2)}, u32[]{:S(2)}) collective-permute-start(bf16[2,32,1536]{2,1,0:T(8,128)(2,1)} %refs_1_.1), channel_id=1, source_target_pairs={{0,1},{1,0},{2,3},{3,2},{4,5},{5,4},{6,7},{7,6},{8,9},{9,8},{10,11... | collective-permute-start | bytes 589832 | tf_op jit(solution)/shard_map/ppermute | solution.py:31
  4.0 4.6 %collective-permute-start.1 = (f32[4,3,1536]{2,0,1:T(4,128)}, f32[4,3,1536]{2,0,1:T(4,128)S(1)}, u32[]{:S(2)}, u32[]{:S(2)}) collective-permute-start(f32[4,3,1536]{2,0,1:T(4,128)} %param.11), channel_id=1, source_target_pairs={{0,1},{1,0},{2,3},{3,2},{4,5},{5,4},{6,7},{7,6},{8,9},{9,8},{10,11... | collective-permute-start | bytes 221192 | tf_op jit(solution)/shard_map/ppermute | solution.py:31
  4.5 8.3 %collective-permute-start.4 = (bf16[192,256]{1,0:T(8,128)(2,1)}, bf16[192,256]{1,0:T(8,128)(2,1)S(1)}, u32[]{:S(2)}, u32[]{:S(2)}) collective-permute-start(bf16[192,256]{1,0:T(8,128)(2,1)} %bitcast.17), channel_id=1, source_target_pairs={{0,16},{2,18},{4,20},{6,22},{8,24},{10,26},{12,28},{14,30},{16,0},... | collective-permute-start | bytes 294920 | tf_op jit(solution)/shard_map/ppermute | solution.py:31
  5.5 9.6 %copy-start.1 = (bf16[2,32,256]{2,1,0:T(8,128)(2,1)S(1)}, bf16[2,32,256]{2,1,0:T(8,128)(2,1)}, u32[]{:S(2)}) copy-start(bf16[2,32,256]{2,1,0:T(8,128)(2,1)} %param.8) | copy-start | bytes 98308
  5.5 14.8 %copy-start = (bf16[256,192]{0,1:T(8,128)(2,1)S(1)}, bf16[256,192]{0,1:T(8,128)(2,1)}, u32[]{:S(2)}) copy-start(bf16[256,192]{0,1:T(8,128)(2,1)} %param.10) | copy-start | bytes 294916
  9.9 5.2 %collective-permute-start.5 = (bf16[2,32,256]{2,1,0:T(8,128)(2,1)S(1)}, bf16[2,32,256]{2,1,0:T(8,128)(2,1)S(1)}, u32[]{:S(2)}, u32[]{:S(2)}) collective-permute-start(bf16[2,32,256]{2,1,0:T(8,128)(2,1)S(1)} %get-tuple-element.25), channel_id=1, source_target_pairs={{0,16},{2,18},{4,20},{6,22},{8,24},{10,26},{12,28},{14,30},{16,0},... | collective-permute-start | bytes 98312 | tf_op jit(solution)/shard_map/ppermute | solution.py:31
  15.1 8.2 %collective-permute-start.6 = (bf16[4,2,32,256]{3,2,1,0:T(8,128)(2,1)S(1)}, bf16[4,2,32,256]{3,2,1,0:T(8,128)(2,1)S(1)}, u32[]{:S(2)}, u32[]{:S(2)}) collective-permute-start(bf16[4,2,32,256]{3,2,1,0:T(8,128)(2,1)S(1)} %pad_maximum_fusion.2.refs_0_), channel_id=1, source_target_pairs={{0,2},{2,0},{4,6},{6,4},{8,10},{10,8},{12,14},{14,12},{16,18},{18,... | collective-permute-start | bytes 393224 | tf_op jit(solution)/shard_map/ppermute | solution.py:31
  16.8 5.0 %collective-permute-start.3 = (bf16[2,32,256]{2,1,0:T(8,128)(2,1)S(1)}, bf16[2,32,256]{2,1,0:T(8,128)(2,1)S(1)}, u32[]{:S(2)}, u32[]{:S(2)}) collective-permute-start(bf16[2,32,256]{2,1,0:T(8,128)(2,1)S(1)} %get-tuple-element.22.q_ref), channel_id=1, source_target_pairs={{0,8},{2,10},{4,12},{6,14},{8,0},{10,2},{12,4},{14,6},{16,24},{18,... | collective-permute-start | bytes 98312 | tf_op jit(solution)/shard_map/ppermute | solution.py:31
  18.2 10.2 %collective-permute-start.7 = (bf16[4,2,32,256]{3,2,1,0:T(8,128)(2,1)S(1)}, bf16[4,2,32,256]{3,2,1,0:T(8,128)(2,1)S(1)}, u32[]{:S(2)}, u32[]{:S(2)}) collective-permute-start(bf16[4,2,32,256]{3,2,1,0:T(8,128)(2,1)S(1)} %pad_maximum_fusion.2.refs_0_), channel_id=1, source_target_pairs={{0,4},{2,6},{4,0},{6,2},{8,12},{10,14},{12,8},{14,10},{16,20},{18,... | collective-permute-start | bytes 393224 | tf_op jit(solution)/shard_map/ppermute | solution.py:31
  19.7 8.7 %collective-permute-start.8 = (bf16[4,2,32,256]{3,2,1,0:T(8,128)(2,1)S(1)}, bf16[4,2,32,256]{3,2,1,0:T(8,128)(2,1)S(1)}, u32[]{:S(2)}, u32[]{:S(2)}) collective-permute-start(bf16[4,2,32,256]{3,2,1,0:T(8,128)(2,1)S(1)} %pad_maximum_fusion.2.refs_0_), channel_id=1, source_target_pairs={{0,6},{2,4},{4,2},{6,0},{8,14},{10,12},{12,10},{14,8},{16,22},{18,... | collective-permute-start | bytes 393224 | tf_op jit(solution)/shard_map/ppermute | solution.py:31
  20.3 14.2 %collective-permute-start.10 = (bf16[2,192,256]{2,1,0:T(8,128)(2,1)S(1)}, bf16[2,192,256]{2,1,0:T(8,128)(2,1)S(1)}, u32[]{:S(2)}, u32[]{:S(2)}) collective-permute-start(bf16[2,192,256]{2,1,0:T(8,128)(2,1)S(1)} %pad_maximum_fusion.refs_1_), channel_id=1, source_target_pairs={{0,2},{2,0},{4,6},{6,4},{8,10},{10,8},{12,14},{14,12},{16,18},{18,... | collective-permute-start | bytes 589832 | tf_op jit(solution)/shard_map/ppermute | solution.py:31
  21.8 12.7 %collective-permute-start.11 = (bf16[2,192,256]{2,1,0:T(8,128)(2,1)S(1)}, bf16[2,192,256]{2,1,0:T(8,128)(2,1)S(1)}, u32[]{:S(2)}, u32[]{:S(2)}) collective-permute-start(bf16[2,192,256]{2,1,0:T(8,128)(2,1)S(1)} %pad_maximum_fusion.refs_1_), channel_id=1, source_target_pairs={{0,4},{2,6},{4,0},{6,2},{8,12},{10,14},{12,8},{14,10},{16,20},{18,... | collective-permute-start | bytes 589832 | tf_op jit(solution)/shard_map/ppermute | solution.py:31
  23.3 11.2 %collective-permute-start.12 = (bf16[2,192,256]{2,1,0:T(8,128)(2,1)S(1)}, bf16[2,192,256]{2,1,0:T(8,128)(2,1)S(1)}, u32[]{:S(2)}, u32[]{:S(2)}) collective-permute-start(bf16[2,192,256]{2,1,0:T(8,128)(2,1)S(1)} %pad_maximum_fusion.refs_1_), channel_id=1, source_target_pairs={{0,6},{2,4},{4,2},{6,0},{8,14},{10,12},{12,10},{14,8},{16,22},{18,... | collective-permute-start | bytes 589832 | tf_op jit(solution)/shard_map/ppermute | solution.py:31
  29.6 4.7 %collective-permute-start.9 = (bf16[128,384]{1,0:T(8,128)(2,1)S(1)}, bf16[128,384]{1,0:T(8,128)(2,1)S(1)}, u32[]{:S(2)}, u32[]{:S(2)}) collective-permute-start(bf16[128,384]{1,0:T(8,128)(2,1)S(1)} %shard_map.75.part_ref), channel_id=1, source_target_pairs={{0,8},{2,10},{4,12},{6,14},{8,0},{10,2},{12,4},{14,6},{16,24},{18,... | collective-permute-start | bytes 294920 | tf_op jit(solution)/shard_map/ppermute | solution.py:31
  34.9 1.5 %collective-permute-start.13 = (bf16[128,768]{1,0:T(8,128)(2,1)S(1)}, bf16[128,768]{1,0:T(8,128)(2,1)S(1)}, u32[]{:S(2)}, u32[]{:S(2)}) collective-permute-start(bf16[128,768]{1,0:T(8,128)(2,1)S(1)} %shard_map.78), channel_id=1, source_target_pairs={{0,1},{1,0},{2,3},{3,2},{4,5},{5,4},{6,7},{7,6},{8,9},{9,8},{10,11... | collective-permute-start | bytes 589832 | tf_op jit(solution)/shard_map/ppermute | solution.py:31
  36.5 4.9 %collective-permute-start.14 = (bf16[2,32,768]{2,1,0:T(8,128)(2,1)S(1)}, bf16[2,32,768]{2,1,0:T(8,128)(2,1)S(1)}, u32[]{:S(2)}, u32[]{:S(2)}) collective-permute-start(bf16[2,32,768]{2,1,0:T(8,128)(2,1)S(1)} %get-tuple-element.29), channel_id=1, source_target_pairs={{0,8},{2,10},{4,12},{6,14},{8,0},{10,2},{12,4},{14,6},{16,24},{18,... | collective-permute-start | bytes 294920 | tf_op jit(solution)/shard_map/ppermute | solution.py:31

commit v7 on v6

--- a/solution.py
+++ b/solution.py
@@ -11,6 +11,7 @@
 DH = 128
 STEPS = 2
 PLANE = 4
+SPLIT = 4
 MIB = 1024 * 1024
 VMEM = pl.BlockSpec(memory_space=pltpu.VMEM)
 SMEM = pl.BlockSpec(memory_space=pltpu.SMEM)
@@ -19,24 +20,23 @@
 NT = (((1,), (1,)), ((), ()))
 
 
-def angle_tables(positions):
-    half = DH // 2
-    frequency = 10000.0 ** (-(2.0 * jnp.arange(half, dtype=F32)) / DH)
-    grid = positions.astype(F32)[:, None] * frequency[None, :]
-    cos, sin = jnp.cos(grid), jnp.sin(grid)
-    return jnp.concatenate([cos, cos], axis=1), jnp.concatenate([-sin, sin], axis=1)
-
-
 def swap(values, axis, count, bit):
     return lax.ppermute(values, axis, [(i, i ^ bit) for i in range(count)])
 
 
-def load_kernel(ids, *refs):
-    count = len(refs) // 2 - 1
-    ids_out, sems = refs[-2:]
+def load_kernel(ids, slab, w_ref, x_ref, mod_ref, w_out, x_out, mod_out, ids_out, cos_ref, sin_ref, sems):
+    part = w_ref.shape[1] // SPLIT
     copies = [
-        pltpu.make_async_copy(refs[i], refs[count + i], sems.at[i]) for i in range(count)
+        pltpu.make_async_copy(
+            w_ref.at[slot, pl.ds(k * part, part)],
+            w_out.at[slot, pl.ds(k * part, part)],
+            sems.at[slot * SPLIT + k],
+        )
+        for slot in range(3)
+        for k in range(SPLIT)
     ]
+    copies.append(pltpu.make_async_copy(x_ref, x_out, sems.at[3 * SPLIT]))
+    copies.append(pltpu.make_async_copy(mod_ref, mod_out, sems.at[3 * SPLIT + 1]))
     for copy in copies:
         copy.start()
     row = lax.broadcasted_iota(jnp.int32, ids_out.shape, 0)
@@ -44,6 +44,14 @@
     for step in range(STEPS):
         tile = jnp.where(row == step, ids[step], tile)
     ids_out[...] = tile
+    rows, half = cos_ref.shape[0], DH // 2
+    lane = lax.broadcasted_iota(jnp.int32, cos_ref.shape, 1)
+    spot = slab[0] * rows + lax.broadcasted_iota(jnp.int32, cos_ref.shape, 0)
+    power = jnp.where(lane < half, lane, lane - half).astype(F32) * (-2.0 / DH)
+    angle = spot.astype(F32) * jnp.exp(power * math.log(10000.0))
+    cos_ref[...] = jnp.cos(angle)
+    sin = jnp.sin(angle)
+    sin_ref[...] = jnp.where(lane < half, -sin, sin)
     for copy in copies:
         copy.wait()
 
@@ -56,46 +64,63 @@
     )
 
 
-def qkv_kernel(n_head, head, ids_ref, *refs):
+def normalized(step, x_refs, mod_refs, ids_ref):
+    hidden = [ref[step].astype(F32) for ref in x_refs]
+    width = sum(part.shape[1] for part in hidden)
+    mean = sum(jnp.sum(part, axis=1, keepdims=True) for part in hidden) / width
+    square = sum(jnp.sum(part * part, axis=1, keepdims=True) for part in hidden) / width
+    inv = lax.rsqrt(square - mean * mean + 1e-06)
+    parts = []
+    for part, mod_ref in zip(hidden, mod_refs):
+        shift = table_row(mod_ref, 0, ids_ref, step)
+        scale = table_row(mod_ref, 1, ids_ref, step)
+        parts.append(((part - mean) * inv * (1.0 + scale) + shift).astype(BF16))
+    return parts
+
+
+def projected(parts, w_ref, slot, head):
+    feats = parts[0].shape[1]
+    total = jnp.zeros((parts[0].shape[0], w_ref.shape[2]), F32)
+    for number, part in enumerate(parts):
+        start = pl.multiple_of((head[0] ^ number) * feats, feats)
+        w = w_ref[slot, pl.ds(start, feats), :]
+        total += jnp.dot(part, w, preferred_element_type=F32)
+    return total
+
+
+def rotated(values, cos, sin):
+    blocks = []
+    for start in range(0, values.shape[1], DH):
+        u = values[:, start : start + DH]
+        blocks.append(u * cos + pltpu.roll(u, DH // 2, 1) * sin)
+    return jnp.concatenate(blocks, axis=1)
+
+
+def fresh_kernel(n_head, head, ids_ref, *refs):
     x_refs, mod_refs = refs[:n_head], refs[n_head : 2 * n_head]
     w_ref, cos_ref, sin_ref = refs[2 * n_head : 2 * n_head + 3]
-    q_ref, kv0_ref, kv1_ref, a_ref = refs[-4:]
-    rows, feats = x_refs[0].shape[1:]
-    width = n_head * feats
-    cols = w_ref.shape[2]
+    a_ref, kv0_ref = refs[-2:]
+    parts = normalized(0, x_refs, mod_refs, ids_ref)
+    for number, part in enumerate(parts):
+        a_ref[number] = part
+    keys = rotated(projected(parts, w_ref, 1, head), cos_ref[...], sin_ref[...])
+    kv0_ref[0] = keys.astype(BF16)
+    kv0_ref[1] = projected(parts, w_ref, 2, head).astype(BF16)
+
+
+def rest_kernel(n_head, head, ids_ref, *refs):
+    x_refs, mod_refs = refs[:n_head], refs[n_head : 2 * n_head]
+    w_ref, cos_ref, sin_ref, a_ref, q_ref, kv1_ref = refs[2 * n_head :]
+    rows = a_ref.shape[1]
+    parts = normalized(1, x_refs, mod_refs, ids_ref)
+    cos, sin = cos_ref[...], sin_ref[...]
+    both = [jnp.concatenate([a_ref[k], part], axis=0) for k, part in enumerate(parts)]
+    queries = projected(both, w_ref, 0, head)
     for step in range(STEPS):
-        total, square = 0.0, 0.0
-        for x_ref in x_refs:
-            hidden = x_ref[step].astype(F32)
-            total += jnp.sum(hidden, axis=1, keepdims=True)
-            square += jnp.sum(hidden * hidden, axis=1, keepdims=True)
-        mean = total / width
-        inv = lax.rsqrt(square / width - mean * mean + 1e-06)
-        for part in range(n_head):
-            shift = table_row(mod_refs[part], 0, ids_ref, step)
-            scale = table_row(mod_refs[part], 1, ids_ref, step)
-            hidden = x_refs[part][step].astype(F32)
-            a = (hidden - mean) * inv * (1.0 + scale) + shift
-            a_ref[part, step * rows : (step + 1) * rows, :] = a.astype(BF16)
-    cos, sin = cos_ref[...], sin_ref[...]
-    for slot in range(3):
-        total = jnp.zeros((STEPS * rows, cols), F32)
-        for part in range(n_head):
-            start = pl.multiple_of((head[0] ^ part) * feats, feats)
-            total += jnp.dot(
-                a_ref[part], w_ref[slot, pl.ds(start, feats), :], preferred_element_type=F32
-            )
-        for step in range(STEPS):
-            for block in range(cols // DH):
-                lanes = slice(block * DH, (block + 1) * DH)
-                u = total[step * rows : (step + 1) * rows, lanes]
-                if slot < 2:
-                    u = u * cos + pltpu.roll(u, DH // 2, 1) * sin
-                u = u.astype(BF16)
-                if slot == 0:
-                    q_ref[step, :, lanes] = u
-                else:
-                    (kv0_ref, kv1_ref)[step][slot - 1, :, lanes] = u
+        spot = slice(step * rows, (step + 1) * rows)
+        q_ref[step] = rotated(queries[spot], cos, sin).astype(BF16)
+    kv1_ref[0] = rotated(projected(parts, w_ref, 1, head), cos, sin).astype(BF16)
+    kv1_ref[1] = projected(parts, w_ref, 2, head).astype(BF16)
 
 
 def split3(values):
@@ -105,24 +130,23 @@
 
 
 def attend_kernel(q_ref, mate_ref, kv1_ref, *refs):
-    kv_refs, out_ref = refs[:PLANE], refs[PLANE]
-    blocks, _, rows, cols = kv_refs[0].shape
-    blocks = blocks // STEPS
+    stale_refs, kv0_refs, out_ref = refs[:PLANE], refs[PLANE : 2 * PLANE], refs[2 * PLANE]
+    blocks, _, rows, cols = kv0_refs[0].shape
     old_rows = PLANE * blocks * rows
     shape = (2 * rows, old_rows + rows)
     mine = lax.broadcasted_iota(jnp.int32, shape, 0) < rows
     drop = lax.broadcasted_iota(jnp.int32, shape, 1) // rows == jnp.where(mine, 0, PLANE * blocks)
     lane = lax.broadcasted_iota(jnp.int32, (2 * rows, DH), 1)
     for step in range(STEPS):
-        spot = slice(step * blocks, (step + 1) * blocks)
-        fresh = (kv_refs[0].at[blocks], kv1_ref)[step]
+        before = (stale_refs, kv0_refs)[step]
+        fresh = (kv0_refs[0].at[0], kv1_ref)[step]
         stats = jnp.zeros((2 * rows, DH), F32)
         mixed = []
         for head in range(cols // DH):
             lanes = slice(head * DH, (head + 1) * DH)
 
             def rows_of(kind):
-                old = [ref[spot, kind, :, lanes].reshape(blocks * rows, DH) for ref in kv_refs]
+                old = [ref[:, kind, :, lanes].reshape(blocks * rows, DH) for ref in before]
                 return jnp.concatenate([*old, fresh[kind, :, lanes]], axis=0)
 
             queries = jnp.concatenate([q_ref[step, :, lanes], mate_ref[step, :, lanes]], axis=0)
@@ -216,13 +240,14 @@
     x_parts = [swap(inputs, "head", n_head, k) for k in range(1, n_head)]
     mod_parts = [swap(mod_table, "head", n_head, k) for k in range(1, n_head)]
     first = (jnp.transpose(w_qkv, (1, 0, 2)), inputs, jnp.transpose(mod_table, (1, 0, 2)))
-    w, x_own, mod_own, ids = call(
+    w, x_own, mod_own, ids, cos, sin = call(
         load_kernel,
-        tuple(pltpu.VMEM(v.shape, v.dtype) for v in first) + (shaped((8, DH), jnp.int32),),
-        [SMEM] + [ANY] * len(first),
-        [pltpu.SemaphoreType.DMA((len(first),))],
+        tuple(pltpu.VMEM(v.shape, v.dtype) for v in first)
+        + (shaped((8, DH), jnp.int32), shaped((rows, DH), F32), shaped((rows, DH), F32)),
+        [SMEM] * 2 + [ANY] * len(first),
+        [pltpu.SemaphoreType.DMA((3 * SPLIT + 2,))],
         size=2 * w_qkv.size,
-    )(*map(in_hbm, (step_ids, *first)))
+    )(in_hbm(step_ids), slab_order, *map(in_hbm, first))
     x_parts = [x_own] + x_parts
     mod_parts = [mod_own] + [jnp.transpose(part, (1, 0, 2)) for part in mod_parts]
 
@@ -238,30 +263,39 @@
     stale_pair = line_of(stale_kv)
     w_pair = line_of(w_out.T)
 
-    positions = slab_order[0] * rows + jnp.arange(rows, dtype=jnp.int32)
-    cos, sin = angle_tables(positions)
     kv_shape = shaped((2, rows, cols), BF16)
-    q, kv0, kv1 = call(
-        functools.partial(qkv_kernel, n_head),
-        (kv_shape,) * 3,
-        [SMEM] + [VMEM] * (2 * n_head + 4) + [ANY] * (n_head - 1),
-        [pltpu.VMEM((n_head, STEPS * rows, feats), BF16)],
-        2 * STEPS * rows * w_qkv.size,
-        2 * w_qkv.size,
-    )(head[None], ids, *x_parts, *mod_parts, w, cos, sin, *stale_pair[1:])
+    common = (head[None], ids, *x_parts, *mod_parts, w, cos, sin)
+    specs = [SMEM] + [VMEM] * (2 * n_head + 4)
+    a, kv0 = call(
+        functools.partial(fresh_kernel, n_head),
+        (shaped((n_head, rows, feats), BF16), kv_shape),
+        specs + [ANY] * (n_head - 1),
+        flops=4 * rows * w_qkv.size // 3,
+        size=2 * w_qkv.size,
+    )(*common, *stale_pair[1:])
+    q, kv1 = call(
+        functools.partial(rest_kernel, n_head),
+        (kv_shape, kv_shape),
+        specs + [VMEM],
+        flops=8 * rows * w_qkv.size // 3,
+        size=2 * w_qkv.size,
+    )(*common, a)
 
     kv_pair = line_of(kv0)
     q_mate = across(q, PLANE)
-    w_pair, kv_pair = lax.optimization_barrier((w_pair, kv_pair))
-    kv_plane = plane_of(jnp.stack(stale_pair + kv_pair))
+    stale_pair, w_pair, kv0 = lax.optimization_barrier((stale_pair, w_pair, kv0))
+    stale_plane = plane_of(jnp.stack(stale_pair))
+    kv_pair, stale_plane, q_mate = lax.optimization_barrier((kv_pair, stale_plane, q_mate))
+    kv_plane = plane_of(jnp.stack(kv_pair))
+    w_pair, kv_plane = lax.optimization_barrier((w_pair, kv_plane))
     w_plane = plane_of(jnp.stack(w_pair))
     tall = 2 * STEPS * rows
     part = call(
         attend_kernel,
         shaped((tall, cols + DH), BF16),
-        [VMEM] * (3 + PLANE),
+        [VMEM] * (3 + 2 * PLANE),
         flops=4 * STEPS * rows * n_patch * rows * cols,
-    )(q, q_mate, kv1, *kv_plane)
+    )(q, q_mate, kv1, *stale_plane, *kv_plane)
     o = call(merge_kernel, shaped((tall, cols), BF16), [VMEM] * 2)(part, across(part, PLANE))
     wide = PLANE * piece
 

time: 42.3 us -> 49.5 us (1.17)
  starting transfers between devices: 16.5 us -> 23.5 us
  Pallas kernels: 6.61 us -> 7.49 us
  waiting for transfers between devices: 17.3 us -> 16.8 us
    ppermute x15 -> x18, starting transfers between devices: 16.5 us -> 23.5 us  [swap(): return lax.ppermute(values, axis, [(i, i ^ bit) for i in range(count)])]
    pallas_call x2 -> x3, Pallas kernels: 2.28 us -> 3.06 us  [the longest x1 1.11 us: body(): call(attend_kernel, shaped((tall, cols + DH), BF16), [VMEM] * (3 + 2 * PL...]
    ppermute x15 -> x18, waiting for transfers between devices: 17.3 us -> 16.8 us  [swap(): return lax.ppermute(values, axis, [(i, i ^ bit) for i in range(count)])]
  transfers between devices with their start and end apart: 15 -> 18, of which waited for: 5 -> 8; matrix products, arithmetic and copies ran while one was open for 1% -> 0% of each run, Pallas kernels for 14% -> 14%
where the time goes in v7:
time: 49.5 us; the launch traced here: 49.3 us
  starting transfers between devices  23.5 us (47%)
  waiting for transfers between devices  16.8 us (34%)
  Pallas kernels  7.49 us (15%)
  between operations  0.81 us (2%)
  other arithmetic  0.75 us (2%)
    ppermute x18, starting transfers between devices, swap(): return lax.ppermute(values, axis, [(i, i ^ bit) for i in range(count)])  23.5 us
    ppermute x18, waiting for transfers between devices, swap(): return lax.ppermute(values, axis, [(i, i ^ bit) for i in range(count)])  16.8 us
    pallas_call x1, Pallas kernels, body(): call(load_kernel, tuple((pltpu.VMEM(v.shape, v.dtype) for v in first)) +...  3.28 us
    pallas_call x1, Pallas kernels, body(): call(attend_kernel, shaped((tall, cols + DH), BF16), [VMEM] * (3 + 2 * PL...  1.11 us
    pallas_call x1, Pallas kernels, body(): call(functools.partial(rest_kernel, n_head), (kv_shape, kv_shape), specs...  1.1 us
  transfers between devices with their start and end apart: 18, of which 8 were waited for; matrix products, arithmetic and copies ran while one was open for 0% of the time, Pallas kernels for 14%

profile of v7, /device:TPU:0, one launch (start us, length us, event | category | flops | bytes accessed | tf_op | source)
XLA Modules:
  0.0 49.3 jit_solution(7768529124289401306)
XLA Ops:
  0.0 0.5 collective-permute-start
  0.5 3.6 %collective-permute-start.4 = (bf16[192,256]{1,0:T(8,128)(2,1)}, bf16[192,256]{1,0:T(8,128)(2,1)S(1)}, u32[]{:S(2)}, u32[]{:S(2)}) collective-permute-start(bf16[192,256]{1,0:T(8,128)(2,1)} %bitcast.17), channel_id=1, source_target_pairs={{0,16},{2,18},{4,20},{6,22},{8,24},{10,26},{12,28},{14,30},{16,0},... | collective-permute-start | bytes 294920 | tf_op jit(solution)/shard_map/ppermute | solution.py:24
  4.0 0.2 collective-permute-start.1
  4.3 0.3 collective-permute-start.2
  5.2 0.0 copy-start.1
  5.2 3.3 %shard_map.73 = (bf16[3,3072,256]{2,1,0:T(8,128)(2,1)S(1)}, bf16[2,32,1536]{2,1,0:T(8,128)(2,1)S(1)}, f32[3,4,1536]{2,1,0:T(4,128)S(1)}, s32[8,128]{1,0:T(8,128)...) custom-call(s32[2]{0:T(128)} %ids.1, s32[1]{0:T(128)S(6)} %copy.8.slab, bf16[3,3072,256]{2,1,0:T(8,128)(2,1)} %bitcast.16, ...), custom_call_target="tpu_custom_call" | custom-call | bytes 4718592 | tf_op jit(solution)/shard_map/pallas_call | solution.py:243
  8.5 2.7 %collective-permute-done.2.refs_7_ = bf16[2,32,256]{2,1,0:T(8,128)(2,1)S(1)} collective-permute-done((bf16[2,32,256]{2,1,0:T(8,128)(2,1)}, bf16[2,32,256]{2,1,0:T(8,128)(2,1)S(1)}, u32[]{:S(2)}, u32[]{:S(2)}) %collective-permute-start.2) | collective-permute-done | bytes 32800 | tf_op jit(solution)/shard_map/ppermute | solution.py:24
  11.2 0.0 collective-permute-done.1
  11.2 0.0 collective-permute-done.refs_1_
  11.2 0.8 %shard_map.74 = (bf16[2,32,1536]{2,1,0:T(8,128)(2,1)S(1)}, bf16[2,32,256]{2,1,0:T(8,128)(2,1)S(1)}) custom-call(s32[1]{0:T(128)} %bitcast.3.head, s32[8,128]{1,0:T(8,128)S(1)} %get-tuple-element.34.ids_ref, bf16[2,32,1536]{2,1,0:T(8,128)(2,1)S(1)} %get-tuple-element.36.refs_0_, bf16[2,32,1536]{2,1,0:T(8,128)(2,1)S(1)} %collective-permute-done.refs_1_, ...), custom_call_target="tpu_custom_call" | custom-call | flops 100663296 | bytes 4718592 | tf_op jit(solution)/shard_map/pallas_call | solution.py:269
  12.1 0.0 collective-permute-done.4
  12.1 0.0 copy-done.1
  12.1 1.6 %collective-permute-start.5 = (bf16[2,2,32,256]{3,2,1,0:T(8,128)(2,1)S(1)}, bf16[2,2,32,256]{3,2,1,0:T(8,128)(2,1)S(1)}, u32[]{:S(2)}, u32[]{:S(2)}) collective-permute-start(bf16[2,2,32,256]{3,2,1,0:T(8,128)(2,1)S(1)} %pad_maximum_fusion.2.refs_0_), channel_id=1, source_target_pairs={{0,2},{2,0},{4,6},{6,4},{8,10},{10,8},{12,14},{14,12},{16,18},{18,... | collective-permute-start | bytes 196616 | tf_op jit(solution)/shard_map/ppermute | solution.py:24
  13.7 1.5 %collective-permute-start.6 = (bf16[2,2,32,256]{3,2,1,0:T(8,128)(2,1)S(1)}, bf16[2,2,32,256]{3,2,1,0:T(8,128)(2,1)S(1)}, u32[]{:S(2)}, u32[]{:S(2)}) collective-permute-start(bf16[2,2,32,256]{3,2,1,0:T(8,128)(2,1)S(1)} %pad_maximum_fusion.2.refs_0_), channel_id=1, source_target_pairs={{0,4},{2,6},{4,0},{6,2},{8,12},{10,14},{12,8},{14,10},{16,20},{18,... | collective-permute-start | bytes 196616 | tf_op jit(solution)/shard_map/ppermute | solution.py:24
  15.3 0.4 collective-permute-start.7
  15.7 0.0 collective-permute-start.3
  15.7 1.1 %shard_map.75 = (bf16[2,32,256]{2,1,0:T(8,128)(2,1)S(1)}, bf16[2,32,256]{2,1,0:T(8,128)(2,1)S(1)}) custom-call(s32[1]{0:T(128)} %bitcast.3.head, s32[8,128]{1,0:T(8,128)S(1)} %get-tuple-element.34.ids_ref, bf16[2,32,1536]{2,1,0:T(8,128)(2,1)S(1)} %get-tuple-element.36.refs_0_, bf16[2,32,1536]{2,1,0:T(8,128)(2,1)S(1)} %collective-permute-done.refs_1_, ...), custom_call_target="tpu_custom_call" | custom-call | flops 201326592 | bytes 4718592 | tf_op jit(solution)/shard_map/pallas_call | solution.py:276
  16.8 4.2 %collective-permute-start.8 = (bf16[2,32,256]{2,1,0:T(8,128)(2,1)S(1)}, bf16[2,32,256]{2,1,0:T(8,128)(2,1)S(1)}, u32[]{:S(2)}, u32[]{:S(2)}) collective-permute-start(bf16[2,32,256]{2,1,0:T(8,128)(2,1)S(1)} %get-tuple-element.41.q_ref), channel_id=1, source_target_pairs={{0,8},{2,10},{4,12},{6,14},{8,0},{10,2},{12,4},{14,6},{16,24},{18,... | collective-permute-start | bytes 98312 | tf_op jit(solution)/shard_map/ppermute | solution.py:24
  21.0 0.0 collective-permute-done.3
  21.0 1.9 %collective-permute-done.8.mate_ref = bf16[2,32,256]{2,1,0:T(8,128)(2,1)S(1)} collective-permute-done((bf16[2,32,256]{2,1,0:T(8,128)(2,1)S(1)}, bf16[2,32,256]{2,1,0:T(8,128)(2,1)S(1)}, u32[]{:S(2)}, u32[]{:S(2)}) %collective-permute-start.8) | collective-permute-done | bytes 32800 | tf_op jit(solution)/shard_map/ppermute | solution.py:24
  22.9 0.0 collective-permute-done.5.refs_1_
  22.9 0.0 collective-permute-done.6.refs_2_
  22.9 0.0 collective-permute-done.7.refs_3_
  22.9 1.6 %collective-permute-start.9 = (bf16[2,2,32,256]{3,2,1,0:T(8,128)(2,1)S(1)}, bf16[2,2,32,256]{3,2,1,0:T(8,128)(2,1)S(1)}, u32[]{:S(2)}, u32[]{:S(2)}) collective-permute-start(bf16[2,2,32,256]{3,2,1,0:T(8,128)(2,1)S(1)} %pad_maximum_fusion.3.refs_4_), channel_id=1, source_target_pairs={{0,2},{2,0},{4,6},{6,4},{8,10},{10,8},{12,14},{14,12},{16,18},{18,... | collective-permute-start | bytes 196616 | tf_op jit(solution)/shard_map/ppermute | solution.py:24
  24.5 1.5 %collective-permute-start.10 = (bf16[2,2,32,256]{3,2,1,0:T(8,128)(2,1)S(1)}, bf16[2,2,32,256]{3,2,1,0:T(8,128)(2,1)S(1)}, u32[]{:S(2)}, u32[]{:S(2)}) collective-permute-start(bf16[2,2,32,256]{3,2,1,0:T(8,128)(2,1)S(1)} %pad_maximum_fusion.3.refs_4_), channel_id=1, source_target_pairs={{0,4},{2,6},{4,0},{6,2},{8,12},{10,14},{12,8},{14,10},{16,20},{18,... | collective-permute-start | bytes 196616 | tf_op jit(solution)/shard_map/ppermute | solution.py:24
  26.0 0.5 collective-permute-start.11
  26.4 1.0 %collective-permute-done.9.refs_5_ = bf16[2,2,32,256]{3,2,1,0:T(8,128)(2,1)S(1)} collective-permute-done((bf16[2,2,32,256]{3,2,1,0:T(8,128)(2,1)S(1)}, bf16[2,2,32,256]{3,2,1,0:T(8,128)(2,1)S(1)}, u32[]{:S(2)}, u32[]{:S(2)}) %collective-permute-start.9) | collective-permute-done | bytes 65568 | tf_op jit(solution)/shard_map/ppermute | solution.py:24
  27.4 1.3 %collective-permute-done.10.refs_6_ = bf16[2,2,32,256]{3,2,1,0:T(8,128)(2,1)S(1)} collective-permute-done((bf16[2,2,32,256]{3,2,1,0:T(8,128)(2,1)S(1)}, bf16[2,2,32,256]{3,2,1,0:T(8,128)(2,1)S(1)}, u32[]{:S(2)}, u32[]{:S(2)}) %collective-permute-start.10) | collective-permute-done | bytes 65568 | tf_op jit(solution)/shard_map/ppermute | solution.py:24
  28.7 3.1 %collective-permute-done.11.refs_7_ = bf16[2,2,32,256]{3,2,1,0:T(8,128)(2,1)S(1)} collective-permute-done((bf16[2,2,32,256]{3,2,1,0:T(8,128)(2,1)S(1)}, bf16[2,2,32,256]{3,2,1,0:T(8,128)(2,1)S(1)}, u32[]{:S(2)}, u32[]{:S(2)}) %collective-permute-start.11) | collective-permute-done | bytes 65568 | tf_op jit(solution)/shard_map/ppermute | solution.py:24
  31.8 0.0 copy-done
  31.9 0.6 %collective-permute-start.13 = (bf16[2,192,256]{2,1,0:T(8,128)(2,1)S(1)}, bf16[2,192,256]{2,1,0:T(8,128)(2,1)S(1)}, u32[]{:S(2)}, u32[]{:S(2)}) collective-permute-start(bf16[2,192,256]{2,1,0:T(8,128)(2,1)S(1)} %pad_maximum_fusion.refs_1_), channel_id=1, source_target_pairs={{0,2},{2,0},{4,6},{6,4},{8,10},{10,8},{12,14},{14,12},{16,18},{18,... | collective-permute-start | bytes 589832 | tf_op jit(solution)/shard_map/ppermute | solution.py:24
  32.5 0.0 collective-permute-start.14
  32.5 3.0 %collective-permute-start.15 = (bf16[2,192,256]{2,1,0:T(8,128)(2,1)S(1)}, bf16[2,192,256]{2,1,0:T(8,128)(2,1)S(1)}, u32[]{:S(2)}, u32[]{:S(2)}) collective-permute-start(bf16[2,192,256]{2,1,0:T(8,128)(2,1)S(1)} %pad_maximum_fusion.refs_1_), channel_id=1, source_target_pairs={{0,6},{2,4},{4,2},{6,0},{8,14},{10,12},{12,10},{14,8},{16,22},{18,... | collective-permute-start | bytes 589832 | tf_op jit(solution)/shard_map/ppermute | solution.py:24
  35.4 1.1 %shard_map.76.part_ref = bf16[128,384]{1,0:T(8,128)(2,1)S(1)} custom-call(bf16[2,32,256]{2,1,0:T(8,128)(2,1)S(1)} %get-tuple-element.41.q_ref, bf16[2,32,256]{2,1,0:T(8,128)(2,1)S(1)} %collective-permute-done.8.mate_ref, bf16[2,32,256]{2,1,0:T(8,128)(2,1)S(1)} %get-tuple-element.46.kv1_ref, bf16[2,2,32,256]{3,2,1,0:T(8,128)(2,1)S(1)} %pad_maximum_fusion.2.refs_0_, ...), custom_call_target="tpu_custom_call" | custom-call | flops 33554432 | tf_op jit(solution)/shard_map/pallas_call | solution.py:293
  36.5 2.0 %collective-permute-start.12 = (bf16[128,384]{1,0:T(8,128)(2,1)S(1)}, bf16[128,384]{1,0:T(8,128)(2,1)S(1)}, u32[]{:S(2)}, u32[]{:S(2)}) collective-permute-start(bf16[128,384]{1,0:T(8,128)(2,1)S(1)} %shard_map.76.part_ref), channel_id=1, source_target_pairs={{0,8},{2,10},{4,12},{6,14},{8,0},{10,2},{12,4},{14,6},{16,24},{18,... | collective-permute-start | bytes 294920 | tf_op jit(solution)/shard_map/ppermute | solution.py:24
  38.5 2.7 %collective-permute-done.12.other_ref = bf16[128,384]{1,0:T(8,128)(2,1)S(1)} collective-permute-done((bf16[128,384]{1,0:T(8,128)(2,1)S(1)}, bf16[128,384]{1,0:T(8,128)(2,1)S(1)}, u32[]{:S(2)}, u32[]{:S(2)}) %collective-permute-start.12) | collective-permute-done | bytes 98336 | tf_op jit(solution)/shard_map/ppermute | solution.py:24
  41.2 0.2 shard_map.77.refs_0_
  41.4 0.0 collective-permute-done.13.refs_2_
  41.4 0.0 collective-permute-done.14.refs_3_
  41.5 0.0 collective-permute-done.15.refs_4_
  41.5 0.4 shard_map.79
  41.9 0.1 collective-permute-start.16
  41.9 0.4 shard_map.78.refs_0_
  42.4 1.0 %collective-permute-done.16.refs_1_ = bf16[128,768]{1,0:T(8,128)(2,1)S(1)} collective-permute-done((bf16[128,768]{1,0:T(8,128)(2,1)S(1)}, bf16[128,768]{1,0:T(8,128)(2,1)S(1)}, u32[]{:S(2)}, u32[]{:S(2)}) %collective-permute-start.16) | collective-permute-done | bytes 196640 | tf_op jit(solution)/shard_map/ppermute | solution.py:24
  43.4 0.1 shard_map.80
  43.5 2.0 %collective-permute-start.17 = (bf16[2,32,768]{2,1,0:T(8,128)(2,1)S(1)}, bf16[2,32,768]{2,1,0:T(8,128)(2,1)S(1)}, u32[]{:S(2)}, u32[]{:S(2)}) collective-permute-start(bf16[2,32,768]{2,1,0:T(8,128)(2,1)S(1)} %get-tuple-element.61), channel_id=1, source_target_pairs={{0,8},{2,10},{4,12},{6,14},{8,0},{10,2},{12,4},{14,6},{16,24},{18,... | collective-permute-start | bytes 294920 | tf_op jit(solution)/shard_map/ppermute | solution.py:24
  45.5 3.1 %collective-permute-done.17 = bf16[2,32,768]{2,1,0:T(8,128)(2,1)S(1)} collective-permute-done((bf16[2,32,768]{2,1,0:T(8,128)(2,1)S(1)}, bf16[2,32,768]{2,1,0:T(8,128)(2,1)S(1)}, u32[]{:S(2)}, u32[]{:S(2)}) %collective-permute-start.17) | collective-permute-done | bytes 98336 | tf_op jit(solution)/shard_map/ppermute | solution.py:24
  48.6 0.7 %pad_maximum_fusion.1 = bf16[2,32,1536]{2,1,0:T(8,128)(2,1)} fusion(bf16[2,32,768]{2,1,0:T(8,128)(2,1)S(1)} %get-tuple-element.64, bf16[2,32,768]{2,1,0:T(8,128)(2,1)S(1)} %get-tuple-element.63), kind=kLoop, calls=%fused_computation.1 | loop fusion | flops 393216 | bytes 393216 | tf_op jit(solution)/shard_map/concatenate | solution.py:322
  (5 shorter events, 0.1 us)
Async XLA Ops:
  0.0 11.2 %collective-permute-start = (bf16[2,32,1536]{2,1,0:T(8,128)(2,1)}, bf16[2,32,1536]{2,1,0:T(8,128)(2,1)S(1)}, u32[]{:S(2)}, u32[]{:S(2)}) collective-permute-start(bf16[2,32,1536]{2,1,0:T(8,128)(2,1)} %x_ref.1), channel_id=1, source_target_pairs={{0,1},{1,0},{2,3},{3,2},{4,5},{5,4},{6,7},{7,6},{8,9},{9,8},{10,11... | collective-permute-start | bytes 589832 | tf_op jit(solution)/shard_map/ppermute | solution.py:24
  0.5 11.6 %collective-permute-start.4 = (bf16[192,256]{1,0:T(8,128)(2,1)}, bf16[192,256]{1,0:T(8,128)(2,1)S(1)}, u32[]{:S(2)}, u32[]{:S(2)}) collective-permute-start(bf16[192,256]{1,0:T(8,128)(2,1)} %bitcast.17), channel_id=1, source_target_pairs={{0,16},{2,18},{4,20},{6,22},{8,24},{10,26},{12,28},{14,30},{16,0},... | collective-permute-start | bytes 294920 | tf_op jit(solution)/shard_map/ppermute | solution.py:24
  4.0 7.2 %collective-permute-start.1 = (f32[4,3,1536]{2,0,1:T(4,128)}, f32[4,3,1536]{2,0,1:T(4,128)S(1)}, u32[]{:S(2)}, u32[]{:S(2)}) collective-permute-start(f32[4,3,1536]{2,0,1:T(4,128)} %param.11), channel_id=1, source_target_pairs={{0,1},{1,0},{2,3},{3,2},{4,5},{5,4},{6,7},{7,6},{8,9},{9,8},{10,11... | collective-permute-start | bytes 221192 | tf_op jit(solution)/shard_map/ppermute | solution.py:24
  4.3 7.0 %collective-permute-start.2 = (bf16[2,32,256]{2,1,0:T(8,128)(2,1)}, bf16[2,32,256]{2,1,0:T(8,128)(2,1)S(1)}, u32[]{:S(2)}, u32[]{:S(2)}) collective-permute-start(bf16[2,32,256]{2,1,0:T(8,128)(2,1)} %param.8), channel_id=1, source_target_pairs={{0,16},{2,18},{4,20},{6,22},{8,24},{10,26},{12,28},{14,30},{16,0},... | collective-permute-start | bytes 98312 | tf_op jit(solution)/shard_map/ppermute | solution.py:24
  5.2 6.9 %copy-start.1 = (bf16[2,32,256]{2,1,0:T(8,128)(2,1)S(1)}, bf16[2,32,256]{2,1,0:T(8,128)(2,1)}, u32[]{:S(2)}) copy-start(bf16[2,32,256]{2,1,0:T(8,128)(2,1)} %param.8) | copy-start | bytes 98308
  11.2 20.6 %copy-start = (bf16[256,192]{0,1:T(8,128)(2,1)S(1)}, bf16[256,192]{0,1:T(8,128)(2,1)}, u32[]{:S(2)}) copy-start(bf16[256,192]{0,1:T(8,128)(2,1)} %param.10) | copy-start | bytes 294916
  12.1 10.7 %collective-permute-start.5 = (bf16[2,2,32,256]{3,2,1,0:T(8,128)(2,1)S(1)}, bf16[2,2,32,256]{3,2,1,0:T(8,128)(2,1)S(1)}, u32[]{:S(2)}, u32[]{:S(2)}) collective-permute-start(bf16[2,2,32,256]{3,2,1,0:T(8,128)(2,1)S(1)} %pad_maximum_fusion.2.refs_0_), channel_id=1, source_target_pairs={{0,2},{2,0},{4,6},{6,4},{8,10},{10,8},{12,14},{14,12},{16,18},{18,... | collective-permute-start | bytes 196616 | tf_op jit(solution)/shard_map/ppermute | solution.py:24
  13.7 9.1 %collective-permute-start.6 = (bf16[2,2,32,256]{3,2,1,0:T(8,128)(2,1)S(1)}, bf16[2,2,32,256]{3,2,1,0:T(8,128)(2,1)S(1)}, u32[]{:S(2)}, u32[]{:S(2)}) collective-permute-start(bf16[2,2,32,256]{3,2,1,0:T(8,128)(2,1)S(1)} %pad_maximum_fusion.2.refs_0_), channel_id=1, source_target_pairs={{0,4},{2,6},{4,0},{6,2},{8,12},{10,14},{12,8},{14,10},{16,20},{18,... | collective-permute-start | bytes 196616 | tf_op jit(solution)/shard_map/ppermute | solution.py:24
  15.3 7.6 %collective-permute-start.7 = (bf16[2,2,32,256]{3,2,1,0:T(8,128)(2,1)S(1)}, bf16[2,2,32,256]{3,2,1,0:T(8,128)(2,1)S(1)}, u32[]{:S(2)}, u32[]{:S(2)}) collective-permute-start(bf16[2,2,32,256]{3,2,1,0:T(8,128)(2,1)S(1)} %pad_maximum_fusion.2.refs_0_), channel_id=1, source_target_pairs={{0,6},{2,4},{4,2},{6,0},{8,14},{10,12},{12,10},{14,8},{16,22},{18,... | collective-permute-start | bytes 196616 | tf_op jit(solution)/shard_map/ppermute | solution.py:24
  15.7 5.3 %collective-permute-start.3 = (bf16[2,32,256]{2,1,0:T(8,128)(2,1)S(1)}, bf16[2,32,256]{2,1,0:T(8,128)(2,1)S(1)}, u32[]{:S(2)}, u32[]{:S(2)}) collective-permute-start(bf16[2,32,256]{2,1,0:T(8,128)(2,1)S(1)} %get-tuple-element.53), channel_id=1, source_target_pairs={{0,16},{2,18},{4,20},{6,22},{8,24},{10,26},{12,28},{14,30},{16,0},... | collective-permute-start | bytes 98312 | tf_op jit(solution)/shard_map/ppermute | solution.py:24
  16.8 6.1 %collective-permute-start.8 = (bf16[2,32,256]{2,1,0:T(8,128)(2,1)S(1)}, bf16[2,32,256]{2,1,0:T(8,128)(2,1)S(1)}, u32[]{:S(2)}, u32[]{:S(2)}) collective-permute-start(bf16[2,32,256]{2,1,0:T(8,128)(2,1)S(1)} %get-tuple-element.41.q_ref), channel_id=1, source_target_pairs={{0,8},{2,10},{4,12},{6,14},{8,0},{10,2},{12,4},{14,6},{16,24},{18,... | collective-permute-start | bytes 98312 | tf_op jit(solution)/shard_map/ppermute | solution.py:24
  22.9 4.5 %collective-permute-start.9 = (bf16[2,2,32,256]{3,2,1,0:T(8,128)(2,1)S(1)}, bf16[2,2,32,256]{3,2,1,0:T(8,128)(2,1)S(1)}, u32[]{:S(2)}, u32[]{:S(2)}) collective-permute-start(bf16[2,2,32,256]{3,2,1,0:T(8,128)(2,1)S(1)} %pad_maximum_fusion.3.refs_4_), channel_id=1, source_target_pairs={{0,2},{2,0},{4,6},{6,4},{8,10},{10,8},{12,14},{14,12},{16,18},{18,... | collective-permute-start | bytes 196616 | tf_op jit(solution)/shard_map/ppermute | solution.py:24
  24.5 4.3 %collective-permute-start.10 = (bf16[2,2,32,256]{3,2,1,0:T(8,128)(2,1)S(1)}, bf16[2,2,32,256]{3,2,1,0:T(8,128)(2,1)S(1)}, u32[]{:S(2)}, u32[]{:S(2)}) collective-permute-start(bf16[2,2,32,256]{3,2,1,0:T(8,128)(2,1)S(1)} %pad_maximum_fusion.3.refs_4_), channel_id=1, source_target_pairs={{0,4},{2,6},{4,0},{6,2},{8,12},{10,14},{12,8},{14,10},{16,20},{18,... | collective-permute-start | bytes 196616 | tf_op jit(solution)/shard_map/ppermute | solution.py:24
  26.0 5.9 %collective-permute-start.11 = (bf16[2,2,32,256]{3,2,1,0:T(8,128)(2,1)S(1)}, bf16[2,2,32,256]{3,2,1,0:T(8,128)(2,1)S(1)}, u32[]{:S(2)}, u32[]{:S(2)}) collective-permute-start(bf16[2,2,32,256]{3,2,1,0:T(8,128)(2,1)S(1)} %pad_maximum_fusion.3.refs_4_), channel_id=1, source_target_pairs={{0,6},{2,4},{4,2},{6,0},{8,14},{10,12},{12,10},{14,8},{16,22},{18,... | collective-permute-start | bytes 196616 | tf_op jit(solution)/shard_map/ppermute | solution.py:24
  31.9 9.6 %collective-permute-start.13 = (bf16[2,192,256]{2,1,0:T(8,128)(2,1)S(1)}, bf16[2,192,256]{2,1,0:T(8,128)(2,1)S(1)}, u32[]{:S(2)}, u32[]{:S(2)}) collective-permute-start(bf16[2,192,256]{2,1,0:T(8,128)(2,1)S(1)} %pad_maximum_fusion.refs_1_), channel_id=1, source_target_pairs={{0,2},{2,0},{4,6},{6,4},{8,10},{10,8},{12,14},{14,12},{16,18},{18,... | collective-permute-start | bytes 589832 | tf_op jit(solution)/shard_map/ppermute | solution.py:24
  32.5 9.0 %collective-permute-start.14 = (bf16[2,192,256]{2,1,0:T(8,128)(2,1)S(1)}, bf16[2,192,256]{2,1,0:T(8,128)(2,1)S(1)}, u32[]{:S(2)}, u32[]{:S(2)}) collective-permute-start(bf16[2,192,256]{2,1,0:T(8,128)(2,1)S(1)} %pad_maximum_fusion.refs_1_), channel_id=1, source_target_pairs={{0,4},{2,6},{4,0},{6,2},{8,12},{10,14},{12,8},{14,10},{16,20},{18,... | collective-permute-start | bytes 589832 | tf_op jit(solution)/shard_map/ppermute | solution.py:24
  32.5 9.0 %collective-permute-start.15 = (bf16[2,192,256]{2,1,0:T(8,128)(2,1)S(1)}, bf16[2,192,256]{2,1,0:T(8,128)(2,1)S(1)}, u32[]{:S(2)}, u32[]{:S(2)}) collective-permute-start(bf16[2,192,256]{2,1,0:T(8,128)(2,1)S(1)} %pad_maximum_fusion.refs_1_), channel_id=1, source_target_pairs={{0,6},{2,4},{4,2},{6,0},{8,14},{10,12},{12,10},{14,8},{16,22},{18,... | collective-permute-start | bytes 589832 | tf_op jit(solution)/shard_map/ppermute | solution.py:24
  36.5 4.7 %collective-permute-start.12 = (bf16[128,384]{1,0:T(8,128)(2,1)S(1)}, bf16[128,384]{1,0:T(8,128)(2,1)S(1)}, u32[]{:S(2)}, u32[]{:S(2)}) collective-permute-start(bf16[128,384]{1,0:T(8,128)(2,1)S(1)} %shard_map.76.part_ref), channel_id=1, source_target_pairs={{0,8},{2,10},{4,12},{6,14},{8,0},{10,2},{12,4},{14,6},{16,24},{18,... | collective-permute-start | bytes 294920 | tf_op jit(solution)/shard_map/ppermute | solution.py:24
  41.9 1.5 %collective-permute-start.16 = (bf16[128,768]{1,0:T(8,128)(2,1)S(1)}, bf16[128,768]{1,0:T(8,128)(2,1)S(1)}, u32[]{:S(2)}, u32[]{:S(2)}) collective-permute-start(bf16[128,768]{1,0:T(8,128)(2,1)S(1)} %shard_map.79), channel_id=1, source_target_pairs={{0,1},{1,0},{2,3},{3,2},{4,5},{5,4},{6,7},{7,6},{8,9},{9,8},{10,11... | collective-permute-start | bytes 589832 | tf_op jit(solution)/shard_map/ppermute | solution.py:24
  43.5 5.1 %collective-permute-start.17 = (bf16[2,32,768]{2,1,0:T(8,128)(2,1)S(1)}, bf16[2,32,768]{2,1,0:T(8,128)(2,1)S(1)}, u32[]{:S(2)}, u32[]{:S(2)}) collective-permute-start(bf16[2,32,768]{2,1,0:T(8,128)(2,1)S(1)} %get-tuple-element.61), channel_id=1, source_target_pairs={{0,8},{2,10},{4,12},{6,14},{8,0},{10,2},{12,4},{14,6},{16,24},{18,... | collective-permute-start | bytes 294920 | tf_op jit(solution)/shard_map/ppermute | solution.py:24

commit v8 on v7

--- a/solution.py
+++ b/solution.py
@@ -11,7 +11,6 @@
 DH = 128
 STEPS = 2
 PLANE = 4
-SPLIT = 4
 MIB = 1024 * 1024
 VMEM = pl.BlockSpec(memory_space=pltpu.VMEM)
 SMEM = pl.BlockSpec(memory_space=pltpu.SMEM)
@@ -25,18 +24,12 @@
 
 
 def load_kernel(ids, slab, w_ref, x_ref, mod_ref, w_out, x_out, mod_out, ids_out, cos_ref, sin_ref, sems):
-    part = w_ref.shape[1] // SPLIT
     copies = [
-        pltpu.make_async_copy(
-            w_ref.at[slot, pl.ds(k * part, part)],
-            w_out.at[slot, pl.ds(k * part, part)],
-            sems.at[slot * SPLIT + k],
-        )
-        for slot in range(3)
-        for k in range(SPLIT)
+        pltpu.make_async_copy(w_ref.at[slot + 1], w_out.at[slot], sems.at[slot])
+        for slot in range(2)
     ]
-    copies.append(pltpu.make_async_copy(x_ref, x_out, sems.at[3 * SPLIT]))
-    copies.append(pltpu.make_async_copy(mod_ref, mod_out, sems.at[3 * SPLIT + 1]))
+    copies.append(pltpu.make_async_copy(x_ref, x_out, sems.at[2]))
+    copies.append(pltpu.make_async_copy(mod_ref, mod_out, sems.at[3]))
     for copy in copies:
         copy.start()
     row = lax.broadcasted_iota(jnp.int32, ids_out.shape, 0)
@@ -103,24 +96,27 @@
     parts = normalized(0, x_refs, mod_refs, ids_ref)
     for number, part in enumerate(parts):
         a_ref[number] = part
-    keys = rotated(projected(parts, w_ref, 1, head), cos_ref[...], sin_ref[...])
+    keys = rotated(projected(parts, w_ref, 0, head), cos_ref[...], sin_ref[...])
     kv0_ref[0] = keys.astype(BF16)
-    kv0_ref[1] = projected(parts, w_ref, 2, head).astype(BF16)
+    kv0_ref[1] = projected(parts, w_ref, 1, head).astype(BF16)
 
 
 def rest_kernel(n_head, head, ids_ref, *refs):
     x_refs, mod_refs = refs[:n_head], refs[n_head : 2 * n_head]
-    w_ref, cos_ref, sin_ref, a_ref, q_ref, kv1_ref = refs[2 * n_head :]
+    w_ref, cos_ref, sin_ref, a_ref, w_far, q_ref, kv1_ref, wq_ref, sem = refs[2 * n_head :]
+    copy = pltpu.make_async_copy(w_far.at[0], wq_ref.at[0], sem)
+    copy.start()
     rows = a_ref.shape[1]
     parts = normalized(1, x_refs, mod_refs, ids_ref)
     cos, sin = cos_ref[...], sin_ref[...]
     both = [jnp.concatenate([a_ref[k], part], axis=0) for k, part in enumerate(parts)]
-    queries = projected(both, w_ref, 0, head)
+    kv1_ref[0] = rotated(projected(parts, w_ref, 0, head), cos, sin).astype(BF16)
+    kv1_ref[1] = projected(parts, w_ref, 1, head).astype(BF16)
+    copy.wait()
+    queries = projected(both, wq_ref, 0, head)
     for step in range(STEPS):
         spot = slice(step * rows, (step + 1) * rows)
         q_ref[step] = rotated(queries[spot], cos, sin).astype(BF16)
-    kv1_ref[0] = rotated(projected(parts, w_ref, 1, head), cos, sin).astype(BF16)
-    kv1_ref[1] = projected(parts, w_ref, 2, head).astype(BF16)
 
 
 def split3(values):
@@ -129,24 +125,25 @@
     return [high, middle, values - high - middle]
 
 
-def attend_kernel(q_ref, mate_ref, kv1_ref, *refs):
-    stale_refs, kv0_refs, out_ref = refs[:PLANE], refs[PLANE : 2 * PLANE], refs[2 * PLANE]
-    blocks, _, rows, cols = kv0_refs[0].shape
+def attend_kernel(patch, q_ref, mate_ref, kv0_ref, kv1_ref, kv_ref, out_ref):
+    rows, cols = kv0_ref.shape[1:]
+    blocks = kv_ref.shape[0] // (2 * STEPS)
     old_rows = PLANE * blocks * rows
     shape = (2 * rows, old_rows + rows)
     mine = lax.broadcasted_iota(jnp.int32, shape, 0) < rows
-    drop = lax.broadcasted_iota(jnp.int32, shape, 1) // rows == jnp.where(mine, 0, PLANE * blocks)
+    stray = jnp.where(mine, patch[0] % PLANE, PLANE * blocks)
+    drop = lax.broadcasted_iota(jnp.int32, shape, 1) // rows == stray
     lane = lax.broadcasted_iota(jnp.int32, (2 * rows, DH), 1)
     for step in range(STEPS):
-        before = (stale_refs, kv0_refs)[step]
-        fresh = (kv0_refs[0].at[0], kv1_ref)[step]
+        first = 2 * blocks * step
+        fresh = (kv0_ref, kv1_ref)[step]
         stats = jnp.zeros((2 * rows, DH), F32)
         mixed = []
         for head in range(cols // DH):
             lanes = slice(head * DH, (head + 1) * DH)
 
             def rows_of(kind):
-                old = [ref[:, kind, :, lanes].reshape(blocks * rows, DH) for ref in before]
+                old = [kv_ref[first + 2 * k + kind, :, lanes] for k in range(blocks)]
                 return jnp.concatenate([*old, fresh[kind, :, lanes]], axis=0)
 
             queries = jnp.concatenate([q_ref[step, :, lanes], mate_ref[step, :, lanes]], axis=0)
@@ -242,10 +239,11 @@
     first = (jnp.transpose(w_qkv, (1, 0, 2)), inputs, jnp.transpose(mod_table, (1, 0, 2)))
     w, x_own, mod_own, ids, cos, sin = call(
         load_kernel,
-        tuple(pltpu.VMEM(v.shape, v.dtype) for v in first)
+        (pltpu.VMEM((2, *first[0].shape[1:]), BF16),)
+        + tuple(pltpu.VMEM(v.shape, v.dtype) for v in first[1:])
         + (shaped((8, DH), jnp.int32), shaped((rows, DH), F32), shaped((rows, DH), F32)),
         [SMEM] * 2 + [ANY] * len(first),
-        [pltpu.SemaphoreType.DMA((3 * SPLIT + 2,))],
+        [pltpu.SemaphoreType.DMA((4,))],
         size=2 * w_qkv.size,
     )(in_hbm(step_ids), slab_order, *map(in_hbm, first))
     x_parts = [x_own] + x_parts
@@ -269,33 +267,34 @@
     a, kv0 = call(
         functools.partial(fresh_kernel, n_head),
         (shaped((n_head, rows, feats), BF16), kv_shape),
-        specs + [ANY] * (n_head - 1),
+        specs,
         flops=4 * rows * w_qkv.size // 3,
         size=2 * w_qkv.size,
-    )(*common, *stale_pair[1:])
+    )(*common)
     q, kv1 = call(
         functools.partial(rest_kernel, n_head),
         (kv_shape, kv_shape),
-        specs + [VMEM],
-        flops=8 * rows * w_qkv.size // 3,
-        size=2 * w_qkv.size,
-    )(*common, a)
+        specs + [VMEM, ANY],
+        [pltpu.VMEM((1, *first[0].shape[1:]), BF16), pltpu.SemaphoreType.DMA],
+        8 * rows * w_qkv.size // 3,
+        2 * w_qkv.size,
+    )(*common, a, in_hbm(first[0]))
 
     kv_pair = line_of(kv0)
     q_mate = across(q, PLANE)
-    stale_pair, w_pair, kv0 = lax.optimization_barrier((stale_pair, w_pair, kv0))
-    stale_plane = plane_of(jnp.stack(stale_pair))
-    kv_pair, stale_plane, q_mate = lax.optimization_barrier((kv_pair, stale_plane, q_mate))
-    kv_plane = plane_of(jnp.stack(kv_pair))
-    w_pair, kv_plane = lax.optimization_barrier((w_pair, kv_plane))
+    w_pair, kv0 = lax.optimization_barrier((w_pair, kv0))
     w_plane = plane_of(jnp.stack(w_pair))
+    planes = [list(range(k, k + PLANE)) for k in range(0, n_patch, PLANE)]
+    kv = lax.all_gather(
+        jnp.concatenate(stale_pair + kv_pair), "patch", axis=1, axis_index_groups=planes, tiled=True
+    )
     tall = 2 * STEPS * rows
     part = call(
         attend_kernel,
         shaped((tall, cols + DH), BF16),
-        [VMEM] * (3 + 2 * PLANE),
+        [SMEM] + [VMEM] * 5,
         flops=4 * STEPS * rows * n_patch * rows * cols,
-    )(q, q_mate, kv1, *stale_plane, *kv_plane)
+    )(patch[None], q, q_mate, kv0, kv1, kv)
     o = call(merge_kernel, shaped((tall, cols), BF16), [VMEM] * 2)(part, across(part, PLANE))
     wide = PLANE * piece
 

time: 49.5 us -> 43.3 us (0.87)
  blocking collectives: 0 us -> 10.1 us
  waiting for transfers between devices: 16.8 us -> 7.33 us
  starting transfers between devices: 23.5 us -> 15.8 us
  Pallas kernels: 7.49 us -> 8.34 us
    all_gather x0 -> x1, blocking collectives: none -> 10.1 us  [body(): lax.all_gather(jnp.concatenate(stale_pair + kv_pair), 'patch', axis=1, ax...]
    ppermute x18 -> x12, waiting for transfers between devices: 16.8 us -> 7.33 us  [swap(): return lax.ppermute(values, axis, [(i, i ^ bit) for i in range(count)])]
    ppermute x18 -> x12, starting transfers between devices: 23.5 us -> 15.8 us  [swap(): return lax.ppermute(values, axis, [(i, i ^ bit) for i in range(count)])]
    pallas_call x1, Pallas kernels: 1.1 us -> 2.64 us  [body(): call(functools.partial(rest_kernel, n_head), (kv_shape, kv_shape), specs...]
    pallas_call x2, Pallas kernels: 4.39 us -> 3.7 us  [the longest x1 2.59 us: body(): call(load_kernel, (pltpu.VMEM((2, *first[0].shape[1:]), BF16),) + tuple((...]
  transfers between devices with their start and end apart: 18 -> 12, of which waited for: 8 -> 3; matrix products, arithmetic and copies ran while one was open for 0% -> 0% of each run, Pallas kernels for 14% -> 18%
where the time goes in v8:
time: 43.3 us; the launch traced here: 43.1 us
  starting transfers between devices  15.8 us (36%)
  blocking collectives  10.1 us (23%)
  Pallas kernels  8.34 us (19%)
  waiting for transfers between devices  7.33 us (17%)
  between operations  0.79 us (2%)
  other arithmetic  0.75 us (2%)
    ppermute x12, starting transfers between devices, swap(): return lax.ppermute(values, axis, [(i, i ^ bit) for i in range(count)])  15.8 us
    all_gather x1, blocking collectives, body(): lax.all_gather(jnp.concatenate(stale_pair + kv_pair), 'patch', axis=1, ax...  10.1 us
    ppermute x12, waiting for transfers between devices, swap(): return lax.ppermute(values, axis, [(i, i ^ bit) for i in range(count)])  7.33 us
    pallas_call x1, Pallas kernels, body(): call(functools.partial(rest_kernel, n_head), (kv_shape, kv_shape), specs...  2.64 us
    pallas_call x1, Pallas kernels, body(): call(load_kernel, (pltpu.VMEM((2, *first[0].shape[1:]), BF16),) + tuple((...  2.59 us
    pallas_call x1, Pallas kernels, body(): call(attend_kernel, shaped((tall, cols + DH), BF16), [SMEM] + [VMEM] * 5,...  1.12 us
  transfers between devices with their start and end apart: 12, of which 3 were waited for; matrix products, arithmetic and copies ran while one was open for 0% of the time, Pallas kernels for 18%

profile of v8, /device:TPU:0, one launch (start us, length us, event | category | flops | bytes accessed | tf_op | source)
XLA Modules:
  0.0 43.1 jit_solution(332755230846844194)
XLA Ops:
  0.0 0.0 copy-start
  0.0 0.5 %collective-permute-start = (bf16[2,32,1536]{2,1,0:T(8,128)(2,1)}, bf16[2,32,1536]{2,1,0:T(8,128)(2,1)S(1)}, u32[]{:S(2)}, u32[]{:S(2)}) collective-permute-start(bf16[2,32,1536]{2,1,0:T(8,128)(2,1)} %x_ref.1), channel_id=1, source_target_pairs={{0,1},{1,0},{2,3},{3,2},{4,5},{5,4},{6,7},{7,6},{8,9},{9,8},{10,11... | collective-permute-start | bytes 589832 | tf_op jit(solution)/shard_map/ppermute | solution.py:23
  0.5 3.6 %collective-permute-start.3 = (bf16[192,256]{1,0:T(8,128)(2,1)}, bf16[192,256]{1,0:T(8,128)(2,1)S(1)}, u32[]{:S(2)}, u32[]{:S(2)}) collective-permute-start(bf16[192,256]{1,0:T(8,128)(2,1)} %bitcast.12), channel_id=1, source_target_pairs={{0,16},{2,18},{4,20},{6,22},{8,24},{10,26},{12,28},{14,30},{16,0},... | collective-permute-start | bytes 294920 | tf_op jit(solution)/shard_map/ppermute | solution.py:23
  4.1 0.2 collective-permute-start.1
  4.3 0.3 collective-permute-start.4
  5.2 2.6 %shard_map.73 = (bf16[2,3072,256]{2,1,0:T(8,128)(2,1)S(1)}, bf16[2,32,1536]{2,1,0:T(8,128)(2,1)S(1)}, f32[3,4,1536]{2,1,0:T(4,128)S(1)}, s32[8,128]{1,0:T(8,128)...) custom-call(s32[2]{0:T(128)} %ids.1, s32[1]{0:T(128)S(6)} %copy.8.slab, bf16[3,3072,256]{2,1,0:T(8,128)(2,1)} %bitcast.10, ...), custom_call_target="tpu_custom_call" | custom-call | bytes 4718592 | tf_op jit(solution)/shard_map/pallas_call | solution.py:240
  7.8 0.0 collective-permute-done.1
  7.8 0.0 collective-permute-done.refs_1_
  7.8 0.8 %shard_map.74 = (bf16[2,32,1536]{2,1,0:T(8,128)(2,1)S(1)}, bf16[2,32,256]{2,1,0:T(8,128)(2,1)S(1)}) custom-call(s32[1]{0:T(128)} %bitcast.3.head, s32[8,128]{1,0:T(8,128)S(1)} %get-tuple-element.20.ids_ref, bf16[2,32,1536]{2,1,0:T(8,128)(2,1)S(1)} %get-tuple-element.22.refs_0_, bf16[2,32,1536]{2,1,0:T(8,128)(2,1)S(1)} %collective-permute-done.refs_1_, ...), custom_call_target="tpu_custom_call" | custom-call | flops 100663296 | bytes 4718592 | tf_op jit(solution)/shard_map/pallas_call | solution.py:267
  8.7 0.0 copy-start.1
  8.7 2.7 %collective-permute-start.5 = (bf16[2,32,256]{2,1,0:T(8,128)(2,1)S(1)}, bf16[2,32,256]{2,1,0:T(8,128)(2,1)S(1)}, u32[]{:S(2)}, u32[]{:S(2)}) collective-permute-start(bf16[2,32,256]{2,1,0:T(8,128)(2,1)S(1)} %get-tuple-element.29.kv0_ref), channel_id=1, source_target_pairs={{0,16},{2,18},{4,20},{6,22},{8,24},{10,26},{12,28},{14,30},{16,0},... | collective-permute-start | bytes 98312 | tf_op jit(solution)/shard_map/ppermute | solution.py:23
  11.4 0.0 collective-permute-done.3
  11.4 0.0 copy-done
  11.4 1.6 %collective-permute-start.7 = (bf16[2,192,256]{2,1,0:T(8,128)(2,1)S(1)}, bf16[2,192,256]{2,1,0:T(8,128)(2,1)S(1)}, u32[]{:S(2)}, u32[]{:S(2)}) collective-permute-start(bf16[2,192,256]{2,1,0:T(8,128)(2,1)S(1)} %pad_maximum_fusion.refs_1_), channel_id=1, source_target_pairs={{0,2},{2,0},{4,6},{6,4},{8,10},{10,8},{12,14},{14,12},{16,18},{18,... | collective-permute-start | bytes 589832 | tf_op jit(solution)/shard_map/ppermute | solution.py:23
  13.0 1.5 %collective-permute-start.8 = (bf16[2,192,256]{2,1,0:T(8,128)(2,1)S(1)}, bf16[2,192,256]{2,1,0:T(8,128)(2,1)S(1)}, u32[]{:S(2)}, u32[]{:S(2)}) collective-permute-start(bf16[2,192,256]{2,1,0:T(8,128)(2,1)S(1)} %pad_maximum_fusion.refs_1_), channel_id=1, source_target_pairs={{0,4},{2,6},{4,0},{6,2},{8,12},{10,14},{12,8},{14,10},{16,20},{18,... | collective-permute-start | bytes 589832 | tf_op jit(solution)/shard_map/ppermute | solution.py:23
  14.5 0.5 %collective-permute-start.9 = (bf16[2,192,256]{2,1,0:T(8,128)(2,1)S(1)}, bf16[2,192,256]{2,1,0:T(8,128)(2,1)S(1)}, u32[]{:S(2)}, u32[]{:S(2)}) collective-permute-start(bf16[2,192,256]{2,1,0:T(8,128)(2,1)S(1)} %pad_maximum_fusion.refs_1_), channel_id=1, source_target_pairs={{0,6},{2,4},{4,2},{6,0},{8,14},{10,12},{12,10},{14,8},{16,22},{18,... | collective-permute-start | bytes 589832 | tf_op jit(solution)/shard_map/ppermute | solution.py:23
  15.0 2.6 %shard_map.75 = (bf16[2,32,256]{2,1,0:T(8,128)(2,1)S(1)}, bf16[2,32,256]{2,1,0:T(8,128)(2,1)S(1)}) custom-call(s32[1]{0:T(128)} %bitcast.3.head, s32[8,128]{1,0:T(8,128)S(1)} %get-tuple-element.20.ids_ref, bf16[2,32,1536]{2,1,0:T(8,128)(2,1)S(1)} %get-tuple-element.22.refs_0_, bf16[2,32,1536]{2,1,0:T(8,128)(2,1)S(1)} %collective-permute-done.refs_1_, ...), custom_call_target="tpu_custom_call" | custom-call | flops 201326592 | bytes 4718592 | tf_op jit(solution)/shard_map/pallas_call | solution.py:274
  17.6 0.0 collective-permute-done.4
  17.6 1.6 %collective-permute-start.2 = (bf16[2,32,256]{2,1,0:T(8,128)(2,1)S(1)}, bf16[2,32,256]{2,1,0:T(8,128)(2,1)S(1)}, u32[]{:S(2)}, u32[]{:S(2)}) collective-permute-start(bf16[2,32,256]{2,1,0:T(8,128)(2,1)S(1)} %get-tuple-element.27.q_ref), channel_id=1, source_target_pairs={{0,8},{2,10},{4,12},{6,14},{8,0},{10,2},{12,4},{14,6},{16,24},{18,... | collective-permute-start | bytes 98312 | tf_op jit(solution)/shard_map/ppermute | solution.py:23
  19.3 0.0 collective-permute-done.5
  19.3 0.0 copy-done.1
  19.3 10.1 %all_gather.3.kv_ref = bf16[8,128,256]{2,1,0:T(8,128)(2,1)S(1)} all-gather(bf16[8,32,256]{2,1,0:T(8,128)(2,1)S(1)} %pad_maximum_fusion.2), channel_id=1, replica_groups={{0,2,4,6},{8,10,12,14},{16,18,20,22},{24,26,28,30},{1,3,5,7},{9,11,13,1..., dimensions={1}, use_global_device_ids=true | all-gather | bytes 655360 | tf_op jit(solution)/shard_map/all_gather | solution.py:288
  29.4 0.0 collective-permute-done.2.mate_ref
  29.4 1.1 %shard_map.76.part_ref = bf16[128,384]{1,0:T(8,128)(2,1)S(1)} custom-call(s32[1]{0:T(128)} %bitcast.patch, bf16[2,32,256]{2,1,0:T(8,128)(2,1)S(1)} %get-tuple-element.27.q_ref, bf16[2,32,256]{2,1,0:T(8,128)(2,1)S(1)} %collective-permute-done.2.mate_ref, bf16[2,32,256]{2,1,0:T(8,128)(2,1)S(1)} %get-tuple-element.29.kv0_ref, ...), custom_call_target="tpu_custom_call" | custom-call | flops 33554432 | tf_op jit(solution)/shard_map/pallas_call | solution.py:292
  30.5 1.6 %collective-permute-start.6 = (bf16[128,384]{1,0:T(8,128)(2,1)S(1)}, bf16[128,384]{1,0:T(8,128)(2,1)S(1)}, u32[]{:S(2)}, u32[]{:S(2)}) collective-permute-start(bf16[128,384]{1,0:T(8,128)(2,1)S(1)} %shard_map.76.part_ref), channel_id=1, source_target_pairs={{0,8},{2,10},{4,12},{6,14},{8,0},{10,2},{12,4},{14,6},{16,24},{18,... | collective-permute-start | bytes 294920 | tf_op jit(solution)/shard_map/ppermute | solution.py:23
  32.1 3.0 %collective-permute-done.6.other_ref = bf16[128,384]{1,0:T(8,128)(2,1)S(1)} collective-permute-done((bf16[128,384]{1,0:T(8,128)(2,1)S(1)}, bf16[128,384]{1,0:T(8,128)(2,1)S(1)}, u32[]{:S(2)}, u32[]{:S(2)}) %collective-permute-start.6) | collective-permute-done | bytes 98336 | tf_op jit(solution)/shard_map/ppermute | solution.py:23
  35.2 0.2 shard_map.77.refs_0_
  35.4 0.0 collective-permute-done.7.refs_2_
  35.4 0.0 collective-permute-done.8.refs_3_
  35.4 0.0 collective-permute-done.9.refs_4_
  35.4 0.4 shard_map.79
  35.8 0.1 collective-permute-start.10
  35.9 0.4 shard_map.78.refs_0_
  36.4 1.0 %collective-permute-done.10.refs_1_ = bf16[128,768]{1,0:T(8,128)(2,1)S(1)} collective-permute-done((bf16[128,768]{1,0:T(8,128)(2,1)S(1)}, bf16[128,768]{1,0:T(8,128)(2,1)S(1)}, u32[]{:S(2)}, u32[]{:S(2)}) %collective-permute-start.10) | collective-permute-done | bytes 196640 | tf_op jit(solution)/shard_map/ppermute | solution.py:23
  37.4 0.1 shard_map.80
  37.5 1.6 %collective-permute-start.11 = (bf16[2,32,768]{2,1,0:T(8,128)(2,1)S(1)}, bf16[2,32,768]{2,1,0:T(8,128)(2,1)S(1)}, u32[]{:S(2)}, u32[]{:S(2)}) collective-permute-start(bf16[2,32,768]{2,1,0:T(8,128)(2,1)S(1)} %get-tuple-element.33), channel_id=1, source_target_pairs={{0,8},{2,10},{4,12},{6,14},{8,0},{10,2},{12,4},{14,6},{16,24},{18,... | collective-permute-start | bytes 294920 | tf_op jit(solution)/shard_map/ppermute | solution.py:23
  39.1 3.3 %collective-permute-done.11 = bf16[2,32,768]{2,1,0:T(8,128)(2,1)S(1)} collective-permute-done((bf16[2,32,768]{2,1,0:T(8,128)(2,1)S(1)}, bf16[2,32,768]{2,1,0:T(8,128)(2,1)S(1)}, u32[]{:S(2)}, u32[]{:S(2)}) %collective-permute-start.11) | collective-permute-done | bytes 98336 | tf_op jit(solution)/shard_map/ppermute | solution.py:23
  42.4 0.7 %pad_maximum_fusion.1 = bf16[2,32,1536]{2,1,0:T(8,128)(2,1)} fusion(bf16[2,32,768]{2,1,0:T(8,128)(2,1)S(1)} %get-tuple-element.36, bf16[2,32,768]{2,1,0:T(8,128)(2,1)S(1)} %get-tuple-element.35), kind=kLoop, calls=%fused_computation.1 | loop fusion | flops 393216 | bytes 393216 | tf_op jit(solution)/shard_map/concatenate | solution.py:321
  (3 shorter events, 0.1 us)
Async XLA Ops:
  0.0 11.4 %copy-start = (bf16[256,192]{0,1:T(8,128)(2,1)S(1)}, bf16[256,192]{0,1:T(8,128)(2,1)}, u32[]{:S(2)}) copy-start(bf16[256,192]{0,1:T(8,128)(2,1)} %param.10) | copy-start | bytes 294916
  0.0 7.8 %collective-permute-start = (bf16[2,32,1536]{2,1,0:T(8,128)(2,1)}, bf16[2,32,1536]{2,1,0:T(8,128)(2,1)S(1)}, u32[]{:S(2)}, u32[]{:S(2)}) collective-permute-start(bf16[2,32,1536]{2,1,0:T(8,128)(2,1)} %x_ref.1), channel_id=1, source_target_pairs={{0,1},{1,0},{2,3},{3,2},{4,5},{5,4},{6,7},{7,6},{8,9},{9,8},{10,11... | collective-permute-start | bytes 589832 | tf_op jit(solution)/shard_map/ppermute | solution.py:23
  0.5 10.9 %collective-permute-start.3 = (bf16[192,256]{1,0:T(8,128)(2,1)}, bf16[192,256]{1,0:T(8,128)(2,1)S(1)}, u32[]{:S(2)}, u32[]{:S(2)}) collective-permute-start(bf16[192,256]{1,0:T(8,128)(2,1)} %bitcast.12), channel_id=1, source_target_pairs={{0,16},{2,18},{4,20},{6,22},{8,24},{10,26},{12,28},{14,30},{16,0},... | collective-permute-start | bytes 294920 | tf_op jit(solution)/shard_map/ppermute | solution.py:23
  4.1 3.7 %collective-permute-start.1 = (f32[4,3,1536]{2,0,1:T(4,128)}, f32[4,3,1536]{2,0,1:T(4,128)S(1)}, u32[]{:S(2)}, u32[]{:S(2)}) collective-permute-start(f32[4,3,1536]{2,0,1:T(4,128)} %param.11), channel_id=1, source_target_pairs={{0,1},{1,0},{2,3},{3,2},{4,5},{5,4},{6,7},{7,6},{8,9},{9,8},{10,11... | collective-permute-start | bytes 221192 | tf_op jit(solution)/shard_map/ppermute | solution.py:23
  4.3 13.4 %collective-permute-start.4 = (bf16[2,32,256]{2,1,0:T(8,128)(2,1)}, bf16[2,32,256]{2,1,0:T(8,128)(2,1)S(1)}, u32[]{:S(2)}, u32[]{:S(2)}) collective-permute-start(bf16[2,32,256]{2,1,0:T(8,128)(2,1)} %param.8), channel_id=1, source_target_pairs={{0,16},{2,18},{4,20},{6,22},{8,24},{10,26},{12,28},{14,30},{16,0},... | collective-permute-start | bytes 98312 | tf_op jit(solution)/shard_map/ppermute | solution.py:23
  8.7 10.6 %copy-start.1 = (bf16[2,32,256]{2,1,0:T(8,128)(2,1)S(1)}, bf16[2,32,256]{2,1,0:T(8,128)(2,1)}, u32[]{:S(2)}) copy-start(bf16[2,32,256]{2,1,0:T(8,128)(2,1)} %param.8) | copy-start | bytes 98308
  8.7 10.6 %collective-permute-start.5 = (bf16[2,32,256]{2,1,0:T(8,128)(2,1)S(1)}, bf16[2,32,256]{2,1,0:T(8,128)(2,1)S(1)}, u32[]{:S(2)}, u32[]{:S(2)}) collective-permute-start(bf16[2,32,256]{2,1,0:T(8,128)(2,1)S(1)} %get-tuple-element.29.kv0_ref), channel_id=1, source_target_pairs={{0,16},{2,18},{4,20},{6,22},{8,24},{10,26},{12,28},{14,30},{16,0},... | collective-permute-start | bytes 98312 | tf_op jit(solution)/shard_map/ppermute | solution.py:23
  11.4 24.0 %collective-permute-start.7 = (bf16[2,192,256]{2,1,0:T(8,128)(2,1)S(1)}, bf16[2,192,256]{2,1,0:T(8,128)(2,1)S(1)}, u32[]{:S(2)}, u32[]{:S(2)}) collective-permute-start(bf16[2,192,256]{2,1,0:T(8,128)(2,1)S(1)} %pad_maximum_fusion.refs_1_), channel_id=1, source_target_pairs={{0,2},{2,0},{4,6},{6,4},{8,10},{10,8},{12,14},{14,12},{16,18},{18,... | collective-permute-start | bytes 589832 | tf_op jit(solution)/shard_map/ppermute | solution.py:23
  13.0 22.4 %collective-permute-start.8 = (bf16[2,192,256]{2,1,0:T(8,128)(2,1)S(1)}, bf16[2,192,256]{2,1,0:T(8,128)(2,1)S(1)}, u32[]{:S(2)}, u32[]{:S(2)}) collective-permute-start(bf16[2,192,256]{2,1,0:T(8,128)(2,1)S(1)} %pad_maximum_fusion.refs_1_), channel_id=1, source_target_pairs={{0,4},{2,6},{4,0},{6,2},{8,12},{10,14},{12,8},{14,10},{16,20},{18,... | collective-permute-start | bytes 589832 | tf_op jit(solution)/shard_map/ppermute | solution.py:23
  14.5 20.9 %collective-permute-start.9 = (bf16[2,192,256]{2,1,0:T(8,128)(2,1)S(1)}, bf16[2,192,256]{2,1,0:T(8,128)(2,1)S(1)}, u32[]{:S(2)}, u32[]{:S(2)}) collective-permute-start(bf16[2,192,256]{2,1,0:T(8,128)(2,1)S(1)} %pad_maximum_fusion.refs_1_), channel_id=1, source_target_pairs={{0,6},{2,4},{4,2},{6,0},{8,14},{10,12},{12,10},{14,8},{16,22},{18,... | collective-permute-start | bytes 589832 | tf_op jit(solution)/shard_map/ppermute | solution.py:23
  17.6 11.7 %collective-permute-start.2 = (bf16[2,32,256]{2,1,0:T(8,128)(2,1)S(1)}, bf16[2,32,256]{2,1,0:T(8,128)(2,1)S(1)}, u32[]{:S(2)}, u32[]{:S(2)}) collective-permute-start(bf16[2,32,256]{2,1,0:T(8,128)(2,1)S(1)} %get-tuple-element.27.q_ref), channel_id=1, source_target_pairs={{0,8},{2,10},{4,12},{6,14},{8,0},{10,2},{12,4},{14,6},{16,24},{18,... | collective-permute-start | bytes 98312 | tf_op jit(solution)/shard_map/ppermute | solution.py:23
  30.5 4.7 %collective-permute-start.6 = (bf16[128,384]{1,0:T(8,128)(2,1)S(1)}, bf16[128,384]{1,0:T(8,128)(2,1)S(1)}, u32[]{:S(2)}, u32[]{:S(2)}) collective-permute-start(bf16[128,384]{1,0:T(8,128)(2,1)S(1)} %shard_map.76.part_ref), channel_id=1, source_target_pairs={{0,8},{2,10},{4,12},{6,14},{8,0},{10,2},{12,4},{14,6},{16,24},{18,... | collective-permute-start | bytes 294920 | tf_op jit(solution)/shard_map/ppermute | solution.py:23
  35.8 1.5 %collective-permute-start.10 = (bf16[128,768]{1,0:T(8,128)(2,1)S(1)}, bf16[128,768]{1,0:T(8,128)(2,1)S(1)}, u32[]{:S(2)}, u32[]{:S(2)}) collective-permute-start(bf16[128,768]{1,0:T(8,128)(2,1)S(1)} %shard_map.79), channel_id=1, source_target_pairs={{0,1},{1,0},{2,3},{3,2},{4,5},{5,4},{6,7},{7,6},{8,9},{9,8},{10,11... | collective-permute-start | bytes 589832 | tf_op jit(solution)/shard_map/ppermute | solution.py:23
  37.5 4.9 %collective-permute-start.11 = (bf16[2,32,768]{2,1,0:T(8,128)(2,1)S(1)}, bf16[2,32,768]{2,1,0:T(8,128)(2,1)S(1)}, u32[]{:S(2)}, u32[]{:S(2)}) collective-permute-start(bf16[2,32,768]{2,1,0:T(8,128)(2,1)S(1)} %get-tuple-element.33), channel_id=1, source_target_pairs={{0,8},{2,10},{4,12},{6,14},{8,0},{10,2},{12,4},{14,6},{16,24},{18,... | collective-permute-start | bytes 294920 | tf_op jit(solution)/shard_map/ppermute | solution.py:23

commit v9 on v8

--- a/solution.py
+++ b/solution.py
@@ -23,13 +23,15 @@
     return lax.ppermute(values, axis, [(i, i ^ bit) for i in range(count)])
 
 
-def load_kernel(ids, slab, w_ref, x_ref, mod_ref, w_out, x_out, mod_out, ids_out, cos_ref, sin_ref, sems):
+def load_kernel(ids, slab, w_ref, x_ref, mod_ref, stale_ref, w_out, x_out, mod_out, stale_out, *refs):
+    ids_out, cos_ref, sin_ref, sems = refs
     copies = [
         pltpu.make_async_copy(w_ref.at[slot + 1], w_out.at[slot], sems.at[slot])
         for slot in range(2)
     ]
     copies.append(pltpu.make_async_copy(x_ref, x_out, sems.at[2]))
     copies.append(pltpu.make_async_copy(mod_ref, mod_out, sems.at[3]))
+    copies.append(pltpu.make_async_copy(stale_ref, stale_out, sems.at[4]))
     for copy in copies:
         copy.start()
     row = lax.broadcasted_iota(jnp.int32, ids_out.shape, 0)
@@ -92,13 +94,14 @@
 def fresh_kernel(n_head, head, ids_ref, *refs):
     x_refs, mod_refs = refs[:n_head], refs[n_head : 2 * n_head]
     w_ref, cos_ref, sin_ref = refs[2 * n_head : 2 * n_head + 3]
-    a_ref, kv0_ref = refs[-2:]
+    stale_ref, a_ref, kv_ref = refs[2 * n_head + 3 :]
+    kv_ref[:2] = stale_ref[...]
     parts = normalized(0, x_refs, mod_refs, ids_ref)
     for number, part in enumerate(parts):
         a_ref[number] = part
     keys = rotated(projected(parts, w_ref, 0, head), cos_ref[...], sin_ref[...])
-    kv0_ref[0] = keys.astype(BF16)
-    kv0_ref[1] = projected(parts, w_ref, 1, head).astype(BF16)
+    kv_ref[2] = keys.astype(BF16)
+    kv_ref[3] = projected(parts, w_ref, 1, head).astype(BF16)
 
 
 def rest_kernel(n_head, head, ids_ref, *refs):
@@ -125,25 +128,24 @@
     return [high, middle, values - high - middle]
 
 
-def attend_kernel(patch, q_ref, mate_ref, kv0_ref, kv1_ref, kv_ref, out_ref):
-    rows, cols = kv0_ref.shape[1:]
-    blocks = kv_ref.shape[0] // (2 * STEPS)
+def attend_kernel(q_ref, mate_ref, kv1_ref, *refs):
+    kv_refs, out_ref = refs[:PLANE], refs[PLANE]
+    blocks, _, rows, cols = kv_refs[0].shape
     old_rows = PLANE * blocks * rows
     shape = (2 * rows, old_rows + rows)
     mine = lax.broadcasted_iota(jnp.int32, shape, 0) < rows
-    stray = jnp.where(mine, patch[0] % PLANE, PLANE * blocks)
+    stray = jnp.where(mine, 0, PLANE * blocks)
     drop = lax.broadcasted_iota(jnp.int32, shape, 1) // rows == stray
     lane = lax.broadcasted_iota(jnp.int32, (2 * rows, DH), 1)
     for step in range(STEPS):
-        first = 2 * blocks * step
-        fresh = (kv0_ref, kv1_ref)[step]
+        fresh = (kv_refs[0].at[0, 2:], kv1_ref)[step]
         stats = jnp.zeros((2 * rows, DH), F32)
         mixed = []
         for head in range(cols // DH):
             lanes = slice(head * DH, (head + 1) * DH)
 
             def rows_of(kind):
-                old = [kv_ref[first + 2 * k + kind, :, lanes] for k in range(blocks)]
+                old = [ref[:, 2 * step + kind, :, lanes].reshape(blocks * rows, DH) for ref in kv_refs]
                 return jnp.concatenate([*old, fresh[kind, :, lanes]], axis=0)
 
             queries = jnp.concatenate([q_ref[step, :, lanes], mate_ref[step, :, lanes]], axis=0)
@@ -236,14 +238,14 @@
 
     x_parts = [swap(inputs, "head", n_head, k) for k in range(1, n_head)]
     mod_parts = [swap(mod_table, "head", n_head, k) for k in range(1, n_head)]
-    first = (jnp.transpose(w_qkv, (1, 0, 2)), inputs, jnp.transpose(mod_table, (1, 0, 2)))
-    w, x_own, mod_own, ids, cos, sin = call(
+    first = (jnp.transpose(w_qkv, (1, 0, 2)), inputs, jnp.transpose(mod_table, (1, 0, 2)), stale_kv)
+    w, x_own, mod_own, stale, ids, cos, sin = call(
         load_kernel,
         (pltpu.VMEM((2, *first[0].shape[1:]), BF16),)
         + tuple(pltpu.VMEM(v.shape, v.dtype) for v in first[1:])
         + (shaped((8, DH), jnp.int32), shaped((rows, DH), F32), shaped((rows, DH), F32)),
         [SMEM] * 2 + [ANY] * len(first),
-        [pltpu.SemaphoreType.DMA((4,))],
+        [pltpu.SemaphoreType.DMA((5,))],
         size=2 * w_qkv.size,
     )(in_hbm(step_ids), slab_order, *map(in_hbm, first))
     x_parts = [x_own] + x_parts
@@ -258,19 +260,18 @@
     def plane_of(values):
         return [values] + [across(values, k) for k in range(1, PLANE)]
 
-    stale_pair = line_of(stale_kv)
     w_pair = line_of(w_out.T)
 
     kv_shape = shaped((2, rows, cols), BF16)
     common = (head[None], ids, *x_parts, *mod_parts, w, cos, sin)
     specs = [SMEM] + [VMEM] * (2 * n_head + 4)
-    a, kv0 = call(
+    a, kv = call(
         functools.partial(fresh_kernel, n_head),
-        (shaped((n_head, rows, feats), BF16), kv_shape),
-        specs,
+        (shaped((n_head, rows, feats), BF16), shaped((4, rows, cols), BF16)),
+        specs + [VMEM],
         flops=4 * rows * w_qkv.size // 3,
         size=2 * w_qkv.size,
-    )(*common)
+    )(*common, stale)
     q, kv1 = call(
         functools.partial(rest_kernel, n_head),
         (kv_shape, kv_shape),
@@ -280,21 +281,18 @@
         2 * w_qkv.size,
     )(*common, a, in_hbm(first[0]))
 
-    kv_pair = line_of(kv0)
+    kv_pair = line_of(kv)
     q_mate = across(q, PLANE)
-    w_pair, kv0 = lax.optimization_barrier((w_pair, kv0))
+    w_pair, kv_pair, kv1 = lax.optimization_barrier((w_pair, kv_pair, kv1))
+    kv_plane = plane_of(jnp.stack(kv_pair))
     w_plane = plane_of(jnp.stack(w_pair))
-    planes = [list(range(k, k + PLANE)) for k in range(0, n_patch, PLANE)]
-    kv = lax.all_gather(
-        jnp.concatenate(stale_pair + kv_pair), "patch", axis=1, axis_index_groups=planes, tiled=True
-    )
     tall = 2 * STEPS * rows
     part = call(
         attend_kernel,
         shaped((tall, cols + DH), BF16),
-        [SMEM] + [VMEM] * 5,
+        [VMEM] * (3 + PLANE),
         flops=4 * STEPS * rows * n_patch * rows * cols,
-    )(patch[None], q, q_mate, kv0, kv1, kv)
+    )(q, q_mate, kv1, *kv_plane)
     o = call(merge_kernel, shaped((tall, cols), BF16), [VMEM] * 2)(part, across(part, PLANE))
     wide = PLANE * piece
 

time: 43.3 us -> 43.2 us (level)
  waiting for transfers between devices: 7.33 us -> 19.8 us
  blocking collectives: 10.1 us -> 0 us
  starting transfers between devices: 15.8 us -> 13.3 us
    ppermute x12 -> x14, waiting for transfers between devices: 7.33 us -> 19.8 us  [swap(): return lax.ppermute(values, axis, [(i, i ^ bit) for i in range(count)])]
    all_gather x1 -> x0, blocking collectives: 10.1 us -> none  [body(): lax.all_gather(jnp.concatenate(stale_pair + kv_pair), 'patch', axis=1, ax...]
    ppermute x12 -> x14, starting transfers between devices: 15.8 us -> 13.3 us  [swap(): return lax.ppermute(values, axis, [(i, i ^ bit) for i in range(count)])]
  transfers between devices with their start and end apart: 12 -> 14, of which waited for: 3 -> 5; matrix products, arithmetic and copies ran while one was open for 0% -> 0% of each run, Pallas kernels for 18% -> 18%
where the time goes in v9:
time: 43.2 us; the launch traced here: 43 us
  waiting for transfers between devices  19.8 us (46%)
  starting transfers between devices  13.3 us (31%)
  Pallas kernels  8.35 us (19%)
  between operations  0.85 us (2%)
  other arithmetic  0.74 us (2%)
    ppermute x14, waiting for transfers between devices, swap(): return lax.ppermute(values, axis, [(i, i ^ bit) for i in range(count)])  19.8 us
    ppermute x14, starting transfers between devices, swap(): return lax.ppermute(values, axis, [(i, i ^ bit) for i in range(count)])  13.3 us
    pallas_call x1, Pallas kernels, body(): call(functools.partial(rest_kernel, n_head), (kv_shape, kv_shape), specs...  2.64 us
    pallas_call x1, Pallas kernels, body(): call(load_kernel, (pltpu.VMEM((2, *first[0].shape[1:]), BF16),) + tuple((...  2.6 us
    pallas_call x1, Pallas kernels, body(): call(attend_kernel, shaped((tall, cols + DH), BF16), [VMEM] * (3 + PLANE)...  1.11 us
  transfers between devices with their start and end apart: 14, of which 5 were waited for; matrix products, arithmetic and copies ran while one was open for 0% of the time, Pallas kernels for 18%

profile of v9, /device:TPU:0, one launch (start us, length us, event | category | flops | bytes accessed | tf_op | source)
XLA Modules:
  0.0 43.0 jit_solution(1069908926567667107)
XLA Ops:
  0.0 0.5 %collective-permute-start = (bf16[2,32,1536]{2,1,0:T(8,128)(2,1)}, bf16[2,32,1536]{2,1,0:T(8,128)(2,1)S(1)}, u32[]{:S(2)}, u32[]{:S(2)}) collective-permute-start(bf16[2,32,1536]{2,1,0:T(8,128)(2,1)} %x_ref.1), channel_id=1, source_target_pairs={{0,1},{1,0},{2,3},{3,2},{4,5},{5,4},{6,7},{7,6},{8,9},{9,8},{10,11... | collective-permute-start | bytes 589832 | tf_op jit(solution)/shard_map/ppermute | solution.py:23
  0.5 0.1 collective-permute-start.1
  0.5 4.0 %collective-permute-start.3 = (bf16[192,256]{1,0:T(8,128)(2,1)}, bf16[192,256]{1,0:T(8,128)(2,1)S(1)}, u32[]{:S(2)}, u32[]{:S(2)}) collective-permute-start(bf16[192,256]{1,0:T(8,128)(2,1)} %bitcast.15), channel_id=1, source_target_pairs={{0,16},{2,18},{4,20},{6,22},{8,24},{10,26},{12,28},{14,30},{16,0},... | collective-permute-start | bytes 294920 | tf_op jit(solution)/shard_map/ppermute | solution.py:23
  5.2 2.6 %shard_map.73 = (bf16[2,3072,256]{2,1,0:T(8,128)(2,1)S(1)}, bf16[2,32,1536]{2,1,0:T(8,128)(2,1)S(1)}, f32[3,4,1536]{2,1,0:T(4,128)S(1)}, bf16[2,32,256]{2,1,0:T(...) custom-call(s32[2]{0:T(128)} %ids.1, s32[1]{0:T(128)S(6)} %copy.8.slab, ...), custom_call_target="tpu_custom_call" | custom-call | bytes 4718592 | tf_op jit(solution)/shard_map/pallas_call | solution.py:242
  7.8 0.0 collective-permute-done.1
  7.8 0.0 collective-permute-done.refs_1_
  7.8 0.8 %shard_map.74 = (bf16[2,32,1536]{2,1,0:T(8,128)(2,1)S(1)}, bf16[4,32,256]{2,1,0:T(8,128)(2,1)S(1)}) custom-call(s32[1]{0:T(128)} %bitcast.3.head, s32[8,128]{1,0:T(8,128)S(1)} %get-tuple-element.23.ids_ref, bf16[2,32,1536]{2,1,0:T(8,128)(2,1)S(1)} %get-tuple-element.25.refs_0_, bf16[2,32,1536]{2,1,0:T(8,128)(2,1)S(1)} %collective-permute-done.refs_1_, ...), custom_call_target="tpu_custom_call" | custom-call | flops 100663296 | bytes 4718592 | tf_op jit(solution)/shard_map/pallas_call | solution.py:268
  8.7 0.0 copy-start
  8.7 0.1 collective-permute-start.4
  8.8 2.6 %shard_map.75 = (bf16[2,32,256]{2,1,0:T(8,128)(2,1)S(1)}, bf16[2,32,256]{2,1,0:T(8,128)(2,1)S(1)}) custom-call(s32[1]{0:T(128)} %bitcast.3.head, s32[8,128]{1,0:T(8,128)S(1)} %get-tuple-element.23.ids_ref, bf16[2,32,1536]{2,1,0:T(8,128)(2,1)S(1)} %get-tuple-element.25.refs_0_, bf16[2,32,1536]{2,1,0:T(8,128)(2,1)S(1)} %collective-permute-done.refs_1_, ...), custom_call_target="tpu_custom_call" | custom-call | flops 201326592 | bytes 4718592 | tf_op jit(solution)/shard_map/pallas_call | solution.py:275
  11.4 0.0 collective-permute-done.3
  11.4 3.7 %collective-permute-done.4 = bf16[4,32,256]{2,1,0:T(8,128)(2,1)S(1)} collective-permute-done((bf16[4,32,256]{2,1,0:T(8,128)(2,1)S(1)}, bf16[4,32,256]{2,1,0:T(8,128)(2,1)S(1)}, u32[]{:S(2)}, u32[]{:S(2)}) %collective-permute-start.4) | collective-permute-done | bytes 65568 | tf_op jit(solution)/shard_map/ppermute | solution.py:23
  15.1 1.6 %collective-permute-start.5 = (bf16[2,4,32,256]{3,2,1,0:T(8,128)(2,1)S(1)}, bf16[2,4,32,256]{3,2,1,0:T(8,128)(2,1)S(1)}, u32[]{:S(2)}, u32[]{:S(2)}) collective-permute-start(bf16[2,4,32,256]{3,2,1,0:T(8,128)(2,1)S(1)} %pad_maximum_fusion.2.refs_0_), channel_id=1, source_target_pairs={{0,2},{2,0},{4,6},{6,4},{8,10},{10,8},{12,14},{14,12},{16,18},{18,... | collective-permute-start | bytes 393224 | tf_op jit(solution)/shard_map/ppermute | solution.py:23
  16.7 0.5 %collective-permute-start.2 = (bf16[2,32,256]{2,1,0:T(8,128)(2,1)S(1)}, bf16[2,32,256]{2,1,0:T(8,128)(2,1)S(1)}, u32[]{:S(2)}, u32[]{:S(2)}) collective-permute-start(bf16[2,32,256]{2,1,0:T(8,128)(2,1)S(1)} %get-tuple-element.31.q_ref), channel_id=1, source_target_pairs={{0,8},{2,10},{4,12},{6,14},{8,0},{10,2},{12,4},{14,6},{16,24},{18,... | collective-permute-start | bytes 98312 | tf_op jit(solution)/shard_map/ppermute | solution.py:23
  17.2 1.5 %collective-permute-start.6 = (bf16[2,4,32,256]{3,2,1,0:T(8,128)(2,1)S(1)}, bf16[2,4,32,256]{3,2,1,0:T(8,128)(2,1)S(1)}, u32[]{:S(2)}, u32[]{:S(2)}) collective-permute-start(bf16[2,4,32,256]{3,2,1,0:T(8,128)(2,1)S(1)} %pad_maximum_fusion.2.refs_0_), channel_id=1, source_target_pairs={{0,4},{2,6},{4,0},{6,2},{8,12},{10,14},{12,8},{14,10},{16,20},{18,... | collective-permute-start | bytes 393224 | tf_op jit(solution)/shard_map/ppermute | solution.py:23
  18.7 0.5 %collective-permute-start.7 = (bf16[2,4,32,256]{3,2,1,0:T(8,128)(2,1)S(1)}, bf16[2,4,32,256]{3,2,1,0:T(8,128)(2,1)S(1)}, u32[]{:S(2)}, u32[]{:S(2)}) collective-permute-start(bf16[2,4,32,256]{3,2,1,0:T(8,128)(2,1)S(1)} %pad_maximum_fusion.2.refs_0_), channel_id=1, source_target_pairs={{0,6},{2,4},{4,2},{6,0},{8,14},{10,12},{12,10},{14,8},{16,22},{18,... | collective-permute-start | bytes 393224 | tf_op jit(solution)/shard_map/ppermute | solution.py:23
  19.2 0.0 copy-done
  19.2 1.6 %collective-permute-start.10 = (bf16[2,192,256]{2,1,0:T(8,128)(2,1)S(1)}, bf16[2,192,256]{2,1,0:T(8,128)(2,1)S(1)}, u32[]{:S(2)}, u32[]{:S(2)}) collective-permute-start(bf16[2,192,256]{2,1,0:T(8,128)(2,1)S(1)} %pad_maximum_fusion.refs_1_), channel_id=1, source_target_pairs={{0,4},{2,6},{4,0},{6,2},{8,12},{10,14},{12,8},{14,10},{16,20},{18,... | collective-permute-start | bytes 589832 | tf_op jit(solution)/shard_map/ppermute | solution.py:23
  20.8 0.0 collective-permute-done.2.mate_ref
  20.8 1.4 %collective-permute-start.11 = (bf16[2,192,256]{2,1,0:T(8,128)(2,1)S(1)}, bf16[2,192,256]{2,1,0:T(8,128)(2,1)S(1)}, u32[]{:S(2)}, u32[]{:S(2)}) collective-permute-start(bf16[2,192,256]{2,1,0:T(8,128)(2,1)S(1)} %pad_maximum_fusion.refs_1_), channel_id=1, source_target_pairs={{0,6},{2,4},{4,2},{6,0},{8,14},{10,12},{12,10},{14,8},{16,22},{18,... | collective-permute-start | bytes 589832 | tf_op jit(solution)/shard_map/ppermute | solution.py:23
  22.2 0.0 collective-permute-done.5.refs_1_
  22.2 1.3 %collective-permute-start.9 = (bf16[2,192,256]{2,1,0:T(8,128)(2,1)S(1)}, bf16[2,192,256]{2,1,0:T(8,128)(2,1)S(1)}, u32[]{:S(2)}, u32[]{:S(2)}) collective-permute-start(bf16[2,192,256]{2,1,0:T(8,128)(2,1)S(1)} %pad_maximum_fusion.refs_1_), channel_id=1, source_target_pairs={{0,2},{2,0},{4,6},{6,4},{8,10},{10,8},{12,14},{14,12},{16,18},{18,... | collective-permute-start | bytes 589832 | tf_op jit(solution)/shard_map/ppermute | solution.py:23
  23.6 5.7 %collective-permute-done.6.refs_2_ = bf16[2,4,32,256]{3,2,1,0:T(8,128)(2,1)S(1)} collective-permute-done((bf16[2,4,32,256]{3,2,1,0:T(8,128)(2,1)S(1)}, bf16[2,4,32,256]{3,2,1,0:T(8,128)(2,1)S(1)}, u32[]{:S(2)}, u32[]{:S(2)}) %collective-permute-start.6) | collective-permute-done | bytes 131104 | tf_op jit(solution)/shard_map/ppermute | solution.py:23
  29.3 0.0 collective-permute-done.7.refs_3_
  29.3 1.1 %shard_map.76.part_ref = bf16[128,384]{1,0:T(8,128)(2,1)S(1)} custom-call(bf16[2,32,256]{2,1,0:T(8,128)(2,1)S(1)} %get-tuple-element.31.q_ref, bf16[2,32,256]{2,1,0:T(8,128)(2,1)S(1)} %collective-permute-done.2.mate_ref, bf16[2,32,256]{2,1,0:T(8,128)(2,1)S(1)} %get-tuple-element.34.kv1_ref, bf16[2,4,32,256]{3,2,1,0:T(8,128)(2,1)S(1)} %pad_maximum_fusion.2.refs_0_, ...), custom_call_target="tpu_custom_call" | custom-call | flops 33554432 | tf_op jit(solution)/shard_map/pallas_call | solution.py:290
  30.4 0.1 collective-permute-start.8
  30.5 4.6 %collective-permute-done.8.other_ref = bf16[128,384]{1,0:T(8,128)(2,1)S(1)} collective-permute-done((bf16[128,384]{1,0:T(8,128)(2,1)S(1)}, bf16[128,384]{1,0:T(8,128)(2,1)S(1)}, u32[]{:S(2)}, u32[]{:S(2)}) %collective-permute-start.8) | collective-permute-done | bytes 98336 | tf_op jit(solution)/shard_map/ppermute | solution.py:23
  35.1 0.2 shard_map.77.refs_0_
  35.3 0.0 collective-permute-done.10.refs_3_
  35.3 0.0 collective-permute-done.11.refs_4_
  35.3 0.0 collective-permute-done.9.refs_2_
  35.3 0.4 shard_map.79
  35.7 0.1 collective-permute-start.12
  35.8 0.4 shard_map.78.refs_0_
  36.3 1.0 %collective-permute-done.12.refs_1_ = bf16[128,768]{1,0:T(8,128)(2,1)S(1)} collective-permute-done((bf16[128,768]{1,0:T(8,128)(2,1)S(1)}, bf16[128,768]{1,0:T(8,128)(2,1)S(1)}, u32[]{:S(2)}, u32[]{:S(2)}) %collective-permute-start.12) | collective-permute-done | bytes 196640 | tf_op jit(solution)/shard_map/ppermute | solution.py:23
  37.3 0.1 shard_map.80
  37.4 0.1 collective-permute-start.13
  37.5 4.8 %collective-permute-done.13 = bf16[2,32,768]{2,1,0:T(8,128)(2,1)S(1)} collective-permute-done((bf16[2,32,768]{2,1,0:T(8,128)(2,1)S(1)}, bf16[2,32,768]{2,1,0:T(8,128)(2,1)S(1)}, u32[]{:S(2)}, u32[]{:S(2)}) %collective-permute-start.13) | collective-permute-done | bytes 98336 | tf_op jit(solution)/shard_map/ppermute | solution.py:23
  42.3 0.7 %pad_maximum_fusion.1 = bf16[2,32,1536]{2,1,0:T(8,128)(2,1)} fusion(bf16[2,32,768]{2,1,0:T(8,128)(2,1)S(1)} %get-tuple-element.42, bf16[2,32,768]{2,1,0:T(8,128)(2,1)S(1)} %get-tuple-element.41), kind=kLoop, calls=%fused_computation.1 | loop fusion | flops 393216 | bytes 393216 | tf_op jit(solution)/shard_map/concatenate | solution.py:319
  (3 shorter events, 0.1 us)
Async XLA Ops:
  0.0 7.8 %collective-permute-start = (bf16[2,32,1536]{2,1,0:T(8,128)(2,1)}, bf16[2,32,1536]{2,1,0:T(8,128)(2,1)S(1)}, u32[]{:S(2)}, u32[]{:S(2)}) collective-permute-start(bf16[2,32,1536]{2,1,0:T(8,128)(2,1)} %x_ref.1), channel_id=1, source_target_pairs={{0,1},{1,0},{2,3},{3,2},{4,5},{5,4},{6,7},{7,6},{8,9},{9,8},{10,11... | collective-permute-start | bytes 589832 | tf_op jit(solution)/shard_map/ppermute | solution.py:23
  0.5 7.4 %collective-permute-start.1 = (f32[4,3,1536]{2,0,1:T(4,128)}, f32[4,3,1536]{2,0,1:T(4,128)S(1)}, u32[]{:S(2)}, u32[]{:S(2)}) collective-permute-start(f32[4,3,1536]{2,0,1:T(4,128)} %param.11), channel_id=1, source_target_pairs={{0,1},{1,0},{2,3},{3,2},{4,5},{5,4},{6,7},{7,6},{8,9},{9,8},{10,11... | collective-permute-start | bytes 221192 | tf_op jit(solution)/shard_map/ppermute | solution.py:23
  0.5 10.9 %collective-permute-start.3 = (bf16[192,256]{1,0:T(8,128)(2,1)}, bf16[192,256]{1,0:T(8,128)(2,1)S(1)}, u32[]{:S(2)}, u32[]{:S(2)}) collective-permute-start(bf16[192,256]{1,0:T(8,128)(2,1)} %bitcast.15), channel_id=1, source_target_pairs={{0,16},{2,18},{4,20},{6,22},{8,24},{10,26},{12,28},{14,30},{16,0},... | collective-permute-start | bytes 294920 | tf_op jit(solution)/shard_map/ppermute | solution.py:23
  8.7 10.5 %copy-start = (bf16[256,192]{0,1:T(8,128)(2,1)S(1)}, bf16[256,192]{0,1:T(8,128)(2,1)}, u32[]{:S(2)}) copy-start(bf16[256,192]{0,1:T(8,128)(2,1)} %param.10) | copy-start | bytes 294916
  8.7 6.4 %collective-permute-start.4 = (bf16[4,32,256]{2,1,0:T(8,128)(2,1)S(1)}, bf16[4,32,256]{2,1,0:T(8,128)(2,1)S(1)}, u32[]{:S(2)}, u32[]{:S(2)}) collective-permute-start(bf16[4,32,256]{2,1,0:T(8,128)(2,1)S(1)} %get-tuple-element.35), channel_id=1, source_target_pairs={{0,16},{2,18},{4,20},{6,22},{8,24},{10,26},{12,28},{14,30},{16,0},... | collective-permute-start | bytes 196616 | tf_op jit(solution)/shard_map/ppermute | solution.py:23
  15.1 7.1 %collective-permute-start.5 = (bf16[2,4,32,256]{3,2,1,0:T(8,128)(2,1)S(1)}, bf16[2,4,32,256]{3,2,1,0:T(8,128)(2,1)S(1)}, u32[]{:S(2)}, u32[]{:S(2)}) collective-permute-start(bf16[2,4,32,256]{3,2,1,0:T(8,128)(2,1)S(1)} %pad_maximum_fusion.2.refs_0_), channel_id=1, source_target_pairs={{0,2},{2,0},{4,6},{6,4},{8,10},{10,8},{12,14},{14,12},{16,18},{18,... | collective-permute-start | bytes 393224 | tf_op jit(solution)/shard_map/ppermute | solution.py:23
  16.7 4.1 %collective-permute-start.2 = (bf16[2,32,256]{2,1,0:T(8,128)(2,1)S(1)}, bf16[2,32,256]{2,1,0:T(8,128)(2,1)S(1)}, u32[]{:S(2)}, u32[]{:S(2)}) collective-permute-start(bf16[2,32,256]{2,1,0:T(8,128)(2,1)S(1)} %get-tuple-element.31.q_ref), channel_id=1, source_target_pairs={{0,8},{2,10},{4,12},{6,14},{8,0},{10,2},{12,4},{14,6},{16,24},{18,... | collective-permute-start | bytes 98312 | tf_op jit(solution)/shard_map/ppermute | solution.py:23
  17.2 12.1 %collective-permute-start.6 = (bf16[2,4,32,256]{3,2,1,0:T(8,128)(2,1)S(1)}, bf16[2,4,32,256]{3,2,1,0:T(8,128)(2,1)S(1)}, u32[]{:S(2)}, u32[]{:S(2)}) collective-permute-start(bf16[2,4,32,256]{3,2,1,0:T(8,128)(2,1)S(1)} %pad_maximum_fusion.2.refs_0_), channel_id=1, source_target_pairs={{0,4},{2,6},{4,0},{6,2},{8,12},{10,14},{12,8},{14,10},{16,20},{18,... | collective-permute-start | bytes 393224 | tf_op jit(solution)/shard_map/ppermute | solution.py:23
  18.7 10.6 %collective-permute-start.7 = (bf16[2,4,32,256]{3,2,1,0:T(8,128)(2,1)S(1)}, bf16[2,4,32,256]{3,2,1,0:T(8,128)(2,1)S(1)}, u32[]{:S(2)}, u32[]{:S(2)}) collective-permute-start(bf16[2,4,32,256]{3,2,1,0:T(8,128)(2,1)S(1)} %pad_maximum_fusion.2.refs_0_), channel_id=1, source_target_pairs={{0,6},{2,4},{4,2},{6,0},{8,14},{10,12},{12,10},{14,8},{16,22},{18,... | collective-permute-start | bytes 393224 | tf_op jit(solution)/shard_map/ppermute | solution.py:23
  19.2 16.1 %collective-permute-start.10 = (bf16[2,192,256]{2,1,0:T(8,128)(2,1)S(1)}, bf16[2,192,256]{2,1,0:T(8,128)(2,1)S(1)}, u32[]{:S(2)}, u32[]{:S(2)}) collective-permute-start(bf16[2,192,256]{2,1,0:T(8,128)(2,1)S(1)} %pad_maximum_fusion.refs_1_), channel_id=1, source_target_pairs={{0,4},{2,6},{4,0},{6,2},{8,12},{10,14},{12,8},{14,10},{16,20},{18,... | collective-permute-start | bytes 589832 | tf_op jit(solution)/shard_map/ppermute | solution.py:23
  20.8 14.5 %collective-permute-start.11 = (bf16[2,192,256]{2,1,0:T(8,128)(2,1)S(1)}, bf16[2,192,256]{2,1,0:T(8,128)(2,1)S(1)}, u32[]{:S(2)}, u32[]{:S(2)}) collective-permute-start(bf16[2,192,256]{2,1,0:T(8,128)(2,1)S(1)} %pad_maximum_fusion.refs_1_), channel_id=1, source_target_pairs={{0,6},{2,4},{4,2},{6,0},{8,14},{10,12},{12,10},{14,8},{16,22},{18,... | collective-permute-start | bytes 589832 | tf_op jit(solution)/shard_map/ppermute | solution.py:23
  22.2 13.1 %collective-permute-start.9 = (bf16[2,192,256]{2,1,0:T(8,128)(2,1)S(1)}, bf16[2,192,256]{2,1,0:T(8,128)(2,1)S(1)}, u32[]{:S(2)}, u32[]{:S(2)}) collective-permute-start(bf16[2,192,256]{2,1,0:T(8,128)(2,1)S(1)} %pad_maximum_fusion.refs_1_), channel_id=1, source_target_pairs={{0,2},{2,0},{4,6},{6,4},{8,10},{10,8},{12,14},{14,12},{16,18},{18,... | collective-permute-start | bytes 589832 | tf_op jit(solution)/shard_map/ppermute | solution.py:23
  30.4 4.7 %collective-permute-start.8 = (bf16[128,384]{1,0:T(8,128)(2,1)S(1)}, bf16[128,384]{1,0:T(8,128)(2,1)S(1)}, u32[]{:S(2)}, u32[]{:S(2)}) collective-permute-start(bf16[128,384]{1,0:T(8,128)(2,1)S(1)} %shard_map.76.part_ref), channel_id=1, source_target_pairs={{0,8},{2,10},{4,12},{6,14},{8,0},{10,2},{12,4},{14,6},{16,24},{18,... | collective-permute-start | bytes 294920 | tf_op jit(solution)/shard_map/ppermute | solution.py:23
  35.7 1.5 %collective-permute-start.12 = (bf16[128,768]{1,0:T(8,128)(2,1)S(1)}, bf16[128,768]{1,0:T(8,128)(2,1)S(1)}, u32[]{:S(2)}, u32[]{:S(2)}) collective-permute-start(bf16[128,768]{1,0:T(8,128)(2,1)S(1)} %shard_map.79), channel_id=1, source_target_pairs={{0,1},{1,0},{2,3},{3,2},{4,5},{5,4},{6,7},{7,6},{8,9},{9,8},{10,11... | collective-permute-start | bytes 589832 | tf_op jit(solution)/shard_map/ppermute | solution.py:23
  37.4 4.9 %collective-permute-start.13 = (bf16[2,32,768]{2,1,0:T(8,128)(2,1)S(1)}, bf16[2,32,768]{2,1,0:T(8,128)(2,1)S(1)}, u32[]{:S(2)}, u32[]{:S(2)}) collective-permute-start(bf16[2,32,768]{2,1,0:T(8,128)(2,1)S(1)} %get-tuple-element.39), channel_id=1, source_target_pairs={{0,8},{2,10},{4,12},{6,14},{8,0},{10,2},{12,4},{14,6},{16,24},{18,... | collective-permute-start | bytes 294920 | tf_op jit(solution)/shard_map/ppermute | solution.py:23

commit v10 on v9

--- a/solution.py
+++ b/solution.py
@@ -260,7 +260,8 @@
     def plane_of(values):
         return [values] + [across(values, k) for k in range(1, PLANE)]
 
-    w_pair = line_of(w_out.T)
+    w_own, *w_rest = line_of(w_out.T)
+    w_x = across(w_own, 1)
 
     kv_shape = shaped((2, rows, cols), BF16)
     common = (head[None], ids, *x_parts, *mod_parts, w, cos, sin)
@@ -283,9 +284,14 @@
 
     kv_pair = line_of(kv)
     q_mate = across(q, PLANE)
-    w_pair, kv_pair, kv1 = lax.optimization_barrier((w_pair, kv_pair, kv1))
+    w_own, w_x, w_rest, kv = lax.optimization_barrier((w_own, w_x, w_rest, kv))
+    w_y = across(jnp.stack([w_own, w_x]), 2)
+    w_rest = jnp.stack(w_rest)
+    rest_y = across(w_rest, 2)
+    kv_pair, q_mate = lax.optimization_barrier((kv_pair, q_mate))
     kv_plane = plane_of(jnp.stack(kv_pair))
-    w_plane = plane_of(jnp.stack(w_pair))
+    w_y, rest_y, kv_plane[1] = lax.optimization_barrier((w_y, rest_y, kv_plane[1]))
+    rest_x = across(jnp.stack([w_rest, rest_y]), 1)
     tall = 2 * STEPS * rows
     part = call(
         attend_kernel,
@@ -294,6 +300,9 @@
         flops=4 * STEPS * rows * n_patch * rows * cols,
     )(q, q_mate, kv1, *kv_plane)
     o = call(merge_kernel, shaped((tall, cols), BF16), [VMEM] * 2)(part, across(part, PLANE))
+    o, w_y, rest_x = lax.optimization_barrier((o, w_y, rest_x))
+    near = [(w_own, w_rest), (w_x, rest_x[0]), (w_y[0], rest_y), (w_y[1], rest_x[1])]
+    w_plane = [jnp.concatenate([first[None], others]) for first, others in near]
     wide = PLANE * piece
 
     def project(bit, dtype):

time: 43.2 us -> 42.4 us (0.981)
  waiting for transfers between devices: 19.8 us -> 16.3 us
  starting transfers between devices: 13.3 us -> 15.9 us
    ppermute x14 -> x15, waiting for transfers between devices: 19.8 us -> 16.3 us  [swap(): return lax.ppermute(values, axis, [(i, i ^ bit) for i in range(count)])]
    ppermute x14 -> x15, starting transfers between devices: 13.3 us -> 15.9 us  [swap(): return lax.ppermute(values, axis, [(i, i ^ bit) for i in range(count)])]
  transfers between devices with their start and end apart: 14 -> 15, of which waited for: 5 -> 6; matrix products, arithmetic and copies ran while one was open for 0% -> 0% of each run, Pallas kernels for 18% -> 19%
where the time goes in v10:
time: 42.4 us; the launch traced here: 42.2 us
  waiting for transfers between devices  16.3 us (38%)
  starting transfers between devices  15.9 us (38%)
  Pallas kernels  8.35 us (20%)
  other arithmetic  0.84 us (2%)
  between operations  0.82 us (2%)
    ppermute x15, waiting for transfers between devices, swap(): return lax.ppermute(values, axis, [(i, i ^ bit) for i in range(count)])  16.3 us
    ppermute x15, starting transfers between devices, swap(): return lax.ppermute(values, axis, [(i, i ^ bit) for i in range(count)])  15.9 us
    pallas_call x1, Pallas kernels, body(): call(functools.partial(rest_kernel, n_head), (kv_shape, kv_shape), specs...  2.64 us
    pallas_call x1, Pallas kernels, body(): call(load_kernel, (pltpu.VMEM((2, *first[0].shape[1:]), BF16),) + tuple((...  2.6 us
    pallas_call x1, Pallas kernels, body(): call(attend_kernel, shaped((tall, cols + DH), BF16), [VMEM] * (3 + PLANE)...  1.11 us
  transfers between devices with their start and end apart: 15, of which 6 were waited for; matrix products, arithmetic and copies ran while one was open for 0% of the time, Pallas kernels for 19%

profile of v10, /device:TPU:0, one launch (start us, length us, event | category | flops | bytes accessed | tf_op | source)
XLA Modules:
  0.0 42.2 jit_solution(17573455678306370492)
XLA Ops:
  0.0 0.5 %collective-permute-start = (bf16[2,32,1536]{2,1,0:T(8,128)(2,1)}, bf16[2,32,1536]{2,1,0:T(8,128)(2,1)S(1)}, u32[]{:S(2)}, u32[]{:S(2)}) collective-permute-start(bf16[2,32,1536]{2,1,0:T(8,128)(2,1)} %x_ref.1), channel_id=1, source_target_pairs={{0,1},{1,0},{2,3},{3,2},{4,5},{5,4},{6,7},{7,6},{8,9},{9,8},{10,11... | collective-permute-start | bytes 589832 | tf_op jit(solution)/shard_map/ppermute | solution.py:23
  0.5 0.1 collective-permute-start.1
  0.5 2.9 %collective-permute-start.4 = (bf16[192,256]{1,0:T(8,128)(2,1)}, bf16[192,256]{1,0:T(8,128)(2,1)S(1)}, u32[]{:S(2)}, u32[]{:S(2)}) collective-permute-start(bf16[192,256]{1,0:T(8,128)(2,1)} %bitcast.28), channel_id=1, source_target_pairs={{0,2},{2,0},{4,6},{6,4},{8,10},{10,8},{12,14},{14,12},{16,18},{18,... | collective-permute-start | bytes 294920 | tf_op jit(solution)/shard_map/ppermute | solution.py:23
  3.5 2.6 %collective-permute-start.5 = (bf16[192,256]{1,0:T(8,128)(2,1)}, bf16[192,256]{1,0:T(8,128)(2,1)S(1)}, u32[]{:S(2)}, u32[]{:S(2)}) collective-permute-start(bf16[192,256]{1,0:T(8,128)(2,1)} %bitcast.29), channel_id=1, source_target_pairs={{0,16},{2,18},{4,20},{6,22},{8,24},{10,26},{12,28},{14,30},{16,0},... | collective-permute-start | bytes 294920 | tf_op jit(solution)/shard_map/ppermute | solution.py:23
  6.7 2.6 %shard_map.73 = (bf16[2,3072,256]{2,1,0:T(8,128)(2,1)S(1)}, bf16[2,32,1536]{2,1,0:T(8,128)(2,1)S(1)}, f32[3,4,1536]{2,1,0:T(4,128)S(1)}, bf16[2,32,256]{2,1,0:T(...) custom-call(s32[2]{0:T(128)} %ids.1, s32[1]{0:T(128)S(6)} %copy.8.slab, ...), custom_call_target="tpu_custom_call" | custom-call | bytes 4718592 | tf_op jit(solution)/shard_map/pallas_call | solution.py:242
  9.3 0.0 collective-permute-done.1
  9.3 0.0 collective-permute-done.refs_1_
  9.3 0.8 %shard_map.74 = (bf16[2,32,1536]{2,1,0:T(8,128)(2,1)S(1)}, bf16[4,32,256]{2,1,0:T(8,128)(2,1)S(1)}) custom-call(s32[1]{0:T(128)} %bitcast.3.head, s32[8,128]{1,0:T(8,128)S(1)} %get-tuple-element.30.ids_ref, bf16[2,32,1536]{2,1,0:T(8,128)(2,1)S(1)} %get-tuple-element.32.refs_0_, bf16[2,32,1536]{2,1,0:T(8,128)(2,1)S(1)} %collective-permute-done.refs_1_, ...), custom_call_target="tpu_custom_call" | custom-call | flops 100663296 | bytes 4718592 | tf_op jit(solution)/shard_map/pallas_call | solution.py:269
  10.2 0.0 copy-start
  10.2 0.4 collective-permute-start.2
  10.6 2.6 %shard_map.75 = (bf16[2,32,256]{2,1,0:T(8,128)(2,1)S(1)}, bf16[2,32,256]{2,1,0:T(8,128)(2,1)S(1)}) custom-call(s32[1]{0:T(128)} %bitcast.3.head, s32[8,128]{1,0:T(8,128)S(1)} %get-tuple-element.30.ids_ref, bf16[2,32,1536]{2,1,0:T(8,128)(2,1)S(1)} %get-tuple-element.32.refs_0_, bf16[2,32,1536]{2,1,0:T(8,128)(2,1)S(1)} %collective-permute-done.refs_1_, ...), custom_call_target="tpu_custom_call" | custom-call | flops 201326592 | bytes 4718592 | tf_op jit(solution)/shard_map/pallas_call | solution.py:276
  13.2 1.6 %collective-permute-start.3 = (bf16[2,32,256]{2,1,0:T(8,128)(2,1)S(1)}, bf16[2,32,256]{2,1,0:T(8,128)(2,1)S(1)}, u32[]{:S(2)}, u32[]{:S(2)}) collective-permute-start(bf16[2,32,256]{2,1,0:T(8,128)(2,1)S(1)} %get-tuple-element.38.q_ref), channel_id=1, source_target_pairs={{0,8},{2,10},{4,12},{6,14},{8,0},{10,2},{12,4},{14,6},{16,24},{18,... | collective-permute-start | bytes 98312 | tf_op jit(solution)/shard_map/ppermute | solution.py:23
  14.9 0.0 collective-permute-done.4
  14.9 0.0 collective-permute-done.5
  14.9 0.0 copy-done
  14.9 1.6 %collective-permute-start.6 = (bf16[2,192,256]{2,1,0:T(8,128)(2,1)S(1)}, bf16[2,192,256]{2,1,0:T(8,128)(2,1)S(1)}, u32[]{:S(2)}, u32[]{:S(2)}) collective-permute-start(bf16[2,192,256]{2,1,0:T(8,128)(2,1)S(1)} %get-tuple-element.62), channel_id=1, source_target_pairs={{0,4},{2,6},{4,0},{6,2},{8,12},{10,14},{12,8},{14,10},{16,20},{18,... | collective-permute-start | bytes 589832 | tf_op jit(solution)/shard_map/ppermute | solution.py:23
  16.5 0.7 %collective-permute-done.3.mate_ref = bf16[2,32,256]{2,1,0:T(8,128)(2,1)S(1)} collective-permute-done((bf16[2,32,256]{2,1,0:T(8,128)(2,1)S(1)}, bf16[2,32,256]{2,1,0:T(8,128)(2,1)S(1)}, u32[]{:S(2)}, u32[]{:S(2)}) %collective-permute-start.3) | collective-permute-done | bytes 32800 | tf_op jit(solution)/shard_map/ppermute | solution.py:23
  17.2 0.0 collective-permute-done.2
  17.2 0.3 collective-permute-start.8
  17.5 1.8 %collective-permute-start.7 = (bf16[1,192,256]{2,1,0:T(8,128)(2,1)S(1)}, bf16[1,192,256]{2,1,0:T(8,128)(2,1)S(1)}, u32[]{:S(2)}, u32[]{:S(2)}) collective-permute-start(bf16[1,192,256]{2,1,0:T(8,128)(2,1)S(1)} %bitcast.26), channel_id=1, source_target_pairs={{0,4},{2,6},{4,0},{6,2},{8,12},{10,14},{12,8},{14,10},{16,20},{18,... | collective-permute-start | bytes 294920 | tf_op jit(solution)/shard_map/ppermute | solution.py:23
  19.4 0.2 collective-permute-start.9
  19.5 2.8 %collective-permute-start.10 = (bf16[2,4,32,256]{3,2,1,0:T(8,128)(2,1)S(1)}, bf16[2,4,32,256]{3,2,1,0:T(8,128)(2,1)S(1)}, u32[]{:S(2)}, u32[]{:S(2)}) collective-permute-start(bf16[2,4,32,256]{3,2,1,0:T(8,128)(2,1)S(1)} %pad_maximum_fusion.7.refs_0_), channel_id=1, source_target_pairs={{0,6},{2,4},{4,2},{6,0},{8,14},{10,12},{12,10},{14,8},{16,22},{18,... | collective-permute-start | bytes 393224 | tf_op jit(solution)/shard_map/ppermute | solution.py:23
  22.3 4.7 %collective-permute-done.7 = bf16[1,192,256]{2,1,0:T(8,128)(2,1)S(1)} collective-permute-done((bf16[1,192,256]{2,1,0:T(8,128)(2,1)S(1)}, bf16[1,192,256]{2,1,0:T(8,128)(2,1)S(1)}, u32[]{:S(2)}, u32[]{:S(2)}) %collective-permute-start.7) | collective-permute-done | bytes 98336 | tf_op jit(solution)/shard_map/ppermute | solution.py:23
  27.0 0.0 collective-permute-done.8.refs_1_
  27.0 0.0 collective-permute-done.6
  27.0 0.1 collective-permute-start.12
  27.1 1.3 %collective-permute-done.9.refs_2_ = bf16[2,4,32,256]{3,2,1,0:T(8,128)(2,1)S(1)} collective-permute-done((bf16[2,4,32,256]{3,2,1,0:T(8,128)(2,1)S(1)}, bf16[2,4,32,256]{3,2,1,0:T(8,128)(2,1)S(1)}, u32[]{:S(2)}, u32[]{:S(2)}) %collective-permute-start.9) | collective-permute-done | bytes 131104 | tf_op jit(solution)/shard_map/ppermute | solution.py:23
  28.4 0.0 collective-permute-done.10.refs_3_
  28.4 1.1 %shard_map.76.part_ref = bf16[128,384]{1,0:T(8,128)(2,1)S(1)} custom-call(bf16[2,32,256]{2,1,0:T(8,128)(2,1)S(1)} %get-tuple-element.38.q_ref, bf16[2,32,256]{2,1,0:T(8,128)(2,1)S(1)} %collective-permute-done.3.mate_ref, bf16[2,32,256]{2,1,0:T(8,128)(2,1)S(1)} %get-tuple-element.41.kv1_ref, bf16[2,4,32,256]{3,2,1,0:T(8,128)(2,1)S(1)} %pad_maximum_fusion.7.refs_0_, ...), custom_call_target="tpu_custom_call" | custom-call | flops 33554432 | tf_op jit(solution)/shard_map/pallas_call | solution.py:296
  29.5 0.5 %collective-permute-start.11 = (bf16[128,384]{1,0:T(8,128)(2,1)S(1)}, bf16[128,384]{1,0:T(8,128)(2,1)S(1)}, u32[]{:S(2)}, u32[]{:S(2)}) collective-permute-start(bf16[128,384]{1,0:T(8,128)(2,1)S(1)} %shard_map.76.part_ref), channel_id=1, source_target_pairs={{0,8},{2,10},{4,12},{6,14},{8,0},{10,2},{12,4},{14,6},{16,24},{18,... | collective-permute-start | bytes 294920 | tf_op jit(solution)/shard_map/ppermute | solution.py:23
  30.0 4.2 %collective-permute-done.11.other_ref = bf16[128,384]{1,0:T(8,128)(2,1)S(1)} collective-permute-done((bf16[128,384]{1,0:T(8,128)(2,1)S(1)}, bf16[128,384]{1,0:T(8,128)(2,1)S(1)}, u32[]{:S(2)}, u32[]{:S(2)}) %collective-permute-start.11) | collective-permute-done | bytes 98336 | tf_op jit(solution)/shard_map/ppermute | solution.py:23
  34.2 0.2 shard_map.77.refs_0_
  34.4 0.0 collective-permute-done.12
  34.5 0.4 shard_map.79
  35.0 0.1 collective-permute-start.13
  35.0 0.4 %shard_map.78.refs_0_ = f32[128,768]{1,0:T(8,128)S(1)} custom-call(s32[1]{0:T(128)} %bitcast.patch, s32[1]{0:T(128)} %bitcast.3.head, bf16[128,256]{1,0:T(8,128)(2,1)S(1)} %shard_map.77.refs_0_, bf16[2,192,256]{2,1,0:T(8,128)(2,1)S(1)} %get-tuple-element.61.refs_1_, bf16[2,192,256]{2,1,0:T(8,128)(2,1)S(1)} %get-tuple-element.63.refs_2_, ...), custom_call_target="tpu_custom_call" | custom-call | flops 50331648 | bytes 393216 | tf_op jit(solution)/shard_map/pallas_call | solution.py:309
  35.5 1.0 %collective-permute-done.13.refs_1_ = bf16[128,768]{1,0:T(8,128)(2,1)S(1)} collective-permute-done((bf16[128,768]{1,0:T(8,128)(2,1)S(1)}, bf16[128,768]{1,0:T(8,128)(2,1)S(1)}, u32[]{:S(2)}, u32[]{:S(2)}) %collective-permute-start.13) | collective-permute-done | bytes 196640 | tf_op jit(solution)/shard_map/ppermute | solution.py:23
  36.5 0.1 shard_map.80
  36.6 0.5 %collective-permute-start.14 = (bf16[2,32,768]{2,1,0:T(8,128)(2,1)S(1)}, bf16[2,32,768]{2,1,0:T(8,128)(2,1)S(1)}, u32[]{:S(2)}, u32[]{:S(2)}) collective-permute-start(bf16[2,32,768]{2,1,0:T(8,128)(2,1)S(1)} %get-tuple-element.53), channel_id=1, source_target_pairs={{0,8},{2,10},{4,12},{6,14},{8,0},{10,2},{12,4},{14,6},{16,24},{18,... | collective-permute-start | bytes 294920 | tf_op jit(solution)/shard_map/ppermute | solution.py:23
  37.1 4.4 %collective-permute-done.14 = bf16[2,32,768]{2,1,0:T(8,128)(2,1)S(1)} collective-permute-done((bf16[2,32,768]{2,1,0:T(8,128)(2,1)S(1)}, bf16[2,32,768]{2,1,0:T(8,128)(2,1)S(1)}, u32[]{:S(2)}, u32[]{:S(2)}) %collective-permute-start.14) | collective-permute-done | bytes 98336 | tf_op jit(solution)/shard_map/ppermute | solution.py:23
  41.5 0.7 %pad_maximum_fusion.6 = bf16[2,32,1536]{2,1,0:T(8,128)(2,1)} fusion(bf16[2,32,768]{2,1,0:T(8,128)(2,1)S(1)} %get-tuple-element.56, bf16[2,32,768]{2,1,0:T(8,128)(2,1)S(1)} %get-tuple-element.55), kind=kLoop, calls=%fused_computation.6 | loop fusion | flops 393216 | bytes 393216 | tf_op jit(solution)/shard_map/concatenate | solution.py:328
  (8 shorter events, 0.2 us)
Async XLA Ops:
  0.0 9.3 %collective-permute-start = (bf16[2,32,1536]{2,1,0:T(8,128)(2,1)}, bf16[2,32,1536]{2,1,0:T(8,128)(2,1)S(1)}, u32[]{:S(2)}, u32[]{:S(2)}) collective-permute-start(bf16[2,32,1536]{2,1,0:T(8,128)(2,1)} %x_ref.1), channel_id=1, source_target_pairs={{0,1},{1,0},{2,3},{3,2},{4,5},{5,4},{6,7},{7,6},{8,9},{9,8},{10,11... | collective-permute-start | bytes 589832 | tf_op jit(solution)/shard_map/ppermute | solution.py:23
  0.5 8.8 %collective-permute-start.1 = (f32[4,3,1536]{2,0,1:T(4,128)}, f32[4,3,1536]{2,0,1:T(4,128)S(1)}, u32[]{:S(2)}, u32[]{:S(2)}) collective-permute-start(f32[4,3,1536]{2,0,1:T(4,128)} %param.11), channel_id=1, source_target_pairs={{0,1},{1,0},{2,3},{3,2},{4,5},{5,4},{6,7},{7,6},{8,9},{9,8},{10,11... | collective-permute-start | bytes 221192 | tf_op jit(solution)/shard_map/ppermute | solution.py:23
  0.5 14.4 %collective-permute-start.4 = (bf16[192,256]{1,0:T(8,128)(2,1)}, bf16[192,256]{1,0:T(8,128)(2,1)S(1)}, u32[]{:S(2)}, u32[]{:S(2)}) collective-permute-start(bf16[192,256]{1,0:T(8,128)(2,1)} %bitcast.28), channel_id=1, source_target_pairs={{0,2},{2,0},{4,6},{6,4},{8,10},{10,8},{12,14},{14,12},{16,18},{18,... | collective-permute-start | bytes 294920 | tf_op jit(solution)/shard_map/ppermute | solution.py:23
  3.5 11.4 %collective-permute-start.5 = (bf16[192,256]{1,0:T(8,128)(2,1)}, bf16[192,256]{1,0:T(8,128)(2,1)S(1)}, u32[]{:S(2)}, u32[]{:S(2)}) collective-permute-start(bf16[192,256]{1,0:T(8,128)(2,1)} %bitcast.29), channel_id=1, source_target_pairs={{0,16},{2,18},{4,20},{6,22},{8,24},{10,26},{12,28},{14,30},{16,0},... | collective-permute-start | bytes 294920 | tf_op jit(solution)/shard_map/ppermute | solution.py:23
  10.2 4.7 %copy-start = (bf16[256,192]{0,1:T(8,128)(2,1)S(1)}, bf16[256,192]{0,1:T(8,128)(2,1)}, u32[]{:S(2)}) copy-start(bf16[256,192]{0,1:T(8,128)(2,1)} %param.10) | copy-start | bytes 294916
  10.2 7.0 %collective-permute-start.2 = (bf16[4,32,256]{2,1,0:T(8,128)(2,1)S(1)}, bf16[4,32,256]{2,1,0:T(8,128)(2,1)S(1)}, u32[]{:S(2)}, u32[]{:S(2)}) collective-permute-start(bf16[4,32,256]{2,1,0:T(8,128)(2,1)S(1)} %get-tuple-element.42), channel_id=1, source_target_pairs={{0,16},{2,18},{4,20},{6,22},{8,24},{10,26},{12,28},{14,30},{16,0},... | collective-permute-start | bytes 196616 | tf_op jit(solution)/shard_map/ppermute | solution.py:23
  13.2 4.0 %collective-permute-start.3 = (bf16[2,32,256]{2,1,0:T(8,128)(2,1)S(1)}, bf16[2,32,256]{2,1,0:T(8,128)(2,1)S(1)}, u32[]{:S(2)}, u32[]{:S(2)}) collective-permute-start(bf16[2,32,256]{2,1,0:T(8,128)(2,1)S(1)} %get-tuple-element.38.q_ref), channel_id=1, source_target_pairs={{0,8},{2,10},{4,12},{6,14},{8,0},{10,2},{12,4},{14,6},{16,24},{18,... | collective-permute-start | bytes 98312 | tf_op jit(solution)/shard_map/ppermute | solution.py:23
  14.9 12.1 %collective-permute-start.6 = (bf16[2,192,256]{2,1,0:T(8,128)(2,1)S(1)}, bf16[2,192,256]{2,1,0:T(8,128)(2,1)S(1)}, u32[]{:S(2)}, u32[]{:S(2)}) collective-permute-start(bf16[2,192,256]{2,1,0:T(8,128)(2,1)S(1)} %get-tuple-element.62), channel_id=1, source_target_pairs={{0,4},{2,6},{4,0},{6,2},{8,12},{10,14},{12,8},{14,10},{16,20},{18,... | collective-permute-start | bytes 589832 | tf_op jit(solution)/shard_map/ppermute | solution.py:23
  17.2 9.8 %collective-permute-start.8 = (bf16[2,4,32,256]{3,2,1,0:T(8,128)(2,1)S(1)}, bf16[2,4,32,256]{3,2,1,0:T(8,128)(2,1)S(1)}, u32[]{:S(2)}, u32[]{:S(2)}) collective-permute-start(bf16[2,4,32,256]{3,2,1,0:T(8,128)(2,1)S(1)} %pad_maximum_fusion.7.refs_0_), channel_id=1, source_target_pairs={{0,2},{2,0},{4,6},{6,4},{8,10},{10,8},{12,14},{14,12},{16,18},{18,... | collective-permute-start | bytes 393224 | tf_op jit(solution)/shard_map/ppermute | solution.py:23
  17.5 9.5 %collective-permute-start.7 = (bf16[1,192,256]{2,1,0:T(8,128)(2,1)S(1)}, bf16[1,192,256]{2,1,0:T(8,128)(2,1)S(1)}, u32[]{:S(2)}, u32[]{:S(2)}) collective-permute-start(bf16[1,192,256]{2,1,0:T(8,128)(2,1)S(1)} %bitcast.26), channel_id=1, source_target_pairs={{0,4},{2,6},{4,0},{6,2},{8,12},{10,14},{12,8},{14,10},{16,20},{18,... | collective-permute-start | bytes 294920 | tf_op jit(solution)/shard_map/ppermute | solution.py:23
  19.4 9.1 %collective-permute-start.9 = (bf16[2,4,32,256]{3,2,1,0:T(8,128)(2,1)S(1)}, bf16[2,4,32,256]{3,2,1,0:T(8,128)(2,1)S(1)}, u32[]{:S(2)}, u32[]{:S(2)}) collective-permute-start(bf16[2,4,32,256]{3,2,1,0:T(8,128)(2,1)S(1)} %pad_maximum_fusion.7.refs_0_), channel_id=1, source_target_pairs={{0,4},{2,6},{4,0},{6,2},{8,12},{10,14},{12,8},{14,10},{16,20},{18,... | collective-permute-start | bytes 393224 | tf_op jit(solution)/shard_map/ppermute | solution.py:23
  19.5 8.9 %collective-permute-start.10 = (bf16[2,4,32,256]{3,2,1,0:T(8,128)(2,1)S(1)}, bf16[2,4,32,256]{3,2,1,0:T(8,128)(2,1)S(1)}, u32[]{:S(2)}, u32[]{:S(2)}) collective-permute-start(bf16[2,4,32,256]{3,2,1,0:T(8,128)(2,1)S(1)} %pad_maximum_fusion.7.refs_0_), channel_id=1, source_target_pairs={{0,6},{2,4},{4,2},{6,0},{8,14},{10,12},{12,10},{14,8},{16,22},{18,... | collective-permute-start | bytes 393224 | tf_op jit(solution)/shard_map/ppermute | solution.py:23
  27.0 7.4 %collective-permute-start.12 = (bf16[2,1,192,256]{3,2,1,0:T(8,128)(2,1)S(1)}, bf16[2,1,192,256]{3,2,1,0:T(8,128)(2,1)S(1)}, u32[]{:S(2)}, u32[]{:S(2)}) collective-permute-start(bf16[2,1,192,256]{3,2,1,0:T(8,128)(2,1)S(1)} %pad_maximum_fusion.2), channel_id=1, source_target_pairs={{0,2},{2,0},{4,6},{6,4},{8,10},{10,8},{12,14},{14,12},{16,18},{18,... | collective-permute-start | bytes 589832 | tf_op jit(solution)/shard_map/ppermute | solution.py:23
  29.5 4.7 %collective-permute-start.11 = (bf16[128,384]{1,0:T(8,128)(2,1)S(1)}, bf16[128,384]{1,0:T(8,128)(2,1)S(1)}, u32[]{:S(2)}, u32[]{:S(2)}) collective-permute-start(bf16[128,384]{1,0:T(8,128)(2,1)S(1)} %shard_map.76.part_ref), channel_id=1, source_target_pairs={{0,8},{2,10},{4,12},{6,14},{8,0},{10,2},{12,4},{14,6},{16,24},{18,... | collective-permute-start | bytes 294920 | tf_op jit(solution)/shard_map/ppermute | solution.py:23
  35.0 1.5 %collective-permute-start.13 = (bf16[128,768]{1,0:T(8,128)(2,1)S(1)}, bf16[128,768]{1,0:T(8,128)(2,1)S(1)}, u32[]{:S(2)}, u32[]{:S(2)}) collective-permute-start(bf16[128,768]{1,0:T(8,128)(2,1)S(1)} %shard_map.79), channel_id=1, source_target_pairs={{0,1},{1,0},{2,3},{3,2},{4,5},{5,4},{6,7},{7,6},{8,9},{9,8},{10,11... | collective-permute-start | bytes 589832 | tf_op jit(solution)/shard_map/ppermute | solution.py:23
  36.6 4.9 %collective-permute-start.14 = (bf16[2,32,768]{2,1,0:T(8,128)(2,1)S(1)}, bf16[2,32,768]{2,1,0:T(8,128)(2,1)S(1)}, u32[]{:S(2)}, u32[]{:S(2)}) collective-permute-start(bf16[2,32,768]{2,1,0:T(8,128)(2,1)S(1)} %get-tuple-element.53), channel_id=1, source_target_pairs={{0,8},{2,10},{4,12},{6,14},{8,0},{10,2},{12,4},{14,6},{16,24},{18,... | collective-permute-start | bytes 294920 | tf_op jit(solution)/shard_map/ppermute | solution.py:23

commit v11 on v10

--- a/solution.py
+++ b/solution.py
@@ -26,12 +26,12 @@
 def load_kernel(ids, slab, w_ref, x_ref, mod_ref, stale_ref, w_out, x_out, mod_out, stale_out, *refs):
     ids_out, cos_ref, sin_ref, sems = refs
     copies = [
-        pltpu.make_async_copy(w_ref.at[slot + 1], w_out.at[slot], sems.at[slot])
-        for slot in range(2)
+        pltpu.make_async_copy(w_ref.at[slot], w_out.at[slot], sems.at[slot])
+        for slot in range(3)
     ]
-    copies.append(pltpu.make_async_copy(x_ref, x_out, sems.at[2]))
-    copies.append(pltpu.make_async_copy(mod_ref, mod_out, sems.at[3]))
-    copies.append(pltpu.make_async_copy(stale_ref, stale_out, sems.at[4]))
+    copies.append(pltpu.make_async_copy(x_ref, x_out, sems.at[3]))
+    copies.append(pltpu.make_async_copy(mod_ref, mod_out, sems.at[4]))
+    copies.append(pltpu.make_async_copy(stale_ref, stale_out, sems.at[5]))
     for copy in copies:
         copy.start()
     row = lax.broadcasted_iota(jnp.int32, ids_out.shape, 0)
@@ -91,35 +91,23 @@
     return jnp.concatenate(blocks, axis=1)
 
 
-def fresh_kernel(n_head, head, ids_ref, *refs):
+def qkv_kernel(n_head, head, ids_ref, *refs):
     x_refs, mod_refs = refs[:n_head], refs[n_head : 2 * n_head]
-    w_ref, cos_ref, sin_ref = refs[2 * n_head : 2 * n_head + 3]
-    stale_ref, a_ref, kv_ref = refs[2 * n_head + 3 :]
-    kv_ref[:2] = stale_ref[...]
-    parts = normalized(0, x_refs, mod_refs, ids_ref)
-    for number, part in enumerate(parts):
-        a_ref[number] = part
-    keys = rotated(projected(parts, w_ref, 0, head), cos_ref[...], sin_ref[...])
-    kv_ref[2] = keys.astype(BF16)
-    kv_ref[3] = projected(parts, w_ref, 1, head).astype(BF16)
-
-
-def rest_kernel(n_head, head, ids_ref, *refs):
-    x_refs, mod_refs = refs[:n_head], refs[n_head : 2 * n_head]
-    w_ref, cos_ref, sin_ref, a_ref, w_far, q_ref, kv1_ref, wq_ref, sem = refs[2 * n_head :]
-    copy = pltpu.make_async_copy(w_far.at[0], wq_ref.at[0], sem)
-    copy.start()
-    rows = a_ref.shape[1]
-    parts = normalized(1, x_refs, mod_refs, ids_ref)
-    cos, sin = cos_ref[...], sin_ref[...]
-    both = [jnp.concatenate([a_ref[k], part], axis=0) for k, part in enumerate(parts)]
-    kv1_ref[0] = rotated(projected(parts, w_ref, 0, head), cos, sin).astype(BF16)
-    kv1_ref[1] = projected(parts, w_ref, 1, head).astype(BF16)
-    copy.wait()
-    queries = projected(both, wq_ref, 0, head)
+    w_ref, cos_ref, sin_ref, stale_ref, q_ref, kv_ref, kv1_ref = refs[2 * n_head :]
+    rows = x_refs[0].shape[1]
+    steps = [normalized(step, x_refs, mod_refs, ids_ref) for step in range(STEPS)]
+    parts = [jnp.concatenate(pair, axis=0) for pair in zip(*steps)]
+    cos = jnp.concatenate([cos_ref[...]] * STEPS, axis=0)
+    sin = jnp.concatenate([sin_ref[...]] * STEPS, axis=0)
+    queries = rotated(projected(parts, w_ref, 0, head), cos, sin).astype(BF16)
+    keys = rotated(projected(parts, w_ref, 1, head), cos, sin).astype(BF16)
+    values = projected(parts, w_ref, 2, head).astype(BF16)
     for step in range(STEPS):
         spot = slice(step * rows, (step + 1) * rows)
-        q_ref[step] = rotated(queries[spot], cos, sin).astype(BF16)
+        q_ref[step] = queries[spot]
+    kv_ref[:2] = stale_ref[...]
+    kv_ref[2], kv_ref[3] = keys[:rows], values[:rows]
+    kv1_ref[0], kv1_ref[1] = keys[rows:], values[rows:]
 
 
 def split3(values):
@@ -241,11 +229,10 @@
     first = (jnp.transpose(w_qkv, (1, 0, 2)), inputs, jnp.transpose(mod_table, (1, 0, 2)), stale_kv)
     w, x_own, mod_own, stale, ids, cos, sin = call(
         load_kernel,
-        (pltpu.VMEM((2, *first[0].shape[1:]), BF16),)
-        + tuple(pltpu.VMEM(v.shape, v.dtype) for v in first[1:])
+        tuple(pltpu.VMEM(v.shape, v.dtype) for v in first)
         + (shaped((8, DH), jnp.int32), shaped((rows, DH), F32), shaped((rows, DH), F32)),
         [SMEM] * 2 + [ANY] * len(first),
-        [pltpu.SemaphoreType.DMA((5,))],
+        [pltpu.SemaphoreType.DMA((6,))],
         size=2 * w_qkv.size,
     )(in_hbm(step_ids), slab_order, *map(in_hbm, first))
     x_parts = [x_own] + x_parts
@@ -260,37 +247,26 @@
     def plane_of(values):
         return [values] + [across(values, k) for k in range(1, PLANE)]
 
-    w_own, *w_rest = line_of(w_out.T)
-    w_x = across(w_own, 1)
 
     kv_shape = shaped((2, rows, cols), BF16)
-    common = (head[None], ids, *x_parts, *mod_parts, w, cos, sin)
-    specs = [SMEM] + [VMEM] * (2 * n_head + 4)
-    a, kv = call(
-        functools.partial(fresh_kernel, n_head),
-        (shaped((n_head, rows, feats), BF16), shaped((4, rows, cols), BF16)),
-        specs + [VMEM],
-        flops=4 * rows * w_qkv.size // 3,
+    q, kv, kv1 = call(
+        functools.partial(qkv_kernel, n_head),
+        (kv_shape, shaped((4, rows, cols), BF16), kv_shape),
+        [SMEM] + [VMEM] * (2 * n_head + 5),
+        flops=2 * STEPS * rows * w_qkv.size,
         size=2 * w_qkv.size,
-    )(*common, stale)
-    q, kv1 = call(
-        functools.partial(rest_kernel, n_head),
-        (kv_shape, kv_shape),
-        specs + [VMEM, ANY],
-        [pltpu.VMEM((1, *first[0].shape[1:]), BF16), pltpu.SemaphoreType.DMA],
-        8 * rows * w_qkv.size // 3,
-        2 * w_qkv.size,
-    )(*common, a, in_hbm(first[0]))
-
+    )(head[None], ids, *x_parts, *mod_parts, w, cos, sin, stale)
+
+    w_own, kv = lax.optimization_barrier((w_out.T, kv))
     kv_pair = line_of(kv)
     q_mate = across(q, PLANE)
-    w_own, w_x, w_rest, kv = lax.optimization_barrier((w_own, w_x, w_rest, kv))
+    w_x = across(w_own, 1)
+    w_rest = jnp.stack(line_of(w_own)[1:])
+    kv_plane = plane_of(jnp.stack(kv_pair))
+    w_x, w_rest, q_mate = lax.optimization_barrier((w_x, w_rest, q_mate))
     w_y = across(jnp.stack([w_own, w_x]), 2)
-    w_rest = jnp.stack(w_rest)
     rest_y = across(w_rest, 2)
-    kv_pair, q_mate = lax.optimization_barrier((kv_pair, q_mate))
-    kv_plane = plane_of(jnp.stack(kv_pair))
-    w_y, rest_y, kv_plane[1] = lax.optimization_barrier((w_y, rest_y, kv_plane[1]))
+    rest_y, *kv_plane[1:] = lax.optimization_barrier((rest_y, *kv_plane[1:]))
     rest_x = across(jnp.stack([w_rest, rest_y]), 1)
     tall = 2 * STEPS * rows
     part = call(

time: 42.4 us -> 41.6 us (0.981)
  starting transfers between devices: 15.9 us -> 19.9 us
  waiting for transfers between devices: 16.3 us -> 13.1 us
  Pallas kernels: 8.35 us -> 6.65 us
    ppermute x15, starting transfers between devices: 15.9 us -> 19.9 us  [swap(): return lax.ppermute(values, axis, [(i, i ^ bit) for i in range(count)])]
    ppermute x15, waiting for transfers between devices: 16.3 us -> 13.1 us  [swap(): return lax.ppermute(values, axis, [(i, i ^ bit) for i in range(count)])]
    pallas_call x3 -> x2, Pallas kernels: 6.08 us -> 4.37 us  [the longest x1 3.21 us: body(): call(load_kernel, tuple((pltpu.VMEM(v.shape, v.dtype) for v in first)) +...]
  transfers between devices with their start and end apart: 15 -> 15, of which waited for: 6 -> 7; matrix products, arithmetic and copies ran while one was open for 0% -> 0% of each run, Pallas kernels for 19% -> 12%
where the time goes in v11:
time: 41.6 us; the launch traced here: 41.3 us
  starting transfers between devices  19.9 us (48%)
  waiting for transfers between devices  13.1 us (31%)
  Pallas kernels  6.65 us (16%)
  other arithmetic  0.85 us (2%)
  between operations  0.79 us (2%)
    ppermute x15, starting transfers between devices, swap(): return lax.ppermute(values, axis, [(i, i ^ bit) for i in range(count)])  19.9 us
    ppermute x15, waiting for transfers between devices, swap(): return lax.ppermute(values, axis, [(i, i ^ bit) for i in range(count)])  13.1 us
    pallas_call x1, Pallas kernels, body(): call(load_kernel, tuple((pltpu.VMEM(v.shape, v.dtype) for v in first)) +...  3.21 us
    pallas_call x1, Pallas kernels, body(): call(functools.partial(qkv_kernel, n_head), (kv_shape, shaped((4, rows, c...  1.16 us
    pallas_call x1, Pallas kernels, body(): call(attend_kernel, shaped((tall, cols + DH), BF16), [VMEM] * (3 + PLANE)...  1.11 us
  transfers between devices with their start and end apart: 15, of which 7 were waited for; matrix products, arithmetic and copies ran while one was open for 0% of the time, Pallas kernels for 12%

profile of v11, /device:TPU:0, one launch (start us, length us, event | category | flops | bytes accessed | tf_op | source)
XLA Modules:
  0.0 41.3 jit_solution(12596883934975614696)
XLA Ops:
  0.0 0.5 %collective-permute-start = (bf16[2,32,1536]{2,1,0:T(8,128)(2,1)}, bf16[2,32,1536]{2,1,0:T(8,128)(2,1)S(1)}, u32[]{:S(2)}, u32[]{:S(2)}) collective-permute-start(bf16[2,32,1536]{2,1,0:T(8,128)(2,1)} %x_ref.1), channel_id=1, source_target_pairs={{0,1},{1,0},{2,3},{3,2},{4,5},{5,4},{6,7},{7,6},{8,9},{9,8},{10,11... | collective-permute-start | bytes 589832 | tf_op jit(solution)/shard_map/ppermute | solution.py:23
  0.5 0.1 collective-permute-start.1
  1.2 0.0 copy-start
  1.2 3.2 %shard_map.73 = (bf16[3,3072,256]{2,1,0:T(8,128)(2,1)S(1)}, bf16[2,32,1536]{2,1,0:T(8,128)(2,1)S(1)}, f32[3,4,1536]{2,1,0:T(4,128)S(1)}, bf16[2,32,256]{2,1,0:T(...) custom-call(s32[2]{0:T(128)} %ids.1, s32[1]{0:T(128)S(6)} %copy.8.slab, ...), custom_call_target="tpu_custom_call" | custom-call | bytes 4718592 | tf_op jit(solution)/shard_map/pallas_call | solution.py:230
  4.4 0.0 collective-permute-done.1
  4.4 0.0 collective-permute-done.refs_1_
  4.4 1.2 %shard_map.74 = (bf16[2,32,256]{2,1,0:T(8,128)(2,1)S(1)}, bf16[4,32,256]{2,1,0:T(8,128)(2,1)S(1)}, bf16[2,32,256]{2,1,0:T(8,128)(2,1)S(1)}) custom-call(s32[1]{0:T(128)} %bitcast.3.head, s32[8,128]{1,0:T(8,128)S(1)} %get-tuple-element.29.ids_ref, bf16[2,32,1536]{2,1,0:T(8,128)(2,1)S(1)} %get-tuple-element.31.refs_0_, ...), custom_call_target="tpu_custom_call" | custom-call | flops 301989888 | bytes 4718592 | tf_op jit(solution)/shard_map/pallas_call | solution.py:252
  5.6 4.1 %collective-permute-start.5 = (bf16[4,32,256]{2,1,0:T(8,128)(2,1)S(1)}, bf16[4,32,256]{2,1,0:T(8,128)(2,1)S(1)}, u32[]{:S(2)}, u32[]{:S(2)}) collective-permute-start(bf16[4,32,256]{2,1,0:T(8,128)(2,1)S(1)} %get-tuple-element.41), channel_id=1, source_target_pairs={{0,16},{2,18},{4,20},{6,22},{8,24},{10,26},{12,28},{14,30},{16,0},... | collective-permute-start | bytes 196616 | tf_op jit(solution)/shard_map/ppermute | solution.py:23
  9.7 0.0 copy-done
  9.7 0.1 collective-permute-start.3
  9.8 1.7 %collective-permute-start.2 = (bf16[192,256]{1,0:T(8,128)(2,1)S(1)}, bf16[192,256]{1,0:T(8,128)(2,1)S(1)}, u32[]{:S(2)}, u32[]{:S(2)}) collective-permute-start(bf16[192,256]{1,0:T(8,128)(2,1)S(1)} %bitcast.27), channel_id=1, source_target_pairs={{0,2},{2,0},{4,6},{6,4},{8,10},{10,8},{12,14},{14,12},{16,18},{18,... | collective-permute-start | bytes 294920 | tf_op jit(solution)/shard_map/ppermute | solution.py:23
  11.5 1.6 %collective-permute-start.4 = (bf16[2,32,256]{2,1,0:T(8,128)(2,1)S(1)}, bf16[2,32,256]{2,1,0:T(8,128)(2,1)S(1)}, u32[]{:S(2)}, u32[]{:S(2)}) collective-permute-start(bf16[2,32,256]{2,1,0:T(8,128)(2,1)S(1)} %get-tuple-element.36.q_ref), channel_id=1, source_target_pairs={{0,8},{2,10},{4,12},{6,14},{8,0},{10,2},{12,4},{14,6},{16,24},{18,... | collective-permute-start | bytes 98312 | tf_op jit(solution)/shard_map/ppermute | solution.py:23
  13.1 0.3 collective-permute-done.5
  13.4 3.3 %collective-permute-start.7 = (bf16[2,4,32,256]{3,2,1,0:T(8,128)(2,1)S(1)}, bf16[2,4,32,256]{3,2,1,0:T(8,128)(2,1)S(1)}, u32[]{:S(2)}, u32[]{:S(2)}) collective-permute-start(bf16[2,4,32,256]{3,2,1,0:T(8,128)(2,1)S(1)} %pad_maximum_fusion.7.refs_0_), channel_id=1, source_target_pairs={{0,2},{2,0},{4,6},{6,4},{8,10},{10,8},{12,14},{14,12},{16,18},{18,... | collective-permute-start | bytes 393224 | tf_op jit(solution)/shard_map/ppermute | solution.py:23
  16.7 1.5 %collective-permute-start.8 = (bf16[2,4,32,256]{3,2,1,0:T(8,128)(2,1)S(1)}, bf16[2,4,32,256]{3,2,1,0:T(8,128)(2,1)S(1)}, u32[]{:S(2)}, u32[]{:S(2)}) collective-permute-start(bf16[2,4,32,256]{3,2,1,0:T(8,128)(2,1)S(1)} %pad_maximum_fusion.7.refs_0_), channel_id=1, source_target_pairs={{0,4},{2,6},{4,0},{6,2},{8,12},{10,14},{12,8},{14,10},{16,20},{18,... | collective-permute-start | bytes 393224 | tf_op jit(solution)/shard_map/ppermute | solution.py:23
  18.2 0.0 collective-permute-done.4.mate_ref
  18.2 0.0 collective-permute-start.9
  18.2 0.0 collective-permute-done.3
  18.2 0.0 collective-permute-done.2
  18.2 2.0 %collective-permute-start.6 = (bf16[1,192,256]{2,1,0:T(8,128)(2,1)S(1)}, bf16[1,192,256]{2,1,0:T(8,128)(2,1)S(1)}, u32[]{:S(2)}, u32[]{:S(2)}) collective-permute-start(bf16[1,192,256]{2,1,0:T(8,128)(2,1)S(1)} %bitcast.23), channel_id=1, source_target_pairs={{0,4},{2,6},{4,0},{6,2},{8,12},{10,14},{12,8},{14,10},{16,20},{18,... | collective-permute-start | bytes 294920 | tf_op jit(solution)/shard_map/ppermute | solution.py:23
  20.2 0.2 collective-permute-start.11
  20.4 0.4 %collective-permute-done.7.refs_1_ = bf16[2,4,32,256]{3,2,1,0:T(8,128)(2,1)S(1)} collective-permute-done((bf16[2,4,32,256]{3,2,1,0:T(8,128)(2,1)S(1)}, bf16[2,4,32,256]{3,2,1,0:T(8,128)(2,1)S(1)}, u32[]{:S(2)}, u32[]{:S(2)}) %collective-permute-start.7) | collective-permute-done | bytes 131104 | tf_op jit(solution)/shard_map/ppermute | solution.py:23
  20.8 3.6 %collective-permute-done.8.refs_2_ = bf16[2,4,32,256]{3,2,1,0:T(8,128)(2,1)S(1)} collective-permute-done((bf16[2,4,32,256]{3,2,1,0:T(8,128)(2,1)S(1)}, bf16[2,4,32,256]{3,2,1,0:T(8,128)(2,1)S(1)}, u32[]{:S(2)}, u32[]{:S(2)}) %collective-permute-start.8) | collective-permute-done | bytes 131104 | tf_op jit(solution)/shard_map/ppermute | solution.py:23
  24.5 0.0 collective-permute-done.9.refs_3_
  24.5 2.1 %collective-permute-done.6 = bf16[1,192,256]{2,1,0:T(8,128)(2,1)S(1)} collective-permute-done((bf16[1,192,256]{2,1,0:T(8,128)(2,1)S(1)}, bf16[1,192,256]{2,1,0:T(8,128)(2,1)S(1)}, u32[]{:S(2)}, u32[]{:S(2)}) %collective-permute-start.6) | collective-permute-done | bytes 98336 | tf_op jit(solution)/shard_map/ppermute | solution.py:23
  26.6 0.3 collective-permute-start.12
  26.9 1.1 %shard_map.75.part_ref = bf16[128,384]{1,0:T(8,128)(2,1)S(1)} custom-call(bf16[2,32,256]{2,1,0:T(8,128)(2,1)S(1)} %get-tuple-element.36.q_ref, bf16[2,32,256]{2,1,0:T(8,128)(2,1)S(1)} %collective-permute-done.4.mate_ref, bf16[2,32,256]{2,1,0:T(8,128)(2,1)S(1)} %get-tuple-element.40.kv1_ref, bf16[2,4,32,256]{3,2,1,0:T(8,128)(2,1)S(1)} %pad_maximum_fusion.7.refs_0_, ...), custom_call_target="tpu_custom_call" | custom-call | flops 33554432 | tf_op jit(solution)/shard_map/pallas_call | solution.py:272
  28.0 2.4 %collective-permute-start.10 = (bf16[128,384]{1,0:T(8,128)(2,1)S(1)}, bf16[128,384]{1,0:T(8,128)(2,1)S(1)}, u32[]{:S(2)}, u32[]{:S(2)}) collective-permute-start(bf16[128,384]{1,0:T(8,128)(2,1)S(1)} %shard_map.75.part_ref), channel_id=1, source_target_pairs={{0,8},{2,10},{4,12},{6,14},{8,0},{10,2},{12,4},{14,6},{16,24},{18,... | collective-permute-start | bytes 294920 | tf_op jit(solution)/shard_map/ppermute | solution.py:23
  30.4 2.6 %collective-permute-done.10.other_ref = bf16[128,384]{1,0:T(8,128)(2,1)S(1)} collective-permute-done((bf16[128,384]{1,0:T(8,128)(2,1)S(1)}, bf16[128,384]{1,0:T(8,128)(2,1)S(1)}, u32[]{:S(2)}, u32[]{:S(2)}) %collective-permute-start.10) | collective-permute-done | bytes 98336 | tf_op jit(solution)/shard_map/ppermute | solution.py:23
  33.0 0.2 shard_map.76.refs_0_
  33.3 0.0 collective-permute-done.11
  33.3 0.0 collective-permute-done.12
  33.4 0.1 pad_maximum_fusion.3
  33.4 0.4 shard_map.78
  33.8 0.1 collective-permute-start.13
  33.9 0.4 %shard_map.77.refs_0_ = f32[128,768]{1,0:T(8,128)S(1)} custom-call(s32[1]{0:T(128)} %bitcast.patch, s32[1]{0:T(128)} %bitcast.3.head, bf16[128,256]{1,0:T(8,128)(2,1)S(1)} %shard_map.76.refs_0_, bf16[2,192,256]{2,1,0:T(8,128)(2,1)S(1)} %get-tuple-element.59.refs_1_, bf16[2,192,256]{2,1,0:T(8,128)(2,1)S(1)} %get-tuple-element.61.refs_2_, ...), custom_call_target="tpu_custom_call" | custom-call | flops 50331648 | bytes 393216 | tf_op jit(solution)/shard_map/pallas_call | solution.py:285
  34.3 1.0 %collective-permute-done.13.refs_1_ = bf16[128,768]{1,0:T(8,128)(2,1)S(1)} collective-permute-done((bf16[128,768]{1,0:T(8,128)(2,1)S(1)}, bf16[128,768]{1,0:T(8,128)(2,1)S(1)}, u32[]{:S(2)}, u32[]{:S(2)}) %collective-permute-start.13) | collective-permute-done | bytes 196640 | tf_op jit(solution)/shard_map/ppermute | solution.py:23
  35.3 0.1 shard_map.79
  35.5 2.1 %collective-permute-start.14 = (bf16[2,32,768]{2,1,0:T(8,128)(2,1)S(1)}, bf16[2,32,768]{2,1,0:T(8,128)(2,1)S(1)}, u32[]{:S(2)}, u32[]{:S(2)}) collective-permute-start(bf16[2,32,768]{2,1,0:T(8,128)(2,1)S(1)} %get-tuple-element.51), channel_id=1, source_target_pairs={{0,8},{2,10},{4,12},{6,14},{8,0},{10,2},{12,4},{14,6},{16,24},{18,... | collective-permute-start | bytes 294920 | tf_op jit(solution)/shard_map/ppermute | solution.py:23
  37.5 3.1 %collective-permute-done.14 = bf16[2,32,768]{2,1,0:T(8,128)(2,1)S(1)} collective-permute-done((bf16[2,32,768]{2,1,0:T(8,128)(2,1)S(1)}, bf16[2,32,768]{2,1,0:T(8,128)(2,1)S(1)}, u32[]{:S(2)}, u32[]{:S(2)}) %collective-permute-start.14) | collective-permute-done | bytes 98336 | tf_op jit(solution)/shard_map/ppermute | solution.py:23
  40.7 0.7 %pad_maximum_fusion.6 = bf16[2,32,1536]{2,1,0:T(8,128)(2,1)} fusion(bf16[2,32,768]{2,1,0:T(8,128)(2,1)S(1)} %get-tuple-element.54, bf16[2,32,768]{2,1,0:T(8,128)(2,1)S(1)} %get-tuple-element.53), kind=kLoop, calls=%fused_computation.6 | loop fusion | flops 393216 | bytes 393216 | tf_op jit(solution)/shard_map/concatenate | solution.py:304
  (7 shorter events, 0.1 us)
Async XLA Ops:
  0.0 4.4 %collective-permute-start = (bf16[2,32,1536]{2,1,0:T(8,128)(2,1)}, bf16[2,32,1536]{2,1,0:T(8,128)(2,1)S(1)}, u32[]{:S(2)}, u32[]{:S(2)}) collective-permute-start(bf16[2,32,1536]{2,1,0:T(8,128)(2,1)} %x_ref.1), channel_id=1, source_target_pairs={{0,1},{1,0},{2,3},{3,2},{4,5},{5,4},{6,7},{7,6},{8,9},{9,8},{10,11... | collective-permute-start | bytes 589832 | tf_op jit(solution)/shard_map/ppermute | solution.py:23
  0.5 3.9 %collective-permute-start.1 = (f32[4,3,1536]{2,0,1:T(4,128)}, f32[4,3,1536]{2,0,1:T(4,128)S(1)}, u32[]{:S(2)}, u32[]{:S(2)}) collective-permute-start(f32[4,3,1536]{2,0,1:T(4,128)} %param.11), channel_id=1, source_target_pairs={{0,1},{1,0},{2,3},{3,2},{4,5},{5,4},{6,7},{7,6},{8,9},{9,8},{10,11... | collective-permute-start | bytes 221192 | tf_op jit(solution)/shard_map/ppermute | solution.py:23
  1.2 8.5 %copy-start = (bf16[256,192]{0,1:T(8,128)(2,1)S(1)}, bf16[256,192]{0,1:T(8,128)(2,1)}, u32[]{:S(2)}) copy-start(bf16[256,192]{0,1:T(8,128)(2,1)} %param.10) | copy-start | bytes 294916
  5.6 7.8 %collective-permute-start.5 = (bf16[4,32,256]{2,1,0:T(8,128)(2,1)S(1)}, bf16[4,32,256]{2,1,0:T(8,128)(2,1)S(1)}, u32[]{:S(2)}, u32[]{:S(2)}) collective-permute-start(bf16[4,32,256]{2,1,0:T(8,128)(2,1)S(1)} %get-tuple-element.41), channel_id=1, source_target_pairs={{0,16},{2,18},{4,20},{6,22},{8,24},{10,26},{12,28},{14,30},{16,0},... | collective-permute-start | bytes 196616 | tf_op jit(solution)/shard_map/ppermute | solution.py:23
  9.7 8.5 %collective-permute-start.3 = (bf16[192,256]{1,0:T(8,128)(2,1)S(1)}, bf16[192,256]{1,0:T(8,128)(2,1)S(1)}, u32[]{:S(2)}, u32[]{:S(2)}) collective-permute-start(bf16[192,256]{1,0:T(8,128)(2,1)S(1)} %bitcast.26), channel_id=1, source_target_pairs={{0,16},{2,18},{4,20},{6,22},{8,24},{10,26},{12,28},{14,30},{16,0},... | collective-permute-start | bytes 294920 | tf_op jit(solution)/shard_map/ppermute | solution.py:23
  9.8 8.5 %collective-permute-start.2 = (bf16[192,256]{1,0:T(8,128)(2,1)S(1)}, bf16[192,256]{1,0:T(8,128)(2,1)S(1)}, u32[]{:S(2)}, u32[]{:S(2)}) collective-permute-start(bf16[192,256]{1,0:T(8,128)(2,1)S(1)} %bitcast.27), channel_id=1, source_target_pairs={{0,2},{2,0},{4,6},{6,4},{8,10},{10,8},{12,14},{14,12},{16,18},{18,... | collective-permute-start | bytes 294920 | tf_op jit(solution)/shard_map/ppermute | solution.py:23
  11.5 6.7 %collective-permute-start.4 = (bf16[2,32,256]{2,1,0:T(8,128)(2,1)S(1)}, bf16[2,32,256]{2,1,0:T(8,128)(2,1)S(1)}, u32[]{:S(2)}, u32[]{:S(2)}) collective-permute-start(bf16[2,32,256]{2,1,0:T(8,128)(2,1)S(1)} %get-tuple-element.36.q_ref), channel_id=1, source_target_pairs={{0,8},{2,10},{4,12},{6,14},{8,0},{10,2},{12,4},{14,6},{16,24},{18,... | collective-permute-start | bytes 98312 | tf_op jit(solution)/shard_map/ppermute | solution.py:23
  13.4 7.5 %collective-permute-start.7 = (bf16[2,4,32,256]{3,2,1,0:T(8,128)(2,1)S(1)}, bf16[2,4,32,256]{3,2,1,0:T(8,128)(2,1)S(1)}, u32[]{:S(2)}, u32[]{:S(2)}) collective-permute-start(bf16[2,4,32,256]{3,2,1,0:T(8,128)(2,1)S(1)} %pad_maximum_fusion.7.refs_0_), channel_id=1, source_target_pairs={{0,2},{2,0},{4,6},{6,4},{8,10},{10,8},{12,14},{14,12},{16,18},{18,... | collective-permute-start | bytes 393224 | tf_op jit(solution)/shard_map/ppermute | solution.py:23
  16.7 7.8 %collective-permute-start.8 = (bf16[2,4,32,256]{3,2,1,0:T(8,128)(2,1)S(1)}, bf16[2,4,32,256]{3,2,1,0:T(8,128)(2,1)S(1)}, u32[]{:S(2)}, u32[]{:S(2)}) collective-permute-start(bf16[2,4,32,256]{3,2,1,0:T(8,128)(2,1)S(1)} %pad_maximum_fusion.7.refs_0_), channel_id=1, source_target_pairs={{0,4},{2,6},{4,0},{6,2},{8,12},{10,14},{12,8},{14,10},{16,20},{18,... | collective-permute-start | bytes 393224 | tf_op jit(solution)/shard_map/ppermute | solution.py:23
  18.2 6.3 %collective-permute-start.9 = (bf16[2,4,32,256]{3,2,1,0:T(8,128)(2,1)S(1)}, bf16[2,4,32,256]{3,2,1,0:T(8,128)(2,1)S(1)}, u32[]{:S(2)}, u32[]{:S(2)}) collective-permute-start(bf16[2,4,32,256]{3,2,1,0:T(8,128)(2,1)S(1)} %pad_maximum_fusion.7.refs_0_), channel_id=1, source_target_pairs={{0,6},{2,4},{4,2},{6,0},{8,14},{10,12},{12,10},{14,8},{16,22},{18,... | collective-permute-start | bytes 393224 | tf_op jit(solution)/shard_map/ppermute | solution.py:23
  18.2 8.3 %collective-permute-start.6 = (bf16[1,192,256]{2,1,0:T(8,128)(2,1)S(1)}, bf16[1,192,256]{2,1,0:T(8,128)(2,1)S(1)}, u32[]{:S(2)}, u32[]{:S(2)}) collective-permute-start(bf16[1,192,256]{2,1,0:T(8,128)(2,1)S(1)} %bitcast.23), channel_id=1, source_target_pairs={{0,4},{2,6},{4,0},{6,2},{8,12},{10,14},{12,8},{14,10},{16,20},{18,... | collective-permute-start | bytes 294920 | tf_op jit(solution)/shard_map/ppermute | solution.py:23
  20.2 13.0 %collective-permute-start.11 = (bf16[2,192,256]{2,1,0:T(8,128)(2,1)S(1)}, bf16[2,192,256]{2,1,0:T(8,128)(2,1)S(1)}, u32[]{:S(2)}, u32[]{:S(2)}) collective-permute-start(bf16[2,192,256]{2,1,0:T(8,128)(2,1)S(1)} %get-tuple-element.60), channel_id=1, source_target_pairs={{0,4},{2,6},{4,0},{6,2},{8,12},{10,14},{12,8},{14,10},{16,20},{18,... | collective-permute-start | bytes 589832 | tf_op jit(solution)/shard_map/ppermute | solution.py:23
  26.6 6.7 %collective-permute-start.12 = (bf16[2,1,192,256]{3,2,1,0:T(8,128)(2,1)S(1)}, bf16[2,1,192,256]{3,2,1,0:T(8,128)(2,1)S(1)}, u32[]{:S(2)}, u32[]{:S(2)}) collective-permute-start(bf16[2,1,192,256]{3,2,1,0:T(8,128)(2,1)S(1)} %pad_maximum_fusion.2), channel_id=1, source_target_pairs={{0,2},{2,0},{4,6},{6,4},{8,10},{10,8},{12,14},{14,12},{16,18},{18,... | collective-permute-start | bytes 589832 | tf_op jit(solution)/shard_map/ppermute | solution.py:23
  28.0 5.0 %collective-permute-start.10 = (bf16[128,384]{1,0:T(8,128)(2,1)S(1)}, bf16[128,384]{1,0:T(8,128)(2,1)S(1)}, u32[]{:S(2)}, u32[]{:S(2)}) collective-permute-start(bf16[128,384]{1,0:T(8,128)(2,1)S(1)} %shard_map.75.part_ref), channel_id=1, source_target_pairs={{0,8},{2,10},{4,12},{6,14},{8,0},{10,2},{12,4},{14,6},{16,24},{18,... | collective-permute-start | bytes 294920 | tf_op jit(solution)/shard_map/ppermute | solution.py:23
  33.8 1.5 %collective-permute-start.13 = (bf16[128,768]{1,0:T(8,128)(2,1)S(1)}, bf16[128,768]{1,0:T(8,128)(2,1)S(1)}, u32[]{:S(2)}, u32[]{:S(2)}) collective-permute-start(bf16[128,768]{1,0:T(8,128)(2,1)S(1)} %shard_map.78), channel_id=1, source_target_pairs={{0,1},{1,0},{2,3},{3,2},{4,5},{5,4},{6,7},{7,6},{8,9},{9,8},{10,11... | collective-permute-start | bytes 589832 | tf_op jit(solution)/shard_map/ppermute | solution.py:23
  35.5 5.2 %collective-permute-start.14 = (bf16[2,32,768]{2,1,0:T(8,128)(2,1)S(1)}, bf16[2,32,768]{2,1,0:T(8,128)(2,1)S(1)}, u32[]{:S(2)}, u32[]{:S(2)}) collective-permute-start(bf16[2,32,768]{2,1,0:T(8,128)(2,1)S(1)} %get-tuple-element.51), channel_id=1, source_target_pairs={{0,8},{2,10},{4,12},{6,14},{8,0},{10,2},{12,4},{14,6},{16,24},{18,... | collective-permute-start | bytes 294920 | tf_op jit(solution)/shard_map/ppermute | solution.py:23

commit v12 on v11

--- a/solution.py
+++ b/solution.py
@@ -257,16 +257,16 @@
         size=2 * w_qkv.size,
     )(head[None], ids, *x_parts, *mod_parts, w, cos, sin, stale)
 
-    w_own, kv = lax.optimization_barrier((w_out.T, kv))
+    w_own, w_rest, kv = lax.optimization_barrier((w_out.T, line_of(w_out.T)[1:], kv))
+    w_rest = jnp.stack(w_rest)
     kv_pair = line_of(kv)
     q_mate = across(q, PLANE)
     w_x = across(w_own, 1)
-    w_rest = jnp.stack(line_of(w_own)[1:])
     kv_plane = plane_of(jnp.stack(kv_pair))
-    w_x, w_rest, q_mate = lax.optimization_barrier((w_x, w_rest, q_mate))
+    w_rest, q_mate = lax.optimization_barrier((w_rest, q_mate))
+    rest_y = across(w_rest, 2)
+    rest_y, w_x, kv_plane[1] = lax.optimization_barrier((rest_y, w_x, kv_plane[1]))
     w_y = across(jnp.stack([w_own, w_x]), 2)
-    rest_y = across(w_rest, 2)
-    rest_y, *kv_plane[1:] = lax.optimization_barrier((rest_y, *kv_plane[1:]))
     rest_x = across(jnp.stack([w_rest, rest_y]), 1)
     tall = 2 * STEPS * rows
     part = call(

time: 41.6 us -> 41.9 us (level)
  transfers between devices with their start and end apart: 15 -> 15, of which waited for: 7 -> 7; matrix products, arithmetic and copies ran while one was open for 0% -> 0% of each run, Pallas kernels for 12% -> 15%
where the time goes in v12:
time: 41.9 us; the launch traced here: 41.8 us
  starting transfers between devices  20 us (48%)
  waiting for transfers between devices  13.4 us (32%)
  Pallas kernels  6.65 us (16%)
  other arithmetic  0.85 us (2%)
  between operations  0.79 us (2%)
    ppermute x15, starting transfers between devices, swap(): return lax.ppermute(values, axis, [(i, i ^ bit) for i in range(count)])  20 us
    ppermute x15, waiting for transfers between devices, swap(): return lax.ppermute(values, axis, [(i, i ^ bit) for i in range(count)])  13.4 us
    pallas_call x1, Pallas kernels, body(): call(load_kernel, tuple((pltpu.VMEM(v.shape, v.dtype) for v in first)) +...  3.21 us
    pallas_call x1, Pallas kernels, body(): call(functools.partial(qkv_kernel, n_head), (kv_shape, shaped((4, rows, c...  1.16 us
    pallas_call x1, Pallas kernels, body(): call(attend_kernel, shaped((tall, cols + DH), BF16), [VMEM] * (3 + PLANE)...  1.11 us
  transfers between devices with their start and end apart: 15, of which 7 were waited for; matrix products, arithmetic and copies ran while one was open for 0% of the time, Pallas kernels for 15%

profile of v12, /device:TPU:0, one launch (start us, length us, event | category | flops | bytes accessed | tf_op | source)
XLA Modules:
  0.0 41.8 jit_solution(16579551710134786803)
XLA Ops:
  0.0 0.5 %collective-permute-start = (bf16[2,32,1536]{2,1,0:T(8,128)(2,1)}, bf16[2,32,1536]{2,1,0:T(8,128)(2,1)S(1)}, u32[]{:S(2)}, u32[]{:S(2)}) collective-permute-start(bf16[2,32,1536]{2,1,0:T(8,128)(2,1)} %x_ref.1), channel_id=1, source_target_pairs={{0,1},{1,0},{2,3},{3,2},{4,5},{5,4},{6,7},{7,6},{8,9},{9,8},{10,11... | collective-permute-start | bytes 589832 | tf_op jit(solution)/shard_map/ppermute | solution.py:23
  0.5 0.1 collective-permute-start.1
  0.5 4.0 %collective-permute-start.2 = (bf16[192,256]{1,0:T(8,128)(2,1)}, bf16[192,256]{1,0:T(8,128)(2,1)S(1)}, u32[]{:S(2)}, u32[]{:S(2)}) collective-permute-start(bf16[192,256]{1,0:T(8,128)(2,1)} %bitcast.26), channel_id=1, source_target_pairs={{0,16},{2,18},{4,20},{6,22},{8,24},{10,26},{12,28},{14,30},{16,0},... | collective-permute-start | bytes 294920 | tf_op jit(solution)/shard_map/ppermute | solution.py:23
  5.2 0.0 copy-start
  5.2 3.2 %shard_map.73 = (bf16[3,3072,256]{2,1,0:T(8,128)(2,1)S(1)}, bf16[2,32,1536]{2,1,0:T(8,128)(2,1)S(1)}, f32[3,4,1536]{2,1,0:T(4,128)S(1)}, bf16[2,32,256]{2,1,0:T(...) custom-call(s32[2]{0:T(128)} %ids.1, s32[1]{0:T(128)S(6)} %copy.8.slab, ...), custom_call_target="tpu_custom_call" | custom-call | bytes 4718592 | tf_op jit(solution)/shard_map/pallas_call | solution.py:230
  8.4 0.0 collective-permute-done.1
  8.4 0.0 collective-permute-done.refs_1_
  8.5 1.2 %shard_map.74 = (bf16[2,32,256]{2,1,0:T(8,128)(2,1)S(1)}, bf16[4,32,256]{2,1,0:T(8,128)(2,1)S(1)}, bf16[2,32,256]{2,1,0:T(8,128)(2,1)S(1)}) custom-call(s32[1]{0:T(128)} %bitcast.3.head, s32[8,128]{1,0:T(8,128)S(1)} %get-tuple-element.28.ids_ref, bf16[2,32,1536]{2,1,0:T(8,128)(2,1)S(1)} %get-tuple-element.30.refs_0_, ...), custom_call_target="tpu_custom_call" | custom-call | flops 301989888 | bytes 4718592 | tf_op jit(solution)/shard_map/pallas_call | solution.py:252
  9.6 0.2 collective-permute-done.2
  9.8 0.6 %collective-permute-start.4 = (bf16[4,32,256]{2,1,0:T(8,128)(2,1)S(1)}, bf16[4,32,256]{2,1,0:T(8,128)(2,1)S(1)}, u32[]{:S(2)}, u32[]{:S(2)}) collective-permute-start(bf16[4,32,256]{2,1,0:T(8,128)(2,1)S(1)} %get-tuple-element.40), channel_id=1, source_target_pairs={{0,16},{2,18},{4,20},{6,22},{8,24},{10,26},{12,28},{14,30},{16,0},... | collective-permute-start | bytes 196616 | tf_op jit(solution)/shard_map/ppermute | solution.py:23
  10.5 3.5 %collective-permute-start.3 = (bf16[2,32,256]{2,1,0:T(8,128)(2,1)S(1)}, bf16[2,32,256]{2,1,0:T(8,128)(2,1)S(1)}, u32[]{:S(2)}, u32[]{:S(2)}) collective-permute-start(bf16[2,32,256]{2,1,0:T(8,128)(2,1)S(1)} %get-tuple-element.35.q_ref), channel_id=1, source_target_pairs={{0,8},{2,10},{4,12},{6,14},{8,0},{10,2},{12,4},{14,6},{16,24},{18,... | collective-permute-start | bytes 98312 | tf_op jit(solution)/shard_map/ppermute | solution.py:23
  13.9 2.4 %collective-permute-done.4 = bf16[4,32,256]{2,1,0:T(8,128)(2,1)S(1)} collective-permute-done((bf16[4,32,256]{2,1,0:T(8,128)(2,1)S(1)}, bf16[4,32,256]{2,1,0:T(8,128)(2,1)S(1)}, u32[]{:S(2)}, u32[]{:S(2)}) %collective-permute-start.4) | collective-permute-done | bytes 65568 | tf_op jit(solution)/shard_map/ppermute | solution.py:23
  16.4 1.6 %collective-permute-start.7 = (bf16[2,4,32,256]{3,2,1,0:T(8,128)(2,1)S(1)}, bf16[2,4,32,256]{3,2,1,0:T(8,128)(2,1)S(1)}, u32[]{:S(2)}, u32[]{:S(2)}) collective-permute-start(bf16[2,4,32,256]{3,2,1,0:T(8,128)(2,1)S(1)} %pad_maximum_fusion.7.refs_0_), channel_id=1, source_target_pairs={{0,2},{2,0},{4,6},{6,4},{8,10},{10,8},{12,14},{14,12},{16,18},{18,... | collective-permute-start | bytes 393224 | tf_op jit(solution)/shard_map/ppermute | solution.py:23
  17.9 0.0 copy-done
  17.9 0.5 %collective-permute-start.6 = (bf16[192,256]{1,0:T(8,128)(2,1)S(1)}, bf16[192,256]{1,0:T(8,128)(2,1)S(1)}, u32[]{:S(2)}, u32[]{:S(2)}) collective-permute-start(bf16[192,256]{1,0:T(8,128)(2,1)S(1)} %bitcast.27), channel_id=1, source_target_pairs={{0,2},{2,0},{4,6},{6,4},{8,10},{10,8},{12,14},{14,12},{16,18},{18,... | collective-permute-start | bytes 294920 | tf_op jit(solution)/shard_map/ppermute | solution.py:23
  18.5 0.0 collective-permute-done.3.mate_ref
  18.5 1.5 %collective-permute-start.5 = (bf16[1,192,256]{2,1,0:T(8,128)(2,1)S(1)}, bf16[1,192,256]{2,1,0:T(8,128)(2,1)S(1)}, u32[]{:S(2)}, u32[]{:S(2)}) collective-permute-start(bf16[1,192,256]{2,1,0:T(8,128)(2,1)S(1)} %bitcast.23), channel_id=1, source_target_pairs={{0,4},{2,6},{4,0},{6,2},{8,12},{10,14},{12,8},{14,10},{16,20},{18,... | collective-permute-start | bytes 294920 | tf_op jit(solution)/shard_map/ppermute | solution.py:23
  20.0 0.5 %collective-permute-start.8 = (bf16[2,4,32,256]{3,2,1,0:T(8,128)(2,1)S(1)}, bf16[2,4,32,256]{3,2,1,0:T(8,128)(2,1)S(1)}, u32[]{:S(2)}, u32[]{:S(2)}) collective-permute-start(bf16[2,4,32,256]{3,2,1,0:T(8,128)(2,1)S(1)} %pad_maximum_fusion.7.refs_0_), channel_id=1, source_target_pairs={{0,4},{2,6},{4,0},{6,2},{8,12},{10,14},{12,8},{14,10},{16,20},{18,... | collective-permute-start | bytes 393224 | tf_op jit(solution)/shard_map/ppermute | solution.py:23
  20.5 2.4 %collective-permute-start.9 = (bf16[2,4,32,256]{3,2,1,0:T(8,128)(2,1)S(1)}, bf16[2,4,32,256]{3,2,1,0:T(8,128)(2,1)S(1)}, u32[]{:S(2)}, u32[]{:S(2)}) collective-permute-start(bf16[2,4,32,256]{3,2,1,0:T(8,128)(2,1)S(1)} %pad_maximum_fusion.7.refs_0_), channel_id=1, source_target_pairs={{0,6},{2,4},{4,2},{6,0},{8,14},{10,12},{12,10},{14,8},{16,22},{18,... | collective-permute-start | bytes 393224 | tf_op jit(solution)/shard_map/ppermute | solution.py:23
  22.9 1.9 %collective-permute-done.6 = bf16[192,256]{1,0:T(8,128)(2,1)S(1)} collective-permute-done((bf16[192,256]{1,0:T(8,128)(2,1)S(1)}, bf16[192,256]{1,0:T(8,128)(2,1)S(1)}, u32[]{:S(2)}, u32[]{:S(2)}) %collective-permute-start.6) | collective-permute-done | bytes 98336 | tf_op jit(solution)/shard_map/ppermute | solution.py:23
  24.9 0.0 collective-permute-done.5
  24.9 0.0 collective-permute-done.7.refs_1_
  24.9 1.6 %collective-permute-start.12 = (bf16[2,1,192,256]{3,2,1,0:T(8,128)(2,1)S(1)}, bf16[2,1,192,256]{3,2,1,0:T(8,128)(2,1)S(1)}, u32[]{:S(2)}, u32[]{:S(2)}) collective-permute-start(bf16[2,1,192,256]{3,2,1,0:T(8,128)(2,1)S(1)} %pad_maximum_fusion.2), channel_id=1, source_target_pairs={{0,2},{2,0},{4,6},{6,4},{8,10},{10,8},{12,14},{14,12},{16,18},{18,... | collective-permute-start | bytes 589832 | tf_op jit(solution)/shard_map/ppermute | solution.py:23
  26.5 1.4 %collective-permute-start.11 = (bf16[2,192,256]{2,1,0:T(8,128)(2,1)S(1)}, bf16[2,192,256]{2,1,0:T(8,128)(2,1)S(1)}, u32[]{:S(2)}, u32[]{:S(2)}) collective-permute-start(bf16[2,192,256]{2,1,0:T(8,128)(2,1)S(1)} %get-tuple-element.58), channel_id=1, source_target_pairs={{0,4},{2,6},{4,0},{6,2},{8,12},{10,14},{12,8},{14,10},{16,20},{18,... | collective-permute-start | bytes 589832 | tf_op jit(solution)/shard_map/ppermute | solution.py:23
  27.9 0.1 collective-permute-done.8.refs_2_
  28.0 0.0 collective-permute-done.9.refs_3_
  28.0 1.1 %shard_map.75.part_ref = bf16[128,384]{1,0:T(8,128)(2,1)S(1)} custom-call(bf16[2,32,256]{2,1,0:T(8,128)(2,1)S(1)} %get-tuple-element.35.q_ref, bf16[2,32,256]{2,1,0:T(8,128)(2,1)S(1)} %collective-permute-done.3.mate_ref, bf16[2,32,256]{2,1,0:T(8,128)(2,1)S(1)} %get-tuple-element.39.kv1_ref, bf16[2,4,32,256]{3,2,1,0:T(8,128)(2,1)S(1)} %pad_maximum_fusion.7.refs_0_, ...), custom_call_target="tpu_custom_call" | custom-call | flops 33554432 | tf_op jit(solution)/shard_map/pallas_call | solution.py:272
  29.1 0.9 %collective-permute-start.10 = (bf16[128,384]{1,0:T(8,128)(2,1)S(1)}, bf16[128,384]{1,0:T(8,128)(2,1)S(1)}, u32[]{:S(2)}, u32[]{:S(2)}) collective-permute-start(bf16[128,384]{1,0:T(8,128)(2,1)S(1)} %shard_map.75.part_ref), channel_id=1, source_target_pairs={{0,8},{2,10},{4,12},{6,14},{8,0},{10,2},{12,4},{14,6},{16,24},{18,... | collective-permute-start | bytes 294920 | tf_op jit(solution)/shard_map/ppermute | solution.py:23
  30.0 3.8 %collective-permute-done.10.other_ref = bf16[128,384]{1,0:T(8,128)(2,1)S(1)} collective-permute-done((bf16[128,384]{1,0:T(8,128)(2,1)S(1)}, bf16[128,384]{1,0:T(8,128)(2,1)S(1)}, u32[]{:S(2)}, u32[]{:S(2)}) %collective-permute-start.10) | collective-permute-done | bytes 98336 | tf_op jit(solution)/shard_map/ppermute | solution.py:23
  33.7 0.2 shard_map.76.refs_0_
  34.0 0.0 collective-permute-done.12
  34.0 0.0 collective-permute-done.11
  34.1 0.1 pad_maximum_fusion.3
  34.1 0.4 shard_map.78
  34.5 0.1 collective-permute-start.13
  34.6 0.4 %shard_map.77.refs_0_ = f32[128,768]{1,0:T(8,128)S(1)} custom-call(s32[1]{0:T(128)} %bitcast.patch, s32[1]{0:T(128)} %bitcast.3.head, bf16[128,256]{1,0:T(8,128)(2,1)S(1)} %shard_map.76.refs_0_, bf16[2,192,256]{2,1,0:T(8,128)(2,1)S(1)} %get-tuple-element.57.refs_1_, bf16[2,192,256]{2,1,0:T(8,128)(2,1)S(1)} %get-tuple-element.59.refs_2_, ...), custom_call_target="tpu_custom_call" | custom-call | flops 50331648 | bytes 393216 | tf_op jit(solution)/shard_map/pallas_call | solution.py:285
  35.0 1.0 %collective-permute-done.13.refs_1_ = bf16[128,768]{1,0:T(8,128)(2,1)S(1)} collective-permute-done((bf16[128,768]{1,0:T(8,128)(2,1)S(1)}, bf16[128,768]{1,0:T(8,128)(2,1)S(1)}, u32[]{:S(2)}, u32[]{:S(2)}) %collective-permute-start.13) | collective-permute-done | bytes 196640 | tf_op jit(solution)/shard_map/ppermute | solution.py:23
  36.0 0.1 shard_map.79
  36.2 0.9 %collective-permute-start.14 = (bf16[2,32,768]{2,1,0:T(8,128)(2,1)S(1)}, bf16[2,32,768]{2,1,0:T(8,128)(2,1)S(1)}, u32[]{:S(2)}, u32[]{:S(2)}) collective-permute-start(bf16[2,32,768]{2,1,0:T(8,128)(2,1)S(1)} %get-tuple-element.49), channel_id=1, source_target_pairs={{0,8},{2,10},{4,12},{6,14},{8,0},{10,2},{12,4},{14,6},{16,24},{18,... | collective-permute-start | bytes 294920 | tf_op jit(solution)/shard_map/ppermute | solution.py:23
  37.1 4.0 %collective-permute-done.14 = bf16[2,32,768]{2,1,0:T(8,128)(2,1)S(1)} collective-permute-done((bf16[2,32,768]{2,1,0:T(8,128)(2,1)S(1)}, bf16[2,32,768]{2,1,0:T(8,128)(2,1)S(1)}, u32[]{:S(2)}, u32[]{:S(2)}) %collective-permute-start.14) | collective-permute-done | bytes 98336 | tf_op jit(solution)/shard_map/ppermute | solution.py:23
  41.1 0.7 %pad_maximum_fusion.6 = bf16[2,32,1536]{2,1,0:T(8,128)(2,1)} fusion(bf16[2,32,768]{2,1,0:T(8,128)(2,1)S(1)} %get-tuple-element.52, bf16[2,32,768]{2,1,0:T(8,128)(2,1)S(1)} %get-tuple-element.51), kind=kLoop, calls=%fused_computation.6 | loop fusion | flops 393216 | bytes 393216 | tf_op jit(solution)/shard_map/concatenate | solution.py:304
  (7 shorter events, 0.1 us)
Async XLA Ops:
  0.0 8.4 %collective-permute-start = (bf16[2,32,1536]{2,1,0:T(8,128)(2,1)}, bf16[2,32,1536]{2,1,0:T(8,128)(2,1)S(1)}, u32[]{:S(2)}, u32[]{:S(2)}) collective-permute-start(bf16[2,32,1536]{2,1,0:T(8,128)(2,1)} %x_ref.1), channel_id=1, source_target_pairs={{0,1},{1,0},{2,3},{3,2},{4,5},{5,4},{6,7},{7,6},{8,9},{9,8},{10,11... | collective-permute-start | bytes 589832 | tf_op jit(solution)/shard_map/ppermute | solution.py:23
  0.5 8.0 %collective-permute-start.1 = (f32[4,3,1536]{2,0,1:T(4,128)}, f32[4,3,1536]{2,0,1:T(4,128)S(1)}, u32[]{:S(2)}, u32[]{:S(2)}) collective-permute-start(f32[4,3,1536]{2,0,1:T(4,128)} %param.11), channel_id=1, source_target_pairs={{0,1},{1,0},{2,3},{3,2},{4,5},{5,4},{6,7},{7,6},{8,9},{9,8},{10,11... | collective-permute-start | bytes 221192 | tf_op jit(solution)/shard_map/ppermute | solution.py:23
  0.5 9.3 %collective-permute-start.2 = (bf16[192,256]{1,0:T(8,128)(2,1)}, bf16[192,256]{1,0:T(8,128)(2,1)S(1)}, u32[]{:S(2)}, u32[]{:S(2)}) collective-permute-start(bf16[192,256]{1,0:T(8,128)(2,1)} %bitcast.26), channel_id=1, source_target_pairs={{0,16},{2,18},{4,20},{6,22},{8,24},{10,26},{12,28},{14,30},{16,0},... | collective-permute-start | bytes 294920 | tf_op jit(solution)/shard_map/ppermute | solution.py:23
  5.2 12.7 %copy-start = (bf16[256,192]{0,1:T(8,128)(2,1)S(1)}, bf16[256,192]{0,1:T(8,128)(2,1)}, u32[]{:S(2)}) copy-start(bf16[256,192]{0,1:T(8,128)(2,1)} %param.10) | copy-start | bytes 294916
  9.8 6.5 %collective-permute-start.4 = (bf16[4,32,256]{2,1,0:T(8,128)(2,1)S(1)}, bf16[4,32,256]{2,1,0:T(8,128)(2,1)S(1)}, u32[]{:S(2)}, u32[]{:S(2)}) collective-permute-start(bf16[4,32,256]{2,1,0:T(8,128)(2,1)S(1)} %get-tuple-element.40), channel_id=1, source_target_pairs={{0,16},{2,18},{4,20},{6,22},{8,24},{10,26},{12,28},{14,30},{16,0},... | collective-permute-start | bytes 196616 | tf_op jit(solution)/shard_map/ppermute | solution.py:23
  10.5 8.0 %collective-permute-start.3 = (bf16[2,32,256]{2,1,0:T(8,128)(2,1)S(1)}, bf16[2,32,256]{2,1,0:T(8,128)(2,1)S(1)}, u32[]{:S(2)}, u32[]{:S(2)}) collective-permute-start(bf16[2,32,256]{2,1,0:T(8,128)(2,1)S(1)} %get-tuple-element.35.q_ref), channel_id=1, source_target_pairs={{0,8},{2,10},{4,12},{6,14},{8,0},{10,2},{12,4},{14,6},{16,24},{18,... | collective-permute-start | bytes 98312 | tf_op jit(solution)/shard_map/ppermute | solution.py:23
  16.4 8.5 %collective-permute-start.7 = (bf16[2,4,32,256]{3,2,1,0:T(8,128)(2,1)S(1)}, bf16[2,4,32,256]{3,2,1,0:T(8,128)(2,1)S(1)}, u32[]{:S(2)}, u32[]{:S(2)}) collective-permute-start(bf16[2,4,32,256]{3,2,1,0:T(8,128)(2,1)S(1)} %pad_maximum_fusion.7.refs_0_), channel_id=1, source_target_pairs={{0,2},{2,0},{4,6},{6,4},{8,10},{10,8},{12,14},{14,12},{16,18},{18,... | collective-permute-start | bytes 393224 | tf_op jit(solution)/shard_map/ppermute | solution.py:23
  17.9 6.9 %collective-permute-start.6 = (bf16[192,256]{1,0:T(8,128)(2,1)S(1)}, bf16[192,256]{1,0:T(8,128)(2,1)S(1)}, u32[]{:S(2)}, u32[]{:S(2)}) collective-permute-start(bf16[192,256]{1,0:T(8,128)(2,1)S(1)} %bitcast.27), channel_id=1, source_target_pairs={{0,2},{2,0},{4,6},{6,4},{8,10},{10,8},{12,14},{14,12},{16,18},{18,... | collective-permute-start | bytes 294920 | tf_op jit(solution)/shard_map/ppermute | solution.py:23
  18.5 6.4 %collective-permute-start.5 = (bf16[1,192,256]{2,1,0:T(8,128)(2,1)S(1)}, bf16[1,192,256]{2,1,0:T(8,128)(2,1)S(1)}, u32[]{:S(2)}, u32[]{:S(2)}) collective-permute-start(bf16[1,192,256]{2,1,0:T(8,128)(2,1)S(1)} %bitcast.23), channel_id=1, source_target_pairs={{0,4},{2,6},{4,0},{6,2},{8,12},{10,14},{12,8},{14,10},{16,20},{18,... | collective-permute-start | bytes 294920 | tf_op jit(solution)/shard_map/ppermute | solution.py:23
  20.0 8.0 %collective-permute-start.8 = (bf16[2,4,32,256]{3,2,1,0:T(8,128)(2,1)S(1)}, bf16[2,4,32,256]{3,2,1,0:T(8,128)(2,1)S(1)}, u32[]{:S(2)}, u32[]{:S(2)}) collective-permute-start(bf16[2,4,32,256]{3,2,1,0:T(8,128)(2,1)S(1)} %pad_maximum_fusion.7.refs_0_), channel_id=1, source_target_pairs={{0,4},{2,6},{4,0},{6,2},{8,12},{10,14},{12,8},{14,10},{16,20},{18,... | collective-permute-start | bytes 393224 | tf_op jit(solution)/shard_map/ppermute | solution.py:23
  20.5 7.5 %collective-permute-start.9 = (bf16[2,4,32,256]{3,2,1,0:T(8,128)(2,1)S(1)}, bf16[2,4,32,256]{3,2,1,0:T(8,128)(2,1)S(1)}, u32[]{:S(2)}, u32[]{:S(2)}) collective-permute-start(bf16[2,4,32,256]{3,2,1,0:T(8,128)(2,1)S(1)} %pad_maximum_fusion.7.refs_0_), channel_id=1, source_target_pairs={{0,6},{2,4},{4,2},{6,0},{8,14},{10,12},{12,10},{14,8},{16,22},{18,... | collective-permute-start | bytes 393224 | tf_op jit(solution)/shard_map/ppermute | solution.py:23
  24.9 9.1 %collective-permute-start.12 = (bf16[2,1,192,256]{3,2,1,0:T(8,128)(2,1)S(1)}, bf16[2,1,192,256]{3,2,1,0:T(8,128)(2,1)S(1)}, u32[]{:S(2)}, u32[]{:S(2)}) collective-permute-start(bf16[2,1,192,256]{3,2,1,0:T(8,128)(2,1)S(1)} %pad_maximum_fusion.2), channel_id=1, source_target_pairs={{0,2},{2,0},{4,6},{6,4},{8,10},{10,8},{12,14},{14,12},{16,18},{18,... | collective-permute-start | bytes 589832 | tf_op jit(solution)/shard_map/ppermute | solution.py:23
  26.5 7.5 %collective-permute-start.11 = (bf16[2,192,256]{2,1,0:T(8,128)(2,1)S(1)}, bf16[2,192,256]{2,1,0:T(8,128)(2,1)S(1)}, u32[]{:S(2)}, u32[]{:S(2)}) collective-permute-start(bf16[2,192,256]{2,1,0:T(8,128)(2,1)S(1)} %get-tuple-element.58), channel_id=1, source_target_pairs={{0,4},{2,6},{4,0},{6,2},{8,12},{10,14},{12,8},{14,10},{16,20},{18,... | collective-permute-start | bytes 589832 | tf_op jit(solution)/shard_map/ppermute | solution.py:23
  29.1 4.7 %collective-permute-start.10 = (bf16[128,384]{1,0:T(8,128)(2,1)S(1)}, bf16[128,384]{1,0:T(8,128)(2,1)S(1)}, u32[]{:S(2)}, u32[]{:S(2)}) collective-permute-start(bf16[128,384]{1,0:T(8,128)(2,1)S(1)} %shard_map.75.part_ref), channel_id=1, source_target_pairs={{0,8},{2,10},{4,12},{6,14},{8,0},{10,2},{12,4},{14,6},{16,24},{18,... | collective-permute-start | bytes 294920 | tf_op jit(solution)/shard_map/ppermute | solution.py:23
  34.5 1.5 %collective-permute-start.13 = (bf16[128,768]{1,0:T(8,128)(2,1)S(1)}, bf16[128,768]{1,0:T(8,128)(2,1)S(1)}, u32[]{:S(2)}, u32[]{:S(2)}) collective-permute-start(bf16[128,768]{1,0:T(8,128)(2,1)S(1)} %shard_map.78), channel_id=1, source_target_pairs={{0,1},{1,0},{2,3},{3,2},{4,5},{5,4},{6,7},{7,6},{8,9},{9,8},{10,11... | collective-permute-start | bytes 589832 | tf_op jit(solution)/shard_map/ppermute | solution.py:23
  36.2 4.9 %collective-permute-start.14 = (bf16[2,32,768]{2,1,0:T(8,128)(2,1)S(1)}, bf16[2,32,768]{2,1,0:T(8,128)(2,1)S(1)}, u32[]{:S(2)}, u32[]{:S(2)}) collective-permute-start(bf16[2,32,768]{2,1,0:T(8,128)(2,1)S(1)} %get-tuple-element.49), channel_id=1, source_target_pairs={{0,8},{2,10},{4,12},{6,14},{8,0},{10,2},{12,4},{14,6},{16,24},{18,... | collective-permute-start | bytes 294920 | tf_op jit(solution)/shard_map/ppermute | solution.py:23

commit v13 on v12

--- a/solution.py
+++ b/solution.py
@@ -117,7 +117,8 @@
 
 
 def attend_kernel(q_ref, mate_ref, kv1_ref, *refs):
-    kv_refs, out_ref = refs[:PLANE], refs[PLANE]
+    own_ref, next_ref, far_ref, out_ref = refs
+    kv_refs = [own_ref, next_ref, far_ref.at[0], far_ref.at[1]]
     blocks, _, rows, cols = kv_refs[0].shape
     old_rows = PLANE * blocks * rows
     shape = (2 * rows, old_rows + rows)
@@ -176,11 +177,13 @@
 
 
 def project_kernel(n_head, n_patch, bit, patch, head, *refs):
-    o_ref, w_refs, (out_ref, sums) = refs[0], refs[1 : 1 + PLANE], refs[1 + PLANE :]
+    o_ref, own_ref, next_ref, far_ref, out_ref, sums = refs
     slot = head[0] ^ bit ^ (patch[0] // (n_patch // n_head))
-    for near in range(PLANE):
+    odd = head[0] % 2
+    blocks = ((0, own_ref), (1 + odd, next_ref), (2 - odd, far_ref.at[0]), (3, far_ref.at[1]))
+    for near, w_ref in blocks:
         sums[(patch[0] % PLANE) ^ near] = lax.dot_general(
-            o_ref[...], w_refs[near][slot], NT, preferred_element_type=F32
+            o_ref[...], w_ref[slot], NT, preferred_element_type=F32
         )
     out = jnp.concatenate([sums[c] for c in range(PLANE)], axis=1)
     out_ref[...] = out.astype(out_ref.dtype)
@@ -244,8 +247,13 @@
     def line_of(values):
         return [values] + [across(values, k) for k in range(2 * PLANE, n_patch, 2 * PLANE)]
 
-    def plane_of(values):
-        return [values] + [across(values, k) for k in range(1, PLANE)]
+    def turn(values, first):
+        pairs = [
+            (p * n_head + h, (p ^ (1 if (h % 2 == 0) == first else 2)) * n_head + h)
+            for p in range(n_patch)
+            for h in range(n_head)
+        ]
+        return lax.ppermute(values, ("patch", "head"), pairs)
 
 
     kv_shape = shaped((2, rows, cols), BF16)
@@ -257,39 +265,33 @@
         size=2 * w_qkv.size,
     )(head[None], ids, *x_parts, *mod_parts, w, cos, sin, stale)
 
-    w_own, w_rest, kv = lax.optimization_barrier((w_out.T, line_of(w_out.T)[1:], kv))
-    w_rest = jnp.stack(w_rest)
-    kv_pair = line_of(kv)
+    w_pair, kv = lax.optimization_barrier((line_of(w_out.T), kv))
+    w_pair = jnp.stack(w_pair)
+    kv_pair = jnp.stack(line_of(kv))
     q_mate = across(q, PLANE)
-    w_x = across(w_own, 1)
-    kv_plane = plane_of(jnp.stack(kv_pair))
-    w_rest, q_mate = lax.optimization_barrier((w_rest, q_mate))
-    rest_y = across(w_rest, 2)
-    rest_y, w_x, kv_plane[1] = lax.optimization_barrier((rest_y, w_x, kv_plane[1]))
-    w_y = across(jnp.stack([w_own, w_x]), 2)
-    rest_x = across(jnp.stack([w_rest, rest_y]), 1)
+    w_next = turn(w_pair, True)
+    kv_next = turn(kv_pair, True)
+    kv_far = turn(jnp.stack([kv_pair, kv_next]), False)
+    w_far = turn(jnp.stack([w_pair, w_next]), False)
     tall = 2 * STEPS * rows
     part = call(
         attend_kernel,
         shaped((tall, cols + DH), BF16),
-        [VMEM] * (3 + PLANE),
+        [VMEM] * 6,
         flops=4 * STEPS * rows * n_patch * rows * cols,
-    )(q, q_mate, kv1, *kv_plane)
+    )(q, q_mate, kv1, kv_pair, kv_next, kv_far)
     o = call(merge_kernel, shaped((tall, cols), BF16), [VMEM] * 2)(part, across(part, PLANE))
-    o, w_y, rest_x = lax.optimization_barrier((o, w_y, rest_x))
-    near = [(w_own, w_rest), (w_x, rest_x[0]), (w_y[0], rest_y), (w_y[1], rest_x[1])]
-    w_plane = [jnp.concatenate([first[None], others]) for first, others in near]
     wide = PLANE * piece
 
     def project(bit, dtype):
         return call(
             functools.partial(project_kernel, n_head, n_patch, bit),
             shaped((tall, wide), dtype),
-            [SMEM] * 2 + [VMEM] * (1 + PLANE),
+            [SMEM] * 2 + [VMEM] * 4,
             [pltpu.VMEM((PLANE, tall, piece), F32)],
             2 * tall * wide * cols,
             2 * wide * cols,
-        )(patch[None], head[None], o, *w_plane)
+        )(patch[None], head[None], o, w_pair, w_next, w_far)
 
     sums = [swap(project(k, BF16), "head", n_head, k) for k in range(1, n_head)]
     sums = [project(0, F32)] + sums

time: 41.9 us -> 44.5 us (1.062)
  waiting for transfers between devices: 13.4 us -> 24.6 us
  starting transfers between devices: 20 us -> 11.5 us
    ppermute x15 -> x8, starting transfers between devices: 20 us -> 7.24 us  [swap(): return lax.ppermute(values, axis, [(i, i ^ bit) for i in range(count)])]
    ppermute x0 -> x4, waiting for transfers between devices: none -> 6.32 us  [turn(): return lax.ppermute(values, ('patch', 'head'), pairs)]
    ppermute x15 -> x8, waiting for transfers between devices: 13.4 us -> 18.3 us  [swap(): return lax.ppermute(values, axis, [(i, i ^ bit) for i in range(count)])]
    ppermute x0 -> x4, starting transfers between devices: none -> 4.25 us  [turn(): return lax.ppermute(values, ('patch', 'head'), pairs)]
  transfers between devices with their start and end apart: 15 -> 12, of which waited for: 7 -> 8; matrix products, arithmetic and copies ran while one was open for 0% -> 0% of each run, Pallas kernels for 15% -> 14%
where the time goes in v13:
time: 44.5 us; the launch traced here: 44.3 us
  waiting for transfers between devices  24.6 us (55%)
  starting transfers between devices  11.5 us (26%)
  Pallas kernels  6.63 us (15%)
  other arithmetic  0.82 us (2%)
  between operations  0.78 us (2%)
    ppermute x8, waiting for transfers between devices, swap(): return lax.ppermute(values, axis, [(i, i ^ bit) for i in range(count)])  18.3 us
    ppermute x8, starting transfers between devices, swap(): return lax.ppermute(values, axis, [(i, i ^ bit) for i in range(count)])  7.24 us
    ppermute x4, waiting for transfers between devices, turn(): return lax.ppermute(values, ('patch', 'head'), pairs)  6.32 us
    ppermute x4, starting transfers between devices, turn(): return lax.ppermute(values, ('patch', 'head'), pairs)  4.25 us
    pallas_call x1, Pallas kernels, body(): call(load_kernel, tuple((pltpu.VMEM(v.shape, v.dtype) for v in first)) +...  3.21 us
    pallas_call x1, Pallas kernels, body(): call(functools.partial(qkv_kernel, n_head), (kv_shape, shaped((4, rows, c...  1.16 us
    pallas_call x1, Pallas kernels, body(): call(attend_kernel, shaped((tall, cols + DH), BF16), [VMEM] * 6, flops=4...  1.11 us
  transfers between devices with their start and end apart: 12, of which 8 were waited for; matrix products, arithmetic and copies ran while one was open for 0% of the time, Pallas kernels for 14%

profile of v13, /device:TPU:0, one launch (start us, length us, event | category | flops | bytes accessed | tf_op | source)
XLA Modules:
  0.0 44.3 jit_solution(17222017590327119091)
XLA Ops:
  0.0 0.5 %collective-permute-start = (bf16[2,32,1536]{2,1,0:T(8,128)(2,1)}, bf16[2,32,1536]{2,1,0:T(8,128)(2,1)S(1)}, u32[]{:S(2)}, u32[]{:S(2)}) collective-permute-start(bf16[2,32,1536]{2,1,0:T(8,128)(2,1)} %x_ref.1), channel_id=1, source_target_pairs={{0,1},{1,0},{2,3},{3,2},{4,5},{5,4},{6,7},{7,6},{8,9},{9,8},{10,11... | collective-permute-start | bytes 589832 | tf_op jit(solution)/shard_map/ppermute | solution.py:23
  0.5 0.1 collective-permute-start.1
  0.5 4.0 %collective-permute-start.3 = (bf16[192,256]{1,0:T(8,128)(2,1)}, bf16[192,256]{1,0:T(8,128)(2,1)S(1)}, u32[]{:S(2)}, u32[]{:S(2)}) collective-permute-start(bf16[192,256]{1,0:T(8,128)(2,1)} %bitcast.21), channel_id=1, source_target_pairs={{0,16},{2,18},{4,20},{6,22},{8,24},{10,26},{12,28},{14,30},{16,0},... | collective-permute-start | bytes 294920 | tf_op jit(solution)/shard_map/ppermute | solution.py:23
  5.2 0.0 copy-start
  5.2 3.2 %shard_map.73 = (bf16[3,3072,256]{2,1,0:T(8,128)(2,1)S(1)}, bf16[2,32,1536]{2,1,0:T(8,128)(2,1)S(1)}, f32[3,4,1536]{2,1,0:T(4,128)S(1)}, bf16[2,32,256]{2,1,0:T(...) custom-call(s32[2]{0:T(128)} %ids.1, s32[1]{0:T(128)S(6)} %copy.8.slab, ...), custom_call_target="tpu_custom_call" | custom-call | bytes 4718592 | tf_op jit(solution)/shard_map/pallas_call | solution.py:233
  8.4 0.0 collective-permute-done.1
  8.4 0.0 collective-permute-done.refs_1_
  8.5 1.2 %shard_map.74 = (bf16[2,32,256]{2,1,0:T(8,128)(2,1)S(1)}, bf16[4,32,256]{2,1,0:T(8,128)(2,1)S(1)}, bf16[2,32,256]{2,1,0:T(8,128)(2,1)S(1)}) custom-call(s32[1]{0:T(128)} %bitcast.3.head, s32[8,128]{1,0:T(8,128)S(1)} %get-tuple-element.20.ids_ref, bf16[2,32,1536]{2,1,0:T(8,128)(2,1)S(1)} %get-tuple-element.22.refs_0_, ...), custom_call_target="tpu_custom_call" | custom-call | flops 301989888 | bytes 4718592 | tf_op jit(solution)/shard_map/pallas_call | solution.py:260
  9.6 0.2 collective-permute-done.3
  9.8 0.0 copy-done
  9.9 1.6 %collective-permute-start.8 = (bf16[2,192,256]{2,1,0:T(8,128)(2,1)S(1)}, bf16[2,192,256]{2,1,0:T(8,128)(2,1)S(1)}, u32[]{:S(2)}, u32[]{:S(2)}) collective-permute-start(bf16[2,192,256]{2,1,0:T(8,128)(2,1)S(1)} %get-tuple-element.38.refs_1_), channel_id=1, source_target_pairs={{0,2},{1,5},{2,0},{3,7},{4,6},{5,1},{6,4},{7,3},{8,10},{9,13},{10,... | collective-permute-start | bytes 589832 | tf_op jit(solution)/shard_map/ppermute | solution.py:256
  11.5 0.6 %collective-permute-start.4 = (bf16[4,32,256]{2,1,0:T(8,128)(2,1)S(1)}, bf16[4,32,256]{2,1,0:T(8,128)(2,1)S(1)}, u32[]{:S(2)}, u32[]{:S(2)}) collective-permute-start(bf16[4,32,256]{2,1,0:T(8,128)(2,1)S(1)} %get-tuple-element.30), channel_id=1, source_target_pairs={{0,16},{2,18},{4,20},{6,22},{8,24},{10,26},{12,28},{14,30},{16,0},... | collective-permute-start | bytes 196616 | tf_op jit(solution)/shard_map/ppermute | solution.py:23
  12.1 5.6 %collective-permute-done.4 = bf16[4,32,256]{2,1,0:T(8,128)(2,1)S(1)} collective-permute-done((bf16[4,32,256]{2,1,0:T(8,128)(2,1)S(1)}, bf16[4,32,256]{2,1,0:T(8,128)(2,1)S(1)}, u32[]{:S(2)}, u32[]{:S(2)}) %collective-permute-start.4) | collective-permute-done | bytes 65568 | tf_op jit(solution)/shard_map/ppermute | solution.py:23
  17.7 0.1 collective-permute-start.5
  17.8 0.0 collective-permute-done.8.refs_2_
  17.8 2.0 %collective-permute-start.9 = (bf16[2,2,192,256]{3,2,1,0:T(8,128)(2,1)S(1)}, bf16[2,2,192,256]{3,2,1,0:T(8,128)(2,1)S(1)}, u32[]{:S(2)}, u32[]{:S(2)}) collective-permute-start(bf16[2,2,192,256]{3,2,1,0:T(8,128)(2,1)S(1)} %pad_maximum_fusion), channel_id=1, source_target_pairs={{0,4},{1,3},{2,6},{3,1},{4,0},{5,7},{6,2},{7,5},{8,12},{9,11},{10,... | collective-permute-start | bytes 1179656 | tf_op jit(solution)/shard_map/ppermute | solution.py:256
  19.9 4.3 %collective-permute-done.5.refs_1_ = bf16[2,4,32,256]{3,2,1,0:T(8,128)(2,1)S(1)} collective-permute-done((bf16[2,4,32,256]{3,2,1,0:T(8,128)(2,1)S(1)}, bf16[2,4,32,256]{3,2,1,0:T(8,128)(2,1)S(1)}, u32[]{:S(2)}, u32[]{:S(2)}) %collective-permute-start.5) | collective-permute-done | bytes 131104 | tf_op jit(solution)/shard_map/ppermute | solution.py:256
  24.2 0.5 %collective-permute-start.6 = (bf16[2,2,4,32,256]{4,3,2,1,0:T(8,128)(2,1)S(1)}, bf16[2,2,4,32,256]{4,3,2,1,0:T(8,128)(2,1)S(1)}, u32[]{:S(2)}, u32[]{:S(2)}) collective-permute-start(bf16[2,2,4,32,256]{4,3,2,1,0:T(8,128)(2,1)S(1)} %pad_maximum_fusion.1), channel_id=1, source_target_pairs={{0,4},{1,3},{2,6},{3,1},{4,0},{5,7},{6,2},{7,5},{8,12},{9,11},{10,... | collective-permute-start | bytes 786440 | tf_op jit(solution)/shard_map/ppermute | solution.py:256
  24.8 1.3 %collective-permute-start.2 = (bf16[2,32,256]{2,1,0:T(8,128)(2,1)S(1)}, bf16[2,32,256]{2,1,0:T(8,128)(2,1)S(1)}, u32[]{:S(2)}, u32[]{:S(2)}) collective-permute-start(bf16[2,32,256]{2,1,0:T(8,128)(2,1)S(1)} %get-tuple-element.27.q_ref), channel_id=1, source_target_pairs={{0,8},{2,10},{4,12},{6,14},{8,0},{10,2},{12,4},{14,6},{16,24},{18,... | collective-permute-start | bytes 98312 | tf_op jit(solution)/shard_map/ppermute | solution.py:23
  26.1 2.6 %collective-permute-done.2.mate_ref = bf16[2,32,256]{2,1,0:T(8,128)(2,1)S(1)} collective-permute-done((bf16[2,32,256]{2,1,0:T(8,128)(2,1)S(1)}, bf16[2,32,256]{2,1,0:T(8,128)(2,1)S(1)}, u32[]{:S(2)}, u32[]{:S(2)}) %collective-permute-start.2) | collective-permute-done | bytes 32800 | tf_op jit(solution)/shard_map/ppermute | solution.py:23
  28.7 2.0 %collective-permute-done.6.refs_2_ = bf16[2,2,4,32,256]{4,3,2,1,0:T(8,128)(2,1)S(1)} collective-permute-done((bf16[2,2,4,32,256]{4,3,2,1,0:T(8,128)(2,1)S(1)}, bf16[2,2,4,32,256]{4,3,2,1,0:T(8,128)(2,1)S(1)}, u32[]{:S(2)}, u32[]{:S(2)}) %collective-permute-start.6) | collective-permute-done | bytes 262176 | tf_op jit(solution)/shard_map/ppermute | solution.py:256
  30.7 1.1 %shard_map.75.part_ref = bf16[128,384]{1,0:T(8,128)(2,1)S(1)} custom-call(bf16[2,32,256]{2,1,0:T(8,128)(2,1)S(1)} %get-tuple-element.27.q_ref, bf16[2,32,256]{2,1,0:T(8,128)(2,1)S(1)} %collective-permute-done.2.mate_ref, bf16[2,32,256]{2,1,0:T(8,128)(2,1)S(1)} %get-tuple-element.28.kv1_ref, bf16[2,4,32,256]{3,2,1,0:T(8,128)(2,1)S(1)} %get-tuple-element.40.refs_0_, ...), custom_call_target="tpu_custom_call" | custom-call | flops 33554432 | tf_op jit(solution)/shard_map/pallas_call | solution.py:277
  31.8 0.4 collective-permute-start.7
  32.1 4.3 %collective-permute-done.7.other_ref = bf16[128,384]{1,0:T(8,128)(2,1)S(1)} collective-permute-done((bf16[128,384]{1,0:T(8,128)(2,1)S(1)}, bf16[128,384]{1,0:T(8,128)(2,1)S(1)}, u32[]{:S(2)}, u32[]{:S(2)}) %collective-permute-start.7) | collective-permute-done | bytes 98336 | tf_op jit(solution)/shard_map/ppermute | solution.py:23
  36.5 0.2 shard_map.76.refs_0_
  36.7 0.0 collective-permute-done.9.refs_3_
  36.7 0.4 shard_map.78
  37.1 0.1 collective-permute-start.10
  37.2 0.4 shard_map.77.refs_0_
  37.6 1.0 %collective-permute-done.10.refs_1_ = bf16[128,768]{1,0:T(8,128)(2,1)S(1)} collective-permute-done((bf16[128,768]{1,0:T(8,128)(2,1)S(1)}, bf16[128,768]{1,0:T(8,128)(2,1)S(1)}, u32[]{:S(2)}, u32[]{:S(2)}) %collective-permute-start.10) | collective-permute-done | bytes 196640 | tf_op jit(solution)/shard_map/ppermute | solution.py:23
  38.6 0.1 shard_map.79
  38.7 0.4 collective-permute-start.11
  39.1 4.5 %collective-permute-done.11 = bf16[2,32,768]{2,1,0:T(8,128)(2,1)S(1)} collective-permute-done((bf16[2,32,768]{2,1,0:T(8,128)(2,1)S(1)}, bf16[2,32,768]{2,1,0:T(8,128)(2,1)S(1)}, u32[]{:S(2)}, u32[]{:S(2)}) %collective-permute-start.11) | collective-permute-done | bytes 98336 | tf_op jit(solution)/shard_map/ppermute | solution.py:23
  43.7 0.7 %pad_maximum_fusion.3 = bf16[2,32,1536]{2,1,0:T(8,128)(2,1)} fusion(bf16[2,32,768]{2,1,0:T(8,128)(2,1)S(1)} %get-tuple-element.36, bf16[2,32,768]{2,1,0:T(8,128)(2,1)S(1)} %get-tuple-element.35), kind=kLoop, calls=%fused_computation.3 | loop fusion | flops 393216 | bytes 393216 | tf_op jit(solution)/shard_map/concatenate | solution.py:306
  (5 shorter events, 0.1 us)
Async XLA Ops:
  0.0 8.4 %collective-permute-start = (bf16[2,32,1536]{2,1,0:T(8,128)(2,1)}, bf16[2,32,1536]{2,1,0:T(8,128)(2,1)S(1)}, u32[]{:S(2)}, u32[]{:S(2)}) collective-permute-start(bf16[2,32,1536]{2,1,0:T(8,128)(2,1)} %x_ref.1), channel_id=1, source_target_pairs={{0,1},{1,0},{2,3},{3,2},{4,5},{5,4},{6,7},{7,6},{8,9},{9,8},{10,11... | collective-permute-start | bytes 589832 | tf_op jit(solution)/shard_map/ppermute | solution.py:23
  0.5 8.0 %collective-permute-start.1 = (f32[4,3,1536]{2,0,1:T(4,128)}, f32[4,3,1536]{2,0,1:T(4,128)S(1)}, u32[]{:S(2)}, u32[]{:S(2)}) collective-permute-start(f32[4,3,1536]{2,0,1:T(4,128)} %param.11), channel_id=1, source_target_pairs={{0,1},{1,0},{2,3},{3,2},{4,5},{5,4},{6,7},{7,6},{8,9},{9,8},{10,11... | collective-permute-start | bytes 221192 | tf_op jit(solution)/shard_map/ppermute | solution.py:23
  0.5 9.3 %collective-permute-start.3 = (bf16[192,256]{1,0:T(8,128)(2,1)}, bf16[192,256]{1,0:T(8,128)(2,1)S(1)}, u32[]{:S(2)}, u32[]{:S(2)}) collective-permute-start(bf16[192,256]{1,0:T(8,128)(2,1)} %bitcast.21), channel_id=1, source_target_pairs={{0,16},{2,18},{4,20},{6,22},{8,24},{10,26},{12,28},{14,30},{16,0},... | collective-permute-start | bytes 294920 | tf_op jit(solution)/shard_map/ppermute | solution.py:23
  5.2 4.6 %copy-start = (bf16[256,192]{0,1:T(8,128)(2,1)S(1)}, bf16[256,192]{0,1:T(8,128)(2,1)}, u32[]{:S(2)}) copy-start(bf16[256,192]{0,1:T(8,128)(2,1)} %param.10) | copy-start | bytes 294916
  9.9 7.9 %collective-permute-start.8 = (bf16[2,192,256]{2,1,0:T(8,128)(2,1)S(1)}, bf16[2,192,256]{2,1,0:T(8,128)(2,1)S(1)}, u32[]{:S(2)}, u32[]{:S(2)}) collective-permute-start(bf16[2,192,256]{2,1,0:T(8,128)(2,1)S(1)} %get-tuple-element.38.refs_1_), channel_id=1, source_target_pairs={{0,2},{1,5},{2,0},{3,7},{4,6},{5,1},{6,4},{7,3},{8,10},{9,13},{10,... | collective-permute-start | bytes 589832 | tf_op jit(solution)/shard_map/ppermute | solution.py:256
  11.5 6.2 %collective-permute-start.4 = (bf16[4,32,256]{2,1,0:T(8,128)(2,1)S(1)}, bf16[4,32,256]{2,1,0:T(8,128)(2,1)S(1)}, u32[]{:S(2)}, u32[]{:S(2)}) collective-permute-start(bf16[4,32,256]{2,1,0:T(8,128)(2,1)S(1)} %get-tuple-element.30), channel_id=1, source_target_pairs={{0,16},{2,18},{4,20},{6,22},{8,24},{10,26},{12,28},{14,30},{16,0},... | collective-permute-start | bytes 196616 | tf_op jit(solution)/shard_map/ppermute | solution.py:23
  17.7 6.5 %collective-permute-start.5 = (bf16[2,4,32,256]{3,2,1,0:T(8,128)(2,1)S(1)}, bf16[2,4,32,256]{3,2,1,0:T(8,128)(2,1)S(1)}, u32[]{:S(2)}, u32[]{:S(2)}) collective-permute-start(bf16[2,4,32,256]{3,2,1,0:T(8,128)(2,1)S(1)} %get-tuple-element.40.refs_0_), channel_id=1, source_target_pairs={{0,2},{1,5},{2,0},{3,7},{4,6},{5,1},{6,4},{7,3},{8,10},{9,13},{10,... | collective-permute-start | bytes 393224 | tf_op jit(solution)/shard_map/ppermute | solution.py:256
  17.8 18.8 %collective-permute-start.9 = (bf16[2,2,192,256]{3,2,1,0:T(8,128)(2,1)S(1)}, bf16[2,2,192,256]{3,2,1,0:T(8,128)(2,1)S(1)}, u32[]{:S(2)}, u32[]{:S(2)}) collective-permute-start(bf16[2,2,192,256]{3,2,1,0:T(8,128)(2,1)S(1)} %pad_maximum_fusion), channel_id=1, source_target_pairs={{0,4},{1,3},{2,6},{3,1},{4,0},{5,7},{6,2},{7,5},{8,12},{9,11},{10,... | collective-permute-start | bytes 1179656 | tf_op jit(solution)/shard_map/ppermute | solution.py:256
  24.2 6.4 %collective-permute-start.6 = (bf16[2,2,4,32,256]{4,3,2,1,0:T(8,128)(2,1)S(1)}, bf16[2,2,4,32,256]{4,3,2,1,0:T(8,128)(2,1)S(1)}, u32[]{:S(2)}, u32[]{:S(2)}) collective-permute-start(bf16[2,2,4,32,256]{4,3,2,1,0:T(8,128)(2,1)S(1)} %pad_maximum_fusion.1), channel_id=1, source_target_pairs={{0,4},{1,3},{2,6},{3,1},{4,0},{5,7},{6,2},{7,5},{8,12},{9,11},{10,... | collective-permute-start | bytes 786440 | tf_op jit(solution)/shard_map/ppermute | solution.py:256
  24.8 3.9 %collective-permute-start.2 = (bf16[2,32,256]{2,1,0:T(8,128)(2,1)S(1)}, bf16[2,32,256]{2,1,0:T(8,128)(2,1)S(1)}, u32[]{:S(2)}, u32[]{:S(2)}) collective-permute-start(bf16[2,32,256]{2,1,0:T(8,128)(2,1)S(1)} %get-tuple-element.27.q_ref), channel_id=1, source_target_pairs={{0,8},{2,10},{4,12},{6,14},{8,0},{10,2},{12,4},{14,6},{16,24},{18,... | collective-permute-start | bytes 98312 | tf_op jit(solution)/shard_map/ppermute | solution.py:23
  31.8 4.7 %collective-permute-start.7 = (bf16[128,384]{1,0:T(8,128)(2,1)S(1)}, bf16[128,384]{1,0:T(8,128)(2,1)S(1)}, u32[]{:S(2)}, u32[]{:S(2)}) collective-permute-start(bf16[128,384]{1,0:T(8,128)(2,1)S(1)} %shard_map.75.part_ref), channel_id=1, source_target_pairs={{0,8},{2,10},{4,12},{6,14},{8,0},{10,2},{12,4},{14,6},{16,24},{18,... | collective-permute-start | bytes 294920 | tf_op jit(solution)/shard_map/ppermute | solution.py:23
  37.1 1.5 %collective-permute-start.10 = (bf16[128,768]{1,0:T(8,128)(2,1)S(1)}, bf16[128,768]{1,0:T(8,128)(2,1)S(1)}, u32[]{:S(2)}, u32[]{:S(2)}) collective-permute-start(bf16[128,768]{1,0:T(8,128)(2,1)S(1)} %shard_map.78), channel_id=1, source_target_pairs={{0,1},{1,0},{2,3},{3,2},{4,5},{5,4},{6,7},{7,6},{8,9},{9,8},{10,11... | collective-permute-start | bytes 589832 | tf_op jit(solution)/shard_map/ppermute | solution.py:23
  38.7 4.9 %collective-permute-start.11 = (bf16[2,32,768]{2,1,0:T(8,128)(2,1)S(1)}, bf16[2,32,768]{2,1,0:T(8,128)(2,1)S(1)}, u32[]{:S(2)}, u32[]{:S(2)}) collective-permute-start(bf16[2,32,768]{2,1,0:T(8,128)(2,1)S(1)} %get-tuple-element.33), channel_id=1, source_target_pairs={{0,8},{2,10},{4,12},{6,14},{8,0},{10,2},{12,4},{14,6},{16,24},{18,... | collective-permute-start | bytes 294920 | tf_op jit(solution)/shard_map/ppermute | solution.py:23

commit v14 on v13

--- a/solution.py
+++ b/solution.py
@@ -23,7 +23,7 @@
     return lax.ppermute(values, axis, [(i, i ^ bit) for i in range(count)])
 
 
-def load_kernel(ids, slab, w_ref, x_ref, mod_ref, stale_ref, w_out, x_out, mod_out, stale_out, *refs):
+def load_kernel(ids, slab, w_ref, x_ref, mod_ref, w_out, x_out, mod_out, *refs):
     ids_out, cos_ref, sin_ref, sems = refs
     copies = [
         pltpu.make_async_copy(w_ref.at[slot], w_out.at[slot], sems.at[slot])
@@ -31,7 +31,6 @@
     ]
     copies.append(pltpu.make_async_copy(x_ref, x_out, sems.at[3]))
     copies.append(pltpu.make_async_copy(mod_ref, mod_out, sems.at[4]))
-    copies.append(pltpu.make_async_copy(stale_ref, stale_out, sems.at[5]))
     for copy in copies:
         copy.start()
     row = lax.broadcasted_iota(jnp.int32, ids_out.shape, 0)
@@ -93,7 +92,8 @@
 
 def qkv_kernel(n_head, head, ids_ref, *refs):
     x_refs, mod_refs = refs[:n_head], refs[n_head : 2 * n_head]
-    w_ref, cos_ref, sin_ref, stale_ref, q_ref, kv_ref, kv1_ref = refs[2 * n_head :]
+    w_ref, cos_ref, sin_ref = refs[2 * n_head : 2 * n_head + 3]
+    q_ref, kv0_ref, kv1_ref = refs[-3:]
     rows = x_refs[0].shape[1]
     steps = [normalized(step, x_refs, mod_refs, ids_ref) for step in range(STEPS)]
     parts = [jnp.concatenate(pair, axis=0) for pair in zip(*steps)]
@@ -105,8 +105,7 @@
     for step in range(STEPS):
         spot = slice(step * rows, (step + 1) * rows)
         q_ref[step] = queries[spot]
-    kv_ref[:2] = stale_ref[...]
-    kv_ref[2], kv_ref[3] = keys[:rows], values[:rows]
+    kv0_ref[0], kv0_ref[1] = keys[:rows], values[:rows]
     kv1_ref[0], kv1_ref[1] = keys[rows:], values[rows:]
 
 
@@ -229,13 +228,13 @@
 
     x_parts = [swap(inputs, "head", n_head, k) for k in range(1, n_head)]
     mod_parts = [swap(mod_table, "head", n_head, k) for k in range(1, n_head)]
-    first = (jnp.transpose(w_qkv, (1, 0, 2)), inputs, jnp.transpose(mod_table, (1, 0, 2)), stale_kv)
-    w, x_own, mod_own, stale, ids, cos, sin = call(
+    first = (jnp.transpose(w_qkv, (1, 0, 2)), inputs, jnp.transpose(mod_table, (1, 0, 2)))
+    w, x_own, mod_own, ids, cos, sin = call(
         load_kernel,
         tuple(pltpu.VMEM(v.shape, v.dtype) for v in first)
         + (shaped((8, DH), jnp.int32), shaped((rows, DH), F32), shaped((rows, DH), F32)),
         [SMEM] * 2 + [ANY] * len(first),
-        [pltpu.SemaphoreType.DMA((6,))],
+        [pltpu.SemaphoreType.DMA((5,))],
         size=2 * w_qkv.size,
     )(in_hbm(step_ids), slab_order, *map(in_hbm, first))
     x_parts = [x_own] + x_parts
@@ -256,22 +255,26 @@
         return lax.ppermute(values, ("patch", "head"), pairs)
 
 
+    stale_pair = line_of(stale_kv)
     kv_shape = shaped((2, rows, cols), BF16)
     q, kv, kv1 = call(
         functools.partial(qkv_kernel, n_head),
-        (kv_shape, shaped((4, rows, cols), BF16), kv_shape),
-        [SMEM] + [VMEM] * (2 * n_head + 5),
+        (kv_shape,) * 3,
+        [SMEM] + [VMEM] * (2 * n_head + 4),
         flops=2 * STEPS * rows * w_qkv.size,
         size=2 * w_qkv.size,
-    )(head[None], ids, *x_parts, *mod_parts, w, cos, sin, stale)
+    )(head[None], ids, *x_parts, *mod_parts, w, cos, sin)
 
     w_pair, kv = lax.optimization_barrier((line_of(w_out.T), kv))
     w_pair = jnp.stack(w_pair)
-    kv_pair = jnp.stack(line_of(kv))
+    stale_pair, kv_line = lax.optimization_barrier((stale_pair, line_of(kv)))
+    kv_pair = jnp.stack([jnp.concatenate(pair) for pair in zip(stale_pair, kv_line)])
     q_mate = across(q, PLANE)
     w_next = turn(w_pair, True)
     kv_next = turn(kv_pair, True)
+    kv_next, w_next, q_mate = lax.optimization_barrier((kv_next, w_next, q_mate))
     kv_far = turn(jnp.stack([kv_pair, kv_next]), False)
+    w_next, kv_far = lax.optimization_barrier((w_next, kv_far))
     w_far = turn(jnp.stack([w_pair, w_next]), False)
     tall = 2 * STEPS * rows
     part = call(

time: 44.5 us -> 43.4 us (0.975)
  waiting for transfers between devices: 24.6 us -> 19.5 us
  starting transfers between devices: 11.5 us -> 15.6 us
    ppermute x8 -> x9, waiting for transfers between devices: 18.3 us -> 14.4 us  [swap(): return lax.ppermute(values, axis, [(i, i ^ bit) for i in range(count)])]
    ppermute x4, starting transfers between devices: 4.25 us -> 6.35 us  [turn(): return lax.ppermute(values, ('patch', 'head'), pairs)]
    ppermute x8 -> x9, starting transfers between devices: 7.24 us -> 9.23 us  [swap(): return lax.ppermute(values, axis, [(i, i ^ bit) for i in range(count)])]
    ppermute x4, waiting for transfers between devices: 6.32 us -> 5.11 us  [turn(): return lax.ppermute(values, ('patch', 'head'), pairs)]
  transfers between devices with their start and end apart: 12 -> 13, of which waited for: 8 -> 8; matrix products, arithmetic and copies ran while one was open for 0% -> 0% of each run, Pallas kernels for 14% -> 14%
where the time goes in v14:
time: 43.4 us; the launch traced here: 43.3 us
  waiting for transfers between devices  19.5 us (45%)
  starting transfers between devices  15.6 us (36%)
  Pallas kernels  6.61 us (15%)
  other arithmetic  0.83 us (2%)
  between operations  0.78 us (2%)
    ppermute x9, waiting for transfers between devices, swap(): return lax.ppermute(values, axis, [(i, i ^ bit) for i in range(count)])  14.4 us
    ppermute x9, starting transfers between devices, swap(): return lax.ppermute(values, axis, [(i, i ^ bit) for i in range(count)])  9.23 us
    ppermute x4, starting transfers between devices, turn(): return lax.ppermute(values, ('patch', 'head'), pairs)  6.35 us
    ppermute x4, waiting for transfers between devices, turn(): return lax.ppermute(values, ('patch', 'head'), pairs)  5.11 us
    pallas_call x1, Pallas kernels, body(): call(load_kernel, tuple((pltpu.VMEM(v.shape, v.dtype) for v in first)) +...  3.2 us
    pallas_call x1, Pallas kernels, body(): call(functools.partial(qkv_kernel, n_head), (kv_shape,) * 3, [SMEM] + [VM...  1.16 us
    pallas_call x1, Pallas kernels, body(): call(attend_kernel, shaped((tall, cols + DH), BF16), [VMEM] * 6, flops=4...  1.11 us
  transfers between devices with their start and end apart: 13, of which 8 were waited for; matrix products, arithmetic and copies ran while one was open for 0% of the time, Pallas kernels for 14%

profile of v14, /device:TPU:0, one launch (start us, length us, event | category | flops | bytes accessed | tf_op | source)
XLA Modules:
  0.0 43.3 jit_solution(12638368634394108871)
XLA Ops:
  0.0 0.5 %collective-permute-start = (bf16[2,32,1536]{2,1,0:T(8,128)(2,1)}, bf16[2,32,1536]{2,1,0:T(8,128)(2,1)S(1)}, u32[]{:S(2)}, u32[]{:S(2)}) collective-permute-start(bf16[2,32,1536]{2,1,0:T(8,128)(2,1)} %x_ref.1), channel_id=1, source_target_pairs={{0,1},{1,0},{2,3},{3,2},{4,5},{5,4},{6,7},{7,6},{8,9},{9,8},{10,11... | collective-permute-start | bytes 589832 | tf_op jit(solution)/shard_map/ppermute | solution.py:23
  0.5 0.1 collective-permute-start.1
  0.5 4.0 %collective-permute-start.3 = (bf16[192,256]{1,0:T(8,128)(2,1)}, bf16[192,256]{1,0:T(8,128)(2,1)S(1)}, u32[]{:S(2)}, u32[]{:S(2)}) collective-permute-start(bf16[192,256]{1,0:T(8,128)(2,1)} %bitcast.22), channel_id=1, source_target_pairs={{0,16},{2,18},{4,20},{6,22},{8,24},{10,26},{12,28},{14,30},{16,0},... | collective-permute-start | bytes 294920 | tf_op jit(solution)/shard_map/ppermute | solution.py:23
  4.5 0.0 collective-permute-start.2
  5.2 0.0 copy-start
  5.2 0.0 copy-start.1
  5.3 3.2 %shard_map.73 = (bf16[3,3072,256]{2,1,0:T(8,128)(2,1)S(1)}, bf16[2,32,1536]{2,1,0:T(8,128)(2,1)S(1)}, f32[3,4,1536]{2,1,0:T(4,128)S(1)}, s32[8,128]{1,0:T(8,128)...) custom-call(s32[2]{0:T(128)} %ids.1, s32[1]{0:T(128)S(6)} %copy.8.slab, bf16[3,3072,256]{2,1,0:T(8,128)(2,1)} %bitcast.21, ...), custom_call_target="tpu_custom_call" | custom-call | bytes 4718592 | tf_op jit(solution)/shard_map/pallas_call | solution.py:232
  8.5 0.0 collective-permute-done.1
  8.5 0.0 collective-permute-done.refs_1_
  8.5 1.2 %shard_map.74 = (bf16[2,32,256]{2,1,0:T(8,128)(2,1)S(1)}, bf16[2,32,256]{2,1,0:T(8,128)(2,1)S(1)}, bf16[2,32,256]{2,1,0:T(8,128)(2,1)S(1)}) custom-call(s32[1]{0:T(128)} %bitcast.3.head, s32[8,128]{1,0:T(8,128)S(1)} %get-tuple-element.28.ids_ref, bf16[2,32,1536]{2,1,0:T(8,128)(2,1)S(1)} %get-tuple-element.30.refs_0_, ...), custom_call_target="tpu_custom_call" | custom-call | flops 301989888 | bytes 4718592 | tf_op jit(solution)/shard_map/pallas_call | solution.py:260
  9.7 1.2 %collective-permute-done.3 = bf16[192,256]{1,0:T(8,128)(2,1)S(1)} collective-permute-done((bf16[192,256]{1,0:T(8,128)(2,1)}, bf16[192,256]{1,0:T(8,128)(2,1)S(1)}, u32[]{:S(2)}, u32[]{:S(2)}) %collective-permute-start.3) | collective-permute-done | bytes 98336 | tf_op jit(solution)/shard_map/ppermute | solution.py:23
  10.9 1.7 %collective-permute-start.4 = (bf16[2,32,256]{2,1,0:T(8,128)(2,1)S(1)}, bf16[2,32,256]{2,1,0:T(8,128)(2,1)S(1)}, u32[]{:S(2)}, u32[]{:S(2)}) collective-permute-start(bf16[2,32,256]{2,1,0:T(8,128)(2,1)S(1)} %get-tuple-element.38), channel_id=1, source_target_pairs={{0,16},{2,18},{4,20},{6,22},{8,24},{10,26},{12,28},{14,30},{16,0},... | collective-permute-start | bytes 98312 | tf_op jit(solution)/shard_map/ppermute | solution.py:23
  12.6 0.0 copy-done
  12.7 1.6 %collective-permute-start.6 = (bf16[2,192,256]{2,1,0:T(8,128)(2,1)S(1)}, bf16[2,192,256]{2,1,0:T(8,128)(2,1)S(1)}, u32[]{:S(2)}, u32[]{:S(2)}) collective-permute-start(bf16[2,192,256]{2,1,0:T(8,128)(2,1)S(1)} %get-tuple-element.54.refs_1_), channel_id=1, source_target_pairs={{0,2},{1,5},{2,0},{3,7},{4,6},{5,1},{6,4},{7,3},{8,10},{9,13},{10,... | collective-permute-start | bytes 589832 | tf_op jit(solution)/shard_map/ppermute | solution.py:255
  14.2 0.0 collective-permute-done.2
  14.2 1.5 %collective-permute-done.4 = bf16[2,32,256]{2,1,0:T(8,128)(2,1)S(1)} collective-permute-done((bf16[2,32,256]{2,1,0:T(8,128)(2,1)S(1)}, bf16[2,32,256]{2,1,0:T(8,128)(2,1)S(1)}, u32[]{:S(2)}, u32[]{:S(2)}) %collective-permute-start.4) | collective-permute-done | bytes 32800 | tf_op jit(solution)/shard_map/ppermute | solution.py:23
  15.7 0.0 copy-done.1
  15.7 1.6 %collective-permute-start.5 = (bf16[2,4,32,256]{3,2,1,0:T(8,128)(2,1)S(1)}, bf16[2,4,32,256]{3,2,1,0:T(8,128)(2,1)S(1)}, u32[]{:S(2)}, u32[]{:S(2)}) collective-permute-start(bf16[2,4,32,256]{3,2,1,0:T(8,128)(2,1)S(1)} %get-tuple-element.56.refs_0_), channel_id=1, source_target_pairs={{0,2},{1,5},{2,0},{3,7},{4,6},{5,1},{6,4},{7,3},{8,10},{9,13},{10,... | collective-permute-start | bytes 393224 | tf_op jit(solution)/shard_map/ppermute | solution.py:255
  17.4 0.9 %collective-permute-start.7 = (bf16[2,32,256]{2,1,0:T(8,128)(2,1)S(1)}, bf16[2,32,256]{2,1,0:T(8,128)(2,1)S(1)}, u32[]{:S(2)}, u32[]{:S(2)}) collective-permute-start(bf16[2,32,256]{2,1,0:T(8,128)(2,1)S(1)} %get-tuple-element.34.q_ref), channel_id=1, source_target_pairs={{0,8},{2,10},{4,12},{6,14},{8,0},{10,2},{12,4},{14,6},{16,24},{18,... | collective-permute-start | bytes 98312 | tf_op jit(solution)/shard_map/ppermute | solution.py:23
  18.3 3.0 %collective-permute-done.7.mate_ref = bf16[2,32,256]{2,1,0:T(8,128)(2,1)S(1)} collective-permute-done((bf16[2,32,256]{2,1,0:T(8,128)(2,1)S(1)}, bf16[2,32,256]{2,1,0:T(8,128)(2,1)S(1)}, u32[]{:S(2)}, u32[]{:S(2)}) %collective-permute-start.7) | collective-permute-done | bytes 32800 | tf_op jit(solution)/shard_map/ppermute | solution.py:23
  21.3 0.0 collective-permute-done.5.refs_1_
  21.3 0.0 collective-permute-done.6.refs_2_
  21.3 1.6 %collective-permute-start.8 = (bf16[2,2,4,32,256]{4,3,2,1,0:T(8,128)(2,1)S(1)}, bf16[2,2,4,32,256]{4,3,2,1,0:T(8,128)(2,1)S(1)}, u32[]{:S(2)}, u32[]{:S(2)}) collective-permute-start(bf16[2,2,4,32,256]{4,3,2,1,0:T(8,128)(2,1)S(1)} %pad_maximum_fusion.1), channel_id=1, source_target_pairs={{0,4},{1,3},{2,6},{3,1},{4,0},{5,7},{6,2},{7,5},{8,12},{9,11},{10,... | collective-permute-start | bytes 786440 | tf_op jit(solution)/shard_map/ppermute | solution.py:255
  22.9 4.9 %collective-permute-done.8.refs_2_ = bf16[2,2,4,32,256]{4,3,2,1,0:T(8,128)(2,1)S(1)} collective-permute-done((bf16[2,2,4,32,256]{4,3,2,1,0:T(8,128)(2,1)S(1)}, bf16[2,2,4,32,256]{4,3,2,1,0:T(8,128)(2,1)S(1)}, u32[]{:S(2)}, u32[]{:S(2)}) %collective-permute-start.8) | collective-permute-done | bytes 262176 | tf_op jit(solution)/shard_map/ppermute | solution.py:255
  27.8 1.6 %collective-permute-start.10 = (bf16[2,2,192,256]{3,2,1,0:T(8,128)(2,1)S(1)}, bf16[2,2,192,256]{3,2,1,0:T(8,128)(2,1)S(1)}, u32[]{:S(2)}, u32[]{:S(2)}) collective-permute-start(bf16[2,2,192,256]{3,2,1,0:T(8,128)(2,1)S(1)} %pad_maximum_fusion), channel_id=1, source_target_pairs={{0,4},{1,3},{2,6},{3,1},{4,0},{5,7},{6,2},{7,5},{8,12},{9,11},{10,... | collective-permute-start | bytes 1179656 | tf_op jit(solution)/shard_map/ppermute | solution.py:255
  29.4 1.1 %shard_map.75.part_ref = bf16[128,384]{1,0:T(8,128)(2,1)S(1)} custom-call(bf16[2,32,256]{2,1,0:T(8,128)(2,1)S(1)} %get-tuple-element.34.q_ref, bf16[2,32,256]{2,1,0:T(8,128)(2,1)S(1)} %collective-permute-done.7.mate_ref, bf16[2,32,256]{2,1,0:T(8,128)(2,1)S(1)} %get-tuple-element.44.kv1_ref, bf16[2,4,32,256]{3,2,1,0:T(8,128)(2,1)S(1)} %get-tuple-element.56.refs_0_, ...), custom_call_target="tpu_custom_call" | custom-call | flops 33554432 | tf_op jit(solution)/shard_map/pallas_call | solution.py:280
  30.5 1.0 %collective-permute-start.9 = (bf16[128,384]{1,0:T(8,128)(2,1)S(1)}, bf16[128,384]{1,0:T(8,128)(2,1)S(1)}, u32[]{:S(2)}, u32[]{:S(2)}) collective-permute-start(bf16[128,384]{1,0:T(8,128)(2,1)S(1)} %shard_map.75.part_ref), channel_id=1, source_target_pairs={{0,8},{2,10},{4,12},{6,14},{8,0},{10,2},{12,4},{14,6},{16,24},{18,... | collective-permute-start | bytes 294920 | tf_op jit(solution)/shard_map/ppermute | solution.py:23
  31.5 3.7 %collective-permute-done.9.other_ref = bf16[128,384]{1,0:T(8,128)(2,1)S(1)} collective-permute-done((bf16[128,384]{1,0:T(8,128)(2,1)S(1)}, bf16[128,384]{1,0:T(8,128)(2,1)S(1)}, u32[]{:S(2)}, u32[]{:S(2)}) %collective-permute-start.9) | collective-permute-done | bytes 98336 | tf_op jit(solution)/shard_map/ppermute | solution.py:23
  35.2 0.2 shard_map.76.refs_0_
  35.4 0.3 collective-permute-done.10.refs_3_
  35.6 0.4 shard_map.78
  36.0 0.1 collective-permute-start.11
  36.1 0.4 shard_map.77.refs_0_
  36.5 1.0 %collective-permute-done.11.refs_1_ = bf16[128,768]{1,0:T(8,128)(2,1)S(1)} collective-permute-done((bf16[128,768]{1,0:T(8,128)(2,1)S(1)}, bf16[128,768]{1,0:T(8,128)(2,1)S(1)}, u32[]{:S(2)}, u32[]{:S(2)}) %collective-permute-start.11) | collective-permute-done | bytes 196640 | tf_op jit(solution)/shard_map/ppermute | solution.py:23
  37.5 0.1 shard_map.79
  37.7 1.0 %collective-permute-start.12 = (bf16[2,32,768]{2,1,0:T(8,128)(2,1)S(1)}, bf16[2,32,768]{2,1,0:T(8,128)(2,1)S(1)}, u32[]{:S(2)}, u32[]{:S(2)}) collective-permute-start(bf16[2,32,768]{2,1,0:T(8,128)(2,1)S(1)} %get-tuple-element.49), channel_id=1, source_target_pairs={{0,8},{2,10},{4,12},{6,14},{8,0},{10,2},{12,4},{14,6},{16,24},{18,... | collective-permute-start | bytes 294920 | tf_op jit(solution)/shard_map/ppermute | solution.py:23
  38.6 3.9 %collective-permute-done.12 = bf16[2,32,768]{2,1,0:T(8,128)(2,1)S(1)} collective-permute-done((bf16[2,32,768]{2,1,0:T(8,128)(2,1)S(1)}, bf16[2,32,768]{2,1,0:T(8,128)(2,1)S(1)}, u32[]{:S(2)}, u32[]{:S(2)}) %collective-permute-start.12) | collective-permute-done | bytes 98336 | tf_op jit(solution)/shard_map/ppermute | solution.py:23
  42.6 0.7 %pad_maximum_fusion.3 = bf16[2,32,1536]{2,1,0:T(8,128)(2,1)} fusion(bf16[2,32,768]{2,1,0:T(8,128)(2,1)S(1)} %get-tuple-element.52, bf16[2,32,768]{2,1,0:T(8,128)(2,1)S(1)} %get-tuple-element.51), kind=kLoop, calls=%fused_computation.3 | loop fusion | flops 393216 | bytes 393216 | tf_op jit(solution)/shard_map/concatenate | solution.py:309
  (6 shorter events, 0.1 us)
Async XLA Ops:
  0.0 8.5 %collective-permute-start = (bf16[2,32,1536]{2,1,0:T(8,128)(2,1)}, bf16[2,32,1536]{2,1,0:T(8,128)(2,1)S(1)}, u32[]{:S(2)}, u32[]{:S(2)}) collective-permute-start(bf16[2,32,1536]{2,1,0:T(8,128)(2,1)} %x_ref.1), channel_id=1, source_target_pairs={{0,1},{1,0},{2,3},{3,2},{4,5},{5,4},{6,7},{7,6},{8,9},{9,8},{10,11... | collective-permute-start | bytes 589832 | tf_op jit(solution)/shard_map/ppermute | solution.py:23
  0.5 8.0 %collective-permute-start.1 = (f32[4,3,1536]{2,0,1:T(4,128)}, f32[4,3,1536]{2,0,1:T(4,128)S(1)}, u32[]{:S(2)}, u32[]{:S(2)}) collective-permute-start(f32[4,3,1536]{2,0,1:T(4,128)} %param.11), channel_id=1, source_target_pairs={{0,1},{1,0},{2,3},{3,2},{4,5},{5,4},{6,7},{7,6},{8,9},{9,8},{10,11... | collective-permute-start | bytes 221192 | tf_op jit(solution)/shard_map/ppermute | solution.py:23
  0.5 10.4 %collective-permute-start.3 = (bf16[192,256]{1,0:T(8,128)(2,1)}, bf16[192,256]{1,0:T(8,128)(2,1)S(1)}, u32[]{:S(2)}, u32[]{:S(2)}) collective-permute-start(bf16[192,256]{1,0:T(8,128)(2,1)} %bitcast.22), channel_id=1, source_target_pairs={{0,16},{2,18},{4,20},{6,22},{8,24},{10,26},{12,28},{14,30},{16,0},... | collective-permute-start | bytes 294920 | tf_op jit(solution)/shard_map/ppermute | solution.py:23
  4.5 9.7 %collective-permute-start.2 = (bf16[2,32,256]{2,1,0:T(8,128)(2,1)}, bf16[2,32,256]{2,1,0:T(8,128)(2,1)S(1)}, u32[]{:S(2)}, u32[]{:S(2)}) collective-permute-start(bf16[2,32,256]{2,1,0:T(8,128)(2,1)} %param.8), channel_id=1, source_target_pairs={{0,16},{2,18},{4,20},{6,22},{8,24},{10,26},{12,28},{14,30},{16,0},... | collective-permute-start | bytes 98312 | tf_op jit(solution)/shard_map/ppermute | solution.py:23
  5.2 7.4 %copy-start = (bf16[256,192]{0,1:T(8,128)(2,1)S(1)}, bf16[256,192]{0,1:T(8,128)(2,1)}, u32[]{:S(2)}) copy-start(bf16[256,192]{0,1:T(8,128)(2,1)} %param.10) | copy-start | bytes 294916
  5.2 10.5 %copy-start.1 = (bf16[2,32,256]{2,1,0:T(8,128)(2,1)S(1)}, bf16[2,32,256]{2,1,0:T(8,128)(2,1)}, u32[]{:S(2)}) copy-start(bf16[2,32,256]{2,1,0:T(8,128)(2,1)} %param.8) | copy-start | bytes 98308
  10.9 4.8 %collective-permute-start.4 = (bf16[2,32,256]{2,1,0:T(8,128)(2,1)S(1)}, bf16[2,32,256]{2,1,0:T(8,128)(2,1)S(1)}, u32[]{:S(2)}, u32[]{:S(2)}) collective-permute-start(bf16[2,32,256]{2,1,0:T(8,128)(2,1)S(1)} %get-tuple-element.38), channel_id=1, source_target_pairs={{0,16},{2,18},{4,20},{6,22},{8,24},{10,26},{12,28},{14,30},{16,0},... | collective-permute-start | bytes 98312 | tf_op jit(solution)/shard_map/ppermute | solution.py:23
  12.7 8.6 %collective-permute-start.6 = (bf16[2,192,256]{2,1,0:T(8,128)(2,1)S(1)}, bf16[2,192,256]{2,1,0:T(8,128)(2,1)S(1)}, u32[]{:S(2)}, u32[]{:S(2)}) collective-permute-start(bf16[2,192,256]{2,1,0:T(8,128)(2,1)S(1)} %get-tuple-element.54.refs_1_), channel_id=1, source_target_pairs={{0,2},{1,5},{2,0},{3,7},{4,6},{5,1},{6,4},{7,3},{8,10},{9,13},{10,... | collective-permute-start | bytes 589832 | tf_op jit(solution)/shard_map/ppermute | solution.py:255
  15.7 5.5 %collective-permute-start.5 = (bf16[2,4,32,256]{3,2,1,0:T(8,128)(2,1)S(1)}, bf16[2,4,32,256]{3,2,1,0:T(8,128)(2,1)S(1)}, u32[]{:S(2)}, u32[]{:S(2)}) collective-permute-start(bf16[2,4,32,256]{3,2,1,0:T(8,128)(2,1)S(1)} %get-tuple-element.56.refs_0_), channel_id=1, source_target_pairs={{0,2},{1,5},{2,0},{3,7},{4,6},{5,1},{6,4},{7,3},{8,10},{9,13},{10,... | collective-permute-start | bytes 393224 | tf_op jit(solution)/shard_map/ppermute | solution.py:255
  17.4 3.9 %collective-permute-start.7 = (bf16[2,32,256]{2,1,0:T(8,128)(2,1)S(1)}, bf16[2,32,256]{2,1,0:T(8,128)(2,1)S(1)}, u32[]{:S(2)}, u32[]{:S(2)}) collective-permute-start(bf16[2,32,256]{2,1,0:T(8,128)(2,1)S(1)} %get-tuple-element.34.q_ref), channel_id=1, source_target_pairs={{0,8},{2,10},{4,12},{6,14},{8,0},{10,2},{12,4},{14,6},{16,24},{18,... | collective-permute-start | bytes 98312 | tf_op jit(solution)/shard_map/ppermute | solution.py:23
  21.3 6.4 %collective-permute-start.8 = (bf16[2,2,4,32,256]{4,3,2,1,0:T(8,128)(2,1)S(1)}, bf16[2,2,4,32,256]{4,3,2,1,0:T(8,128)(2,1)S(1)}, u32[]{:S(2)}, u32[]{:S(2)}) collective-permute-start(bf16[2,2,4,32,256]{4,3,2,1,0:T(8,128)(2,1)S(1)} %pad_maximum_fusion.1), channel_id=1, source_target_pairs={{0,4},{1,3},{2,6},{3,1},{4,0},{5,7},{6,2},{7,5},{8,12},{9,11},{10,... | collective-permute-start | bytes 786440 | tf_op jit(solution)/shard_map/ppermute | solution.py:255
  27.8 7.8 %collective-permute-start.10 = (bf16[2,2,192,256]{3,2,1,0:T(8,128)(2,1)S(1)}, bf16[2,2,192,256]{3,2,1,0:T(8,128)(2,1)S(1)}, u32[]{:S(2)}, u32[]{:S(2)}) collective-permute-start(bf16[2,2,192,256]{3,2,1,0:T(8,128)(2,1)S(1)} %pad_maximum_fusion), channel_id=1, source_target_pairs={{0,4},{1,3},{2,6},{3,1},{4,0},{5,7},{6,2},{7,5},{8,12},{9,11},{10,... | collective-permute-start | bytes 1179656 | tf_op jit(solution)/shard_map/ppermute | solution.py:255
  30.5 4.7 %collective-permute-start.9 = (bf16[128,384]{1,0:T(8,128)(2,1)S(1)}, bf16[128,384]{1,0:T(8,128)(2,1)S(1)}, u32[]{:S(2)}, u32[]{:S(2)}) collective-permute-start(bf16[128,384]{1,0:T(8,128)(2,1)S(1)} %shard_map.75.part_ref), channel_id=1, source_target_pairs={{0,8},{2,10},{4,12},{6,14},{8,0},{10,2},{12,4},{14,6},{16,24},{18,... | collective-permute-start | bytes 294920 | tf_op jit(solution)/shard_map/ppermute | solution.py:23
  36.0 1.5 %collective-permute-start.11 = (bf16[128,768]{1,0:T(8,128)(2,1)S(1)}, bf16[128,768]{1,0:T(8,128)(2,1)S(1)}, u32[]{:S(2)}, u32[]{:S(2)}) collective-permute-start(bf16[128,768]{1,0:T(8,128)(2,1)S(1)} %shard_map.78), channel_id=1, source_target_pairs={{0,1},{1,0},{2,3},{3,2},{4,5},{5,4},{6,7},{7,6},{8,9},{9,8},{10,11... | collective-permute-start | bytes 589832 | tf_op jit(solution)/shard_map/ppermute | solution.py:23
  37.7 4.9 %collective-permute-start.12 = (bf16[2,32,768]{2,1,0:T(8,128)(2,1)S(1)}, bf16[2,32,768]{2,1,0:T(8,128)(2,1)S(1)}, u32[]{:S(2)}, u32[]{:S(2)}) collective-permute-start(bf16[2,32,768]{2,1,0:T(8,128)(2,1)S(1)} %get-tuple-element.49), channel_id=1, source_target_pairs={{0,8},{2,10},{4,12},{6,14},{8,0},{10,2},{12,4},{14,6},{16,24},{18,... | collective-permute-start | bytes 294920 | tf_op jit(solution)/shard_map/ppermute | solution.py:23

commit v15 on v14

--- a/solution.py
+++ b/solution.py
@@ -116,8 +116,7 @@
 
 
 def attend_kernel(q_ref, mate_ref, kv1_ref, *refs):
-    own_ref, next_ref, far_ref, out_ref = refs
-    kv_refs = [own_ref, next_ref, far_ref.at[0], far_ref.at[1]]
+    kv_refs, out_ref = refs[:PLANE], refs[PLANE]
     blocks, _, rows, cols = kv_refs[0].shape
     old_rows = PLANE * blocks * rows
     shape = (2 * rows, old_rows + rows)
@@ -176,14 +175,17 @@
 
 
 def project_kernel(n_head, n_patch, bit, patch, head, *refs):
-    o_ref, own_ref, next_ref, far_ref, out_ref, sums = refs
+    o_ref, low_ref, high_ref, out_ref, sums = refs
     slot = head[0] ^ bit ^ (patch[0] // (n_patch // n_head))
-    odd = head[0] % 2
-    blocks = ((0, own_ref), (1 + odd, next_ref), (2 - odd, far_ref.at[0]), (3, far_ref.at[1]))
-    for near, w_ref in blocks:
-        sums[(patch[0] % PLANE) ^ near] = lax.dot_general(
-            o_ref[...], w_ref[slot], NT, preferred_element_type=F32
-        )
+    for core, w_ref in enumerate((low_ref, high_ref)):
+
+        @pl.when(head[0] % 2 == core)
+        def _():
+            for near in range(PLANE):
+                sums[(patch[0] % PLANE) ^ near] = lax.dot_general(
+                    o_ref[...], w_ref[near, slot], NT, preferred_element_type=F32
+                )
+
     out = jnp.concatenate([sums[c] for c in range(PLANE)], axis=1)
     out_ref[...] = out.astype(out_ref.dtype)
 
@@ -246,16 +248,32 @@
     def line_of(values):
         return [values] + [across(values, k) for k in range(2 * PLANE, n_patch, 2 * PLANE)]
 
-    def turn(values, first):
-        pairs = [
-            (p * n_head + h, (p ^ (1 if (h % 2 == 0) == first else 2)) * n_head + h)
+    def pairs_of(moves):
+        return [
+            (p * n_head + h, q * n_head + g)
             for p in range(n_patch)
             for h in range(n_head)
+            for q, g in moves(p, h)
         ]
+
+    def lone(values, k):
+        pairs = pairs_of(lambda p, h: [(p ^ k, h)] if h % 2 else [])
         return lax.ppermute(values, ("patch", "head"), pairs)
 
+    def lift(values):
+        pairs = pairs_of(lambda p, h: [] if h % 2 else [(p, h + 1)])
+        return lax.ppermute(values, ("patch", "head"), pairs)
+
+    def lower(values):
+        pairs = pairs_of(lambda p, h: [(p, h - 1)] if h % 2 else [])
+        return lax.ppermute(values, ("patch", "head"), pairs)
+
+    def plane_of(values):
+        return [values] + [across(values, k) for k in range(1, PLANE)]
 
     stale_pair = line_of(stale_kv)
+    w_own, *w_rest = line_of(w_out.T)
+    w_even = lift(w_own)
     kv_shape = shaped((2, rows, cols), BF16)
     q, kv, kv1 = call(
         functools.partial(qkv_kernel, n_head),
@@ -265,36 +283,47 @@
         size=2 * w_qkv.size,
     )(head[None], ids, *x_parts, *mod_parts, w, cos, sin)
 
-    w_pair, kv = lax.optimization_barrier((line_of(w_out.T), kv))
-    w_pair = jnp.stack(w_pair)
+    w_own, w_even, w_rest, kv = lax.optimization_barrier((w_own, w_even, w_rest, kv))
+    w_rest = jnp.stack(w_rest)
+    w_both = jnp.stack([w_even, w_own])
+    rest_both = jnp.stack([lift(w_rest), w_rest], axis=1)
     stale_pair, kv_line = lax.optimization_barrier((stale_pair, line_of(kv)))
     kv_pair = jnp.stack([jnp.concatenate(pair) for pair in zip(stale_pair, kv_line)])
     q_mate = across(q, PLANE)
-    w_next = turn(w_pair, True)
-    kv_next = turn(kv_pair, True)
-    kv_next, w_next, q_mate = lax.optimization_barrier((kv_next, w_next, q_mate))
-    kv_far = turn(jnp.stack([kv_pair, kv_next]), False)
-    w_next, kv_far = lax.optimization_barrier((w_next, kv_far))
-    w_far = turn(jnp.stack([w_pair, w_next]), False)
+    kv_plane = plane_of(kv_pair)
+    w_x = lone(w_both, 1)
+    rest_y = lone(rest_both, 2)
+    w_x, rest_y, q_mate, kv_plane[1] = lax.optimization_barrier(
+        (w_x, rest_y, q_mate, kv_plane[1])
+    )
+    w_y = lone(jnp.stack([w_both, w_x]), 2)
+    rest_x = lone(jnp.stack([rest_both, rest_y]), 1)
     tall = 2 * STEPS * rows
     part = call(
         attend_kernel,
         shaped((tall, cols + DH), BF16),
-        [VMEM] * 6,
+        [VMEM] * (3 + PLANE),
         flops=4 * STEPS * rows * n_patch * rows * cols,
-    )(q, q_mate, kv1, kv_pair, kv_next, kv_far)
+    )(q, q_mate, kv1, *kv_plane)
     o = call(merge_kernel, shaped((tall, cols), BF16), [VMEM] * 2)(part, across(part, PLANE))
+    o, w_y, rest_x = lax.optimization_barrier((o, w_y, rest_x))
+    near = [(w_both, rest_both), (w_x, rest_x[0]), (w_y[0], rest_y), (w_y[1], rest_x[1])]
+    w_all = [
+        jnp.stack([jnp.concatenate([first[None, k], others[:, k]]) for first, others in near])
+        for k in range(2)
+    ]
+    w_low, w_high = lower(w_all[0]), w_all[1]
     wide = PLANE * piece
 
     def project(bit, dtype):
         return call(
             functools.partial(project_kernel, n_head, n_patch, bit),
             shaped((tall, wide), dtype),
-            [SMEM] * 2 + [VMEM] * 4,
+            [SMEM] * 2 + [VMEM] * 3,
             [pltpu.VMEM((PLANE, tall, piece), F32)],
             2 * tall * wide * cols,
             2 * wide * cols,
-        )(patch[None], head[None], o, w_pair, w_next, w_far)
+        )(patch[None], head[None], o, w_low, w_high)
 
     sums = [swap(project(k, BF16), "head", n_head, k) for k in range(1, n_head)]
     sums = [project(0, F32)] + sums

time: 43.4 us -> 50.4 us (1.16)
  starting transfers between devices: 15.6 us -> 23.9 us
  waiting for transfers between devices: 19.5 us -> 17.2 us
    ppermute x9 -> x12, starting transfers between devices: 9.23 us -> 16.3 us  [swap(): return lax.ppermute(values, axis, [(i, i ^ bit) for i in range(count)])]
    ppermute x9 -> x12, waiting for transfers between devices: 14.4 us -> 12.4 us  [swap(): return lax.ppermute(values, axis, [(i, i ^ bit) for i in range(count)])]
    ppermute x4 -> x7, starting transfers between devices: 6.35 us -> 7.64 us  [the longest x2 3.63 us: lift(): return lax.ppermute(values, ('patch', 'head'), pairs)]
    ppermute x4 -> x7, waiting for transfers between devices: 5.11 us -> 4.74 us  [the longest x1 4.73 us: lower(): return lax.ppermute(values, ('patch', 'head'), pairs)]
  transfers between devices with their start and end apart: 13 -> 19, of which waited for: 8 -> 9; matrix products, arithmetic and copies ran while one was open for 0% -> 1% of each run, Pallas kernels for 14% -> 12%
where the time goes in v15:
time: 50.4 us; the launch traced here: 50.1 us
  starting transfers between devices  23.9 us (47%)
  waiting for transfers between devices  17.2 us (34%)
  Pallas kernels  6.61 us (13%)
  other arithmetic  1.23 us (2%)
  between operations  1 us (2%)
    ppermute x12, starting transfers between devices, swap(): return lax.ppermute(values, axis, [(i, i ^ bit) for i in range(count)])  16.3 us
    ppermute x12, waiting for transfers between devices, swap(): return lax.ppermute(values, axis, [(i, i ^ bit) for i in range(count)])  12.4 us
    ppermute x1, waiting for transfers between devices, lower(): return lax.ppermute(values, ('patch', 'head'), pairs)  4.73 us
    ppermute x2, starting transfers between devices, lift(): return lax.ppermute(values, ('patch', 'head'), pairs)  3.63 us
    pallas_call x1, Pallas kernels, body(): call(load_kernel, tuple((pltpu.VMEM(v.shape, v.dtype) for v in first)) +...  3.2 us
    ppermute x4, starting transfers between devices, lone(): return lax.ppermute(values, ('patch', 'head'), pairs)  2.72 us
    ppermute x1, starting transfers between devices, lower(): return lax.ppermute(values, ('patch', 'head'), pairs)  1.29 us
    pallas_call x1, Pallas kernels, body(): call(functools.partial(qkv_kernel, n_head), (kv_shape,) * 3, [SMEM] + [VM...  1.16 us
  transfers between devices with their start and end apart: 19, of which 9 were waited for; matrix products, arithmetic and copies ran while one was open for 1% of the time, Pallas kernels for 12%

profile of v15, /device:TPU:0, one launch (start us, length us, event | category | flops | bytes accessed | tf_op | source)
XLA Modules:
  0.0 50.1 jit_solution(12776757575792402115)
XLA Ops:
  0.0 0.5 collective-permute-start
  0.5 0.1 collective-permute-start.1
  0.5 2.3 %collective-permute-start.2 = (bf16[192,256]{1,0:T(8,128)(2,1)}, bf16[192,256]{1,0:T(8,128)(2,1)S(1)}, u32[]{:S(2)}, u32[]{:S(2)}) collective-permute-start(bf16[192,256]{1,0:T(8,128)(2,1)} %bitcast.69), channel_id=1, source_target_pairs={{0,1},{2,3},{4,5},{6,7},{8,9},{10,11},{12,13},{14,15},{16,17},{18,... | collective-permute-start | bytes 294920 | tf_op jit(solution)/shard_map/ppermute | solution.py:265
  2.9 3.7 %collective-permute-start.3 = (bf16[192,256]{1,0:T(8,128)(2,1)}, bf16[192,256]{1,0:T(8,128)(2,1)S(1)}, u32[]{:S(2)}, u32[]{:S(2)}) collective-permute-start(bf16[192,256]{1,0:T(8,128)(2,1)} %bitcast.70), channel_id=1, source_target_pairs={{0,16},{2,18},{4,20},{6,22},{8,24},{10,26},{12,28},{14,30},{16,0},... | collective-permute-start | bytes 294920 | tf_op jit(solution)/shard_map/ppermute | solution.py:23
  6.5 0.1 collective-permute-start.8
  7.3 3.2 %shard_map.73 = (bf16[3,3072,256]{2,1,0:T(8,128)(2,1)S(1)}, bf16[2,32,1536]{2,1,0:T(8,128)(2,1)S(1)}, f32[3,4,1536]{2,1,0:T(4,128)S(1)}, s32[8,128]{1,0:T(8,128)...) custom-call(s32[2]{0:T(128)} %ids.1, s32[1]{0:T(128)S(6)} %copy.8.slab, bf16[3,3072,256]{2,1,0:T(8,128)(2,1)} %bitcast.62, ...), custom_call_target="tpu_custom_call" | custom-call | bytes 4718592 | tf_op jit(solution)/shard_map/pallas_call | solution.py:234
  10.5 0.0 collective-permute-done.1
  10.5 0.0 collective-permute-done.refs_1_
  10.5 1.2 %shard_map.74 = (bf16[2,32,256]{2,1,0:T(8,128)(2,1)S(1)}, bf16[2,32,256]{2,1,0:T(8,128)(2,1)S(1)}, bf16[2,32,256]{2,1,0:T(8,128)(2,1)S(1)}) custom-call(s32[1]{0:T(128)} %bitcast.3.head, s32[8,128]{1,0:T(8,128)S(1)} %get-tuple-element.31.ids_ref, bf16[2,32,1536]{2,1,0:T(8,128)(2,1)S(1)} %get-tuple-element.33.refs_0_, ...), custom_call_target="tpu_custom_call" | custom-call | flops 301989888 | bytes 4718592 | tf_op jit(solution)/shard_map/pallas_call | solution.py:278
  11.7 0.0 collective-permute-done.2
  11.7 0.2 collective-permute-done.3
  11.9 2.7 %collective-permute-start.9 = (bf16[2,32,256]{2,1,0:T(8,128)(2,1)S(1)}, bf16[2,32,256]{2,1,0:T(8,128)(2,1)S(1)}, u32[]{:S(2)}, u32[]{:S(2)}) collective-permute-start(bf16[2,32,256]{2,1,0:T(8,128)(2,1)S(1)} %get-tuple-element.44), channel_id=1, source_target_pairs={{0,16},{2,18},{4,20},{6,22},{8,24},{10,26},{12,28},{14,30},{16,0},... | collective-permute-start | bytes 98312 | tf_op jit(solution)/shard_map/ppermute | solution.py:23
  14.6 1.3 %collective-permute-start.5 = (bf16[1,192,256]{2,1,0:T(8,128)(2,1)S(1)}, bf16[1,192,256]{2,1,0:T(8,128)(2,1)S(1)}, u32[]{:S(2)}, u32[]{:S(2)}) collective-permute-start(bf16[1,192,256]{2,1,0:T(8,128)(2,1)S(1)} %bitcast.65), channel_id=1, source_target_pairs={{0,1},{2,3},{4,5},{6,7},{8,9},{10,11},{12,13},{14,15},{16,17},{18,... | collective-permute-start | bytes 294920 | tf_op jit(solution)/shard_map/ppermute | solution.py:265
  15.9 0.0 collective-permute-done.8
  15.9 1.0 %collective-permute-done.9 = bf16[2,32,256]{2,1,0:T(8,128)(2,1)S(1)} collective-permute-done((bf16[2,32,256]{2,1,0:T(8,128)(2,1)S(1)}, bf16[2,32,256]{2,1,0:T(8,128)(2,1)S(1)}, u32[]{:S(2)}, u32[]{:S(2)}) %collective-permute-start.9) | collective-permute-done | bytes 32800 | tf_op jit(solution)/shard_map/ppermute | solution.py:23
  16.9 0.0 collective-permute-done.5
  16.9 0.1 fusion.2
  17.0 0.7 %collective-permute-start.4 = (bf16[2,192,256]{2,1,0:T(8,128)(2,1)S(1)}, bf16[2,192,256]{2,1,0:T(8,128)(2,1)S(1)}, u32[]{:S(2)}, u32[]{:S(2)}) collective-permute-start(bf16[2,192,256]{2,1,0:T(8,128)(2,1)S(1)} %get-tuple-element.76), channel_id=1, source_target_pairs={{1,3},{3,1},{5,7},{7,5},{9,11},{11,9},{13,15},{15,13},{17,19},{19,... | collective-permute-start | bytes 589832 | tf_op jit(solution)/shard_map/ppermute | solution.py:261
  17.7 0.7 %collective-permute-start.6 = (bf16[1,2,192,256]{3,2,1,0:T(8,128)(2,1)S(1)}, bf16[1,2,192,256]{3,2,1,0:T(8,128)(2,1)S(1)}, u32[]{:S(2)}, u32[]{:S(2)}) collective-permute-start(bf16[1,2,192,256]{3,2,1,0:T(8,128)(2,1)S(1)} %get-tuple-element.74), channel_id=1, source_target_pairs={{1,5},{3,7},{5,1},{7,3},{9,13},{11,15},{13,9},{15,11},{17,21},{19,... | collective-permute-start | bytes 589832 | tf_op jit(solution)/shard_map/ppermute | solution.py:261
  18.4 1.6 %collective-permute-start.10 = (bf16[2,4,32,256]{3,2,1,0:T(8,128)(2,1)S(1)}, bf16[2,4,32,256]{3,2,1,0:T(8,128)(2,1)S(1)}, u32[]{:S(2)}, u32[]{:S(2)}) collective-permute-start(bf16[2,4,32,256]{3,2,1,0:T(8,128)(2,1)S(1)} %pad_maximum_fusion.8.refs_0_), channel_id=1, source_target_pairs={{0,2},{2,0},{4,6},{6,4},{8,10},{10,8},{12,14},{14,12},{16,18},{18,... | collective-permute-start | bytes 393224 | tf_op jit(solution)/shard_map/ppermute | solution.py:23
  20.0 1.5 %collective-permute-start.7 = (bf16[2,32,256]{2,1,0:T(8,128)(2,1)S(1)}, bf16[2,32,256]{2,1,0:T(8,128)(2,1)S(1)}, u32[]{:S(2)}, u32[]{:S(2)}) collective-permute-start(bf16[2,32,256]{2,1,0:T(8,128)(2,1)S(1)} %get-tuple-element.37.q_ref), channel_id=1, source_target_pairs={{0,8},{2,10},{4,12},{6,14},{8,0},{10,2},{12,4},{14,6},{16,24},{18,... | collective-permute-start | bytes 98312 | tf_op jit(solution)/shard_map/ppermute | solution.py:23
  21.5 1.5 %collective-permute-start.11 = (bf16[2,4,32,256]{3,2,1,0:T(8,128)(2,1)S(1)}, bf16[2,4,32,256]{3,2,1,0:T(8,128)(2,1)S(1)}, u32[]{:S(2)}, u32[]{:S(2)}) collective-permute-start(bf16[2,4,32,256]{3,2,1,0:T(8,128)(2,1)S(1)} %pad_maximum_fusion.8.refs_0_), channel_id=1, source_target_pairs={{0,4},{2,6},{4,0},{6,2},{8,12},{10,14},{12,8},{14,10},{16,20},{18,... | collective-permute-start | bytes 393224 | tf_op jit(solution)/shard_map/ppermute | solution.py:23
  23.0 0.9 %collective-permute-done.7.mate_ref = bf16[2,32,256]{2,1,0:T(8,128)(2,1)S(1)} collective-permute-done((bf16[2,32,256]{2,1,0:T(8,128)(2,1)S(1)}, bf16[2,32,256]{2,1,0:T(8,128)(2,1)S(1)}, u32[]{:S(2)}, u32[]{:S(2)}) %collective-permute-start.7) | collective-permute-done | bytes 32800 | tf_op jit(solution)/shard_map/ppermute | solution.py:23
  23.9 1.5 %collective-permute-start.12 = (bf16[2,4,32,256]{3,2,1,0:T(8,128)(2,1)S(1)}, bf16[2,4,32,256]{3,2,1,0:T(8,128)(2,1)S(1)}, u32[]{:S(2)}, u32[]{:S(2)}) collective-permute-start(bf16[2,4,32,256]{3,2,1,0:T(8,128)(2,1)S(1)} %pad_maximum_fusion.8.refs_0_), channel_id=1, source_target_pairs={{0,6},{2,4},{4,2},{6,0},{8,14},{10,12},{12,10},{14,8},{16,22},{18,... | collective-permute-start | bytes 393224 | tf_op jit(solution)/shard_map/ppermute | solution.py:23
  25.4 0.0 collective-permute-done.10.refs_1_
  25.4 0.0 collective-permute-done.4
  25.4 0.0 collective-permute-done.6
  25.5 0.7 %collective-permute-start.15 = (bf16[2,1,2,192,256]{4,3,2,1,0:T(8,128)(2,1)S(1)}, bf16[2,1,2,192,256]{4,3,2,1,0:T(8,128)(2,1)S(1)}, u32[]{:S(2)}, u32[]{:S(2)}) collective-permute-start(bf16[2,1,2,192,256]{4,3,2,1,0:T(8,128)(2,1)S(1)} %pad_maximum_fusion.3), channel_id=1, source_target_pairs={{1,3},{3,1},{5,7},{7,5},{9,11},{11,9},{13,15},{15,13},{17,19},{19,... | collective-permute-start | bytes 1179656 | tf_op jit(solution)/shard_map/ppermute | solution.py:261
  26.2 0.7 %collective-permute-start.14 = (bf16[2,2,192,256]{3,2,1,0:T(8,128)(2,1)S(1)}, bf16[2,2,192,256]{3,2,1,0:T(8,128)(2,1)S(1)}, u32[]{:S(2)}, u32[]{:S(2)}) collective-permute-start(bf16[2,2,192,256]{3,2,1,0:T(8,128)(2,1)S(1)} %pad_maximum_fusion.2), channel_id=1, source_target_pairs={{1,5},{3,7},{5,1},{7,3},{9,13},{11,15},{13,9},{15,11},{17,21},{19,... | collective-permute-start | bytes 1179656 | tf_op jit(solution)/shard_map/ppermute | solution.py:261
  26.9 1.0 %collective-permute-done.11.refs_2_ = bf16[2,4,32,256]{3,2,1,0:T(8,128)(2,1)S(1)} collective-permute-done((bf16[2,4,32,256]{3,2,1,0:T(8,128)(2,1)S(1)}, bf16[2,4,32,256]{3,2,1,0:T(8,128)(2,1)S(1)}, u32[]{:S(2)}, u32[]{:S(2)}) %collective-permute-start.11) | collective-permute-done | bytes 131104 | tf_op jit(solution)/shard_map/ppermute | solution.py:23
  27.9 2.0 %collective-permute-done.12.refs_3_ = bf16[2,4,32,256]{3,2,1,0:T(8,128)(2,1)S(1)} collective-permute-done((bf16[2,4,32,256]{3,2,1,0:T(8,128)(2,1)S(1)}, bf16[2,4,32,256]{3,2,1,0:T(8,128)(2,1)S(1)}, u32[]{:S(2)}, u32[]{:S(2)}) %collective-permute-start.12) | collective-permute-done | bytes 131104 | tf_op jit(solution)/shard_map/ppermute | solution.py:23
  29.9 1.1 %shard_map.75.part_ref = bf16[128,384]{1,0:T(8,128)(2,1)S(1)} custom-call(bf16[2,32,256]{2,1,0:T(8,128)(2,1)S(1)} %get-tuple-element.37.q_ref, bf16[2,32,256]{2,1,0:T(8,128)(2,1)S(1)} %collective-permute-done.7.mate_ref, bf16[2,32,256]{2,1,0:T(8,128)(2,1)S(1)} %get-tuple-element.48.kv1_ref, bf16[2,4,32,256]{3,2,1,0:T(8,128)(2,1)S(1)} %pad_maximum_fusion.8.refs_0_, ...), custom_call_target="tpu_custom_call" | custom-call | flops 33554432 | tf_op jit(solution)/shard_map/pallas_call | solution.py:302
  31.0 1.6 %collective-permute-start.13 = (bf16[128,384]{1,0:T(8,128)(2,1)S(1)}, bf16[128,384]{1,0:T(8,128)(2,1)S(1)}, u32[]{:S(2)}, u32[]{:S(2)}) collective-permute-start(bf16[128,384]{1,0:T(8,128)(2,1)S(1)} %shard_map.75.part_ref), channel_id=1, source_target_pairs={{0,8},{2,10},{4,12},{6,14},{8,0},{10,2},{12,4},{14,6},{16,24},{18,... | collective-permute-start | bytes 294920 | tf_op jit(solution)/shard_map/ppermute | solution.py:23
  32.6 3.1 %collective-permute-done.13.other_ref = bf16[128,384]{1,0:T(8,128)(2,1)S(1)} collective-permute-done((bf16[128,384]{1,0:T(8,128)(2,1)S(1)}, bf16[128,384]{1,0:T(8,128)(2,1)S(1)}, u32[]{:S(2)}, u32[]{:S(2)}) %collective-permute-start.13) | collective-permute-done | bytes 98336 | tf_op jit(solution)/shard_map/ppermute | solution.py:23
  35.7 0.2 shard_map.76.refs_0_
  35.9 0.0 collective-permute-done.14
  36.1 0.1 pad_maximum_fusion
  36.2 1.3 %collective-permute-start.16 = (bf16[4,2,192,256]{3,2,1,0:T(8,128)(2,1)S(1)}, bf16[4,2,192,256]{3,2,1,0:T(8,128)(2,1)S(1)}, u32[]{:S(2)}, u32[]{:S(2)}) collective-permute-start(bf16[4,2,192,256]{3,2,1,0:T(8,128)(2,1)S(1)} %pad_maximum_fusion), channel_id=1, source_target_pairs={{1,0},{3,2},{5,4},{7,6},{9,8},{11,10},{13,12},{15,14},{17,16},{19,... | collective-permute-start | bytes 2359304 | tf_op jit(solution)/shard_map/ppermute | solution.py:269
  37.6 0.1 pad_maximum_fusion.1.refs_2_
  37.7 4.7 %collective-permute-done.16.refs_1_ = bf16[4,2,192,256]{3,2,1,0:T(8,128)(2,1)S(1)} collective-permute-done((bf16[4,2,192,256]{3,2,1,0:T(8,128)(2,1)S(1)}, bf16[4,2,192,256]{3,2,1,0:T(8,128)(2,1)S(1)}, u32[]{:S(2)}, u32[]{:S(2)}) %collective-permute-start.16) | collective-permute-done | bytes 786464 | tf_op jit(solution)/shard_map/ppermute | solution.py:269
  42.5 0.4 shard_map.78
  42.9 0.2 collective-permute-start.17
  43.0 0.4 shard_map.77.refs_0_
  43.5 0.9 %collective-permute-done.17.refs_1_ = bf16[128,768]{1,0:T(8,128)(2,1)S(1)} collective-permute-done((bf16[128,768]{1,0:T(8,128)(2,1)S(1)}, bf16[128,768]{1,0:T(8,128)(2,1)S(1)}, u32[]{:S(2)}, u32[]{:S(2)}) %collective-permute-start.17) | collective-permute-done | bytes 196640 | tf_op jit(solution)/shard_map/ppermute | solution.py:23
  44.4 0.1 shard_map.79
  44.5 1.5 %collective-permute-start.18 = (bf16[2,32,768]{2,1,0:T(8,128)(2,1)S(1)}, bf16[2,32,768]{2,1,0:T(8,128)(2,1)S(1)}, u32[]{:S(2)}, u32[]{:S(2)}) collective-permute-start(bf16[2,32,768]{2,1,0:T(8,128)(2,1)S(1)} %get-tuple-element.55), channel_id=1, source_target_pairs={{0,8},{2,10},{4,12},{6,14},{8,0},{10,2},{12,4},{14,6},{16,24},{18,... | collective-permute-start | bytes 294920 | tf_op jit(solution)/shard_map/ppermute | solution.py:23
  46.0 3.4 %collective-permute-done.18 = bf16[2,32,768]{2,1,0:T(8,128)(2,1)S(1)} collective-permute-done((bf16[2,32,768]{2,1,0:T(8,128)(2,1)S(1)}, bf16[2,32,768]{2,1,0:T(8,128)(2,1)S(1)}, u32[]{:S(2)}, u32[]{:S(2)}) %collective-permute-start.18) | collective-permute-done | bytes 98336 | tf_op jit(solution)/shard_map/ppermute | solution.py:23
  49.4 0.7 %pad_maximum_fusion.7 = bf16[2,32,1536]{2,1,0:T(8,128)(2,1)} fusion(bf16[2,32,768]{2,1,0:T(8,128)(2,1)S(1)} %get-tuple-element.64, bf16[2,32,768]{2,1,0:T(8,128)(2,1)S(1)} %get-tuple-element.63), kind=kLoop, calls=%fused_computation.15 | loop fusion | flops 393216 | bytes 393216 | tf_op jit(solution)/shard_map/concatenate | solution.py:338
  (23 shorter events, 0.4 us)
Async XLA Ops:
  0.0 10.5 %collective-permute-start = (bf16[2,32,1536]{2,1,0:T(8,128)(2,1)}, bf16[2,32,1536]{2,1,0:T(8,128)(2,1)S(1)}, u32[]{:S(2)}, u32[]{:S(2)}) collective-permute-start(bf16[2,32,1536]{2,1,0:T(8,128)(2,1)} %x_ref.1), channel_id=1, source_target_pairs={{0,1},{1,0},{2,3},{3,2},{4,5},{5,4},{6,7},{7,6},{8,9},{9,8},{10,11... | collective-permute-start | bytes 589832 | tf_op jit(solution)/shard_map/ppermute | solution.py:23
  0.5 10.0 %collective-permute-start.1 = (f32[4,3,1536]{2,0,1:T(4,128)}, f32[4,3,1536]{2,0,1:T(4,128)S(1)}, u32[]{:S(2)}, u32[]{:S(2)}) collective-permute-start(f32[4,3,1536]{2,0,1:T(4,128)} %param.11), channel_id=1, source_target_pairs={{0,1},{1,0},{2,3},{3,2},{4,5},{5,4},{6,7},{7,6},{8,9},{9,8},{10,11... | collective-permute-start | bytes 221192 | tf_op jit(solution)/shard_map/ppermute | solution.py:23
  0.5 11.2 %collective-permute-start.2 = (bf16[192,256]{1,0:T(8,128)(2,1)}, bf16[192,256]{1,0:T(8,128)(2,1)S(1)}, u32[]{:S(2)}, u32[]{:S(2)}) collective-permute-start(bf16[192,256]{1,0:T(8,128)(2,1)} %bitcast.69), channel_id=1, source_target_pairs={{0,1},{2,3},{4,5},{6,7},{8,9},{10,11},{12,13},{14,15},{16,17},{18,... | collective-permute-start | bytes 294920 | tf_op jit(solution)/shard_map/ppermute | solution.py:265
  2.9 9.0 %collective-permute-start.3 = (bf16[192,256]{1,0:T(8,128)(2,1)}, bf16[192,256]{1,0:T(8,128)(2,1)S(1)}, u32[]{:S(2)}, u32[]{:S(2)}) collective-permute-start(bf16[192,256]{1,0:T(8,128)(2,1)} %bitcast.70), channel_id=1, source_target_pairs={{0,16},{2,18},{4,20},{6,22},{8,24},{10,26},{12,28},{14,30},{16,0},... | collective-permute-start | bytes 294920 | tf_op jit(solution)/shard_map/ppermute | solution.py:23
  6.5 9.4 %collective-permute-start.8 = (bf16[2,32,256]{2,1,0:T(8,128)(2,1)}, bf16[2,32,256]{2,1,0:T(8,128)(2,1)S(1)}, u32[]{:S(2)}, u32[]{:S(2)}) collective-permute-start(bf16[2,32,256]{2,1,0:T(8,128)(2,1)} %param.8), channel_id=1, source_target_pairs={{0,16},{2,18},{4,20},{6,22},{8,24},{10,26},{12,28},{14,30},{16,0},... | collective-permute-start | bytes 98312 | tf_op jit(solution)/shard_map/ppermute | solution.py:23
  7.3 9.7 %copy-start.1 = (bf16[2,32,256]{2,1,0:T(8,128)(2,1)S(1)}, bf16[2,32,256]{2,1,0:T(8,128)(2,1)}, u32[]{:S(2)}) copy-start(bf16[2,32,256]{2,1,0:T(8,128)(2,1)} %param.8) | copy-start | bytes 98308
  7.3 9.7 %copy-start = (bf16[256,192]{0,1:T(8,128)(2,1)S(1)}, bf16[256,192]{0,1:T(8,128)(2,1)}, u32[]{:S(2)}) copy-start(bf16[256,192]{0,1:T(8,128)(2,1)} %param.10) | copy-start | bytes 294916
  11.9 5.0 %collective-permute-start.9 = (bf16[2,32,256]{2,1,0:T(8,128)(2,1)S(1)}, bf16[2,32,256]{2,1,0:T(8,128)(2,1)S(1)}, u32[]{:S(2)}, u32[]{:S(2)}) collective-permute-start(bf16[2,32,256]{2,1,0:T(8,128)(2,1)S(1)} %get-tuple-element.44), channel_id=1, source_target_pairs={{0,16},{2,18},{4,20},{6,22},{8,24},{10,26},{12,28},{14,30},{16,0},... | collective-permute-start | bytes 98312 | tf_op jit(solution)/shard_map/ppermute | solution.py:23
  14.6 2.3 %collective-permute-start.5 = (bf16[1,192,256]{2,1,0:T(8,128)(2,1)S(1)}, bf16[1,192,256]{2,1,0:T(8,128)(2,1)S(1)}, u32[]{:S(2)}, u32[]{:S(2)}) collective-permute-start(bf16[1,192,256]{2,1,0:T(8,128)(2,1)S(1)} %bitcast.65), channel_id=1, source_target_pairs={{0,1},{2,3},{4,5},{6,7},{8,9},{10,11},{12,13},{14,15},{16,17},{18,... | collective-permute-start | bytes 294920 | tf_op jit(solution)/shard_map/ppermute | solution.py:265
  17.0 8.4 %collective-permute-start.4 = (bf16[2,192,256]{2,1,0:T(8,128)(2,1)S(1)}, bf16[2,192,256]{2,1,0:T(8,128)(2,1)S(1)}, u32[]{:S(2)}, u32[]{:S(2)}) collective-permute-start(bf16[2,192,256]{2,1,0:T(8,128)(2,1)S(1)} %get-tuple-element.76), channel_id=1, source_target_pairs={{1,3},{3,1},{5,7},{7,5},{9,11},{11,9},{13,15},{15,13},{17,19},{19,... | collective-permute-start | bytes 589832 | tf_op jit(solution)/shard_map/ppermute | solution.py:261
  17.7 7.7 %collective-permute-start.6 = (bf16[1,2,192,256]{3,2,1,0:T(8,128)(2,1)S(1)}, bf16[1,2,192,256]{3,2,1,0:T(8,128)(2,1)S(1)}, u32[]{:S(2)}, u32[]{:S(2)}) collective-permute-start(bf16[1,2,192,256]{3,2,1,0:T(8,128)(2,1)S(1)} %get-tuple-element.74), channel_id=1, source_target_pairs={{1,5},{3,7},{5,1},{7,3},{9,13},{11,15},{13,9},{15,11},{17,21},{19,... | collective-permute-start | bytes 589832 | tf_op jit(solution)/shard_map/ppermute | solution.py:261
  18.4 7.0 %collective-permute-start.10 = (bf16[2,4,32,256]{3,2,1,0:T(8,128)(2,1)S(1)}, bf16[2,4,32,256]{3,2,1,0:T(8,128)(2,1)S(1)}, u32[]{:S(2)}, u32[]{:S(2)}) collective-permute-start(bf16[2,4,32,256]{3,2,1,0:T(8,128)(2,1)S(1)} %pad_maximum_fusion.8.refs_0_), channel_id=1, source_target_pairs={{0,2},{2,0},{4,6},{6,4},{8,10},{10,8},{12,14},{14,12},{16,18},{18,... | collective-permute-start | bytes 393224 | tf_op jit(solution)/shard_map/ppermute | solution.py:23
  20.0 3.9 %collective-permute-start.7 = (bf16[2,32,256]{2,1,0:T(8,128)(2,1)S(1)}, bf16[2,32,256]{2,1,0:T(8,128)(2,1)S(1)}, u32[]{:S(2)}, u32[]{:S(2)}) collective-permute-start(bf16[2,32,256]{2,1,0:T(8,128)(2,1)S(1)} %get-tuple-element.37.q_ref), channel_id=1, source_target_pairs={{0,8},{2,10},{4,12},{6,14},{8,0},{10,2},{12,4},{14,6},{16,24},{18,... | collective-permute-start | bytes 98312 | tf_op jit(solution)/shard_map/ppermute | solution.py:23
  21.5 6.4 %collective-permute-start.11 = (bf16[2,4,32,256]{3,2,1,0:T(8,128)(2,1)S(1)}, bf16[2,4,32,256]{3,2,1,0:T(8,128)(2,1)S(1)}, u32[]{:S(2)}, u32[]{:S(2)}) collective-permute-start(bf16[2,4,32,256]{3,2,1,0:T(8,128)(2,1)S(1)} %pad_maximum_fusion.8.refs_0_), channel_id=1, source_target_pairs={{0,4},{2,6},{4,0},{6,2},{8,12},{10,14},{12,8},{14,10},{16,20},{18,... | collective-permute-start | bytes 393224 | tf_op jit(solution)/shard_map/ppermute | solution.py:23
  23.9 6.0 %collective-permute-start.12 = (bf16[2,4,32,256]{3,2,1,0:T(8,128)(2,1)S(1)}, bf16[2,4,32,256]{3,2,1,0:T(8,128)(2,1)S(1)}, u32[]{:S(2)}, u32[]{:S(2)}) collective-permute-start(bf16[2,4,32,256]{3,2,1,0:T(8,128)(2,1)S(1)} %pad_maximum_fusion.8.refs_0_), channel_id=1, source_target_pairs={{0,6},{2,4},{4,2},{6,0},{8,14},{10,12},{12,10},{14,8},{16,22},{18,... | collective-permute-start | bytes 393224 | tf_op jit(solution)/shard_map/ppermute | solution.py:23
  25.5 10.4 %collective-permute-start.15 = (bf16[2,1,2,192,256]{4,3,2,1,0:T(8,128)(2,1)S(1)}, bf16[2,1,2,192,256]{4,3,2,1,0:T(8,128)(2,1)S(1)}, u32[]{:S(2)}, u32[]{:S(2)}) collective-permute-start(bf16[2,1,2,192,256]{4,3,2,1,0:T(8,128)(2,1)S(1)} %pad_maximum_fusion.3), channel_id=1, source_target_pairs={{1,3},{3,1},{5,7},{7,5},{9,11},{11,9},{13,15},{15,13},{17,19},{19,... | collective-permute-start | bytes 1179656 | tf_op jit(solution)/shard_map/ppermute | solution.py:261
  26.2 9.7 %collective-permute-start.14 = (bf16[2,2,192,256]{3,2,1,0:T(8,128)(2,1)S(1)}, bf16[2,2,192,256]{3,2,1,0:T(8,128)(2,1)S(1)}, u32[]{:S(2)}, u32[]{:S(2)}) collective-permute-start(bf16[2,2,192,256]{3,2,1,0:T(8,128)(2,1)S(1)} %pad_maximum_fusion.2), channel_id=1, source_target_pairs={{1,5},{3,7},{5,1},{7,3},{9,13},{11,15},{13,9},{15,11},{17,21},{19,... | collective-permute-start | bytes 1179656 | tf_op jit(solution)/shard_map/ppermute | solution.py:261
  31.0 4.7 %collective-permute-start.13 = (bf16[128,384]{1,0:T(8,128)(2,1)S(1)}, bf16[128,384]{1,0:T(8,128)(2,1)S(1)}, u32[]{:S(2)}, u32[]{:S(2)}) collective-permute-start(bf16[128,384]{1,0:T(8,128)(2,1)S(1)} %shard_map.75.part_ref), channel_id=1, source_target_pairs={{0,8},{2,10},{4,12},{6,14},{8,0},{10,2},{12,4},{14,6},{16,24},{18,... | collective-permute-start | bytes 294920 | tf_op jit(solution)/shard_map/ppermute | solution.py:23
  36.2 6.2 %collective-permute-start.16 = (bf16[4,2,192,256]{3,2,1,0:T(8,128)(2,1)S(1)}, bf16[4,2,192,256]{3,2,1,0:T(8,128)(2,1)S(1)}, u32[]{:S(2)}, u32[]{:S(2)}) collective-permute-start(bf16[4,2,192,256]{3,2,1,0:T(8,128)(2,1)S(1)} %pad_maximum_fusion), channel_id=1, source_target_pairs={{1,0},{3,2},{5,4},{7,6},{9,8},{11,10},{13,12},{15,14},{17,16},{19,... | collective-permute-start | bytes 2359304 | tf_op jit(solution)/shard_map/ppermute | solution.py:269
  42.9 1.5 %collective-permute-start.17 = (bf16[128,768]{1,0:T(8,128)(2,1)S(1)}, bf16[128,768]{1,0:T(8,128)(2,1)S(1)}, u32[]{:S(2)}, u32[]{:S(2)}) collective-permute-start(bf16[128,768]{1,0:T(8,128)(2,1)S(1)} %shard_map.78), channel_id=1, source_target_pairs={{0,1},{1,0},{2,3},{3,2},{4,5},{5,4},{6,7},{7,6},{8,9},{9,8},{10,11... | collective-permute-start | bytes 589832 | tf_op jit(solution)/shard_map/ppermute | solution.py:23
  44.5 4.9 %collective-permute-start.18 = (bf16[2,32,768]{2,1,0:T(8,128)(2,1)S(1)}, bf16[2,32,768]{2,1,0:T(8,128)(2,1)S(1)}, u32[]{:S(2)}, u32[]{:S(2)}) collective-permute-start(bf16[2,32,768]{2,1,0:T(8,128)(2,1)S(1)} %get-tuple-element.55), channel_id=1, source_target_pairs={{0,8},{2,10},{4,12},{6,14},{8,0},{10,2},{12,4},{14,6},{16,24},{18,... | collective-permute-start | bytes 294920 | tf_op jit(solution)/shard_map/ppermute | solution.py:23

commit v16 on v9

--- a/solution.py
+++ b/solution.py
@@ -188,11 +188,13 @@
 
 
 def project_kernel(n_head, n_patch, bit, patch, head, *refs):
-    o_ref, w_refs, (out_ref, sums) = refs[0], refs[1 : 1 + PLANE], refs[1 + PLANE :]
+    o_ref, own_ref, next_ref, far_ref, out_ref, sums = refs
     slot = head[0] ^ bit ^ (patch[0] // (n_patch // n_head))
-    for near in range(PLANE):
+    odd = head[0] % 2
+    blocks = ((0, own_ref), (1 + odd, next_ref), (2 - odd, far_ref.at[0]), (3, far_ref.at[1]))
+    for near, w_ref in blocks:
         sums[(patch[0] % PLANE) ^ near] = lax.dot_general(
-            o_ref[...], w_refs[near][slot], NT, preferred_element_type=F32
+            o_ref[...], w_ref[slot], NT, preferred_element_type=F32
         )
     out = jnp.concatenate([sums[c] for c in range(PLANE)], axis=1)
     out_ref[...] = out.astype(out_ref.dtype)
@@ -259,6 +261,14 @@
 
     def plane_of(values):
         return [values] + [across(values, k) for k in range(1, PLANE)]
+
+    def turn(values, first):
+        pairs = [
+            (p * n_head + h, (p ^ (1 if (h % 2 == 0) == first else 2)) * n_head + h)
+            for p in range(n_patch)
+            for h in range(n_head)
+        ]
+        return lax.ppermute(values, ("patch", "head"), pairs)
 
     w_pair = line_of(w_out.T)
 
@@ -283,9 +293,12 @@
 
     kv_pair = line_of(kv)
     q_mate = across(q, PLANE)
-    w_pair, kv_pair, kv1 = lax.optimization_barrier((w_pair, kv_pair, kv1))
+    kv_pair, w_pair, kv1 = lax.optimization_barrier((kv_pair, w_pair, kv1))
+    w_pair = jnp.stack(w_pair)
+    w_next = turn(w_pair, True)
     kv_plane = plane_of(jnp.stack(kv_pair))
-    w_plane = plane_of(jnp.stack(w_pair))
+    w_next, q_mate, kv_plane = lax.optimization_barrier((w_next, q_mate, kv_plane))
+    w_far = turn(jnp.stack([w_pair, w_next]), False)
     tall = 2 * STEPS * rows
     part = call(
         attend_kernel,
@@ -300,11 +313,11 @@
         return call(
             functools.partial(project_kernel, n_head, n_patch, bit),
             shaped((tall, wide), dtype),
-            [SMEM] * 2 + [VMEM] * (1 + PLANE),
+            [SMEM] * 2 + [VMEM] * 4,
             [pltpu.VMEM((PLANE, tall, piece), F32)],
             2 * tall * wide * cols,
             2 * wide * cols,
-        )(patch[None], head[None], o, *w_plane)
+        )(patch[None], head[None], o, w_pair, w_next, w_far)
 
     sums = [swap(project(k, BF16), "head", n_head, k) for k in range(1, n_head)]
     sums = [project(0, F32)] + sums

time: 43.2 us -> 42.2 us (0.977)
  waiting for transfers between devices: 19.8 us -> 18.4 us
    ppermute x0 -> x2, starting transfers between devices: none -> 4.66 us  [turn(): return lax.ppermute(values, ('patch', 'head'), pairs)]
    ppermute x14 -> x11, starting transfers between devices: 13.3 us -> 8.97 us  [swap(): return lax.ppermute(values, axis, [(i, i ^ bit) for i in range(count)])]
    ppermute x14 -> x11, waiting for transfers between devices: 19.8 us -> 18.4 us  [swap(): return lax.ppermute(values, axis, [(i, i ^ bit) for i in range(count)])]
  transfers between devices with their start and end apart: 14 -> 13, of which waited for: 5 -> 6; matrix products, arithmetic and copies ran while one was open for 0% -> 0% of each run, Pallas kernels for 18% -> 19%
where the time goes in v16:
time: 42.2 us; the launch traced here: 42 us
  waiting for transfers between devices  18.4 us (44%)
  starting transfers between devices  13.6 us (32%)
  Pallas kernels  8.34 us (20%)
  between operations  0.8 us (2%)
  other arithmetic  0.79 us (2%)
    ppermute x11, waiting for transfers between devices, swap(): return lax.ppermute(values, axis, [(i, i ^ bit) for i in range(count)])  18.4 us
    ppermute x11, starting transfers between devices, swap(): return lax.ppermute(values, axis, [(i, i ^ bit) for i in range(count)])  8.97 us
    ppermute x2, starting transfers between devices, turn(): return lax.ppermute(values, ('patch', 'head'), pairs)  4.66 us
    pallas_call x1, Pallas kernels, body(): call(functools.partial(rest_kernel, n_head), (kv_shape, kv_shape), specs...  2.64 us
    pallas_call x1, Pallas kernels, body(): call(load_kernel, (pltpu.VMEM((2, *first[0].shape[1:]), BF16),) + tuple((...  2.6 us
    pallas_call x1, Pallas kernels, body(): call(attend_kernel, shaped((tall, cols + DH), BF16), [VMEM] * (3 + PLANE)...  1.11 us
    pallas_call x1, Pallas kernels, body(): call(functools.partial(fresh_kernel, n_head), (shaped((n_head, rows, feat...  0.85 us
  transfers between devices with their start and end apart: 13, of which 6 were waited for; matrix products, arithmetic and copies ran while one was open for 0% of the time, Pallas kernels for 19%

profile of v16, /device:TPU:0, one launch (start us, length us, event | category | flops | bytes accessed | tf_op | source)
XLA Modules:
  0.0 42.0 jit_solution(9792729588290292827)
XLA Ops:
  0.0 0.5 %collective-permute-start = (bf16[2,32,1536]{2,1,0:T(8,128)(2,1)}, bf16[2,32,1536]{2,1,0:T(8,128)(2,1)S(1)}, u32[]{:S(2)}, u32[]{:S(2)}) collective-permute-start(bf16[2,32,1536]{2,1,0:T(8,128)(2,1)} %x_ref.1), channel_id=1, source_target_pairs={{0,1},{1,0},{2,3},{3,2},{4,5},{5,4},{6,7},{7,6},{8,9},{9,8},{10,11... | collective-permute-start | bytes 589832 | tf_op jit(solution)/shard_map/ppermute | solution.py:23
  0.5 0.1 collective-permute-start.1
  0.5 4.0 %collective-permute-start.3 = (bf16[192,256]{1,0:T(8,128)(2,1)}, bf16[192,256]{1,0:T(8,128)(2,1)S(1)}, u32[]{:S(2)}, u32[]{:S(2)}) collective-permute-start(bf16[192,256]{1,0:T(8,128)(2,1)} %bitcast.19), channel_id=1, source_target_pairs={{0,16},{2,18},{4,20},{6,22},{8,24},{10,26},{12,28},{14,30},{16,0},... | collective-permute-start | bytes 294920 | tf_op jit(solution)/shard_map/ppermute | solution.py:23
  5.2 2.6 %shard_map.73 = (bf16[2,3072,256]{2,1,0:T(8,128)(2,1)S(1)}, bf16[2,32,1536]{2,1,0:T(8,128)(2,1)S(1)}, f32[3,4,1536]{2,1,0:T(4,128)S(1)}, bf16[2,32,256]{2,1,0:T(...) custom-call(s32[2]{0:T(128)} %ids.1, s32[1]{0:T(128)S(6)} %copy.8.slab, ...), custom_call_target="tpu_custom_call" | custom-call | bytes 4718592 | tf_op jit(solution)/shard_map/pallas_call | solution.py:244
  7.8 0.0 collective-permute-done.1
  7.8 0.0 collective-permute-done.refs_1_
  7.8 0.8 %shard_map.74 = (bf16[2,32,1536]{2,1,0:T(8,128)(2,1)S(1)}, bf16[4,32,256]{2,1,0:T(8,128)(2,1)S(1)}) custom-call(s32[1]{0:T(128)} %bitcast.3.head, s32[8,128]{1,0:T(8,128)S(1)} %get-tuple-element.29.ids_ref, bf16[2,32,1536]{2,1,0:T(8,128)(2,1)S(1)} %get-tuple-element.31.refs_0_, bf16[2,32,1536]{2,1,0:T(8,128)(2,1)S(1)} %collective-permute-done.refs_1_, ...), custom_call_target="tpu_custom_call" | custom-call | flops 100663296 | bytes 4718592 | tf_op jit(solution)/shard_map/pallas_call | solution.py:278
  8.7 0.0 copy-start
  8.7 0.1 collective-permute-start.2
  8.8 2.6 %shard_map.75 = (bf16[2,32,256]{2,1,0:T(8,128)(2,1)S(1)}, bf16[2,32,256]{2,1,0:T(8,128)(2,1)S(1)}) custom-call(s32[1]{0:T(128)} %bitcast.3.head, s32[8,128]{1,0:T(8,128)S(1)} %get-tuple-element.29.ids_ref, bf16[2,32,1536]{2,1,0:T(8,128)(2,1)S(1)} %get-tuple-element.31.refs_0_, bf16[2,32,1536]{2,1,0:T(8,128)(2,1)S(1)} %collective-permute-done.refs_1_, ...), custom_call_target="tpu_custom_call" | custom-call | flops 201326592 | bytes 4718592 | tf_op jit(solution)/shard_map/pallas_call | solution.py:285
  11.4 0.0 collective-permute-done.3
  11.4 3.7 %collective-permute-done.2 = bf16[4,32,256]{2,1,0:T(8,128)(2,1)S(1)} collective-permute-done((bf16[4,32,256]{2,1,0:T(8,128)(2,1)S(1)}, bf16[4,32,256]{2,1,0:T(8,128)(2,1)S(1)}, u32[]{:S(2)}, u32[]{:S(2)}) %collective-permute-start.2) | collective-permute-done | bytes 65568 | tf_op jit(solution)/shard_map/ppermute | solution.py:23
  15.1 0.0 copy-done
  15.1 1.6 %collective-permute-start.4 = (bf16[2,192,256]{2,1,0:T(8,128)(2,1)S(1)}, bf16[2,192,256]{2,1,0:T(8,128)(2,1)S(1)}, u32[]{:S(2)}, u32[]{:S(2)}) collective-permute-start(bf16[2,192,256]{2,1,0:T(8,128)(2,1)S(1)} %get-tuple-element.56.refs_1_), channel_id=1, source_target_pairs={{0,2},{1,5},{2,0},{3,7},{4,6},{5,1},{6,4},{7,3},{8,10},{9,13},{10,... | collective-permute-start | bytes 589832 | tf_op jit(solution)/shard_map/ppermute | solution.py:271
  16.7 0.6 %collective-permute-start.6 = (bf16[2,4,32,256]{3,2,1,0:T(8,128)(2,1)S(1)}, bf16[2,4,32,256]{3,2,1,0:T(8,128)(2,1)S(1)}, u32[]{:S(2)}, u32[]{:S(2)}) collective-permute-start(bf16[2,4,32,256]{3,2,1,0:T(8,128)(2,1)S(1)} %pad_maximum_fusion.3.refs_0_), channel_id=1, source_target_pairs={{0,2},{2,0},{4,6},{6,4},{8,10},{10,8},{12,14},{14,12},{16,18},{18,... | collective-permute-start | bytes 393224 | tf_op jit(solution)/shard_map/ppermute | solution.py:23
  17.3 1.5 %collective-permute-start.7 = (bf16[2,4,32,256]{3,2,1,0:T(8,128)(2,1)S(1)}, bf16[2,4,32,256]{3,2,1,0:T(8,128)(2,1)S(1)}, u32[]{:S(2)}, u32[]{:S(2)}) collective-permute-start(bf16[2,4,32,256]{3,2,1,0:T(8,128)(2,1)S(1)} %pad_maximum_fusion.3.refs_0_), channel_id=1, source_target_pairs={{0,4},{2,6},{4,0},{6,2},{8,12},{10,14},{12,8},{14,10},{16,20},{18,... | collective-permute-start | bytes 393224 | tf_op jit(solution)/shard_map/ppermute | solution.py:23
  18.8 1.4 %collective-permute-start.8 = (bf16[2,4,32,256]{3,2,1,0:T(8,128)(2,1)S(1)}, bf16[2,4,32,256]{3,2,1,0:T(8,128)(2,1)S(1)}, u32[]{:S(2)}, u32[]{:S(2)}) collective-permute-start(bf16[2,4,32,256]{3,2,1,0:T(8,128)(2,1)S(1)} %pad_maximum_fusion.3.refs_0_), channel_id=1, source_target_pairs={{0,6},{2,4},{4,2},{6,0},{8,14},{10,12},{12,10},{14,8},{16,22},{18,... | collective-permute-start | bytes 393224 | tf_op jit(solution)/shard_map/ppermute | solution.py:23
  20.3 0.5 %collective-permute-start.5 = (bf16[2,32,256]{2,1,0:T(8,128)(2,1)S(1)}, bf16[2,32,256]{2,1,0:T(8,128)(2,1)S(1)}, u32[]{:S(2)}, u32[]{:S(2)}) collective-permute-start(bf16[2,32,256]{2,1,0:T(8,128)(2,1)S(1)} %get-tuple-element.37.q_ref), channel_id=1, source_target_pairs={{0,8},{2,10},{4,12},{6,14},{8,0},{10,2},{12,4},{14,6},{16,24},{18,... | collective-permute-start | bytes 98312 | tf_op jit(solution)/shard_map/ppermute | solution.py:23
  20.8 3.4 %collective-permute-done.5.mate_ref = bf16[2,32,256]{2,1,0:T(8,128)(2,1)S(1)} collective-permute-done((bf16[2,32,256]{2,1,0:T(8,128)(2,1)S(1)}, bf16[2,32,256]{2,1,0:T(8,128)(2,1)S(1)}, u32[]{:S(2)}, u32[]{:S(2)}) %collective-permute-start.5) | collective-permute-done | bytes 32800 | tf_op jit(solution)/shard_map/ppermute | solution.py:23
  24.2 0.0 collective-permute-done.6.refs_1_
  24.2 0.0 collective-permute-done.7.refs_2_
  24.2 1.0 %collective-permute-done.8.refs_3_ = bf16[2,4,32,256]{3,2,1,0:T(8,128)(2,1)S(1)} collective-permute-done((bf16[2,4,32,256]{3,2,1,0:T(8,128)(2,1)S(1)}, bf16[2,4,32,256]{3,2,1,0:T(8,128)(2,1)S(1)}, u32[]{:S(2)}, u32[]{:S(2)}) %collective-permute-start.8) | collective-permute-done | bytes 131104 | tf_op jit(solution)/shard_map/ppermute | solution.py:23
  25.2 0.0 collective-permute-done.4.refs_2_
  25.2 3.1 %collective-permute-start.10 = (bf16[2,2,192,256]{3,2,1,0:T(8,128)(2,1)S(1)}, bf16[2,2,192,256]{3,2,1,0:T(8,128)(2,1)S(1)}, u32[]{:S(2)}, u32[]{:S(2)}) collective-permute-start(bf16[2,2,192,256]{3,2,1,0:T(8,128)(2,1)S(1)} %pad_maximum_fusion), channel_id=1, source_target_pairs={{0,4},{1,3},{2,6},{3,1},{4,0},{5,7},{6,2},{7,5},{8,12},{9,11},{10,... | collective-permute-start | bytes 1179656 | tf_op jit(solution)/shard_map/ppermute | solution.py:271
  28.3 1.1 %shard_map.76.part_ref = bf16[128,384]{1,0:T(8,128)(2,1)S(1)} custom-call(bf16[2,32,256]{2,1,0:T(8,128)(2,1)S(1)} %get-tuple-element.37.q_ref, bf16[2,32,256]{2,1,0:T(8,128)(2,1)S(1)} %collective-permute-done.5.mate_ref, bf16[2,32,256]{2,1,0:T(8,128)(2,1)S(1)} %get-tuple-element.45.kv1_ref, bf16[2,4,32,256]{3,2,1,0:T(8,128)(2,1)S(1)} %pad_maximum_fusion.3.refs_0_, ...), custom_call_target="tpu_custom_call" | custom-call | flops 33554432 | tf_op jit(solution)/shard_map/pallas_call | solution.py:303
  29.4 0.1 collective-permute-start.9
  29.5 4.6 %collective-permute-done.9.other_ref = bf16[128,384]{1,0:T(8,128)(2,1)S(1)} collective-permute-done((bf16[128,384]{1,0:T(8,128)(2,1)S(1)}, bf16[128,384]{1,0:T(8,128)(2,1)S(1)}, u32[]{:S(2)}, u32[]{:S(2)}) %collective-permute-start.9) | collective-permute-done | bytes 98336 | tf_op jit(solution)/shard_map/ppermute | solution.py:23
  34.1 0.2 shard_map.77.refs_0_
  34.3 0.0 collective-permute-done.10.refs_3_
  34.3 0.4 shard_map.79
  34.7 0.1 collective-permute-start.11
  34.8 0.4 %shard_map.78.refs_0_ = f32[128,768]{1,0:T(8,128)S(1)} custom-call(s32[1]{0:T(128)} %bitcast.patch, s32[1]{0:T(128)} %bitcast.3.head, bf16[128,256]{1,0:T(8,128)(2,1)S(1)} %shard_map.77.refs_0_, bf16[2,192,256]{2,1,0:T(8,128)(2,1)S(1)} %get-tuple-element.56.refs_1_, bf16[2,192,256]{2,1,0:T(8,128)(2,1)S(1)} %collective-permute-done.4.refs_2_, ...), custom_call_target="tpu_custom_call" | custom-call | flops 50331648 | bytes 393216 | tf_op jit(solution)/shard_map/pallas_call | solution.py:313
  35.2 1.0 %collective-permute-done.11.refs_1_ = bf16[128,768]{1,0:T(8,128)(2,1)S(1)} collective-permute-done((bf16[128,768]{1,0:T(8,128)(2,1)S(1)}, bf16[128,768]{1,0:T(8,128)(2,1)S(1)}, u32[]{:S(2)}, u32[]{:S(2)}) %collective-permute-start.11) | collective-permute-done | bytes 196640 | tf_op jit(solution)/shard_map/ppermute | solution.py:23
  36.2 0.1 shard_map.80
  36.4 0.1 collective-permute-start.12
  36.5 4.8 %collective-permute-done.12 = bf16[2,32,768]{2,1,0:T(8,128)(2,1)S(1)} collective-permute-done((bf16[2,32,768]{2,1,0:T(8,128)(2,1)S(1)}, bf16[2,32,768]{2,1,0:T(8,128)(2,1)S(1)}, u32[]{:S(2)}, u32[]{:S(2)}) %collective-permute-start.12) | collective-permute-done | bytes 98336 | tf_op jit(solution)/shard_map/ppermute | solution.py:23
  41.3 0.7 %pad_maximum_fusion.2 = bf16[2,32,1536]{2,1,0:T(8,128)(2,1)} fusion(bf16[2,32,768]{2,1,0:T(8,128)(2,1)S(1)} %get-tuple-element.54, bf16[2,32,768]{2,1,0:T(8,128)(2,1)S(1)} %get-tuple-element.53), kind=kLoop, calls=%fused_computation.2 | loop fusion | flops 393216 | bytes 393216 | tf_op jit(solution)/shard_map/concatenate | solution.py:332
  (4 shorter events, 0.1 us)
Async XLA Ops:
  0.0 7.8 %collective-permute-start = (bf16[2,32,1536]{2,1,0:T(8,128)(2,1)}, bf16[2,32,1536]{2,1,0:T(8,128)(2,1)S(1)}, u32[]{:S(2)}, u32[]{:S(2)}) collective-permute-start(bf16[2,32,1536]{2,1,0:T(8,128)(2,1)} %x_ref.1), channel_id=1, source_target_pairs={{0,1},{1,0},{2,3},{3,2},{4,5},{5,4},{6,7},{7,6},{8,9},{9,8},{10,11... | collective-permute-start | bytes 589832 | tf_op jit(solution)/shard_map/ppermute | solution.py:23
  0.5 7.4 %collective-permute-start.1 = (f32[4,3,1536]{2,0,1:T(4,128)}, f32[4,3,1536]{2,0,1:T(4,128)S(1)}, u32[]{:S(2)}, u32[]{:S(2)}) collective-permute-start(f32[4,3,1536]{2,0,1:T(4,128)} %param.11), channel_id=1, source_target_pairs={{0,1},{1,0},{2,3},{3,2},{4,5},{5,4},{6,7},{7,6},{8,9},{9,8},{10,11... | collective-permute-start | bytes 221192 | tf_op jit(solution)/shard_map/ppermute | solution.py:23
  0.5 10.9 %collective-permute-start.3 = (bf16[192,256]{1,0:T(8,128)(2,1)}, bf16[192,256]{1,0:T(8,128)(2,1)S(1)}, u32[]{:S(2)}, u32[]{:S(2)}) collective-permute-start(bf16[192,256]{1,0:T(8,128)(2,1)} %bitcast.19), channel_id=1, source_target_pairs={{0,16},{2,18},{4,20},{6,22},{8,24},{10,26},{12,28},{14,30},{16,0},... | collective-permute-start | bytes 294920 | tf_op jit(solution)/shard_map/ppermute | solution.py:23
  8.7 6.4 %copy-start = (bf16[256,192]{0,1:T(8,128)(2,1)S(1)}, bf16[256,192]{0,1:T(8,128)(2,1)}, u32[]{:S(2)}) copy-start(bf16[256,192]{0,1:T(8,128)(2,1)} %param.10) | copy-start | bytes 294916
  8.7 6.4 %collective-permute-start.2 = (bf16[4,32,256]{2,1,0:T(8,128)(2,1)S(1)}, bf16[4,32,256]{2,1,0:T(8,128)(2,1)S(1)}, u32[]{:S(2)}, u32[]{:S(2)}) collective-permute-start(bf16[4,32,256]{2,1,0:T(8,128)(2,1)S(1)} %get-tuple-element.42), channel_id=1, source_target_pairs={{0,16},{2,18},{4,20},{6,22},{8,24},{10,26},{12,28},{14,30},{16,0},... | collective-permute-start | bytes 196616 | tf_op jit(solution)/shard_map/ppermute | solution.py:23
  15.1 10.0 %collective-permute-start.4 = (bf16[2,192,256]{2,1,0:T(8,128)(2,1)S(1)}, bf16[2,192,256]{2,1,0:T(8,128)(2,1)S(1)}, u32[]{:S(2)}, u32[]{:S(2)}) collective-permute-start(bf16[2,192,256]{2,1,0:T(8,128)(2,1)S(1)} %get-tuple-element.56.refs_1_), channel_id=1, source_target_pairs={{0,2},{1,5},{2,0},{3,7},{4,6},{5,1},{6,4},{7,3},{8,10},{9,13},{10,... | collective-permute-start | bytes 589832 | tf_op jit(solution)/shard_map/ppermute | solution.py:271
  16.7 7.5 %collective-permute-start.6 = (bf16[2,4,32,256]{3,2,1,0:T(8,128)(2,1)S(1)}, bf16[2,4,32,256]{3,2,1,0:T(8,128)(2,1)S(1)}, u32[]{:S(2)}, u32[]{:S(2)}) collective-permute-start(bf16[2,4,32,256]{3,2,1,0:T(8,128)(2,1)S(1)} %pad_maximum_fusion.3.refs_0_), channel_id=1, source_target_pairs={{0,2},{2,0},{4,6},{6,4},{8,10},{10,8},{12,14},{14,12},{16,18},{18,... | collective-permute-start | bytes 393224 | tf_op jit(solution)/shard_map/ppermute | solution.py:23
  17.3 6.9 %collective-permute-start.7 = (bf16[2,4,32,256]{3,2,1,0:T(8,128)(2,1)S(1)}, bf16[2,4,32,256]{3,2,1,0:T(8,128)(2,1)S(1)}, u32[]{:S(2)}, u32[]{:S(2)}) collective-permute-start(bf16[2,4,32,256]{3,2,1,0:T(8,128)(2,1)S(1)} %pad_maximum_fusion.3.refs_0_), channel_id=1, source_target_pairs={{0,4},{2,6},{4,0},{6,2},{8,12},{10,14},{12,8},{14,10},{16,20},{18,... | collective-permute-start | bytes 393224 | tf_op jit(solution)/shard_map/ppermute | solution.py:23
  18.8 6.3 %collective-permute-start.8 = (bf16[2,4,32,256]{3,2,1,0:T(8,128)(2,1)S(1)}, bf16[2,4,32,256]{3,2,1,0:T(8,128)(2,1)S(1)}, u32[]{:S(2)}, u32[]{:S(2)}) collective-permute-start(bf16[2,4,32,256]{3,2,1,0:T(8,128)(2,1)S(1)} %pad_maximum_fusion.3.refs_0_), channel_id=1, source_target_pairs={{0,6},{2,4},{4,2},{6,0},{8,14},{10,12},{12,10},{14,8},{16,22},{18,... | collective-permute-start | bytes 393224 | tf_op jit(solution)/shard_map/ppermute | solution.py:23
  20.3 3.9 %collective-permute-start.5 = (bf16[2,32,256]{2,1,0:T(8,128)(2,1)S(1)}, bf16[2,32,256]{2,1,0:T(8,128)(2,1)S(1)}, u32[]{:S(2)}, u32[]{:S(2)}) collective-permute-start(bf16[2,32,256]{2,1,0:T(8,128)(2,1)S(1)} %get-tuple-element.37.q_ref), channel_id=1, source_target_pairs={{0,8},{2,10},{4,12},{6,14},{8,0},{10,2},{12,4},{14,6},{16,24},{18,... | collective-permute-start | bytes 98312 | tf_op jit(solution)/shard_map/ppermute | solution.py:23
  25.2 9.1 %collective-permute-start.10 = (bf16[2,2,192,256]{3,2,1,0:T(8,128)(2,1)S(1)}, bf16[2,2,192,256]{3,2,1,0:T(8,128)(2,1)S(1)}, u32[]{:S(2)}, u32[]{:S(2)}) collective-permute-start(bf16[2,2,192,256]{3,2,1,0:T(8,128)(2,1)S(1)} %pad_maximum_fusion), channel_id=1, source_target_pairs={{0,4},{1,3},{2,6},{3,1},{4,0},{5,7},{6,2},{7,5},{8,12},{9,11},{10,... | collective-permute-start | bytes 1179656 | tf_op jit(solution)/shard_map/ppermute | solution.py:271
  29.4 4.7 %collective-permute-start.9 = (bf16[128,384]{1,0:T(8,128)(2,1)S(1)}, bf16[128,384]{1,0:T(8,128)(2,1)S(1)}, u32[]{:S(2)}, u32[]{:S(2)}) collective-permute-start(bf16[128,384]{1,0:T(8,128)(2,1)S(1)} %shard_map.76.part_ref), channel_id=1, source_target_pairs={{0,8},{2,10},{4,12},{6,14},{8,0},{10,2},{12,4},{14,6},{16,24},{18,... | collective-permute-start | bytes 294920 | tf_op jit(solution)/shard_map/ppermute | solution.py:23
  34.7 1.5 %collective-permute-start.11 = (bf16[128,768]{1,0:T(8,128)(2,1)S(1)}, bf16[128,768]{1,0:T(8,128)(2,1)S(1)}, u32[]{:S(2)}, u32[]{:S(2)}) collective-permute-start(bf16[128,768]{1,0:T(8,128)(2,1)S(1)} %shard_map.79), channel_id=1, source_target_pairs={{0,1},{1,0},{2,3},{3,2},{4,5},{5,4},{6,7},{7,6},{8,9},{9,8},{10,11... | collective-permute-start | bytes 589832 | tf_op jit(solution)/shard_map/ppermute | solution.py:23
  36.4 4.9 %collective-permute-start.12 = (bf16[2,32,768]{2,1,0:T(8,128)(2,1)S(1)}, bf16[2,32,768]{2,1,0:T(8,128)(2,1)S(1)}, u32[]{:S(2)}, u32[]{:S(2)}) collective-permute-start(bf16[2,32,768]{2,1,0:T(8,128)(2,1)S(1)} %get-tuple-element.51), channel_id=1, source_target_pairs={{0,8},{2,10},{4,12},{6,14},{8,0},{10,2},{12,4},{14,6},{16,24},{18,... | collective-permute-start | bytes 294920 | tf_op jit(solution)/shard_map/ppermute | solution.py:23

commit v17 on v13

--- a/solution.py
+++ b/solution.py
@@ -117,8 +117,7 @@
 
 
 def attend_kernel(q_ref, mate_ref, kv1_ref, *refs):
-    own_ref, next_ref, far_ref, out_ref = refs
-    kv_refs = [own_ref, next_ref, far_ref.at[0], far_ref.at[1]]
+    kv_refs, out_ref = refs[:PLANE], refs[PLANE]
     blocks, _, rows, cols = kv_refs[0].shape
     old_rows = PLANE * blocks * rows
     shape = (2 * rows, old_rows + rows)
@@ -247,6 +246,9 @@
     def line_of(values):
         return [values] + [across(values, k) for k in range(2 * PLANE, n_patch, 2 * PLANE)]
 
+    def plane_of(values):
+        return [values] + [across(values, k) for k in range(1, PLANE)]
+
     def turn(values, first):
         pairs = [
             (p * n_head + h, (p ^ (1 if (h % 2 == 0) == first else 2)) * n_head + h)
@@ -255,6 +257,7 @@
         ]
         return lax.ppermute(values, ("patch", "head"), pairs)
 
+    w_pair = line_of(w_out.T)
 
     kv_shape = shaped((2, rows, cols), BF16)
     q, kv, kv1 = call(
@@ -265,21 +268,22 @@
         size=2 * w_qkv.size,
     )(head[None], ids, *x_parts, *mod_parts, w, cos, sin, stale)
 
-    w_pair, kv = lax.optimization_barrier((line_of(w_out.T), kv))
+    kv_pair = line_of(kv)
+    q_mate = across(q, PLANE)
+    w_pair, q = lax.optimization_barrier((w_pair, q))
     w_pair = jnp.stack(w_pair)
-    kv_pair = jnp.stack(line_of(kv))
-    q_mate = across(q, PLANE)
     w_next = turn(w_pair, True)
-    kv_next = turn(kv_pair, True)
-    kv_far = turn(jnp.stack([kv_pair, kv_next]), False)
+    kv_pair, q_mate = lax.optimization_barrier((kv_pair, q_mate))
+    kv_plane = plane_of(jnp.stack(kv_pair))
+    w_next, kv_plane = lax.optimization_barrier((w_next, kv_plane))
     w_far = turn(jnp.stack([w_pair, w_next]), False)
     tall = 2 * STEPS * rows
     part = call(
         attend_kernel,
         shaped((tall, cols + DH), BF16),
-        [VMEM] * 6,
+        [VMEM] * (3 + PLANE),
         flops=4 * STEPS * rows * n_patch * rows * cols,
-    )(q, q_mate, kv1, kv_pair, kv_next, kv_far)
+    )(q, q_mate, kv1, *kv_plane)
     o = call(merge_kernel, shaped((tall, cols), BF16), [VMEM] * 2)(part, across(part, PLANE))
     wide = PLANE * piece
 

time: 44.5 us -> 41.7 us (0.937)
  waiting for transfers between devices: 24.6 us -> 20.8 us
  starting transfers between devices: 11.5 us -> 12.5 us
    ppermute x4 -> x2, waiting for transfers between devices: 6.32 us -> 1.75 us  [turn(): return lax.ppermute(values, ('patch', 'head'), pairs)]
    ppermute x8 -> x11, starting transfers between devices: 7.24 us -> 10.8 us  [swap(): return lax.ppermute(values, axis, [(i, i ^ bit) for i in range(count)])]
    ppermute x4 -> x2, starting transfers between devices: 4.25 us -> 1.63 us  [turn(): return lax.ppermute(values, ('patch', 'head'), pairs)]
    ppermute x8 -> x11, waiting for transfers between devices: 18.3 us -> 19.1 us  [swap(): return lax.ppermute(values, axis, [(i, i ^ bit) for i in range(count)])]
  transfers between devices with their start and end apart: 12 -> 13, of which waited for: 8 -> 9; matrix products, arithmetic and copies ran while one was open for 0% -> 0% of each run, Pallas kernels for 14% -> 15%
where the time goes in v17:
time: 41.7 us; the launch traced here: 41.5 us
  waiting for transfers between devices  20.8 us (50%)
  starting transfers between devices  12.5 us (30%)
  Pallas kernels  6.62 us (16%)
  between operations  0.81 us (2%)
  other arithmetic  0.79 us (2%)
    ppermute x11, waiting for transfers between devices, swap(): return lax.ppermute(values, axis, [(i, i ^ bit) for i in range(count)])  19.1 us
    ppermute x11, starting transfers between devices, swap(): return lax.ppermute(values, axis, [(i, i ^ bit) for i in range(count)])  10.8 us
    pallas_call x1, Pallas kernels, body(): call(load_kernel, tuple((pltpu.VMEM(v.shape, v.dtype) for v in first)) +...  3.21 us
    ppermute x2, waiting for transfers between devices, turn(): return lax.ppermute(values, ('patch', 'head'), pairs)  1.75 us
    ppermute x2, starting transfers between devices, turn(): return lax.ppermute(values, ('patch', 'head'), pairs)  1.63 us
    pallas_call x1, Pallas kernels, body(): call(functools.partial(qkv_kernel, n_head), (kv_shape, shaped((4, rows, c...  1.16 us
    pallas_call x1, Pallas kernels, body(): call(attend_kernel, shaped((tall, cols + DH), BF16), [VMEM] * (3 + PLANE)...  1.11 us
  transfers between devices with their start and end apart: 13, of which 9 were waited for; matrix products, arithmetic and copies ran while one was open for 0% of the time, Pallas kernels for 15%

profile of v17, /device:TPU:0, one launch (start us, length us, event | category | flops | bytes accessed | tf_op | source)
XLA Modules:
  0.0 41.5 jit_solution(1270100047237457636)
XLA Ops:
  0.0 0.5 %collective-permute-start.1 = (bf16[2,32,1536]{2,1,0:T(8,128)(2,1)}, bf16[2,32,1536]{2,1,0:T(8,128)(2,1)S(1)}, u32[]{:S(2)}, u32[]{:S(2)}) collective-permute-start(bf16[2,32,1536]{2,1,0:T(8,128)(2,1)} %x_ref.1), channel_id=1, source_target_pairs={{0,1},{1,0},{2,3},{3,2},{4,5},{5,4},{6,7},{7,6},{8,9},{9,8},{10,11... | collective-permute-start | bytes 589832 | tf_op jit(solution)/shard_map/ppermute | solution.py:23
  0.5 0.1 collective-permute-start.2
  0.5 4.0 %collective-permute-start = (bf16[192,256]{1,0:T(8,128)(2,1)}, bf16[192,256]{1,0:T(8,128)(2,1)S(1)}, u32[]{:S(2)}, u32[]{:S(2)}) collective-permute-start(bf16[192,256]{1,0:T(8,128)(2,1)} %bitcast.17), channel_id=1, source_target_pairs={{0,16},{2,18},{4,20},{6,22},{8,24},{10,26},{12,28},{14,30},{16,0},... | collective-permute-start | bytes 294920 | tf_op jit(solution)/shard_map/ppermute | solution.py:23
  5.2 0.0 copy-start
  5.2 3.2 %shard_map.73 = (bf16[3,3072,256]{2,1,0:T(8,128)(2,1)S(1)}, bf16[2,32,1536]{2,1,0:T(8,128)(2,1)S(1)}, f32[3,4,1536]{2,1,0:T(4,128)S(1)}, bf16[2,32,256]{2,1,0:T(...) custom-call(s32[2]{0:T(128)} %ids.1, s32[1]{0:T(128)S(6)} %copy.8.slab, ...), custom_call_target="tpu_custom_call" | custom-call | bytes 4718592 | tf_op jit(solution)/shard_map/pallas_call | solution.py:232
  8.4 0.0 collective-permute-done.2
  8.4 0.0 collective-permute-done.1.refs_1_
  8.5 1.2 %shard_map.74 = (bf16[2,32,256]{2,1,0:T(8,128)(2,1)S(1)}, bf16[4,32,256]{2,1,0:T(8,128)(2,1)S(1)}, bf16[2,32,256]{2,1,0:T(8,128)(2,1)S(1)}) custom-call(s32[1]{0:T(128)} %bitcast.3.head, s32[8,128]{1,0:T(8,128)S(1)} %get-tuple-element.28.ids_ref, bf16[2,32,1536]{2,1,0:T(8,128)(2,1)S(1)} %get-tuple-element.30.refs_0_, ...), custom_call_target="tpu_custom_call" | custom-call | flops 301989888 | bytes 4718592 | tf_op jit(solution)/shard_map/pallas_call | solution.py:263
  9.6 0.1 collective-permute-start.3
  9.7 1.9 %collective-permute-start.4 = (bf16[2,32,256]{2,1,0:T(8,128)(2,1)S(1)}, bf16[2,32,256]{2,1,0:T(8,128)(2,1)S(1)}, u32[]{:S(2)}, u32[]{:S(2)}) collective-permute-start(bf16[2,32,256]{2,1,0:T(8,128)(2,1)S(1)} %get-tuple-element.36.q_ref), channel_id=1, source_target_pairs={{0,8},{2,10},{4,12},{6,14},{8,0},{10,2},{12,4},{14,6},{16,24},{18,... | collective-permute-start | bytes 98312 | tf_op jit(solution)/shard_map/ppermute | solution.py:23
  11.6 0.0 collective-permute-done
  11.6 0.0 copy-done
  11.6 1.6 %collective-permute-start.5 = (bf16[2,192,256]{2,1,0:T(8,128)(2,1)S(1)}, bf16[2,192,256]{2,1,0:T(8,128)(2,1)S(1)}, u32[]{:S(2)}, u32[]{:S(2)}) collective-permute-start(bf16[2,192,256]{2,1,0:T(8,128)(2,1)S(1)} %get-tuple-element.54.refs_1_), channel_id=1, source_target_pairs={{0,2},{1,5},{2,0},{3,7},{4,6},{5,1},{6,4},{7,3},{8,10},{9,13},{10,... | collective-permute-start | bytes 589832 | tf_op jit(solution)/shard_map/ppermute | solution.py:258
  13.2 0.8 %collective-permute-done.4.mate_ref = bf16[2,32,256]{2,1,0:T(8,128)(2,1)S(1)} collective-permute-done((bf16[2,32,256]{2,1,0:T(8,128)(2,1)S(1)}, bf16[2,32,256]{2,1,0:T(8,128)(2,1)S(1)}, u32[]{:S(2)}, u32[]{:S(2)}) %collective-permute-start.4) | collective-permute-done | bytes 32800 | tf_op jit(solution)/shard_map/ppermute | solution.py:23
  14.0 2.1 %collective-permute-done.3 = bf16[4,32,256]{2,1,0:T(8,128)(2,1)S(1)} collective-permute-done((bf16[4,32,256]{2,1,0:T(8,128)(2,1)S(1)}, bf16[4,32,256]{2,1,0:T(8,128)(2,1)S(1)}, u32[]{:S(2)}, u32[]{:S(2)}) %collective-permute-start.3) | collective-permute-done | bytes 65568 | tf_op jit(solution)/shard_map/ppermute | solution.py:23
  16.0 1.6 %collective-permute-start.6 = (bf16[2,4,32,256]{3,2,1,0:T(8,128)(2,1)S(1)}, bf16[2,4,32,256]{3,2,1,0:T(8,128)(2,1)S(1)}, u32[]{:S(2)}, u32[]{:S(2)}) collective-permute-start(bf16[2,4,32,256]{3,2,1,0:T(8,128)(2,1)S(1)} %pad_maximum_fusion.3.refs_0_), channel_id=1, source_target_pairs={{0,2},{2,0},{4,6},{6,4},{8,10},{10,8},{12,14},{14,12},{16,18},{18,... | collective-permute-start | bytes 393224 | tf_op jit(solution)/shard_map/ppermute | solution.py:23
  17.6 1.5 %collective-permute-start.7 = (bf16[2,4,32,256]{3,2,1,0:T(8,128)(2,1)S(1)}, bf16[2,4,32,256]{3,2,1,0:T(8,128)(2,1)S(1)}, u32[]{:S(2)}, u32[]{:S(2)}) collective-permute-start(bf16[2,4,32,256]{3,2,1,0:T(8,128)(2,1)S(1)} %pad_maximum_fusion.3.refs_0_), channel_id=1, source_target_pairs={{0,4},{2,6},{4,0},{6,2},{8,12},{10,14},{12,8},{14,10},{16,20},{18,... | collective-permute-start | bytes 393224 | tf_op jit(solution)/shard_map/ppermute | solution.py:23
  19.1 0.5 %collective-permute-start.8 = (bf16[2,4,32,256]{3,2,1,0:T(8,128)(2,1)S(1)}, bf16[2,4,32,256]{3,2,1,0:T(8,128)(2,1)S(1)}, u32[]{:S(2)}, u32[]{:S(2)}) collective-permute-start(bf16[2,4,32,256]{3,2,1,0:T(8,128)(2,1)S(1)} %pad_maximum_fusion.3.refs_0_), channel_id=1, source_target_pairs={{0,6},{2,4},{4,2},{6,0},{8,14},{10,12},{12,10},{14,8},{16,22},{18,... | collective-permute-start | bytes 393224 | tf_op jit(solution)/shard_map/ppermute | solution.py:23
  19.6 2.0 %collective-permute-done.6.refs_1_ = bf16[2,4,32,256]{3,2,1,0:T(8,128)(2,1)S(1)} collective-permute-done((bf16[2,4,32,256]{3,2,1,0:T(8,128)(2,1)S(1)}, bf16[2,4,32,256]{3,2,1,0:T(8,128)(2,1)S(1)}, u32[]{:S(2)}, u32[]{:S(2)}) %collective-permute-start.6) | collective-permute-done | bytes 131104 | tf_op jit(solution)/shard_map/ppermute | solution.py:23
  21.6 1.2 %collective-permute-done.7.refs_2_ = bf16[2,4,32,256]{3,2,1,0:T(8,128)(2,1)S(1)} collective-permute-done((bf16[2,4,32,256]{3,2,1,0:T(8,128)(2,1)S(1)}, bf16[2,4,32,256]{3,2,1,0:T(8,128)(2,1)S(1)}, u32[]{:S(2)}, u32[]{:S(2)}) %collective-permute-start.7) | collective-permute-done | bytes 131104 | tf_op jit(solution)/shard_map/ppermute | solution.py:23
  22.8 3.2 %collective-permute-done.8.refs_3_ = bf16[2,4,32,256]{3,2,1,0:T(8,128)(2,1)S(1)} collective-permute-done((bf16[2,4,32,256]{3,2,1,0:T(8,128)(2,1)S(1)}, bf16[2,4,32,256]{3,2,1,0:T(8,128)(2,1)S(1)}, u32[]{:S(2)}, u32[]{:S(2)}) %collective-permute-start.8) | collective-permute-done | bytes 131104 | tf_op jit(solution)/shard_map/ppermute | solution.py:23
  26.0 0.0 collective-permute-done.5.refs_2_
  26.0 0.1 collective-permute-start.10
  26.1 1.1 %shard_map.75.part_ref = bf16[128,384]{1,0:T(8,128)(2,1)S(1)} custom-call(bf16[2,32,256]{2,1,0:T(8,128)(2,1)S(1)} %get-tuple-element.36.q_ref, bf16[2,32,256]{2,1,0:T(8,128)(2,1)S(1)} %collective-permute-done.4.mate_ref, bf16[2,32,256]{2,1,0:T(8,128)(2,1)S(1)} %get-tuple-element.39.kv1_ref, bf16[2,4,32,256]{3,2,1,0:T(8,128)(2,1)S(1)} %pad_maximum_fusion.3.refs_0_, ...), custom_call_target="tpu_custom_call" | custom-call | flops 33554432 | tf_op jit(solution)/shard_map/pallas_call | solution.py:281
  27.2 0.6 %collective-permute-start.9 = (bf16[128,384]{1,0:T(8,128)(2,1)S(1)}, bf16[128,384]{1,0:T(8,128)(2,1)S(1)}, u32[]{:S(2)}, u32[]{:S(2)}) collective-permute-start(bf16[128,384]{1,0:T(8,128)(2,1)S(1)} %shard_map.75.part_ref), channel_id=1, source_target_pairs={{0,8},{2,10},{4,12},{6,14},{8,0},{10,2},{12,4},{14,6},{16,24},{18,... | collective-permute-start | bytes 294920 | tf_op jit(solution)/shard_map/ppermute | solution.py:23
  27.9 4.1 %collective-permute-done.9.other_ref = bf16[128,384]{1,0:T(8,128)(2,1)S(1)} collective-permute-done((bf16[128,384]{1,0:T(8,128)(2,1)S(1)}, bf16[128,384]{1,0:T(8,128)(2,1)S(1)}, u32[]{:S(2)}, u32[]{:S(2)}) %collective-permute-start.9) | collective-permute-done | bytes 98336 | tf_op jit(solution)/shard_map/ppermute | solution.py:23
  31.9 0.2 shard_map.76.refs_0_
  32.1 1.8 %collective-permute-done.10.refs_3_ = bf16[2,2,192,256]{3,2,1,0:T(8,128)(2,1)S(1)} collective-permute-done((bf16[2,2,192,256]{3,2,1,0:T(8,128)(2,1)S(1)}, bf16[2,2,192,256]{3,2,1,0:T(8,128)(2,1)S(1)}, u32[]{:S(2)}, u32[]{:S(2)}) %collective-permute-start.10) | collective-permute-done | bytes 393248 | tf_op jit(solution)/shard_map/ppermute | solution.py:258
  33.9 0.4 shard_map.78
  34.3 0.1 collective-permute-start.11
  34.3 0.4 %shard_map.77.refs_0_ = f32[128,768]{1,0:T(8,128)S(1)} custom-call(s32[1]{0:T(128)} %bitcast.patch, s32[1]{0:T(128)} %bitcast.3.head, bf16[128,256]{1,0:T(8,128)(2,1)S(1)} %shard_map.76.refs_0_, bf16[2,192,256]{2,1,0:T(8,128)(2,1)S(1)} %get-tuple-element.54.refs_1_, bf16[2,192,256]{2,1,0:T(8,128)(2,1)S(1)} %collective-permute-done.5.refs_2_, ...), custom_call_target="tpu_custom_call" | custom-call | flops 50331648 | bytes 393216 | tf_op jit(solution)/shard_map/pallas_call | solution.py:291
  34.8 1.0 %collective-permute-done.11.refs_1_ = bf16[128,768]{1,0:T(8,128)(2,1)S(1)} collective-permute-done((bf16[128,768]{1,0:T(8,128)(2,1)S(1)}, bf16[128,768]{1,0:T(8,128)(2,1)S(1)}, u32[]{:S(2)}, u32[]{:S(2)}) %collective-permute-start.11) | collective-permute-done | bytes 196640 | tf_op jit(solution)/shard_map/ppermute | solution.py:23
  35.8 0.1 shard_map.79
  35.9 0.1 collective-permute-start.12
  36.0 4.8 %collective-permute-done.12 = bf16[2,32,768]{2,1,0:T(8,128)(2,1)S(1)} collective-permute-done((bf16[2,32,768]{2,1,0:T(8,128)(2,1)S(1)}, bf16[2,32,768]{2,1,0:T(8,128)(2,1)S(1)}, u32[]{:S(2)}, u32[]{:S(2)}) %collective-permute-start.12) | collective-permute-done | bytes 98336 | tf_op jit(solution)/shard_map/ppermute | solution.py:23
  40.8 0.7 %pad_maximum_fusion.2 = bf16[2,32,1536]{2,1,0:T(8,128)(2,1)} fusion(bf16[2,32,768]{2,1,0:T(8,128)(2,1)S(1)} %get-tuple-element.52, bf16[2,32,768]{2,1,0:T(8,128)(2,1)S(1)} %get-tuple-element.51), kind=kLoop, calls=%fused_computation.2 | loop fusion | flops 393216 | bytes 393216 | tf_op jit(solution)/shard_map/concatenate | solution.py:310
  (4 shorter events, 0.1 us)
Async XLA Ops:
  0.0 8.4 %collective-permute-start.1 = (bf16[2,32,1536]{2,1,0:T(8,128)(2,1)}, bf16[2,32,1536]{2,1,0:T(8,128)(2,1)S(1)}, u32[]{:S(2)}, u32[]{:S(2)}) collective-permute-start(bf16[2,32,1536]{2,1,0:T(8,128)(2,1)} %x_ref.1), channel_id=1, source_target_pairs={{0,1},{1,0},{2,3},{3,2},{4,5},{5,4},{6,7},{7,6},{8,9},{9,8},{10,11... | collective-permute-start | bytes 589832 | tf_op jit(solution)/shard_map/ppermute | solution.py:23
  0.5 8.0 %collective-permute-start.2 = (f32[4,3,1536]{2,0,1:T(4,128)}, f32[4,3,1536]{2,0,1:T(4,128)S(1)}, u32[]{:S(2)}, u32[]{:S(2)}) collective-permute-start(f32[4,3,1536]{2,0,1:T(4,128)} %param.11), channel_id=1, source_target_pairs={{0,1},{1,0},{2,3},{3,2},{4,5},{5,4},{6,7},{7,6},{8,9},{9,8},{10,11... | collective-permute-start | bytes 221192 | tf_op jit(solution)/shard_map/ppermute | solution.py:23
  0.5 11.1 %collective-permute-start = (bf16[192,256]{1,0:T(8,128)(2,1)}, bf16[192,256]{1,0:T(8,128)(2,1)S(1)}, u32[]{:S(2)}, u32[]{:S(2)}) collective-permute-start(bf16[192,256]{1,0:T(8,128)(2,1)} %bitcast.17), channel_id=1, source_target_pairs={{0,16},{2,18},{4,20},{6,22},{8,24},{10,26},{12,28},{14,30},{16,0},... | collective-permute-start | bytes 294920 | tf_op jit(solution)/shard_map/ppermute | solution.py:23
  5.2 6.4 %copy-start = (bf16[256,192]{0,1:T(8,128)(2,1)S(1)}, bf16[256,192]{0,1:T(8,128)(2,1)}, u32[]{:S(2)}) copy-start(bf16[256,192]{0,1:T(8,128)(2,1)} %param.10) | copy-start | bytes 294916
  9.6 6.4 %collective-permute-start.3 = (bf16[4,32,256]{2,1,0:T(8,128)(2,1)S(1)}, bf16[4,32,256]{2,1,0:T(8,128)(2,1)S(1)}, u32[]{:S(2)}, u32[]{:S(2)}) collective-permute-start(bf16[4,32,256]{2,1,0:T(8,128)(2,1)S(1)} %get-tuple-element.42), channel_id=1, source_target_pairs={{0,16},{2,18},{4,20},{6,22},{8,24},{10,26},{12,28},{14,30},{16,0},... | collective-permute-start | bytes 196616 | tf_op jit(solution)/shard_map/ppermute | solution.py:23
  9.7 4.3 %collective-permute-start.4 = (bf16[2,32,256]{2,1,0:T(8,128)(2,1)S(1)}, bf16[2,32,256]{2,1,0:T(8,128)(2,1)S(1)}, u32[]{:S(2)}, u32[]{:S(2)}) collective-permute-start(bf16[2,32,256]{2,1,0:T(8,128)(2,1)S(1)} %get-tuple-element.36.q_ref), channel_id=1, source_target_pairs={{0,8},{2,10},{4,12},{6,14},{8,0},{10,2},{12,4},{14,6},{16,24},{18,... | collective-permute-start | bytes 98312 | tf_op jit(solution)/shard_map/ppermute | solution.py:23
  11.6 14.4 %collective-permute-start.5 = (bf16[2,192,256]{2,1,0:T(8,128)(2,1)S(1)}, bf16[2,192,256]{2,1,0:T(8,128)(2,1)S(1)}, u32[]{:S(2)}, u32[]{:S(2)}) collective-permute-start(bf16[2,192,256]{2,1,0:T(8,128)(2,1)S(1)} %get-tuple-element.54.refs_1_), channel_id=1, source_target_pairs={{0,2},{1,5},{2,0},{3,7},{4,6},{5,1},{6,4},{7,3},{8,10},{9,13},{10,... | collective-permute-start | bytes 589832 | tf_op jit(solution)/shard_map/ppermute | solution.py:258
  16.0 5.5 %collective-permute-start.6 = (bf16[2,4,32,256]{3,2,1,0:T(8,128)(2,1)S(1)}, bf16[2,4,32,256]{3,2,1,0:T(8,128)(2,1)S(1)}, u32[]{:S(2)}, u32[]{:S(2)}) collective-permute-start(bf16[2,4,32,256]{3,2,1,0:T(8,128)(2,1)S(1)} %pad_maximum_fusion.3.refs_0_), channel_id=1, source_target_pairs={{0,2},{2,0},{4,6},{6,4},{8,10},{10,8},{12,14},{14,12},{16,18},{18,... | collective-permute-start | bytes 393224 | tf_op jit(solution)/shard_map/ppermute | solution.py:23
  17.6 5.2 %collective-permute-start.7 = (bf16[2,4,32,256]{3,2,1,0:T(8,128)(2,1)S(1)}, bf16[2,4,32,256]{3,2,1,0:T(8,128)(2,1)S(1)}, u32[]{:S(2)}, u32[]{:S(2)}) collective-permute-start(bf16[2,4,32,256]{3,2,1,0:T(8,128)(2,1)S(1)} %pad_maximum_fusion.3.refs_0_), channel_id=1, source_target_pairs={{0,4},{2,6},{4,0},{6,2},{8,12},{10,14},{12,8},{14,10},{16,20},{18,... | collective-permute-start | bytes 393224 | tf_op jit(solution)/shard_map/ppermute | solution.py:23
  19.1 6.9 %collective-permute-start.8 = (bf16[2,4,32,256]{3,2,1,0:T(8,128)(2,1)S(1)}, bf16[2,4,32,256]{3,2,1,0:T(8,128)(2,1)S(1)}, u32[]{:S(2)}, u32[]{:S(2)}) collective-permute-start(bf16[2,4,32,256]{3,2,1,0:T(8,128)(2,1)S(1)} %pad_maximum_fusion.3.refs_0_), channel_id=1, source_target_pairs={{0,6},{2,4},{4,2},{6,0},{8,14},{10,12},{12,10},{14,8},{16,22},{18,... | collective-permute-start | bytes 393224 | tf_op jit(solution)/shard_map/ppermute | solution.py:23
  26.0 7.8 %collective-permute-start.10 = (bf16[2,2,192,256]{3,2,1,0:T(8,128)(2,1)S(1)}, bf16[2,2,192,256]{3,2,1,0:T(8,128)(2,1)S(1)}, u32[]{:S(2)}, u32[]{:S(2)}) collective-permute-start(bf16[2,2,192,256]{3,2,1,0:T(8,128)(2,1)S(1)} %pad_maximum_fusion), channel_id=1, source_target_pairs={{0,4},{1,3},{2,6},{3,1},{4,0},{5,7},{6,2},{7,5},{8,12},{9,11},{10,... | collective-permute-start | bytes 1179656 | tf_op jit(solution)/shard_map/ppermute | solution.py:258
  27.2 4.7 %collective-permute-start.9 = (bf16[128,384]{1,0:T(8,128)(2,1)S(1)}, bf16[128,384]{1,0:T(8,128)(2,1)S(1)}, u32[]{:S(2)}, u32[]{:S(2)}) collective-permute-start(bf16[128,384]{1,0:T(8,128)(2,1)S(1)} %shard_map.75.part_ref), channel_id=1, source_target_pairs={{0,8},{2,10},{4,12},{6,14},{8,0},{10,2},{12,4},{14,6},{16,24},{18,... | collective-permute-start | bytes 294920 | tf_op jit(solution)/shard_map/ppermute | solution.py:23
  34.3 1.5 %collective-permute-start.11 = (bf16[128,768]{1,0:T(8,128)(2,1)S(1)}, bf16[128,768]{1,0:T(8,128)(2,1)S(1)}, u32[]{:S(2)}, u32[]{:S(2)}) collective-permute-start(bf16[128,768]{1,0:T(8,128)(2,1)S(1)} %shard_map.78), channel_id=1, source_target_pairs={{0,1},{1,0},{2,3},{3,2},{4,5},{5,4},{6,7},{7,6},{8,9},{9,8},{10,11... | collective-permute-start | bytes 589832 | tf_op jit(solution)/shard_map/ppermute | solution.py:23
  35.9 4.9 %collective-permute-start.12 = (bf16[2,32,768]{2,1,0:T(8,128)(2,1)S(1)}, bf16[2,32,768]{2,1,0:T(8,128)(2,1)S(1)}, u32[]{:S(2)}, u32[]{:S(2)}) collective-permute-start(bf16[2,32,768]{2,1,0:T(8,128)(2,1)S(1)} %get-tuple-element.49), channel_id=1, source_target_pairs={{0,8},{2,10},{4,12},{6,14},{8,0},{10,2},{12,4},{14,6},{16,24},{18,... | collective-permute-start | bytes 294920 | tf_op jit(solution)/shard_map/ppermute | solution.py:23

commit v18 on v14

--- a/solution.py
+++ b/solution.py
@@ -116,9 +116,11 @@
 
 
 def attend_kernel(q_ref, mate_ref, kv1_ref, *refs):
-    own_ref, next_ref, far_ref, out_ref = refs
-    kv_refs = [own_ref, next_ref, far_ref.at[0], far_ref.at[1]]
+    own_ref, next_ref, far_ref = refs[:3]
+    cargo_refs = [own_ref, next_ref, far_ref.at[0], far_ref.at[1]]
+    kv_refs, out_ref = refs[3 : 3 + PLANE], refs[3 + PLANE]
     blocks, _, rows, cols = kv_refs[0].shape
+    skip = own_ref.shape[1] - 2 * rows
     old_rows = PLANE * blocks * rows
     shape = (2 * rows, old_rows + rows)
     mine = lax.broadcasted_iota(jnp.int32, shape, 0) < rows
@@ -126,14 +128,19 @@
     drop = lax.broadcasted_iota(jnp.int32, shape, 1) // rows == stray
     lane = lax.broadcasted_iota(jnp.int32, (2 * rows, DH), 1)
     for step in range(STEPS):
-        fresh = (kv_refs[0].at[0, 2:], kv1_ref)[step]
+        fresh = (kv_refs[0].at[0], kv1_ref)[step]
         stats = jnp.zeros((2 * rows, DH), F32)
         mixed = []
         for head in range(cols // DH):
             lanes = slice(head * DH, (head + 1) * DH)
 
             def rows_of(kind):
-                old = [ref[:, 2 * step + kind, :, lanes].reshape(blocks * rows, DH) for ref in kv_refs]
+                if step:
+                    old = [ref[:, kind, :, lanes] for ref in kv_refs]
+                else:
+                    spot = slice(skip + kind * rows, skip + (kind + 1) * rows)
+                    old = [ref[:, spot, lanes] for ref in cargo_refs]
+                old = [piece.reshape(blocks * rows, DH) for piece in old]
                 return jnp.concatenate([*old, fresh[kind, :, lanes]], axis=0)
 
             queries = jnp.concatenate([q_ref[step, :, lanes], mate_ref[step, :, lanes]], axis=0)
@@ -182,7 +189,7 @@
     blocks = ((0, own_ref), (1 + odd, next_ref), (2 - odd, far_ref.at[0]), (3, far_ref.at[1]))
     for near, w_ref in blocks:
         sums[(patch[0] % PLANE) ^ near] = lax.dot_general(
-            o_ref[...], w_ref[slot], NT, preferred_element_type=F32
+            o_ref[...], w_ref[slot, : sums.shape[2], :], NT, preferred_element_type=F32
         )
     out = jnp.concatenate([sums[c] for c in range(PLANE)], axis=1)
     out_ref[...] = out.astype(out_ref.dtype)
@@ -246,6 +253,9 @@
     def line_of(values):
         return [values] + [across(values, k) for k in range(2 * PLANE, n_patch, 2 * PLANE)]
 
+    def plane_of(values):
+        return [values] + [across(values, k) for k in range(1, PLANE)]
+
     def turn(values, first):
         pairs = [
             (p * n_head + h, (p ^ (1 if (h % 2 == 0) == first else 2)) * n_head + h)
@@ -254,6 +264,7 @@
         ]
         return lax.ppermute(values, ("patch", "head"), pairs)
 
+    w_pair = line_of(w_out.T)
 
     stale_pair = line_of(stale_kv)
     kv_shape = shaped((2, rows, cols), BF16)
@@ -265,24 +276,27 @@
         size=2 * w_qkv.size,
     )(head[None], ids, *x_parts, *mod_parts, w, cos, sin)
 
-    w_pair, kv = lax.optimization_barrier((line_of(w_out.T), kv))
-    w_pair = jnp.stack(w_pair)
-    stale_pair, kv_line = lax.optimization_barrier((stale_pair, line_of(kv)))
-    kv_pair = jnp.stack([jnp.concatenate(pair) for pair in zip(stale_pair, kv_line)])
+    kv_pair = line_of(kv)
     q_mate = across(q, PLANE)
-    w_next = turn(w_pair, True)
-    kv_next = turn(kv_pair, True)
-    kv_next, w_next, q_mate = lax.optimization_barrier((kv_next, w_next, q_mate))
-    kv_far = turn(jnp.stack([kv_pair, kv_next]), False)
-    w_next, kv_far = lax.optimization_barrier((w_next, kv_far))
-    w_far = turn(jnp.stack([w_pair, w_next]), False)
+    w_pair, stale_pair, q = lax.optimization_barrier((w_pair, stale_pair, q))
+    cargo = jnp.stack(
+        [
+            jnp.concatenate([w_block, kv_block.reshape(2 * rows, cols)])
+            for w_block, kv_block in zip(w_pair, stale_pair)
+        ]
+    )
+    next_cargo = turn(cargo, True)
+    kv_pair, q_mate = lax.optimization_barrier((kv_pair, q_mate))
+    kv_plane = plane_of(jnp.stack(kv_pair))
+    next_cargo, kv_pair = lax.optimization_barrier((next_cargo, kv_pair))
+    far_cargo = turn(jnp.stack([cargo, next_cargo]), False)
     tall = 2 * STEPS * rows
     part = call(
         attend_kernel,
         shaped((tall, cols + DH), BF16),
-        [VMEM] * 6,
+        [VMEM] * (6 + PLANE),
         flops=4 * STEPS * rows * n_patch * rows * cols,
-    )(q, q_mate, kv1, kv_pair, kv_next, kv_far)
+    )(q, q_mate, kv1, cargo, next_cargo, far_cargo, *kv_plane)
     o = call(merge_kernel, shaped((tall, cols), BF16), [VMEM] * 2)(part, across(part, PLANE))
     wide = PLANE * piece
 
@@ -294,7 +308,7 @@
             [pltpu.VMEM((PLANE, tall, piece), F32)],
             2 * tall * wide * cols,
             2 * wide * cols,
-        )(patch[None], head[None], o, w_pair, w_next, w_far)
+        )(patch[None], head[None], o, cargo, next_cargo, far_cargo)
 
     sums = [swap(project(k, BF16), "head", n_head, k) for k in range(1, n_head)]
     sums = [project(0, F32)] + sums

time: 43.4 us -> 45.1 us (1.039)
  starting transfers between devices: 15.6 us -> 19.6 us
  waiting for transfers between devices: 19.5 us -> 17.1 us
    ppermute x9 -> x12, starting transfers between devices: 9.23 us -> 16.4 us  [swap(): return lax.ppermute(values, axis, [(i, i ^ bit) for i in range(count)])]
    ppermute x4 -> x2, waiting for transfers between devices: 5.11 us -> 0.01 us  [turn(): return lax.ppermute(values, ('patch', 'head'), pairs)]
    ppermute x4 -> x2, starting transfers between devices: 6.35 us -> 3.19 us  [turn(): return lax.ppermute(values, ('patch', 'head'), pairs)]
    ppermute x9 -> x12, waiting for transfers between devices: 14.4 us -> 17.1 us  [swap(): return lax.ppermute(values, axis, [(i, i ^ bit) for i in range(count)])]
  transfers between devices with their start and end apart: 13 -> 14, of which waited for: 8 -> 9; matrix products, arithmetic and copies ran while one was open for 0% -> 0% of each run, Pallas kernels for 14% -> 11%
where the time goes in v18:
time: 45.1 us; the launch traced here: 44.9 us
  starting transfers between devices  19.6 us (43%)
  waiting for transfers between devices  17.1 us (38%)
  Pallas kernels  6.62 us (15%)
  other arithmetic  0.82 us (2%)
  between operations  0.78 us (2%)
    ppermute x12, waiting for transfers between devices, swap(): return lax.ppermute(values, axis, [(i, i ^ bit) for i in range(count)])  17.1 us
    ppermute x12, starting transfers between devices, swap(): return lax.ppermute(values, axis, [(i, i ^ bit) for i in range(count)])  16.4 us
    pallas_call x1, Pallas kernels, body(): call(load_kernel, tuple((pltpu.VMEM(v.shape, v.dtype) for v in first)) +...  3.2 us
    ppermute x2, starting transfers between devices, turn(): return lax.ppermute(values, ('patch', 'head'), pairs)  3.19 us
    pallas_call x1, Pallas kernels, body(): call(functools.partial(qkv_kernel, n_head), (kv_shape,) * 3, [SMEM] + [VM...  1.16 us
    pallas_call x1, Pallas kernels, body(): call(attend_kernel, shaped((tall, cols + DH), BF16), [VMEM] * (6 + PLANE)...  1.11 us
  transfers between devices with their start and end apart: 14, of which 9 were waited for; matrix products, arithmetic and copies ran while one was open for 0% of the time, Pallas kernels for 11%

profile of v18, /device:TPU:0, one launch (start us, length us, event | category | flops | bytes accessed | tf_op | source)
XLA Modules:
  0.0 44.9 jit_solution(13542387801297630276)
XLA Ops:
  0.0 0.5 %collective-permute-start.2 = (bf16[2,32,1536]{2,1,0:T(8,128)(2,1)}, bf16[2,32,1536]{2,1,0:T(8,128)(2,1)S(1)}, u32[]{:S(2)}, u32[]{:S(2)}) collective-permute-start(bf16[2,32,1536]{2,1,0:T(8,128)(2,1)} %x_ref.1), channel_id=1, source_target_pairs={{0,1},{1,0},{2,3},{3,2},{4,5},{5,4},{6,7},{7,6},{8,9},{9,8},{10,11... | collective-permute-start | bytes 589832 | tf_op jit(solution)/shard_map/ppermute | solution.py:23
  0.5 0.1 collective-permute-start.3
  0.5 4.0 %collective-permute-start = (bf16[192,256]{1,0:T(8,128)(2,1)}, bf16[192,256]{1,0:T(8,128)(2,1)S(1)}, u32[]{:S(2)}, u32[]{:S(2)}) collective-permute-start(bf16[192,256]{1,0:T(8,128)(2,1)} %bitcast.21), channel_id=1, source_target_pairs={{0,16},{2,18},{4,20},{6,22},{8,24},{10,26},{12,28},{14,30},{16,0},... | collective-permute-start | bytes 294920 | tf_op jit(solution)/shard_map/ppermute | solution.py:23
  4.5 0.0 collective-permute-start.1
  5.2 0.0 copy-start
  5.2 0.0 copy-start.1
  5.3 3.2 %shard_map.73 = (bf16[3,3072,256]{2,1,0:T(8,128)(2,1)S(1)}, bf16[2,32,1536]{2,1,0:T(8,128)(2,1)S(1)}, f32[3,4,1536]{2,1,0:T(4,128)S(1)}, s32[8,128]{1,0:T(8,128)...) custom-call(s32[2]{0:T(128)} %ids.1, s32[1]{0:T(128)S(6)} %copy.8.slab, bf16[3,3072,256]{2,1,0:T(8,128)(2,1)} %bitcast.20, ...), custom_call_target="tpu_custom_call" | custom-call | bytes 4718592 | tf_op jit(solution)/shard_map/pallas_call | solution.py:239
  8.5 0.0 collective-permute-done.3
  8.5 0.0 collective-permute-done.2.refs_1_
  8.5 1.2 %shard_map.74 = (bf16[2,32,256]{2,1,0:T(8,128)(2,1)S(1)}, bf16[2,32,256]{2,1,0:T(8,128)(2,1)S(1)}, bf16[2,32,256]{2,1,0:T(8,128)(2,1)S(1)}) custom-call(s32[1]{0:T(128)} %bitcast.3.head, s32[8,128]{1,0:T(8,128)S(1)} %get-tuple-element.25.ids_ref, bf16[2,32,1536]{2,1,0:T(8,128)(2,1)S(1)} %get-tuple-element.27.refs_0_, ...), custom_call_target="tpu_custom_call" | custom-call | flops 301989888 | bytes 4718592 | tf_op jit(solution)/shard_map/pallas_call | solution.py:271
  9.7 1.6 %collective-permute-done.1 = bf16[2,32,256]{2,1,0:T(8,128)(2,1)S(1)} collective-permute-done((bf16[2,32,256]{2,1,0:T(8,128)(2,1)}, bf16[2,32,256]{2,1,0:T(8,128)(2,1)S(1)}, u32[]{:S(2)}, u32[]{:S(2)}) %collective-permute-start.1) | collective-permute-done | bytes 32800 | tf_op jit(solution)/shard_map/ppermute | solution.py:23
  11.2 0.0 collective-permute-done
  11.2 0.0 copy-done
  11.2 0.0 copy-done.1
  11.3 1.6 %collective-permute-start.6 = (bf16[2,256,256]{2,1,0:T(8,128)(2,1)S(1)}, bf16[2,256,256]{2,1,0:T(8,128)(2,1)S(1)}, u32[]{:S(2)}, u32[]{:S(2)}) collective-permute-start(bf16[2,256,256]{2,1,0:T(8,128)(2,1)S(1)} %get-tuple-element.46.refs_0_.refs_1_), channel_id=1, source_target_pairs={{0,2},{1,5},{2,0},{3,7},{4,6},{5,1},{6,4},{7,3},{8,10},{9,13},{10,... | collective-permute-start | bytes 786440 | tf_op jit(solution)/shard_map/ppermute | solution.py:265
  12.9 1.3 %collective-permute-start.4 = (bf16[2,32,256]{2,1,0:T(8,128)(2,1)S(1)}, bf16[2,32,256]{2,1,0:T(8,128)(2,1)S(1)}, u32[]{:S(2)}, u32[]{:S(2)}) collective-permute-start(bf16[2,32,256]{2,1,0:T(8,128)(2,1)S(1)} %get-tuple-element.40), channel_id=1, source_target_pairs={{0,16},{2,18},{4,20},{6,22},{8,24},{10,26},{12,28},{14,30},{16,0},... | collective-permute-start | bytes 98312 | tf_op jit(solution)/shard_map/ppermute | solution.py:23
  14.2 2.8 %collective-permute-start.5 = (bf16[2,32,256]{2,1,0:T(8,128)(2,1)S(1)}, bf16[2,32,256]{2,1,0:T(8,128)(2,1)S(1)}, u32[]{:S(2)}, u32[]{:S(2)}) collective-permute-start(bf16[2,32,256]{2,1,0:T(8,128)(2,1)S(1)} %get-tuple-element.32.q_ref), channel_id=1, source_target_pairs={{0,8},{2,10},{4,12},{6,14},{8,0},{10,2},{12,4},{14,6},{16,24},{18,... | collective-permute-start | bytes 98312 | tf_op jit(solution)/shard_map/ppermute | solution.py:23
  17.0 0.9 %collective-permute-done.4 = bf16[2,32,256]{2,1,0:T(8,128)(2,1)S(1)} collective-permute-done((bf16[2,32,256]{2,1,0:T(8,128)(2,1)S(1)}, bf16[2,32,256]{2,1,0:T(8,128)(2,1)S(1)}, u32[]{:S(2)}, u32[]{:S(2)}) %collective-permute-start.4) | collective-permute-done | bytes 32800 | tf_op jit(solution)/shard_map/ppermute | solution.py:23
  17.8 1.0 %collective-permute-done.5.mate_ref = bf16[2,32,256]{2,1,0:T(8,128)(2,1)S(1)} collective-permute-done((bf16[2,32,256]{2,1,0:T(8,128)(2,1)S(1)}, bf16[2,32,256]{2,1,0:T(8,128)(2,1)S(1)}, u32[]{:S(2)}, u32[]{:S(2)}) %collective-permute-start.5) | collective-permute-done | bytes 32800 | tf_op jit(solution)/shard_map/ppermute | solution.py:23
  18.9 0.0 collective-permute-done.6.refs_1_.refs_2_
  18.9 0.1 pad_maximum_fusion
  18.9 1.6 %collective-permute-start.7 = (bf16[2,2,256,256]{3,2,1,0:T(8,128)(2,1)S(1)}, bf16[2,2,256,256]{3,2,1,0:T(8,128)(2,1)S(1)}, u32[]{:S(2)}, u32[]{:S(2)}) collective-permute-start(bf16[2,2,256,256]{3,2,1,0:T(8,128)(2,1)S(1)} %pad_maximum_fusion), channel_id=1, source_target_pairs={{0,4},{1,3},{2,6},{3,1},{4,0},{5,7},{6,2},{7,5},{8,12},{9,11},{10,... | collective-permute-start | bytes 1572872 | tf_op jit(solution)/shard_map/ppermute | solution.py:265
  20.5 0.6 %collective-permute-start.10 = (bf16[2,2,32,256]{3,2,1,0:T(8,128)(2,1)S(1)}, bf16[2,2,32,256]{3,2,1,0:T(8,128)(2,1)S(1)}, u32[]{:S(2)}, u32[]{:S(2)}) collective-permute-start(bf16[2,2,32,256]{3,2,1,0:T(8,128)(2,1)S(1)} %pad_maximum_fusion.3.refs_3_), channel_id=1, source_target_pairs={{0,6},{2,4},{4,2},{6,0},{8,14},{10,12},{12,10},{14,8},{16,22},{18,... | collective-permute-start | bytes 196616 | tf_op jit(solution)/shard_map/ppermute | solution.py:23
  21.2 1.4 %collective-permute-start.8 = (bf16[2,2,32,256]{3,2,1,0:T(8,128)(2,1)S(1)}, bf16[2,2,32,256]{3,2,1,0:T(8,128)(2,1)S(1)}, u32[]{:S(2)}, u32[]{:S(2)}) collective-permute-start(bf16[2,2,32,256]{3,2,1,0:T(8,128)(2,1)S(1)} %pad_maximum_fusion.3.refs_3_), channel_id=1, source_target_pairs={{0,2},{2,0},{4,6},{6,4},{8,10},{10,8},{12,14},{14,12},{16,18},{18,... | collective-permute-start | bytes 196616 | tf_op jit(solution)/shard_map/ppermute | solution.py:23
  22.5 1.5 %collective-permute-start.9 = (bf16[2,2,32,256]{3,2,1,0:T(8,128)(2,1)S(1)}, bf16[2,2,32,256]{3,2,1,0:T(8,128)(2,1)S(1)}, u32[]{:S(2)}, u32[]{:S(2)}) collective-permute-start(bf16[2,2,32,256]{3,2,1,0:T(8,128)(2,1)S(1)} %pad_maximum_fusion.3.refs_3_), channel_id=1, source_target_pairs={{0,4},{2,6},{4,0},{6,2},{8,12},{10,14},{12,8},{14,10},{16,20},{18,... | collective-permute-start | bytes 196616 | tf_op jit(solution)/shard_map/ppermute | solution.py:23
  24.1 2.4 %collective-permute-done.10.refs_6_ = bf16[2,2,32,256]{3,2,1,0:T(8,128)(2,1)S(1)} collective-permute-done((bf16[2,2,32,256]{3,2,1,0:T(8,128)(2,1)S(1)}, bf16[2,2,32,256]{3,2,1,0:T(8,128)(2,1)S(1)}, u32[]{:S(2)}, u32[]{:S(2)}) %collective-permute-start.10) | collective-permute-done | bytes 65568 | tf_op jit(solution)/shard_map/ppermute | solution.py:23
  26.5 0.4 collective-permute-done.8.refs_4_
  27.0 4.0 %collective-permute-done.9.refs_5_ = bf16[2,2,32,256]{3,2,1,0:T(8,128)(2,1)S(1)} collective-permute-done((bf16[2,2,32,256]{3,2,1,0:T(8,128)(2,1)S(1)}, bf16[2,2,32,256]{3,2,1,0:T(8,128)(2,1)S(1)}, u32[]{:S(2)}, u32[]{:S(2)}) %collective-permute-start.9) | collective-permute-done | bytes 65568 | tf_op jit(solution)/shard_map/ppermute | solution.py:23
  31.0 0.0 collective-permute-done.7.refs_2_.refs_3_
  31.0 1.1 %shard_map.75.part_ref = bf16[128,384]{1,0:T(8,128)(2,1)S(1)} custom-call(bf16[2,32,256]{2,1,0:T(8,128)(2,1)S(1)} %get-tuple-element.32.q_ref, bf16[2,32,256]{2,1,0:T(8,128)(2,1)S(1)} %collective-permute-done.5.mate_ref, bf16[2,32,256]{2,1,0:T(8,128)(2,1)S(1)} %get-tuple-element.35.kv1_ref, bf16[2,256,256]{2,1,0:T(8,128)(2,1)S(1)} %get-tuple-element.46.refs_0_.refs_1_, ...), custom_call_target="tpu_custom_call" | custom-call | flops 33554432 | tf_op jit(solution)/shard_map/pallas_call | solution.py:294
  32.1 2.1 %collective-permute-start.11 = (bf16[128,384]{1,0:T(8,128)(2,1)S(1)}, bf16[128,384]{1,0:T(8,128)(2,1)S(1)}, u32[]{:S(2)}, u32[]{:S(2)}) collective-permute-start(bf16[128,384]{1,0:T(8,128)(2,1)S(1)} %shard_map.75.part_ref), channel_id=1, source_target_pairs={{0,8},{2,10},{4,12},{6,14},{8,0},{10,2},{12,4},{14,6},{16,24},{18,... | collective-permute-start | bytes 294920 | tf_op jit(solution)/shard_map/ppermute | solution.py:23
  34.2 2.6 %collective-permute-done.11.other_ref = bf16[128,384]{1,0:T(8,128)(2,1)S(1)} collective-permute-done((bf16[128,384]{1,0:T(8,128)(2,1)S(1)}, bf16[128,384]{1,0:T(8,128)(2,1)S(1)}, u32[]{:S(2)}, u32[]{:S(2)}) %collective-permute-start.11) | collective-permute-done | bytes 98336 | tf_op jit(solution)/shard_map/ppermute | solution.py:23
  36.8 0.2 shard_map.76.refs_0_
  37.0 0.4 shard_map.78
  37.4 0.1 collective-permute-start.12
  37.5 0.4 shard_map.77.refs_0_
  37.9 1.0 %collective-permute-done.12.refs_1_ = bf16[128,768]{1,0:T(8,128)(2,1)S(1)} collective-permute-done((bf16[128,768]{1,0:T(8,128)(2,1)S(1)}, bf16[128,768]{1,0:T(8,128)(2,1)S(1)}, u32[]{:S(2)}, u32[]{:S(2)}) %collective-permute-start.12) | collective-permute-done | bytes 196640 | tf_op jit(solution)/shard_map/ppermute | solution.py:23
  38.9 0.1 shard_map.79
  39.0 2.1 %collective-permute-start.13 = (bf16[2,32,768]{2,1,0:T(8,128)(2,1)S(1)}, bf16[2,32,768]{2,1,0:T(8,128)(2,1)S(1)}, u32[]{:S(2)}, u32[]{:S(2)}) collective-permute-start(bf16[2,32,768]{2,1,0:T(8,128)(2,1)S(1)} %get-tuple-element.43), channel_id=1, source_target_pairs={{0,8},{2,10},{4,12},{6,14},{8,0},{10,2},{12,4},{14,6},{16,24},{18,... | collective-permute-start | bytes 294920 | tf_op jit(solution)/shard_map/ppermute | solution.py:23
  41.1 3.1 %collective-permute-done.13 = bf16[2,32,768]{2,1,0:T(8,128)(2,1)S(1)} collective-permute-done((bf16[2,32,768]{2,1,0:T(8,128)(2,1)S(1)}, bf16[2,32,768]{2,1,0:T(8,128)(2,1)S(1)}, u32[]{:S(2)}, u32[]{:S(2)}) %collective-permute-start.13) | collective-permute-done | bytes 98336 | tf_op jit(solution)/shard_map/ppermute | solution.py:23
  44.2 0.7 %pad_maximum_fusion.2 = bf16[2,32,1536]{2,1,0:T(8,128)(2,1)} fusion(bf16[2,32,768]{2,1,0:T(8,128)(2,1)S(1)} %get-tuple-element.48, bf16[2,32,768]{2,1,0:T(8,128)(2,1)S(1)} %get-tuple-element.47), kind=kLoop, calls=%fused_computation.2 | loop fusion | flops 393216 | bytes 393216 | tf_op jit(solution)/shard_map/concatenate | solution.py:323
  (4 shorter events, 0.1 us)
Async XLA Ops:
  0.0 8.5 %collective-permute-start.2 = (bf16[2,32,1536]{2,1,0:T(8,128)(2,1)}, bf16[2,32,1536]{2,1,0:T(8,128)(2,1)S(1)}, u32[]{:S(2)}, u32[]{:S(2)}) collective-permute-start(bf16[2,32,1536]{2,1,0:T(8,128)(2,1)} %x_ref.1), channel_id=1, source_target_pairs={{0,1},{1,0},{2,3},{3,2},{4,5},{5,4},{6,7},{7,6},{8,9},{9,8},{10,11... | collective-permute-start | bytes 589832 | tf_op jit(solution)/shard_map/ppermute | solution.py:23
  0.5 8.0 %collective-permute-start.3 = (f32[4,3,1536]{2,0,1:T(4,128)}, f32[4,3,1536]{2,0,1:T(4,128)S(1)}, u32[]{:S(2)}, u32[]{:S(2)}) collective-permute-start(f32[4,3,1536]{2,0,1:T(4,128)} %param.11), channel_id=1, source_target_pairs={{0,1},{1,0},{2,3},{3,2},{4,5},{5,4},{6,7},{7,6},{8,9},{9,8},{10,11... | collective-permute-start | bytes 221192 | tf_op jit(solution)/shard_map/ppermute | solution.py:23
  0.5 10.7 %collective-permute-start = (bf16[192,256]{1,0:T(8,128)(2,1)}, bf16[192,256]{1,0:T(8,128)(2,1)S(1)}, u32[]{:S(2)}, u32[]{:S(2)}) collective-permute-start(bf16[192,256]{1,0:T(8,128)(2,1)} %bitcast.21), channel_id=1, source_target_pairs={{0,16},{2,18},{4,20},{6,22},{8,24},{10,26},{12,28},{14,30},{16,0},... | collective-permute-start | bytes 294920 | tf_op jit(solution)/shard_map/ppermute | solution.py:23
  4.5 6.7 %collective-permute-start.1 = (bf16[2,32,256]{2,1,0:T(8,128)(2,1)}, bf16[2,32,256]{2,1,0:T(8,128)(2,1)S(1)}, u32[]{:S(2)}, u32[]{:S(2)}) collective-permute-start(bf16[2,32,256]{2,1,0:T(8,128)(2,1)} %param.8), channel_id=1, source_target_pairs={{0,16},{2,18},{4,20},{6,22},{8,24},{10,26},{12,28},{14,30},{16,0},... | collective-permute-start | bytes 98312 | tf_op jit(solution)/shard_map/ppermute | solution.py:23
  5.2 6.0 %copy-start = (bf16[256,192]{0,1:T(8,128)(2,1)S(1)}, bf16[256,192]{0,1:T(8,128)(2,1)}, u32[]{:S(2)}) copy-start(bf16[256,192]{0,1:T(8,128)(2,1)} %param.10) | copy-start | bytes 294916
  5.2 6.0 %copy-start.1 = (bf16[2,32,256]{2,1,0:T(8,128)(2,1)S(1)}, bf16[2,32,256]{2,1,0:T(8,128)(2,1)}, u32[]{:S(2)}) copy-start(bf16[2,32,256]{2,1,0:T(8,128)(2,1)} %param.8) | copy-start | bytes 98308
  11.3 7.6 %collective-permute-start.6 = (bf16[2,256,256]{2,1,0:T(8,128)(2,1)S(1)}, bf16[2,256,256]{2,1,0:T(8,128)(2,1)S(1)}, u32[]{:S(2)}, u32[]{:S(2)}) collective-permute-start(bf16[2,256,256]{2,1,0:T(8,128)(2,1)S(1)} %get-tuple-element.46.refs_0_.refs_1_), channel_id=1, source_target_pairs={{0,2},{1,5},{2,0},{3,7},{4,6},{5,1},{6,4},{7,3},{8,10},{9,13},{10,... | collective-permute-start | bytes 786440 | tf_op jit(solution)/shard_map/ppermute | solution.py:265
  12.9 4.9 %collective-permute-start.4 = (bf16[2,32,256]{2,1,0:T(8,128)(2,1)S(1)}, bf16[2,32,256]{2,1,0:T(8,128)(2,1)S(1)}, u32[]{:S(2)}, u32[]{:S(2)}) collective-permute-start(bf16[2,32,256]{2,1,0:T(8,128)(2,1)S(1)} %get-tuple-element.40), channel_id=1, source_target_pairs={{0,16},{2,18},{4,20},{6,22},{8,24},{10,26},{12,28},{14,30},{16,0},... | collective-permute-start | bytes 98312 | tf_op jit(solution)/shard_map/ppermute | solution.py:23
  14.2 4.7 %collective-permute-start.5 = (bf16[2,32,256]{2,1,0:T(8,128)(2,1)S(1)}, bf16[2,32,256]{2,1,0:T(8,128)(2,1)S(1)}, u32[]{:S(2)}, u32[]{:S(2)}) collective-permute-start(bf16[2,32,256]{2,1,0:T(8,128)(2,1)S(1)} %get-tuple-element.32.q_ref), channel_id=1, source_target_pairs={{0,8},{2,10},{4,12},{6,14},{8,0},{10,2},{12,4},{14,6},{16,24},{18,... | collective-permute-start | bytes 98312 | tf_op jit(solution)/shard_map/ppermute | solution.py:23
  18.9 12.1 %collective-permute-start.7 = (bf16[2,2,256,256]{3,2,1,0:T(8,128)(2,1)S(1)}, bf16[2,2,256,256]{3,2,1,0:T(8,128)(2,1)S(1)}, u32[]{:S(2)}, u32[]{:S(2)}) collective-permute-start(bf16[2,2,256,256]{3,2,1,0:T(8,128)(2,1)S(1)} %pad_maximum_fusion), channel_id=1, source_target_pairs={{0,4},{1,3},{2,6},{3,1},{4,0},{5,7},{6,2},{7,5},{8,12},{9,11},{10,... | collective-permute-start | bytes 1572872 | tf_op jit(solution)/shard_map/ppermute | solution.py:265
  20.5 6.0 %collective-permute-start.10 = (bf16[2,2,32,256]{3,2,1,0:T(8,128)(2,1)S(1)}, bf16[2,2,32,256]{3,2,1,0:T(8,128)(2,1)S(1)}, u32[]{:S(2)}, u32[]{:S(2)}) collective-permute-start(bf16[2,2,32,256]{3,2,1,0:T(8,128)(2,1)S(1)} %pad_maximum_fusion.3.refs_3_), channel_id=1, source_target_pairs={{0,6},{2,4},{4,2},{6,0},{8,14},{10,12},{12,10},{14,8},{16,22},{18,... | collective-permute-start | bytes 196616 | tf_op jit(solution)/shard_map/ppermute | solution.py:23
  21.2 5.8 %collective-permute-start.8 = (bf16[2,2,32,256]{3,2,1,0:T(8,128)(2,1)S(1)}, bf16[2,2,32,256]{3,2,1,0:T(8,128)(2,1)S(1)}, u32[]{:S(2)}, u32[]{:S(2)}) collective-permute-start(bf16[2,2,32,256]{3,2,1,0:T(8,128)(2,1)S(1)} %pad_maximum_fusion.3.refs_3_), channel_id=1, source_target_pairs={{0,2},{2,0},{4,6},{6,4},{8,10},{10,8},{12,14},{14,12},{16,18},{18,... | collective-permute-start | bytes 196616 | tf_op jit(solution)/shard_map/ppermute | solution.py:23
  22.5 8.4 %collective-permute-start.9 = (bf16[2,2,32,256]{3,2,1,0:T(8,128)(2,1)S(1)}, bf16[2,2,32,256]{3,2,1,0:T(8,128)(2,1)S(1)}, u32[]{:S(2)}, u32[]{:S(2)}) collective-permute-start(bf16[2,2,32,256]{3,2,1,0:T(8,128)(2,1)S(1)} %pad_maximum_fusion.3.refs_3_), channel_id=1, source_target_pairs={{0,4},{2,6},{4,0},{6,2},{8,12},{10,14},{12,8},{14,10},{16,20},{18,... | collective-permute-start | bytes 196616 | tf_op jit(solution)/shard_map/ppermute | solution.py:23
  32.1 4.7 %collective-permute-start.11 = (bf16[128,384]{1,0:T(8,128)(2,1)S(1)}, bf16[128,384]{1,0:T(8,128)(2,1)S(1)}, u32[]{:S(2)}, u32[]{:S(2)}) collective-permute-start(bf16[128,384]{1,0:T(8,128)(2,1)S(1)} %shard_map.75.part_ref), channel_id=1, source_target_pairs={{0,8},{2,10},{4,12},{6,14},{8,0},{10,2},{12,4},{14,6},{16,24},{18,... | collective-permute-start | bytes 294920 | tf_op jit(solution)/shard_map/ppermute | solution.py:23
  37.4 1.5 %collective-permute-start.12 = (bf16[128,768]{1,0:T(8,128)(2,1)S(1)}, bf16[128,768]{1,0:T(8,128)(2,1)S(1)}, u32[]{:S(2)}, u32[]{:S(2)}) collective-permute-start(bf16[128,768]{1,0:T(8,128)(2,1)S(1)} %shard_map.78), channel_id=1, source_target_pairs={{0,1},{1,0},{2,3},{3,2},{4,5},{5,4},{6,7},{7,6},{8,9},{9,8},{10,11... | collective-permute-start | bytes 589832 | tf_op jit(solution)/shard_map/ppermute | solution.py:23
  39.0 5.2 %collective-permute-start.13 = (bf16[2,32,768]{2,1,0:T(8,128)(2,1)S(1)}, bf16[2,32,768]{2,1,0:T(8,128)(2,1)S(1)}, u32[]{:S(2)}, u32[]{:S(2)}) collective-permute-start(bf16[2,32,768]{2,1,0:T(8,128)(2,1)S(1)} %get-tuple-element.43), channel_id=1, source_target_pairs={{0,8},{2,10},{4,12},{6,14},{8,0},{10,2},{12,4},{14,6},{16,24},{18,... | collective-permute-start | bytes 294920 | tf_op jit(solution)/shard_map/ppermute | solution.py:23

commit v19 on v11

--- a/solution.py
+++ b/solution.py
@@ -261,9 +261,10 @@
     kv_pair = line_of(kv)
     q_mate = across(q, PLANE)
     w_x = across(w_own, 1)
-    w_rest = jnp.stack(line_of(w_own)[1:])
+    w_late, q_mate = lax.optimization_barrier((w_own, q_mate))
+    w_rest = jnp.stack(line_of(w_late)[1:])
     kv_plane = plane_of(jnp.stack(kv_pair))
-    w_x, w_rest, q_mate = lax.optimization_barrier((w_x, w_rest, q_mate))
+    w_rest, q_mate = lax.optimization_barrier((w_rest, q_mate))
     w_y = across(jnp.stack([w_own, w_x]), 2)
     rest_y = across(w_rest, 2)
     rest_y, *kv_plane[1:] = lax.optimization_barrier((rest_y, *kv_plane[1:]))

time: 41.6 us -> 41.8 us (level)
  waiting for transfers between devices: 13.1 us -> 16.6 us
  starting transfers between devices: 19.9 us -> 16.6 us
    ppermute x15, waiting for transfers between devices: 13.1 us -> 16.6 us  [swap(): return lax.ppermute(values, axis, [(i, i ^ bit) for i in range(count)])]
    ppermute x15, starting transfers between devices: 19.9 us -> 16.6 us  [swap(): return lax.ppermute(values, axis, [(i, i ^ bit) for i in range(count)])]
where the time goes in v19:
time: 41.8 us; the launch traced here: 41.6 us
  starting transfers between devices  16.6 us (40%)
  waiting for transfers between devices  16.6 us (40%)
  Pallas kernels  6.65 us (16%)
  other arithmetic  0.85 us (2%)
  between operations  0.81 us (2%)
    ppermute x15, starting transfers between devices, swap(): return lax.ppermute(values, axis, [(i, i ^ bit) for i in range(count)])  16.6 us
    ppermute x15, waiting for transfers between devices, swap(): return lax.ppermute(values, axis, [(i, i ^ bit) for i in range(count)])  16.6 us
    pallas_call x1, Pallas kernels, body(): call(load_kernel, tuple((pltpu.VMEM(v.shape, v.dtype) for v in first)) +...  3.21 us
    pallas_call x1, Pallas kernels, body(): call(functools.partial(qkv_kernel, n_head), (kv_shape, shaped((4, rows, c...  1.16 us
    pallas_call x1, Pallas kernels, body(): call(attend_kernel, shaped((tall, cols + DH), BF16), [VMEM] * (3 + PLANE)...  1.11 us
  transfers between devices with their start and end apart: 15, of which 7 were waited for; matrix products, arithmetic and copies ran while one was open for 0% of the time, Pallas kernels for 12%

profile of v19, /device:TPU:0, one launch (start us, length us, event | category | flops | bytes accessed | tf_op | source)
XLA Modules:
  0.0 41.6 jit_solution(2895913109178902181)
XLA Ops:
  0.0 0.5 %collective-permute-start = (bf16[2,32,1536]{2,1,0:T(8,128)(2,1)}, bf16[2,32,1536]{2,1,0:T(8,128)(2,1)S(1)}, u32[]{:S(2)}, u32[]{:S(2)}) collective-permute-start(bf16[2,32,1536]{2,1,0:T(8,128)(2,1)} %x_ref.1), channel_id=1, source_target_pairs={{0,1},{1,0},{2,3},{3,2},{4,5},{5,4},{6,7},{7,6},{8,9},{9,8},{10,11... | collective-permute-start | bytes 589832 | tf_op jit(solution)/shard_map/ppermute | solution.py:23
  0.5 0.1 collective-permute-start.1
  1.2 0.0 copy-start
  1.2 3.2 %shard_map.73 = (bf16[3,3072,256]{2,1,0:T(8,128)(2,1)S(1)}, bf16[2,32,1536]{2,1,0:T(8,128)(2,1)S(1)}, f32[3,4,1536]{2,1,0:T(4,128)S(1)}, bf16[2,32,256]{2,1,0:T(...) custom-call(s32[2]{0:T(128)} %ids.1, s32[1]{0:T(128)S(6)} %copy.8.slab, ...), custom_call_target="tpu_custom_call" | custom-call | bytes 4718592 | tf_op jit(solution)/shard_map/pallas_call | solution.py:230
  4.4 0.0 collective-permute-done.1
  4.4 0.0 collective-permute-done.refs_1_
  4.4 1.2 %shard_map.74 = (bf16[2,32,256]{2,1,0:T(8,128)(2,1)S(1)}, bf16[4,32,256]{2,1,0:T(8,128)(2,1)S(1)}, bf16[2,32,256]{2,1,0:T(8,128)(2,1)S(1)}) custom-call(s32[1]{0:T(128)} %bitcast.3.head, s32[8,128]{1,0:T(8,128)S(1)} %get-tuple-element.30.ids_ref, bf16[2,32,1536]{2,1,0:T(8,128)(2,1)S(1)} %get-tuple-element.32.refs_0_, ...), custom_call_target="tpu_custom_call" | custom-call | flops 301989888 | bytes 4718592 | tf_op jit(solution)/shard_map/pallas_call | solution.py:252
  5.6 4.1 %collective-permute-start.4 = (bf16[4,32,256]{2,1,0:T(8,128)(2,1)S(1)}, bf16[4,32,256]{2,1,0:T(8,128)(2,1)S(1)}, u32[]{:S(2)}, u32[]{:S(2)}) collective-permute-start(bf16[4,32,256]{2,1,0:T(8,128)(2,1)S(1)} %get-tuple-element.44), channel_id=1, source_target_pairs={{0,16},{2,18},{4,20},{6,22},{8,24},{10,26},{12,28},{14,30},{16,0},... | collective-permute-start | bytes 196616 | tf_op jit(solution)/shard_map/ppermute | solution.py:23
  9.7 1.6 %collective-permute-start.2 = (bf16[2,32,256]{2,1,0:T(8,128)(2,1)S(1)}, bf16[2,32,256]{2,1,0:T(8,128)(2,1)S(1)}, u32[]{:S(2)}, u32[]{:S(2)}) collective-permute-start(bf16[2,32,256]{2,1,0:T(8,128)(2,1)S(1)} %get-tuple-element.37.q_ref), channel_id=1, source_target_pairs={{0,8},{2,10},{4,12},{6,14},{8,0},{10,2},{12,4},{14,6},{16,24},{18,... | collective-permute-start | bytes 98312 | tf_op jit(solution)/shard_map/ppermute | solution.py:23
  11.3 0.0 copy-done
  11.3 1.5 %collective-permute-start.10 = (bf16[192,256]{1,0:T(8,128)(2,1)S(1)}, bf16[192,256]{1,0:T(8,128)(2,1)S(1)}, u32[]{:S(2)}, u32[]{:S(2)}) collective-permute-start(bf16[192,256]{1,0:T(8,128)(2,1)S(1)} %bitcast.26), channel_id=1, source_target_pairs={{0,2},{2,0},{4,6},{6,4},{8,10},{10,8},{12,14},{14,12},{16,18},{18,... | collective-permute-start | bytes 294920 | tf_op jit(solution)/shard_map/ppermute | solution.py:23
  12.8 0.8 %collective-permute-done.2.mate_ref = bf16[2,32,256]{2,1,0:T(8,128)(2,1)S(1)} collective-permute-done((bf16[2,32,256]{2,1,0:T(8,128)(2,1)S(1)}, bf16[2,32,256]{2,1,0:T(8,128)(2,1)S(1)}, u32[]{:S(2)}, u32[]{:S(2)}) %collective-permute-start.2) | collective-permute-done | bytes 32800 | tf_op jit(solution)/shard_map/ppermute | solution.py:23
  13.6 0.7 %collective-permute-start.3 = (bf16[192,256]{1,0:T(8,128)(2,1)S(1)}, bf16[192,256]{1,0:T(8,128)(2,1)S(1)}, u32[]{:S(2)}, u32[]{:S(2)}) collective-permute-start(bf16[192,256]{1,0:T(8,128)(2,1)S(1)} %bitcast.27), channel_id=1, source_target_pairs={{0,16},{2,18},{4,20},{6,22},{8,24},{10,26},{12,28},{14,30},{16,0},... | collective-permute-start | bytes 294920 | tf_op jit(solution)/shard_map/ppermute | solution.py:23
  14.3 0.0 collective-permute-done.4
  14.3 1.6 %collective-permute-start.6 = (bf16[2,4,32,256]{3,2,1,0:T(8,128)(2,1)S(1)}, bf16[2,4,32,256]{3,2,1,0:T(8,128)(2,1)S(1)}, u32[]{:S(2)}, u32[]{:S(2)}) collective-permute-start(bf16[2,4,32,256]{3,2,1,0:T(8,128)(2,1)S(1)} %pad_maximum_fusion.7.refs_0_), channel_id=1, source_target_pairs={{0,2},{2,0},{4,6},{6,4},{8,10},{10,8},{12,14},{14,12},{16,18},{18,... | collective-permute-start | bytes 393224 | tf_op jit(solution)/shard_map/ppermute | solution.py:23
  15.9 1.5 %collective-permute-start.7 = (bf16[2,4,32,256]{3,2,1,0:T(8,128)(2,1)S(1)}, bf16[2,4,32,256]{3,2,1,0:T(8,128)(2,1)S(1)}, u32[]{:S(2)}, u32[]{:S(2)}) collective-permute-start(bf16[2,4,32,256]{3,2,1,0:T(8,128)(2,1)S(1)} %pad_maximum_fusion.7.refs_0_), channel_id=1, source_target_pairs={{0,4},{2,6},{4,0},{6,2},{8,12},{10,14},{12,8},{14,10},{16,20},{18,... | collective-permute-start | bytes 393224 | tf_op jit(solution)/shard_map/ppermute | solution.py:23
  17.4 0.5 %collective-permute-start.8 = (bf16[2,4,32,256]{3,2,1,0:T(8,128)(2,1)S(1)}, bf16[2,4,32,256]{3,2,1,0:T(8,128)(2,1)S(1)}, u32[]{:S(2)}, u32[]{:S(2)}) collective-permute-start(bf16[2,4,32,256]{3,2,1,0:T(8,128)(2,1)S(1)} %pad_maximum_fusion.7.refs_0_), channel_id=1, source_target_pairs={{0,6},{2,4},{4,2},{6,0},{8,14},{10,12},{12,10},{14,8},{16,22},{18,... | collective-permute-start | bytes 393224 | tf_op jit(solution)/shard_map/ppermute | solution.py:23
  17.9 1.3 %collective-permute-done.3 = bf16[192,256]{1,0:T(8,128)(2,1)S(1)} collective-permute-done((bf16[192,256]{1,0:T(8,128)(2,1)S(1)}, bf16[192,256]{1,0:T(8,128)(2,1)S(1)}, u32[]{:S(2)}, u32[]{:S(2)}) %collective-permute-start.3) | collective-permute-done | bytes 98336 | tf_op jit(solution)/shard_map/ppermute | solution.py:23
  19.1 2.8 %collective-permute-start.5 = (bf16[1,192,256]{2,1,0:T(8,128)(2,1)S(1)}, bf16[1,192,256]{2,1,0:T(8,128)(2,1)S(1)}, u32[]{:S(2)}, u32[]{:S(2)}) collective-permute-start(bf16[1,192,256]{2,1,0:T(8,128)(2,1)S(1)} %bitcast.23), channel_id=1, source_target_pairs={{0,4},{2,6},{4,0},{6,2},{8,12},{10,14},{12,8},{14,10},{16,20},{18,... | collective-permute-start | bytes 294920 | tf_op jit(solution)/shard_map/ppermute | solution.py:23
  22.0 0.0 collective-permute-done.10
  22.0 0.1 collective-permute-start.11
  22.1 0.0 collective-permute-done.6.refs_1_
  22.1 2.6 %collective-permute-done.7.refs_2_ = bf16[2,4,32,256]{3,2,1,0:T(8,128)(2,1)S(1)} collective-permute-done((bf16[2,4,32,256]{3,2,1,0:T(8,128)(2,1)S(1)}, bf16[2,4,32,256]{3,2,1,0:T(8,128)(2,1)S(1)}, u32[]{:S(2)}, u32[]{:S(2)}) %collective-permute-start.7) | collective-permute-done | bytes 131104 | tf_op jit(solution)/shard_map/ppermute | solution.py:23
  24.8 0.0 collective-permute-done.8.refs_3_
  24.8 2.1 %collective-permute-done.5 = bf16[1,192,256]{2,1,0:T(8,128)(2,1)S(1)} collective-permute-done((bf16[1,192,256]{2,1,0:T(8,128)(2,1)S(1)}, bf16[1,192,256]{2,1,0:T(8,128)(2,1)S(1)}, u32[]{:S(2)}, u32[]{:S(2)}) %collective-permute-start.5) | collective-permute-done | bytes 98336 | tf_op jit(solution)/shard_map/ppermute | solution.py:23
  26.9 0.9 %collective-permute-start.12 = (bf16[2,1,192,256]{3,2,1,0:T(8,128)(2,1)S(1)}, bf16[2,1,192,256]{3,2,1,0:T(8,128)(2,1)S(1)}, u32[]{:S(2)}, u32[]{:S(2)}) collective-permute-start(bf16[2,1,192,256]{3,2,1,0:T(8,128)(2,1)S(1)} %pad_maximum_fusion.2), channel_id=1, source_target_pairs={{0,2},{2,0},{4,6},{6,4},{8,10},{10,8},{12,14},{14,12},{16,18},{18,... | collective-permute-start | bytes 589832 | tf_op jit(solution)/shard_map/ppermute | solution.py:23
  27.8 1.1 %shard_map.75.part_ref = bf16[128,384]{1,0:T(8,128)(2,1)S(1)} custom-call(bf16[2,32,256]{2,1,0:T(8,128)(2,1)S(1)} %get-tuple-element.37.q_ref, bf16[2,32,256]{2,1,0:T(8,128)(2,1)S(1)} %collective-permute-done.2.mate_ref, bf16[2,32,256]{2,1,0:T(8,128)(2,1)S(1)} %get-tuple-element.43.kv1_ref, bf16[2,4,32,256]{3,2,1,0:T(8,128)(2,1)S(1)} %pad_maximum_fusion.7.refs_0_, ...), custom_call_target="tpu_custom_call" | custom-call | flops 33554432 | tf_op jit(solution)/shard_map/pallas_call | solution.py:273
  28.9 0.4 %collective-permute-start.9 = (bf16[128,384]{1,0:T(8,128)(2,1)S(1)}, bf16[128,384]{1,0:T(8,128)(2,1)S(1)}, u32[]{:S(2)}, u32[]{:S(2)}) collective-permute-start(bf16[128,384]{1,0:T(8,128)(2,1)S(1)} %shard_map.75.part_ref), channel_id=1, source_target_pairs={{0,8},{2,10},{4,12},{6,14},{8,0},{10,2},{12,4},{14,6},{16,24},{18,... | collective-permute-start | bytes 294920 | tf_op jit(solution)/shard_map/ppermute | solution.py:23
  29.3 4.3 %collective-permute-done.9.other_ref = bf16[128,384]{1,0:T(8,128)(2,1)S(1)} collective-permute-done((bf16[128,384]{1,0:T(8,128)(2,1)S(1)}, bf16[128,384]{1,0:T(8,128)(2,1)S(1)}, u32[]{:S(2)}, u32[]{:S(2)}) %collective-permute-start.9) | collective-permute-done | bytes 98336 | tf_op jit(solution)/shard_map/ppermute | solution.py:23
  33.6 0.2 shard_map.76.refs_0_
  33.8 0.0 collective-permute-done.11
  33.8 0.0 collective-permute-done.12
  33.9 0.1 pad_maximum_fusion.3
  33.9 0.4 shard_map.78
  34.4 0.1 collective-permute-start.13
  34.4 0.4 %shard_map.77.refs_0_ = f32[128,768]{1,0:T(8,128)S(1)} custom-call(s32[1]{0:T(128)} %bitcast.patch, s32[1]{0:T(128)} %bitcast.3.head, bf16[128,256]{1,0:T(8,128)(2,1)S(1)} %shard_map.76.refs_0_, bf16[2,192,256]{2,1,0:T(8,128)(2,1)S(1)} %get-tuple-element.61.refs_1_, bf16[2,192,256]{2,1,0:T(8,128)(2,1)S(1)} %get-tuple-element.63.refs_2_, ...), custom_call_target="tpu_custom_call" | custom-call | flops 50331648 | bytes 393216 | tf_op jit(solution)/shard_map/pallas_call | solution.py:286
  34.9 1.0 %collective-permute-done.13.refs_1_ = bf16[128,768]{1,0:T(8,128)(2,1)S(1)} collective-permute-done((bf16[128,768]{1,0:T(8,128)(2,1)S(1)}, bf16[128,768]{1,0:T(8,128)(2,1)S(1)}, u32[]{:S(2)}, u32[]{:S(2)}) %collective-permute-start.13) | collective-permute-done | bytes 196640 | tf_op jit(solution)/shard_map/ppermute | solution.py:23
  35.9 0.1 shard_map.79
  36.0 0.4 %collective-permute-start.14 = (bf16[2,32,768]{2,1,0:T(8,128)(2,1)S(1)}, bf16[2,32,768]{2,1,0:T(8,128)(2,1)S(1)}, u32[]{:S(2)}, u32[]{:S(2)}) collective-permute-start(bf16[2,32,768]{2,1,0:T(8,128)(2,1)S(1)} %get-tuple-element.53), channel_id=1, source_target_pairs={{0,8},{2,10},{4,12},{6,14},{8,0},{10,2},{12,4},{14,6},{16,24},{18,... | collective-permute-start | bytes 294920 | tf_op jit(solution)/shard_map/ppermute | solution.py:23
  36.4 4.5 %collective-permute-done.14 = bf16[2,32,768]{2,1,0:T(8,128)(2,1)S(1)} collective-permute-done((bf16[2,32,768]{2,1,0:T(8,128)(2,1)S(1)}, bf16[2,32,768]{2,1,0:T(8,128)(2,1)S(1)}, u32[]{:S(2)}, u32[]{:S(2)}) %collective-permute-start.14) | collective-permute-done | bytes 98336 | tf_op jit(solution)/shard_map/ppermute | solution.py:23
  40.9 0.7 %pad_maximum_fusion.6 = bf16[2,32,1536]{2,1,0:T(8,128)(2,1)} fusion(bf16[2,32,768]{2,1,0:T(8,128)(2,1)S(1)} %get-tuple-element.56, bf16[2,32,768]{2,1,0:T(8,128)(2,1)S(1)} %get-tuple-element.55), kind=kLoop, calls=%fused_computation.6 | loop fusion | flops 393216 | bytes 393216 | tf_op jit(solution)/shard_map/concatenate | solution.py:305
  (7 shorter events, 0.1 us)
Async XLA Ops:
  0.0 4.4 %collective-permute-start = (bf16[2,32,1536]{2,1,0:T(8,128)(2,1)}, bf16[2,32,1536]{2,1,0:T(8,128)(2,1)S(1)}, u32[]{:S(2)}, u32[]{:S(2)}) collective-permute-start(bf16[2,32,1536]{2,1,0:T(8,128)(2,1)} %x_ref.1), channel_id=1, source_target_pairs={{0,1},{1,0},{2,3},{3,2},{4,5},{5,4},{6,7},{7,6},{8,9},{9,8},{10,11... | collective-permute-start | bytes 589832 | tf_op jit(solution)/shard_map/ppermute | solution.py:23
  0.5 3.9 %collective-permute-start.1 = (f32[4,3,1536]{2,0,1:T(4,128)}, f32[4,3,1536]{2,0,1:T(4,128)S(1)}, u32[]{:S(2)}, u32[]{:S(2)}) collective-permute-start(f32[4,3,1536]{2,0,1:T(4,128)} %param.11), channel_id=1, source_target_pairs={{0,1},{1,0},{2,3},{3,2},{4,5},{5,4},{6,7},{7,6},{8,9},{9,8},{10,11... | collective-permute-start | bytes 221192 | tf_op jit(solution)/shard_map/ppermute | solution.py:23
  1.2 10.1 %copy-start = (bf16[256,192]{0,1:T(8,128)(2,1)S(1)}, bf16[256,192]{0,1:T(8,128)(2,1)}, u32[]{:S(2)}) copy-start(bf16[256,192]{0,1:T(8,128)(2,1)} %param.10) | copy-start | bytes 294916
  5.6 8.7 %collective-permute-start.4 = (bf16[4,32,256]{2,1,0:T(8,128)(2,1)S(1)}, bf16[4,32,256]{2,1,0:T(8,128)(2,1)S(1)}, u32[]{:S(2)}, u32[]{:S(2)}) collective-permute-start(bf16[4,32,256]{2,1,0:T(8,128)(2,1)S(1)} %get-tuple-element.44), channel_id=1, source_target_pairs={{0,16},{2,18},{4,20},{6,22},{8,24},{10,26},{12,28},{14,30},{16,0},... | collective-permute-start | bytes 196616 | tf_op jit(solution)/shard_map/ppermute | solution.py:23
  9.7 3.9 %collective-permute-start.2 = (bf16[2,32,256]{2,1,0:T(8,128)(2,1)S(1)}, bf16[2,32,256]{2,1,0:T(8,128)(2,1)S(1)}, u32[]{:S(2)}, u32[]{:S(2)}) collective-permute-start(bf16[2,32,256]{2,1,0:T(8,128)(2,1)S(1)} %get-tuple-element.37.q_ref), channel_id=1, source_target_pairs={{0,8},{2,10},{4,12},{6,14},{8,0},{10,2},{12,4},{14,6},{16,24},{18,... | collective-permute-start | bytes 98312 | tf_op jit(solution)/shard_map/ppermute | solution.py:23
  11.3 10.7 %collective-permute-start.10 = (bf16[192,256]{1,0:T(8,128)(2,1)S(1)}, bf16[192,256]{1,0:T(8,128)(2,1)S(1)}, u32[]{:S(2)}, u32[]{:S(2)}) collective-permute-start(bf16[192,256]{1,0:T(8,128)(2,1)S(1)} %bitcast.26), channel_id=1, source_target_pairs={{0,2},{2,0},{4,6},{6,4},{8,10},{10,8},{12,14},{14,12},{16,18},{18,... | collective-permute-start | bytes 294920 | tf_op jit(solution)/shard_map/ppermute | solution.py:23
  13.6 5.5 %collective-permute-start.3 = (bf16[192,256]{1,0:T(8,128)(2,1)S(1)}, bf16[192,256]{1,0:T(8,128)(2,1)S(1)}, u32[]{:S(2)}, u32[]{:S(2)}) collective-permute-start(bf16[192,256]{1,0:T(8,128)(2,1)S(1)} %bitcast.27), channel_id=1, source_target_pairs={{0,16},{2,18},{4,20},{6,22},{8,24},{10,26},{12,28},{14,30},{16,0},... | collective-permute-start | bytes 294920 | tf_op jit(solution)/shard_map/ppermute | solution.py:23
  14.3 7.8 %collective-permute-start.6 = (bf16[2,4,32,256]{3,2,1,0:T(8,128)(2,1)S(1)}, bf16[2,4,32,256]{3,2,1,0:T(8,128)(2,1)S(1)}, u32[]{:S(2)}, u32[]{:S(2)}) collective-permute-start(bf16[2,4,32,256]{3,2,1,0:T(8,128)(2,1)S(1)} %pad_maximum_fusion.7.refs_0_), channel_id=1, source_target_pairs={{0,2},{2,0},{4,6},{6,4},{8,10},{10,8},{12,14},{14,12},{16,18},{18,... | collective-permute-start | bytes 393224 | tf_op jit(solution)/shard_map/ppermute | solution.py:23
  15.9 8.9 %collective-permute-start.7 = (bf16[2,4,32,256]{3,2,1,0:T(8,128)(2,1)S(1)}, bf16[2,4,32,256]{3,2,1,0:T(8,128)(2,1)S(1)}, u32[]{:S(2)}, u32[]{:S(2)}) collective-permute-start(bf16[2,4,32,256]{3,2,1,0:T(8,128)(2,1)S(1)} %pad_maximum_fusion.7.refs_0_), channel_id=1, source_target_pairs={{0,4},{2,6},{4,0},{6,2},{8,12},{10,14},{12,8},{14,10},{16,20},{18,... | collective-permute-start | bytes 393224 | tf_op jit(solution)/shard_map/ppermute | solution.py:23
  17.4 7.4 %collective-permute-start.8 = (bf16[2,4,32,256]{3,2,1,0:T(8,128)(2,1)S(1)}, bf16[2,4,32,256]{3,2,1,0:T(8,128)(2,1)S(1)}, u32[]{:S(2)}, u32[]{:S(2)}) collective-permute-start(bf16[2,4,32,256]{3,2,1,0:T(8,128)(2,1)S(1)} %pad_maximum_fusion.7.refs_0_), channel_id=1, source_target_pairs={{0,6},{2,4},{4,2},{6,0},{8,14},{10,12},{12,10},{14,8},{16,22},{18,... | collective-permute-start | bytes 393224 | tf_op jit(solution)/shard_map/ppermute | solution.py:23
  19.1 7.7 %collective-permute-start.5 = (bf16[1,192,256]{2,1,0:T(8,128)(2,1)S(1)}, bf16[1,192,256]{2,1,0:T(8,128)(2,1)S(1)}, u32[]{:S(2)}, u32[]{:S(2)}) collective-permute-start(bf16[1,192,256]{2,1,0:T(8,128)(2,1)S(1)} %bitcast.23), channel_id=1, source_target_pairs={{0,4},{2,6},{4,0},{6,2},{8,12},{10,14},{12,8},{14,10},{16,20},{18,... | collective-permute-start | bytes 294920 | tf_op jit(solution)/shard_map/ppermute | solution.py:23
  22.0 11.8 %collective-permute-start.11 = (bf16[2,192,256]{2,1,0:T(8,128)(2,1)S(1)}, bf16[2,192,256]{2,1,0:T(8,128)(2,1)S(1)}, u32[]{:S(2)}, u32[]{:S(2)}) collective-permute-start(bf16[2,192,256]{2,1,0:T(8,128)(2,1)S(1)} %get-tuple-element.62), channel_id=1, source_target_pairs={{0,4},{2,6},{4,0},{6,2},{8,12},{10,14},{12,8},{14,10},{16,20},{18,... | collective-permute-start | bytes 589832 | tf_op jit(solution)/shard_map/ppermute | solution.py:23
  26.9 6.9 %collective-permute-start.12 = (bf16[2,1,192,256]{3,2,1,0:T(8,128)(2,1)S(1)}, bf16[2,1,192,256]{3,2,1,0:T(8,128)(2,1)S(1)}, u32[]{:S(2)}, u32[]{:S(2)}) collective-permute-start(bf16[2,1,192,256]{3,2,1,0:T(8,128)(2,1)S(1)} %pad_maximum_fusion.2), channel_id=1, source_target_pairs={{0,2},{2,0},{4,6},{6,4},{8,10},{10,8},{12,14},{14,12},{16,18},{18,... | collective-permute-start | bytes 589832 | tf_op jit(solution)/shard_map/ppermute | solution.py:23
  28.9 4.7 %collective-permute-start.9 = (bf16[128,384]{1,0:T(8,128)(2,1)S(1)}, bf16[128,384]{1,0:T(8,128)(2,1)S(1)}, u32[]{:S(2)}, u32[]{:S(2)}) collective-permute-start(bf16[128,384]{1,0:T(8,128)(2,1)S(1)} %shard_map.75.part_ref), channel_id=1, source_target_pairs={{0,8},{2,10},{4,12},{6,14},{8,0},{10,2},{12,4},{14,6},{16,24},{18,... | collective-permute-start | bytes 294920 | tf_op jit(solution)/shard_map/ppermute | solution.py:23
  34.4 1.5 %collective-permute-start.13 = (bf16[128,768]{1,0:T(8,128)(2,1)S(1)}, bf16[128,768]{1,0:T(8,128)(2,1)S(1)}, u32[]{:S(2)}, u32[]{:S(2)}) collective-permute-start(bf16[128,768]{1,0:T(8,128)(2,1)S(1)} %shard_map.78), channel_id=1, source_target_pairs={{0,1},{1,0},{2,3},{3,2},{4,5},{5,4},{6,7},{7,6},{8,9},{9,8},{10,11... | collective-permute-start | bytes 589832 | tf_op jit(solution)/shard_map/ppermute | solution.py:23
  36.0 4.9 %collective-permute-start.14 = (bf16[2,32,768]{2,1,0:T(8,128)(2,1)S(1)}, bf16[2,32,768]{2,1,0:T(8,128)(2,1)S(1)}, u32[]{:S(2)}, u32[]{:S(2)}) collective-permute-start(bf16[2,32,768]{2,1,0:T(8,128)(2,1)S(1)} %get-tuple-element.53), channel_id=1, source_target_pairs={{0,8},{2,10},{4,12},{6,14},{8,0},{10,2},{12,4},{14,6},{16,24},{18,... | collective-permute-start | bytes 294920 | tf_op jit(solution)/shard_map/ppermute | solution.py:23

commit v20 on v19

--- a/solution.py
+++ b/solution.py
@@ -175,29 +175,31 @@
         o_ref[:, lanes] = (mixed / sum(scales)).astype(BF16)
 
 
-def project_kernel(n_head, n_patch, bit, patch, head, *refs):
-    o_ref, w_refs, (out_ref, sums) = refs[0], refs[1 : 1 + PLANE], refs[1 + PLANE :]
+def project_kernel(n_head, n_patch, bit, mate, patch, head, o_ref, *refs):
+    w_refs, (out_ref, sums) = refs[:PLANE], refs[PLANE:]
+    rows = out_ref.shape[0]
     slot = head[0] ^ bit ^ (patch[0] // (n_patch // n_head))
     for near in range(PLANE):
         sums[(patch[0] % PLANE) ^ near] = lax.dot_general(
-            o_ref[...], w_refs[near][slot], NT, preferred_element_type=F32
+            o_ref[mate * rows : (mate + 1) * rows, :],
+            w_refs[near][slot],
+            NT,
+            preferred_element_type=F32,
         )
     out = jnp.concatenate([sums[c] for c in range(PLANE)], axis=1)
     out_ref[...] = out.astype(out_ref.dtype)
 
 
 def gate_kernel(n_patch, patch, ids_ref, mod_ref, *refs):
-    sum_refs, (own_out, mate_out) = refs[:-2], refs[-2:]
+    sum_refs, out_ref = refs[:-1], refs[-1]
     total = sum(ref[...].astype(F32) for ref in sum_refs)
     rows, width = total.shape
-    each = rows // 2 // STEPS
+    each = rows // STEPS
     second = (patch[0] // PLANE) % 2 == 1
     for step in range(STEPS):
         gate = table_row(mod_ref, 2, ids_ref, step)
         gate = jnp.where(second, gate[:, width:], gate[:, :width])
-        for mate, ref in enumerate((own_out, mate_out)):
-            start = mate * (rows // 2) + step * each
-            ref[step] = (gate * total[start : start + each]).astype(BF16)
+        out_ref[step] = (gate * total[step * each : (step + 1) * each]).astype(BF16)
 
 
 def in_hbm(values):
@@ -267,8 +269,6 @@
     w_rest, q_mate = lax.optimization_barrier((w_rest, q_mate))
     w_y = across(jnp.stack([w_own, w_x]), 2)
     rest_y = across(w_rest, 2)
-    rest_y, *kv_plane[1:] = lax.optimization_barrier((rest_y, *kv_plane[1:]))
-    rest_x = across(jnp.stack([w_rest, rest_y]), 1)
     tall = 2 * STEPS * rows
     part = call(
         attend_kernel,
@@ -276,31 +276,36 @@
         [VMEM] * (3 + PLANE),
         flops=4 * STEPS * rows * n_patch * rows * cols,
     )(q, q_mate, kv1, *kv_plane)
+    rest_y, part = lax.optimization_barrier((rest_y, part))
+    rest_x = across(jnp.stack([w_rest, rest_y]), 1)
     o = call(merge_kernel, shaped((tall, cols), BF16), [VMEM] * 2)(part, across(part, PLANE))
     o, w_y, rest_x = lax.optimization_barrier((o, w_y, rest_x))
     near = [(w_own, w_rest), (w_x, rest_x[0]), (w_y[0], rest_y), (w_y[1], rest_x[1])]
     w_plane = [jnp.concatenate([first[None], others]) for first, others in near]
     wide = PLANE * piece
 
-    def project(bit, dtype):
+    half = tall // 2
+
+    def project(mate, bit, dtype):
         return call(
-            functools.partial(project_kernel, n_head, n_patch, bit),
-            shaped((tall, wide), dtype),
+            functools.partial(project_kernel, n_head, n_patch, bit, mate),
+            shaped((half, wide), dtype),
             [SMEM] * 2 + [VMEM] * (1 + PLANE),
-            [pltpu.VMEM((PLANE, tall, piece), F32)],
-            2 * tall * wide * cols,
+            [pltpu.VMEM((PLANE, half, piece), F32)],
+            2 * half * wide * cols,
             2 * wide * cols,
         )(patch[None], head[None], o, *w_plane)
 
-    sums = [swap(project(k, BF16), "head", n_head, k) for k in range(1, n_head)]
-    sums = [project(0, F32)] + sums
-    out_half = shaped((STEPS, rows, wide), BF16)
-    out_own, out_mate = call(
-        functools.partial(gate_kernel, n_patch),
-        (out_half, out_half),
-        [SMEM] + [VMEM] * (2 + n_head),
-    )(patch[None], ids, mod_own, *sums)
-    out_back = across(out_mate, PLANE)
+    def gated(mate):
+        sent = [swap(project(mate, k, BF16), "head", n_head, k) for k in range(1, n_head)]
+        return call(
+            functools.partial(gate_kernel, n_patch),
+            shaped((STEPS, rows, wide), BF16),
+            [SMEM] + [VMEM] * (2 + n_head),
+        )(patch[None], ids, mod_own, project(mate, 0, F32), *sent)
+
+    out_back = across(gated(1), PLANE)
+    out_own = gated(0)
     second = (patch // PLANE) % 2 == 1
     return jnp.concatenate(
         [jnp.where(second, out_back, out_own), jnp.where(second, out_own, out_back)], axis=2

time: 41.8 us -> 40.4 us (0.967)
  waiting for transfers between devices: 16.6 us -> 13.2 us
  starting transfers between devices: 16.6 us -> 18 us
  Pallas kernels: 6.65 us -> 7.33 us
    ppermute x15 -> x16, waiting for transfers between devices: 16.6 us -> 13.2 us  [swap(): return lax.ppermute(values, axis, [(i, i ^ bit) for i in range(count)])]
    ppermute x15 -> x16, starting transfers between devices: 16.6 us -> 18 us  [swap(): return lax.ppermute(values, axis, [(i, i ^ bit) for i in range(count)])]
    pallas_call x3 -> x6, Pallas kernels: 0.95 us -> 1.63 us  [the longest x4 1.4 us: project(): call(functools.partial(project_kernel, n_head, n_patch, bit, mate), shape...]
  transfers between devices with their start and end apart: 15 -> 16, of which waited for: 7 -> 6; matrix products, arithmetic and copies ran while one was open for 0% -> 0% of each run, Pallas kernels for 12% -> 14%
where the time goes in v20:
time: 40.4 us; the launch traced here: 40.2 us
  starting transfers between devices  18 us (45%)
  waiting for transfers between devices  13.2 us (33%)
  Pallas kernels  7.33 us (18%)
  other arithmetic  0.84 us (2%)
  between operations  0.84 us (2%)
    ppermute x16, starting transfers between devices, swap(): return lax.ppermute(values, axis, [(i, i ^ bit) for i in range(count)])  18 us
    ppermute x16, waiting for transfers between devices, swap(): return lax.ppermute(values, axis, [(i, i ^ bit) for i in range(count)])  13.2 us
    pallas_call x1, Pallas kernels, body(): call(load_kernel, tuple((pltpu.VMEM(v.shape, v.dtype) for v in first)) +...  3.21 us
    pallas_call x4, Pallas kernels, project(): call(functools.partial(project_kernel, n_head, n_patch, bit, mate), shape...  1.4 us
    pallas_call x1, Pallas kernels, body(): call(functools.partial(qkv_kernel, n_head), (kv_shape, shaped((4, rows, c...  1.16 us
    pallas_call x1, Pallas kernels, body(): call(attend_kernel, shaped((tall, cols + DH), BF16), [VMEM] * (3 + PLANE)...  1.11 us
  transfers between devices with their start and end apart: 16, of which 6 were waited for; matrix products, arithmetic and copies ran while one was open for 0% of the time, Pallas kernels for 14%

profile of v20, /device:TPU:0, one launch (start us, length us, event | category | flops | bytes accessed | tf_op | source)
XLA Modules:
  0.0 40.2 jit_solution(820151737839668610)
XLA Ops:
  0.0 0.5 %collective-permute-start = (bf16[2,32,1536]{2,1,0:T(8,128)(2,1)}, bf16[2,32,1536]{2,1,0:T(8,128)(2,1)S(1)}, u32[]{:S(2)}, u32[]{:S(2)}) collective-permute-start(bf16[2,32,1536]{2,1,0:T(8,128)(2,1)} %x_ref.1), channel_id=1, source_target_pairs={{0,1},{1,0},{2,3},{3,2},{4,5},{5,4},{6,7},{7,6},{8,9},{9,8},{10,11... | collective-permute-start | bytes 589832 | tf_op jit(solution)/shard_map/ppermute | solution.py:23
  0.5 0.1 collective-permute-start.1
  1.2 0.0 copy-start
  1.2 3.2 %shard_map.73 = (bf16[3,3072,256]{2,1,0:T(8,128)(2,1)S(1)}, bf16[2,32,1536]{2,1,0:T(8,128)(2,1)S(1)}, f32[3,4,1536]{2,1,0:T(4,128)S(1)}, bf16[2,32,256]{2,1,0:T(...) custom-call(s32[2]{0:T(128)} %ids.1, s32[1]{0:T(128)S(6)} %copy.8.slab, ...), custom_call_target="tpu_custom_call" | custom-call | bytes 4718592 | tf_op jit(solution)/shard_map/pallas_call | solution.py:232
  4.4 0.0 collective-permute-done.1
  4.4 0.0 collective-permute-done.refs_1_
  4.4 1.2 %shard_map.74 = (bf16[2,32,256]{2,1,0:T(8,128)(2,1)S(1)}, bf16[4,32,256]{2,1,0:T(8,128)(2,1)S(1)}, bf16[2,32,256]{2,1,0:T(8,128)(2,1)S(1)}) custom-call(s32[1]{0:T(128)} %bitcast.3.head, s32[8,128]{1,0:T(8,128)S(1)} %get-tuple-element.26.ids_ref, bf16[2,32,1536]{2,1,0:T(8,128)(2,1)S(1)} %get-tuple-element.28.refs_0_, ...), custom_call_target="tpu_custom_call" | custom-call | flops 301989888 | bytes 4718592 | tf_op jit(solution)/shard_map/pallas_call | solution.py:254
  5.6 4.1 %collective-permute-start.5 = (bf16[4,32,256]{2,1,0:T(8,128)(2,1)S(1)}, bf16[4,32,256]{2,1,0:T(8,128)(2,1)S(1)}, u32[]{:S(2)}, u32[]{:S(2)}) collective-permute-start(bf16[4,32,256]{2,1,0:T(8,128)(2,1)S(1)} %get-tuple-element.41), channel_id=1, source_target_pairs={{0,16},{2,18},{4,20},{6,22},{8,24},{10,26},{12,28},{14,30},{16,0},... | collective-permute-start | bytes 196616 | tf_op jit(solution)/shard_map/ppermute | solution.py:23
  9.7 1.6 %collective-permute-start.2 = (bf16[2,32,256]{2,1,0:T(8,128)(2,1)S(1)}, bf16[2,32,256]{2,1,0:T(8,128)(2,1)S(1)}, u32[]{:S(2)}, u32[]{:S(2)}) collective-permute-start(bf16[2,32,256]{2,1,0:T(8,128)(2,1)S(1)} %get-tuple-element.35.q_ref), channel_id=1, source_target_pairs={{0,8},{2,10},{4,12},{6,14},{8,0},{10,2},{12,4},{14,6},{16,24},{18,... | collective-permute-start | bytes 98312 | tf_op jit(solution)/shard_map/ppermute | solution.py:23
  11.3 0.0 copy-done
  11.3 1.5 %collective-permute-start.10 = (bf16[192,256]{1,0:T(8,128)(2,1)S(1)}, bf16[192,256]{1,0:T(8,128)(2,1)S(1)}, u32[]{:S(2)}, u32[]{:S(2)}) collective-permute-start(bf16[192,256]{1,0:T(8,128)(2,1)S(1)} %bitcast.26), channel_id=1, source_target_pairs={{0,2},{2,0},{4,6},{6,4},{8,10},{10,8},{12,14},{14,12},{16,18},{18,... | collective-permute-start | bytes 294920 | tf_op jit(solution)/shard_map/ppermute | solution.py:23
  12.8 0.8 %collective-permute-done.2.mate_ref = bf16[2,32,256]{2,1,0:T(8,128)(2,1)S(1)} collective-permute-done((bf16[2,32,256]{2,1,0:T(8,128)(2,1)S(1)}, bf16[2,32,256]{2,1,0:T(8,128)(2,1)S(1)}, u32[]{:S(2)}, u32[]{:S(2)}) %collective-permute-start.2) | collective-permute-done | bytes 32800 | tf_op jit(solution)/shard_map/ppermute | solution.py:23
  13.6 0.7 %collective-permute-start.3 = (bf16[192,256]{1,0:T(8,128)(2,1)S(1)}, bf16[192,256]{1,0:T(8,128)(2,1)S(1)}, u32[]{:S(2)}, u32[]{:S(2)}) collective-permute-start(bf16[192,256]{1,0:T(8,128)(2,1)S(1)} %bitcast.27), channel_id=1, source_target_pairs={{0,16},{2,18},{4,20},{6,22},{8,24},{10,26},{12,28},{14,30},{16,0},... | collective-permute-start | bytes 294920 | tf_op jit(solution)/shard_map/ppermute | solution.py:23
  14.3 0.0 collective-permute-done.5
  14.3 1.6 %collective-permute-start.6 = (bf16[2,4,32,256]{3,2,1,0:T(8,128)(2,1)S(1)}, bf16[2,4,32,256]{3,2,1,0:T(8,128)(2,1)S(1)}, u32[]{:S(2)}, u32[]{:S(2)}) collective-permute-start(bf16[2,4,32,256]{3,2,1,0:T(8,128)(2,1)S(1)} %pad_maximum_fusion.7.refs_0_), channel_id=1, source_target_pairs={{0,2},{2,0},{4,6},{6,4},{8,10},{10,8},{12,14},{14,12},{16,18},{18,... | collective-permute-start | bytes 393224 | tf_op jit(solution)/shard_map/ppermute | solution.py:23
  15.9 1.5 %collective-permute-start.7 = (bf16[2,4,32,256]{3,2,1,0:T(8,128)(2,1)S(1)}, bf16[2,4,32,256]{3,2,1,0:T(8,128)(2,1)S(1)}, u32[]{:S(2)}, u32[]{:S(2)}) collective-permute-start(bf16[2,4,32,256]{3,2,1,0:T(8,128)(2,1)S(1)} %pad_maximum_fusion.7.refs_0_), channel_id=1, source_target_pairs={{0,4},{2,6},{4,0},{6,2},{8,12},{10,14},{12,8},{14,10},{16,20},{18,... | collective-permute-start | bytes 393224 | tf_op jit(solution)/shard_map/ppermute | solution.py:23
  17.4 0.5 %collective-permute-start.8 = (bf16[2,4,32,256]{3,2,1,0:T(8,128)(2,1)S(1)}, bf16[2,4,32,256]{3,2,1,0:T(8,128)(2,1)S(1)}, u32[]{:S(2)}, u32[]{:S(2)}) collective-permute-start(bf16[2,4,32,256]{3,2,1,0:T(8,128)(2,1)S(1)} %pad_maximum_fusion.7.refs_0_), channel_id=1, source_target_pairs={{0,6},{2,4},{4,2},{6,0},{8,14},{10,12},{12,10},{14,8},{16,22},{18,... | collective-permute-start | bytes 393224 | tf_op jit(solution)/shard_map/ppermute | solution.py:23
  17.9 1.3 %collective-permute-done.3 = bf16[192,256]{1,0:T(8,128)(2,1)S(1)} collective-permute-done((bf16[192,256]{1,0:T(8,128)(2,1)S(1)}, bf16[192,256]{1,0:T(8,128)(2,1)S(1)}, u32[]{:S(2)}, u32[]{:S(2)}) %collective-permute-start.3) | collective-permute-done | bytes 98336 | tf_op jit(solution)/shard_map/ppermute | solution.py:23
  19.1 2.8 %collective-permute-start.4 = (bf16[1,192,256]{2,1,0:T(8,128)(2,1)S(1)}, bf16[1,192,256]{2,1,0:T(8,128)(2,1)S(1)}, u32[]{:S(2)}, u32[]{:S(2)}) collective-permute-start(bf16[1,192,256]{2,1,0:T(8,128)(2,1)S(1)} %bitcast.23), channel_id=1, source_target_pairs={{0,4},{2,6},{4,0},{6,2},{8,12},{10,14},{12,8},{14,10},{16,20},{18,... | collective-permute-start | bytes 294920 | tf_op jit(solution)/shard_map/ppermute | solution.py:23
  22.0 0.0 collective-permute-done.10
  22.0 0.1 collective-permute-start.11
  22.1 0.0 collective-permute-done.6.refs_1_
  22.1 2.6 %collective-permute-done.7.refs_2_ = bf16[2,4,32,256]{3,2,1,0:T(8,128)(2,1)S(1)} collective-permute-done((bf16[2,4,32,256]{3,2,1,0:T(8,128)(2,1)S(1)}, bf16[2,4,32,256]{3,2,1,0:T(8,128)(2,1)S(1)}, u32[]{:S(2)}, u32[]{:S(2)}) %collective-permute-start.7) | collective-permute-done | bytes 131104 | tf_op jit(solution)/shard_map/ppermute | solution.py:23
  24.8 0.0 collective-permute-done.8.refs_3_
  24.8 1.1 %shard_map.75.part_ref = bf16[128,384]{1,0:T(8,128)(2,1)S(1)} custom-call(bf16[2,32,256]{2,1,0:T(8,128)(2,1)S(1)} %get-tuple-element.35.q_ref, bf16[2,32,256]{2,1,0:T(8,128)(2,1)S(1)} %collective-permute-done.2.mate_ref, bf16[2,32,256]{2,1,0:T(8,128)(2,1)S(1)} %get-tuple-element.40.kv1_ref, bf16[2,4,32,256]{3,2,1,0:T(8,128)(2,1)S(1)} %pad_maximum_fusion.7.refs_0_, ...), custom_call_target="tpu_custom_call" | custom-call | flops 33554432 | tf_op jit(solution)/shard_map/pallas_call | solution.py:273
  25.9 1.0 %collective-permute-done.4 = bf16[1,192,256]{2,1,0:T(8,128)(2,1)S(1)} collective-permute-done((bf16[1,192,256]{2,1,0:T(8,128)(2,1)S(1)}, bf16[1,192,256]{2,1,0:T(8,128)(2,1)S(1)}, u32[]{:S(2)}, u32[]{:S(2)}) %collective-permute-start.4) | collective-permute-done | bytes 98336 | tf_op jit(solution)/shard_map/ppermute | solution.py:23
  26.9 0.9 %collective-permute-start.12 = (bf16[2,1,192,256]{3,2,1,0:T(8,128)(2,1)S(1)}, bf16[2,1,192,256]{3,2,1,0:T(8,128)(2,1)S(1)}, u32[]{:S(2)}, u32[]{:S(2)}) collective-permute-start(bf16[2,1,192,256]{3,2,1,0:T(8,128)(2,1)S(1)} %pad_maximum_fusion.2), channel_id=1, source_target_pairs={{0,2},{2,0},{4,6},{6,4},{8,10},{10,8},{12,14},{14,12},{16,18},{18,... | collective-permute-start | bytes 589832 | tf_op jit(solution)/shard_map/ppermute | solution.py:23
  27.8 0.4 %collective-permute-start.9 = (bf16[128,384]{1,0:T(8,128)(2,1)S(1)}, bf16[128,384]{1,0:T(8,128)(2,1)S(1)}, u32[]{:S(2)}, u32[]{:S(2)}) collective-permute-start(bf16[128,384]{1,0:T(8,128)(2,1)S(1)} %shard_map.75.part_ref), channel_id=1, source_target_pairs={{0,8},{2,10},{4,12},{6,14},{8,0},{10,2},{12,4},{14,6},{16,24},{18,... | collective-permute-start | bytes 294920 | tf_op jit(solution)/shard_map/ppermute | solution.py:23
  28.2 4.2 %collective-permute-done.9.other_ref = bf16[128,384]{1,0:T(8,128)(2,1)S(1)} collective-permute-done((bf16[128,384]{1,0:T(8,128)(2,1)S(1)}, bf16[128,384]{1,0:T(8,128)(2,1)S(1)}, u32[]{:S(2)}, u32[]{:S(2)}) %collective-permute-start.9) | collective-permute-done | bytes 98336 | tf_op jit(solution)/shard_map/ppermute | solution.py:23
  32.4 0.2 shard_map.76.o_ref
  32.6 0.0 collective-permute-done.11
  32.6 0.0 collective-permute-done.12
  32.8 0.4 shard_map.78
  33.1 0.1 collective-permute-start.13
  33.2 0.4 shard_map.81
  33.6 0.6 %collective-permute-start.15 = (bf16[64,768]{1,0:T(8,128)(2,1)S(1)}, bf16[64,768]{1,0:T(8,128)(2,1)S(1)}, u32[]{:S(2)}, u32[]{:S(2)}) collective-permute-start(bf16[64,768]{1,0:T(8,128)(2,1)S(1)} %shard_map.81), channel_id=1, source_target_pairs={{0,1},{1,0},{2,3},{3,2},{4,5},{5,4},{6,7},{7,6},{8,9},{9,8},{10,11... | collective-permute-start | bytes 294920 | tf_op jit(solution)/shard_map/ppermute | solution.py:23
  34.1 0.4 shard_map.77.refs_0_
  34.5 0.0 collective-permute-done.13.refs_1_
  34.5 0.1 shard_map.79
  34.6 1.2 %collective-permute-start.14 = (bf16[2,32,768]{2,1,0:T(8,128)(2,1)S(1)}, bf16[2,32,768]{2,1,0:T(8,128)(2,1)S(1)}, u32[]{:S(2)}, u32[]{:S(2)}) collective-permute-start(bf16[2,32,768]{2,1,0:T(8,128)(2,1)S(1)} %shard_map.79), channel_id=1, source_target_pairs={{0,8},{2,10},{4,12},{6,14},{8,0},{10,2},{12,4},{14,6},{16,24},{18,... | collective-permute-start | bytes 294920 | tf_op jit(solution)/shard_map/ppermute | solution.py:23
  35.8 0.4 shard_map.80.refs_0_
  36.2 0.0 collective-permute-done.15.refs_1_
  36.2 0.1 shard_map.82
  36.3 3.2 %collective-permute-done.14 = bf16[2,32,768]{2,1,0:T(8,128)(2,1)S(1)} collective-permute-done((bf16[2,32,768]{2,1,0:T(8,128)(2,1)S(1)}, bf16[2,32,768]{2,1,0:T(8,128)(2,1)S(1)}, u32[]{:S(2)}, u32[]{:S(2)}) %collective-permute-start.14) | collective-permute-done | bytes 98336 | tf_op jit(solution)/shard_map/ppermute | solution.py:23
  39.5 0.7 %pad_maximum_fusion.6 = bf16[2,32,1536]{2,1,0:T(8,128)(2,1)} fusion(bf16[2,32,768]{2,1,0:T(8,128)(2,1)S(1)} %get-tuple-element.48, bf16[2,32,768]{2,1,0:T(8,128)(2,1)S(1)} %get-tuple-element.47), kind=kLoop, calls=%fused_computation.6 | loop fusion | flops 393216 | bytes 393216 | tf_op jit(solution)/shard_map/concatenate | solution.py:310
  (8 shorter events, 0.2 us)
Async XLA Ops:
  0.0 4.4 %collective-permute-start = (bf16[2,32,1536]{2,1,0:T(8,128)(2,1)}, bf16[2,32,1536]{2,1,0:T(8,128)(2,1)S(1)}, u32[]{:S(2)}, u32[]{:S(2)}) collective-permute-start(bf16[2,32,1536]{2,1,0:T(8,128)(2,1)} %x_ref.1), channel_id=1, source_target_pairs={{0,1},{1,0},{2,3},{3,2},{4,5},{5,4},{6,7},{7,6},{8,9},{9,8},{10,11... | collective-permute-start | bytes 589832 | tf_op jit(solution)/shard_map/ppermute | solution.py:23
  0.5 3.9 %collective-permute-start.1 = (f32[4,3,1536]{2,0,1:T(4,128)}, f32[4,3,1536]{2,0,1:T(4,128)S(1)}, u32[]{:S(2)}, u32[]{:S(2)}) collective-permute-start(f32[4,3,1536]{2,0,1:T(4,128)} %param.11), channel_id=1, source_target_pairs={{0,1},{1,0},{2,3},{3,2},{4,5},{5,4},{6,7},{7,6},{8,9},{9,8},{10,11... | collective-permute-start | bytes 221192 | tf_op jit(solution)/shard_map/ppermute | solution.py:23
  1.2 10.1 %copy-start = (bf16[256,192]{0,1:T(8,128)(2,1)S(1)}, bf16[256,192]{0,1:T(8,128)(2,1)}, u32[]{:S(2)}) copy-start(bf16[256,192]{0,1:T(8,128)(2,1)} %param.10) | copy-start | bytes 294916
  5.6 8.7 %collective-permute-start.5 = (bf16[4,32,256]{2,1,0:T(8,128)(2,1)S(1)}, bf16[4,32,256]{2,1,0:T(8,128)(2,1)S(1)}, u32[]{:S(2)}, u32[]{:S(2)}) collective-permute-start(bf16[4,32,256]{2,1,0:T(8,128)(2,1)S(1)} %get-tuple-element.41), channel_id=1, source_target_pairs={{0,16},{2,18},{4,20},{6,22},{8,24},{10,26},{12,28},{14,30},{16,0},... | collective-permute-start | bytes 196616 | tf_op jit(solution)/shard_map/ppermute | solution.py:23
  9.7 3.9 %collective-permute-start.2 = (bf16[2,32,256]{2,1,0:T(8,128)(2,1)S(1)}, bf16[2,32,256]{2,1,0:T(8,128)(2,1)S(1)}, u32[]{:S(2)}, u32[]{:S(2)}) collective-permute-start(bf16[2,32,256]{2,1,0:T(8,128)(2,1)S(1)} %get-tuple-element.35.q_ref), channel_id=1, source_target_pairs={{0,8},{2,10},{4,12},{6,14},{8,0},{10,2},{12,4},{14,6},{16,24},{18,... | collective-permute-start | bytes 98312 | tf_op jit(solution)/shard_map/ppermute | solution.py:23
  11.3 10.7 %collective-permute-start.10 = (bf16[192,256]{1,0:T(8,128)(2,1)S(1)}, bf16[192,256]{1,0:T(8,128)(2,1)S(1)}, u32[]{:S(2)}, u32[]{:S(2)}) collective-permute-start(bf16[192,256]{1,0:T(8,128)(2,1)S(1)} %bitcast.26), channel_id=1, source_target_pairs={{0,2},{2,0},{4,6},{6,4},{8,10},{10,8},{12,14},{14,12},{16,18},{18,... | collective-permute-start | bytes 294920 | tf_op jit(solution)/shard_map/ppermute | solution.py:23
  13.6 5.5 %collective-permute-start.3 = (bf16[192,256]{1,0:T(8,128)(2,1)S(1)}, bf16[192,256]{1,0:T(8,128)(2,1)S(1)}, u32[]{:S(2)}, u32[]{:S(2)}) collective-permute-start(bf16[192,256]{1,0:T(8,128)(2,1)S(1)} %bitcast.27), channel_id=1, source_target_pairs={{0,16},{2,18},{4,20},{6,22},{8,24},{10,26},{12,28},{14,30},{16,0},... | collective-permute-start | bytes 294920 | tf_op jit(solution)/shard_map/ppermute | solution.py:23
  14.3 7.8 %collective-permute-start.6 = (bf16[2,4,32,256]{3,2,1,0:T(8,128)(2,1)S(1)}, bf16[2,4,32,256]{3,2,1,0:T(8,128)(2,1)S(1)}, u32[]{:S(2)}, u32[]{:S(2)}) collective-permute-start(bf16[2,4,32,256]{3,2,1,0:T(8,128)(2,1)S(1)} %pad_maximum_fusion.7.refs_0_), channel_id=1, source_target_pairs={{0,2},{2,0},{4,6},{6,4},{8,10},{10,8},{12,14},{14,12},{16,18},{18,... | collective-permute-start | bytes 393224 | tf_op jit(solution)/shard_map/ppermute | solution.py:23
  15.9 8.9 %collective-permute-start.7 = (bf16[2,4,32,256]{3,2,1,0:T(8,128)(2,1)S(1)}, bf16[2,4,32,256]{3,2,1,0:T(8,128)(2,1)S(1)}, u32[]{:S(2)}, u32[]{:S(2)}) collective-permute-start(bf16[2,4,32,256]{3,2,1,0:T(8,128)(2,1)S(1)} %pad_maximum_fusion.7.refs_0_), channel_id=1, source_target_pairs={{0,4},{2,6},{4,0},{6,2},{8,12},{10,14},{12,8},{14,10},{16,20},{18,... | collective-permute-start | bytes 393224 | tf_op jit(solution)/shard_map/ppermute | solution.py:23
  17.4 7.4 %collective-permute-start.8 = (bf16[2,4,32,256]{3,2,1,0:T(8,128)(2,1)S(1)}, bf16[2,4,32,256]{3,2,1,0:T(8,128)(2,1)S(1)}, u32[]{:S(2)}, u32[]{:S(2)}) collective-permute-start(bf16[2,4,32,256]{3,2,1,0:T(8,128)(2,1)S(1)} %pad_maximum_fusion.7.refs_0_), channel_id=1, source_target_pairs={{0,6},{2,4},{4,2},{6,0},{8,14},{10,12},{12,10},{14,8},{16,22},{18,... | collective-permute-start | bytes 393224 | tf_op jit(solution)/shard_map/ppermute | solution.py:23
  19.1 7.7 %collective-permute-start.4 = (bf16[1,192,256]{2,1,0:T(8,128)(2,1)S(1)}, bf16[1,192,256]{2,1,0:T(8,128)(2,1)S(1)}, u32[]{:S(2)}, u32[]{:S(2)}) collective-permute-start(bf16[1,192,256]{2,1,0:T(8,128)(2,1)S(1)} %bitcast.23), channel_id=1, source_target_pairs={{0,4},{2,6},{4,0},{6,2},{8,12},{10,14},{12,8},{14,10},{16,20},{18,... | collective-permute-start | bytes 294920 | tf_op jit(solution)/shard_map/ppermute | solution.py:23
  22.0 10.6 %collective-permute-start.11 = (bf16[2,192,256]{2,1,0:T(8,128)(2,1)S(1)}, bf16[2,192,256]{2,1,0:T(8,128)(2,1)S(1)}, u32[]{:S(2)}, u32[]{:S(2)}) collective-permute-start(bf16[2,192,256]{2,1,0:T(8,128)(2,1)S(1)} %get-tuple-element.54), channel_id=1, source_target_pairs={{0,4},{2,6},{4,0},{6,2},{8,12},{10,14},{12,8},{14,10},{16,20},{18,... | collective-permute-start | bytes 589832 | tf_op jit(solution)/shard_map/ppermute | solution.py:23
  26.9 5.7 %collective-permute-start.12 = (bf16[2,1,192,256]{3,2,1,0:T(8,128)(2,1)S(1)}, bf16[2,1,192,256]{3,2,1,0:T(8,128)(2,1)S(1)}, u32[]{:S(2)}, u32[]{:S(2)}) collective-permute-start(bf16[2,1,192,256]{3,2,1,0:T(8,128)(2,1)S(1)} %pad_maximum_fusion.2), channel_id=1, source_target_pairs={{0,2},{2,0},{4,6},{6,4},{8,10},{10,8},{12,14},{14,12},{16,18},{18,... | collective-permute-start | bytes 589832 | tf_op jit(solution)/shard_map/ppermute | solution.py:23
  27.8 4.6 %collective-permute-start.9 = (bf16[128,384]{1,0:T(8,128)(2,1)S(1)}, bf16[128,384]{1,0:T(8,128)(2,1)S(1)}, u32[]{:S(2)}, u32[]{:S(2)}) collective-permute-start(bf16[128,384]{1,0:T(8,128)(2,1)S(1)} %shard_map.75.part_ref), channel_id=1, source_target_pairs={{0,8},{2,10},{4,12},{6,14},{8,0},{10,2},{12,4},{14,6},{16,24},{18,... | collective-permute-start | bytes 294920 | tf_op jit(solution)/shard_map/ppermute | solution.py:23
  33.1 1.4 %collective-permute-start.13 = (bf16[64,768]{1,0:T(8,128)(2,1)S(1)}, bf16[64,768]{1,0:T(8,128)(2,1)S(1)}, u32[]{:S(2)}, u32[]{:S(2)}) collective-permute-start(bf16[64,768]{1,0:T(8,128)(2,1)S(1)} %shard_map.78), channel_id=1, source_target_pairs={{0,1},{1,0},{2,3},{3,2},{4,5},{5,4},{6,7},{7,6},{8,9},{9,8},{10,11... | collective-permute-start | bytes 294920 | tf_op jit(solution)/shard_map/ppermute | solution.py:23
  33.6 2.6 %collective-permute-start.15 = (bf16[64,768]{1,0:T(8,128)(2,1)S(1)}, bf16[64,768]{1,0:T(8,128)(2,1)S(1)}, u32[]{:S(2)}, u32[]{:S(2)}) collective-permute-start(bf16[64,768]{1,0:T(8,128)(2,1)S(1)} %shard_map.81), channel_id=1, source_target_pairs={{0,1},{1,0},{2,3},{3,2},{4,5},{5,4},{6,7},{7,6},{8,9},{9,8},{10,11... | collective-permute-start | bytes 294920 | tf_op jit(solution)/shard_map/ppermute | solution.py:23
  34.6 4.9 %collective-permute-start.14 = (bf16[2,32,768]{2,1,0:T(8,128)(2,1)S(1)}, bf16[2,32,768]{2,1,0:T(8,128)(2,1)S(1)}, u32[]{:S(2)}, u32[]{:S(2)}) collective-permute-start(bf16[2,32,768]{2,1,0:T(8,128)(2,1)S(1)} %shard_map.79), channel_id=1, source_target_pairs={{0,8},{2,10},{4,12},{6,14},{8,0},{10,2},{12,4},{14,6},{16,24},{18,... | collective-permute-start | bytes 294920 | tf_op jit(solution)/shard_map/ppermute | solution.py:23

commit v21 on v20

--- a/solution.py
+++ b/solution.py
@@ -268,7 +268,10 @@
     kv_plane = plane_of(jnp.stack(kv_pair))
     w_rest, q_mate = lax.optimization_barrier((w_rest, q_mate))
     w_y = across(jnp.stack([w_own, w_x]), 2)
-    rest_y = across(w_rest, 2)
+    rest_plane = plane_of(w_rest)
+    rest_plane[1], rest_plane[2], kv_plane[3] = lax.optimization_barrier(
+        (rest_plane[1], rest_plane[2], kv_plane[3])
+    )
     tall = 2 * STEPS * rows
     part = call(
         attend_kernel,
@@ -276,11 +279,9 @@
         [VMEM] * (3 + PLANE),
         flops=4 * STEPS * rows * n_patch * rows * cols,
     )(q, q_mate, kv1, *kv_plane)
-    rest_y, part = lax.optimization_barrier((rest_y, part))
-    rest_x = across(jnp.stack([w_rest, rest_y]), 1)
     o = call(merge_kernel, shaped((tall, cols), BF16), [VMEM] * 2)(part, across(part, PLANE))
-    o, w_y, rest_x = lax.optimization_barrier((o, w_y, rest_x))
-    near = [(w_own, w_rest), (w_x, rest_x[0]), (w_y[0], rest_y), (w_y[1], rest_x[1])]
+    o, w_y, rest_plane = lax.optimization_barrier((o, w_y, rest_plane))
+    near = zip((w_own, w_x, w_y[0], w_y[1]), rest_plane)
     w_plane = [jnp.concatenate([first[None], others]) for first, others in near]
     wide = PLANE * piece
 

time: 40.4 us -> 42.3 us (1.047)
  starting transfers between devices: 18 us -> 21.2 us
  waiting for transfers between devices: 13.2 us -> 12 us
    ppermute x16 -> x17, starting transfers between devices: 18 us -> 21.2 us  [swap(): return lax.ppermute(values, axis, [(i, i ^ bit) for i in range(count)])]
    ppermute x16 -> x17, waiting for transfers between devices: 13.2 us -> 12 us  [swap(): return lax.ppermute(values, axis, [(i, i ^ bit) for i in range(count)])]
  transfers between devices with their start and end apart: 16 -> 17, of which waited for: 6 -> 7; matrix products, arithmetic and copies ran while one was open for 0% -> 0% of each run, Pallas kernels for 14% -> 14%
where the time goes in v21:
time: 42.3 us; the launch traced here: 42.2 us
  starting transfers between devices  21.2 us (50%)
  waiting for transfers between devices  12 us (28%)
  Pallas kernels  7.33 us (17%)
  other arithmetic  0.82 us (2%)
  between operations  0.81 us (2%)
    ppermute x17, starting transfers between devices, swap(): return lax.ppermute(values, axis, [(i, i ^ bit) for i in range(count)])  21.2 us
    ppermute x17, waiting for transfers between devices, swap(): return lax.ppermute(values, axis, [(i, i ^ bit) for i in range(count)])  12 us
    pallas_call x1, Pallas kernels, body(): call(load_kernel, tuple((pltpu.VMEM(v.shape, v.dtype) for v in first)) +...  3.21 us
    pallas_call x4, Pallas kernels, project(): call(functools.partial(project_kernel, n_head, n_patch, bit, mate), shape...  1.4 us
    pallas_call x1, Pallas kernels, body(): call(functools.partial(qkv_kernel, n_head), (kv_shape, shaped((4, rows, c...  1.16 us
    pallas_call x1, Pallas kernels, body(): call(attend_kernel, shaped((tall, cols + DH), BF16), [VMEM] * (3 + PLANE)...  1.11 us
  transfers between devices with their start and end apart: 17, of which 7 were waited for; matrix products, arithmetic and copies ran while one was open for 0% of the time, Pallas kernels for 14%

profile of v21, /device:TPU:0, one launch (start us, length us, event | category | flops | bytes accessed | tf_op | source)
XLA Modules:
  0.0 42.2 jit_solution(973087107863160470)
XLA Ops:
  0.0 0.5 %collective-permute-start = (bf16[2,32,1536]{2,1,0:T(8,128)(2,1)}, bf16[2,32,1536]{2,1,0:T(8,128)(2,1)S(1)}, u32[]{:S(2)}, u32[]{:S(2)}) collective-permute-start(bf16[2,32,1536]{2,1,0:T(8,128)(2,1)} %x_ref.1), channel_id=1, source_target_pairs={{0,1},{1,0},{2,3},{3,2},{4,5},{5,4},{6,7},{7,6},{8,9},{9,8},{10,11... | collective-permute-start | bytes 589832 | tf_op jit(solution)/shard_map/ppermute | solution.py:23
  0.5 0.1 collective-permute-start.1
  1.2 0.0 copy-start
  1.2 3.2 %shard_map.73 = (bf16[3,3072,256]{2,1,0:T(8,128)(2,1)S(1)}, bf16[2,32,1536]{2,1,0:T(8,128)(2,1)S(1)}, f32[3,4,1536]{2,1,0:T(4,128)S(1)}, bf16[2,32,256]{2,1,0:T(...) custom-call(s32[2]{0:T(128)} %ids.1, s32[1]{0:T(128)S(6)} %copy.8.slab, ...), custom_call_target="tpu_custom_call" | custom-call | bytes 4718592 | tf_op jit(solution)/shard_map/pallas_call | solution.py:232
  4.4 0.0 collective-permute-done.1
  4.4 0.0 collective-permute-done.refs_1_
  4.4 1.2 %shard_map.74 = (bf16[2,32,256]{2,1,0:T(8,128)(2,1)S(1)}, bf16[4,32,256]{2,1,0:T(8,128)(2,1)S(1)}, bf16[2,32,256]{2,1,0:T(8,128)(2,1)S(1)}) custom-call(s32[1]{0:T(128)} %bitcast.3.head, s32[8,128]{1,0:T(8,128)S(1)} %get-tuple-element.30.ids_ref, bf16[2,32,1536]{2,1,0:T(8,128)(2,1)S(1)} %get-tuple-element.32.refs_0_, ...), custom_call_target="tpu_custom_call" | custom-call | flops 301989888 | bytes 4718592 | tf_op jit(solution)/shard_map/pallas_call | solution.py:254
  5.6 4.1 %collective-permute-start.4 = (bf16[4,32,256]{2,1,0:T(8,128)(2,1)S(1)}, bf16[4,32,256]{2,1,0:T(8,128)(2,1)S(1)}, u32[]{:S(2)}, u32[]{:S(2)}) collective-permute-start(bf16[4,32,256]{2,1,0:T(8,128)(2,1)S(1)} %get-tuple-element.44), channel_id=1, source_target_pairs={{0,16},{2,18},{4,20},{6,22},{8,24},{10,26},{12,28},{14,30},{16,0},... | collective-permute-start | bytes 196616 | tf_op jit(solution)/shard_map/ppermute | solution.py:23
  9.7 1.6 %collective-permute-start.2 = (bf16[2,32,256]{2,1,0:T(8,128)(2,1)S(1)}, bf16[2,32,256]{2,1,0:T(8,128)(2,1)S(1)}, u32[]{:S(2)}, u32[]{:S(2)}) collective-permute-start(bf16[2,32,256]{2,1,0:T(8,128)(2,1)S(1)} %get-tuple-element.37.q_ref), channel_id=1, source_target_pairs={{0,8},{2,10},{4,12},{6,14},{8,0},{10,2},{12,4},{14,6},{16,24},{18,... | collective-permute-start | bytes 98312 | tf_op jit(solution)/shard_map/ppermute | solution.py:23
  11.3 0.0 copy-done
  11.3 1.5 %collective-permute-start.11 = (bf16[192,256]{1,0:T(8,128)(2,1)S(1)}, bf16[192,256]{1,0:T(8,128)(2,1)S(1)}, u32[]{:S(2)}, u32[]{:S(2)}) collective-permute-start(bf16[192,256]{1,0:T(8,128)(2,1)S(1)} %bitcast.14), channel_id=1, source_target_pairs={{0,2},{2,0},{4,6},{6,4},{8,10},{10,8},{12,14},{14,12},{16,18},{18,... | collective-permute-start | bytes 294920 | tf_op jit(solution)/shard_map/ppermute | solution.py:23
  12.8 0.8 %collective-permute-done.2.mate_ref = bf16[2,32,256]{2,1,0:T(8,128)(2,1)S(1)} collective-permute-done((bf16[2,32,256]{2,1,0:T(8,128)(2,1)S(1)}, bf16[2,32,256]{2,1,0:T(8,128)(2,1)S(1)}, u32[]{:S(2)}, u32[]{:S(2)}) %collective-permute-start.2) | collective-permute-done | bytes 32800 | tf_op jit(solution)/shard_map/ppermute | solution.py:23
  13.6 0.7 %collective-permute-start.3 = (bf16[192,256]{1,0:T(8,128)(2,1)S(1)}, bf16[192,256]{1,0:T(8,128)(2,1)S(1)}, u32[]{:S(2)}, u32[]{:S(2)}) collective-permute-start(bf16[192,256]{1,0:T(8,128)(2,1)S(1)} %bitcast.15), channel_id=1, source_target_pairs={{0,16},{2,18},{4,20},{6,22},{8,24},{10,26},{12,28},{14,30},{16,0},... | collective-permute-start | bytes 294920 | tf_op jit(solution)/shard_map/ppermute | solution.py:23
  14.3 0.0 collective-permute-done.4
  14.3 2.5 %collective-permute-start.9 = (bf16[2,4,32,256]{3,2,1,0:T(8,128)(2,1)S(1)}, bf16[2,4,32,256]{3,2,1,0:T(8,128)(2,1)S(1)}, u32[]{:S(2)}, u32[]{:S(2)}) collective-permute-start(bf16[2,4,32,256]{3,2,1,0:T(8,128)(2,1)S(1)} %pad_maximum_fusion.6.refs_0_), channel_id=1, source_target_pairs={{0,6},{2,4},{4,2},{6,0},{8,14},{10,12},{12,10},{14,8},{16,22},{18,... | collective-permute-start | bytes 393224 | tf_op jit(solution)/shard_map/ppermute | solution.py:23
  16.8 0.5 %collective-permute-start.5 = (bf16[2,4,32,256]{3,2,1,0:T(8,128)(2,1)S(1)}, bf16[2,4,32,256]{3,2,1,0:T(8,128)(2,1)S(1)}, u32[]{:S(2)}, u32[]{:S(2)}) collective-permute-start(bf16[2,4,32,256]{3,2,1,0:T(8,128)(2,1)S(1)} %pad_maximum_fusion.6.refs_0_), channel_id=1, source_target_pairs={{0,2},{2,0},{4,6},{6,4},{8,10},{10,8},{12,14},{14,12},{16,18},{18,... | collective-permute-start | bytes 393224 | tf_op jit(solution)/shard_map/ppermute | solution.py:23
  17.3 0.5 %collective-permute-start.6 = (bf16[2,4,32,256]{3,2,1,0:T(8,128)(2,1)S(1)}, bf16[2,4,32,256]{3,2,1,0:T(8,128)(2,1)S(1)}, u32[]{:S(2)}, u32[]{:S(2)}) collective-permute-start(bf16[2,4,32,256]{3,2,1,0:T(8,128)(2,1)S(1)} %pad_maximum_fusion.6.refs_0_), channel_id=1, source_target_pairs={{0,4},{2,6},{4,0},{6,2},{8,12},{10,14},{12,8},{14,10},{16,20},{18,... | collective-permute-start | bytes 393224 | tf_op jit(solution)/shard_map/ppermute | solution.py:23
  17.9 1.3 %collective-permute-done.3 = bf16[192,256]{1,0:T(8,128)(2,1)S(1)} collective-permute-done((bf16[192,256]{1,0:T(8,128)(2,1)S(1)}, bf16[192,256]{1,0:T(8,128)(2,1)S(1)}, u32[]{:S(2)}, u32[]{:S(2)}) %collective-permute-start.3) | collective-permute-done | bytes 98336 | tf_op jit(solution)/shard_map/ppermute | solution.py:23
  19.1 2.8 %collective-permute-start.7 = (bf16[1,192,256]{2,1,0:T(8,128)(2,1)S(1)}, bf16[1,192,256]{2,1,0:T(8,128)(2,1)S(1)}, u32[]{:S(2)}, u32[]{:S(2)}) collective-permute-start(bf16[1,192,256]{2,1,0:T(8,128)(2,1)S(1)} %bitcast.20), channel_id=1, source_target_pairs={{0,2},{2,0},{4,6},{6,4},{8,10},{10,8},{12,14},{14,12},{16,18},{18,... | collective-permute-start | bytes 294920 | tf_op jit(solution)/shard_map/ppermute | solution.py:23
  22.0 0.0 collective-permute-done.11
  22.0 1.5 %collective-permute-start.8 = (bf16[1,192,256]{2,1,0:T(8,128)(2,1)S(1)}, bf16[1,192,256]{2,1,0:T(8,128)(2,1)S(1)}, u32[]{:S(2)}, u32[]{:S(2)}) collective-permute-start(bf16[1,192,256]{2,1,0:T(8,128)(2,1)S(1)} %bitcast.21), channel_id=1, source_target_pairs={{0,4},{2,6},{4,0},{6,2},{8,12},{10,14},{12,8},{14,10},{16,20},{18,... | collective-permute-start | bytes 294920 | tf_op jit(solution)/shard_map/ppermute | solution.py:23
  23.5 0.0 collective-permute-done.9.refs_3_
  23.5 0.6 %collective-permute-start.12 = (bf16[2,192,256]{2,1,0:T(8,128)(2,1)S(1)}, bf16[2,192,256]{2,1,0:T(8,128)(2,1)S(1)}, u32[]{:S(2)}, u32[]{:S(2)}) collective-permute-start(bf16[2,192,256]{2,1,0:T(8,128)(2,1)S(1)} %pad_maximum_fusion.1), channel_id=1, source_target_pairs={{0,4},{2,6},{4,0},{6,2},{8,12},{10,14},{12,8},{14,10},{16,20},{18,... | collective-permute-start | bytes 589832 | tf_op jit(solution)/shard_map/ppermute | solution.py:23
  24.1 0.5 %collective-permute-done.7 = bf16[1,192,256]{2,1,0:T(8,128)(2,1)S(1)} collective-permute-done((bf16[1,192,256]{2,1,0:T(8,128)(2,1)S(1)}, bf16[1,192,256]{2,1,0:T(8,128)(2,1)S(1)}, u32[]{:S(2)}, u32[]{:S(2)}) %collective-permute-start.7) | collective-permute-done | bytes 98336 | tf_op jit(solution)/shard_map/ppermute | solution.py:23
  24.6 2.2 %collective-permute-done.8 = bf16[1,192,256]{2,1,0:T(8,128)(2,1)S(1)} collective-permute-done((bf16[1,192,256]{2,1,0:T(8,128)(2,1)S(1)}, bf16[1,192,256]{2,1,0:T(8,128)(2,1)S(1)}, u32[]{:S(2)}, u32[]{:S(2)}) %collective-permute-start.8) | collective-permute-done | bytes 98336 | tf_op jit(solution)/shard_map/ppermute | solution.py:23
  26.8 0.0 collective-permute-done.5.refs_1_
  26.8 0.0 collective-permute-done.6.refs_2_
  26.8 1.1 %shard_map.75.part_ref = bf16[128,384]{1,0:T(8,128)(2,1)S(1)} custom-call(bf16[2,32,256]{2,1,0:T(8,128)(2,1)S(1)} %get-tuple-element.37.q_ref, bf16[2,32,256]{2,1,0:T(8,128)(2,1)S(1)} %collective-permute-done.2.mate_ref, bf16[2,32,256]{2,1,0:T(8,128)(2,1)S(1)} %get-tuple-element.43.kv1_ref, bf16[2,4,32,256]{3,2,1,0:T(8,128)(2,1)S(1)} %pad_maximum_fusion.6.refs_0_, ...), custom_call_target="tpu_custom_call" | custom-call | flops 33554432 | tf_op jit(solution)/shard_map/pallas_call | solution.py:276
  27.9 1.2 %collective-permute-start.10 = (bf16[128,384]{1,0:T(8,128)(2,1)S(1)}, bf16[128,384]{1,0:T(8,128)(2,1)S(1)}, u32[]{:S(2)}, u32[]{:S(2)}) collective-permute-start(bf16[128,384]{1,0:T(8,128)(2,1)S(1)} %shard_map.75.part_ref), channel_id=1, source_target_pairs={{0,8},{2,10},{4,12},{6,14},{8,0},{10,2},{12,4},{14,6},{16,24},{18,... | collective-permute-start | bytes 294920 | tf_op jit(solution)/shard_map/ppermute | solution.py:23
  29.1 1.6 %collective-permute-start.13 = (bf16[1,192,256]{2,1,0:T(8,128)(2,1)S(1)}, bf16[1,192,256]{2,1,0:T(8,128)(2,1)S(1)}, u32[]{:S(2)}, u32[]{:S(2)}) collective-permute-start(bf16[1,192,256]{2,1,0:T(8,128)(2,1)S(1)} %bitcast.22), channel_id=1, source_target_pairs={{0,6},{2,4},{4,2},{6,0},{8,14},{10,12},{12,10},{14,8},{16,22},{18,... | collective-permute-start | bytes 294920 | tf_op jit(solution)/shard_map/ppermute | solution.py:23
  30.6 2.0 %collective-permute-done.10.other_ref = bf16[128,384]{1,0:T(8,128)(2,1)S(1)} collective-permute-done((bf16[128,384]{1,0:T(8,128)(2,1)S(1)}, bf16[128,384]{1,0:T(8,128)(2,1)S(1)}, u32[]{:S(2)}, u32[]{:S(2)}) %collective-permute-start.10) | collective-permute-done | bytes 98336 | tf_op jit(solution)/shard_map/ppermute | solution.py:23
  32.6 0.2 shard_map.76.o_ref
  32.8 1.8 %collective-permute-done.13 = bf16[1,192,256]{2,1,0:T(8,128)(2,1)S(1)} collective-permute-done((bf16[1,192,256]{2,1,0:T(8,128)(2,1)S(1)}, bf16[1,192,256]{2,1,0:T(8,128)(2,1)S(1)}, u32[]{:S(2)}, u32[]{:S(2)}) %collective-permute-start.13) | collective-permute-done | bytes 98336 | tf_op jit(solution)/shard_map/ppermute | solution.py:23
  34.6 0.0 collective-permute-done.12
  34.7 0.4 shard_map.78
  35.1 0.1 collective-permute-start.14
  35.1 0.4 shard_map.81
  35.5 0.6 %collective-permute-start.16 = (bf16[64,768]{1,0:T(8,128)(2,1)S(1)}, bf16[64,768]{1,0:T(8,128)(2,1)S(1)}, u32[]{:S(2)}, u32[]{:S(2)}) collective-permute-start(bf16[64,768]{1,0:T(8,128)(2,1)S(1)} %shard_map.81), channel_id=1, source_target_pairs={{0,1},{1,0},{2,3},{3,2},{4,5},{5,4},{6,7},{7,6},{8,9},{9,8},{10,11... | collective-permute-start | bytes 294920 | tf_op jit(solution)/shard_map/ppermute | solution.py:23
  36.0 0.4 shard_map.77.refs_0_
  36.4 0.0 collective-permute-done.14.refs_1_
  36.4 0.1 shard_map.79
  36.5 1.0 %collective-permute-start.15 = (bf16[2,32,768]{2,1,0:T(8,128)(2,1)S(1)}, bf16[2,32,768]{2,1,0:T(8,128)(2,1)S(1)}, u32[]{:S(2)}, u32[]{:S(2)}) collective-permute-start(bf16[2,32,768]{2,1,0:T(8,128)(2,1)S(1)} %shard_map.79), channel_id=1, source_target_pairs={{0,8},{2,10},{4,12},{6,14},{8,0},{10,2},{12,4},{14,6},{16,24},{18,... | collective-permute-start | bytes 294920 | tf_op jit(solution)/shard_map/ppermute | solution.py:23
  37.5 0.4 shard_map.80.refs_0_
  37.9 0.0 collective-permute-done.16.refs_1_
  37.9 0.1 shard_map.82
  38.0 3.4 %collective-permute-done.15 = bf16[2,32,768]{2,1,0:T(8,128)(2,1)S(1)} collective-permute-done((bf16[2,32,768]{2,1,0:T(8,128)(2,1)S(1)}, bf16[2,32,768]{2,1,0:T(8,128)(2,1)S(1)}, u32[]{:S(2)}, u32[]{:S(2)}) %collective-permute-start.15) | collective-permute-done | bytes 98336 | tf_op jit(solution)/shard_map/ppermute | solution.py:23
  41.5 0.7 %pad_maximum_fusion.5 = bf16[2,32,1536]{2,1,0:T(8,128)(2,1)} fusion(bf16[2,32,768]{2,1,0:T(8,128)(2,1)S(1)} %get-tuple-element.56, bf16[2,32,768]{2,1,0:T(8,128)(2,1)S(1)} %get-tuple-element.55), kind=kLoop, calls=%fused_computation.5 | loop fusion | flops 393216 | bytes 393216 | tf_op jit(solution)/shard_map/concatenate | solution.py:311
  (6 shorter events, 0.1 us)
Async XLA Ops:
  0.0 4.4 %collective-permute-start = (bf16[2,32,1536]{2,1,0:T(8,128)(2,1)}, bf16[2,32,1536]{2,1,0:T(8,128)(2,1)S(1)}, u32[]{:S(2)}, u32[]{:S(2)}) collective-permute-start(bf16[2,32,1536]{2,1,0:T(8,128)(2,1)} %x_ref.1), channel_id=1, source_target_pairs={{0,1},{1,0},{2,3},{3,2},{4,5},{5,4},{6,7},{7,6},{8,9},{9,8},{10,11... | collective-permute-start | bytes 589832 | tf_op jit(solution)/shard_map/ppermute | solution.py:23
  0.5 3.9 %collective-permute-start.1 = (f32[4,3,1536]{2,0,1:T(4,128)}, f32[4,3,1536]{2,0,1:T(4,128)S(1)}, u32[]{:S(2)}, u32[]{:S(2)}) collective-permute-start(f32[4,3,1536]{2,0,1:T(4,128)} %param.11), channel_id=1, source_target_pairs={{0,1},{1,0},{2,3},{3,2},{4,5},{5,4},{6,7},{7,6},{8,9},{9,8},{10,11... | collective-permute-start | bytes 221192 | tf_op jit(solution)/shard_map/ppermute | solution.py:23
  1.2 10.1 %copy-start = (bf16[256,192]{0,1:T(8,128)(2,1)S(1)}, bf16[256,192]{0,1:T(8,128)(2,1)}, u32[]{:S(2)}) copy-start(bf16[256,192]{0,1:T(8,128)(2,1)} %param.10) | copy-start | bytes 294916
  5.6 8.7 %collective-permute-start.4 = (bf16[4,32,256]{2,1,0:T(8,128)(2,1)S(1)}, bf16[4,32,256]{2,1,0:T(8,128)(2,1)S(1)}, u32[]{:S(2)}, u32[]{:S(2)}) collective-permute-start(bf16[4,32,256]{2,1,0:T(8,128)(2,1)S(1)} %get-tuple-element.44), channel_id=1, source_target_pairs={{0,16},{2,18},{4,20},{6,22},{8,24},{10,26},{12,28},{14,30},{16,0},... | collective-permute-start | bytes 196616 | tf_op jit(solution)/shard_map/ppermute | solution.py:23
  9.7 3.9 %collective-permute-start.2 = (bf16[2,32,256]{2,1,0:T(8,128)(2,1)S(1)}, bf16[2,32,256]{2,1,0:T(8,128)(2,1)S(1)}, u32[]{:S(2)}, u32[]{:S(2)}) collective-permute-start(bf16[2,32,256]{2,1,0:T(8,128)(2,1)S(1)} %get-tuple-element.37.q_ref), channel_id=1, source_target_pairs={{0,8},{2,10},{4,12},{6,14},{8,0},{10,2},{12,4},{14,6},{16,24},{18,... | collective-permute-start | bytes 98312 | tf_op jit(solution)/shard_map/ppermute | solution.py:23
  11.3 10.7 %collective-permute-start.11 = (bf16[192,256]{1,0:T(8,128)(2,1)S(1)}, bf16[192,256]{1,0:T(8,128)(2,1)S(1)}, u32[]{:S(2)}, u32[]{:S(2)}) collective-permute-start(bf16[192,256]{1,0:T(8,128)(2,1)S(1)} %bitcast.14), channel_id=1, source_target_pairs={{0,2},{2,0},{4,6},{6,4},{8,10},{10,8},{12,14},{14,12},{16,18},{18,... | collective-permute-start | bytes 294920 | tf_op jit(solution)/shard_map/ppermute | solution.py:23
  13.6 5.5 %collective-permute-start.3 = (bf16[192,256]{1,0:T(8,128)(2,1)S(1)}, bf16[192,256]{1,0:T(8,128)(2,1)S(1)}, u32[]{:S(2)}, u32[]{:S(2)}) collective-permute-start(bf16[192,256]{1,0:T(8,128)(2,1)S(1)} %bitcast.15), channel_id=1, source_target_pairs={{0,16},{2,18},{4,20},{6,22},{8,24},{10,26},{12,28},{14,30},{16,0},... | collective-permute-start | bytes 294920 | tf_op jit(solution)/shard_map/ppermute | solution.py:23
  14.3 9.2 %collective-permute-start.9 = (bf16[2,4,32,256]{3,2,1,0:T(8,128)(2,1)S(1)}, bf16[2,4,32,256]{3,2,1,0:T(8,128)(2,1)S(1)}, u32[]{:S(2)}, u32[]{:S(2)}) collective-permute-start(bf16[2,4,32,256]{3,2,1,0:T(8,128)(2,1)S(1)} %pad_maximum_fusion.6.refs_0_), channel_id=1, source_target_pairs={{0,6},{2,4},{4,2},{6,0},{8,14},{10,12},{12,10},{14,8},{16,22},{18,... | collective-permute-start | bytes 393224 | tf_op jit(solution)/shard_map/ppermute | solution.py:23
  16.8 10.0 %collective-permute-start.5 = (bf16[2,4,32,256]{3,2,1,0:T(8,128)(2,1)S(1)}, bf16[2,4,32,256]{3,2,1,0:T(8,128)(2,1)S(1)}, u32[]{:S(2)}, u32[]{:S(2)}) collective-permute-start(bf16[2,4,32,256]{3,2,1,0:T(8,128)(2,1)S(1)} %pad_maximum_fusion.6.refs_0_), channel_id=1, source_target_pairs={{0,2},{2,0},{4,6},{6,4},{8,10},{10,8},{12,14},{14,12},{16,18},{18,... | collective-permute-start | bytes 393224 | tf_op jit(solution)/shard_map/ppermute | solution.py:23
  17.3 9.5 %collective-permute-start.6 = (bf16[2,4,32,256]{3,2,1,0:T(8,128)(2,1)S(1)}, bf16[2,4,32,256]{3,2,1,0:T(8,128)(2,1)S(1)}, u32[]{:S(2)}, u32[]{:S(2)}) collective-permute-start(bf16[2,4,32,256]{3,2,1,0:T(8,128)(2,1)S(1)} %pad_maximum_fusion.6.refs_0_), channel_id=1, source_target_pairs={{0,4},{2,6},{4,0},{6,2},{8,12},{10,14},{12,8},{14,10},{16,20},{18,... | collective-permute-start | bytes 393224 | tf_op jit(solution)/shard_map/ppermute | solution.py:23
  19.1 5.4 %collective-permute-start.7 = (bf16[1,192,256]{2,1,0:T(8,128)(2,1)S(1)}, bf16[1,192,256]{2,1,0:T(8,128)(2,1)S(1)}, u32[]{:S(2)}, u32[]{:S(2)}) collective-permute-start(bf16[1,192,256]{2,1,0:T(8,128)(2,1)S(1)} %bitcast.20), channel_id=1, source_target_pairs={{0,2},{2,0},{4,6},{6,4},{8,10},{10,8},{12,14},{14,12},{16,18},{18,... | collective-permute-start | bytes 294920 | tf_op jit(solution)/shard_map/ppermute | solution.py:23
  22.0 4.8 %collective-permute-start.8 = (bf16[1,192,256]{2,1,0:T(8,128)(2,1)S(1)}, bf16[1,192,256]{2,1,0:T(8,128)(2,1)S(1)}, u32[]{:S(2)}, u32[]{:S(2)}) collective-permute-start(bf16[1,192,256]{2,1,0:T(8,128)(2,1)S(1)} %bitcast.21), channel_id=1, source_target_pairs={{0,4},{2,6},{4,0},{6,2},{8,12},{10,14},{12,8},{14,10},{16,20},{18,... | collective-permute-start | bytes 294920 | tf_op jit(solution)/shard_map/ppermute | solution.py:23
  23.5 11.1 %collective-permute-start.12 = (bf16[2,192,256]{2,1,0:T(8,128)(2,1)S(1)}, bf16[2,192,256]{2,1,0:T(8,128)(2,1)S(1)}, u32[]{:S(2)}, u32[]{:S(2)}) collective-permute-start(bf16[2,192,256]{2,1,0:T(8,128)(2,1)S(1)} %pad_maximum_fusion.1), channel_id=1, source_target_pairs={{0,4},{2,6},{4,0},{6,2},{8,12},{10,14},{12,8},{14,10},{16,20},{18,... | collective-permute-start | bytes 589832 | tf_op jit(solution)/shard_map/ppermute | solution.py:23
  27.9 4.7 %collective-permute-start.10 = (bf16[128,384]{1,0:T(8,128)(2,1)S(1)}, bf16[128,384]{1,0:T(8,128)(2,1)S(1)}, u32[]{:S(2)}, u32[]{:S(2)}) collective-permute-start(bf16[128,384]{1,0:T(8,128)(2,1)S(1)} %shard_map.75.part_ref), channel_id=1, source_target_pairs={{0,8},{2,10},{4,12},{6,14},{8,0},{10,2},{12,4},{14,6},{16,24},{18,... | collective-permute-start | bytes 294920 | tf_op jit(solution)/shard_map/ppermute | solution.py:23
  29.1 5.5 %collective-permute-start.13 = (bf16[1,192,256]{2,1,0:T(8,128)(2,1)S(1)}, bf16[1,192,256]{2,1,0:T(8,128)(2,1)S(1)}, u32[]{:S(2)}, u32[]{:S(2)}) collective-permute-start(bf16[1,192,256]{2,1,0:T(8,128)(2,1)S(1)} %bitcast.22), channel_id=1, source_target_pairs={{0,6},{2,4},{4,2},{6,0},{8,14},{10,12},{12,10},{14,8},{16,22},{18,... | collective-permute-start | bytes 294920 | tf_op jit(solution)/shard_map/ppermute | solution.py:23
  35.1 1.4 %collective-permute-start.14 = (bf16[64,768]{1,0:T(8,128)(2,1)S(1)}, bf16[64,768]{1,0:T(8,128)(2,1)S(1)}, u32[]{:S(2)}, u32[]{:S(2)}) collective-permute-start(bf16[64,768]{1,0:T(8,128)(2,1)S(1)} %shard_map.78), channel_id=1, source_target_pairs={{0,1},{1,0},{2,3},{3,2},{4,5},{5,4},{6,7},{7,6},{8,9},{9,8},{10,11... | collective-permute-start | bytes 294920 | tf_op jit(solution)/shard_map/ppermute | solution.py:23
  35.5 2.4 %collective-permute-start.16 = (bf16[64,768]{1,0:T(8,128)(2,1)S(1)}, bf16[64,768]{1,0:T(8,128)(2,1)S(1)}, u32[]{:S(2)}, u32[]{:S(2)}) collective-permute-start(bf16[64,768]{1,0:T(8,128)(2,1)S(1)} %shard_map.81), channel_id=1, source_target_pairs={{0,1},{1,0},{2,3},{3,2},{4,5},{5,4},{6,7},{7,6},{8,9},{9,8},{10,11... | collective-permute-start | bytes 294920 | tf_op jit(solution)/shard_map/ppermute | solution.py:23
  36.5 4.9 %collective-permute-start.15 = (bf16[2,32,768]{2,1,0:T(8,128)(2,1)S(1)}, bf16[2,32,768]{2,1,0:T(8,128)(2,1)S(1)}, u32[]{:S(2)}, u32[]{:S(2)}) collective-permute-start(bf16[2,32,768]{2,1,0:T(8,128)(2,1)S(1)} %shard_map.79), channel_id=1, source_target_pairs={{0,8},{2,10},{4,12},{6,14},{8,0},{10,2},{12,4},{14,6},{16,24},{18,... | collective-permute-start | bytes 294920 | tf_op jit(solution)/shard_map/ppermute | solution.py:23

commit v22 on v20

--- a/solution.py
+++ b/solution.py
@@ -91,23 +91,31 @@
     return jnp.concatenate(blocks, axis=1)
 
 
-def qkv_kernel(n_head, head, ids_ref, *refs):
+def fresh_kernel(n_head, head, ids_ref, *refs):
     x_refs, mod_refs = refs[:n_head], refs[n_head : 2 * n_head]
-    w_ref, cos_ref, sin_ref, stale_ref, q_ref, kv_ref, kv1_ref = refs[2 * n_head :]
-    rows = x_refs[0].shape[1]
-    steps = [normalized(step, x_refs, mod_refs, ids_ref) for step in range(STEPS)]
-    parts = [jnp.concatenate(pair, axis=0) for pair in zip(*steps)]
-    cos = jnp.concatenate([cos_ref[...]] * STEPS, axis=0)
-    sin = jnp.concatenate([sin_ref[...]] * STEPS, axis=0)
-    queries = rotated(projected(parts, w_ref, 0, head), cos, sin).astype(BF16)
-    keys = rotated(projected(parts, w_ref, 1, head), cos, sin).astype(BF16)
-    values = projected(parts, w_ref, 2, head).astype(BF16)
+    w_ref, cos_ref, sin_ref, stale_ref, a_ref, kv_ref = refs[2 * n_head :]
+    parts = normalized(0, x_refs, mod_refs, ids_ref)
+    for number, part in enumerate(parts):
+        a_ref[number] = part
+    keys = rotated(projected(parts, w_ref, 1, head), cos_ref[...], sin_ref[...])
+    kv_ref[:2] = stale_ref[...]
+    kv_ref[2] = keys.astype(BF16)
+    kv_ref[3] = projected(parts, w_ref, 2, head).astype(BF16)
+
+
+def rest_kernel(n_head, head, ids_ref, *refs):
+    x_refs, mod_refs = refs[:n_head], refs[n_head : 2 * n_head]
+    w_ref, cos_ref, sin_ref, a_ref, q_ref, kv1_ref = refs[2 * n_head :]
+    rows = a_ref.shape[1]
+    parts = normalized(1, x_refs, mod_refs, ids_ref)
+    cos, sin = cos_ref[...], sin_ref[...]
+    both = [jnp.concatenate([a_ref[k], part], axis=0) for k, part in enumerate(parts)]
+    queries = projected(both, w_ref, 0, head)
     for step in range(STEPS):
         spot = slice(step * rows, (step + 1) * rows)
-        q_ref[step] = queries[spot]
-    kv_ref[:2] = stale_ref[...]
-    kv_ref[2], kv_ref[3] = keys[:rows], values[:rows]
-    kv1_ref[0], kv1_ref[1] = keys[rows:], values[rows:]
+        q_ref[step] = rotated(queries[spot], cos, sin).astype(BF16)
+    kv1_ref[0] = rotated(projected(parts, w_ref, 1, head), cos, sin).astype(BF16)
+    kv1_ref[1] = projected(parts, w_ref, 2, head).astype(BF16)
 
 
 def split3(values):
@@ -251,20 +259,28 @@
 
 
     kv_shape = shaped((2, rows, cols), BF16)
-    q, kv, kv1 = call(
-        functools.partial(qkv_kernel, n_head),
-        (kv_shape, shaped((4, rows, cols), BF16), kv_shape),
-        [SMEM] + [VMEM] * (2 * n_head + 5),
-        flops=2 * STEPS * rows * w_qkv.size,
+    common = (head[None], ids, *x_parts, *mod_parts, w, cos, sin)
+    specs = [SMEM] + [VMEM] * (2 * n_head + 5)
+    a, kv = call(
+        functools.partial(fresh_kernel, n_head),
+        (shaped((n_head, rows, feats), BF16), shaped((4, rows, cols), BF16)),
+        specs,
+        flops=4 * rows * w_qkv.size // 3,
         size=2 * w_qkv.size,
-    )(head[None], ids, *x_parts, *mod_parts, w, cos, sin, stale)
-
-    w_own, kv = lax.optimization_barrier((w_out.T, kv))
+    )(*common, stale)
+    q, kv1 = call(
+        functools.partial(rest_kernel, n_head),
+        (kv_shape, kv_shape),
+        specs,
+        flops=8 * rows * w_qkv.size // 3,
+        size=2 * w_qkv.size,
+    )(*common, a)
+
+    w_own, kv1 = lax.optimization_barrier((w_out.T, kv1))
     kv_pair = line_of(kv)
     q_mate = across(q, PLANE)
     w_x = across(w_own, 1)
-    w_late, q_mate = lax.optimization_barrier((w_own, q_mate))
-    w_rest = jnp.stack(line_of(w_late)[1:])
+    w_rest = jnp.stack(line_of(w_own)[1:])
     kv_plane = plane_of(jnp.stack(kv_pair))
     w_rest, q_mate = lax.optimization_barrier((w_rest, q_mate))
     w_y = across(jnp.stack([w_own, w_x]), 2)

time: 40.4 us -> 40.6 us (level)
  waiting for transfers between devices: 13.2 us -> 10.6 us
  starting transfers between devices: 18 us -> 20.2 us
  Pallas kernels: 7.33 us -> 7.98 us
    ppermute x16, waiting for transfers between devices: 13.2 us -> 10.6 us  [swap(): return lax.ppermute(values, axis, [(i, i ^ bit) for i in range(count)])]
    ppermute x16, starting transfers between devices: 18 us -> 20.2 us  [swap(): return lax.ppermute(values, axis, [(i, i ^ bit) for i in range(count)])]
    pallas_call x1 -> x2, Pallas kernels: 1.16 us -> 1.95 us  [the longest x1 1.11 us: body(): call(functools.partial(rest_kernel, n_head), (kv_shape, kv_shape), specs,...]
  transfers between devices with their start and end apart: 16 -> 16, of which waited for: 6 -> 6; matrix products, arithmetic and copies ran while one was open for 0% -> 0% of each run, Pallas kernels for 14% -> 17%
where the time goes in v22:
time: 40.6 us; the launch traced here: 40.5 us
  starting transfers between devices  20.2 us (50%)
  waiting for transfers between devices  10.6 us (26%)
  Pallas kernels  7.98 us (20%)
  other arithmetic  0.84 us (2%)
  between operations  0.84 us (2%)
    ppermute x16, starting transfers between devices, swap(): return lax.ppermute(values, axis, [(i, i ^ bit) for i in range(count)])  20.2 us
    ppermute x16, waiting for transfers between devices, swap(): return lax.ppermute(values, axis, [(i, i ^ bit) for i in range(count)])  10.6 us
    pallas_call x1, Pallas kernels, body(): call(load_kernel, tuple((pltpu.VMEM(v.shape, v.dtype) for v in first)) +...  3.08 us
    pallas_call x4, Pallas kernels, project(): call(functools.partial(project_kernel, n_head, n_patch, bit, mate), shape...  1.4 us
    pallas_call x1, Pallas kernels, body(): call(attend_kernel, shaped((tall, cols + DH), BF16), [VMEM] * (3 + PLANE)...  1.11 us
    pallas_call x1, Pallas kernels, body(): call(functools.partial(rest_kernel, n_head), (kv_shape, kv_shape), specs,...  1.11 us
    pallas_call x1, Pallas kernels, body(): call(functools.partial(fresh_kernel, n_head), (shaped((n_head, rows, feat...  0.85 us
  transfers between devices with their start and end apart: 16, of which 6 were waited for; matrix products, arithmetic and copies ran while one was open for 0% of the time, Pallas kernels for 17%

profile of v22, /device:TPU:0, one launch (start us, length us, event | category | flops | bytes accessed | tf_op | source)
XLA Modules:
  0.0 40.5 jit_solution(11994582633341183913)
XLA Ops:
  0.0 0.5 %collective-permute-start = (bf16[2,32,1536]{2,1,0:T(8,128)(2,1)}, bf16[2,32,1536]{2,1,0:T(8,128)(2,1)S(1)}, u32[]{:S(2)}, u32[]{:S(2)}) collective-permute-start(bf16[2,32,1536]{2,1,0:T(8,128)(2,1)} %x_ref.1), channel_id=1, source_target_pairs={{0,1},{1,0},{2,3},{3,2},{4,5},{5,4},{6,7},{7,6},{8,9},{9,8},{10,11... | collective-permute-start | bytes 589832 | tf_op jit(solution)/shard_map/ppermute | solution.py:23
  0.5 0.1 collective-permute-start.1
  1.2 3.1 %shard_map.73 = (bf16[3,3072,256]{2,1,0:T(8,128)(2,1)S(1)}, bf16[2,32,1536]{2,1,0:T(8,128)(2,1)S(1)}, f32[3,4,1536]{2,1,0:T(4,128)S(1)}, bf16[2,32,256]{2,1,0:T(...) custom-call(s32[2]{0:T(128)} %ids.1, s32[1]{0:T(128)S(6)} %copy.8.slab, ...), custom_call_target="tpu_custom_call" | custom-call | bytes 4718592 | tf_op jit(solution)/shard_map/pallas_call | solution.py:240
  4.3 0.0 collective-permute-done.1
  4.3 0.0 collective-permute-done.refs_1_
  4.3 0.0 copy-start
  4.3 0.8 %shard_map.74 = (bf16[2,32,1536]{2,1,0:T(8,128)(2,1)S(1)}, bf16[4,32,256]{2,1,0:T(8,128)(2,1)S(1)}) custom-call(s32[1]{0:T(128)} %bitcast.3.head, s32[8,128]{1,0:T(8,128)S(1)} %get-tuple-element.25.ids_ref, bf16[2,32,1536]{2,1,0:T(8,128)(2,1)S(1)} %get-tuple-element.27.refs_0_, bf16[2,32,1536]{2,1,0:T(8,128)(2,1)S(1)} %collective-permute-done.refs_1_, ...), custom_call_target="tpu_custom_call" | custom-call | flops 100663296 | bytes 4718592 | tf_op jit(solution)/shard_map/pallas_call | solution.py:264
  5.1 4.1 %collective-permute-start.5 = (bf16[4,32,256]{2,1,0:T(8,128)(2,1)S(1)}, bf16[4,32,256]{2,1,0:T(8,128)(2,1)S(1)}, u32[]{:S(2)}, u32[]{:S(2)}) collective-permute-start(bf16[4,32,256]{2,1,0:T(8,128)(2,1)S(1)} %get-tuple-element.39), channel_id=1, source_target_pairs={{0,16},{2,18},{4,20},{6,22},{8,24},{10,26},{12,28},{14,30},{16,0},... | collective-permute-start | bytes 196616 | tf_op jit(solution)/shard_map/ppermute | solution.py:23
  9.2 1.1 %shard_map.75 = (bf16[2,32,256]{2,1,0:T(8,128)(2,1)S(1)}, bf16[2,32,256]{2,1,0:T(8,128)(2,1)S(1)}) custom-call(s32[1]{0:T(128)} %bitcast.3.head, s32[8,128]{1,0:T(8,128)S(1)} %get-tuple-element.25.ids_ref, bf16[2,32,1536]{2,1,0:T(8,128)(2,1)S(1)} %get-tuple-element.27.refs_0_, bf16[2,32,1536]{2,1,0:T(8,128)(2,1)S(1)} %collective-permute-done.refs_1_, ...), custom_call_target="tpu_custom_call" | custom-call | flops 201326592 | bytes 4718592 | tf_op jit(solution)/shard_map/pallas_call | solution.py:271
  10.4 0.0 copy-done
  10.4 0.1 collective-permute-start.2
  10.5 1.8 %collective-permute-start.10 = (bf16[192,256]{1,0:T(8,128)(2,1)S(1)}, bf16[192,256]{1,0:T(8,128)(2,1)S(1)}, u32[]{:S(2)}, u32[]{:S(2)}) collective-permute-start(bf16[192,256]{1,0:T(8,128)(2,1)S(1)} %bitcast.28), channel_id=1, source_target_pairs={{0,2},{2,0},{4,6},{6,4},{8,10},{10,8},{12,14},{14,12},{16,18},{18,... | collective-permute-start | bytes 294920 | tf_op jit(solution)/shard_map/ppermute | solution.py:23
  12.3 1.6 %collective-permute-start.3 = (bf16[2,32,256]{2,1,0:T(8,128)(2,1)S(1)}, bf16[2,32,256]{2,1,0:T(8,128)(2,1)S(1)}, u32[]{:S(2)}, u32[]{:S(2)}) collective-permute-start(bf16[2,32,256]{2,1,0:T(8,128)(2,1)S(1)} %get-tuple-element.35.q_ref), channel_id=1, source_target_pairs={{0,8},{2,10},{4,12},{6,14},{8,0},{10,2},{12,4},{14,6},{16,24},{18,... | collective-permute-start | bytes 98312 | tf_op jit(solution)/shard_map/ppermute | solution.py:23
  13.8 0.0 collective-permute-done.5
  13.9 1.0 %collective-permute-start.6 = (bf16[2,4,32,256]{3,2,1,0:T(8,128)(2,1)S(1)}, bf16[2,4,32,256]{3,2,1,0:T(8,128)(2,1)S(1)}, u32[]{:S(2)}, u32[]{:S(2)}) collective-permute-start(bf16[2,4,32,256]{3,2,1,0:T(8,128)(2,1)S(1)} %pad_maximum_fusion.7.refs_0_), channel_id=1, source_target_pairs={{0,2},{2,0},{4,6},{6,4},{8,10},{10,8},{12,14},{14,12},{16,18},{18,... | collective-permute-start | bytes 393224 | tf_op jit(solution)/shard_map/ppermute | solution.py:23
  14.8 1.5 %collective-permute-start.7 = (bf16[2,4,32,256]{3,2,1,0:T(8,128)(2,1)S(1)}, bf16[2,4,32,256]{3,2,1,0:T(8,128)(2,1)S(1)}, u32[]{:S(2)}, u32[]{:S(2)}) collective-permute-start(bf16[2,4,32,256]{3,2,1,0:T(8,128)(2,1)S(1)} %pad_maximum_fusion.7.refs_0_), channel_id=1, source_target_pairs={{0,4},{2,6},{4,0},{6,2},{8,12},{10,14},{12,8},{14,10},{16,20},{18,... | collective-permute-start | bytes 393224 | tf_op jit(solution)/shard_map/ppermute | solution.py:23
  16.3 0.1 collective-permute-done.3.mate_ref
  16.5 1.2 %collective-permute-start.8 = (bf16[2,4,32,256]{3,2,1,0:T(8,128)(2,1)S(1)}, bf16[2,4,32,256]{3,2,1,0:T(8,128)(2,1)S(1)}, u32[]{:S(2)}, u32[]{:S(2)}) collective-permute-start(bf16[2,4,32,256]{3,2,1,0:T(8,128)(2,1)S(1)} %pad_maximum_fusion.7.refs_0_), channel_id=1, source_target_pairs={{0,6},{2,4},{4,2},{6,0},{8,14},{10,12},{12,10},{14,8},{16,22},{18,... | collective-permute-start | bytes 393224 | tf_op jit(solution)/shard_map/ppermute | solution.py:23
  17.7 0.2 collective-permute-done.2
  17.9 1.5 %collective-permute-start.4 = (bf16[1,192,256]{2,1,0:T(8,128)(2,1)S(1)}, bf16[1,192,256]{2,1,0:T(8,128)(2,1)S(1)}, u32[]{:S(2)}, u32[]{:S(2)}) collective-permute-start(bf16[1,192,256]{2,1,0:T(8,128)(2,1)S(1)} %bitcast.24), channel_id=1, source_target_pairs={{0,4},{2,6},{4,0},{6,2},{8,12},{10,14},{12,8},{14,10},{16,20},{18,... | collective-permute-start | bytes 294920 | tf_op jit(solution)/shard_map/ppermute | solution.py:23
  19.4 0.0 collective-permute-done.10
  19.4 0.6 %collective-permute-start.11 = (bf16[2,192,256]{2,1,0:T(8,128)(2,1)S(1)}, bf16[2,192,256]{2,1,0:T(8,128)(2,1)S(1)}, u32[]{:S(2)}, u32[]{:S(2)}) collective-permute-start(bf16[2,192,256]{2,1,0:T(8,128)(2,1)S(1)} %get-tuple-element.52), channel_id=1, source_target_pairs={{0,4},{2,6},{4,0},{6,2},{8,12},{10,14},{12,8},{14,10},{16,20},{18,... | collective-permute-start | bytes 589832 | tf_op jit(solution)/shard_map/ppermute | solution.py:23
  20.0 0.0 collective-permute-done.6.refs_1_
  20.0 4.0 %collective-permute-done.7.refs_2_ = bf16[2,4,32,256]{3,2,1,0:T(8,128)(2,1)S(1)} collective-permute-done((bf16[2,4,32,256]{3,2,1,0:T(8,128)(2,1)S(1)}, bf16[2,4,32,256]{3,2,1,0:T(8,128)(2,1)S(1)}, u32[]{:S(2)}, u32[]{:S(2)}) %collective-permute-start.7) | collective-permute-done | bytes 131104 | tf_op jit(solution)/shard_map/ppermute | solution.py:23
  24.0 0.0 collective-permute-done.8.refs_3_
  24.0 1.1 %shard_map.76.part_ref = bf16[128,384]{1,0:T(8,128)(2,1)S(1)} custom-call(bf16[2,32,256]{2,1,0:T(8,128)(2,1)S(1)} %get-tuple-element.35.q_ref, bf16[2,32,256]{2,1,0:T(8,128)(2,1)S(1)} %collective-permute-done.3.mate_ref, bf16[2,32,256]{2,1,0:T(8,128)(2,1)S(1)} %get-tuple-element.38.kv1_ref, bf16[2,4,32,256]{3,2,1,0:T(8,128)(2,1)S(1)} %pad_maximum_fusion.7.refs_0_, ...), custom_call_target="tpu_custom_call" | custom-call | flops 33554432 | tf_op jit(solution)/shard_map/pallas_call | solution.py:289
  25.1 1.0 %collective-permute-done.4 = bf16[1,192,256]{2,1,0:T(8,128)(2,1)S(1)} collective-permute-done((bf16[1,192,256]{2,1,0:T(8,128)(2,1)S(1)}, bf16[1,192,256]{2,1,0:T(8,128)(2,1)S(1)}, u32[]{:S(2)}, u32[]{:S(2)}) %collective-permute-start.4) | collective-permute-done | bytes 98336 | tf_op jit(solution)/shard_map/ppermute | solution.py:23
  26.1 0.6 %collective-permute-start.12 = (bf16[2,1,192,256]{3,2,1,0:T(8,128)(2,1)S(1)}, bf16[2,1,192,256]{3,2,1,0:T(8,128)(2,1)S(1)}, u32[]{:S(2)}, u32[]{:S(2)}) collective-permute-start(bf16[2,1,192,256]{3,2,1,0:T(8,128)(2,1)S(1)} %pad_maximum_fusion.2), channel_id=1, source_target_pairs={{0,2},{2,0},{4,6},{6,4},{8,10},{10,8},{12,14},{14,12},{16,18},{18,... | collective-permute-start | bytes 589832 | tf_op jit(solution)/shard_map/ppermute | solution.py:23
  26.7 2.3 %collective-permute-start.9 = (bf16[128,384]{1,0:T(8,128)(2,1)S(1)}, bf16[128,384]{1,0:T(8,128)(2,1)S(1)}, u32[]{:S(2)}, u32[]{:S(2)}) collective-permute-start(bf16[128,384]{1,0:T(8,128)(2,1)S(1)} %shard_map.76.part_ref), channel_id=1, source_target_pairs={{0,8},{2,10},{4,12},{6,14},{8,0},{10,2},{12,4},{14,6},{16,24},{18,... | collective-permute-start | bytes 294920 | tf_op jit(solution)/shard_map/ppermute | solution.py:23
  29.0 2.6 %collective-permute-done.9.other_ref = bf16[128,384]{1,0:T(8,128)(2,1)S(1)} collective-permute-done((bf16[128,384]{1,0:T(8,128)(2,1)S(1)}, bf16[128,384]{1,0:T(8,128)(2,1)S(1)}, u32[]{:S(2)}, u32[]{:S(2)}) %collective-permute-start.9) | collective-permute-done | bytes 98336 | tf_op jit(solution)/shard_map/ppermute | solution.py:23
  31.6 0.2 shard_map.77.o_ref
  31.8 0.0 collective-permute-done.11
  31.9 0.0 collective-permute-done.12
  32.0 0.3 shard_map.79
  32.3 0.1 collective-permute-start.13
  32.4 0.4 shard_map.82
  32.8 0.6 %collective-permute-start.15 = (bf16[64,768]{1,0:T(8,128)(2,1)S(1)}, bf16[64,768]{1,0:T(8,128)(2,1)S(1)}, u32[]{:S(2)}, u32[]{:S(2)}) collective-permute-start(bf16[64,768]{1,0:T(8,128)(2,1)S(1)} %shard_map.82), channel_id=1, source_target_pairs={{0,1},{1,0},{2,3},{3,2},{4,5},{5,4},{6,7},{7,6},{8,9},{9,8},{10,11... | collective-permute-start | bytes 294920 | tf_op jit(solution)/shard_map/ppermute | solution.py:23
  33.3 0.4 shard_map.78.refs_0_
  33.7 0.0 collective-permute-done.13.refs_1_
  33.7 0.1 shard_map.80
  33.8 2.8 %collective-permute-start.14 = (bf16[2,32,768]{2,1,0:T(8,128)(2,1)S(1)}, bf16[2,32,768]{2,1,0:T(8,128)(2,1)S(1)}, u32[]{:S(2)}, u32[]{:S(2)}) collective-permute-start(bf16[2,32,768]{2,1,0:T(8,128)(2,1)S(1)} %shard_map.80), channel_id=1, source_target_pairs={{0,8},{2,10},{4,12},{6,14},{8,0},{10,2},{12,4},{14,6},{16,24},{18,... | collective-permute-start | bytes 294920 | tf_op jit(solution)/shard_map/ppermute | solution.py:23
  36.6 0.3 shard_map.81.refs_0_
  37.0 0.0 collective-permute-done.15.refs_1_
  37.0 0.1 shard_map.83
  37.1 2.6 %collective-permute-done.14 = bf16[2,32,768]{2,1,0:T(8,128)(2,1)S(1)} collective-permute-done((bf16[2,32,768]{2,1,0:T(8,128)(2,1)S(1)}, bf16[2,32,768]{2,1,0:T(8,128)(2,1)S(1)}, u32[]{:S(2)}, u32[]{:S(2)}) %collective-permute-start.14) | collective-permute-done | bytes 98336 | tf_op jit(solution)/shard_map/ppermute | solution.py:23
  39.8 0.7 %pad_maximum_fusion.6 = bf16[2,32,1536]{2,1,0:T(8,128)(2,1)} fusion(bf16[2,32,768]{2,1,0:T(8,128)(2,1)S(1)} %get-tuple-element.46, bf16[2,32,768]{2,1,0:T(8,128)(2,1)S(1)} %get-tuple-element.45), kind=kLoop, calls=%fused_computation.6 | loop fusion | flops 393216 | bytes 393216 | tf_op jit(solution)/shard_map/concatenate | solution.py:326
  (8 shorter events, 0.2 us)
Async XLA Ops:
  0.0 4.3 %collective-permute-start = (bf16[2,32,1536]{2,1,0:T(8,128)(2,1)}, bf16[2,32,1536]{2,1,0:T(8,128)(2,1)S(1)}, u32[]{:S(2)}, u32[]{:S(2)}) collective-permute-start(bf16[2,32,1536]{2,1,0:T(8,128)(2,1)} %x_ref.1), channel_id=1, source_target_pairs={{0,1},{1,0},{2,3},{3,2},{4,5},{5,4},{6,7},{7,6},{8,9},{9,8},{10,11... | collective-permute-start | bytes 589832 | tf_op jit(solution)/shard_map/ppermute | solution.py:23
  0.5 3.8 %collective-permute-start.1 = (f32[4,3,1536]{2,0,1:T(4,128)}, f32[4,3,1536]{2,0,1:T(4,128)S(1)}, u32[]{:S(2)}, u32[]{:S(2)}) collective-permute-start(f32[4,3,1536]{2,0,1:T(4,128)} %param.11), channel_id=1, source_target_pairs={{0,1},{1,0},{2,3},{3,2},{4,5},{5,4},{6,7},{7,6},{8,9},{9,8},{10,11... | collective-permute-start | bytes 221192 | tf_op jit(solution)/shard_map/ppermute | solution.py:23
  4.3 6.1 %copy-start = (bf16[256,192]{0,1:T(8,128)(2,1)S(1)}, bf16[256,192]{0,1:T(8,128)(2,1)}, u32[]{:S(2)}) copy-start(bf16[256,192]{0,1:T(8,128)(2,1)} %param.10) | copy-start | bytes 294916
  5.1 8.7 %collective-permute-start.5 = (bf16[4,32,256]{2,1,0:T(8,128)(2,1)S(1)}, bf16[4,32,256]{2,1,0:T(8,128)(2,1)S(1)}, u32[]{:S(2)}, u32[]{:S(2)}) collective-permute-start(bf16[4,32,256]{2,1,0:T(8,128)(2,1)S(1)} %get-tuple-element.39), channel_id=1, source_target_pairs={{0,16},{2,18},{4,20},{6,22},{8,24},{10,26},{12,28},{14,30},{16,0},... | collective-permute-start | bytes 196616 | tf_op jit(solution)/shard_map/ppermute | solution.py:23
  10.4 7.5 %collective-permute-start.2 = (bf16[192,256]{1,0:T(8,128)(2,1)S(1)}, bf16[192,256]{1,0:T(8,128)(2,1)S(1)}, u32[]{:S(2)}, u32[]{:S(2)}) collective-permute-start(bf16[192,256]{1,0:T(8,128)(2,1)S(1)} %bitcast.27), channel_id=1, source_target_pairs={{0,16},{2,18},{4,20},{6,22},{8,24},{10,26},{12,28},{14,30},{16,0},... | collective-permute-start | bytes 294920 | tf_op jit(solution)/shard_map/ppermute | solution.py:23
  10.5 8.9 %collective-permute-start.10 = (bf16[192,256]{1,0:T(8,128)(2,1)S(1)}, bf16[192,256]{1,0:T(8,128)(2,1)S(1)}, u32[]{:S(2)}, u32[]{:S(2)}) collective-permute-start(bf16[192,256]{1,0:T(8,128)(2,1)S(1)} %bitcast.28), channel_id=1, source_target_pairs={{0,2},{2,0},{4,6},{6,4},{8,10},{10,8},{12,14},{14,12},{16,18},{18,... | collective-permute-start | bytes 294920 | tf_op jit(solution)/shard_map/ppermute | solution.py:23
  12.3 4.2 %collective-permute-start.3 = (bf16[2,32,256]{2,1,0:T(8,128)(2,1)S(1)}, bf16[2,32,256]{2,1,0:T(8,128)(2,1)S(1)}, u32[]{:S(2)}, u32[]{:S(2)}) collective-permute-start(bf16[2,32,256]{2,1,0:T(8,128)(2,1)S(1)} %get-tuple-element.35.q_ref), channel_id=1, source_target_pairs={{0,8},{2,10},{4,12},{6,14},{8,0},{10,2},{12,4},{14,6},{16,24},{18,... | collective-permute-start | bytes 98312 | tf_op jit(solution)/shard_map/ppermute | solution.py:23
  13.9 6.1 %collective-permute-start.6 = (bf16[2,4,32,256]{3,2,1,0:T(8,128)(2,1)S(1)}, bf16[2,4,32,256]{3,2,1,0:T(8,128)(2,1)S(1)}, u32[]{:S(2)}, u32[]{:S(2)}) collective-permute-start(bf16[2,4,32,256]{3,2,1,0:T(8,128)(2,1)S(1)} %pad_maximum_fusion.7.refs_0_), channel_id=1, source_target_pairs={{0,2},{2,0},{4,6},{6,4},{8,10},{10,8},{12,14},{14,12},{16,18},{18,... | collective-permute-start | bytes 393224 | tf_op jit(solution)/shard_map/ppermute | solution.py:23
  14.8 9.2 %collective-permute-start.7 = (bf16[2,4,32,256]{3,2,1,0:T(8,128)(2,1)S(1)}, bf16[2,4,32,256]{3,2,1,0:T(8,128)(2,1)S(1)}, u32[]{:S(2)}, u32[]{:S(2)}) collective-permute-start(bf16[2,4,32,256]{3,2,1,0:T(8,128)(2,1)S(1)} %pad_maximum_fusion.7.refs_0_), channel_id=1, source_target_pairs={{0,4},{2,6},{4,0},{6,2},{8,12},{10,14},{12,8},{14,10},{16,20},{18,... | collective-permute-start | bytes 393224 | tf_op jit(solution)/shard_map/ppermute | solution.py:23
  16.5 7.5 %collective-permute-start.8 = (bf16[2,4,32,256]{3,2,1,0:T(8,128)(2,1)S(1)}, bf16[2,4,32,256]{3,2,1,0:T(8,128)(2,1)S(1)}, u32[]{:S(2)}, u32[]{:S(2)}) collective-permute-start(bf16[2,4,32,256]{3,2,1,0:T(8,128)(2,1)S(1)} %pad_maximum_fusion.7.refs_0_), channel_id=1, source_target_pairs={{0,6},{2,4},{4,2},{6,0},{8,14},{10,12},{12,10},{14,8},{16,22},{18,... | collective-permute-start | bytes 393224 | tf_op jit(solution)/shard_map/ppermute | solution.py:23
  17.9 8.2 %collective-permute-start.4 = (bf16[1,192,256]{2,1,0:T(8,128)(2,1)S(1)}, bf16[1,192,256]{2,1,0:T(8,128)(2,1)S(1)}, u32[]{:S(2)}, u32[]{:S(2)}) collective-permute-start(bf16[1,192,256]{2,1,0:T(8,128)(2,1)S(1)} %bitcast.24), channel_id=1, source_target_pairs={{0,4},{2,6},{4,0},{6,2},{8,12},{10,14},{12,8},{14,10},{16,20},{18,... | collective-permute-start | bytes 294920 | tf_op jit(solution)/shard_map/ppermute | solution.py:23
  19.4 12.4 %collective-permute-start.11 = (bf16[2,192,256]{2,1,0:T(8,128)(2,1)S(1)}, bf16[2,192,256]{2,1,0:T(8,128)(2,1)S(1)}, u32[]{:S(2)}, u32[]{:S(2)}) collective-permute-start(bf16[2,192,256]{2,1,0:T(8,128)(2,1)S(1)} %get-tuple-element.52), channel_id=1, source_target_pairs={{0,4},{2,6},{4,0},{6,2},{8,12},{10,14},{12,8},{14,10},{16,20},{18,... | collective-permute-start | bytes 589832 | tf_op jit(solution)/shard_map/ppermute | solution.py:23
  26.1 5.7 %collective-permute-start.12 = (bf16[2,1,192,256]{3,2,1,0:T(8,128)(2,1)S(1)}, bf16[2,1,192,256]{3,2,1,0:T(8,128)(2,1)S(1)}, u32[]{:S(2)}, u32[]{:S(2)}) collective-permute-start(bf16[2,1,192,256]{3,2,1,0:T(8,128)(2,1)S(1)} %pad_maximum_fusion.2), channel_id=1, source_target_pairs={{0,2},{2,0},{4,6},{6,4},{8,10},{10,8},{12,14},{14,12},{16,18},{18,... | collective-permute-start | bytes 589832 | tf_op jit(solution)/shard_map/ppermute | solution.py:23
  26.7 4.9 %collective-permute-start.9 = (bf16[128,384]{1,0:T(8,128)(2,1)S(1)}, bf16[128,384]{1,0:T(8,128)(2,1)S(1)}, u32[]{:S(2)}, u32[]{:S(2)}) collective-permute-start(bf16[128,384]{1,0:T(8,128)(2,1)S(1)} %shard_map.76.part_ref), channel_id=1, source_target_pairs={{0,8},{2,10},{4,12},{6,14},{8,0},{10,2},{12,4},{14,6},{16,24},{18,... | collective-permute-start | bytes 294920 | tf_op jit(solution)/shard_map/ppermute | solution.py:23
  32.3 1.4 %collective-permute-start.13 = (bf16[64,768]{1,0:T(8,128)(2,1)S(1)}, bf16[64,768]{1,0:T(8,128)(2,1)S(1)}, u32[]{:S(2)}, u32[]{:S(2)}) collective-permute-start(bf16[64,768]{1,0:T(8,128)(2,1)S(1)} %shard_map.79), channel_id=1, source_target_pairs={{0,1},{1,0},{2,3},{3,2},{4,5},{5,4},{6,7},{7,6},{8,9},{9,8},{10,11... | collective-permute-start | bytes 294920 | tf_op jit(solution)/shard_map/ppermute | solution.py:23
  32.8 4.2 %collective-permute-start.15 = (bf16[64,768]{1,0:T(8,128)(2,1)S(1)}, bf16[64,768]{1,0:T(8,128)(2,1)S(1)}, u32[]{:S(2)}, u32[]{:S(2)}) collective-permute-start(bf16[64,768]{1,0:T(8,128)(2,1)S(1)} %shard_map.82), channel_id=1, source_target_pairs={{0,1},{1,0},{2,3},{3,2},{4,5},{5,4},{6,7},{7,6},{8,9},{9,8},{10,11... | collective-permute-start | bytes 294920 | tf_op jit(solution)/shard_map/ppermute | solution.py:23
  33.8 5.9 %collective-permute-start.14 = (bf16[2,32,768]{2,1,0:T(8,128)(2,1)S(1)}, bf16[2,32,768]{2,1,0:T(8,128)(2,1)S(1)}, u32[]{:S(2)}, u32[]{:S(2)}) collective-permute-start(bf16[2,32,768]{2,1,0:T(8,128)(2,1)S(1)} %shard_map.80), channel_id=1, source_target_pairs={{0,8},{2,10},{4,12},{6,14},{8,0},{10,2},{12,4},{14,6},{16,24},{18,... | collective-permute-start | bytes 294920 | tf_op jit(solution)/shard_map/ppermute | solution.py:23

commit v23 on v20

--- a/solution.py
+++ b/solution.py
@@ -263,7 +263,7 @@
     kv_pair = line_of(kv)
     q_mate = across(q, PLANE)
     w_x = across(w_own, 1)
-    w_late, q_mate = lax.optimization_barrier((w_own, q_mate))
+    w_late, kv_pair = lax.optimization_barrier((w_own, kv_pair))
     w_rest = jnp.stack(line_of(w_late)[1:])
     kv_plane = plane_of(jnp.stack(kv_pair))
     w_rest, q_mate = lax.optimization_barrier((w_rest, q_mate))

time: 40.4 us -> 41.8 us (1.035)
  starting transfers between devices: 18 us -> 22.1 us
  waiting for transfers between devices: 13.2 us -> 10.5 us
    ppermute x16, starting transfers between devices: 18 us -> 22.1 us  [swap(): return lax.ppermute(values, axis, [(i, i ^ bit) for i in range(count)])]
    ppermute x16, waiting for transfers between devices: 13.2 us -> 10.5 us  [swap(): return lax.ppermute(values, axis, [(i, i ^ bit) for i in range(count)])]
  transfers between devices with their start and end apart: 16 -> 16, of which waited for: 6 -> 5; matrix products, arithmetic and copies ran while one was open for 0% -> 0% of each run, Pallas kernels for 14% -> 14%
where the time goes in v23:
time: 41.8 us; the launch traced here: 41.7 us
  starting transfers between devices  22.1 us (53%)
  waiting for transfers between devices  10.5 us (25%)
  Pallas kernels  7.33 us (18%)
  other arithmetic  0.84 us (2%)
  between operations  0.82 us (2%)
    ppermute x16, starting transfers between devices, swap(): return lax.ppermute(values, axis, [(i, i ^ bit) for i in range(count)])  22.1 us
    ppermute x16, waiting for transfers between devices, swap(): return lax.ppermute(values, axis, [(i, i ^ bit) for i in range(count)])  10.5 us
    pallas_call x1, Pallas kernels, body(): call(load_kernel, tuple((pltpu.VMEM(v.shape, v.dtype) for v in first)) +...  3.21 us
    pallas_call x4, Pallas kernels, project(): call(functools.partial(project_kernel, n_head, n_patch, bit, mate), shape...  1.4 us
    pallas_call x1, Pallas kernels, body(): call(functools.partial(qkv_kernel, n_head), (kv_shape, shaped((4, rows, c...  1.16 us
    pallas_call x1, Pallas kernels, body(): call(attend_kernel, shaped((tall, cols + DH), BF16), [VMEM] * (3 + PLANE)...  1.11 us
  transfers between devices with their start and end apart: 16, of which 5 were waited for; matrix products, arithmetic and copies ran while one was open for 0% of the time, Pallas kernels for 14%

profile of v23, /device:TPU:0, one launch (start us, length us, event | category | flops | bytes accessed | tf_op | source)
XLA Modules:
  0.0 41.7 jit_solution(9167276574014246937)
XLA Ops:
  0.0 0.5 %collective-permute-start = (bf16[2,32,1536]{2,1,0:T(8,128)(2,1)}, bf16[2,32,1536]{2,1,0:T(8,128)(2,1)S(1)}, u32[]{:S(2)}, u32[]{:S(2)}) collective-permute-start(bf16[2,32,1536]{2,1,0:T(8,128)(2,1)} %x_ref.1), channel_id=1, source_target_pairs={{0,1},{1,0},{2,3},{3,2},{4,5},{5,4},{6,7},{7,6},{8,9},{9,8},{10,11... | collective-permute-start | bytes 589832 | tf_op jit(solution)/shard_map/ppermute | solution.py:23
  0.5 0.1 collective-permute-start.1
  1.2 0.0 copy-start
  1.2 3.2 %shard_map.73 = (bf16[3,3072,256]{2,1,0:T(8,128)(2,1)S(1)}, bf16[2,32,1536]{2,1,0:T(8,128)(2,1)S(1)}, f32[3,4,1536]{2,1,0:T(4,128)S(1)}, bf16[2,32,256]{2,1,0:T(...) custom-call(s32[2]{0:T(128)} %ids.1, s32[1]{0:T(128)S(6)} %copy.8.slab, ...), custom_call_target="tpu_custom_call" | custom-call | bytes 4718592 | tf_op jit(solution)/shard_map/pallas_call | solution.py:232
  4.4 0.0 collective-permute-done.1
  4.4 0.0 collective-permute-done.refs_1_
  4.4 1.2 %shard_map.74 = (bf16[2,32,256]{2,1,0:T(8,128)(2,1)S(1)}, bf16[4,32,256]{2,1,0:T(8,128)(2,1)S(1)}, bf16[2,32,256]{2,1,0:T(8,128)(2,1)S(1)}) custom-call(s32[1]{0:T(128)} %bitcast.3.head, s32[8,128]{1,0:T(8,128)S(1)} %get-tuple-element.27.ids_ref, bf16[2,32,1536]{2,1,0:T(8,128)(2,1)S(1)} %get-tuple-element.29.refs_0_, ...), custom_call_target="tpu_custom_call" | custom-call | flops 301989888 | bytes 4718592 | tf_op jit(solution)/shard_map/pallas_call | solution.py:254
  5.6 4.1 %collective-permute-start.2 = (bf16[4,32,256]{2,1,0:T(8,128)(2,1)S(1)}, bf16[4,32,256]{2,1,0:T(8,128)(2,1)S(1)}, u32[]{:S(2)}, u32[]{:S(2)}) collective-permute-start(bf16[4,32,256]{2,1,0:T(8,128)(2,1)S(1)} %get-tuple-element.42), channel_id=1, source_target_pairs={{0,16},{2,18},{4,20},{6,22},{8,24},{10,26},{12,28},{14,30},{16,0},... | collective-permute-start | bytes 196616 | tf_op jit(solution)/shard_map/ppermute | solution.py:23
  9.7 1.6 %collective-permute-start.4 = (bf16[2,32,256]{2,1,0:T(8,128)(2,1)S(1)}, bf16[2,32,256]{2,1,0:T(8,128)(2,1)S(1)}, u32[]{:S(2)}, u32[]{:S(2)}) collective-permute-start(bf16[2,32,256]{2,1,0:T(8,128)(2,1)S(1)} %get-tuple-element.38.q_ref), channel_id=1, source_target_pairs={{0,8},{2,10},{4,12},{6,14},{8,0},{10,2},{12,4},{14,6},{16,24},{18,... | collective-permute-start | bytes 98312 | tf_op jit(solution)/shard_map/ppermute | solution.py:23
  11.3 0.0 copy-done
  11.3 1.5 %collective-permute-start.10 = (bf16[192,256]{1,0:T(8,128)(2,1)S(1)}, bf16[192,256]{1,0:T(8,128)(2,1)S(1)}, u32[]{:S(2)}, u32[]{:S(2)}) collective-permute-start(bf16[192,256]{1,0:T(8,128)(2,1)S(1)} %bitcast.26), channel_id=1, source_target_pairs={{0,2},{2,0},{4,6},{6,4},{8,10},{10,8},{12,14},{14,12},{16,18},{18,... | collective-permute-start | bytes 294920 | tf_op jit(solution)/shard_map/ppermute | solution.py:23
  12.8 0.0 collective-permute-done.2
  12.8 2.4 %collective-permute-start.3 = (bf16[192,256]{1,0:T(8,128)(2,1)S(1)}, bf16[192,256]{1,0:T(8,128)(2,1)S(1)}, u32[]{:S(2)}, u32[]{:S(2)}) collective-permute-start(bf16[192,256]{1,0:T(8,128)(2,1)S(1)} %bitcast.27), channel_id=1, source_target_pairs={{0,16},{2,18},{4,20},{6,22},{8,24},{10,26},{12,28},{14,30},{16,0},... | collective-permute-start | bytes 294920 | tf_op jit(solution)/shard_map/ppermute | solution.py:23
  15.2 1.6 %collective-permute-start.6 = (bf16[2,4,32,256]{3,2,1,0:T(8,128)(2,1)S(1)}, bf16[2,4,32,256]{3,2,1,0:T(8,128)(2,1)S(1)}, u32[]{:S(2)}, u32[]{:S(2)}) collective-permute-start(bf16[2,4,32,256]{3,2,1,0:T(8,128)(2,1)S(1)} %pad_maximum_fusion.7.refs_0_), channel_id=1, source_target_pairs={{0,2},{2,0},{4,6},{6,4},{8,10},{10,8},{12,14},{14,12},{16,18},{18,... | collective-permute-start | bytes 393224 | tf_op jit(solution)/shard_map/ppermute | solution.py:23
  16.8 1.5 %collective-permute-start.7 = (bf16[2,4,32,256]{3,2,1,0:T(8,128)(2,1)S(1)}, bf16[2,4,32,256]{3,2,1,0:T(8,128)(2,1)S(1)}, u32[]{:S(2)}, u32[]{:S(2)}) collective-permute-start(bf16[2,4,32,256]{3,2,1,0:T(8,128)(2,1)S(1)} %pad_maximum_fusion.7.refs_0_), channel_id=1, source_target_pairs={{0,4},{2,6},{4,0},{6,2},{8,12},{10,14},{12,8},{14,10},{16,20},{18,... | collective-permute-start | bytes 393224 | tf_op jit(solution)/shard_map/ppermute | solution.py:23
  18.3 0.0 collective-permute-done.4.mate_ref
  18.3 0.5 %collective-permute-start.8 = (bf16[2,4,32,256]{3,2,1,0:T(8,128)(2,1)S(1)}, bf16[2,4,32,256]{3,2,1,0:T(8,128)(2,1)S(1)}, u32[]{:S(2)}, u32[]{:S(2)}) collective-permute-start(bf16[2,4,32,256]{3,2,1,0:T(8,128)(2,1)S(1)} %pad_maximum_fusion.7.refs_0_), channel_id=1, source_target_pairs={{0,6},{2,4},{4,2},{6,0},{8,14},{10,12},{12,10},{14,8},{16,22},{18,... | collective-permute-start | bytes 393224 | tf_op jit(solution)/shard_map/ppermute | solution.py:23
  18.8 1.6 %collective-permute-done.3 = bf16[192,256]{1,0:T(8,128)(2,1)S(1)} collective-permute-done((bf16[192,256]{1,0:T(8,128)(2,1)S(1)}, bf16[192,256]{1,0:T(8,128)(2,1)S(1)}, u32[]{:S(2)}, u32[]{:S(2)}) %collective-permute-start.3) | collective-permute-done | bytes 98336 | tf_op jit(solution)/shard_map/ppermute | solution.py:23
  20.4 1.9 %collective-permute-start.5 = (bf16[1,192,256]{2,1,0:T(8,128)(2,1)S(1)}, bf16[1,192,256]{2,1,0:T(8,128)(2,1)S(1)}, u32[]{:S(2)}, u32[]{:S(2)}) collective-permute-start(bf16[1,192,256]{2,1,0:T(8,128)(2,1)S(1)} %bitcast.23), channel_id=1, source_target_pairs={{0,4},{2,6},{4,0},{6,2},{8,12},{10,14},{12,8},{14,10},{16,20},{18,... | collective-permute-start | bytes 294920 | tf_op jit(solution)/shard_map/ppermute | solution.py:23
  22.3 0.0 collective-permute-done.10
  22.3 0.2 collective-permute-start.11
  22.5 0.0 collective-permute-done.6.refs_1_
  22.5 2.9 %collective-permute-done.7.refs_2_ = bf16[2,4,32,256]{3,2,1,0:T(8,128)(2,1)S(1)} collective-permute-done((bf16[2,4,32,256]{3,2,1,0:T(8,128)(2,1)S(1)}, bf16[2,4,32,256]{3,2,1,0:T(8,128)(2,1)S(1)}, u32[]{:S(2)}, u32[]{:S(2)}) %collective-permute-start.7) | collective-permute-done | bytes 131104 | tf_op jit(solution)/shard_map/ppermute | solution.py:23
  25.5 0.0 collective-permute-done.8.refs_3_
  25.5 1.1 %shard_map.75.part_ref = bf16[128,384]{1,0:T(8,128)(2,1)S(1)} custom-call(bf16[2,32,256]{2,1,0:T(8,128)(2,1)S(1)} %get-tuple-element.38.q_ref, bf16[2,32,256]{2,1,0:T(8,128)(2,1)S(1)} %collective-permute-done.4.mate_ref, bf16[2,32,256]{2,1,0:T(8,128)(2,1)S(1)} %get-tuple-element.41.kv1_ref, bf16[2,4,32,256]{3,2,1,0:T(8,128)(2,1)S(1)} %pad_maximum_fusion.7.refs_0_, ...), custom_call_target="tpu_custom_call" | custom-call | flops 33554432 | tf_op jit(solution)/shard_map/pallas_call | solution.py:273
  26.6 0.7 %collective-permute-done.5 = bf16[1,192,256]{2,1,0:T(8,128)(2,1)S(1)} collective-permute-done((bf16[1,192,256]{2,1,0:T(8,128)(2,1)S(1)}, bf16[1,192,256]{2,1,0:T(8,128)(2,1)S(1)}, u32[]{:S(2)}, u32[]{:S(2)}) %collective-permute-start.5) | collective-permute-done | bytes 98336 | tf_op jit(solution)/shard_map/ppermute | solution.py:23
  27.3 0.7 %collective-permute-start.12 = (bf16[2,1,192,256]{3,2,1,0:T(8,128)(2,1)S(1)}, bf16[2,1,192,256]{3,2,1,0:T(8,128)(2,1)S(1)}, u32[]{:S(2)}, u32[]{:S(2)}) collective-permute-start(bf16[2,1,192,256]{3,2,1,0:T(8,128)(2,1)S(1)} %pad_maximum_fusion.2), channel_id=1, source_target_pairs={{0,2},{2,0},{4,6},{6,4},{8,10},{10,8},{12,14},{14,12},{16,18},{18,... | collective-permute-start | bytes 589832 | tf_op jit(solution)/shard_map/ppermute | solution.py:23
  28.1 2.2 %collective-permute-start.9 = (bf16[128,384]{1,0:T(8,128)(2,1)S(1)}, bf16[128,384]{1,0:T(8,128)(2,1)S(1)}, u32[]{:S(2)}, u32[]{:S(2)}) collective-permute-start(bf16[128,384]{1,0:T(8,128)(2,1)S(1)} %shard_map.75.part_ref), channel_id=1, source_target_pairs={{0,8},{2,10},{4,12},{6,14},{8,0},{10,2},{12,4},{14,6},{16,24},{18,... | collective-permute-start | bytes 294920 | tf_op jit(solution)/shard_map/ppermute | solution.py:23
  30.2 2.6 %collective-permute-done.9.other_ref = bf16[128,384]{1,0:T(8,128)(2,1)S(1)} collective-permute-done((bf16[128,384]{1,0:T(8,128)(2,1)S(1)}, bf16[128,384]{1,0:T(8,128)(2,1)S(1)}, u32[]{:S(2)}, u32[]{:S(2)}) %collective-permute-start.9) | collective-permute-done | bytes 98336 | tf_op jit(solution)/shard_map/ppermute | solution.py:23
  32.8 0.2 shard_map.76.o_ref
  33.1 0.0 collective-permute-done.11
  33.1 0.0 collective-permute-done.12
  33.2 0.4 shard_map.78
  33.6 0.1 collective-permute-start.13
  33.6 0.4 shard_map.81
  34.0 0.6 %collective-permute-start.15 = (bf16[64,768]{1,0:T(8,128)(2,1)S(1)}, bf16[64,768]{1,0:T(8,128)(2,1)S(1)}, u32[]{:S(2)}, u32[]{:S(2)}) collective-permute-start(bf16[64,768]{1,0:T(8,128)(2,1)S(1)} %shard_map.81), channel_id=1, source_target_pairs={{0,1},{1,0},{2,3},{3,2},{4,5},{5,4},{6,7},{7,6},{8,9},{9,8},{10,11... | collective-permute-start | bytes 294920 | tf_op jit(solution)/shard_map/ppermute | solution.py:23
  34.5 0.4 shard_map.77.refs_0_
  34.9 0.0 collective-permute-done.13.refs_1_
  34.9 0.1 shard_map.79
  35.0 2.8 %collective-permute-start.14 = (bf16[2,32,768]{2,1,0:T(8,128)(2,1)S(1)}, bf16[2,32,768]{2,1,0:T(8,128)(2,1)S(1)}, u32[]{:S(2)}, u32[]{:S(2)}) collective-permute-start(bf16[2,32,768]{2,1,0:T(8,128)(2,1)S(1)} %shard_map.79), channel_id=1, source_target_pairs={{0,8},{2,10},{4,12},{6,14},{8,0},{10,2},{12,4},{14,6},{16,24},{18,... | collective-permute-start | bytes 294920 | tf_op jit(solution)/shard_map/ppermute | solution.py:23
  37.9 0.4 shard_map.80.refs_0_
  38.2 0.0 collective-permute-done.15.refs_1_
  38.2 0.1 shard_map.82
  38.3 2.6 %collective-permute-done.14 = bf16[2,32,768]{2,1,0:T(8,128)(2,1)S(1)} collective-permute-done((bf16[2,32,768]{2,1,0:T(8,128)(2,1)S(1)}, bf16[2,32,768]{2,1,0:T(8,128)(2,1)S(1)}, u32[]{:S(2)}, u32[]{:S(2)}) %collective-permute-start.14) | collective-permute-done | bytes 98336 | tf_op jit(solution)/shard_map/ppermute | solution.py:23
  41.0 0.7 %pad_maximum_fusion.6 = bf16[2,32,1536]{2,1,0:T(8,128)(2,1)} fusion(bf16[2,32,768]{2,1,0:T(8,128)(2,1)S(1)} %get-tuple-element.50, bf16[2,32,768]{2,1,0:T(8,128)(2,1)S(1)} %get-tuple-element.49), kind=kLoop, calls=%fused_computation.6 | loop fusion | flops 393216 | bytes 393216 | tf_op jit(solution)/shard_map/concatenate | solution.py:310
  (8 shorter events, 0.2 us)
Async XLA Ops:
  0.0 4.4 %collective-permute-start = (bf16[2,32,1536]{2,1,0:T(8,128)(2,1)}, bf16[2,32,1536]{2,1,0:T(8,128)(2,1)S(1)}, u32[]{:S(2)}, u32[]{:S(2)}) collective-permute-start(bf16[2,32,1536]{2,1,0:T(8,128)(2,1)} %x_ref.1), channel_id=1, source_target_pairs={{0,1},{1,0},{2,3},{3,2},{4,5},{5,4},{6,7},{7,6},{8,9},{9,8},{10,11... | collective-permute-start | bytes 589832 | tf_op jit(solution)/shard_map/ppermute | solution.py:23
  0.5 3.9 %collective-permute-start.1 = (f32[4,3,1536]{2,0,1:T(4,128)}, f32[4,3,1536]{2,0,1:T(4,128)S(1)}, u32[]{:S(2)}, u32[]{:S(2)}) collective-permute-start(f32[4,3,1536]{2,0,1:T(4,128)} %param.11), channel_id=1, source_target_pairs={{0,1},{1,0},{2,3},{3,2},{4,5},{5,4},{6,7},{7,6},{8,9},{9,8},{10,11... | collective-permute-start | bytes 221192 | tf_op jit(solution)/shard_map/ppermute | solution.py:23
  1.2 10.1 %copy-start = (bf16[256,192]{0,1:T(8,128)(2,1)S(1)}, bf16[256,192]{0,1:T(8,128)(2,1)}, u32[]{:S(2)}) copy-start(bf16[256,192]{0,1:T(8,128)(2,1)} %param.10) | copy-start | bytes 294916
  5.6 7.2 %collective-permute-start.2 = (bf16[4,32,256]{2,1,0:T(8,128)(2,1)S(1)}, bf16[4,32,256]{2,1,0:T(8,128)(2,1)S(1)}, u32[]{:S(2)}, u32[]{:S(2)}) collective-permute-start(bf16[4,32,256]{2,1,0:T(8,128)(2,1)S(1)} %get-tuple-element.42), channel_id=1, source_target_pairs={{0,16},{2,18},{4,20},{6,22},{8,24},{10,26},{12,28},{14,30},{16,0},... | collective-permute-start | bytes 196616 | tf_op jit(solution)/shard_map/ppermute | solution.py:23
  9.7 8.6 %collective-permute-start.4 = (bf16[2,32,256]{2,1,0:T(8,128)(2,1)S(1)}, bf16[2,32,256]{2,1,0:T(8,128)(2,1)S(1)}, u32[]{:S(2)}, u32[]{:S(2)}) collective-permute-start(bf16[2,32,256]{2,1,0:T(8,128)(2,1)S(1)} %get-tuple-element.38.q_ref), channel_id=1, source_target_pairs={{0,8},{2,10},{4,12},{6,14},{8,0},{10,2},{12,4},{14,6},{16,24},{18,... | collective-permute-start | bytes 98312 | tf_op jit(solution)/shard_map/ppermute | solution.py:23
  11.3 11.0 %collective-permute-start.10 = (bf16[192,256]{1,0:T(8,128)(2,1)S(1)}, bf16[192,256]{1,0:T(8,128)(2,1)S(1)}, u32[]{:S(2)}, u32[]{:S(2)}) collective-permute-start(bf16[192,256]{1,0:T(8,128)(2,1)S(1)} %bitcast.26), channel_id=1, source_target_pairs={{0,2},{2,0},{4,6},{6,4},{8,10},{10,8},{12,14},{14,12},{16,18},{18,... | collective-permute-start | bytes 294920 | tf_op jit(solution)/shard_map/ppermute | solution.py:23
  12.8 7.6 %collective-permute-start.3 = (bf16[192,256]{1,0:T(8,128)(2,1)S(1)}, bf16[192,256]{1,0:T(8,128)(2,1)S(1)}, u32[]{:S(2)}, u32[]{:S(2)}) collective-permute-start(bf16[192,256]{1,0:T(8,128)(2,1)S(1)} %bitcast.27), channel_id=1, source_target_pairs={{0,16},{2,18},{4,20},{6,22},{8,24},{10,26},{12,28},{14,30},{16,0},... | collective-permute-start | bytes 294920 | tf_op jit(solution)/shard_map/ppermute | solution.py:23
  15.2 7.3 %collective-permute-start.6 = (bf16[2,4,32,256]{3,2,1,0:T(8,128)(2,1)S(1)}, bf16[2,4,32,256]{3,2,1,0:T(8,128)(2,1)S(1)}, u32[]{:S(2)}, u32[]{:S(2)}) collective-permute-start(bf16[2,4,32,256]{3,2,1,0:T(8,128)(2,1)S(1)} %pad_maximum_fusion.7.refs_0_), channel_id=1, source_target_pairs={{0,2},{2,0},{4,6},{6,4},{8,10},{10,8},{12,14},{14,12},{16,18},{18,... | collective-permute-start | bytes 393224 | tf_op jit(solution)/shard_map/ppermute | solution.py:23
  16.8 8.7 %collective-permute-start.7 = (bf16[2,4,32,256]{3,2,1,0:T(8,128)(2,1)S(1)}, bf16[2,4,32,256]{3,2,1,0:T(8,128)(2,1)S(1)}, u32[]{:S(2)}, u32[]{:S(2)}) collective-permute-start(bf16[2,4,32,256]{3,2,1,0:T(8,128)(2,1)S(1)} %pad_maximum_fusion.7.refs_0_), channel_id=1, source_target_pairs={{0,4},{2,6},{4,0},{6,2},{8,12},{10,14},{12,8},{14,10},{16,20},{18,... | collective-permute-start | bytes 393224 | tf_op jit(solution)/shard_map/ppermute | solution.py:23
  18.3 7.2 %collective-permute-start.8 = (bf16[2,4,32,256]{3,2,1,0:T(8,128)(2,1)S(1)}, bf16[2,4,32,256]{3,2,1,0:T(8,128)(2,1)S(1)}, u32[]{:S(2)}, u32[]{:S(2)}) collective-permute-start(bf16[2,4,32,256]{3,2,1,0:T(8,128)(2,1)S(1)} %pad_maximum_fusion.7.refs_0_), channel_id=1, source_target_pairs={{0,6},{2,4},{4,2},{6,0},{8,14},{10,12},{12,10},{14,8},{16,22},{18,... | collective-permute-start | bytes 393224 | tf_op jit(solution)/shard_map/ppermute | solution.py:23
  20.4 6.9 %collective-permute-start.5 = (bf16[1,192,256]{2,1,0:T(8,128)(2,1)S(1)}, bf16[1,192,256]{2,1,0:T(8,128)(2,1)S(1)}, u32[]{:S(2)}, u32[]{:S(2)}) collective-permute-start(bf16[1,192,256]{2,1,0:T(8,128)(2,1)S(1)} %bitcast.23), channel_id=1, source_target_pairs={{0,4},{2,6},{4,0},{6,2},{8,12},{10,14},{12,8},{14,10},{16,20},{18,... | collective-permute-start | bytes 294920 | tf_op jit(solution)/shard_map/ppermute | solution.py:23
  22.3 10.8 %collective-permute-start.11 = (bf16[2,192,256]{2,1,0:T(8,128)(2,1)S(1)}, bf16[2,192,256]{2,1,0:T(8,128)(2,1)S(1)}, u32[]{:S(2)}, u32[]{:S(2)}) collective-permute-start(bf16[2,192,256]{2,1,0:T(8,128)(2,1)S(1)} %get-tuple-element.56), channel_id=1, source_target_pairs={{0,4},{2,6},{4,0},{6,2},{8,12},{10,14},{12,8},{14,10},{16,20},{18,... | collective-permute-start | bytes 589832 | tf_op jit(solution)/shard_map/ppermute | solution.py:23
  27.3 5.7 %collective-permute-start.12 = (bf16[2,1,192,256]{3,2,1,0:T(8,128)(2,1)S(1)}, bf16[2,1,192,256]{3,2,1,0:T(8,128)(2,1)S(1)}, u32[]{:S(2)}, u32[]{:S(2)}) collective-permute-start(bf16[2,1,192,256]{3,2,1,0:T(8,128)(2,1)S(1)} %pad_maximum_fusion.2), channel_id=1, source_target_pairs={{0,2},{2,0},{4,6},{6,4},{8,10},{10,8},{12,14},{14,12},{16,18},{18,... | collective-permute-start | bytes 589832 | tf_op jit(solution)/shard_map/ppermute | solution.py:23
  28.1 4.8 %collective-permute-start.9 = (bf16[128,384]{1,0:T(8,128)(2,1)S(1)}, bf16[128,384]{1,0:T(8,128)(2,1)S(1)}, u32[]{:S(2)}, u32[]{:S(2)}) collective-permute-start(bf16[128,384]{1,0:T(8,128)(2,1)S(1)} %shard_map.75.part_ref), channel_id=1, source_target_pairs={{0,8},{2,10},{4,12},{6,14},{8,0},{10,2},{12,4},{14,6},{16,24},{18,... | collective-permute-start | bytes 294920 | tf_op jit(solution)/shard_map/ppermute | solution.py:23
  33.6 1.4 %collective-permute-start.13 = (bf16[64,768]{1,0:T(8,128)(2,1)S(1)}, bf16[64,768]{1,0:T(8,128)(2,1)S(1)}, u32[]{:S(2)}, u32[]{:S(2)}) collective-permute-start(bf16[64,768]{1,0:T(8,128)(2,1)S(1)} %shard_map.78), channel_id=1, source_target_pairs={{0,1},{1,0},{2,3},{3,2},{4,5},{5,4},{6,7},{7,6},{8,9},{9,8},{10,11... | collective-permute-start | bytes 294920 | tf_op jit(solution)/shard_map/ppermute | solution.py:23
  34.0 4.2 %collective-permute-start.15 = (bf16[64,768]{1,0:T(8,128)(2,1)S(1)}, bf16[64,768]{1,0:T(8,128)(2,1)S(1)}, u32[]{:S(2)}, u32[]{:S(2)}) collective-permute-start(bf16[64,768]{1,0:T(8,128)(2,1)S(1)} %shard_map.81), channel_id=1, source_target_pairs={{0,1},{1,0},{2,3},{3,2},{4,5},{5,4},{6,7},{7,6},{8,9},{9,8},{10,11... | collective-permute-start | bytes 294920 | tf_op jit(solution)/shard_map/ppermute | solution.py:23
  35.0 5.9 %collective-permute-start.14 = (bf16[2,32,768]{2,1,0:T(8,128)(2,1)S(1)}, bf16[2,32,768]{2,1,0:T(8,128)(2,1)S(1)}, u32[]{:S(2)}, u32[]{:S(2)}) collective-permute-start(bf16[2,32,768]{2,1,0:T(8,128)(2,1)S(1)} %shard_map.79), channel_id=1, source_target_pairs={{0,8},{2,10},{4,12},{6,14},{8,0},{10,2},{12,4},{14,6},{16,24},{18,... | collective-permute-start | bytes 294920 | tf_op jit(solution)/shard_map/ppermute | solution.py:23

commit v24 on v22

--- a/solution.py
+++ b/solution.py
@@ -280,7 +280,8 @@
     kv_pair = line_of(kv)
     q_mate = across(q, PLANE)
     w_x = across(w_own, 1)
-    w_rest = jnp.stack(line_of(w_own)[1:])
+    w_late, q_mate = lax.optimization_barrier((w_own, q_mate))
+    w_rest = jnp.stack(line_of(w_late)[1:])
     kv_plane = plane_of(jnp.stack(kv_pair))
     w_rest, q_mate = lax.optimization_barrier((w_rest, q_mate))
     w_y = across(jnp.stack([w_own, w_x]), 2)

time: 40.6 us -> 41 us (level)
  waiting for transfers between devices: 10.6 us -> 11.6 us
  starting transfers between devices: 20.2 us -> 19.5 us
    ppermute x16, waiting for transfers between devices: 10.6 us -> 11.6 us  [swap(): return lax.ppermute(values, axis, [(i, i ^ bit) for i in range(count)])]
    ppermute x16, starting transfers between devices: 20.2 us -> 19.5 us  [swap(): return lax.ppermute(values, axis, [(i, i ^ bit) for i in range(count)])]
where the time goes in v24:
time: 41 us; the launch traced here: 40.8 us
  starting transfers between devices  19.5 us (48%)
  waiting for transfers between devices  11.6 us (28%)
  Pallas kernels  7.99 us (19%)
  between operations  0.85 us (2%)
  other arithmetic  0.84 us (2%)
    ppermute x16, starting transfers between devices, swap(): return lax.ppermute(values, axis, [(i, i ^ bit) for i in range(count)])  19.5 us
    ppermute x16, waiting for transfers between devices, swap(): return lax.ppermute(values, axis, [(i, i ^ bit) for i in range(count)])  11.6 us
    pallas_call x1, Pallas kernels, body(): call(load_kernel, tuple((pltpu.VMEM(v.shape, v.dtype) for v in first)) +...  3.08 us
    pallas_call x4, Pallas kernels, project(): call(functools.partial(project_kernel, n_head, n_patch, bit, mate), shape...  1.41 us
    pallas_call x1, Pallas kernels, body(): call(attend_kernel, shaped((tall, cols + DH), BF16), [VMEM] * (3 + PLANE)...  1.11 us
    pallas_call x1, Pallas kernels, body(): call(functools.partial(rest_kernel, n_head), (kv_shape, kv_shape), specs,...  1.11 us
    pallas_call x1, Pallas kernels, body(): call(functools.partial(fresh_kernel, n_head), (shaped((n_head, rows, feat...  0.85 us
  transfers between devices with their start and end apart: 16, of which 6 were waited for; matrix products, arithmetic and copies ran while one was open for 0% of the time, Pallas kernels for 17%

profile of v24, /device:TPU:0, one launch (start us, length us, event | category | flops | bytes accessed | tf_op | source)
XLA Modules:
  0.0 40.8 jit_solution(16047139204481536677)
XLA Ops:
  0.0 0.5 %collective-permute-start = (bf16[2,32,1536]{2,1,0:T(8,128)(2,1)}, bf16[2,32,1536]{2,1,0:T(8,128)(2,1)S(1)}, u32[]{:S(2)}, u32[]{:S(2)}) collective-permute-start(bf16[2,32,1536]{2,1,0:T(8,128)(2,1)} %x_ref.1), channel_id=1, source_target_pairs={{0,1},{1,0},{2,3},{3,2},{4,5},{5,4},{6,7},{7,6},{8,9},{9,8},{10,11... | collective-permute-start | bytes 589832 | tf_op jit(solution)/shard_map/ppermute | solution.py:23
  0.5 0.1 collective-permute-start.1
  1.2 3.1 %shard_map.73 = (bf16[3,3072,256]{2,1,0:T(8,128)(2,1)S(1)}, bf16[2,32,1536]{2,1,0:T(8,128)(2,1)S(1)}, f32[3,4,1536]{2,1,0:T(4,128)S(1)}, bf16[2,32,256]{2,1,0:T(...) custom-call(s32[2]{0:T(128)} %ids.1, s32[1]{0:T(128)S(6)} %copy.8.slab, ...), custom_call_target="tpu_custom_call" | custom-call | bytes 4718592 | tf_op jit(solution)/shard_map/pallas_call | solution.py:240
  4.3 0.0 collective-permute-done.1
  4.3 0.0 collective-permute-done.refs_1_
  4.3 0.0 copy-start
  4.3 0.8 %shard_map.74 = (bf16[2,32,1536]{2,1,0:T(8,128)(2,1)S(1)}, bf16[4,32,256]{2,1,0:T(8,128)(2,1)S(1)}) custom-call(s32[1]{0:T(128)} %bitcast.3.head, s32[8,128]{1,0:T(8,128)S(1)} %get-tuple-element.27.ids_ref, bf16[2,32,1536]{2,1,0:T(8,128)(2,1)S(1)} %get-tuple-element.29.refs_0_, bf16[2,32,1536]{2,1,0:T(8,128)(2,1)S(1)} %collective-permute-done.refs_1_, ...), custom_call_target="tpu_custom_call" | custom-call | flops 100663296 | bytes 4718592 | tf_op jit(solution)/shard_map/pallas_call | solution.py:264
  5.1 4.1 %collective-permute-start.5 = (bf16[4,32,256]{2,1,0:T(8,128)(2,1)S(1)}, bf16[4,32,256]{2,1,0:T(8,128)(2,1)S(1)}, u32[]{:S(2)}, u32[]{:S(2)}) collective-permute-start(bf16[4,32,256]{2,1,0:T(8,128)(2,1)S(1)} %get-tuple-element.43), channel_id=1, source_target_pairs={{0,16},{2,18},{4,20},{6,22},{8,24},{10,26},{12,28},{14,30},{16,0},... | collective-permute-start | bytes 196616 | tf_op jit(solution)/shard_map/ppermute | solution.py:23
  9.2 1.1 %shard_map.75 = (bf16[2,32,256]{2,1,0:T(8,128)(2,1)S(1)}, bf16[2,32,256]{2,1,0:T(8,128)(2,1)S(1)}) custom-call(s32[1]{0:T(128)} %bitcast.3.head, s32[8,128]{1,0:T(8,128)S(1)} %get-tuple-element.27.ids_ref, bf16[2,32,1536]{2,1,0:T(8,128)(2,1)S(1)} %get-tuple-element.29.refs_0_, bf16[2,32,1536]{2,1,0:T(8,128)(2,1)S(1)} %collective-permute-done.refs_1_, ...), custom_call_target="tpu_custom_call" | custom-call | flops 201326592 | bytes 4718592 | tf_op jit(solution)/shard_map/pallas_call | solution.py:271
  10.4 1.6 %collective-permute-start.2 = (bf16[2,32,256]{2,1,0:T(8,128)(2,1)S(1)}, bf16[2,32,256]{2,1,0:T(8,128)(2,1)S(1)}, u32[]{:S(2)}, u32[]{:S(2)}) collective-permute-start(bf16[2,32,256]{2,1,0:T(8,128)(2,1)S(1)} %get-tuple-element.37.q_ref), channel_id=1, source_target_pairs={{0,8},{2,10},{4,12},{6,14},{8,0},{10,2},{12,4},{14,6},{16,24},{18,... | collective-permute-start | bytes 98312 | tf_op jit(solution)/shard_map/ppermute | solution.py:23
  12.0 0.0 copy-done
  12.0 1.5 %collective-permute-start.10 = (bf16[192,256]{1,0:T(8,128)(2,1)S(1)}, bf16[192,256]{1,0:T(8,128)(2,1)S(1)}, u32[]{:S(2)}, u32[]{:S(2)}) collective-permute-start(bf16[192,256]{1,0:T(8,128)(2,1)S(1)} %bitcast.27), channel_id=1, source_target_pairs={{0,2},{2,0},{4,6},{6,4},{8,10},{10,8},{12,14},{14,12},{16,18},{18,... | collective-permute-start | bytes 294920 | tf_op jit(solution)/shard_map/ppermute | solution.py:23
  13.5 0.8 %collective-permute-done.2.mate_ref = bf16[2,32,256]{2,1,0:T(8,128)(2,1)S(1)} collective-permute-done((bf16[2,32,256]{2,1,0:T(8,128)(2,1)S(1)}, bf16[2,32,256]{2,1,0:T(8,128)(2,1)S(1)}, u32[]{:S(2)}, u32[]{:S(2)}) %collective-permute-start.2) | collective-permute-done | bytes 32800 | tf_op jit(solution)/shard_map/ppermute | solution.py:23
  14.3 0.6 %collective-permute-start.3 = (bf16[192,256]{1,0:T(8,128)(2,1)S(1)}, bf16[192,256]{1,0:T(8,128)(2,1)S(1)}, u32[]{:S(2)}, u32[]{:S(2)}) collective-permute-start(bf16[192,256]{1,0:T(8,128)(2,1)S(1)} %bitcast.28), channel_id=1, source_target_pairs={{0,16},{2,18},{4,20},{6,22},{8,24},{10,26},{12,28},{14,30},{16,0},... | collective-permute-start | bytes 294920 | tf_op jit(solution)/shard_map/ppermute | solution.py:23
  14.9 0.0 collective-permute-done.5
  14.9 1.6 %collective-permute-start.6 = (bf16[2,4,32,256]{3,2,1,0:T(8,128)(2,1)S(1)}, bf16[2,4,32,256]{3,2,1,0:T(8,128)(2,1)S(1)}, u32[]{:S(2)}, u32[]{:S(2)}) collective-permute-start(bf16[2,4,32,256]{3,2,1,0:T(8,128)(2,1)S(1)} %pad_maximum_fusion.7.refs_0_), channel_id=1, source_target_pairs={{0,2},{2,0},{4,6},{6,4},{8,10},{10,8},{12,14},{14,12},{16,18},{18,... | collective-permute-start | bytes 393224 | tf_op jit(solution)/shard_map/ppermute | solution.py:23
  16.5 1.5 %collective-permute-start.7 = (bf16[2,4,32,256]{3,2,1,0:T(8,128)(2,1)S(1)}, bf16[2,4,32,256]{3,2,1,0:T(8,128)(2,1)S(1)}, u32[]{:S(2)}, u32[]{:S(2)}) collective-permute-start(bf16[2,4,32,256]{3,2,1,0:T(8,128)(2,1)S(1)} %pad_maximum_fusion.7.refs_0_), channel_id=1, source_target_pairs={{0,4},{2,6},{4,0},{6,2},{8,12},{10,14},{12,8},{14,10},{16,20},{18,... | collective-permute-start | bytes 393224 | tf_op jit(solution)/shard_map/ppermute | solution.py:23
  18.0 0.5 %collective-permute-start.8 = (bf16[2,4,32,256]{3,2,1,0:T(8,128)(2,1)S(1)}, bf16[2,4,32,256]{3,2,1,0:T(8,128)(2,1)S(1)}, u32[]{:S(2)}, u32[]{:S(2)}) collective-permute-start(bf16[2,4,32,256]{3,2,1,0:T(8,128)(2,1)S(1)} %pad_maximum_fusion.7.refs_0_), channel_id=1, source_target_pairs={{0,6},{2,4},{4,2},{6,0},{8,14},{10,12},{12,10},{14,8},{16,22},{18,... | collective-permute-start | bytes 393224 | tf_op jit(solution)/shard_map/ppermute | solution.py:23
  18.5 1.4 %collective-permute-done.3 = bf16[192,256]{1,0:T(8,128)(2,1)S(1)} collective-permute-done((bf16[192,256]{1,0:T(8,128)(2,1)S(1)}, bf16[192,256]{1,0:T(8,128)(2,1)S(1)}, u32[]{:S(2)}, u32[]{:S(2)}) %collective-permute-start.3) | collective-permute-done | bytes 98336 | tf_op jit(solution)/shard_map/ppermute | solution.py:23
  19.9 2.7 %collective-permute-start.4 = (bf16[1,192,256]{2,1,0:T(8,128)(2,1)S(1)}, bf16[1,192,256]{2,1,0:T(8,128)(2,1)S(1)}, u32[]{:S(2)}, u32[]{:S(2)}) collective-permute-start(bf16[1,192,256]{2,1,0:T(8,128)(2,1)S(1)} %bitcast.24), channel_id=1, source_target_pairs={{0,4},{2,6},{4,0},{6,2},{8,12},{10,14},{12,8},{14,10},{16,20},{18,... | collective-permute-start | bytes 294920 | tf_op jit(solution)/shard_map/ppermute | solution.py:23
  22.6 0.0 collective-permute-done.10
  22.6 0.1 collective-permute-start.11
  22.7 0.0 collective-permute-done.6.refs_1_
  22.7 1.8 %collective-permute-done.7.refs_2_ = bf16[2,4,32,256]{3,2,1,0:T(8,128)(2,1)S(1)} collective-permute-done((bf16[2,4,32,256]{3,2,1,0:T(8,128)(2,1)S(1)}, bf16[2,4,32,256]{3,2,1,0:T(8,128)(2,1)S(1)}, u32[]{:S(2)}, u32[]{:S(2)}) %collective-permute-start.7) | collective-permute-done | bytes 131104 | tf_op jit(solution)/shard_map/ppermute | solution.py:23
  24.5 0.0 collective-permute-done.8.refs_3_
  24.5 1.1 %shard_map.76.part_ref = bf16[128,384]{1,0:T(8,128)(2,1)S(1)} custom-call(bf16[2,32,256]{2,1,0:T(8,128)(2,1)S(1)} %get-tuple-element.37.q_ref, bf16[2,32,256]{2,1,0:T(8,128)(2,1)S(1)} %collective-permute-done.2.mate_ref, bf16[2,32,256]{2,1,0:T(8,128)(2,1)S(1)} %get-tuple-element.42.kv1_ref, bf16[2,4,32,256]{3,2,1,0:T(8,128)(2,1)S(1)} %pad_maximum_fusion.7.refs_0_, ...), custom_call_target="tpu_custom_call" | custom-call | flops 33554432 | tf_op jit(solution)/shard_map/pallas_call | solution.py:290
  25.6 1.0 %collective-permute-done.4 = bf16[1,192,256]{2,1,0:T(8,128)(2,1)S(1)} collective-permute-done((bf16[1,192,256]{2,1,0:T(8,128)(2,1)S(1)}, bf16[1,192,256]{2,1,0:T(8,128)(2,1)S(1)}, u32[]{:S(2)}, u32[]{:S(2)}) %collective-permute-start.4) | collective-permute-done | bytes 98336 | tf_op jit(solution)/shard_map/ppermute | solution.py:23
  26.6 1.7 %collective-permute-start.12 = (bf16[2,1,192,256]{3,2,1,0:T(8,128)(2,1)S(1)}, bf16[2,1,192,256]{3,2,1,0:T(8,128)(2,1)S(1)}, u32[]{:S(2)}, u32[]{:S(2)}) collective-permute-start(bf16[2,1,192,256]{3,2,1,0:T(8,128)(2,1)S(1)} %pad_maximum_fusion.2), channel_id=1, source_target_pairs={{0,2},{2,0},{4,6},{6,4},{8,10},{10,8},{12,14},{14,12},{16,18},{18,... | collective-permute-start | bytes 589832 | tf_op jit(solution)/shard_map/ppermute | solution.py:23
  28.4 1.1 %collective-permute-start.9 = (bf16[128,384]{1,0:T(8,128)(2,1)S(1)}, bf16[128,384]{1,0:T(8,128)(2,1)S(1)}, u32[]{:S(2)}, u32[]{:S(2)}) collective-permute-start(bf16[128,384]{1,0:T(8,128)(2,1)S(1)} %shard_map.76.part_ref), channel_id=1, source_target_pairs={{0,8},{2,10},{4,12},{6,14},{8,0},{10,2},{12,4},{14,6},{16,24},{18,... | collective-permute-start | bytes 294920 | tf_op jit(solution)/shard_map/ppermute | solution.py:23
  29.4 3.5 %collective-permute-done.9.other_ref = bf16[128,384]{1,0:T(8,128)(2,1)S(1)} collective-permute-done((bf16[128,384]{1,0:T(8,128)(2,1)S(1)}, bf16[128,384]{1,0:T(8,128)(2,1)S(1)}, u32[]{:S(2)}, u32[]{:S(2)}) %collective-permute-start.9) | collective-permute-done | bytes 98336 | tf_op jit(solution)/shard_map/ppermute | solution.py:23
  33.0 0.2 shard_map.77.o_ref
  33.2 0.0 collective-permute-done.11
  33.2 0.0 collective-permute-done.12
  33.3 0.4 shard_map.79
  33.7 0.1 collective-permute-start.13
  33.8 0.4 shard_map.82
  34.1 0.6 %collective-permute-start.15 = (bf16[64,768]{1,0:T(8,128)(2,1)S(1)}, bf16[64,768]{1,0:T(8,128)(2,1)S(1)}, u32[]{:S(2)}, u32[]{:S(2)}) collective-permute-start(bf16[64,768]{1,0:T(8,128)(2,1)S(1)} %shard_map.82), channel_id=1, source_target_pairs={{0,1},{1,0},{2,3},{3,2},{4,5},{5,4},{6,7},{7,6},{8,9},{9,8},{10,11... | collective-permute-start | bytes 294920 | tf_op jit(solution)/shard_map/ppermute | solution.py:23
  34.7 0.4 shard_map.78.refs_0_
  35.1 0.0 collective-permute-done.13.refs_1_
  35.1 0.1 shard_map.80
  35.2 1.4 %collective-permute-start.14 = (bf16[2,32,768]{2,1,0:T(8,128)(2,1)S(1)}, bf16[2,32,768]{2,1,0:T(8,128)(2,1)S(1)}, u32[]{:S(2)}, u32[]{:S(2)}) collective-permute-start(bf16[2,32,768]{2,1,0:T(8,128)(2,1)S(1)} %shard_map.80), channel_id=1, source_target_pairs={{0,8},{2,10},{4,12},{6,14},{8,0},{10,2},{12,4},{14,6},{16,24},{18,... | collective-permute-start | bytes 294920 | tf_op jit(solution)/shard_map/ppermute | solution.py:23
  36.6 0.4 shard_map.81.refs_0_
  37.0 0.0 collective-permute-done.15.refs_1_
  37.0 0.1 shard_map.83
  37.1 3.0 %collective-permute-done.14 = bf16[2,32,768]{2,1,0:T(8,128)(2,1)S(1)} collective-permute-done((bf16[2,32,768]{2,1,0:T(8,128)(2,1)S(1)}, bf16[2,32,768]{2,1,0:T(8,128)(2,1)S(1)}, u32[]{:S(2)}, u32[]{:S(2)}) %collective-permute-start.14) | collective-permute-done | bytes 98336 | tf_op jit(solution)/shard_map/ppermute | solution.py:23
  40.1 0.7 %pad_maximum_fusion.6 = bf16[2,32,1536]{2,1,0:T(8,128)(2,1)} fusion(bf16[2,32,768]{2,1,0:T(8,128)(2,1)S(1)} %get-tuple-element.50, bf16[2,32,768]{2,1,0:T(8,128)(2,1)S(1)} %get-tuple-element.49), kind=kLoop, calls=%fused_computation.6 | loop fusion | flops 393216 | bytes 393216 | tf_op jit(solution)/shard_map/concatenate | solution.py:327
  (8 shorter events, 0.2 us)
Async XLA Ops:
  0.0 4.3 %collective-permute-start = (bf16[2,32,1536]{2,1,0:T(8,128)(2,1)}, bf16[2,32,1536]{2,1,0:T(8,128)(2,1)S(1)}, u32[]{:S(2)}, u32[]{:S(2)}) collective-permute-start(bf16[2,32,1536]{2,1,0:T(8,128)(2,1)} %x_ref.1), channel_id=1, source_target_pairs={{0,1},{1,0},{2,3},{3,2},{4,5},{5,4},{6,7},{7,6},{8,9},{9,8},{10,11... | collective-permute-start | bytes 589832 | tf_op jit(solution)/shard_map/ppermute | solution.py:23
  0.5 3.8 %collective-permute-start.1 = (f32[4,3,1536]{2,0,1:T(4,128)}, f32[4,3,1536]{2,0,1:T(4,128)S(1)}, u32[]{:S(2)}, u32[]{:S(2)}) collective-permute-start(f32[4,3,1536]{2,0,1:T(4,128)} %param.11), channel_id=1, source_target_pairs={{0,1},{1,0},{2,3},{3,2},{4,5},{5,4},{6,7},{7,6},{8,9},{9,8},{10,11... | collective-permute-start | bytes 221192 | tf_op jit(solution)/shard_map/ppermute | solution.py:23
  4.3 7.7 %copy-start = (bf16[256,192]{0,1:T(8,128)(2,1)S(1)}, bf16[256,192]{0,1:T(8,128)(2,1)}, u32[]{:S(2)}) copy-start(bf16[256,192]{0,1:T(8,128)(2,1)} %param.10) | copy-start | bytes 294916
  5.1 9.8 %collective-permute-start.5 = (bf16[4,32,256]{2,1,0:T(8,128)(2,1)S(1)}, bf16[4,32,256]{2,1,0:T(8,128)(2,1)S(1)}, u32[]{:S(2)}, u32[]{:S(2)}) collective-permute-start(bf16[4,32,256]{2,1,0:T(8,128)(2,1)S(1)} %get-tuple-element.43), channel_id=1, source_target_pairs={{0,16},{2,18},{4,20},{6,22},{8,24},{10,26},{12,28},{14,30},{16,0},... | collective-permute-start | bytes 196616 | tf_op jit(solution)/shard_map/ppermute | solution.py:23
  10.4 4.0 %collective-permute-start.2 = (bf16[2,32,256]{2,1,0:T(8,128)(2,1)S(1)}, bf16[2,32,256]{2,1,0:T(8,128)(2,1)S(1)}, u32[]{:S(2)}, u32[]{:S(2)}) collective-permute-start(bf16[2,32,256]{2,1,0:T(8,128)(2,1)S(1)} %get-tuple-element.37.q_ref), channel_id=1, source_target_pairs={{0,8},{2,10},{4,12},{6,14},{8,0},{10,2},{12,4},{14,6},{16,24},{18,... | collective-permute-start | bytes 98312 | tf_op jit(solution)/shard_map/ppermute | solution.py:23
  12.0 10.6 %collective-permute-start.10 = (bf16[192,256]{1,0:T(8,128)(2,1)S(1)}, bf16[192,256]{1,0:T(8,128)(2,1)S(1)}, u32[]{:S(2)}, u32[]{:S(2)}) collective-permute-start(bf16[192,256]{1,0:T(8,128)(2,1)S(1)} %bitcast.27), channel_id=1, source_target_pairs={{0,2},{2,0},{4,6},{6,4},{8,10},{10,8},{12,14},{14,12},{16,18},{18,... | collective-permute-start | bytes 294920 | tf_op jit(solution)/shard_map/ppermute | solution.py:23
  14.3 5.5 %collective-permute-start.3 = (bf16[192,256]{1,0:T(8,128)(2,1)S(1)}, bf16[192,256]{1,0:T(8,128)(2,1)S(1)}, u32[]{:S(2)}, u32[]{:S(2)}) collective-permute-start(bf16[192,256]{1,0:T(8,128)(2,1)S(1)} %bitcast.28), channel_id=1, source_target_pairs={{0,16},{2,18},{4,20},{6,22},{8,24},{10,26},{12,28},{14,30},{16,0},... | collective-permute-start | bytes 294920 | tf_op jit(solution)/shard_map/ppermute | solution.py:23
  14.9 7.8 %collective-permute-start.6 = (bf16[2,4,32,256]{3,2,1,0:T(8,128)(2,1)S(1)}, bf16[2,4,32,256]{3,2,1,0:T(8,128)(2,1)S(1)}, u32[]{:S(2)}, u32[]{:S(2)}) collective-permute-start(bf16[2,4,32,256]{3,2,1,0:T(8,128)(2,1)S(1)} %pad_maximum_fusion.7.refs_0_), channel_id=1, source_target_pairs={{0,2},{2,0},{4,6},{6,4},{8,10},{10,8},{12,14},{14,12},{16,18},{18,... | collective-permute-start | bytes 393224 | tf_op jit(solution)/shard_map/ppermute | solution.py:23
  16.5 8.0 %collective-permute-start.7 = (bf16[2,4,32,256]{3,2,1,0:T(8,128)(2,1)S(1)}, bf16[2,4,32,256]{3,2,1,0:T(8,128)(2,1)S(1)}, u32[]{:S(2)}, u32[]{:S(2)}) collective-permute-start(bf16[2,4,32,256]{3,2,1,0:T(8,128)(2,1)S(1)} %pad_maximum_fusion.7.refs_0_), channel_id=1, source_target_pairs={{0,4},{2,6},{4,0},{6,2},{8,12},{10,14},{12,8},{14,10},{16,20},{18,... | collective-permute-start | bytes 393224 | tf_op jit(solution)/shard_map/ppermute | solution.py:23
  18.0 6.5 %collective-permute-start.8 = (bf16[2,4,32,256]{3,2,1,0:T(8,128)(2,1)S(1)}, bf16[2,4,32,256]{3,2,1,0:T(8,128)(2,1)S(1)}, u32[]{:S(2)}, u32[]{:S(2)}) collective-permute-start(bf16[2,4,32,256]{3,2,1,0:T(8,128)(2,1)S(1)} %pad_maximum_fusion.7.refs_0_), channel_id=1, source_target_pairs={{0,6},{2,4},{4,2},{6,0},{8,14},{10,12},{12,10},{14,8},{16,22},{18,... | collective-permute-start | bytes 393224 | tf_op jit(solution)/shard_map/ppermute | solution.py:23
  19.9 6.7 %collective-permute-start.4 = (bf16[1,192,256]{2,1,0:T(8,128)(2,1)S(1)}, bf16[1,192,256]{2,1,0:T(8,128)(2,1)S(1)}, u32[]{:S(2)}, u32[]{:S(2)}) collective-permute-start(bf16[1,192,256]{2,1,0:T(8,128)(2,1)S(1)} %bitcast.24), channel_id=1, source_target_pairs={{0,4},{2,6},{4,0},{6,2},{8,12},{10,14},{12,8},{14,10},{16,20},{18,... | collective-permute-start | bytes 294920 | tf_op jit(solution)/shard_map/ppermute | solution.py:23
  22.6 10.6 %collective-permute-start.11 = (bf16[2,192,256]{2,1,0:T(8,128)(2,1)S(1)}, bf16[2,192,256]{2,1,0:T(8,128)(2,1)S(1)}, u32[]{:S(2)}, u32[]{:S(2)}) collective-permute-start(bf16[2,192,256]{2,1,0:T(8,128)(2,1)S(1)} %get-tuple-element.56), channel_id=1, source_target_pairs={{0,4},{2,6},{4,0},{6,2},{8,12},{10,14},{12,8},{14,10},{16,20},{18,... | collective-permute-start | bytes 589832 | tf_op jit(solution)/shard_map/ppermute | solution.py:23
  26.6 6.6 %collective-permute-start.12 = (bf16[2,1,192,256]{3,2,1,0:T(8,128)(2,1)S(1)}, bf16[2,1,192,256]{3,2,1,0:T(8,128)(2,1)S(1)}, u32[]{:S(2)}, u32[]{:S(2)}) collective-permute-start(bf16[2,1,192,256]{3,2,1,0:T(8,128)(2,1)S(1)} %pad_maximum_fusion.2), channel_id=1, source_target_pairs={{0,2},{2,0},{4,6},{6,4},{8,10},{10,8},{12,14},{14,12},{16,18},{18,... | collective-permute-start | bytes 589832 | tf_op jit(solution)/shard_map/ppermute | solution.py:23
  28.4 4.6 %collective-permute-start.9 = (bf16[128,384]{1,0:T(8,128)(2,1)S(1)}, bf16[128,384]{1,0:T(8,128)(2,1)S(1)}, u32[]{:S(2)}, u32[]{:S(2)}) collective-permute-start(bf16[128,384]{1,0:T(8,128)(2,1)S(1)} %shard_map.76.part_ref), channel_id=1, source_target_pairs={{0,8},{2,10},{4,12},{6,14},{8,0},{10,2},{12,4},{14,6},{16,24},{18,... | collective-permute-start | bytes 294920 | tf_op jit(solution)/shard_map/ppermute | solution.py:23
  33.7 1.4 %collective-permute-start.13 = (bf16[64,768]{1,0:T(8,128)(2,1)S(1)}, bf16[64,768]{1,0:T(8,128)(2,1)S(1)}, u32[]{:S(2)}, u32[]{:S(2)}) collective-permute-start(bf16[64,768]{1,0:T(8,128)(2,1)S(1)} %shard_map.79), channel_id=1, source_target_pairs={{0,1},{1,0},{2,3},{3,2},{4,5},{5,4},{6,7},{7,6},{8,9},{9,8},{10,11... | collective-permute-start | bytes 294920 | tf_op jit(solution)/shard_map/ppermute | solution.py:23
  34.1 2.8 %collective-permute-start.15 = (bf16[64,768]{1,0:T(8,128)(2,1)S(1)}, bf16[64,768]{1,0:T(8,128)(2,1)S(1)}, u32[]{:S(2)}, u32[]{:S(2)}) collective-permute-start(bf16[64,768]{1,0:T(8,128)(2,1)S(1)} %shard_map.82), channel_id=1, source_target_pairs={{0,1},{1,0},{2,3},{3,2},{4,5},{5,4},{6,7},{7,6},{8,9},{9,8},{10,11... | collective-permute-start | bytes 294920 | tf_op jit(solution)/shard_map/ppermute | solution.py:23
  35.2 4.9 %collective-permute-start.14 = (bf16[2,32,768]{2,1,0:T(8,128)(2,1)S(1)}, bf16[2,32,768]{2,1,0:T(8,128)(2,1)S(1)}, u32[]{:S(2)}, u32[]{:S(2)}) collective-permute-start(bf16[2,32,768]{2,1,0:T(8,128)(2,1)S(1)} %shard_map.80), channel_id=1, source_target_pairs={{0,8},{2,10},{4,12},{6,14},{8,0},{10,2},{12,4},{14,6},{16,24},{18,... | collective-permute-start | bytes 294920 | tf_op jit(solution)/shard_map/ppermute | solution.py:23

commit v25 on v20

--- a/solution.py
+++ b/solution.py
@@ -262,13 +262,13 @@
     w_own, kv = lax.optimization_barrier((w_out.T, kv))
     kv_pair = line_of(kv)
     q_mate = across(q, PLANE)
-    w_x = across(w_own, 1)
+    w_x = across(w_own, 2)
     w_late, q_mate = lax.optimization_barrier((w_own, q_mate))
     w_rest = jnp.stack(line_of(w_late)[1:])
     kv_plane = plane_of(jnp.stack(kv_pair))
     w_rest, q_mate = lax.optimization_barrier((w_rest, q_mate))
-    w_y = across(jnp.stack([w_own, w_x]), 2)
-    rest_y = across(w_rest, 2)
+    w_y = across(jnp.stack([w_own, w_x]), 1)
+    rest_y = across(w_rest, 1)
     tall = 2 * STEPS * rows
     part = call(
         attend_kernel,
@@ -277,10 +277,10 @@
         flops=4 * STEPS * rows * n_patch * rows * cols,
     )(q, q_mate, kv1, *kv_plane)
     rest_y, part = lax.optimization_barrier((rest_y, part))
-    rest_x = across(jnp.stack([w_rest, rest_y]), 1)
+    rest_x = across(jnp.stack([w_rest, rest_y]), 2)
     o = call(merge_kernel, shaped((tall, cols), BF16), [VMEM] * 2)(part, across(part, PLANE))
     o, w_y, rest_x = lax.optimization_barrier((o, w_y, rest_x))
-    near = [(w_own, w_rest), (w_x, rest_x[0]), (w_y[0], rest_y), (w_y[1], rest_x[1])]
+    near = [(w_own, w_rest), (w_y[0], rest_y), (w_x, rest_x[0]), (w_y[1], rest_x[1])]
     w_plane = [jnp.concatenate([first[None], others]) for first, others in near]
     wide = PLANE * piece
 

time: 40.4 us -> 40.4 us (level)
  starting transfers between devices: 18 us -> 19.7 us
  waiting for transfers between devices: 13.2 us -> 11.6 us
    ppermute x16, starting transfers between devices: 18 us -> 19.7 us  [swap(): return lax.ppermute(values, axis, [(i, i ^ bit) for i in range(count)])]
    ppermute x16, waiting for transfers between devices: 13.2 us -> 11.6 us  [swap(): return lax.ppermute(values, axis, [(i, i ^ bit) for i in range(count)])]
  transfers between devices with their start and end apart: 16 -> 16, of which waited for: 6 -> 5; matrix products, arithmetic and copies ran while one was open for 0% -> 0% of each run, Pallas kernels for 14% -> 14%
where the time goes in v25:
time: 40.4 us; the launch traced here: 40.3 us
  starting transfers between devices  19.7 us (49%)
  waiting for transfers between devices  11.6 us (29%)
  Pallas kernels  7.32 us (18%)
  other arithmetic  0.85 us (2%)
  between operations  0.84 us (2%)
    ppermute x16, starting transfers between devices, swap(): return lax.ppermute(values, axis, [(i, i ^ bit) for i in range(count)])  19.7 us
    ppermute x16, waiting for transfers between devices, swap(): return lax.ppermute(values, axis, [(i, i ^ bit) for i in range(count)])  11.6 us
    pallas_call x1, Pallas kernels, body(): call(load_kernel, tuple((pltpu.VMEM(v.shape, v.dtype) for v in first)) +...  3.21 us
    pallas_call x4, Pallas kernels, project(): call(functools.partial(project_kernel, n_head, n_patch, bit, mate), shape...  1.4 us
    pallas_call x1, Pallas kernels, body(): call(functools.partial(qkv_kernel, n_head), (kv_shape, shaped((4, rows, c...  1.16 us
    pallas_call x1, Pallas kernels, body(): call(attend_kernel, shaped((tall, cols + DH), BF16), [VMEM] * (3 + PLANE)...  1.11 us
  transfers between devices with their start and end apart: 16, of which 5 were waited for; matrix products, arithmetic and copies ran while one was open for 0% of the time, Pallas kernels for 14%

profile of v25, /device:TPU:0, one launch (start us, length us, event | category | flops | bytes accessed | tf_op | source)
XLA Modules:
  0.0 40.3 jit_solution(6209656467027755813)
XLA Ops:
  0.0 0.5 %collective-permute-start = (bf16[2,32,1536]{2,1,0:T(8,128)(2,1)}, bf16[2,32,1536]{2,1,0:T(8,128)(2,1)S(1)}, u32[]{:S(2)}, u32[]{:S(2)}) collective-permute-start(bf16[2,32,1536]{2,1,0:T(8,128)(2,1)} %x_ref.1), channel_id=1, source_target_pairs={{0,1},{1,0},{2,3},{3,2},{4,5},{5,4},{6,7},{7,6},{8,9},{9,8},{10,11... | collective-permute-start | bytes 589832 | tf_op jit(solution)/shard_map/ppermute | solution.py:23
  0.5 0.1 collective-permute-start.1
  1.2 0.0 copy-start
  1.2 3.2 %shard_map.73 = (bf16[3,3072,256]{2,1,0:T(8,128)(2,1)S(1)}, bf16[2,32,1536]{2,1,0:T(8,128)(2,1)S(1)}, f32[3,4,1536]{2,1,0:T(4,128)S(1)}, bf16[2,32,256]{2,1,0:T(...) custom-call(s32[2]{0:T(128)} %ids.1, s32[1]{0:T(128)S(6)} %copy.8.slab, ...), custom_call_target="tpu_custom_call" | custom-call | bytes 4718592 | tf_op jit(solution)/shard_map/pallas_call | solution.py:232
  4.4 0.0 collective-permute-done.1
  4.4 0.0 collective-permute-done.refs_1_
  4.4 1.2 %shard_map.74 = (bf16[2,32,256]{2,1,0:T(8,128)(2,1)S(1)}, bf16[4,32,256]{2,1,0:T(8,128)(2,1)S(1)}, bf16[2,32,256]{2,1,0:T(8,128)(2,1)S(1)}) custom-call(s32[1]{0:T(128)} %bitcast.3.head, s32[8,128]{1,0:T(8,128)S(1)} %get-tuple-element.26.ids_ref, bf16[2,32,1536]{2,1,0:T(8,128)(2,1)S(1)} %get-tuple-element.28.refs_0_, ...), custom_call_target="tpu_custom_call" | custom-call | flops 301989888 | bytes 4718592 | tf_op jit(solution)/shard_map/pallas_call | solution.py:254
  5.6 4.1 %collective-permute-start.5 = (bf16[4,32,256]{2,1,0:T(8,128)(2,1)S(1)}, bf16[4,32,256]{2,1,0:T(8,128)(2,1)S(1)}, u32[]{:S(2)}, u32[]{:S(2)}) collective-permute-start(bf16[4,32,256]{2,1,0:T(8,128)(2,1)S(1)} %get-tuple-element.41), channel_id=1, source_target_pairs={{0,16},{2,18},{4,20},{6,22},{8,24},{10,26},{12,28},{14,30},{16,0},... | collective-permute-start | bytes 196616 | tf_op jit(solution)/shard_map/ppermute | solution.py:23
  9.7 1.6 %collective-permute-start.2 = (bf16[2,32,256]{2,1,0:T(8,128)(2,1)S(1)}, bf16[2,32,256]{2,1,0:T(8,128)(2,1)S(1)}, u32[]{:S(2)}, u32[]{:S(2)}) collective-permute-start(bf16[2,32,256]{2,1,0:T(8,128)(2,1)S(1)} %get-tuple-element.35.q_ref), channel_id=1, source_target_pairs={{0,8},{2,10},{4,12},{6,14},{8,0},{10,2},{12,4},{14,6},{16,24},{18,... | collective-permute-start | bytes 98312 | tf_op jit(solution)/shard_map/ppermute | solution.py:23
  11.3 0.0 copy-done
  11.3 1.5 %collective-permute-start.10 = (bf16[192,256]{1,0:T(8,128)(2,1)S(1)}, bf16[192,256]{1,0:T(8,128)(2,1)S(1)}, u32[]{:S(2)}, u32[]{:S(2)}) collective-permute-start(bf16[192,256]{1,0:T(8,128)(2,1)S(1)} %bitcast.26), channel_id=1, source_target_pairs={{0,4},{2,6},{4,0},{6,2},{8,12},{10,14},{12,8},{14,10},{16,20},{18,... | collective-permute-start | bytes 294920 | tf_op jit(solution)/shard_map/ppermute | solution.py:23
  12.8 0.8 %collective-permute-done.2.mate_ref = bf16[2,32,256]{2,1,0:T(8,128)(2,1)S(1)} collective-permute-done((bf16[2,32,256]{2,1,0:T(8,128)(2,1)S(1)}, bf16[2,32,256]{2,1,0:T(8,128)(2,1)S(1)}, u32[]{:S(2)}, u32[]{:S(2)}) %collective-permute-start.2) | collective-permute-done | bytes 32800 | tf_op jit(solution)/shard_map/ppermute | solution.py:23
  13.6 0.7 %collective-permute-start.3 = (bf16[192,256]{1,0:T(8,128)(2,1)S(1)}, bf16[192,256]{1,0:T(8,128)(2,1)S(1)}, u32[]{:S(2)}, u32[]{:S(2)}) collective-permute-start(bf16[192,256]{1,0:T(8,128)(2,1)S(1)} %bitcast.27), channel_id=1, source_target_pairs={{0,16},{2,18},{4,20},{6,22},{8,24},{10,26},{12,28},{14,30},{16,0},... | collective-permute-start | bytes 294920 | tf_op jit(solution)/shard_map/ppermute | solution.py:23
  14.3 0.0 collective-permute-done.5
  14.3 1.6 %collective-permute-start.6 = (bf16[2,4,32,256]{3,2,1,0:T(8,128)(2,1)S(1)}, bf16[2,4,32,256]{3,2,1,0:T(8,128)(2,1)S(1)}, u32[]{:S(2)}, u32[]{:S(2)}) collective-permute-start(bf16[2,4,32,256]{3,2,1,0:T(8,128)(2,1)S(1)} %pad_maximum_fusion.7.refs_0_), channel_id=1, source_target_pairs={{0,2},{2,0},{4,6},{6,4},{8,10},{10,8},{12,14},{14,12},{16,18},{18,... | collective-permute-start | bytes 393224 | tf_op jit(solution)/shard_map/ppermute | solution.py:23
  15.9 1.5 %collective-permute-start.7 = (bf16[2,4,32,256]{3,2,1,0:T(8,128)(2,1)S(1)}, bf16[2,4,32,256]{3,2,1,0:T(8,128)(2,1)S(1)}, u32[]{:S(2)}, u32[]{:S(2)}) collective-permute-start(bf16[2,4,32,256]{3,2,1,0:T(8,128)(2,1)S(1)} %pad_maximum_fusion.7.refs_0_), channel_id=1, source_target_pairs={{0,4},{2,6},{4,0},{6,2},{8,12},{10,14},{12,8},{14,10},{16,20},{18,... | collective-permute-start | bytes 393224 | tf_op jit(solution)/shard_map/ppermute | solution.py:23
  17.4 0.5 %collective-permute-start.8 = (bf16[2,4,32,256]{3,2,1,0:T(8,128)(2,1)S(1)}, bf16[2,4,32,256]{3,2,1,0:T(8,128)(2,1)S(1)}, u32[]{:S(2)}, u32[]{:S(2)}) collective-permute-start(bf16[2,4,32,256]{3,2,1,0:T(8,128)(2,1)S(1)} %pad_maximum_fusion.7.refs_0_), channel_id=1, source_target_pairs={{0,6},{2,4},{4,2},{6,0},{8,14},{10,12},{12,10},{14,8},{16,22},{18,... | collective-permute-start | bytes 393224 | tf_op jit(solution)/shard_map/ppermute | solution.py:23
  17.9 1.3 %collective-permute-done.3 = bf16[192,256]{1,0:T(8,128)(2,1)S(1)} collective-permute-done((bf16[192,256]{1,0:T(8,128)(2,1)S(1)}, bf16[192,256]{1,0:T(8,128)(2,1)S(1)}, u32[]{:S(2)}, u32[]{:S(2)}) %collective-permute-start.3) | collective-permute-done | bytes 98336 | tf_op jit(solution)/shard_map/ppermute | solution.py:23
  19.1 2.8 %collective-permute-start.4 = (bf16[1,192,256]{2,1,0:T(8,128)(2,1)S(1)}, bf16[1,192,256]{2,1,0:T(8,128)(2,1)S(1)}, u32[]{:S(2)}, u32[]{:S(2)}) collective-permute-start(bf16[1,192,256]{2,1,0:T(8,128)(2,1)S(1)} %bitcast.23), channel_id=1, source_target_pairs={{0,2},{2,0},{4,6},{6,4},{8,10},{10,8},{12,14},{14,12},{16,18},{18,... | collective-permute-start | bytes 294920 | tf_op jit(solution)/shard_map/ppermute | solution.py:23
  22.0 0.0 collective-permute-done.10
  22.0 0.1 collective-permute-start.11
  22.1 0.0 collective-permute-done.6.refs_1_
  22.1 0.0 collective-permute-done.7.refs_2_
  22.1 2.6 %collective-permute-done.8.refs_3_ = bf16[2,4,32,256]{3,2,1,0:T(8,128)(2,1)S(1)} collective-permute-done((bf16[2,4,32,256]{3,2,1,0:T(8,128)(2,1)S(1)}, bf16[2,4,32,256]{3,2,1,0:T(8,128)(2,1)S(1)}, u32[]{:S(2)}, u32[]{:S(2)}) %collective-permute-start.8) | collective-permute-done | bytes 131104 | tf_op jit(solution)/shard_map/ppermute | solution.py:23
  24.7 1.1 %shard_map.75.part_ref = bf16[128,384]{1,0:T(8,128)(2,1)S(1)} custom-call(bf16[2,32,256]{2,1,0:T(8,128)(2,1)S(1)} %get-tuple-element.35.q_ref, bf16[2,32,256]{2,1,0:T(8,128)(2,1)S(1)} %collective-permute-done.2.mate_ref, bf16[2,32,256]{2,1,0:T(8,128)(2,1)S(1)} %get-tuple-element.40.kv1_ref, bf16[2,4,32,256]{3,2,1,0:T(8,128)(2,1)S(1)} %pad_maximum_fusion.7.refs_0_, ...), custom_call_target="tpu_custom_call" | custom-call | flops 33554432 | tf_op jit(solution)/shard_map/pallas_call | solution.py:273
  25.8 0.0 collective-permute-done.4
  25.9 1.9 %collective-permute-start.12 = (bf16[2,1,192,256]{3,2,1,0:T(8,128)(2,1)S(1)}, bf16[2,1,192,256]{3,2,1,0:T(8,128)(2,1)S(1)}, u32[]{:S(2)}, u32[]{:S(2)}) collective-permute-start(bf16[2,1,192,256]{3,2,1,0:T(8,128)(2,1)S(1)} %pad_maximum_fusion.2), channel_id=1, source_target_pairs={{0,4},{2,6},{4,0},{6,2},{8,12},{10,14},{12,8},{14,10},{16,20},{18,... | collective-permute-start | bytes 589832 | tf_op jit(solution)/shard_map/ppermute | solution.py:23
  27.8 1.1 %collective-permute-start.9 = (bf16[128,384]{1,0:T(8,128)(2,1)S(1)}, bf16[128,384]{1,0:T(8,128)(2,1)S(1)}, u32[]{:S(2)}, u32[]{:S(2)}) collective-permute-start(bf16[128,384]{1,0:T(8,128)(2,1)S(1)} %shard_map.75.part_ref), channel_id=1, source_target_pairs={{0,8},{2,10},{4,12},{6,14},{8,0},{10,2},{12,4},{14,6},{16,24},{18,... | collective-permute-start | bytes 294920 | tf_op jit(solution)/shard_map/ppermute | solution.py:23
  28.9 3.5 %collective-permute-done.9.other_ref = bf16[128,384]{1,0:T(8,128)(2,1)S(1)} collective-permute-done((bf16[128,384]{1,0:T(8,128)(2,1)S(1)}, bf16[128,384]{1,0:T(8,128)(2,1)S(1)}, u32[]{:S(2)}, u32[]{:S(2)}) %collective-permute-start.9) | collective-permute-done | bytes 98336 | tf_op jit(solution)/shard_map/ppermute | solution.py:23
  32.4 0.2 shard_map.76.o_ref
  32.7 0.0 collective-permute-done.11
  32.7 0.0 collective-permute-done.12
  32.8 0.3 shard_map.78
  33.2 0.1 collective-permute-start.13
  33.2 0.4 shard_map.81
  33.6 0.6 %collective-permute-start.15 = (bf16[64,768]{1,0:T(8,128)(2,1)S(1)}, bf16[64,768]{1,0:T(8,128)(2,1)S(1)}, u32[]{:S(2)}, u32[]{:S(2)}) collective-permute-start(bf16[64,768]{1,0:T(8,128)(2,1)S(1)} %shard_map.81), channel_id=1, source_target_pairs={{0,1},{1,0},{2,3},{3,2},{4,5},{5,4},{6,7},{7,6},{8,9},{9,8},{10,11... | collective-permute-start | bytes 294920 | tf_op jit(solution)/shard_map/ppermute | solution.py:23
  34.1 0.4 shard_map.77.refs_0_
  34.5 0.0 collective-permute-done.13.refs_1_
  34.5 0.1 shard_map.79
  34.6 1.2 %collective-permute-start.14 = (bf16[2,32,768]{2,1,0:T(8,128)(2,1)S(1)}, bf16[2,32,768]{2,1,0:T(8,128)(2,1)S(1)}, u32[]{:S(2)}, u32[]{:S(2)}) collective-permute-start(bf16[2,32,768]{2,1,0:T(8,128)(2,1)S(1)} %shard_map.79), channel_id=1, source_target_pairs={{0,8},{2,10},{4,12},{6,14},{8,0},{10,2},{12,4},{14,6},{16,24},{18,... | collective-permute-start | bytes 294920 | tf_op jit(solution)/shard_map/ppermute | solution.py:23
  35.8 0.3 shard_map.80.refs_0_
  36.2 0.0 collective-permute-done.15.refs_1_
  36.2 0.1 shard_map.82
  36.3 3.3 %collective-permute-done.14 = bf16[2,32,768]{2,1,0:T(8,128)(2,1)S(1)} collective-permute-done((bf16[2,32,768]{2,1,0:T(8,128)(2,1)S(1)}, bf16[2,32,768]{2,1,0:T(8,128)(2,1)S(1)}, u32[]{:S(2)}, u32[]{:S(2)}) %collective-permute-start.14) | collective-permute-done | bytes 98336 | tf_op jit(solution)/shard_map/ppermute | solution.py:23
  39.6 0.7 %pad_maximum_fusion.6 = bf16[2,32,1536]{2,1,0:T(8,128)(2,1)} fusion(bf16[2,32,768]{2,1,0:T(8,128)(2,1)S(1)} %get-tuple-element.48, bf16[2,32,768]{2,1,0:T(8,128)(2,1)S(1)} %get-tuple-element.47), kind=kLoop, calls=%fused_computation.6 | loop fusion | flops 393216 | bytes 393216 | tf_op jit(solution)/shard_map/concatenate | solution.py:310
  (8 shorter events, 0.2 us)
Async XLA Ops:
  0.0 4.4 %collective-permute-start = (bf16[2,32,1536]{2,1,0:T(8,128)(2,1)}, bf16[2,32,1536]{2,1,0:T(8,128)(2,1)S(1)}, u32[]{:S(2)}, u32[]{:S(2)}) collective-permute-start(bf16[2,32,1536]{2,1,0:T(8,128)(2,1)} %x_ref.1), channel_id=1, source_target_pairs={{0,1},{1,0},{2,3},{3,2},{4,5},{5,4},{6,7},{7,6},{8,9},{9,8},{10,11... | collective-permute-start | bytes 589832 | tf_op jit(solution)/shard_map/ppermute | solution.py:23
  0.5 3.9 %collective-permute-start.1 = (f32[4,3,1536]{2,0,1:T(4,128)}, f32[4,3,1536]{2,0,1:T(4,128)S(1)}, u32[]{:S(2)}, u32[]{:S(2)}) collective-permute-start(f32[4,3,1536]{2,0,1:T(4,128)} %param.11), channel_id=1, source_target_pairs={{0,1},{1,0},{2,3},{3,2},{4,5},{5,4},{6,7},{7,6},{8,9},{9,8},{10,11... | collective-permute-start | bytes 221192 | tf_op jit(solution)/shard_map/ppermute | solution.py:23
  1.2 10.1 %copy-start = (bf16[256,192]{0,1:T(8,128)(2,1)S(1)}, bf16[256,192]{0,1:T(8,128)(2,1)}, u32[]{:S(2)}) copy-start(bf16[256,192]{0,1:T(8,128)(2,1)} %param.10) | copy-start | bytes 294916
  5.6 8.7 %collective-permute-start.5 = (bf16[4,32,256]{2,1,0:T(8,128)(2,1)S(1)}, bf16[4,32,256]{2,1,0:T(8,128)(2,1)S(1)}, u32[]{:S(2)}, u32[]{:S(2)}) collective-permute-start(bf16[4,32,256]{2,1,0:T(8,128)(2,1)S(1)} %get-tuple-element.41), channel_id=1, source_target_pairs={{0,16},{2,18},{4,20},{6,22},{8,24},{10,26},{12,28},{14,30},{16,0},... | collective-permute-start | bytes 196616 | tf_op jit(solution)/shard_map/ppermute | solution.py:23
  9.7 3.9 %collective-permute-start.2 = (bf16[2,32,256]{2,1,0:T(8,128)(2,1)S(1)}, bf16[2,32,256]{2,1,0:T(8,128)(2,1)S(1)}, u32[]{:S(2)}, u32[]{:S(2)}) collective-permute-start(bf16[2,32,256]{2,1,0:T(8,128)(2,1)S(1)} %get-tuple-element.35.q_ref), channel_id=1, source_target_pairs={{0,8},{2,10},{4,12},{6,14},{8,0},{10,2},{12,4},{14,6},{16,24},{18,... | collective-permute-start | bytes 98312 | tf_op jit(solution)/shard_map/ppermute | solution.py:23
  11.3 10.7 %collective-permute-start.10 = (bf16[192,256]{1,0:T(8,128)(2,1)S(1)}, bf16[192,256]{1,0:T(8,128)(2,1)S(1)}, u32[]{:S(2)}, u32[]{:S(2)}) collective-permute-start(bf16[192,256]{1,0:T(8,128)(2,1)S(1)} %bitcast.26), channel_id=1, source_target_pairs={{0,4},{2,6},{4,0},{6,2},{8,12},{10,14},{12,8},{14,10},{16,20},{18,... | collective-permute-start | bytes 294920 | tf_op jit(solution)/shard_map/ppermute | solution.py:23
  13.6 5.5 %collective-permute-start.3 = (bf16[192,256]{1,0:T(8,128)(2,1)S(1)}, bf16[192,256]{1,0:T(8,128)(2,1)S(1)}, u32[]{:S(2)}, u32[]{:S(2)}) collective-permute-start(bf16[192,256]{1,0:T(8,128)(2,1)S(1)} %bitcast.27), channel_id=1, source_target_pairs={{0,16},{2,18},{4,20},{6,22},{8,24},{10,26},{12,28},{14,30},{16,0},... | collective-permute-start | bytes 294920 | tf_op jit(solution)/shard_map/ppermute | solution.py:23
  14.3 7.8 %collective-permute-start.6 = (bf16[2,4,32,256]{3,2,1,0:T(8,128)(2,1)S(1)}, bf16[2,4,32,256]{3,2,1,0:T(8,128)(2,1)S(1)}, u32[]{:S(2)}, u32[]{:S(2)}) collective-permute-start(bf16[2,4,32,256]{3,2,1,0:T(8,128)(2,1)S(1)} %pad_maximum_fusion.7.refs_0_), channel_id=1, source_target_pairs={{0,2},{2,0},{4,6},{6,4},{8,10},{10,8},{12,14},{14,12},{16,18},{18,... | collective-permute-start | bytes 393224 | tf_op jit(solution)/shard_map/ppermute | solution.py:23
  15.9 6.2 %collective-permute-start.7 = (bf16[2,4,32,256]{3,2,1,0:T(8,128)(2,1)S(1)}, bf16[2,4,32,256]{3,2,1,0:T(8,128)(2,1)S(1)}, u32[]{:S(2)}, u32[]{:S(2)}) collective-permute-start(bf16[2,4,32,256]{3,2,1,0:T(8,128)(2,1)S(1)} %pad_maximum_fusion.7.refs_0_), channel_id=1, source_target_pairs={{0,4},{2,6},{4,0},{6,2},{8,12},{10,14},{12,8},{14,10},{16,20},{18,... | collective-permute-start | bytes 393224 | tf_op jit(solution)/shard_map/ppermute | solution.py:23
  17.4 7.3 %collective-permute-start.8 = (bf16[2,4,32,256]{3,2,1,0:T(8,128)(2,1)S(1)}, bf16[2,4,32,256]{3,2,1,0:T(8,128)(2,1)S(1)}, u32[]{:S(2)}, u32[]{:S(2)}) collective-permute-start(bf16[2,4,32,256]{3,2,1,0:T(8,128)(2,1)S(1)} %pad_maximum_fusion.7.refs_0_), channel_id=1, source_target_pairs={{0,6},{2,4},{4,2},{6,0},{8,14},{10,12},{12,10},{14,8},{16,22},{18,... | collective-permute-start | bytes 393224 | tf_op jit(solution)/shard_map/ppermute | solution.py:23
  19.1 6.7 %collective-permute-start.4 = (bf16[1,192,256]{2,1,0:T(8,128)(2,1)S(1)}, bf16[1,192,256]{2,1,0:T(8,128)(2,1)S(1)}, u32[]{:S(2)}, u32[]{:S(2)}) collective-permute-start(bf16[1,192,256]{2,1,0:T(8,128)(2,1)S(1)} %bitcast.23), channel_id=1, source_target_pairs={{0,2},{2,0},{4,6},{6,4},{8,10},{10,8},{12,14},{14,12},{16,18},{18,... | collective-permute-start | bytes 294920 | tf_op jit(solution)/shard_map/ppermute | solution.py:23
  22.0 10.7 %collective-permute-start.11 = (bf16[2,192,256]{2,1,0:T(8,128)(2,1)S(1)}, bf16[2,192,256]{2,1,0:T(8,128)(2,1)S(1)}, u32[]{:S(2)}, u32[]{:S(2)}) collective-permute-start(bf16[2,192,256]{2,1,0:T(8,128)(2,1)S(1)} %get-tuple-element.54), channel_id=1, source_target_pairs={{0,2},{2,0},{4,6},{6,4},{8,10},{10,8},{12,14},{14,12},{16,18},{18,... | collective-permute-start | bytes 589832 | tf_op jit(solution)/shard_map/ppermute | solution.py:23
  25.9 6.8 %collective-permute-start.12 = (bf16[2,1,192,256]{3,2,1,0:T(8,128)(2,1)S(1)}, bf16[2,1,192,256]{3,2,1,0:T(8,128)(2,1)S(1)}, u32[]{:S(2)}, u32[]{:S(2)}) collective-permute-start(bf16[2,1,192,256]{3,2,1,0:T(8,128)(2,1)S(1)} %pad_maximum_fusion.2), channel_id=1, source_target_pairs={{0,4},{2,6},{4,0},{6,2},{8,12},{10,14},{12,8},{14,10},{16,20},{18,... | collective-permute-start | bytes 589832 | tf_op jit(solution)/shard_map/ppermute | solution.py:23
  27.8 4.6 %collective-permute-start.9 = (bf16[128,384]{1,0:T(8,128)(2,1)S(1)}, bf16[128,384]{1,0:T(8,128)(2,1)S(1)}, u32[]{:S(2)}, u32[]{:S(2)}) collective-permute-start(bf16[128,384]{1,0:T(8,128)(2,1)S(1)} %shard_map.75.part_ref), channel_id=1, source_target_pairs={{0,8},{2,10},{4,12},{6,14},{8,0},{10,2},{12,4},{14,6},{16,24},{18,... | collective-permute-start | bytes 294920 | tf_op jit(solution)/shard_map/ppermute | solution.py:23
  33.2 1.4 %collective-permute-start.13 = (bf16[64,768]{1,0:T(8,128)(2,1)S(1)}, bf16[64,768]{1,0:T(8,128)(2,1)S(1)}, u32[]{:S(2)}, u32[]{:S(2)}) collective-permute-start(bf16[64,768]{1,0:T(8,128)(2,1)S(1)} %shard_map.78), channel_id=1, source_target_pairs={{0,1},{1,0},{2,3},{3,2},{4,5},{5,4},{6,7},{7,6},{8,9},{9,8},{10,11... | collective-permute-start | bytes 294920 | tf_op jit(solution)/shard_map/ppermute | solution.py:23
  33.6 2.6 %collective-permute-start.15 = (bf16[64,768]{1,0:T(8,128)(2,1)S(1)}, bf16[64,768]{1,0:T(8,128)(2,1)S(1)}, u32[]{:S(2)}, u32[]{:S(2)}) collective-permute-start(bf16[64,768]{1,0:T(8,128)(2,1)S(1)} %shard_map.81), channel_id=1, source_target_pairs={{0,1},{1,0},{2,3},{3,2},{4,5},{5,4},{6,7},{7,6},{8,9},{9,8},{10,11... | collective-permute-start | bytes 294920 | tf_op jit(solution)/shard_map/ppermute | solution.py:23
  34.6 4.9 %collective-permute-start.14 = (bf16[2,32,768]{2,1,0:T(8,128)(2,1)S(1)}, bf16[2,32,768]{2,1,0:T(8,128)(2,1)S(1)}, u32[]{:S(2)}, u32[]{:S(2)}) collective-permute-start(bf16[2,32,768]{2,1,0:T(8,128)(2,1)S(1)} %shard_map.79), channel_id=1, source_target_pairs={{0,8},{2,10},{4,12},{6,14},{8,0},{10,2},{12,4},{14,6},{16,24},{18,... | collective-permute-start | bytes 294920 | tf_op jit(solution)/shard_map/ppermute | solution.py:23
